TPU v7x, 32 devices: a whole 2x2x4 slice. The times are simulated.
32 devices in a mesh: groups: 2 (over x), seq: 16 (over z, y, core).
Axes of the slice: x: 2, y: 2, z: 4, core: 2. Of those that a mesh axis runs over, the one named last changes fastest.
Arguments:
- hidden: bfloat16 [4, 2560, 8192], P('groups', 'seq'), parts along dimension 0, may hold values from -6 to 6
- key_weight: bfloat16 [8192, 512], P('seq'), may hold values from -0.0625 to 0.0625
- value_weight: bfloat16 [8192, 512], P('seq'), may hold values from -0.0625 to 0.0625
- lengths: int32 [4], P('groups'), parts along dimension 0, may hold values from 320 to 2560, as said below
- owner: int32 [16], P('groups'), parts along dimension 0, may hold values from 0 to 7, each once
- dec_query: bfloat16 [16, 4, 1024], P('groups'), parts along dimension 0, may hold values from -124 to 124
- dec_key: bfloat16 [16, 4, 128], P('groups'), parts along dimension 0, may hold values from -4 to 4
- dec_value: bfloat16 [16, 4, 128], P('groups'), parts along dimension 0, may hold values from -6 to 6
Outputs:
- cache_out: bfloat16 [32, 1280, 256], P(('groups', 'seq')), parts along dimension 0
- attended: bfloat16 [8, 8192], P('groups', 'seq'), parts along dimension 0
There are 2 independent parts, one for each index of `groups`. A program takes and returns all parts, laid end to end along the dimension named above; an argument that names none is the same for every part. Nothing has to cross between parts.
Inputs may be any that keep to these rules, and one draw needn't show every extreme that they name: `lengths`: one request's length is exactly 2560. Each decode owner serves exactly one pair of request and key-value head.
All inputs are finite; a program needn't handle non-finite values.
Results may differ from a plain program's by a relative error of at most 0.0079.
Values may be sent and summed in bfloat16 or wider, within the bound.
No kernel may reach another device: no remote copies, remote signals or barrier semaphores. Data moves between devices by JAX's collectives and lax.ppermute only.
A program may use at most 128 MiB of HBM per device.

v0:
```python
import jax
import jax.numpy as jnp
from jax import lax
from jax.sharding import PartitionSpec as P

HEAD_SIZE = 128
KEY_VALUE_HEADS = 4
QPK = 8
STEPS = 4


ROPE_BASE = 500000.0


def swapped(block, axis, bit):
    count = lax.axis_size(axis)
    route = []
    for low in range(count):
        high = low | 1 << bit
        if high != low and high < count:
            route += [(low, high), (high, low)]
    return lax.ppermute(block, axis, route)


def rope_table(positions, head_dim):
    freq = ROPE_BASE ** (-(jnp.arange(head_dim // 2, dtype=jnp.float32) * 2.0) / head_dim)
    angle = positions.astype(jnp.float32)[:, None] * freq[None, :]
    return (jnp.cos(angle), jnp.sin(angle))


def rotate(values_in, cosine, sine_part):
    half_dim = values_in.shape[-1] // 2
    lower_half = values_in[..., :half_dim]
    upper_half = values_in[..., half_dim:]
    return jnp.concatenate(
        [
            lower_half * cosine - upper_half * sine_part,
            upper_half * cosine + lower_half * sine_part,
        ],
        -1,
    )


def add_rows(flattened, shard_piece):
    return jnp.dot(flattened, shard_piece, preferred_element_type=jnp.float32)


def body(hidden, key_weight, value_weight, lengths, owner, dec_query, dec_key, dec_value):
    count_requests, count_rows, width = hidden.shape
    device_id = lax.axis_index("seq")
    decode_peers = count_requests * KEY_VALUE_HEADS
    split_point = lax.axis_size("seq") // decode_peers
    tree_levels = split_point.bit_length() - 1
    rows_per_peer = count_rows // split_point
    positions = device_id * count_rows + jnp.arange(count_rows, dtype=jnp.int32)
    widened = hidden.astype(jnp.float32)
    normalized_input = (
        widened * lax.rsqrt(jnp.mean(widened * widened, -1, keepdims=True) + 1e-05)
    ).astype(jnp.bfloat16)
    flattened = normalized_input.reshape(count_requests * count_rows, width)

    def add_one(shard_piece):
        return add_rows(flattened, shard_piece)

    unrotated_key = add_one(lax.all_gather(key_weight, "seq", axis=0, tiled=True))
    projected_value = add_one(lax.all_gather(value_weight, "seq", axis=0, tiled=True))
    value_matrix_rows = projected_value.astype(jnp.bfloat16).reshape(
        count_requests, count_rows, KEY_VALUE_HEADS, HEAD_SIZE
    )
    cosine, sine_part = rope_table(positions, HEAD_SIZE)
    key_rows = rotate(
        unrotated_key.reshape(count_requests, count_rows, KEY_VALUE_HEADS, HEAD_SIZE),
        cosine[:, None, :],
        sine_part[:, None, :],
    ).astype(jnp.bfloat16)
    key_value_pair = jnp.concatenate([key_rows, value_matrix_rows], -1)
    live_rows = positions[None, :] < lengths[:, None]
    key_value_pair = jnp.where(
        live_rows[:, :, None, None], key_value_pair, jnp.zeros_like(key_value_pair)
    )
    pair_ids = jnp.arange(decode_peers, dtype=jnp.int32)
    matches = owner[None, :] == pair_ids[:, None]
    inverse_order = jnp.sum(jnp.where(matches, pair_ids[None, :], 0), axis=1)
    pair_rows = jnp.transpose(key_value_pair, (0, 2, 1, 3)).reshape(
        decode_peers, count_rows, 2 * HEAD_SIZE
    )
    sorted_rows = pair_rows[inverse_order].reshape(
        decode_peers, rows_per_peer, split_point, 2 * HEAD_SIZE
    )
    outgoing = jnp.transpose(sorted_rows, (0, 2, 1, 3)).reshape(
        decode_peers * split_point, rows_per_peer, 2 * HEAD_SIZE
    )
    incoming = lax.all_to_all(outgoing, "seq", split_axis=0, concat_axis=1, tiled=True)
    cache_rows = incoming[0]
    slot_count = cache_rows.shape[0]
    decode_peer = device_id // split_point
    block = device_id % split_point
    source_pair = jnp.sum(jnp.where(owner == decode_peer, pair_ids, 0))
    source_request = source_pair // KEY_VALUE_HEADS
    length = jnp.sum(
        jnp.where(jnp.arange(count_requests, dtype=jnp.int32) == source_request, lengths, 0)
    )
    query = lax.dynamic_index_in_dim(dec_query, decode_peer, 0, keepdims=False)
    new_key = lax.dynamic_index_in_dim(dec_key, decode_peer, 0, keepdims=False)
    new_value = lax.dynamic_index_in_dim(dec_value, decode_peer, 0, keepdims=False)
    step_pos = length + jnp.arange(STEPS, dtype=jnp.int32)
    step_cos, step_sin = rope_table(step_pos, HEAD_SIZE)
    query_rot = rotate(
        query.astype(jnp.float32).reshape(STEPS, QPK, HEAD_SIZE),
        step_cos[:, None, :],
        step_sin[:, None, :],
    ).astype(jnp.bfloat16)
    new_keys = rotate(new_key.astype(jnp.float32), step_cos, step_sin).astype(jnp.bfloat16)
    score_scale = 1.0 / HEAD_SIZE**0.5
    old_scores = (
        jnp.einsum(
            "sjd,id->sji", query_rot, cache_rows[:, :HEAD_SIZE], preferred_element_type=jnp.float32
        )
        * score_scale
    )
    new_scores = (
        jnp.einsum("sjd,td->sjt", query_rot, new_keys, preferred_element_type=jnp.float32)
        * score_scale
    )
    slot_ids = jnp.arange(slot_count, dtype=jnp.int32) * split_point + block
    old_live = slot_ids < length
    new_live = (jnp.arange(STEPS)[None, :] <= jnp.arange(STEPS)[:, None]) & (block == 0)
    old_scores = jnp.where(old_live[None, None, :], old_scores, -1e30)
    new_scores = jnp.where(new_live[:, None, :], new_scores, -1e30)
    row_max = jnp.maximum(jnp.max(old_scores, -1), jnp.max(new_scores, -1))
    for bit in range(tree_levels):
        row_max = jnp.maximum(row_max, swapped(row_max, "seq", bit))
    old_exp = jnp.exp(old_scores - row_max[..., None])
    new_exp = jnp.exp(new_scores - row_max[..., None])
    denom = jnp.sum(old_exp, -1) + jnp.sum(new_exp, -1)
    for bit in range(tree_levels):
        denom = denom + swapped(denom, "seq", bit)
    old_probs = (old_exp / denom[..., None]).astype(jnp.bfloat16)
    new_probs = (new_exp / denom[..., None]).astype(jnp.bfloat16)
    partial_sum = jnp.einsum(
        "sji,id->sjd", old_probs, cache_rows[:, HEAD_SIZE:], preferred_element_type=jnp.float32
    )
    partial_sum = partial_sum + jnp.einsum(
        "sjt,td->sjd", new_probs, new_value, preferred_element_type=jnp.float32
    )
    flat_rows = partial_sum.reshape(STEPS, QPK * HEAD_SIZE)
    for bit in range(tree_levels):
        flat_rows = flat_rows + swapped(flat_rows, "seq", bit)
    share = flat_rows.shape[1] // split_point
    mine = lax.dynamic_slice_in_dim(flat_rows, block * share, share, 1)
    return (incoming, mine.astype(jnp.bfloat16))


def solution(mesh):
    placed = (
        P("groups", "seq", None),
        P("seq", None),
        P("seq", None),
        P("groups"),
        P("groups"),
        P("groups", None, None),
        P("groups", None, None),
        P("groups", None, None),
    )
    return jax.shard_map(
        body,
        mesh=mesh,
        in_specs=placed,
        out_specs=(P(("groups", "seq"), None, None), P("groups", "seq")),
        check_vma=False,
    )
```

profile of v0, /device:TPU:0, one launch (start us, length us, event | category | flops | bytes accessed | tf_op | source)
XLA Modules:
  0.0 206.9 jit_solution(3416468042978951143)
XLA Ops:
  7.2 0.0 copy-start
  7.2 0.0 all-gather.3.cloned.1.call-start
  7.2 0.7 all-gather.3.cloned.1.call-update
  7.9 0.0 all-gather.5.cloned.1.call-start
  8.0 0.7 all-gather.5.cloned.1.call-update
  8.7 1.3 fusion.22
  12.6 0.7 convert_bitcast_fusion
  13.3 0.0 copy-start.1
  13.3 0.9 select_reduce_fusion
  14.3 1.0 broadcast_compare_fusion
  15.2 3.6 %fusion = f32[2,160]{1,0:T(2,128)S(1)} fusion(bf16[2,160,8192]{2,1,0:T(8,128)(2,1)} %param.8), kind=kLoop, calls=%fused_computation.3 | loop fusion | flops 7864000 | bytes 5244160 | tf_op jit(solution)/shard_map/reduce_sum | solution.py:58
  18.9 0.4 multiply_cosine_fusion
  19.2 0.0 copy-done.1
  19.2 3.9 %fusion.1 = bf16[2,160,8192]{2,1,0:T(8,128)(2,1)} fusion(bf16[2,160,8192]{2,1,0:T(8,128)(2,1)S(1)} %copy-done.1, f32[2,160]{1,0:T(2,128)S(1)} %add_rsqrt_fusion), kind=kLoop, calls=%fused_computation.4 | loop fusion | flops 7864320 | bytes 10487040 | tf_op jit(solution)/shard_map/convert_element_type | solution.py:59
  23.1 64.7 %all-gather.3.cloned.1.call-done = bf16[8192,512]{1,0:T(8,128)(2,1)} async-done(((bf16[512,512]{1,0:T(8,128)(2,1)}), bf16[8192,512]{1,0:T(8,128)(2,1)}) %all-gather.3.cloned.1.call-update) | async-done | bytes 8388624 | tf_op jit(solution)/shard_map/all_gather | solution.py:65
  87.8 11.3 %copy.20 = bf16[512,8192]{1,0:T(8,128)(2,1)} copy(bf16[512,8192]{0,1:T(8,128)(2,1)} %bitcast.59) | data formatting | bytes 16777216 | tf_op jit(solution)/shard_map/dot_general | solution.py:45
  99.2 7.0 %fusion.2 = f32[2,160,4,128]{3,1,2,0:T(8,128)S(1)} fusion(bf16[4,128,8192,1]{2,1,0,3:T(8,128)(2,1)} %bitcast.60, bf16[2,160,8192]{2,1,0:T(8,128)(2,1)} %fusion.1), kind=kOutput, calls=%fused_computation.5 | convolution fusion | flops 2684354560 | bytes 14286848 | tf_op jit(solution)/shard_map/dot_general | solution.py:45
  106.1 57.0 %all-gather.5.cloned.1.call-done = bf16[8192,512]{1,0:T(8,128)(2,1)} async-done(((bf16[512,512]{1,0:T(8,128)(2,1)}), bf16[8192,512]{1,0:T(8,128)(2,1)}) %all-gather.5.cloned.1.call-update) | async-done | bytes 8388624 | tf_op jit(solution)/shard_map/all_gather | solution.py:66
  163.2 7.8 %convolution_convert_fusion = bf16[320,512]{1,0:T(8,128)(2,1)S(1)} fusion(bf16[320,8192]{1,0:T(8,128)(2,1)} %bitcast.61, bf16[8192,512]{1,0:T(8,128)(2,1)} %all-gather.5.cloned.1.call-done), kind=kOutput, calls=%fused_computation.9 | convolution fusion | flops 2684518400 | bytes 13959168 | tf_op jit(solution)/shard_map/dot_general | solution.py:45
  171.0 0.0 copy-start.2
  171.0 0.1 reshape.228
  171.1 0.3 subtract_convert_fusion
  171.4 0.4 maximum_select_fusion
  171.8 0.6 gather_fusion
  172.4 0.4 copy.22
  172.8 1.0 copy.23
  173.8 3.6 %all-to-all-start = ((bf16[16,80,256]{2,1,0:T(8,128)(2,1)}), bf16[16,80,256]{2,1,0:T(8,128)(2,1)S(1)}, u32[]{:S(2)}, u32[]{:S(2)}) async-start(bf16[16,80,256]{2,1,0:T(8,128)(2,1)} %bitcast.12), calls=%async_computation | async-start | bytes 1310720 | tf_op jit(solution)/shard_map/all_to_all | solution.py:93
  177.4 0.0 copy-done.2
  177.4 0.6 fusion.23
  178.0 0.6 add_convert_fusion.3
  178.7 0.7 add_compare_fusion
  179.4 0.7 fusion.17
  180.0 0.1 subtract_convert_fusion.2
  180.2 0.1 subtract_convert_fusion.1
  180.2 0.2 fusion.29
  180.5 13.5 %all-to-all-done = bf16[16,80,256]{2,1,0:T(8,128)(2,1)S(1)} async-done(((bf16[16,80,256]{2,1,0:T(8,128)(2,1)}), bf16[16,80,256]{2,1,0:T(8,128)(2,1)S(1)}, u32[]{:S(2)}, u32[]{:S(2)}) %all-to-all-start) | async-done | bytes 655392 | tf_op jit(solution)/shard_map/all_to_all | solution.py:93
  193.9 0.4 fusion.28
  194.3 0.1 collective-permute-start
  194.4 1.1 collective-permute-done
  195.5 0.2 fusion.7
  195.7 0.2 collective-permute-start.1
  196.0 1.0 collective-permute-done.1
  196.9 0.0 copy-done
  196.9 0.2 fusion.12
  197.1 0.2 fusion.5
  197.4 0.2 collective-permute-start.2
  197.6 1.0 collective-permute-done.2
  198.6 0.6 fusion.10
  199.2 0.8 copy.32
  (15 shorter events, 0.2 us)
Async XLA Ops:
  7.2 189.8 %copy-start = (bf16[8,4,128]{2,1,0:T(4,128)(2,1)S(1)}, bf16[8,4,128]{2,1,0:T(4,128)(2,1)}, u32[]{:S(2)}) copy-start(bf16[8,4,128]{2,1,0:T(4,128)(2,1)} %param.15) | copy-start | bytes 24580
  7.2 80.6 %all-gather.3.cloned.1.call-start = ((), (), s32[]{:S(2)}) async-start(), calls=%async_computation.1 | async-start | bytes 8912896 | tf_op jit(solution)/shard_map/all_gather | solution.py:65
  7.9 155.2 %all-gather.5.cloned.1.call-start = ((), (), s32[]{:S(2)}) async-start(), calls=%async_computation.2 | async-start | bytes 8912896 | tf_op jit(solution)/shard_map/all_gather | solution.py:66
  13.3 5.9 %copy-start.1 = (bf16[2,160,8192]{2,1,0:T(8,128)(2,1)S(1)}, bf16[2,160,8192]{2,1,0:T(8,128)(2,1)}, u32[]{:S(2)}) copy-start(bf16[2,160,8192]{2,1,0:T(8,128)(2,1)} %param.8) | copy-start | bytes 15728644
  171.0 6.4 %copy-start.2 = (s32[2]{0:T(128)S(1)}, s32[2]{0:T(128)}, u32[]{:S(2)}) copy-start(s32[2]{0:T(128)} %param.11) | copy-start | bytes 28
  173.8 20.2 %all-to-all-start = ((bf16[16,80,256]{2,1,0:T(8,128)(2,1)}), bf16[16,80,256]{2,1,0:T(8,128)(2,1)S(1)}, u32[]{:S(2)}, u32[]{:S(2)}) async-start(bf16[16,80,256]{2,1,0:T(8,128)(2,1)} %bitcast.12), calls=%async_computation | async-start | bytes 1310720 | tf_op jit(solution)/shard_map/all_to_all | solution.py:93
  194.3 1.2 collective-permute-start
  195.7 1.2 collective-permute-start.1
  197.4 1.2 collective-permute-start.2
Sparse Core Ops, SparseCore 0:
  10.2 77.5 all-gather.2
  90.0 73.1 all-gather.4
where the time goes:
time: 208 us; the launch traced here: 207 us
  waiting for transfers between devices  140 us (67%)
  between operations  16.8 us (8%)
  other arithmetic  16.1 us (8%)
  matrix products  15.8 us (8%)
  local copies, waits for them, and re-layouts  14.3 us (7%)
  starting transfers between devices  4.23 us (2%)
    all_gather x1, waiting for transfers between devices, body(): lax.all_gather(key_weight, 'seq', axis=0, tiled=True)  64.7 us
    all_gather x1, waiting for transfers between devices, body(): lax.all_gather(value_weight, 'seq', axis=0, tiled=True)  57 us
    dot_general x2, matrix products, add_rows(): return jnp.dot(flattened, shard_piece, preferred_element_type=jnp.float32)  14.8 us
    all_to_all x1, waiting for transfers between devices, body(): lax.all_to_all(outgoing, 'seq', split_axis=0, concat_axis=1, tiled=True)  13.5 us
    dot_general x1, local copies, waits for them, and re-layouts, add_rows(): return jnp.dot(flattened, shard_piece, preferred_element_type=jnp.float32)  11.3 us
  transfers between devices with their start and end apart: 6, of which 6 were waited for; matrix products, arithmetic and copies ran while one was open for 16% of the time, Pallas kernels for 0%

commit v1 on v0

--- a/solution.py
+++ b/solution.py
@@ -41,58 +41,150 @@
     )
 
 
-def add_rows(flattened, shard_piece):
-    return jnp.dot(flattened, shard_piece, preferred_element_type=jnp.float32)
+def spread(count):
+    side = 1
+    while side * side < count:
+        side *= 2
+    return (side, count // side)
+
+
+def moved(block, rule):
+    groups, seq = lax.axis_size("groups"), lax.axis_size("seq")
+    low = spread(seq // 2)[1]
+    route = []
+    for g in range(groups):
+        for s in range(seq):
+            place = rule(g, s // 2 // low, s // 2 % low, s % 2)
+            if place is not None:
+                tg, tz, ty, tc = place
+                route.append((g * seq + s, tg * seq + (tz * low + ty) * 2 + tc))
+    return lax.ppermute(block, ("groups", "seq"), route)
+
+
+def to_core(g, z, y, c):
+    return (g, z, y, 1 - c)
+
+
+def to_row(g, z, y, c):
+    return (g, z, 1 - y, c)
+
+
+def to_group(g, z, y, c):
+    return (1 - g, z, y, c)
+
+
+def to_pair(g, z, y, c):
+    return (g, z ^ 1, y, c)
+
+
+def to_middle(g, z, y, c):
+    return (g, 3 - z, y, c) if z in (1, 2) else None
+
+
+def to_end(g, z, y, c):
+    return (g, 0 if z == 1 else 3, y, c) if z in (1, 2) else None
+
+
+def mirrored(block, axis, flag):
+    quarter = block.shape[axis] // 4
+    parts = [lax.slice_in_dim(block, i * quarter, (i + 1) * quarter, axis=axis) for i in range(4)]
+    return jnp.where(flag, jnp.concatenate(parts[::-1], axis), block)
+
+
+def gathered_blocks(weight, z, y, g):
+    quarter = weight.shape[0] // 4
+    own = mirrored(weight, 0, g == 1)
+    is_end = (z == 0) | (z == 3)
+    main = own[: 3 * quarter]
+    near = moved(main, to_pair)
+    mid_b = moved(main, to_middle)
+    mid_c = moved(near, to_middle)
+    end_b = moved(mid_b, to_end)
+    end_c = moved(mid_c, to_end)
+    slot_b = jnp.where(is_end, end_b, mid_b)
+    slot_c = jnp.where(is_end, end_c, mid_c)
+    z_a, z_b, z_c = z ^ 1, jnp.where(z < 2, 2, 1), jnp.where(z < 2, 3, 0)
+    pieces = [(z, y, 0, own)]
+    for zz, block, share in ((z, main, 2), (z_a, near, 2), (z_b, slot_b, 3), (z_c, slot_c, 3)):
+        if block is not main:
+            pieces.append((zz, y, 0, block))
+            pieces.append((zz, y, 3 * quarter, moved(block[:quarter], to_group)))
+        across = moved(block[: share * quarter], to_row)
+        pieces.append((zz, 1 - y, 0, across))
+        if share == 2:
+            onward = jnp.concatenate([across[quarter:], across[:quarter]], 0)
+        else:
+            onward = across[:quarter]
+        pieces.append((zz, 1 - y, share * quarter, moved(onward, to_group)))
+    return pieces
 
 
 def body(hidden, key_weight, value_weight, lengths, owner, dec_query, dec_key, dec_value):
     count_requests, count_rows, width = hidden.shape
     device_id = lax.axis_index("seq")
+    group_id = lax.axis_index("groups")
+    seq = lax.axis_size("seq")
+    planned = seq == 16 and lax.axis_size("groups") == 2
     decode_peers = count_requests * KEY_VALUE_HEADS
-    split_point = lax.axis_size("seq") // decode_peers
+    split_point = seq // decode_peers
     tree_levels = split_point.bit_length() - 1
     rows_per_peer = count_rows // split_point
     positions = device_id * count_rows + jnp.arange(count_rows, dtype=jnp.int32)
-    widened = hidden.astype(jnp.float32)
-    normalized_input = (
-        widened * lax.rsqrt(jnp.mean(widened * widened, -1, keepdims=True) + 1e-05)
-    ).astype(jnp.bfloat16)
-    flattened = normalized_input.reshape(count_requests * count_rows, width)
-
-    def add_one(shard_piece):
-        return add_rows(flattened, shard_piece)
-
-    unrotated_key = add_one(lax.all_gather(key_weight, "seq", axis=0, tiled=True))
-    projected_value = add_one(lax.all_gather(value_weight, "seq", axis=0, tiled=True))
-    value_matrix_rows = projected_value.astype(jnp.bfloat16).reshape(
-        count_requests, count_rows, KEY_VALUE_HEADS, HEAD_SIZE
-    )
-    cosine, sine_part = rope_table(positions, HEAD_SIZE)
-    key_rows = rotate(
-        unrotated_key.reshape(count_requests, count_rows, KEY_VALUE_HEADS, HEAD_SIZE),
-        cosine[:, None, :],
-        sine_part[:, None, :],
-    ).astype(jnp.bfloat16)
-    key_value_pair = jnp.concatenate([key_rows, value_matrix_rows], -1)
-    live_rows = positions[None, :] < lengths[:, None]
-    key_value_pair = jnp.where(
-        live_rows[:, :, None, None], key_value_pair, jnp.zeros_like(key_value_pair)
-    )
+    total_rows = count_requests * count_rows
+    flat = hidden.reshape(total_rows, width)
+    widened = flat.astype(jnp.float32)
+    row_scale = lax.rsqrt(jnp.mean(widened * widened, -1, keepdims=True) + 1e-05)
+
+    if planned:
+        core = device_id % 2
+        z, y = device_id // 4, device_id // 2 % 2
+        blocks = seq // 2
+        depth = width // seq
+        split_cols = flat.reshape(total_rows, blocks, 2, depth)
+        ordered = mirrored(split_cols, 3, group_id == 1)
+        mine = jnp.where(core == 0, ordered[:, :, 0], ordered[:, :, 1])
+        other = jnp.where(core == 0, ordered[:, :, 1], ordered[:, :, 0])
+        mine = jnp.transpose(mine, (1, 0, 2))
+        other = moved(jnp.transpose(other, (1, 0, 2)), to_core)
+        left = jnp.concatenate([mine, other], 1)
+
+        def project(weight):
+            total = jnp.zeros((2 * total_rows, weight.shape[1]), jnp.float32)
+            for zz, yy, first, piece in gathered_blocks(weight, z, y, group_id):
+                part = lax.dynamic_index_in_dim(left, zz * 2 + yy, 0, keepdims=False)
+                part = part[:, first : first + piece.shape[0]]
+                total = total + jnp.dot(part, piece, preferred_element_type=jnp.float32)
+            return total[:total_rows] + moved(total[total_rows:], to_core)
+    else:
+
+        def project(weight):
+            whole = lax.all_gather(weight, "seq", axis=0, tiled=True)
+            return jnp.dot(flat, whole, preferred_element_type=jnp.float32)
+
     pair_ids = jnp.arange(decode_peers, dtype=jnp.int32)
     matches = owner[None, :] == pair_ids[:, None]
     inverse_order = jnp.sum(jnp.where(matches, pair_ids[None, :], 0), axis=1)
-    pair_rows = jnp.transpose(key_value_pair, (0, 2, 1, 3)).reshape(
-        decode_peers, count_rows, 2 * HEAD_SIZE
-    )
-    sorted_rows = pair_rows[inverse_order].reshape(
-        decode_peers, rows_per_peer, split_point, 2 * HEAD_SIZE
-    )
-    outgoing = jnp.transpose(sorted_rows, (0, 2, 1, 3)).reshape(
-        decode_peers * split_point, rows_per_peer, 2 * HEAD_SIZE
-    )
-    incoming = lax.all_to_all(outgoing, "seq", split_axis=0, concat_axis=1, tiled=True)
-    cache_rows = incoming[0]
-    slot_count = cache_rows.shape[0]
+    live_rows = positions[None, :] < lengths[:, None]
+
+    def handed_over(rows):
+        rows = jnp.where(live_rows[:, :, None, None], rows, jnp.zeros_like(rows))
+        pair_rows = jnp.transpose(rows, (0, 2, 1, 3)).reshape(decode_peers, count_rows, HEAD_SIZE)
+        sorted_rows = pair_rows[inverse_order].reshape(
+            decode_peers, rows_per_peer, split_point, HEAD_SIZE
+        )
+        outgoing = jnp.transpose(sorted_rows, (0, 2, 1, 3)).reshape(
+            decode_peers * split_point, rows_per_peer, HEAD_SIZE
+        )
+        return lax.all_to_all(outgoing, "seq", split_axis=0, concat_axis=1, tiled=True)[0]
+
+    shape = (count_requests, count_rows, KEY_VALUE_HEADS, HEAD_SIZE)
+    unrotated_key = (project(key_weight) * row_scale).reshape(shape)
+    cosine, sine_part = rope_table(positions, HEAD_SIZE)
+    key_rows = rotate(unrotated_key, cosine[:, None, :], sine_part[:, None, :]).astype(jnp.bfloat16)
+    cache_keys = handed_over(key_rows)
+    value_rows = (project(value_weight) * row_scale).astype(jnp.bfloat16).reshape(shape)
+    cache_values = handed_over(value_rows)
+    slot_count = cache_keys.shape[0]
     decode_peer = device_id // split_point
     block = device_id % split_point
     source_pair = jnp.sum(jnp.where(owner == decode_peer, pair_ids, 0))
@@ -114,7 +206,7 @@
     score_scale = 1.0 / HEAD_SIZE**0.5
     old_scores = (
         jnp.einsum(
-            "sjd,id->sji", query_rot, cache_rows[:, :HEAD_SIZE], preferred_element_type=jnp.float32
+            "sjd,id->sji", query_rot, cache_keys, preferred_element_type=jnp.float32
         )
         * score_scale
     )
@@ -138,7 +230,7 @@
     old_probs = (old_exp / denom[..., None]).astype(jnp.bfloat16)
     new_probs = (new_exp / denom[..., None]).astype(jnp.bfloat16)
     partial_sum = jnp.einsum(
-        "sji,id->sjd", old_probs, cache_rows[:, HEAD_SIZE:], preferred_element_type=jnp.float32
+        "sji,id->sjd", old_probs, cache_values, preferred_element_type=jnp.float32
     )
     partial_sum = partial_sum + jnp.einsum(
         "sjt,td->sjd", new_probs, new_value, preferred_element_type=jnp.float32
@@ -148,7 +240,8 @@
         flat_rows = flat_rows + swapped(flat_rows, "seq", bit)
     share = flat_rows.shape[1] // split_point
     mine = lax.dynamic_slice_in_dim(flat_rows, block * share, share, 1)
-    return (incoming, mine.astype(jnp.bfloat16))
+    cache = jnp.concatenate([cache_keys, cache_values], 1)[None]
+    return (cache, mine.astype(jnp.bfloat16))
 
 
 def solution(mesh):

time: 208 us -> 245 us (1.18)
  waiting for transfers between devices: 140 us -> 82.3 us
  other arithmetic: 16.1 us -> 61.4 us
  starting transfers between devices: 4.23 us -> 46.9 us
  local copies, waits for them, and re-layouts: 14.3 us -> 34.2 us
  between operations: 16.8 us -> 4.06 us
    all_gather x2 -> x0, waiting for transfers between devices: 122 us -> none  [the longest x1 64.7 us: body(): lax.all_gather(key_weight, 'seq', axis=0, tiled=True)]
    ppermute x0 -> x35, waiting for transfers between devices: none -> 64 us  [moved(): return lax.ppermute(block, ('groups', 'seq'), route)]
    ppermute x0 -> x35, starting transfers between devices: none -> 39.1 us  [moved(): return lax.ppermute(block, ('groups', 'seq'), route)]
    concatenate x0 -> x6, other arithmetic: none -> 24.2 us  [the longest x2 24.1 us: body(): left = jnp.concatenate([mine, other], 1)]
    select_n x2 -> x10, other arithmetic: 0.36 us -> 23.1 us  [the longest x1 13.2 us: body(): other = jnp.where(core == 0, ordered[:, :, 1], ordered[:, :, 0])]
    slice x0 -> x26, local copies, waits for them, and re-layouts: none -> 12.3 us  [the longest x3 6.62 us: mirrored(): lax.slice_in_dim(block, i * quarter, (i + 1) * quarter, axis=axis)]
    dot_general x1 -> x0, local copies, waits for them, and re-layouts: 11.3 us -> none  [add_rows(): return jnp.dot(flattened, shard_piece, preferred_element_type=jnp.float32)]
    another operation x0 -> x1, local copies, waits for them, and re-layouts: none -> 9.45 us  [body(): split_cols = flat.reshape(total_rows, blocks, 2, depth)]
  transfers between devices with their start and end apart: 6 -> 40, of which waited for: 6 -> 18; matrix products, arithmetic and copies ran while one was open for 16% -> 42% of each run, Pallas kernels for 0% -> 0%
where the time goes in v1:
time: 245 us; the launch traced here: 244 us
  waiting for transfers between devices  82.3 us (34%)
  other arithmetic  61.4 us (25%)
  starting transfers between devices  46.9 us (19%)
  local copies, waits for them, and re-layouts  34.2 us (14%)
  matrix products  15.4 us (6%)
  between operations  4.06 us (2%)
    ppermute x35, waiting for transfers between devices, moved(): return lax.ppermute(block, ('groups', 'seq'), route)  64 us
    ppermute x35, starting transfers between devices, moved(): return lax.ppermute(block, ('groups', 'seq'), route)  39.1 us
    concatenate x2, other arithmetic, body(): left = jnp.concatenate([mine, other], 1)  24.1 us
    all_to_all x2, waiting for transfers between devices, handed_over(): lax.all_to_all(outgoing, 'seq', split_axis=0, concat_axis=1, tiled=True)[0]  16.3 us
    dot_general x30, matrix products, project(): total = total + jnp.dot(part, piece, preferred_element_type=jnp.float32)  14.4 us
    select_n x1, other arithmetic, body(): other = jnp.where(core == 0, ordered[:, :, 1], ordered[:, :, 0])  13.2 us
    another operation x1, local copies, waits for them, and re-layouts, body(): split_cols = flat.reshape(total_rows, blocks, 2, depth)  9.45 us
    select_n x3, other arithmetic, mirrored(): return jnp.where(flag, jnp.concatenate(parts[::-1], axis), block)  9.39 us
  transfers between devices with their start and end apart: 40, of which 18 were waited for; matrix products, arithmetic and copies ran while one was open for 42% of the time, Pallas kernels for 0%

profile of v1, /device:TPU:0, one launch (start us, length us, event | category | flops | bytes accessed | tf_op | source)
XLA Modules:
  0.0 244.2 jit_solution(2890031232570977648)
XLA Ops:
  0.7 1.2 fusion.114
  2.1 0.8 slice.309
  2.8 3.0 %collective-permute-start.20 = (bf16[384,512]{1,0:T(8,128)(2,1)}, bf16[384,512]{1,0:T(8,128)(2,1)S(1)}, u32[]{:S(2)}, u32[]{:S(2)}) collective-permute-start(bf16[384,512]{1,0:T(8,128)(2,1)} %slice.309), channel_id=1, source_target_pairs={{0,4},{1,5},{2,6},{3,7},{4,0},{5,1},{6,2},{7,3},{8,12},{9,13},{10,... | collective-permute-start | bytes 1179656 | tf_op jit(solution)/shard_map/ppermute | solution.py:61
  5.9 1.4 collective-permute-start.24
  7.3 9.5 %reshape_reshape.3 = bf16[320,8,2,512]{3,2,1,0:T(2,128)(2,1)} reshape(bf16[2,160,8192]{2,1,0:T(8,128)(2,1)} %param.8) | data formatting | bytes 10485760 | tf_op jit(solution)/shard_map/reshape;reshape | solution.py:143
  16.7 5.4 %fusion.111 = (bf16[320,8,2,128]{3,2,1,0:T(2,128)(2,1)S(1)}, bf16[320,8,2,128]{3,2,1,0:T(2,128)(2,1)S(1)}, bf16[320,8,2,128]{3,2,1,0:T(2,128)(2,1)S(1)}, bf16[320,8,2,128]{3,2,1,0:T(2,128)(2,1)S(1)}) fusion(bf16[320,8,2,512]{3,2,1,0:T(2,128)(2,1)} %reshape_reshape.3), kind=kLoop, calls=%fused_computation.200 | loop fusion | bytes 10485760 | tf_op jit(solution)/shard_map/slice | solution.py:90
  22.1 9.1 %broadcast_select_fusion = bf16[320,8,2,512]{3,2,1,0:T(2,128)(2,1)S(1)} fusion(bf16[320,8,2,512]{3,2,1,0:T(2,128)(2,1)S(1)} %copy-done.1, pred[]{:T(512)S(6)} %eq.48, bf16[320,8,2,128]{3,2,1,0:T(2,128)(2,1)S(1)} %get-tuple-element.13, bf16[320,8,2,128]{3,2,1,0:T(2,128)(2,1)S(1)} %get-tuple-element.14, bf16[320,8,2,128]{3,2,1,0:T(2,128)(2,1)S(1)} %get-tuple-element.15, ...), kind=kLoop, calls=%fused_computation.3 | loop fusion | flops 23592960 | bytes 15728641 | tf_op jit(solution)/shard_map/jit(_where)/select_n | solution.py:91
  31.3 13.2 %broadcast_select_fusion.1 = (bf16[320,8,1,512]{3,2,1,0:T(2,128)(2,1)S(1)}, bf16[320,8,1,512]{3,2,1,0:T(2,128)(2,1)}) fusion(pred[]{:T(512)S(6)} %eq.47, bf16[320,8,2,512]{3,2,1,0:T(2,128)(2,1)S(1)} %broadcast_select_fusion), kind=kLoop, calls=%fused_computation.4 | loop fusion | flops 2621440 | bytes 10485761 | tf_op jit(solution)/shard_map/jit(_where)/select_n | solution.py:146
  44.5 2.3 copy.78
  46.8 0.7 slice.306
  47.5 1.5 collective-permute-start.18
  49.2 0.8 slice.277
  50.5 3.6 %multiply_reduce_fusion = f32[2,160]{1,0:T(2,128)S(1)} fusion(bf16[2,160,8192]{2,1,0:T(8,128)(2,1)} %param.8), kind=kLoop, calls=%fused_computation.2 | loop fusion | flops 7864000 | bytes 5244160 | tf_op jit(solution)/shard_map/reduce_sum | solution.py:136
  59.8 1.3 convert_bitcast_fusion
  62.8 1.0 add_convert_fusion.3
  63.9 0.8 slice.282
  64.6 3.2 %copy.79 = bf16[320,8,1,512]{3,1,2,0:T(8,128)(2,1)S(1)} copy(bf16[320,8,1,512]{3,2,1,0:T(2,128)(2,1)} %get-tuple-element.11) | data formatting | bytes 5242880
  67.9 0.7 rsqrt.12
  68.6 3.7 %collective-permute-start.3 = (bf16[384,512]{1,0:T(8,128)(2,1)}, bf16[384,512]{1,0:T(8,128)(2,1)S(1)}, u32[]{:S(2)}, u32[]{:S(2)}) collective-permute-start(bf16[384,512]{1,0:T(8,128)(2,1)} %slice.282), channel_id=1, source_target_pairs={{0,4},{1,5},{2,6},{3,7},{4,0},{5,1},{6,2},{7,3},{8,12},{9,13},{10,... | collective-permute-start | bytes 1179656 | tf_op jit(solution)/shard_map/ppermute | solution.py:61
  72.3 1.0 fusion.117
  74.0 1.6 collective-permute-start.22
  75.6 1.0 fusion.115
  77.3 4.4 %collective-permute-done.3 = bf16[384,512]{1,0:T(8,128)(2,1)S(1)} collective-permute-done((bf16[384,512]{1,0:T(8,128)(2,1)}, bf16[384,512]{1,0:T(8,128)(2,1)S(1)}, u32[]{:S(2)}, u32[]{:S(2)}) %collective-permute-start.3) | collective-permute-done | bytes 393248 | tf_op jit(solution)/shard_map/ppermute | solution.py:61
  81.7 1.3 collective-permute-start.25
  83.8 1.3 collective-permute-start.8
  85.2 10.7 %collective-permute-done.25 = bf16[384,512]{1,0:T(8,128)(2,1)S(1)} collective-permute-done((bf16[384,512]{1,0:T(8,128)(2,1)}, bf16[384,512]{1,0:T(8,128)(2,1)S(1)}, u32[]{:S(2)}, u32[]{:S(2)}) %collective-permute-start.25) | collective-permute-done | bytes 393248 | tf_op jit(solution)/shard_map/ppermute | solution.py:61
  95.8 1.5 collective-permute-start.5
  97.4 1.3 collective-permute-start.30
  98.7 5.5 %collective-permute-done.8 = bf16[384,512]{1,0:T(8,128)(2,1)S(1)} collective-permute-done((bf16[384,512]{1,0:T(8,128)(2,1)S(1)}, bf16[384,512]{1,0:T(8,128)(2,1)S(1)}, u32[]{:S(2)}, u32[]{:S(2)}) %collective-permute-start.8) | collective-permute-done | bytes 393248 | tf_op jit(solution)/shard_map/ppermute | solution.py:61
  104.3 1.5 collective-permute-start.27
  105.8 1.5 collective-permute-start.13
  107.3 5.4 %collective-permute-done.30 = bf16[384,512]{1,0:T(8,128)(2,1)S(1)} collective-permute-done((bf16[384,512]{1,0:T(8,128)(2,1)S(1)}, bf16[384,512]{1,0:T(8,128)(2,1)S(1)}, u32[]{:S(2)}, u32[]{:S(2)}) %collective-permute-start.30) | collective-permute-done | bytes 393248 | tf_op jit(solution)/shard_map/ppermute | solution.py:61
  112.7 1.5 collective-permute-start.10
  114.3 5.2 %collective-permute-done.13 = bf16[384,512]{1,0:T(8,128)(2,1)S(1)} collective-permute-done((bf16[384,512]{1,0:T(8,128)(2,1)S(1)}, bf16[384,512]{1,0:T(8,128)(2,1)S(1)}, u32[]{:S(2)}, u32[]{:S(2)}) %collective-permute-start.13) | collective-permute-done | bytes 393248 | tf_op jit(solution)/shard_map/ppermute | solution.py:61
  119.5 1.5 collective-permute-start.32
  121.8 1.6 collective-permute-start.19
  124.0 7.5 %collective-permute-done.32 = bf16[384,512]{1,0:T(8,128)(2,1)S(1)} collective-permute-done((bf16[384,512]{1,0:T(8,128)(2,1)S(1)}, bf16[384,512]{1,0:T(8,128)(2,1)S(1)}, u32[]{:S(2)}, u32[]{:S(2)}) %collective-permute-start.32) | collective-permute-done | bytes 393248 | tf_op jit(solution)/shard_map/ppermute | solution.py:61
  131.6 1.5 collective-permute-start.21
  133.1 4.4 %collective-permute-done.15 = bf16[384,512]{1,0:T(8,128)(2,1)S(1)} collective-permute-done((bf16[384,512]{1,0:T(8,128)(2,1)S(1)}, bf16[384,512]{1,0:T(8,128)(2,1)S(1)}, u32[]{:S(2)}, u32[]{:S(2)}) %collective-permute-start.15) | collective-permute-done | bytes 393248 | tf_op jit(solution)/shard_map/ppermute | solution.py:61
  137.4 1.5 collective-permute-start.4
  139.5 13.0 %fusion.23 = (bf16[1,640,512]{2,0,1:T(2,128)(2,1)S(1)}, bf16[1,640,512]{2,0,1:T(2,128)(2,1)S(1)}, bf16[1,640,512]{2,0,1:T(2,128)(2,1)S(1)}, bf16[1,640,512]{2,0,...) fusion(s32[]{:T(128)S(6)} %select_n.200, bf16[8,320,512]{2,0,1:T(8,128)(2,1)S(1)} %bitcast.115, ...), kind=kLoop, calls=%fused_computation.54 | loop fusion | flops 7864320 | bytes 9175064 | tf_op jit(solution)/shard_map/concatenate | solution.py:149
  155.1 1.6 collective-permute-start.6
  158.0 11.2 %fusion.28 = (bf16[1,640,512]{2,0,1:T(2,128)(2,1)S(1)}, bf16[1,640,512]{2,0,1:T(2,128)(2,1)S(1)}) fusion(s32[]{:T(128)S(6)} %select_n.209, bf16[8,320,512]{2,0,1:T(8,128)(2,1)S(1)} %bitcast.116, bf16[8,320,512]{2,0,1:T(8,128)(2,1)} %collective-permute-done, s32[]{:T(128)S(6)} %select_n.211), kind=kLoop, calls=%fused_computation.59 | loop fusion | flops 2621440 | bytes 6553608 | tf_op jit(solution)/shard_map/concatenate | solution.py:149
  169.2 1.3 fusion.64
  171.4 5.1 %collective-permute-done.28 = bf16[128,512]{1,0:T(8,128)(2,1)S(1)} collective-permute-done((bf16[128,512]{1,0:T(8,128)(2,1)S(1)}, bf16[128,512]{1,0:T(8,128)(2,1)S(1)}, u32[]{:S(2)}, u32[]{:S(2)}) %collective-permute-start.28) | collective-permute-done | bytes 131104 | tf_op jit(solution)/shard_map/ppermute | solution.py:61
  177.7 5.2 %collective-permute-done.26 = bf16[128,512]{1,0:T(8,128)(2,1)S(1)} collective-permute-done((bf16[128,512]{1,0:T(8,128)(2,1)S(1)}, bf16[128,512]{1,0:T(8,128)(2,1)S(1)}, u32[]{:S(2)}, u32[]{:S(2)}) %collective-permute-start.26) | collective-permute-done | bytes 131104 | tf_op jit(solution)/shard_map/ppermute | solution.py:61
  183.7 1.6 collective-permute-start.33
  187.0 2.9 %collective-permute-done.33 = bf16[128,512]{1,0:T(8,128)(2,1)S(1)} collective-permute-done((bf16[128,512]{1,0:T(8,128)(2,1)S(1)}, bf16[128,512]{1,0:T(8,128)(2,1)S(1)}, u32[]{:S(2)}, u32[]{:S(2)}) %collective-permute-start.33) | collective-permute-done | bytes 131104 | tf_op jit(solution)/shard_map/ppermute | solution.py:61
  190.8 4.6 %collective-permute-done.31 = bf16[128,512]{1,0:T(8,128)(2,1)S(1)} collective-permute-done((bf16[128,512]{1,0:T(8,128)(2,1)S(1)}, bf16[128,512]{1,0:T(8,128)(2,1)S(1)}, u32[]{:S(2)}, u32[]{:S(2)}) %collective-permute-start.31) | collective-permute-done | bytes 131104 | tf_op jit(solution)/shard_map/ppermute | solution.py:61
  197.7 1.3 fusion.66
  199.0 2.1 collective-permute-start.14
  204.5 2.0 collective-permute-done.16
  208.6 1.0 collective-permute-done.17
  211.1 0.9 gather_fusion
  212.1 0.8 copy.36
  212.9 3.5 %all-to-all-start = ((bf16[16,80,128]{2,1,0:T(8,128)(2,1)}), bf16[16,80,128]{2,1,0:T(8,128)(2,1)S(1)}, u32[]{:S(2)}, u32[]{:S(2)}) async-start(bf16[16,80,128]{2,1,0:T(8,128)(2,1)} %bitcast.8), calls=%async_computation | async-start | bytes 655360 | tf_op jit(solution)/shard_map/all_to_all | solution.py:178
  217.4 0.7 gather_fusion.1
  218.2 0.8 copy.39
  219.0 8.4 %all-to-all-done = bf16[16,80,128]{2,1,0:T(8,128)(2,1)S(1)} async-done(((bf16[16,80,128]{2,1,0:T(8,128)(2,1)}), bf16[16,80,128]{2,1,0:T(8,128)(2,1)S(1)}, u32[]{:S(2)}, u32[]{:S(2)}) %all-to-all-start) | async-done | bytes 327712 | tf_op jit(solution)/shard_map/all_to_all | solution.py:178
  227.5 3.5 %all-to-all-start.1 = ((bf16[16,80,128]{2,1,0:T(8,128)(2,1)}), bf16[16,80,128]{2,1,0:T(8,128)(2,1)S(1)}, u32[]{:S(2)}, u32[]{:S(2)}) async-start(bf16[16,80,128]{2,1,0:T(8,128)(2,1)} %bitcast.14), calls=%async_computation.1 | async-start | bytes 655360 | tf_op jit(solution)/shard_map/all_to_all | solution.py:178
  231.7 0.9 collective-permute-done.35
  233.2 0.9 collective-permute-done.36
  234.2 7.9 %all-to-all-done.1 = bf16[16,80,128]{2,1,0:T(8,128)(2,1)S(1)} async-done(((bf16[16,80,128]{2,1,0:T(8,128)(2,1)}), bf16[16,80,128]{2,1,0:T(8,128)(2,1)S(1)}, u32[]{:S(2)}, u32[]{:S(2)}) %all-to-all-start.1) | async-done | bytes 327712 | tf_op jit(solution)/shard_map/all_to_all | solution.py:178
  242.4 0.9 maximum_bitcast_fusion
  (167 shorter events, 32.3 us)
Async XLA Ops:
  0.6 233.4 %copy-start = (bf16[8,4,128]{2,1,0:T(4,128)(2,1)S(1)}, bf16[8,4,128]{2,1,0:T(4,128)(2,1)}, u32[]{:S(2)}) copy-start(bf16[8,4,128]{2,1,0:T(4,128)(2,1)} %param.15) | copy-start | bytes 24580
  0.6 1.3 copy-start.4
  2.8 70.4 %collective-permute-start.20 = (bf16[384,512]{1,0:T(8,128)(2,1)}, bf16[384,512]{1,0:T(8,128)(2,1)S(1)}, u32[]{:S(2)}, u32[]{:S(2)}) collective-permute-start(bf16[384,512]{1,0:T(8,128)(2,1)} %slice.309), channel_id=1, source_target_pairs={{0,4},{1,5},{2,6},{3,7},{4,0},{5,1},{6,2},{7,3},{8,12},{9,13},{10,... | collective-permute-start | bytes 1179656 | tf_op jit(solution)/shard_map/ppermute | solution.py:61
  5.9 70.7 %collective-permute-start.24 = (bf16[384,512]{1,0:T(8,128)(2,1)}, bf16[384,512]{1,0:T(8,128)(2,1)}, u32[]{:S(2)}, u32[]{:S(2)}) collective-permute-start(bf16[384,512]{1,0:T(8,128)(2,1)} %slice.309), channel_id=1, source_target_pairs={{4,8},{5,9},{6,10},{7,11},{8,4},{9,5},{10,6},{11,7},{20,24},{21,25... | collective-permute-start | bytes 1179656 | tf_op jit(solution)/shard_map/ppermute | solution.py:61
  16.7 5.4 %copy-start.1 = (bf16[320,8,2,512]{3,2,1,0:T(2,128)(2,1)S(1)}, bf16[320,8,2,512]{3,2,1,0:T(2,128)(2,1)}, u32[]{:S(2)}) copy-start(bf16[320,8,2,512]{3,2,1,0:T(2,128)(2,1)} %reshape_reshape.3) | copy-start | bytes 15728644
  44.5 4.5 %copy-start.5 = (bf16[512,512]{1,0:T(8,128)(2,1)S(1)}, bf16[512,512]{1,0:T(8,128)(2,1)}, u32[]{:S(2)}) copy-start(bf16[512,512]{1,0:T(8,128)(2,1)} %param.9) | copy-start | bytes 1572868
  46.8 92.2 %collective-permute-start = (bf16[8,320,512]{2,0,1:T(8,128)(2,1)}, bf16[8,320,512]{2,0,1:T(8,128)(2,1)}, u32[]{:S(2)}, u32[]{:S(2)}) collective-permute-start(bf16[8,320,512]{2,0,1:T(8,128)(2,1)} %bitcast.108), channel_id=1, source_target_pairs={{0,1},{1,0},{2,3},{3,2},{4,5},{5,4},{6,7},{7,6},{8,9},{9,8},{10,11... | collective-permute-start | bytes 7864328 | tf_op jit(solution)/shard_map/ppermute | solution.py:61
  47.5 21.1 %collective-permute-start.18 = (bf16[256,512]{1,0:T(8,128)(2,1)}, bf16[256,512]{1,0:T(8,128)(2,1)}, u32[]{:S(2)}, u32[]{:S(2)}) collective-permute-start(bf16[256,512]{1,0:T(8,128)(2,1)} %slice.306), channel_id=1, source_target_pairs={{0,2},{1,3},{2,0},{3,1},{4,6},{5,7},{6,4},{7,5},{8,10},{9,11},{10,... | collective-permute-start | bytes 786440 | tf_op jit(solution)/shard_map/ppermute | solution.py:61
  49.2 14.7 %copy-start.2 = (bf16[512,512]{1,0:T(8,128)(2,1)}, bf16[512,512]{1,0:T(8,128)(2,1)S(1)}, u32[]{:S(2)}) copy-start(bf16[512,512]{1,0:T(8,128)(2,1)S(1)} %maximum_select_fusion) | copy-start | bytes 1572868
  50.0 24.0 %collective-permute-start.1 = (bf16[256,512]{1,0:T(8,128)(2,1)}, bf16[256,512]{1,0:T(8,128)(2,1)}, u32[]{:S(2)}, u32[]{:S(2)}) collective-permute-start(bf16[256,512]{1,0:T(8,128)(2,1)} %slice.277), channel_id=1, source_target_pairs={{0,2},{1,3},{2,0},{3,1},{4,6},{5,7},{6,4},{7,5},{8,10},{9,11},{10,... | collective-permute-start | bytes 786440 | tf_op jit(solution)/shard_map/ppermute | solution.py:61
  50.5 3.6 %copy-start.13 = (s32[8]{0:T(128)S(1)}, s32[8]{0:T(128)}, u32[]{:S(2)}) copy-start(s32[8]{0:T(128)} %param.12) | copy-start | bytes 100
  50.5 10.6 %copy-start.10 = (s32[2]{0:T(128)S(1)}, s32[2]{0:T(128)}, u32[]{:S(2)}) copy-start(s32[2]{0:T(128)} %param.11) | copy-start | bytes 28
  68.6 13.1 %collective-permute-start.3 = (bf16[384,512]{1,0:T(8,128)(2,1)}, bf16[384,512]{1,0:T(8,128)(2,1)S(1)}, u32[]{:S(2)}, u32[]{:S(2)}) collective-permute-start(bf16[384,512]{1,0:T(8,128)(2,1)} %slice.282), channel_id=1, source_target_pairs={{0,4},{1,5},{2,6},{3,7},{4,0},{5,1},{6,2},{7,3},{8,12},{9,13},{10,... | collective-permute-start | bytes 1179656 | tf_op jit(solution)/shard_map/ppermute | solution.py:61
  73.3 9.8 %collective-permute-start.7 = (bf16[384,512]{1,0:T(8,128)(2,1)}, bf16[384,512]{1,0:T(8,128)(2,1)S(1)}, u32[]{:S(2)}, u32[]{:S(2)}) collective-permute-start(bf16[384,512]{1,0:T(8,128)(2,1)} %slice.282), channel_id=1, source_target_pairs={{4,8},{5,9},{6,10},{7,11},{8,4},{9,5},{10,6},{11,7},{20,24},{21,25... | collective-permute-start | bytes 1179656 | tf_op jit(solution)/shard_map/ppermute | solution.py:61
  74.0 9.8 %collective-permute-start.22 = (bf16[256,512]{1,0:T(8,128)(2,1)S(1)}, bf16[256,512]{1,0:T(8,128)(2,1)S(1)}, u32[]{:S(2)}, u32[]{:S(2)}) collective-permute-start(bf16[256,512]{1,0:T(8,128)(2,1)S(1)} %slice.311), channel_id=1, source_target_pairs={{0,2},{1,3},{2,0},{3,1},{4,6},{5,7},{6,4},{7,5},{8,10},{9,11},{10,... | collective-permute-start | bytes 786440 | tf_op jit(solution)/shard_map/ppermute | solution.py:61
  76.6 20.8 %collective-permute-start.29 = (bf16[384,512]{1,0:T(8,128)(2,1)S(1)}, bf16[384,512]{1,0:T(8,128)(2,1)S(1)}, u32[]{:S(2)}, u32[]{:S(2)}) collective-permute-start(bf16[384,512]{1,0:T(8,128)(2,1)S(1)} %collective-permute-done.20), channel_id=1, source_target_pairs={{4,8},{5,9},{6,10},{7,11},{8,4},{9,5},{10,6},{11,7},{20,24},{21,25... | collective-permute-start | bytes 1179656 | tf_op jit(solution)/shard_map/ppermute | solution.py:61
  81.7 14.1 %collective-permute-start.25 = (bf16[384,512]{1,0:T(8,128)(2,1)}, bf16[384,512]{1,0:T(8,128)(2,1)S(1)}, u32[]{:S(2)}, u32[]{:S(2)}) collective-permute-start(bf16[384,512]{1,0:T(8,128)(2,1)} %collective-permute-done.24), channel_id=1, source_target_pairs={{4,0},{5,1},{6,2},{7,3},{8,12},{9,13},{10,14},{11,15},{20,16},{21,... | collective-permute-start | bytes 1179656 | tf_op jit(solution)/shard_map/ppermute | solution.py:61
  83.1 22.7 %collective-permute-start.12 = (bf16[384,512]{1,0:T(8,128)(2,1)S(1)}, bf16[384,512]{1,0:T(8,128)(2,1)S(1)}, u32[]{:S(2)}, u32[]{:S(2)}) collective-permute-start(bf16[384,512]{1,0:T(8,128)(2,1)S(1)} %collective-permute-done.3), channel_id=1, source_target_pairs={{4,8},{5,9},{6,10},{7,11},{8,4},{9,5},{10,6},{11,7},{20,24},{21,25... | collective-permute-start | bytes 1179656 | tf_op jit(solution)/shard_map/ppermute | solution.py:61
  83.8 20.4 %collective-permute-start.8 = (bf16[384,512]{1,0:T(8,128)(2,1)S(1)}, bf16[384,512]{1,0:T(8,128)(2,1)S(1)}, u32[]{:S(2)}, u32[]{:S(2)}) collective-permute-start(bf16[384,512]{1,0:T(8,128)(2,1)S(1)} %collective-permute-done.7), channel_id=1, source_target_pairs={{4,0},{5,1},{6,2},{7,3},{8,12},{9,13},{10,14},{11,15},{20,16},{21,... | collective-permute-start | bytes 1179656 | tf_op jit(solution)/shard_map/ppermute | solution.py:61
  95.8 25.2 %collective-permute-start.5 = (bf16[256,512]{1,0:T(8,128)(2,1)S(1)}, bf16[256,512]{1,0:T(8,128)(2,1)S(1)}, u32[]{:S(2)}, u32[]{:S(2)}) collective-permute-start(bf16[256,512]{1,0:T(8,128)(2,1)S(1)} %slice.286), channel_id=1, source_target_pairs={{0,2},{1,3},{2,0},{3,1},{4,6},{5,7},{6,4},{7,5},{8,10},{9,11},{10,... | collective-permute-start | bytes 786440 | tf_op jit(solution)/shard_map/ppermute | solution.py:61
  97.4 15.3 %collective-permute-start.30 = (bf16[384,512]{1,0:T(8,128)(2,1)S(1)}, bf16[384,512]{1,0:T(8,128)(2,1)S(1)}, u32[]{:S(2)}, u32[]{:S(2)}) collective-permute-start(bf16[384,512]{1,0:T(8,128)(2,1)S(1)} %collective-permute-done.29), channel_id=1, source_target_pairs={{4,0},{5,1},{6,2},{7,3},{8,12},{9,13},{10,14},{11,15},{20,16},{21,... | collective-permute-start | bytes 1179656 | tf_op jit(solution)/shard_map/ppermute | solution.py:61
  104.3 17.5 %collective-permute-start.27 = (bf16[384,512]{1,0:T(8,128)(2,1)S(1)}, bf16[384,512]{1,0:T(8,128)(2,1)S(1)}, u32[]{:S(2)}, u32[]{:S(2)}) collective-permute-start(bf16[384,512]{1,0:T(8,128)(2,1)S(1)} %broadcast_select_fusion.4), channel_id=1, source_target_pairs={{0,2},{1,3},{2,0},{3,1},{4,6},{5,7},{6,4},{7,5},{8,10},{9,11},{10,... | collective-permute-start | bytes 1179656 | tf_op jit(solution)/shard_map/ppermute | solution.py:61
  105.8 13.7 %collective-permute-start.13 = (bf16[384,512]{1,0:T(8,128)(2,1)S(1)}, bf16[384,512]{1,0:T(8,128)(2,1)S(1)}, u32[]{:S(2)}, u32[]{:S(2)}) collective-permute-start(bf16[384,512]{1,0:T(8,128)(2,1)S(1)} %collective-permute-done.12), channel_id=1, source_target_pairs={{4,0},{5,1},{6,2},{7,3},{8,12},{9,13},{10,14},{11,15},{20,16},{21,... | collective-permute-start | bytes 1179656 | tf_op jit(solution)/shard_map/ppermute | solution.py:61
  112.7 10.7 %collective-permute-start.10 = (bf16[384,512]{1,0:T(8,128)(2,1)S(1)}, bf16[384,512]{1,0:T(8,128)(2,1)S(1)}, u32[]{:S(2)}, u32[]{:S(2)}) collective-permute-start(bf16[384,512]{1,0:T(8,128)(2,1)S(1)} %broadcast_select_fusion.6), channel_id=1, source_target_pairs={{0,2},{1,3},{2,0},{3,1},{4,6},{5,7},{6,4},{7,5},{8,10},{9,11},{10,... | collective-permute-start | bytes 1179656 | tf_op jit(solution)/shard_map/ppermute | solution.py:61
  119.5 12.1 %collective-permute-start.32 = (bf16[384,512]{1,0:T(8,128)(2,1)S(1)}, bf16[384,512]{1,0:T(8,128)(2,1)S(1)}, u32[]{:S(2)}, u32[]{:S(2)}) collective-permute-start(bf16[384,512]{1,0:T(8,128)(2,1)S(1)} %broadcast_select_fusion.3), channel_id=1, source_target_pairs={{0,2},{1,3},{2,0},{3,1},{4,6},{5,7},{6,4},{7,5},{8,10},{9,11},{10,... | collective-permute-start | bytes 1179656 | tf_op jit(solution)/shard_map/ppermute | solution.py:61
  121.1 16.4 %collective-permute-start.15 = (bf16[384,512]{1,0:T(8,128)(2,1)S(1)}, bf16[384,512]{1,0:T(8,128)(2,1)S(1)}, u32[]{:S(2)}, u32[]{:S(2)}) collective-permute-start(bf16[384,512]{1,0:T(8,128)(2,1)S(1)} %broadcast_select_fusion.5), channel_id=1, source_target_pairs={{0,2},{1,3},{2,0},{3,1},{4,6},{5,7},{6,4},{7,5},{8,10},{9,11},{10,... | collective-permute-start | bytes 1179656 | tf_op jit(solution)/shard_map/ppermute | solution.py:61
  121.8 61.9 %collective-permute-start.19 = (bf16[256,512]{1,0:T(8,128)(2,1)S(1)}, bf16[256,512]{1,0:T(8,128)(2,1)S(1)}, u32[]{:S(2)}, u32[]{:S(2)}) collective-permute-start(bf16[256,512]{1,0:T(8,128)(2,1)S(1)} %pad_maximum_fusion.2), channel_id=1, source_target_pairs={{0,16},{1,17},{2,18},{3,19},{4,20},{5,21},{6,22},{7,23},{8,24},{9,... | collective-permute-start | bytes 786440 | tf_op jit(solution)/shard_map/ppermute | solution.py:61
  123.4 79.2 %collective-permute-start.2 = (bf16[256,512]{1,0:T(8,128)(2,1)S(1)}, bf16[256,512]{1,0:T(8,128)(2,1)S(1)}, u32[]{:S(2)}, u32[]{:S(2)}) collective-permute-start(bf16[256,512]{1,0:T(8,128)(2,1)S(1)} %pad_maximum_fusion), channel_id=1, source_target_pairs={{0,16},{1,17},{2,18},{3,19},{4,20},{5,21},{6,22},{7,23},{8,24},{9,... | collective-permute-start | bytes 786440 | tf_op jit(solution)/shard_map/ppermute | solution.py:61
  131.6 38.9 %collective-permute-start.21 = (bf16[128,512]{1,0:T(8,128)(2,1)S(1)}, bf16[128,512]{1,0:T(8,128)(2,1)S(1)}, u32[]{:S(2)}, u32[]{:S(2)}) collective-permute-start(bf16[128,512]{1,0:T(8,128)(2,1)S(1)} %slice.310), channel_id=1, source_target_pairs={{0,16},{1,17},{2,18},{3,19},{4,20},{5,21},{6,22},{7,23},{8,24},{9,... | collective-permute-start | bytes 393224 | tf_op jit(solution)/shard_map/ppermute | solution.py:61
  137.4 64.0 %collective-permute-start.4 = (bf16[128,512]{1,0:T(8,128)(2,1)S(1)}, bf16[128,512]{1,0:T(8,128)(2,1)S(1)}, u32[]{:S(2)}, u32[]{:S(2)}) collective-permute-start(bf16[128,512]{1,0:T(8,128)(2,1)S(1)} %slice.284), channel_id=1, source_target_pairs={{0,16},{1,17},{2,18},{3,19},{4,20},{5,21},{6,22},{7,23},{8,24},{9,... | collective-permute-start | bytes 393224 | tf_op jit(solution)/shard_map/ppermute | solution.py:61
  138.9 16.2 %collective-permute-start.23 = (bf16[256,512]{1,0:T(8,128)(2,1)S(1)}, bf16[256,512]{1,0:T(8,128)(2,1)S(1)}, u32[]{:S(2)}, u32[]{:S(2)}) collective-permute-start(bf16[256,512]{1,0:T(8,128)(2,1)S(1)} %pad_maximum_fusion.3), channel_id=1, source_target_pairs={{0,16},{1,17},{2,18},{3,19},{4,20},{5,21},{6,22},{7,23},{8,24},{9,... | collective-permute-start | bytes 786440 | tf_op jit(solution)/shard_map/ppermute | solution.py:61
  152.5 1.0 copy-start.3
  155.1 43.9 %collective-permute-start.6 = (bf16[256,512]{1,0:T(8,128)(2,1)S(1)}, bf16[256,512]{1,0:T(8,128)(2,1)S(1)}, u32[]{:S(2)}, u32[]{:S(2)}) collective-permute-start(bf16[256,512]{1,0:T(8,128)(2,1)S(1)} %pad_maximum_fusion.1), channel_id=1, source_target_pairs={{0,16},{1,17},{2,18},{3,19},{4,20},{5,21},{6,22},{7,23},{8,24},{9,... | collective-permute-start | bytes 786440 | tf_op jit(solution)/shard_map/ppermute | solution.py:61
  170.5 6.0 %collective-permute-start.28 = (bf16[128,512]{1,0:T(8,128)(2,1)S(1)}, bf16[128,512]{1,0:T(8,128)(2,1)S(1)}, u32[]{:S(2)}, u32[]{:S(2)}) collective-permute-start(bf16[128,512]{1,0:T(8,128)(2,1)S(1)} %slice.315), channel_id=1, source_target_pairs={{0,16},{1,17},{2,18},{3,19},{4,20},{5,21},{6,22},{7,23},{8,24},{9,... | collective-permute-start | bytes 393224 | tf_op jit(solution)/shard_map/ppermute | solution.py:61
  176.5 6.4 %collective-permute-start.26 = (bf16[128,512]{1,0:T(8,128)(2,1)S(1)}, bf16[128,512]{1,0:T(8,128)(2,1)S(1)}, u32[]{:S(2)}, u32[]{:S(2)}) collective-permute-start(bf16[128,512]{1,0:T(8,128)(2,1)S(1)} %slice.314), channel_id=1, source_target_pairs={{0,16},{1,17},{2,18},{3,19},{4,20},{5,21},{6,22},{7,23},{8,24},{9,... | collective-permute-start | bytes 393224 | tf_op jit(solution)/shard_map/ppermute | solution.py:61
  182.9 19.0 %collective-permute-start.9 = (bf16[128,512]{1,0:T(8,128)(2,1)S(1)}, bf16[128,512]{1,0:T(8,128)(2,1)S(1)}, u32[]{:S(2)}, u32[]{:S(2)}) collective-permute-start(bf16[128,512]{1,0:T(8,128)(2,1)S(1)} %slice.292), channel_id=1, source_target_pairs={{0,16},{1,17},{2,18},{3,19},{4,20},{5,21},{6,22},{7,23},{8,24},{9,... | collective-permute-start | bytes 393224 | tf_op jit(solution)/shard_map/ppermute | solution.py:61
  183.7 6.1 %collective-permute-start.33 = (bf16[128,512]{1,0:T(8,128)(2,1)S(1)}, bf16[128,512]{1,0:T(8,128)(2,1)S(1)}, u32[]{:S(2)}, u32[]{:S(2)}) collective-permute-start(bf16[128,512]{1,0:T(8,128)(2,1)S(1)} %slice.317), channel_id=1, source_target_pairs={{0,16},{1,17},{2,18},{3,19},{4,20},{5,21},{6,22},{7,23},{8,24},{9,... | collective-permute-start | bytes 393224 | tf_op jit(solution)/shard_map/ppermute | solution.py:61
  189.8 5.6 %collective-permute-start.31 = (bf16[128,512]{1,0:T(8,128)(2,1)S(1)}, bf16[128,512]{1,0:T(8,128)(2,1)S(1)}, u32[]{:S(2)}, u32[]{:S(2)}) collective-permute-start(bf16[128,512]{1,0:T(8,128)(2,1)S(1)} %slice.316), channel_id=1, source_target_pairs={{0,16},{1,17},{2,18},{3,19},{4,20},{5,21},{6,22},{7,23},{8,24},{9,... | collective-permute-start | bytes 393224 | tf_op jit(solution)/shard_map/ppermute | solution.py:61
  195.4 6.9 %collective-permute-start.11 = (bf16[128,512]{1,0:T(8,128)(2,1)S(1)}, bf16[128,512]{1,0:T(8,128)(2,1)S(1)}, u32[]{:S(2)}, u32[]{:S(2)}) collective-permute-start(bf16[128,512]{1,0:T(8,128)(2,1)S(1)} %slice.295), channel_id=1, source_target_pairs={{0,16},{1,17},{2,18},{3,19},{4,20},{5,21},{6,22},{7,23},{8,24},{9,... | collective-permute-start | bytes 393224 | tf_op jit(solution)/shard_map/ppermute | solution.py:61
  199.0 5.2 %collective-permute-start.14 = (bf16[128,512]{1,0:T(8,128)(2,1)S(1)}, bf16[128,512]{1,0:T(8,128)(2,1)S(1)}, u32[]{:S(2)}, u32[]{:S(2)}) collective-permute-start(bf16[128,512]{1,0:T(8,128)(2,1)S(1)} %slice.298), channel_id=1, source_target_pairs={{0,16},{1,17},{2,18},{3,19},{4,20},{5,21},{6,22},{7,23},{8,24},{9,... | collective-permute-start | bytes 393224 | tf_op jit(solution)/shard_map/ppermute | solution.py:61
  201.4 5.0 %collective-permute-start.16 = (bf16[128,512]{1,0:T(8,128)(2,1)S(1)}, bf16[128,512]{1,0:T(8,128)(2,1)S(1)}, u32[]{:S(2)}, u32[]{:S(2)}) collective-permute-start(bf16[128,512]{1,0:T(8,128)(2,1)S(1)} %slice.301), channel_id=1, source_target_pairs={{0,16},{1,17},{2,18},{3,19},{4,20},{5,21},{6,22},{7,23},{8,24},{9,... | collective-permute-start | bytes 393224 | tf_op jit(solution)/shard_map/ppermute | solution.py:61
  201.9 6.7 %collective-permute-start.34 = (f32[320,512]{1,0:T(8,128)S(1)}, f32[320,512]{1,0:T(8,128)S(1)}, u32[]{:S(2)}, u32[]{:S(2)}) collective-permute-start(f32[320,512]{1,0:T(8,128)S(1)} %slice.319), channel_id=1, source_target_pairs={{0,1},{1,0},{2,3},{3,2},{4,5},{5,4},{6,7},{7,6},{8,9},{9,8},{10,11... | collective-permute-start | bytes 1966088 | tf_op jit(solution)/shard_map/ppermute | solution.py:61
  207.4 0.6 copy-start.9
  207.4 0.7 copy-start.11
  207.4 0.7 copy-start.7
  207.4 0.7 copy-start.12
  207.4 0.8 copy-start.8
  207.5 2.2 collective-permute-start.17
  211.1 5.4 %copy-start.6 = (f32[1,4,8,128]{3,1,2,0:T(4,128)S(1)}, f32[1,4,8,128]{3,1,2,0:T(4,128)}, u32[]{:S(2)}) copy-start(f32[1,4,8,128]{3,1,2,0:T(4,128)} %convert_bitcast_fusion) | copy-start | bytes 49156
  212.9 14.6 %all-to-all-start = ((bf16[16,80,128]{2,1,0:T(8,128)(2,1)}), bf16[16,80,128]{2,1,0:T(8,128)(2,1)S(1)}, u32[]{:S(2)}, u32[]{:S(2)}) async-start(bf16[16,80,128]{2,1,0:T(8,128)(2,1)} %bitcast.8), calls=%async_computation | async-start | bytes 655360 | tf_op jit(solution)/shard_map/all_to_all | solution.py:178
  227.5 14.6 %all-to-all-start.1 = ((bf16[16,80,128]{2,1,0:T(8,128)(2,1)}), bf16[16,80,128]{2,1,0:T(8,128)(2,1)S(1)}, u32[]{:S(2)}, u32[]{:S(2)}) async-start(bf16[16,80,128]{2,1,0:T(8,128)(2,1)} %bitcast.14), calls=%async_computation.1 | async-start | bytes 655360 | tf_op jit(solution)/shard_map/all_to_all | solution.py:178
  231.4 1.2 collective-permute-start.35
  232.8 1.2 collective-permute-start.36
  242.3 1.2 collective-permute-start.37

commit v2 on v1

--- a/solution.py
+++ b/solution.py
@@ -1,6 +1,10 @@
+import functools
+
 import jax
 import jax.numpy as jnp
 from jax import lax
+from jax.experimental import pallas as pl
+from jax.experimental.pallas import tpu as pltpu
 from jax.sharding import PartitionSpec as P
 
 HEAD_SIZE = 128
@@ -91,7 +95,142 @@
     return jnp.where(flag, jnp.concatenate(parts[::-1], axis), block)
 
 
-def gathered_blocks(weight, z, y, g):
+def small_cost():
+    return pl.CostEstimate(flops=1000, bytes_accessed=1000, transcendentals=0)
+
+
+def whole_block(array):
+    return pl.BlockSpec(array.shape, lambda *_: (0,) * array.ndim)
+
+
+def prepare_kernel(place, rows_in, mine, other):
+    blocks, _, depth = mine.shape
+    quarter = depth // 4
+    wide = rows_in[...].astype(jnp.float32)
+    scale = lax.rsqrt(jnp.mean(wide * wide, -1, keepdims=True) + 1e-05)
+    for g in range(2):
+        for core in range(2):
+
+            @pl.when((place[0] == g) & (place[1] == core))
+            def _():
+                for j in range(blocks):
+                    for c in range(2):
+                        target = mine if c == core else other
+                        for q in range(4):
+                            first = (2 * j + c) * depth + q * quarter
+                            part = rows_in[:, first : first + quarter].astype(jnp.float32)
+                            spot = 3 - q if g else q
+                            target[j, :, spot * quarter : (spot + 1) * quarter] = (
+                                part * scale
+                            ).astype(jnp.bfloat16)
+
+
+def prepared(flat, group_id, core, blocks):
+    rows, width = flat.shape
+    depth = width // (2 * blocks)
+    tile = 64 if rows % 64 == 0 else rows
+    out = jax.ShapeDtypeStruct((blocks, rows, depth), jnp.bfloat16)
+    spec = pl.BlockSpec((blocks, tile, depth), lambda i, place: (0, i, 0))
+    return pl.pallas_call(
+        prepare_kernel,
+        grid_spec=pltpu.PrefetchScalarGridSpec(
+            num_scalar_prefetch=1,
+            grid=(rows // tile,),
+            in_specs=[pl.BlockSpec((tile, width), lambda i, place: (i, 0))],
+            out_specs=[spec, spec],
+        ),
+        out_shape=[out, out],
+        compiler_params=pltpu.CompilerParams(vmem_limit_bytes=32 << 20),
+        cost_estimate=small_cost(),
+        name="normed_halves",
+    )(jnp.stack([group_id, core]).astype(jnp.int32), flat)
+
+
+def product_kernel(count_near, has_total, which, *refs):
+    left = refs[:4]
+    pieces = [ref[...] for ref in refs[4 : -2 - 2 * has_total]]
+    near = jnp.concatenate(pieces[:count_near], 0) if count_near > 1 else pieces[0]
+    far = jnp.concatenate(pieces[count_near:], 0)
+    for half in range(2):
+        total = jnp.dot(left[2 * half][0], near, preferred_element_type=jnp.float32)
+        total += jnp.dot(left[2 * half + 1][0], far, preferred_element_type=jnp.float32)
+        if has_total:
+            total += refs[half - 4][...]
+        refs[half - 2][...] = total
+
+
+def product(which, mine, other, near, far, totals):
+    _, rows, depth = mine.shape
+    columns = near[0].shape[1]
+    operands = [*near, *far, *totals]
+    left_specs = [
+        pl.BlockSpec((1, rows, depth), functools.partial(lambda k, _, which: (which[k], 0, 0), k))
+        for k in (0, 1)
+    ]
+    out = jax.ShapeDtypeStruct((rows, columns), jnp.float32)
+    first_total = 1 + 4 + len(near) + len(far)
+    return pl.pallas_call(
+        functools.partial(product_kernel, len(near), len(totals) // 2),
+        grid_spec=pltpu.PrefetchScalarGridSpec(
+            num_scalar_prefetch=1,
+            grid=(1,),
+            in_specs=left_specs * 2 + [whole_block(piece) for piece in operands],
+            out_specs=[whole_block(out)] * 2,
+        ),
+        out_shape=[out, out],
+        input_output_aliases={first_total + i: i for i in range(len(totals))},
+        compiler_params=pltpu.CompilerParams(vmem_limit_bytes=32 << 20),
+        cost_estimate=small_cost(),
+        name="add_product",
+    )(which, mine, mine, other, other, *operands)
+
+
+def rows_kernel(rotated, place, lengths, owner, *refs):
+    out, scratch = refs[-2:]
+    total, came = refs[:2]
+    count_requests, count_rows = lengths.shape[0], scratch.shape[0]
+    first = place[0] * count_rows
+    index = first + lax.broadcasted_iota(jnp.int32, scratch.shape, 0)
+    for r in range(count_requests):
+        live = index < lengths[r]
+        for h in range(KEY_VALUE_HEADS):
+            area = (
+                slice(r * count_rows, (r + 1) * count_rows),
+                slice(h * HEAD_SIZE, (h + 1) * HEAD_SIZE),
+            )
+            rows = total[area] + came[area]
+            if rotated:
+                turned = jnp.concatenate([rows[:, HEAD_SIZE // 2 :], rows[:, : HEAD_SIZE // 2]], 1)
+                rows = rows * refs[2][...] + turned * refs[3][...]
+            scratch[...] = jnp.where(live, rows, 0.0)
+            peer = owner[r * KEY_VALUE_HEADS + h]
+            for b in range(2):
+                picked = scratch[pl.ds(b, count_rows // 2, stride=2), :]
+                out[peer * 2 + b] = picked.astype(jnp.bfloat16)
+
+
+def outgoing_rows(total, came, place, lengths, owner, turn):
+    count_rows = total.shape[0] // lengths.shape[0]
+    operands = [total, came, *turn]
+    peers = owner.shape[0] * 2
+    out = jax.ShapeDtypeStruct((peers, count_rows // 2, HEAD_SIZE), jnp.bfloat16)
+    return pl.pallas_call(
+        functools.partial(rows_kernel, bool(turn)),
+        grid_spec=pltpu.PrefetchScalarGridSpec(
+            num_scalar_prefetch=3,
+            grid=(1,),
+            in_specs=[whole_block(x) for x in operands],
+            out_specs=whole_block(out),
+            scratch_shapes=[pltpu.VMEM((count_rows, HEAD_SIZE), jnp.float32)],
+        ),
+        out_shape=out,
+        compiler_params=pltpu.CompilerParams(vmem_limit_bytes=32 << 20),
+        cost_estimate=small_cost(),
+        name="cache_rows",
+    )(place, lengths, owner, *operands)
+
+
+def planned_totals(weight, mine, other, z, y, g):
     quarter = weight.shape[0] // 4
     own = mirrored(weight, 0, g == 1)
     is_end = (z == 0) | (z == 3)
@@ -104,19 +243,20 @@
     slot_b = jnp.where(is_end, end_b, mid_b)
     slot_c = jnp.where(is_end, end_c, mid_c)
     z_a, z_b, z_c = z ^ 1, jnp.where(z < 2, 2, 1), jnp.where(z < 2, 3, 0)
-    pieces = [(z, y, 0, own)]
-    for zz, block, share in ((z, main, 2), (z_a, near, 2), (z_b, slot_b, 3), (z_c, slot_c, 3)):
-        if block is not main:
-            pieces.append((zz, y, 0, block))
-            pieces.append((zz, y, 3 * quarter, moved(block[:quarter], to_group)))
+    totals = []
+    for zz, block, share in ((z, own, 2), (z_a, near, 2), (z_b, slot_b, 3), (z_c, slot_c, 3)):
+        here = [block]
+        if block is not own:
+            here.append(moved(block[:quarter], to_group))
         across = moved(block[: share * quarter], to_row)
-        pieces.append((zz, 1 - y, 0, across))
         if share == 2:
             onward = jnp.concatenate([across[quarter:], across[:quarter]], 0)
         else:
             onward = across[:quarter]
-        pieces.append((zz, 1 - y, share * quarter, moved(onward, to_group)))
-    return pieces
+        there = [across, moved(onward, to_group)]
+        which = jnp.stack([zz * 2 + y, zz * 2 + 1 - y]).astype(jnp.int32)
+        totals = product(which, mine, other, here, there, totals)
+    return totals
 
 
 def body(hidden, key_weight, value_weight, lengths, owner, dec_query, dec_key, dec_value):
@@ -132,34 +272,20 @@
     positions = device_id * count_rows + jnp.arange(count_rows, dtype=jnp.int32)
     total_rows = count_requests * count_rows
     flat = hidden.reshape(total_rows, width)
-    widened = flat.astype(jnp.float32)
-    row_scale = lax.rsqrt(jnp.mean(widened * widened, -1, keepdims=True) + 1e-05)
-
     if planned:
         core = device_id % 2
         z, y = device_id // 4, device_id // 2 % 2
-        blocks = seq // 2
-        depth = width // seq
-        split_cols = flat.reshape(total_rows, blocks, 2, depth)
-        ordered = mirrored(split_cols, 3, group_id == 1)
-        mine = jnp.where(core == 0, ordered[:, :, 0], ordered[:, :, 1])
-        other = jnp.where(core == 0, ordered[:, :, 1], ordered[:, :, 0])
-        mine = jnp.transpose(mine, (1, 0, 2))
-        other = moved(jnp.transpose(other, (1, 0, 2)), to_core)
-        left = jnp.concatenate([mine, other], 1)
-
-        def project(weight):
-            total = jnp.zeros((2 * total_rows, weight.shape[1]), jnp.float32)
-            for zz, yy, first, piece in gathered_blocks(weight, z, y, group_id):
-                part = lax.dynamic_index_in_dim(left, zz * 2 + yy, 0, keepdims=False)
-                part = part[:, first : first + piece.shape[0]]
-                total = total + jnp.dot(part, piece, preferred_element_type=jnp.float32)
-            return total[:total_rows] + moved(total[total_rows:], to_core)
+        mine, other = prepared(flat, group_id, core, seq // 2)
+        other = moved(other, to_core)
     else:
+        widened = flat.astype(jnp.float32)
+        normed = (
+            widened * lax.rsqrt(jnp.mean(widened * widened, -1, keepdims=True) + 1e-05)
+        ).astype(jnp.bfloat16)
 
         def project(weight):
             whole = lax.all_gather(weight, "seq", axis=0, tiled=True)
-            return jnp.dot(flat, whole, preferred_element_type=jnp.float32)
+            return jnp.dot(normed, whole, preferred_element_type=jnp.float32)
 
     pair_ids = jnp.arange(decode_peers, dtype=jnp.int32)
     matches = owner[None, :] == pair_ids[:, None]
@@ -177,13 +303,30 @@
         )
         return lax.all_to_all(outgoing, "seq", split_axis=0, concat_axis=1, tiled=True)[0]
 
-    shape = (count_requests, count_rows, KEY_VALUE_HEADS, HEAD_SIZE)
-    unrotated_key = (project(key_weight) * row_scale).reshape(shape)
     cosine, sine_part = rope_table(positions, HEAD_SIZE)
-    key_rows = rotate(unrotated_key, cosine[:, None, :], sine_part[:, None, :]).astype(jnp.bfloat16)
-    cache_keys = handed_over(key_rows)
-    value_rows = (project(value_weight) * row_scale).astype(jnp.bfloat16).reshape(shape)
-    cache_values = handed_over(value_rows)
+    if planned:
+        turn = (
+            jnp.concatenate([cosine, cosine], 1),
+            jnp.concatenate([-sine_part, sine_part], 1),
+        )
+        place = device_id.astype(jnp.int32).reshape(1)
+
+        def cached(weight, turn):
+            total, came = planned_totals(weight, mine, other, z, y, group_id)
+            came = moved(came, to_core)
+            outgoing = outgoing_rows(total, came, place, lengths, owner, turn)
+            return lax.all_to_all(outgoing, "seq", split_axis=0, concat_axis=1, tiled=True)[0]
+
+        cache_keys = cached(key_weight, turn)
+        cache_values = cached(value_weight, ())
+    else:
+        shape = (count_requests, count_rows, KEY_VALUE_HEADS, HEAD_SIZE)
+        unrotated_key = project(key_weight).reshape(shape)
+        key_rows = rotate(
+            unrotated_key, cosine[:, None, :], sine_part[:, None, :]
+        ).astype(jnp.bfloat16)
+        cache_keys = handed_over(key_rows)
+        cache_values = handed_over(project(value_weight).astype(jnp.bfloat16).reshape(shape))
     slot_count = cache_keys.shape[0]
     decode_peer = device_id // split_point
     block = device_id % split_point

time: 245 us -> 174 us (0.71)
  other arithmetic: 61.4 us -> 13.6 us
  Pallas kernels: 0 us -> 37.1 us
  waiting for transfers between devices: 82.3 us -> 53.8 us
  local copies, waits for them, and re-layouts: 34.2 us -> 17.4 us
  matrix products: 15.4 us -> 1.02 us
    pallas_call x0 -> x11, Pallas kernels: none -> 37.1 us  [the longest x8 28.3 us: product(): pl.pallas_call(functools.partial(product_kernel, len(near), len(totals) /...]
    ppermute x35, waiting for transfers between devices: 64 us -> 35.4 us  [moved(): return lax.ppermute(block, ('groups', 'seq'), route)]
    concatenate x6 -> x5, other arithmetic: 24.2 us -> 0.18 us  [the longest x1 0.11 us: body(): jnp.concatenate([cosine, cosine], 1)]
    dot_general x30 -> x0, matrix products: 14.4 us -> none  [project(): total = total + jnp.dot(part, piece, preferred_element_type=jnp.float32)]
    select_n x7 -> x4, other arithmetic: 13.7 us -> 0.2 us  [the longest x2 0.11 us: planned_totals(): slot_c = jnp.where(is_end, end_c, mid_c)]
    another operation x1 -> x0, local copies, waits for them, and re-layouts: 9.45 us -> none  [body(): split_cols = flat.reshape(total_rows, blocks, 2, depth)]
    select_n x3 -> x2, other arithmetic: 9.39 us -> 1.32 us  [mirrored(): return jnp.where(flag, jnp.concatenate(parts[::-1], axis), block)]
    slice x3 -> x2, local copies, waits for them, and re-layouts: 6.62 us -> 1.17 us  [mirrored(): lax.slice_in_dim(block, i * quarter, (i + 1) * quarter, axis=axis)]
  transfers between devices with their start and end apart: 40 -> 40, of which waited for: 18 -> 13; matrix products, arithmetic and copies ran while one was open for 42% -> 11% of each run, Pallas kernels for 0% -> 21%
where the time goes in v2:
time: 174 us; the launch traced here: 173 us
  waiting for transfers between devices  53.8 us (31%)
  starting transfers between devices  46.7 us (27%)
  Pallas kernels  37.1 us (21%)
  local copies, waits for them, and re-layouts  17.4 us (10%)
  other arithmetic  13.6 us (8%)
  between operations  3.64 us (2%)
    ppermute x35, starting transfers between devices, moved(): return lax.ppermute(block, ('groups', 'seq'), route)  38.9 us
    ppermute x35, waiting for transfers between devices, moved(): return lax.ppermute(block, ('groups', 'seq'), route)  35.4 us
    pallas_call x8, Pallas kernels, product(): pl.pallas_call(functools.partial(product_kernel, len(near), len(totals) /...  28.3 us
    all_to_all x2, waiting for transfers between devices, cached(): lax.all_to_all(outgoing, 'seq', split_axis=0, concat_axis=1, tiled=True)[0]  16.4 us
    unnamed x88, local copies, waits for them, and re-layouts  8.31 us
    all_to_all x2, starting transfers between devices, cached(): lax.all_to_all(outgoing, 'seq', split_axis=0, concat_axis=1, tiled=True)[0]  7.09 us
    pallas_call x1, Pallas kernels, prepared(): pl.pallas_call(prepare_kernel, grid_spec=pltpu.PrefetchScalarGridSpec(num...  4.59 us
    pallas_call x2, Pallas kernels, outgoing_rows(): pl.pallas_call(functools.partial(rows_kernel, bool(turn)), grid_spec=pltp...  4.2 us
  transfers between devices with their start and end apart: 40, of which 13 were waited for; matrix products, arithmetic and copies ran while one was open for 11% of the time, Pallas kernels for 21%

profile of v2, /device:TPU:0, one launch (start us, length us, event | category | flops | bytes accessed | tf_op | source)
XLA Modules:
  0.0 173.3 jit_solution(11265647205330652175)
XLA Ops:
  0.7 1.1 fusion.23
  1.8 1.2 maximum_select_fusion.refs_4_
  3.0 0.8 slice.144
  3.8 3.0 %collective-permute-start.1 = (bf16[384,512]{1,0:T(8,128)(2,1)}, bf16[384,512]{1,0:T(8,128)(2,1)S(1)}, u32[]{:S(2)}, u32[]{:S(2)}) collective-permute-start(bf16[384,512]{1,0:T(8,128)(2,1)} %slice.144), channel_id=1, source_target_pairs={{0,4},{1,5},{2,6},{3,7},{4,0},{5,1},{6,2},{7,3},{8,12},{9,13},{10,... | collective-permute-start | bytes 1179656 | tf_op jit(solution)/shard_map/ppermute | solution.py:65
  6.8 1.4 collective-permute-start.7
  8.3 2.5 %copy-done.7 = bf16[2,160,8192]{2,1,0:T(8,128)(2,1)S(1)} copy-done((bf16[2,160,8192]{2,1,0:T(8,128)(2,1)S(1)}, bf16[2,160,8192]{2,1,0:T(8,128)(2,1)}, u32[]{:S(2)}) %copy-start.7) | copy-done | bytes 5242904
  10.8 4.6 %normed_halves.1 = (bf16[8,320,512]{2,1,0:T(8,128)(2,1)S(1)}, bf16[8,320,512]{2,1,0:T(8,128)(2,1)}) custom-call(s32[2]{0:T(128)S(1)} %pad_add_fusion.1.place, bf16[320,8192]{1,0:T(8,128)(2,1)S(1)} %bitcast.47), custom_call_target="tpu_custom_call" | custom-call | flops 1000 | bytes 1000 | tf_op jit(solution)/shard_map/normed_halves/pallas_call | solution.py:134
  15.4 0.7 slice.153
  16.1 1.5 collective-permute-start.15
  17.9 0.8 slice.165
  20.9 1.7 %fusion.6 = (f32[160,64]{1,0:T(8,128)}, f32[160,64]{1,0:T(8,128)}, f32[160,64]{1,0:T(8,128)}) fusion(f32[64]{0:T(128)} %multiply_power_fusion, f32[160]{0:T(256)} %add_convert_fusion.2), kind=kLoop, calls=%fused_computation.26 | loop fusion | flops 20480 | bytes 123776 | tf_op jit(solution)/shard_map/neg | solution.py:310
  22.6 1.3 fusion.14
  28.1 0.8 slice.156
  28.9 3.7 %collective-permute-start.18 = (bf16[384,512]{1,0:T(8,128)(2,1)}, bf16[384,512]{1,0:T(8,128)(2,1)S(1)}, u32[]{:S(2)}, u32[]{:S(2)}) collective-permute-start(bf16[384,512]{1,0:T(8,128)(2,1)} %slice.156), channel_id=1, source_target_pairs={{0,4},{1,5},{2,6},{3,7},{4,0},{5,1},{6,2},{7,3},{8,12},{9,13},{10,... | collective-permute-start | bytes 1179656 | tf_op jit(solution)/shard_map/ppermute | solution.py:65
  33.3 1.0 fusion.25
  35.0 1.3 collective-permute-start.8
  36.3 1.0 fusion.27
  37.3 1.3 collective-permute-start.3
  38.6 4.1 %collective-permute-done.18.refs_4_ = bf16[384,512]{1,0:T(8,128)(2,1)S(1)} collective-permute-done((bf16[384,512]{1,0:T(8,128)(2,1)}, bf16[384,512]{1,0:T(8,128)(2,1)S(1)}, u32[]{:S(2)}, u32[]{:S(2)}) %collective-permute-start.18) | collective-permute-done | bytes 393248 | tf_op jit(solution)/shard_map/ppermute | solution.py:65
  42.7 1.5 collective-permute-start.13
  44.3 6.8 %collective-permute-done.8 = bf16[384,512]{1,0:T(8,128)(2,1)S(1)} collective-permute-done((bf16[384,512]{1,0:T(8,128)(2,1)}, bf16[384,512]{1,0:T(8,128)(2,1)S(1)}, u32[]{:S(2)}, u32[]{:S(2)}) %collective-permute-start.8) | collective-permute-done | bytes 393248 | tf_op jit(solution)/shard_map/ppermute | solution.py:65
  51.2 1.5 collective-permute-start.30
  53.4 1.3 collective-permute-start.25
  54.7 4.8 %collective-permute-done.3 = bf16[384,512]{1,0:T(8,128)(2,1)S(1)} collective-permute-done((bf16[384,512]{1,0:T(8,128)(2,1)S(1)}, bf16[384,512]{1,0:T(8,128)(2,1)S(1)}, u32[]{:S(2)}, u32[]{:S(2)}) %collective-permute-start.3) | collective-permute-done | bytes 393248 | tf_op jit(solution)/shard_map/ppermute | solution.py:65
  59.6 1.5 collective-permute-start.10
  61.8 5.5 %collective-permute-done.25 = bf16[384,512]{1,0:T(8,128)(2,1)S(1)} collective-permute-done((bf16[384,512]{1,0:T(8,128)(2,1)S(1)}, bf16[384,512]{1,0:T(8,128)(2,1)S(1)}, u32[]{:S(2)}, u32[]{:S(2)}) %collective-permute-start.25) | collective-permute-done | bytes 393248 | tf_op jit(solution)/shard_map/ppermute | solution.py:65
  67.9 1.4 collective-permute-start.14
  69.3 2.3 %collective-permute-done.10.refs_6_ = bf16[384,512]{1,0:T(8,128)(2,1)S(1)} collective-permute-done((bf16[384,512]{1,0:T(8,128)(2,1)S(1)}, bf16[384,512]{1,0:T(8,128)(2,1)S(1)}, u32[]{:S(2)}, u32[]{:S(2)}) %collective-permute-start.10) | collective-permute-done | bytes 393248 | tf_op jit(solution)/shard_map/ppermute | solution.py:65
  71.6 1.3 collective-permute-start.20
  73.0 4.8 %collective-permute-done.5.refs_6_ = bf16[384,512]{1,0:T(8,128)(2,1)S(1)} collective-permute-done((bf16[384,512]{1,0:T(8,128)(2,1)S(1)}, bf16[384,512]{1,0:T(8,128)(2,1)S(1)}, u32[]{:S(2)}, u32[]{:S(2)}) %collective-permute-start.5) | collective-permute-done | bytes 393248 | tf_op jit(solution)/shard_map/ppermute | solution.py:65
  78.4 1.5 collective-permute-start.9
  79.9 4.8 %collective-permute-done.12.refs_5_ = bf16[128,512]{1,0:T(8,128)(2,1)S(1)} collective-permute-done((bf16[128,512]{1,0:T(8,128)(2,1)S(1)}, bf16[128,512]{1,0:T(8,128)(2,1)S(1)}, u32[]{:S(2)}, u32[]{:S(2)}) %collective-permute-start.12) | collective-permute-done | bytes 131104 | tf_op jit(solution)/shard_map/ppermute | solution.py:65
  84.8 1.5 collective-permute-start.27
  86.9 1.4 collective-permute-start.4
  89.0 3.4 %add_product.8 = (f32[320,512]{1,0:T(8,128)S(1)}, f32[320,512]{1,0:T(8,128)}) custom-call(s32[2]{0:T(128)S(1)} %copy-done.26, bf16[8,320,512]{2,1,0:T(8,128)(2,1)S(1)} %get-tuple-element.20.refs_0_.refs_1_, bf16[8,320,512]{2,1,0:T(8,128)(2,1)S(1)} %get-tuple-element.20.refs_0_.refs_1_, bf16[8,320,512]{2,1,0:T(8,128)(2,1)} %collective-permute-done.refs_2_.refs_3_, ...), custom_call_target="tpu_custom_call" | custom-call | flops 1000 | bytes 1000 | tf_op jit(solution)/shard_map/add_product/pallas_call | solution.py:172
  92.4 3.6 %add_product.9 = (f32[320,512]{1,0:T(8,128)S(1)}, f32[320,512]{1,0:T(8,128)}) custom-call(s32[2]{0:T(128)S(1)} %copy-done.28, bf16[8,320,512]{2,1,0:T(8,128)(2,1)S(1)} %get-tuple-element.20.refs_0_.refs_1_, bf16[8,320,512]{2,1,0:T(8,128)(2,1)S(1)} %get-tuple-element.20.refs_0_.refs_1_, ...), custom_call_target="tpu_custom_call", output_to_operand_aliasing={{0}: (9, {}), {1}: (10, {})} | custom-call | flops 1000 | bytes 1000 | tf_op jit(solution)/shard_map/add_product/pallas_call | solution.py:172
  96.0 1.4 collective-permute-start.33
  97.9 3.6 %add_product.10 = (f32[320,512]{1,0:T(8,128)S(1)}, f32[320,512]{1,0:T(8,128)}) custom-call(s32[2]{0:T(128)S(1)} %pad_add_fusion.2.which, bf16[8,320,512]{2,1,0:T(8,128)(2,1)S(1)} %get-tuple-element.20.refs_0_.refs_1_, bf16[8,320,512]{2,1,0:T(8,128)(2,1)S(1)} %get-tuple-element.20.refs_0_.refs_1_, ...), custom_call_target="tpu_custom_call", output_to_operand_aliasing={{0}: (9, {}), {1}: (10, {})} | custom-call | flops 1000 | bytes 1000 | tf_op jit(solution)/shard_map/add_product/pallas_call | solution.py:172
  101.5 3.6 %add_product.11 = (f32[320,512]{1,0:T(8,128)S(1)}, f32[320,512]{1,0:T(8,128)}) custom-call(s32[2]{0:T(128)S(1)} %pad_add_fusion.which, bf16[8,320,512]{2,1,0:T(8,128)(2,1)S(1)} %get-tuple-element.20.refs_0_.refs_1_, bf16[8,320,512]{2,1,0:T(8,128)(2,1)S(1)} %get-tuple-element.20.refs_0_.refs_1_, ...), custom_call_target="tpu_custom_call", output_to_operand_aliasing={{0}: (9, {}), {1}: (10, {})} | custom-call | flops 1000 | bytes 1000 | tf_op jit(solution)/shard_map/add_product/pallas_call | solution.py:172
  105.1 0.8 copy-done.1
  107.3 1.5 collective-permute-start.29
  110.2 0.7 slice.157
  112.8 0.8 copy-done.18
  113.6 0.7 copy-done.20
  114.3 1.4 collective-permute-start.28
  115.7 2.2 %collective-permute-done.29.refs_5_ = bf16[128,512]{1,0:T(8,128)(2,1)S(1)} collective-permute-done((bf16[128,512]{1,0:T(8,128)(2,1)S(1)}, bf16[128,512]{1,0:T(8,128)(2,1)S(1)}, u32[]{:S(2)}, u32[]{:S(2)}) %collective-permute-start.29) | collective-permute-done | bytes 131104 | tf_op jit(solution)/shard_map/ppermute | solution.py:65
  119.2 0.7 copy-done.22
  119.9 1.5 collective-permute-start.23
  121.3 1.3 convert_bitcast_fusion
  122.8 1.0 copy-done.4
  123.8 0.9 copy-done.21
  124.8 3.4 %add_product.12 = (f32[320,512]{1,0:T(8,128)S(1)}, f32[320,512]{1,0:T(8,128)}) custom-call(s32[2]{0:T(128)S(1)} %copy-done.27, bf16[8,320,512]{2,1,0:T(8,128)(2,1)S(1)} %get-tuple-element.20.refs_0_.refs_1_, bf16[8,320,512]{2,1,0:T(8,128)(2,1)S(1)} %get-tuple-element.20.refs_0_.refs_1_, bf16[8,320,512]{2,1,0:T(8,128)(2,1)} %collective-permute-done.refs_2_.refs_3_, ...), custom_call_target="tpu_custom_call" | custom-call | flops 1000 | bytes 1000 | tf_op jit(solution)/shard_map/add_product/pallas_call | solution.py:172
  128.2 3.5 %add_product.13 = (f32[320,512]{1,0:T(8,128)S(1)}, f32[320,512]{1,0:T(8,128)}) custom-call(s32[2]{0:T(128)S(1)} %copy-done.29, bf16[8,320,512]{2,1,0:T(8,128)(2,1)S(1)} %get-tuple-element.20.refs_0_.refs_1_, bf16[8,320,512]{2,1,0:T(8,128)(2,1)S(1)} %get-tuple-element.20.refs_0_.refs_1_, ...), custom_call_target="tpu_custom_call", output_to_operand_aliasing={{0}: (9, {}), {1}: (10, {})} | custom-call | flops 1000 | bytes 1000 | tf_op jit(solution)/shard_map/add_product/pallas_call | solution.py:172
  131.8 3.7 %add_product.14 = (f32[320,512]{1,0:T(8,128)S(1)}, f32[320,512]{1,0:T(8,128)}) custom-call(s32[2]{0:T(128)S(1)} %pad_add_fusion.2.which, bf16[8,320,512]{2,1,0:T(8,128)(2,1)S(1)} %get-tuple-element.20.refs_0_.refs_1_, bf16[8,320,512]{2,1,0:T(8,128)(2,1)S(1)} %get-tuple-element.20.refs_0_.refs_1_, ...), custom_call_target="tpu_custom_call", output_to_operand_aliasing={{0}: (9, {}), {1}: (10, {})} | custom-call | flops 1000 | bytes 1000 | tf_op jit(solution)/shard_map/add_product/pallas_call | solution.py:172
  135.6 3.7 %add_product.15 = (f32[320,512]{1,0:T(8,128)S(1)}, f32[320,512]{1,0:T(8,128)}) custom-call(s32[2]{0:T(128)S(1)} %pad_add_fusion.which, bf16[8,320,512]{2,1,0:T(8,128)(2,1)S(1)} %get-tuple-element.20.refs_0_.refs_1_, bf16[8,320,512]{2,1,0:T(8,128)(2,1)S(1)} %get-tuple-element.20.refs_0_.refs_1_, ...), custom_call_target="tpu_custom_call", output_to_operand_aliasing={{0}: (9, {}), {1}: (10, {})} | custom-call | flops 1000 | bytes 1000 | tf_op jit(solution)/shard_map/add_product/pallas_call | solution.py:172
  139.3 2.7 %cache_rows.2 = bf16[16,80,128]{2,1,0:T(8,128)(2,1)} custom-call(s32[1]{0:T(128)} %bitcast.place, s32[2]{0:T(128)S(1)} %copy-done.31, s32[8]{0:T(128)S(1)} %copy-done.33, f32[320,512]{1,0:T(8,128)S(1)} %copy-done.2, f32[320,512]{1,0:T(8,128)} %collective-permute-done.17.refs_1_, f32[160,128]{1,0:T(8,128)S(1)} %get-tuple-element.67.refs_2_, ...), custom_call_target="tpu_custom_call" | custom-call | flops 1000 | bytes 1000 | tf_op jit(solution)/shard_map/cache_rows/pallas_call | solution.py:217
  142.0 3.5 %all-to-all-start = ((bf16[16,80,128]{2,1,0:T(8,128)(2,1)}), bf16[16,80,128]{2,1,0:T(8,128)(2,1)S(1)}, u32[]{:S(2)}, u32[]{:S(2)}) async-start(bf16[16,80,128]{2,1,0:T(8,128)(2,1)} %cache_rows.2), calls=%async_computation | async-start | bytes 655360 | tf_op jit(solution)/shard_map/all_to_all | solution.py:318
  146.6 1.5 cache_rows.3
  148.0 8.6 %all-to-all-done = bf16[16,80,128]{2,1,0:T(8,128)(2,1)S(1)} async-done(((bf16[16,80,128]{2,1,0:T(8,128)(2,1)}), bf16[16,80,128]{2,1,0:T(8,128)(2,1)S(1)}, u32[]{:S(2)}, u32[]{:S(2)}) %all-to-all-start) | async-done | bytes 327712 | tf_op jit(solution)/shard_map/all_to_all | solution.py:318
  156.6 3.5 %all-to-all-start.1 = ((bf16[16,80,128]{2,1,0:T(8,128)(2,1)}), bf16[16,80,128]{2,1,0:T(8,128)(2,1)S(1)}, u32[]{:S(2)}, u32[]{:S(2)}) async-start(bf16[16,80,128]{2,1,0:T(8,128)(2,1)} %cache_rows.3), calls=%async_computation.1 | async-start | bytes 655360 | tf_op jit(solution)/shard_map/all_to_all | solution.py:318
  160.8 0.9 collective-permute-done.35
  162.3 0.9 collective-permute-done.36
  163.3 7.9 %all-to-all-done.1 = bf16[16,80,128]{2,1,0:T(8,128)(2,1)S(1)} async-done(((bf16[16,80,128]{2,1,0:T(8,128)(2,1)}), bf16[16,80,128]{2,1,0:T(8,128)(2,1)S(1)}, u32[]{:S(2)}, u32[]{:S(2)}) %all-to-all-start.1) | async-done | bytes 327712 | tf_op jit(solution)/shard_map/all_to_all | solution.py:318
  171.5 0.9 maximum_bitcast_fusion
  (177 shorter events, 20.1 us)
Async XLA Ops:
  0.6 162.5 %copy-start = (bf16[8,4,128]{2,1,0:T(4,128)(2,1)S(1)}, bf16[8,4,128]{2,1,0:T(4,128)(2,1)}, u32[]{:S(2)}) copy-start(bf16[8,4,128]{2,1,0:T(4,128)(2,1)} %param.15) | copy-start | bytes 24580
  3.0 12.4 %copy-start.5 = (bf16[512,512]{1,0:T(8,128)(2,1)}, bf16[512,512]{1,0:T(8,128)(2,1)S(1)}, u32[]{:S(2)}) copy-start(bf16[512,512]{1,0:T(8,128)(2,1)S(1)} %maximum_select_fusion.refs_4_) | copy-start | bytes 1572868
  3.8 28.8 %collective-permute-start.1 = (bf16[384,512]{1,0:T(8,128)(2,1)}, bf16[384,512]{1,0:T(8,128)(2,1)S(1)}, u32[]{:S(2)}, u32[]{:S(2)}) collective-permute-start(bf16[384,512]{1,0:T(8,128)(2,1)} %slice.144), channel_id=1, source_target_pairs={{0,4},{1,5},{2,6},{3,7},{4,0},{5,1},{6,2},{7,3},{8,12},{9,13},{10,... | collective-permute-start | bytes 1179656 | tf_op jit(solution)/shard_map/ppermute | solution.py:65
  6.8 28.1 %collective-permute-start.7 = (bf16[384,512]{1,0:T(8,128)(2,1)}, bf16[384,512]{1,0:T(8,128)(2,1)}, u32[]{:S(2)}, u32[]{:S(2)}) collective-permute-start(bf16[384,512]{1,0:T(8,128)(2,1)} %slice.144), channel_id=1, source_target_pairs={{4,8},{5,9},{6,10},{7,11},{8,4},{9,5},{10,6},{11,7},{20,24},{21,25... | collective-permute-start | bytes 1179656 | tf_op jit(solution)/shard_map/ppermute | solution.py:65
  10.8 6.9 %copy-start.34 = (bf16[512,512]{1,0:T(8,128)(2,1)S(1)}, bf16[512,512]{1,0:T(8,128)(2,1)}, u32[]{:S(2)}) copy-start(bf16[512,512]{1,0:T(8,128)(2,1)} %param.10) | copy-start | bytes 1572868
  15.4 4.9 %copy-start.32 = (s32[8]{0:T(128)S(1)}, s32[8]{0:T(128)}, u32[]{:S(2)}) copy-start(s32[8]{0:T(128)} %owner.3) | copy-start | bytes 100
  15.4 10.7 %copy-start.30 = (s32[2]{0:T(128)S(1)}, s32[2]{0:T(128)}, u32[]{:S(2)}) copy-start(s32[2]{0:T(128)} %lengths.3) | copy-start | bytes 28
  15.4 72.9 %collective-permute-start = (bf16[8,320,512]{2,1,0:T(8,128)(2,1)}, bf16[8,320,512]{2,1,0:T(8,128)(2,1)}, u32[]{:S(2)}, u32[]{:S(2)}) collective-permute-start(bf16[8,320,512]{2,1,0:T(8,128)(2,1)} %get-tuple-element.21), channel_id=1, source_target_pairs={{0,1},{1,0},{2,3},{3,2},{4,5},{5,4},{6,7},{7,6},{8,9},{9,8},{10,11... | collective-permute-start | bytes 7864328 | tf_op jit(solution)/shard_map/ppermute | solution.py:65
  16.1 12.8 %collective-permute-start.15 = (bf16[256,512]{1,0:T(8,128)(2,1)}, bf16[256,512]{1,0:T(8,128)(2,1)}, u32[]{:S(2)}, u32[]{:S(2)}) collective-permute-start(bf16[256,512]{1,0:T(8,128)(2,1)} %slice.153), channel_id=1, source_target_pairs={{0,2},{1,3},{2,0},{3,1},{4,6},{5,7},{6,4},{7,5},{8,10},{9,11},{10,... | collective-permute-start | bytes 786440 | tf_op jit(solution)/shard_map/ppermute | solution.py:65
  17.9 34.9 %copy-start.3 = (bf16[512,512]{1,0:T(8,128)(2,1)}, bf16[512,512]{1,0:T(8,128)(2,1)S(1)}, u32[]{:S(2)}) copy-start(bf16[512,512]{1,0:T(8,128)(2,1)S(1)} %maximum_select_fusion.1.refs_4_) | copy-start | bytes 1572868
  18.6 15.6 %collective-permute-start.32 = (bf16[256,512]{1,0:T(8,128)(2,1)}, bf16[256,512]{1,0:T(8,128)(2,1)}, u32[]{:S(2)}, u32[]{:S(2)}) collective-permute-start(bf16[256,512]{1,0:T(8,128)(2,1)} %slice.165), channel_id=1, source_target_pairs={{0,2},{1,3},{2,0},{3,1},{4,6},{5,7},{6,4},{7,5},{8,10},{9,11},{10,... | collective-permute-start | bytes 786440 | tf_op jit(solution)/shard_map/ppermute | solution.py:65
  28.9 13.8 %collective-permute-start.18 = (bf16[384,512]{1,0:T(8,128)(2,1)}, bf16[384,512]{1,0:T(8,128)(2,1)S(1)}, u32[]{:S(2)}, u32[]{:S(2)}) collective-permute-start(bf16[384,512]{1,0:T(8,128)(2,1)} %slice.156), channel_id=1, source_target_pairs={{0,4},{1,5},{2,6},{3,7},{4,0},{5,1},{6,2},{7,3},{8,12},{9,13},{10,... | collective-permute-start | bytes 1179656 | tf_op jit(solution)/shard_map/ppermute | solution.py:65
  32.6 4.7 %collective-permute-start.2 = (bf16[384,512]{1,0:T(8,128)(2,1)S(1)}, bf16[384,512]{1,0:T(8,128)(2,1)S(1)}, u32[]{:S(2)}, u32[]{:S(2)}) collective-permute-start(bf16[384,512]{1,0:T(8,128)(2,1)S(1)} %collective-permute-done.1.refs_4_), channel_id=1, source_target_pairs={{4,8},{5,9},{6,10},{7,11},{8,4},{9,5},{10,6},{11,7},{20,24},{21,25... | collective-permute-start | bytes 1179656 | tf_op jit(solution)/shard_map/ppermute | solution.py:65
  34.3 18.5 %collective-permute-start.24 = (bf16[384,512]{1,0:T(8,128)(2,1)}, bf16[384,512]{1,0:T(8,128)(2,1)S(1)}, u32[]{:S(2)}, u32[]{:S(2)}) collective-permute-start(bf16[384,512]{1,0:T(8,128)(2,1)} %slice.156), channel_id=1, source_target_pairs={{4,8},{5,9},{6,10},{7,11},{8,4},{9,5},{10,6},{11,7},{20,24},{21,25... | collective-permute-start | bytes 1179656 | tf_op jit(solution)/shard_map/ppermute | solution.py:65
  35.0 16.2 %collective-permute-start.8 = (bf16[384,512]{1,0:T(8,128)(2,1)}, bf16[384,512]{1,0:T(8,128)(2,1)S(1)}, u32[]{:S(2)}, u32[]{:S(2)}) collective-permute-start(bf16[384,512]{1,0:T(8,128)(2,1)} %collective-permute-done.7), channel_id=1, source_target_pairs={{4,0},{5,1},{6,2},{7,3},{8,12},{9,13},{10,14},{11,15},{20,16},{21,... | collective-permute-start | bytes 1179656 | tf_op jit(solution)/shard_map/ppermute | solution.py:65
  37.3 22.3 %collective-permute-start.3 = (bf16[384,512]{1,0:T(8,128)(2,1)S(1)}, bf16[384,512]{1,0:T(8,128)(2,1)S(1)}, u32[]{:S(2)}, u32[]{:S(2)}) collective-permute-start(bf16[384,512]{1,0:T(8,128)(2,1)S(1)} %collective-permute-done.2), channel_id=1, source_target_pairs={{4,0},{5,1},{6,2},{7,3},{8,12},{9,13},{10,14},{11,15},{20,16},{21,... | collective-permute-start | bytes 1179656 | tf_op jit(solution)/shard_map/ppermute | solution.py:65
  42.7 64.5 %copy-start.12 = (bf16[384,512]{1,0:T(8,128)(2,1)}, bf16[384,512]{1,0:T(8,128)(2,1)S(1)}, u32[]{:S(2)}) copy-start(bf16[384,512]{1,0:T(8,128)(2,1)S(1)} %collective-permute-done.18.refs_4_) | copy-start | bytes 1179652
  42.7 10.7 %collective-permute-start.13 = (bf16[256,512]{1,0:T(8,128)(2,1)S(1)}, bf16[256,512]{1,0:T(8,128)(2,1)S(1)}, u32[]{:S(2)}, u32[]{:S(2)}) collective-permute-start(bf16[256,512]{1,0:T(8,128)(2,1)S(1)} %slice.150), channel_id=1, source_target_pairs={{0,2},{1,3},{2,0},{3,1},{4,6},{5,7},{6,4},{7,5},{8,10},{9,11},{10,... | collective-permute-start | bytes 786440 | tf_op jit(solution)/shard_map/ppermute | solution.py:65
  51.2 10.0 %collective-permute-start.30 = (bf16[256,512]{1,0:T(8,128)(2,1)S(1)}, bf16[256,512]{1,0:T(8,128)(2,1)S(1)}, u32[]{:S(2)}, u32[]{:S(2)}) collective-permute-start(bf16[256,512]{1,0:T(8,128)(2,1)S(1)} %slice.162), channel_id=1, source_target_pairs={{0,2},{1,3},{2,0},{3,1},{4,6},{5,7},{6,4},{7,5},{8,10},{9,11},{10,... | collective-permute-start | bytes 786440 | tf_op jit(solution)/shard_map/ppermute | solution.py:65
  52.7 15.1 %collective-permute-start.19 = (bf16[384,512]{1,0:T(8,128)(2,1)S(1)}, bf16[384,512]{1,0:T(8,128)(2,1)S(1)}, u32[]{:S(2)}, u32[]{:S(2)}) collective-permute-start(bf16[384,512]{1,0:T(8,128)(2,1)S(1)} %collective-permute-done.18.refs_4_), channel_id=1, source_target_pairs={{4,8},{5,9},{6,10},{7,11},{8,4},{9,5},{10,6},{11,7},{20,24},{21,25... | collective-permute-start | bytes 1179656 | tf_op jit(solution)/shard_map/ppermute | solution.py:65
  53.4 13.9 %collective-permute-start.25 = (bf16[384,512]{1,0:T(8,128)(2,1)S(1)}, bf16[384,512]{1,0:T(8,128)(2,1)S(1)}, u32[]{:S(2)}, u32[]{:S(2)}) collective-permute-start(bf16[384,512]{1,0:T(8,128)(2,1)S(1)} %collective-permute-done.24), channel_id=1, source_target_pairs={{4,0},{5,1},{6,2},{7,3},{8,12},{9,13},{10,14},{11,15},{20,16},{21,... | collective-permute-start | bytes 1179656 | tf_op jit(solution)/shard_map/ppermute | solution.py:65
  59.6 12.1 %collective-permute-start.10 = (bf16[384,512]{1,0:T(8,128)(2,1)S(1)}, bf16[384,512]{1,0:T(8,128)(2,1)S(1)}, u32[]{:S(2)}, u32[]{:S(2)}) collective-permute-start(bf16[384,512]{1,0:T(8,128)(2,1)S(1)} %broadcast_select_fusion.2.refs_4_), channel_id=1, source_target_pairs={{0,2},{1,3},{2,0},{3,1},{4,6},{5,7},{6,4},{7,5},{8,10},{9,11},{10,... | collective-permute-start | bytes 1179656 | tf_op jit(solution)/shard_map/ppermute | solution.py:65
  61.2 27.8 %copy-start.6 = (bf16[512,512]{1,0:T(8,128)(2,1)S(1)}, bf16[512,512]{1,0:T(8,128)(2,1)}, u32[]{:S(2)}) copy-start(bf16[512,512]{1,0:T(8,128)(2,1)} %copy-done.5) | copy-start | bytes 1572868
  61.2 27.8 %copy-start.26 = (s32[2]{0:T(128)S(1)}, s32[2]{0:T(128)}, u32[]{:S(2)}) copy-start(s32[2]{0:T(128)} %pad_add_fusion.4.which) | copy-start | bytes 28
  61.2 27.8 %copy-start.14 = (bf16[256,512]{1,0:T(8,128)(2,1)}, bf16[256,512]{1,0:T(8,128)(2,1)S(1)}, u32[]{:S(2)}) copy-start(bf16[256,512]{1,0:T(8,128)(2,1)S(1)} %collective-permute-done.30.refs_6_) | copy-start | bytes 786436
  61.2 16.5 %collective-permute-start.5 = (bf16[384,512]{1,0:T(8,128)(2,1)S(1)}, bf16[384,512]{1,0:T(8,128)(2,1)S(1)}, u32[]{:S(2)}, u32[]{:S(2)}) collective-permute-start(bf16[384,512]{1,0:T(8,128)(2,1)S(1)} %broadcast_select_fusion.3.refs_4_), channel_id=1, source_target_pairs={{0,2},{1,3},{2,0},{3,1},{4,6},{5,7},{6,4},{7,5},{8,10},{9,11},{10,... | collective-permute-start | bytes 1179656 | tf_op jit(solution)/shard_map/ppermute | solution.py:65
  67.3 11.1 %collective-permute-start.16 = (bf16[256,512]{1,0:T(8,128)(2,1)S(1)}, bf16[256,512]{1,0:T(8,128)(2,1)S(1)}, u32[]{:S(2)}, u32[]{:S(2)}) collective-permute-start(bf16[256,512]{1,0:T(8,128)(2,1)S(1)} %pad_maximum_fusion.1), channel_id=1, source_target_pairs={{0,16},{1,17},{2,18},{3,19},{4,20},{5,21},{6,22},{7,23},{8,24},{9,... | collective-permute-start | bytes 786440 | tf_op jit(solution)/shard_map/ppermute | solution.py:65
  67.9 18.4 %collective-permute-start.14 = (bf16[256,512]{1,0:T(8,128)(2,1)S(1)}, bf16[256,512]{1,0:T(8,128)(2,1)S(1)}, u32[]{:S(2)}, u32[]{:S(2)}) collective-permute-start(bf16[256,512]{1,0:T(8,128)(2,1)S(1)} %pad_maximum_fusion), channel_id=1, source_target_pairs={{0,16},{1,17},{2,18},{3,19},{4,20},{5,21},{6,22},{7,23},{8,24},{9,... | collective-permute-start | bytes 786440 | tf_op jit(solution)/shard_map/ppermute | solution.py:65
  71.6 15.3 %collective-permute-start.20 = (bf16[384,512]{1,0:T(8,128)(2,1)S(1)}, bf16[384,512]{1,0:T(8,128)(2,1)S(1)}, u32[]{:S(2)}, u32[]{:S(2)}) collective-permute-start(bf16[384,512]{1,0:T(8,128)(2,1)S(1)} %collective-permute-done.19), channel_id=1, source_target_pairs={{4,0},{5,1},{6,2},{7,3},{8,12},{9,13},{10,14},{11,15},{20,16},{21,... | collective-permute-start | bytes 1179656 | tf_op jit(solution)/shard_map/ppermute | solution.py:65
  77.7 7.0 %collective-permute-start.12 = (bf16[128,512]{1,0:T(8,128)(2,1)S(1)}, bf16[128,512]{1,0:T(8,128)(2,1)S(1)}, u32[]{:S(2)}, u32[]{:S(2)}) collective-permute-start(bf16[128,512]{1,0:T(8,128)(2,1)S(1)} %slice.149), channel_id=1, source_target_pairs={{0,16},{1,17},{2,18},{3,19},{4,20},{5,21},{6,22},{7,23},{8,24},{9,... | collective-permute-start | bytes 393224 | tf_op jit(solution)/shard_map/ppermute | solution.py:65
  78.4 31.1 %copy-start.8 = (bf16[384,512]{1,0:T(8,128)(2,1)}, bf16[384,512]{1,0:T(8,128)(2,1)S(1)}, u32[]{:S(2)}) copy-start(bf16[384,512]{1,0:T(8,128)(2,1)S(1)} %broadcast_select_fusion.refs_4_) | copy-start | bytes 1179652
  78.4 17.6 %collective-permute-start.9 = (bf16[128,512]{1,0:T(8,128)(2,1)S(1)}, bf16[128,512]{1,0:T(8,128)(2,1)S(1)}, u32[]{:S(2)}, u32[]{:S(2)}) collective-permute-start(bf16[128,512]{1,0:T(8,128)(2,1)S(1)} %slice.147), channel_id=1, source_target_pairs={{0,16},{1,17},{2,18},{3,19},{4,20},{5,21},{6,22},{7,23},{8,24},{9,... | collective-permute-start | bytes 393224 | tf_op jit(solution)/shard_map/ppermute | solution.py:65
  84.8 22.5 %collective-permute-start.27 = (bf16[384,512]{1,0:T(8,128)(2,1)S(1)}, bf16[384,512]{1,0:T(8,128)(2,1)S(1)}, u32[]{:S(2)}, u32[]{:S(2)}) collective-permute-start(bf16[384,512]{1,0:T(8,128)(2,1)S(1)} %broadcast_select_fusion.refs_4_), channel_id=1, source_target_pairs={{0,2},{1,3},{2,0},{3,1},{4,6},{5,7},{6,4},{7,5},{8,10},{9,11},{10,... | collective-permute-start | bytes 1179656 | tf_op jit(solution)/shard_map/ppermute | solution.py:65
  86.3 11.1 %collective-permute-start.11 = (bf16[128,512]{1,0:T(8,128)(2,1)S(1)}, bf16[128,512]{1,0:T(8,128)(2,1)S(1)}, u32[]{:S(2)}, u32[]{:S(2)}) collective-permute-start(bf16[128,512]{1,0:T(8,128)(2,1)S(1)} %slice.148), channel_id=1, source_target_pairs={{0,16},{1,17},{2,18},{3,19},{4,20},{5,21},{6,22},{7,23},{8,24},{9,... | collective-permute-start | bytes 393224 | tf_op jit(solution)/shard_map/ppermute | solution.py:65
  86.9 14.6 %collective-permute-start.4 = (bf16[128,512]{1,0:T(8,128)(2,1)S(1)}, bf16[128,512]{1,0:T(8,128)(2,1)S(1)}, u32[]{:S(2)}, u32[]{:S(2)}) collective-permute-start(bf16[128,512]{1,0:T(8,128)(2,1)S(1)} %slice.145), channel_id=1, source_target_pairs={{0,16},{1,17},{2,18},{3,19},{4,20},{5,21},{6,22},{7,23},{8,24},{9,... | collective-permute-start | bytes 393224 | tf_op jit(solution)/shard_map/ppermute | solution.py:65
  88.3 13.1 %collective-permute-start.6 = (bf16[128,512]{1,0:T(8,128)(2,1)S(1)}, bf16[128,512]{1,0:T(8,128)(2,1)S(1)}, u32[]{:S(2)}, u32[]{:S(2)}) collective-permute-start(bf16[128,512]{1,0:T(8,128)(2,1)S(1)} %slice.146), channel_id=1, source_target_pairs={{0,16},{1,17},{2,18},{3,19},{4,20},{5,21},{6,22},{7,23},{8,24},{9,... | collective-permute-start | bytes 393224 | tf_op jit(solution)/shard_map/ppermute | solution.py:65
  89.0 21.2 %copy-start.10 = (bf16[384,512]{1,0:T(8,128)(2,1)}, bf16[384,512]{1,0:T(8,128)(2,1)S(1)}, u32[]{:S(2)}) copy-start(bf16[384,512]{1,0:T(8,128)(2,1)S(1)} %broadcast_select_fusion.1.refs_4_) | copy-start | bytes 1179652
  96.0 17.6 %collective-permute-start.33 = (bf16[256,512]{1,0:T(8,128)(2,1)S(1)}, bf16[256,512]{1,0:T(8,128)(2,1)S(1)}, u32[]{:S(2)}, u32[]{:S(2)}) collective-permute-start(bf16[256,512]{1,0:T(8,128)(2,1)S(1)} %pad_maximum_fusion.3), channel_id=1, source_target_pairs={{0,16},{1,17},{2,18},{3,19},{4,20},{5,21},{6,22},{7,23},{8,24},{9,... | collective-permute-start | bytes 786440 | tf_op jit(solution)/shard_map/ppermute | solution.py:65
  97.4 14.1 %collective-permute-start.22 = (bf16[384,512]{1,0:T(8,128)(2,1)S(1)}, bf16[384,512]{1,0:T(8,128)(2,1)S(1)}, u32[]{:S(2)}, u32[]{:S(2)}) collective-permute-start(bf16[384,512]{1,0:T(8,128)(2,1)S(1)} %broadcast_select_fusion.1.refs_4_), channel_id=1, source_target_pairs={{0,2},{1,3},{2,0},{3,1},{4,6},{5,7},{6,4},{7,5},{8,10},{9,11},{10,... | collective-permute-start | bytes 1179656 | tf_op jit(solution)/shard_map/ppermute | solution.py:65
  101.5 7.3 %copy-start.39 = (f32[4,128]{1,0:T(4,128)S(1)}, f32[4,128]{1,0:T(4,128)}, u32[]{:S(2)}) copy-start(f32[4,128]{1,0:T(4,128)} %fusion.14) | copy-start | bytes 6148
  101.5 7.3 %copy-start.40 = (f32[64]{0:T(128)S(1)}, f32[64]{0:T(128)}, u32[]{:S(2)}) copy-start(f32[64]{0:T(128)} %multiply_power_fusion) | copy-start | bytes 772
  101.5 21.1 %copy-start.35 = (f32[160,64]{1,0:T(8,128)S(1)}, f32[160,64]{1,0:T(8,128)}, u32[]{:S(2)}) copy-start(f32[160,64]{1,0:T(8,128)} %get-tuple-element.58) | copy-start | bytes 122884
  101.5 21.1 %copy-start.36 = (f32[160,64]{1,0:T(8,128)S(1)}, f32[160,64]{1,0:T(8,128)}, u32[]{:S(2)}) copy-start(f32[160,64]{1,0:T(8,128)} %get-tuple-element.59) | copy-start | bytes 122884
  101.5 21.1 %copy-start.37 = (f32[160,64]{1,0:T(8,128)S(1)}, f32[160,64]{1,0:T(8,128)}, u32[]{:S(2)}) copy-start(f32[160,64]{1,0:T(8,128)} %get-tuple-element.60) | copy-start | bytes 122884
  101.5 21.3 %copy-start.27 = (s32[2]{0:T(128)S(1)}, s32[2]{0:T(128)}, u32[]{:S(2)}) copy-start(s32[2]{0:T(128)} %pad_add_fusion.4.which) | copy-start | bytes 28
  105.9 33.3 %collective-permute-start.17 = (f32[320,512]{1,0:T(8,128)}, f32[320,512]{1,0:T(8,128)}, u32[]{:S(2)}, u32[]{:S(2)}) collective-permute-start(f32[320,512]{1,0:T(8,128)} %get-tuple-element.29), channel_id=1, source_target_pairs={{0,1},{1,0},{2,3},{3,2},{4,5},{5,4},{6,7},{7,6},{8,9},{9,8},{10,11... | collective-permute-start | bytes 1966088 | tf_op jit(solution)/shard_map/ppermute | solution.py:65
  106.0 13.2 %collective-permute-start.31 = (bf16[256,512]{1,0:T(8,128)(2,1)S(1)}, bf16[256,512]{1,0:T(8,128)(2,1)S(1)}, u32[]{:S(2)}, u32[]{:S(2)}) collective-permute-start(bf16[256,512]{1,0:T(8,128)(2,1)S(1)} %pad_maximum_fusion.2), channel_id=1, source_target_pairs={{0,16},{1,17},{2,18},{3,19},{4,20},{5,21},{6,22},{7,23},{8,24},{9,... | collective-permute-start | bytes 786440 | tf_op jit(solution)/shard_map/ppermute | solution.py:65
  107.3 15.5 %copy-start.16 = (bf16[384,512]{1,0:T(8,128)(2,1)}, bf16[384,512]{1,0:T(8,128)(2,1)S(1)}, u32[]{:S(2)}) copy-start(bf16[384,512]{1,0:T(8,128)(2,1)S(1)} %collective-permute-done.27.refs_6_) | copy-start | bytes 1179652
  107.3 10.6 %collective-permute-start.29 = (bf16[128,512]{1,0:T(8,128)(2,1)S(1)}, bf16[128,512]{1,0:T(8,128)(2,1)S(1)}, u32[]{:S(2)}, u32[]{:S(2)}) collective-permute-start(bf16[128,512]{1,0:T(8,128)(2,1)S(1)} %slice.161), channel_id=1, source_target_pairs={{0,16},{1,17},{2,18},{3,19},{4,20},{5,21},{6,22},{7,23},{8,24},{9,... | collective-permute-start | bytes 393224 | tf_op jit(solution)/shard_map/ppermute | solution.py:65
  111.5 20.2 %collective-permute-start.26 = (bf16[128,512]{1,0:T(8,128)(2,1)}, bf16[128,512]{1,0:T(8,128)(2,1)}, u32[]{:S(2)}, u32[]{:S(2)}) collective-permute-start(bf16[128,512]{1,0:T(8,128)(2,1)} %slice.159), channel_id=1, source_target_pairs={{0,16},{1,17},{2,18},{3,19},{4,20},{5,21},{6,22},{7,23},{8,24},{9,... | collective-permute-start | bytes 393224 | tf_op jit(solution)/shard_map/ppermute | solution.py:65
  114.3 17.5 %collective-permute-start.28 = (bf16[128,512]{1,0:T(8,128)(2,1)}, bf16[128,512]{1,0:T(8,128)(2,1)}, u32[]{:S(2)}, u32[]{:S(2)}) collective-permute-start(bf16[128,512]{1,0:T(8,128)(2,1)} %slice.160), channel_id=1, source_target_pairs={{0,16},{1,17},{2,18},{3,19},{4,20},{5,21},{6,22},{7,23},{8,24},{9,... | collective-permute-start | bytes 393224 | tf_op jit(solution)/shard_map/ppermute | solution.py:65
  118.6 16.9 %collective-permute-start.21 = (bf16[128,512]{1,0:T(8,128)(2,1)}, bf16[128,512]{1,0:T(8,128)(2,1)}, u32[]{:S(2)}, u32[]{:S(2)}) collective-permute-start(bf16[128,512]{1,0:T(8,128)(2,1)} %slice.157), channel_id=1, source_target_pairs={{0,16},{1,17},{2,18},{3,19},{4,20},{5,21},{6,22},{7,23},{8,24},{9,... | collective-permute-start | bytes 393224 | tf_op jit(solution)/shard_map/ppermute | solution.py:65
  119.9 15.6 %collective-permute-start.23 = (bf16[128,512]{1,0:T(8,128)(2,1)}, bf16[128,512]{1,0:T(8,128)(2,1)}, u32[]{:S(2)}, u32[]{:S(2)}) collective-permute-start(bf16[128,512]{1,0:T(8,128)(2,1)} %slice.158), channel_id=1, source_target_pairs={{0,16},{1,17},{2,18},{3,19},{4,20},{5,21},{6,22},{7,23},{8,24},{9,... | collective-permute-start | bytes 393224 | tf_op jit(solution)/shard_map/ppermute | solution.py:65
  135.5 3.7 %copy-start.2 = (f32[320,512]{1,0:T(8,128)S(1)}, f32[320,512]{1,0:T(8,128)}, u32[]{:S(2)}) copy-start(f32[320,512]{1,0:T(8,128)} %copy-done.1) | copy-start | bytes 1966084
  135.5 3.7 %copy-start.31 = (s32[2]{0:T(128)S(1)}, s32[2]{0:T(128)}, u32[]{:S(2)}) copy-start(s32[2]{0:T(128)} %lengths.3) | copy-start | bytes 28
  135.5 10.0 %copy-start.38 = (f32[1,4,8,128]{3,1,2,0:T(4,128)S(1)}, f32[1,4,8,128]{3,1,2,0:T(4,128)}, u32[]{:S(2)}) copy-start(f32[1,4,8,128]{3,1,2,0:T(4,128)} %convert_bitcast_fusion) | copy-start | bytes 49156
  135.5 10.8 %copy-start.41 = (bf16[4,64]{1,0:T(4,128)(2,1)S(1)}, bf16[4,64]{1,0:T(4,128)(2,1)}, u32[]{:S(2)}) copy-start(bf16[4,64]{1,0:T(4,128)(2,1)} %get-tuple-element.56) | copy-start | bytes 1540
  135.6 10.7 %copy-start.42 = (bf16[4,64]{1,0:T(4,128)(2,1)S(1)}, bf16[4,64]{1,0:T(4,128)(2,1)}, u32[]{:S(2)}) copy-start(bf16[4,64]{1,0:T(4,128)(2,1)} %get-tuple-element.57) | copy-start | bytes 1540
  139.2 7.3 %collective-permute-start.34 = (f32[320,512]{1,0:T(8,128)}, f32[320,512]{1,0:T(8,128)S(1)}, u32[]{:S(2)}, u32[]{:S(2)}) collective-permute-start(f32[320,512]{1,0:T(8,128)} %get-tuple-element.37), channel_id=1, source_target_pairs={{0,1},{1,0},{2,3},{3,2},{4,5},{5,4},{6,7},{7,6},{8,9},{9,8},{10,11... | collective-permute-start | bytes 1966088 | tf_op jit(solution)/shard_map/ppermute | solution.py:65
  142.0 14.6 %all-to-all-start = ((bf16[16,80,128]{2,1,0:T(8,128)(2,1)}), bf16[16,80,128]{2,1,0:T(8,128)(2,1)S(1)}, u32[]{:S(2)}, u32[]{:S(2)}) async-start(bf16[16,80,128]{2,1,0:T(8,128)(2,1)} %cache_rows.2), calls=%async_computation | async-start | bytes 655360 | tf_op jit(solution)/shard_map/all_to_all | solution.py:318
  156.6 14.6 %all-to-all-start.1 = ((bf16[16,80,128]{2,1,0:T(8,128)(2,1)}), bf16[16,80,128]{2,1,0:T(8,128)(2,1)S(1)}, u32[]{:S(2)}, u32[]{:S(2)}) async-start(bf16[16,80,128]{2,1,0:T(8,128)(2,1)} %cache_rows.3), calls=%async_computation.1 | async-start | bytes 655360 | tf_op jit(solution)/shard_map/all_to_all | solution.py:318
  160.5 1.2 collective-permute-start.35
  161.9 1.2 collective-permute-start.36
  171.5 1.2 collective-permute-start.37
  (19 other events, 46.8 us)

commit v3 on v2

--- a/solution.py
+++ b/solution.py
@@ -89,12 +89,6 @@
     return (g, 0 if z == 1 else 3, y, c) if z in (1, 2) else None
 
 
-def mirrored(block, axis, flag):
-    quarter = block.shape[axis] // 4
-    parts = [lax.slice_in_dim(block, i * quarter, (i + 1) * quarter, axis=axis) for i in range(4)]
-    return jnp.where(flag, jnp.concatenate(parts[::-1], axis), block)
-
-
 def small_cost():
     return pl.CostEstimate(flops=1000, bytes_accessed=1000, transcendentals=0)
 
@@ -103,7 +97,7 @@
     return pl.BlockSpec(array.shape, lambda *_: (0,) * array.ndim)
 
 
-def prepare_kernel(place, rows_in, mine, other):
+def prepare_kernel(place, rows_in, token, mine, other):
     blocks, _, depth = mine.shape
     quarter = depth // 4
     wide = rows_in[...].astype(jnp.float32)
@@ -125,7 +119,7 @@
                             ).astype(jnp.bfloat16)
 
 
-def prepared(flat, group_id, core, blocks):
+def prepared(flat, place, token, blocks):
     rows, width = flat.shape
     depth = width // (2 * blocks)
     tile = 64 if rows % 64 == 0 else rows
@@ -136,53 +130,148 @@
         grid_spec=pltpu.PrefetchScalarGridSpec(
             num_scalar_prefetch=1,
             grid=(rows // tile,),
-            in_specs=[pl.BlockSpec((tile, width), lambda i, place: (i, 0))],
+            in_specs=[pl.BlockSpec((tile, width), lambda i, place: (i, 0)), pl.BlockSpec(memory_space=pl.ANY)],
             out_specs=[spec, spec],
         ),
         out_shape=[out, out],
         compiler_params=pltpu.CompilerParams(vmem_limit_bytes=32 << 20),
-        cost_estimate=small_cost(),
+        cost_estimate=pl.CostEstimate(
+            flops=8 * rows * width, bytes_accessed=4 * rows * width, transcendentals=0
+        ),
         name="normed_halves",
-    )(jnp.stack([group_id, core]).astype(jnp.int32), flat)
-
-
-def product_kernel(count_near, has_total, which, *refs):
-    left = refs[:4]
-    pieces = [ref[...] for ref in refs[4 : -2 - 2 * has_total]]
-    near = jnp.concatenate(pieces[:count_near], 0) if count_near > 1 else pieces[0]
-    far = jnp.concatenate(pieces[count_near:], 0)
-    for half in range(2):
-        total = jnp.dot(left[2 * half][0], near, preferred_element_type=jnp.float32)
-        total += jnp.dot(left[2 * half + 1][0], far, preferred_element_type=jnp.float32)
-        if has_total:
-            total += refs[half - 4][...]
-        refs[half - 2][...] = total
-
-
-def product(which, mine, other, near, far, totals):
-    _, rows, depth = mine.shape
-    columns = near[0].shape[1]
-    operands = [*near, *far, *totals]
-    left_specs = [
-        pl.BlockSpec((1, rows, depth), functools.partial(lambda k, _, which: (which[k], 0, 0), k))
-        for k in (0, 1)
-    ]
-    out = jax.ShapeDtypeStruct((rows, columns), jnp.float32)
-    first_total = 1 + 4 + len(near) + len(far)
+    )(place, flat, token)
+
+
+VMEM_REF = pl.BlockSpec(memory_space=pltpu.VMEM)
+SMEM_REF = pl.BlockSpec(memory_space=pltpu.SMEM)
+ANY_REF = pl.BlockSpec(memory_space=pl.ANY)
+
+
+def local_call(name, kernel, place, token, inputs, outs, flops=1000):
+    def wrapped(place_ref, token_ref, *refs):
+        kernel(place_ref, *refs)
+
     return pl.pallas_call(
-        functools.partial(product_kernel, len(near), len(totals) // 2),
-        grid_spec=pltpu.PrefetchScalarGridSpec(
-            num_scalar_prefetch=1,
-            grid=(1,),
-            in_specs=left_specs * 2 + [whole_block(piece) for piece in operands],
-            out_specs=[whole_block(out)] * 2,
-        ),
-        out_shape=[out, out],
-        input_output_aliases={first_total + i: i for i in range(len(totals))},
-        compiler_params=pltpu.CompilerParams(vmem_limit_bytes=32 << 20),
-        cost_estimate=small_cost(),
-        name="add_product",
-    )(which, mine, mine, other, other, *operands)
+        wrapped,
+        in_specs=[SMEM_REF, ANY_REF] + [VMEM_REF] * len(inputs),
+        out_specs=[VMEM_REF] * len(outs),
+        out_shape=[jax.ShapeDtypeStruct(shape, dtype) for shape, dtype in outs],
+        compiler_params=pltpu.CompilerParams(vmem_limit_bytes=24 << 20),
+        cost_estimate=pl.CostEstimate(flops=flops, bytes_accessed=1000, transcendentals=0),
+        name=name,
+    )(place, token, *inputs)
+
+
+def first_cut(place, *refs):
+    count = len(refs) // 4
+    for weight, own, main, across in zip(
+        refs[:count], refs[count::3], refs[count + 1 :: 3], refs[count + 2 :: 3]
+    ):
+        quarter = weight.shape[0] // 4
+        for g in range(2):
+
+            @pl.when(place[0] == g)
+            def _():
+                for spot in range(4):
+                    q = 3 - spot if g else spot
+                    part = weight[q * quarter : (q + 1) * quarter]
+                    area = slice(spot * quarter, (spot + 1) * quarter)
+                    own[area] = part
+                    if spot < 3:
+                        main[area] = part
+                    if spot < 2:
+                        across[area] = part
+
+
+def second_cut(place, near, across, onward, short):
+    quarter = near.shape[0] // 3
+    onward[:quarter] = near[:quarter]
+    onward[quarter : 2 * quarter] = across[quarter:]
+    onward[2 * quarter :] = across[:quarter]
+    short[...] = near[: 2 * quarter]
+
+
+def third_cut(place, end_b, mid_b, across_a, slot_b, onward):
+    quarter = end_b.shape[0] // 3
+
+    @pl.when(place[2] == 1)
+    def _():
+        slot_b[...] = end_b[...]
+        onward[:quarter] = end_b[:quarter]
+
+    @pl.when(place[2] == 0)
+    def _():
+        slot_b[...] = mid_b[...]
+        onward[:quarter] = mid_b[:quarter]
+
+    onward[quarter:] = across_a[:quarter]
+
+
+def fourth_cut(place, end_c, mid_c, across_b, slot_c, onward):
+    quarter = end_c.shape[0] // 2
+
+    def put(block):
+        slot_c[...] = block[...]
+        onward[:quarter] = block[quarter:]
+        onward[quarter : 2 * quarter] = block[:quarter]
+
+    @pl.when(place[2] == 1)
+    def _():
+        put(end_c)
+
+    @pl.when(place[2] == 0)
+    def _():
+        put(mid_c)
+
+    onward[2 * quarter :] = across_b[:quarter]
+
+
+def last_cut(place, across_c, onward):
+    quarter = across_c.shape[0] // 2
+    onward[:quarter] = across_c[quarter:]
+    onward[quarter:] = across_c[:quarter]
+
+
+def times(left, block, first, piece):
+    part = left[block][:, first : first + piece.shape[0]]
+    return jnp.dot(part, piece, preferred_element_type=jnp.float32)
+
+
+def early_product(place, mine, other, own, near, across, slot_b, across_a, sent, *totals):
+    quarter = own.shape[0] // 4
+    for left, total in zip((mine, other), totals):
+        home = jnp.concatenate([across[...], sent[quarter:]], 0)
+        next_door = jnp.concatenate([near[...], sent[:quarter]], 0)
+        value = times(left, place[4], 0, own[...])
+        value += times(left, place[5], 0, home)
+        value += times(left, place[6], 0, next_door)
+        value += times(left, place[7], 0, across_a[...])
+        value += times(left, place[8], 0, slot_b[...])
+        total[...] = value
+
+
+def late_product(
+    place, mine, other, slot_c, across_b, across_c, sent_b, sent_c, mine_in, other_in, *totals
+):
+    quarter = slot_c.shape[0] // 2
+    depth = 4 * quarter
+    for left, before, total in zip((mine, other), (mine_in, other_in), totals):
+        value = before[...]
+        ends = jnp.concatenate(
+            [left[place[8]][:, depth - quarter :], left[place[7]][:, depth - quarter :]], 1
+        )
+        value += jnp.dot(ends, sent_b[...], preferred_element_type=jnp.float32)
+        full_b = jnp.concatenate([across_b[...], sent_c[2 * quarter :]], 0)
+        value += times(left, place[9], 0, full_b)
+        full_c = jnp.concatenate([slot_c[...], sent_c[: 2 * quarter]], 0)
+        value += times(left, place[10], 0, full_c)
+        value += times(left, place[11], 0, across_c[...])
+        total[...] = value
+
+
+def last_product(place, mine, other, sent, mine_in, other_in, *totals):
+    for left, before, total in zip((mine, other), (mine_in, other_in), totals):
+        total[...] = before[...] + times(left, place[11], sent.shape[0], sent[...])
 
 
 def rows_kernel(rotated, place, lengths, owner, *refs):
@@ -230,33 +319,60 @@
     )(place, lengths, owner, *operands)
 
 
-def planned_totals(weight, mine, other, z, y, g):
-    quarter = weight.shape[0] // 4
-    own = mirrored(weight, 0, g == 1)
-    is_end = (z == 0) | (z == 3)
-    main = own[: 3 * quarter]
-    near = moved(main, to_pair)
-    mid_b = moved(main, to_middle)
-    mid_c = moved(near, to_middle)
-    end_b = moved(mid_b, to_end)
-    end_c = moved(mid_c, to_end)
-    slot_b = jnp.where(is_end, end_b, mid_b)
-    slot_c = jnp.where(is_end, end_c, mid_c)
-    z_a, z_b, z_c = z ^ 1, jnp.where(z < 2, 2, 1), jnp.where(z < 2, 3, 0)
-    totals = []
-    for zz, block, share in ((z, own, 2), (z_a, near, 2), (z_b, slot_b, 3), (z_c, slot_c, 3)):
-        here = [block]
-        if block is not own:
-            here.append(moved(block[:quarter], to_group))
-        across = moved(block[: share * quarter], to_row)
-        if share == 2:
-            onward = jnp.concatenate([across[quarter:], across[:quarter]], 0)
-        else:
-            onward = across[:quarter]
-        there = [across, moved(onward, to_group)]
-        which = jnp.stack([zz * 2 + y, zz * 2 + 1 - y]).astype(jnp.int32)
-        totals = product(which, mine, other, here, there, totals)
-    return totals
+def planned_totals(weights, mine_other, place, token):
+    depth, columns = weights[0].shape
+    quarter = depth // 4
+    kind = weights[0].dtype
+
+    def rows(count):
+        return ((count * quarter, columns), kind)
+
+    def round_of(name, kernel, inputs, *counts):
+        nonlocal token
+        outs = local_call(name, kernel, place, token, inputs, [rows(n) for n in counts])
+        token = outs[0]
+        return outs
+
+    count = len(weights)
+    cuts = round_of("cut_own", first_cut, weights, *[4, 3, 2] * count)
+    states = [cuts[3 * i : 3 * i + 3] for i in range(count)]
+    first = []
+    for own, main, side in states:
+        first.append((own, moved(main, to_pair), moved(main, to_middle), moved(side, to_row)))
+    mine, other = mine_other(cuts[0])
+    total_rows = mine.shape[1]
+    sums = [((total_rows, columns), jnp.float32)] * 2
+    flops = 2 * 2 * total_rows * columns * quarter
+
+    second = []
+    for own, near, mid_b, across in first:
+        onward, short = round_of("cut_near", second_cut, [near, across], 3, 2)
+        second.append(
+            (moved(mid_b, to_end), moved(short, to_middle), moved(near, to_row), moved(onward, to_group))
+        )
+    third, totals = [], []
+    for (own, near, mid_b, across), (end_b, mid_c, across_a, sent) in zip(first, second):
+        slot_b, onward = round_of("cut_middle", third_cut, [end_b, mid_b, across_a], 3, 2)
+        third.append((moved(mid_c, to_end), moved(slot_b, to_row), moved(onward, to_group)))
+        operands = [mine, other, own, near, across, slot_b, across_a, sent]
+        totals.append(
+            local_call("early_product", early_product, place, slot_b, operands, sums, 18 * flops)
+        )
+    fourth = []
+    for (_, mid_c, _, _), (end_c, across_b, sent_b) in zip(second, third):
+        slot_c, onward = round_of("cut_far", fourth_cut, [end_c, mid_c, across_b], 2, 3)
+        fourth.append((slot_c, moved(slot_c, to_row), moved(onward, to_group)))
+    results = []
+    for (_, across_b, sent_b), (slot_c, across_c, sent_c), total in zip(third, fourth, totals):
+        (onward,) = round_of("cut_last", last_cut, [across_c], 2)
+        last = moved(onward, to_group)
+        operands = [mine, other, slot_c, across_b, across_c, sent_b, sent_c, *total]
+        total = local_call("late_product", late_product, place, onward, operands, sums, 12 * flops)
+        operands = [mine, other, last, *total]
+        results.append(
+            local_call("last_product", last_product, place, last, operands, sums, 2 * flops)
+        )
+    return results
 
 
 def body(hidden, key_weight, value_weight, lengths, owner, dec_query, dec_key, dec_value):
@@ -275,8 +391,14 @@
     if planned:
         core = device_id % 2
         z, y = device_id // 4, device_id // 2 % 2
-        mine, other = prepared(flat, group_id, core, seq // 2)
-        other = moved(other, to_core)
+        z_a, z_b, z_c = z ^ 1, jnp.where(z < 2, 2, 1), jnp.where(z < 2, 3, 0)
+        place = [group_id, core, (z == 0) | (z == 3), 0, z * 2 + y, z * 2 + 1 - y, z_a * 2 + y]
+        place += [z_a * 2 + 1 - y, z_b * 2 + y, z_b * 2 + 1 - y, z_c * 2 + y, z_c * 2 + 1 - y]
+        place = jnp.stack([jnp.asarray(entry, jnp.int32) for entry in place])
+
+        def mine_other(token):
+            mine, other = prepared(flat, place, token, seq // 2)
+            return mine, moved(other, to_core)
     else:
         widened = flat.astype(jnp.float32)
         normed = (
@@ -309,16 +431,17 @@
             jnp.concatenate([cosine, cosine], 1),
             jnp.concatenate([-sine_part, sine_part], 1),
         )
-        place = device_id.astype(jnp.int32).reshape(1)
-
-        def cached(weight, turn):
-            total, came = planned_totals(weight, mine, other, z, y, group_id)
+        weights = (key_weight, value_weight)
+        caches = []
+        for (total, came), turned in zip(
+            planned_totals(weights, mine_other, place, key_weight), (turn, ())
+        ):
             came = moved(came, to_core)
-            outgoing = outgoing_rows(total, came, place, lengths, owner, turn)
-            return lax.all_to_all(outgoing, "seq", split_axis=0, concat_axis=1, tiled=True)[0]
-
-        cache_keys = cached(key_weight, turn)
-        cache_values = cached(value_weight, ())
+            outgoing = outgoing_rows(total, came, device_id.reshape(1), lengths, owner, turned)
+            caches.append(
+                lax.all_to_all(outgoing, "seq", split_axis=0, concat_axis=1, tiled=True)[0]
+            )
+        cache_keys, cache_values = caches
     else:
         shape = (count_requests, count_rows, KEY_VALUE_HEADS, HEAD_SIZE)
         unrotated_key = project(key_weight).reshape(shape)

time: 174 us -> 164 us (0.943)
  waiting for transfers between devices: 53.8 us -> 44.9 us
  starting transfers between devices: 46.7 us -> 42.5 us
  other arithmetic: 13.6 us -> 9.82 us
  Pallas kernels: 37.1 us -> 40.6 us
  local copies, waits for them, and re-layouts: 17.4 us -> 19.9 us
    unnamed x88 -> x100, local copies, waits for them, and re-layouts: 8.31 us -> 19.8 us
    slice x22 -> x0, local copies, waits for them, and re-layouts: 9.13 us -> none  [the longest x4 2.01 us: planned_totals(): onward = jnp.concatenate([across[quarter:], across[:quarter]], 0)]
    ppermute x35 -> x29, waiting for transfers between devices: 35.4 us -> 26.4 us  [moved(): return lax.ppermute(block, ('groups', 'seq'), route)]
    ppermute x35 -> x29, starting transfers between devices: 38.9 us -> 33.3 us  [moved(): return lax.ppermute(block, ('groups', 'seq'), route)]
    pallas_call x8 -> x15, Pallas kernels: 28.3 us -> 31.8 us  [local_call(): pl.pallas_call(wrapped, in_specs=[SMEM_REF, ANY_REF] + [VMEM_REF] * len(i...]
  transfers between devices with their start and end apart: 40 -> 34, of which waited for: 13 -> 12; matrix products, arithmetic and copies ran while one was open for 11% -> 6% of each run, Pallas kernels for 21% -> 22%
where the time goes in v3:
time: 164 us; the launch traced here: 162 us
  waiting for transfers between devices  44.9 us (27%)
  starting transfers between devices  42.5 us (26%)
  Pallas kernels  40.6 us (25%)
  local copies, waits for them, and re-layouts  19.9 us (12%)
  other arithmetic  9.82 us (6%)
  between operations  3.71 us (2%)
    ppermute x29, starting transfers between devices, moved(): return lax.ppermute(block, ('groups', 'seq'), route)  33.3 us
    pallas_call x15, Pallas kernels, local_call(): pl.pallas_call(wrapped, in_specs=[SMEM_REF, ANY_REF] + [VMEM_REF] * len(i...  31.8 us
    ppermute x29, waiting for transfers between devices, moved(): return lax.ppermute(block, ('groups', 'seq'), route)  26.4 us
    unnamed x100, local copies, waits for them, and re-layouts  19.8 us
    all_to_all x2, waiting for transfers between devices, body(): lax.all_to_all(outgoing, 'seq', split_axis=0, concat_axis=1, tiled=True)[0]  16.5 us
    all_to_all x2, starting transfers between devices, body(): lax.all_to_all(outgoing, 'seq', split_axis=0, concat_axis=1, tiled=True)[0]  8.46 us
    pallas_call x1, Pallas kernels, prepared(): pl.pallas_call(prepare_kernel, grid_spec=pltpu.PrefetchScalarGridSpec(num...  4.54 us
    pallas_call x2, Pallas kernels, outgoing_rows(): pl.pallas_call(functools.partial(rows_kernel, bool(turn)), grid_spec=pltp...  4.2 us
  transfers between devices with their start and end apart: 34, of which 12 were waited for; matrix products, arithmetic and copies ran while one was open for 6% of the time, Pallas kernels for 22%

profile of v3, /device:TPU:0, one launch (start us, length us, event | category | flops | bytes accessed | tf_op | source)
XLA Modules:
  0.0 162.4 jit_solution(8542062310454302565)
XLA Ops:
  0.8 1.0 copy-done.4
  1.9 1.0 copy-done.26
  3.6 0.8 copy-done.24
  4.4 2.5 %copy-done.1 = bf16[2,160,8192]{2,1,0:T(8,128)(2,1)S(1)} copy-done((bf16[2,160,8192]{2,1,0:T(8,128)(2,1)S(1)}, bf16[2,160,8192]{2,1,0:T(8,128)(2,1)}, u32[]{:S(2)}) %copy-start.1) | copy-done | bytes 5242904
  6.9 4.5 %normed_halves.1 = (bf16[8,320,512]{2,1,0:T(8,128)(2,1)S(1)}, bf16[8,320,512]{2,1,0:T(8,128)(2,1)}) custom-call(s32[12]{0:T(128)S(1)} %stack.51.place_ref.place, bf16[320,8192]{1,0:T(8,128)(2,1)S(1)} %bitcast.48, bf16[512,512]{1,0:T(8,128)(2,1)S(1)} %get-tuple-element.34.token_ref.token.refs_2_), custom_call_target="tpu_custom_call" | custom-call | flops 20971520 | bytes 10485760 | tf_op jit(solution)/shard_map/normed_halves/pallas_call | solution.py:128
  12.7 5.3 %collective-permute-start = (bf16[384,512]{1,0:T(8,128)(2,1)S(1)}, bf16[384,512]{1,0:T(8,128)(2,1)S(1)}, u32[]{:S(2)}, u32[]{:S(2)}) collective-permute-start(bf16[384,512]{1,0:T(8,128)(2,1)S(1)} %get-tuple-element.35), channel_id=1, source_target_pairs={{0,4},{1,5},{2,6},{3,7},{4,0},{5,1},{6,2},{7,3},{8,12},{9,13},{10,... | collective-permute-start | bytes 1179656 | tf_op jit(solution)/shard_map/ppermute | solution.py:65
  18.0 1.5 collective-permute-start.1
  20.0 7.2 %collective-permute-done.1.refs_1_.refs_4_ = bf16[256,512]{1,0:T(8,128)(2,1)S(1)} collective-permute-done((bf16[256,512]{1,0:T(8,128)(2,1)S(1)}, bf16[256,512]{1,0:T(8,128)(2,1)S(1)}, u32[]{:S(2)}, u32[]{:S(2)}) %collective-permute-start.1) | collective-permute-done | bytes 262176 | tf_op jit(solution)/shard_map/ppermute | solution.py:65
  27.2 4.6 %collective-permute-done.3.refs_1_.refs_4_ = bf16[256,512]{1,0:T(8,128)(2,1)S(1)} collective-permute-done((bf16[256,512]{1,0:T(8,128)(2,1)S(1)}, bf16[256,512]{1,0:T(8,128)(2,1)S(1)}, u32[]{:S(2)}, u32[]{:S(2)}) %collective-permute-start.3) | collective-permute-done | bytes 262176 | tf_op jit(solution)/shard_map/ppermute | solution.py:65
  31.8 1.4 collective-permute-start.7
  33.2 1.3 collective-permute-start.5
  35.2 1.5 collective-permute-start.6
  36.8 1.4 cut_near.2
  38.2 1.4 collective-permute-start.10
  39.6 1.3 collective-permute-start.8
  40.9 4.3 %collective-permute-done.5.refs_0_ = bf16[384,512]{1,0:T(8,128)(2,1)S(1)} collective-permute-done((bf16[384,512]{1,0:T(8,128)(2,1)S(1)}, bf16[384,512]{1,0:T(8,128)(2,1)S(1)}, u32[]{:S(2)}, u32[]{:S(2)}) %collective-permute-start.5) | collective-permute-done | bytes 393248 | tf_op jit(solution)/shard_map/ppermute | solution.py:65
  45.2 1.5 collective-permute-start.9
  46.7 1.3 cut_near.3
  49.5 1.4 collective-permute-start.13
  50.9 1.0 copy-done.10
  51.9 1.0 copy-done.28
  52.9 1.0 copy-done.30
  53.9 1.0 copy-done.32
  56.7 1.3 collective-permute-start.11
  58.0 1.3 collective-permute-start.14
  59.3 2.0 %cut_middle.3 = (bf16[384,512]{1,0:T(8,128)(2,1)S(1)}, bf16[256,512]{1,0:T(8,128)(2,1)}) custom-call(s32[12]{0:T(128)S(1)} %stack.51.place_ref.place, bf16[384,512]{1,0:T(8,128)(2,1)S(1)} %get-tuple-element.41.token_ref.refs_5_, bf16[384,512]{1,0:T(8,128)(2,1)} %collective-permute-done.8.refs_0_, bf16[384,512]{1,0:T(8,128)(2,1)} %collective-permute-done.7.refs_1_, ...), custom_call_target="tpu_custom_call" | custom-call | flops 1000 | bytes 1000 | tf_op jit(solution)/shard_map/cut_middle/pallas_call | solution.py:154
  61.3 1.5 collective-permute-start.15
  62.8 1.1 fusion.6
  63.9 3.6 %collective-permute-done.11.refs_0_ = bf16[256,512]{1,0:T(8,128)(2,1)S(1)} collective-permute-done((bf16[256,512]{1,0:T(8,128)(2,1)}, bf16[256,512]{1,0:T(8,128)(2,1)S(1)}, u32[]{:S(2)}, u32[]{:S(2)}) %collective-permute-start.11) | collective-permute-done | bytes 262176 | tf_op jit(solution)/shard_map/ppermute | solution.py:65
  67.6 1.6 collective-permute-start.21
  69.2 1.7 %cut_far.2 = (bf16[256,512]{1,0:T(8,128)(2,1)}, bf16[384,512]{1,0:T(8,128)(2,1)S(1)}) custom-call(s32[12]{0:T(128)S(1)} %stack.51.place_ref.place, bf16[384,512]{1,0:T(8,128)(2,1)S(1)} %get-tuple-element.42.token_ref.refs_5_, bf16[256,512]{1,0:T(8,128)(2,1)S(1)} %collective-permute-done.11.refs_0_, bf16[256,512]{1,0:T(8,128)(2,1)} %collective-permute-done.10.refs_1_, ...), custom_call_target="tpu_custom_call" | custom-call | flops 1000 | bytes 1000 | tf_op jit(solution)/shard_map/cut_far/pallas_call | solution.py:154
  72.4 1.5 collective-permute-start.16
  73.9 1.3 fusion.19
  78.9 1.6 collective-permute-start.19
  81.2 2.0 %cut_far.3 = (bf16[256,512]{1,0:T(8,128)(2,1)S(1)}, bf16[384,512]{1,0:T(8,128)(2,1)}) custom-call(s32[12]{0:T(128)S(1)} %stack.51.place_ref.place, bf16[256,512]{1,0:T(8,128)(2,1)} %get-tuple-element.44.token_ref.refs_2_, bf16[256,512]{1,0:T(8,128)(2,1)} %collective-permute-done.14.refs_0_, bf16[256,512]{1,0:T(8,128)(2,1)} %collective-permute-done.13.refs_1_, ...), custom_call_target="tpu_custom_call" | custom-call | flops 1000 | bytes 1000 | tf_op jit(solution)/shard_map/cut_far/pallas_call | solution.py:154
  83.2 1.1 cut_last.2.token_ref
  85.4 1.7 %collective-permute-start.27 = (bf16[384,512]{1,0:T(8,128)(2,1)}, bf16[384,512]{1,0:T(8,128)(2,1)}, u32[]{:S(2)}, u32[]{:S(2)}) collective-permute-start(bf16[384,512]{1,0:T(8,128)(2,1)} %copy-done.27), channel_id=1, source_target_pairs={{0,16},{1,17},{2,18},{3,19},{4,20},{5,21},{6,22},{7,23},{8,24},{9,... | collective-permute-start | bytes 1179656 | tf_op jit(solution)/shard_map/ppermute | solution.py:65
  87.6 1.0 copy-done.3
  88.6 1.0 copy-done.8
  89.6 1.0 copy-done.11
  90.6 0.9 copy-done.17
  91.5 3.7 %early_product.2 = (f32[320,512]{1,0:T(8,128)S(1)}, f32[320,512]{1,0:T(8,128)S(1)}) custom-call(s32[12]{0:T(128)S(1)} %stack.51.place_ref.place, bf16[384,512]{1,0:T(8,128)(2,1)S(1)} %copy-done.3, bf16[8,320,512]{2,1,0:T(8,128)(2,1)S(1)} %get-tuple-element.47.refs_0_, bf16[8,320,512]{2,1,0:T(8,128)(2,1)} %collective-permute-done.18.refs_1_, ...), custom_call_target="tpu_custom_call" | custom-call | flops 1509949440 | bytes 1000 | tf_op jit(solution)/shard_map/early_product/pallas_call | solution.py:154
  96.1 3.1 %late_product.2 = (f32[320,512]{1,0:T(8,128)S(1)}, f32[320,512]{1,0:T(8,128)S(1)}) custom-call(s32[12]{0:T(128)S(1)} %stack.51.place_ref.place, bf16[256,512]{1,0:T(8,128)(2,1)S(1)} %cut_last.2.token_ref, bf16[8,320,512]{2,1,0:T(8,128)(2,1)S(1)} %get-tuple-element.47.refs_0_, bf16[8,320,512]{2,1,0:T(8,128)(2,1)} %collective-permute-done.18.refs_1_, ...), custom_call_target="tpu_custom_call" | custom-call | flops 1006632960 | bytes 1000 | tf_op jit(solution)/shard_map/late_product/pallas_call | solution.py:154
  99.3 2.1 %collective-permute-done.17.token_ref.refs_2_ = bf16[256,512]{1,0:T(8,128)(2,1)S(1)} collective-permute-done((bf16[256,512]{1,0:T(8,128)(2,1)S(1)}, bf16[256,512]{1,0:T(8,128)(2,1)S(1)}, u32[]{:S(2)}, u32[]{:S(2)}) %collective-permute-start.17) | collective-permute-done | bytes 262176 | tf_op jit(solution)/shard_map/ppermute | solution.py:65
  101.3 3.0 %last_product.2 = (f32[320,512]{1,0:T(8,128)S(1)}, f32[320,512]{1,0:T(8,128)}) custom-call(s32[12]{0:T(128)S(1)} %stack.51.place_ref.place, bf16[256,512]{1,0:T(8,128)(2,1)S(1)} %collective-permute-done.17.token_ref.refs_2_, bf16[8,320,512]{2,1,0:T(8,128)(2,1)S(1)} %get-tuple-element.47.refs_0_, bf16[8,320,512]{2,1,0:T(8,128)(2,1)} %collective-permute-done.18.refs_1_, ...), custom_call_target="tpu_custom_call" | custom-call | flops 167772160 | bytes 1000 | tf_op jit(solution)/shard_map/last_product/pallas_call | solution.py:154
  104.3 0.9 subtract_convert_fusion.1
  106.4 1.3 cut_last.3.token_ref
  107.7 1.6 collective-permute-start.24
  109.3 1.3 convert_bitcast_fusion
  110.6 0.9 copy-done.15
  111.6 1.0 copy-done.25
  112.6 3.8 %early_product.3 = (f32[320,512]{1,0:T(8,128)S(1)}, f32[320,512]{1,0:T(8,128)S(1)}) custom-call(s32[12]{0:T(128)S(1)} %stack.51.place_ref.place, bf16[384,512]{1,0:T(8,128)(2,1)S(1)} %get-tuple-element.42.token_ref.refs_5_, bf16[8,320,512]{2,1,0:T(8,128)(2,1)S(1)} %get-tuple-element.47.refs_0_, bf16[8,320,512]{2,1,0:T(8,128)(2,1)} %collective-permute-done.18.refs_1_, ...), custom_call_target="tpu_custom_call" | custom-call | flops 1509949440 | bytes 1000 | tf_op jit(solution)/shard_map/early_product/pallas_call | solution.py:154
  116.4 4.2 %collective-permute-done.25.refs_5_ = bf16[256,512]{1,0:T(8,128)(2,1)} collective-permute-done((bf16[256,512]{1,0:T(8,128)(2,1)}, bf16[256,512]{1,0:T(8,128)(2,1)}, u32[]{:S(2)}, u32[]{:S(2)}) %collective-permute-start.25) | collective-permute-done | bytes 262176 | tf_op jit(solution)/shard_map/ppermute | solution.py:65
  120.6 3.2 %late_product.3 = (f32[320,512]{1,0:T(8,128)S(1)}, f32[320,512]{1,0:T(8,128)S(1)}) custom-call(s32[12]{0:T(128)S(1)} %stack.51.place_ref.place, bf16[256,512]{1,0:T(8,128)(2,1)} %cut_last.3.token_ref, bf16[8,320,512]{2,1,0:T(8,128)(2,1)S(1)} %get-tuple-element.47.refs_0_, bf16[8,320,512]{2,1,0:T(8,128)(2,1)} %collective-permute-done.18.refs_1_, ...), custom_call_target="tpu_custom_call" | custom-call | flops 1006632960 | bytes 1000 | tf_op jit(solution)/shard_map/late_product/pallas_call | solution.py:154
  123.9 3.0 %last_product.3 = (f32[320,512]{1,0:T(8,128)S(1)}, f32[320,512]{1,0:T(8,128)}) custom-call(s32[12]{0:T(128)S(1)} %stack.51.place_ref.place, bf16[256,512]{1,0:T(8,128)(2,1)} %collective-permute-done.24.token_ref.refs_2_, bf16[8,320,512]{2,1,0:T(8,128)(2,1)S(1)} %get-tuple-element.47.refs_0_, bf16[8,320,512]{2,1,0:T(8,128)(2,1)} %collective-permute-done.18.refs_1_, ...), custom_call_target="tpu_custom_call" | custom-call | flops 167772160 | bytes 1000 | tf_op jit(solution)/shard_map/last_product/pallas_call | solution.py:154
  126.9 2.7 %cache_rows.2 = bf16[16,80,128]{2,1,0:T(8,128)(2,1)} custom-call(s32[1]{0:T(128)} %bitcast.place, s32[2]{0:T(128)S(1)} %copy-done.35, s32[8]{0:T(128)S(1)} %copy-done.36, f32[320,512]{1,0:T(8,128)S(1)} %copy-done.23, f32[320,512]{1,0:T(8,128)} %collective-permute-done.22.refs_1_, f32[160,128]{1,0:T(8,128)S(1)} %copy-done.33, f32[160,128]{1,0:T(8,128)S(1)} %copy-done.34), custom_call_target="tpu_custom_call" | custom-call | flops 1000 | bytes 1000 | tf_op jit(solution)/shard_map/cache_rows/pallas_call | solution.py:306
  129.6 4.9 %all-to-all-start = ((bf16[16,80,128]{2,1,0:T(8,128)(2,1)}), bf16[16,80,128]{2,1,0:T(8,128)(2,1)S(1)}, u32[]{:S(2)}, u32[]{:S(2)}) async-start(bf16[16,80,128]{2,1,0:T(8,128)(2,1)} %cache_rows.2), calls=%async_computation | async-start | bytes 655360 | tf_op jit(solution)/shard_map/all_to_all | solution.py:442
  135.6 1.5 cache_rows.3
  137.1 8.6 %all-to-all-done = bf16[16,80,128]{2,1,0:T(8,128)(2,1)S(1)} async-done(((bf16[16,80,128]{2,1,0:T(8,128)(2,1)}), bf16[16,80,128]{2,1,0:T(8,128)(2,1)S(1)}, u32[]{:S(2)}, u32[]{:S(2)}) %all-to-all-start) | async-done | bytes 327712 | tf_op jit(solution)/shard_map/all_to_all | solution.py:442
  145.7 3.5 %all-to-all-start.1 = ((bf16[16,80,128]{2,1,0:T(8,128)(2,1)}), bf16[16,80,128]{2,1,0:T(8,128)(2,1)S(1)}, u32[]{:S(2)}, u32[]{:S(2)}) async-start(bf16[16,80,128]{2,1,0:T(8,128)(2,1)} %cache_rows.3), calls=%async_computation.1 | async-start | bytes 655360 | tf_op jit(solution)/shard_map/all_to_all | solution.py:442
  149.9 0.9 collective-permute-done.29
  151.3 0.9 collective-permute-done.30
  152.4 7.9 %all-to-all-done.1 = bf16[16,80,128]{2,1,0:T(8,128)(2,1)S(1)} async-done(((bf16[16,80,128]{2,1,0:T(8,128)(2,1)}), bf16[16,80,128]{2,1,0:T(8,128)(2,1)S(1)}, u32[]{:S(2)}, u32[]{:S(2)}) %all-to-all-start.1) | async-done | bytes 327712 | tf_op jit(solution)/shard_map/all_to_all | solution.py:442
  160.6 0.9 maximum_bitcast_fusion
  (148 shorter events, 17.5 us)
Async XLA Ops:
  0.6 151.6 %copy-start = (bf16[8,4,128]{2,1,0:T(4,128)(2,1)S(1)}, bf16[8,4,128]{2,1,0:T(4,128)(2,1)}, u32[]{:S(2)}) copy-start(bf16[8,4,128]{2,1,0:T(4,128)(2,1)} %param.15) | copy-start | bytes 24580
  4.4 2.5 %copy-start.1 = (bf16[2,160,8192]{2,1,0:T(8,128)(2,1)S(1)}, bf16[2,160,8192]{2,1,0:T(8,128)(2,1)}, u32[]{:S(2)}) copy-start(bf16[2,160,8192]{2,1,0:T(8,128)(2,1)} %param.8) | copy-start | bytes 15728644
  11.4 75.7 %collective-permute-start.18 = (bf16[8,320,512]{2,1,0:T(8,128)(2,1)}, bf16[8,320,512]{2,1,0:T(8,128)(2,1)}, u32[]{:S(2)}, u32[]{:S(2)}) collective-permute-start(bf16[8,320,512]{2,1,0:T(8,128)(2,1)} %get-tuple-element.48), channel_id=1, source_target_pairs={{0,1},{1,0},{2,3},{3,2},{4,5},{5,4},{6,7},{7,6},{8,9},{9,8},{10,11... | collective-permute-start | bytes 7864328 | tf_op jit(solution)/shard_map/ppermute | solution.py:65
  12.0 21.2 %collective-permute-start.4 = (bf16[384,512]{1,0:T(8,128)(2,1)S(1)}, bf16[384,512]{1,0:T(8,128)(2,1)S(1)}, u32[]{:S(2)}, u32[]{:S(2)}) collective-permute-start(bf16[384,512]{1,0:T(8,128)(2,1)S(1)} %get-tuple-element.35), channel_id=1, source_target_pairs={{4,8},{5,9},{6,10},{7,11},{8,4},{9,5},{10,6},{11,7},{20,24},{21,25... | collective-permute-start | bytes 1179656 | tf_op jit(solution)/shard_map/ppermute | solution.py:65
  12.7 22.5 %collective-permute-start = (bf16[384,512]{1,0:T(8,128)(2,1)S(1)}, bf16[384,512]{1,0:T(8,128)(2,1)S(1)}, u32[]{:S(2)}, u32[]{:S(2)}) collective-permute-start(bf16[384,512]{1,0:T(8,128)(2,1)S(1)} %get-tuple-element.35), channel_id=1, source_target_pairs={{0,4},{1,5},{2,6},{3,7},{4,0},{5,1},{6,2},{7,3},{8,12},{9,13},{10,... | collective-permute-start | bytes 1179656 | tf_op jit(solution)/shard_map/ppermute | solution.py:65
  18.0 9.2 %collective-permute-start.1 = (bf16[256,512]{1,0:T(8,128)(2,1)S(1)}, bf16[256,512]{1,0:T(8,128)(2,1)S(1)}, u32[]{:S(2)}, u32[]{:S(2)}) collective-permute-start(bf16[256,512]{1,0:T(8,128)(2,1)S(1)} %get-tuple-element.36), channel_id=1, source_target_pairs={{0,2},{1,3},{2,0},{3,1},{4,6},{5,7},{6,4},{7,5},{8,10},{9,11},{10,... | collective-permute-start | bytes 786440 | tf_op jit(solution)/shard_map/ppermute | solution.py:65
  19.5 12.3 %collective-permute-start.3 = (bf16[256,512]{1,0:T(8,128)(2,1)S(1)}, bf16[256,512]{1,0:T(8,128)(2,1)S(1)}, u32[]{:S(2)}, u32[]{:S(2)}) collective-permute-start(bf16[256,512]{1,0:T(8,128)(2,1)S(1)} %get-tuple-element.39), channel_id=1, source_target_pairs={{0,2},{1,3},{2,0},{3,1},{4,6},{5,7},{6,4},{7,5},{8,10},{9,11},{10,... | collective-permute-start | bytes 786440 | tf_op jit(solution)/shard_map/ppermute | solution.py:65
  27.2 18.0 %copy-start.16 = (bf16[256,512]{1,0:T(8,128)(2,1)}, bf16[256,512]{1,0:T(8,128)(2,1)S(1)}, u32[]{:S(2)}) copy-start(bf16[256,512]{1,0:T(8,128)(2,1)S(1)} %collective-permute-done.1.refs_1_.refs_4_) | copy-start | bytes 786436
  27.2 11.0 %collective-permute-start.2 = (bf16[384,512]{1,0:T(8,128)(2,1)S(1)}, bf16[384,512]{1,0:T(8,128)(2,1)S(1)}, u32[]{:S(2)}, u32[]{:S(2)}) collective-permute-start(bf16[384,512]{1,0:T(8,128)(2,1)S(1)} %get-tuple-element.38), channel_id=1, source_target_pairs={{0,4},{1,5},{2,6},{3,7},{4,0},{5,1},{6,2},{7,3},{8,12},{9,13},{10,... | collective-permute-start | bytes 1179656 | tf_op jit(solution)/shard_map/ppermute | solution.py:65
  31.8 17.0 %copy-start.14 = (bf16[256,512]{1,0:T(8,128)(2,1)}, bf16[256,512]{1,0:T(8,128)(2,1)S(1)}, u32[]{:S(2)}) copy-start(bf16[256,512]{1,0:T(8,128)(2,1)S(1)} %collective-permute-done.3.refs_1_.refs_4_) | copy-start | bytes 786436
  31.8 7.8 %collective-permute-start.7 = (bf16[384,512]{1,0:T(8,128)(2,1)S(1)}, bf16[384,512]{1,0:T(8,128)(2,1)}, u32[]{:S(2)}, u32[]{:S(2)}) collective-permute-start(bf16[384,512]{1,0:T(8,128)(2,1)S(1)} %get-tuple-element.38), channel_id=1, source_target_pairs={{4,8},{5,9},{6,10},{7,11},{8,4},{9,5},{10,6},{11,7},{20,24},{21,25... | collective-permute-start | bytes 1179656 | tf_op jit(solution)/shard_map/ppermute | solution.py:65
  33.2 12.0 %collective-permute-start.5 = (bf16[384,512]{1,0:T(8,128)(2,1)S(1)}, bf16[384,512]{1,0:T(8,128)(2,1)S(1)}, u32[]{:S(2)}, u32[]{:S(2)}) collective-permute-start(bf16[384,512]{1,0:T(8,128)(2,1)S(1)} %collective-permute-done.4.refs_1_), channel_id=1, source_target_pairs={{4,0},{5,1},{6,2},{7,3},{8,12},{9,13},{10,14},{11,15},{20,16},{21,... | collective-permute-start | bytes 1179656 | tf_op jit(solution)/shard_map/ppermute | solution.py:65
  35.2 5.6 %copy-start.7 = (bf16[384,512]{1,0:T(8,128)(2,1)}, bf16[384,512]{1,0:T(8,128)(2,1)S(1)}, u32[]{:S(2)}) copy-start(bf16[384,512]{1,0:T(8,128)(2,1)S(1)} %collective-permute-done.refs_0_.refs_3_) | copy-start | bytes 1179652
  35.2 13.5 %collective-permute-start.6 = (bf16[384,512]{1,0:T(8,128)(2,1)S(1)}, bf16[384,512]{1,0:T(8,128)(2,1)S(1)}, u32[]{:S(2)}, u32[]{:S(2)}) collective-permute-start(bf16[384,512]{1,0:T(8,128)(2,1)S(1)} %collective-permute-done.refs_0_.refs_3_), channel_id=1, source_target_pairs={{0,2},{1,3},{2,0},{3,1},{4,6},{5,7},{6,4},{7,5},{8,10},{9,11},{10,... | collective-permute-start | bytes 1179656 | tf_op jit(solution)/shard_map/ppermute | solution.py:65
  38.2 21.1 %copy-start.5 = (bf16[384,512]{1,0:T(8,128)(2,1)}, bf16[384,512]{1,0:T(8,128)(2,1)S(1)}, u32[]{:S(2)}) copy-start(bf16[384,512]{1,0:T(8,128)(2,1)S(1)} %collective-permute-done.2.refs_0_.refs_3_) | copy-start | bytes 1179652
  38.2 18.0 %collective-permute-start.10 = (bf16[256,512]{1,0:T(8,128)(2,1)}, bf16[256,512]{1,0:T(8,128)(2,1)}, u32[]{:S(2)}, u32[]{:S(2)}) collective-permute-start(bf16[256,512]{1,0:T(8,128)(2,1)} %get-tuple-element.43), channel_id=1, source_target_pairs={{4,8},{5,9},{6,10},{7,11},{8,4},{9,5},{10,6},{11,7},{20,24},{21,25... | collective-permute-start | bytes 786440 | tf_op jit(solution)/shard_map/ppermute | solution.py:65
  39.6 18.4 %collective-permute-start.8 = (bf16[384,512]{1,0:T(8,128)(2,1)}, bf16[384,512]{1,0:T(8,128)(2,1)}, u32[]{:S(2)}, u32[]{:S(2)}) collective-permute-start(bf16[384,512]{1,0:T(8,128)(2,1)} %collective-permute-done.7.refs_1_), channel_id=1, source_target_pairs={{4,0},{5,1},{6,2},{7,3},{8,12},{9,13},{10,14},{11,15},{20,16},{21,... | collective-permute-start | bytes 1179656 | tf_op jit(solution)/shard_map/ppermute | solution.py:65
  45.2 4.3 %copy-start.31 = (bf16[384,512]{1,0:T(8,128)(2,1)}, bf16[384,512]{1,0:T(8,128)(2,1)S(1)}, u32[]{:S(2)}) copy-start(bf16[384,512]{1,0:T(8,128)(2,1)S(1)} %collective-permute-done.5.refs_0_) | copy-start | bytes 1179652
  45.2 14.1 %collective-permute-start.9 = (bf16[384,512]{1,0:T(8,128)(2,1)S(1)}, bf16[384,512]{1,0:T(8,128)(2,1)}, u32[]{:S(2)}, u32[]{:S(2)}) collective-permute-start(bf16[384,512]{1,0:T(8,128)(2,1)S(1)} %collective-permute-done.2.refs_0_.refs_3_), channel_id=1, source_target_pairs={{0,2},{1,3},{2,0},{3,1},{4,6},{5,7},{6,4},{7,5},{8,10},{9,11},{10,... | collective-permute-start | bytes 1179656 | tf_op jit(solution)/shard_map/ppermute | solution.py:65
  48.7 29.5 %copy-start.35 = (s32[2]{0:T(128)S(1)}, s32[2]{0:T(128)}, u32[]{:S(2)}) copy-start(s32[2]{0:T(128)} %lengths.3) | copy-start | bytes 28
  49.5 7.2 %collective-permute-start.13 = (bf16[256,512]{1,0:T(8,128)(2,1)}, bf16[256,512]{1,0:T(8,128)(2,1)}, u32[]{:S(2)}, u32[]{:S(2)}) collective-permute-start(bf16[256,512]{1,0:T(8,128)(2,1)} %get-tuple-element.45), channel_id=1, source_target_pairs={{4,8},{5,9},{6,10},{7,11},{8,4},{9,5},{10,6},{11,7},{20,24},{21,25... | collective-permute-start | bytes 786440 | tf_op jit(solution)/shard_map/ppermute | solution.py:65
  56.2 5.2 %copy-start.2 = (bf16[384,512]{1,0:T(8,128)(2,1)}, bf16[384,512]{1,0:T(8,128)(2,1)S(1)}, u32[]{:S(2)}) copy-start(bf16[384,512]{1,0:T(8,128)(2,1)S(1)} %get-tuple-element.41.token_ref.refs_5_) | copy-start | bytes 1179652
  56.2 13.0 %collective-permute-start.12 = (bf16[384,512]{1,0:T(8,128)(2,1)S(1)}, bf16[384,512]{1,0:T(8,128)(2,1)S(1)}, u32[]{:S(2)}, u32[]{:S(2)}) collective-permute-start(bf16[384,512]{1,0:T(8,128)(2,1)S(1)} %get-tuple-element.41.token_ref.refs_5_), channel_id=1, source_target_pairs={{0,2},{1,3},{2,0},{3,1},{4,6},{5,7},{6,4},{7,5},{8,10},{9,11},{10,... | collective-permute-start | bytes 1179656 | tf_op jit(solution)/shard_map/ppermute | solution.py:65
  56.7 10.9 %collective-permute-start.11 = (bf16[256,512]{1,0:T(8,128)(2,1)}, bf16[256,512]{1,0:T(8,128)(2,1)S(1)}, u32[]{:S(2)}, u32[]{:S(2)}) collective-permute-start(bf16[256,512]{1,0:T(8,128)(2,1)} %collective-permute-done.10.refs_1_), channel_id=1, source_target_pairs={{4,0},{5,1},{6,2},{7,3},{8,12},{9,13},{10,14},{11,15},{20,16},{21,... | collective-permute-start | bytes 786440 | tf_op jit(solution)/shard_map/ppermute | solution.py:65
  58.0 12.9 %copy-start.45 = (f32[64]{0:T(128)}, f32[64]{0:T(128)S(1)}, u32[]{:S(2)}) copy-start(f32[64]{0:T(128)S(1)} %multiply_power_fusion) | copy-start | bytes 772
  58.0 19.7 %collective-permute-start.14 = (bf16[256,512]{1,0:T(8,128)(2,1)}, bf16[256,512]{1,0:T(8,128)(2,1)}, u32[]{:S(2)}, u32[]{:S(2)}) collective-permute-start(bf16[256,512]{1,0:T(8,128)(2,1)} %collective-permute-done.13.refs_1_), channel_id=1, source_target_pairs={{4,0},{5,1},{6,2},{7,3},{8,12},{9,13},{10,14},{11,15},{20,16},{21,... | collective-permute-start | bytes 786440 | tf_op jit(solution)/shard_map/ppermute | solution.py:65
  61.3 17.6 %collective-permute-start.15 = (bf16[384,512]{1,0:T(8,128)(2,1)S(1)}, bf16[384,512]{1,0:T(8,128)(2,1)}, u32[]{:S(2)}, u32[]{:S(2)}) collective-permute-start(bf16[384,512]{1,0:T(8,128)(2,1)S(1)} %get-tuple-element.42.token_ref.refs_5_), channel_id=1, source_target_pairs={{0,2},{1,3},{2,0},{3,1},{4,6},{5,7},{6,4},{7,5},{8,10},{9,11},{10,... | collective-permute-start | bytes 1179656 | tf_op jit(solution)/shard_map/ppermute | solution.py:65
  67.6 17.8 %collective-permute-start.21 = (bf16[384,512]{1,0:T(8,128)(2,1)}, bf16[384,512]{1,0:T(8,128)(2,1)}, u32[]{:S(2)}, u32[]{:S(2)}) collective-permute-start(bf16[384,512]{1,0:T(8,128)(2,1)} %get-tuple-element.37.token_ref), channel_id=1, source_target_pairs={{0,16},{1,17},{2,18},{3,19},{4,20},{5,21},{6,22},{7,23},{8,24},{9,... | collective-permute-start | bytes 1179656 | tf_op jit(solution)/shard_map/ppermute | solution.py:65
  72.4 10.8 %collective-permute-start.16 = (bf16[256,512]{1,0:T(8,128)(2,1)}, bf16[256,512]{1,0:T(8,128)(2,1)}, u32[]{:S(2)}, u32[]{:S(2)}) collective-permute-start(bf16[256,512]{1,0:T(8,128)(2,1)} %get-tuple-element.44.token_ref.refs_2_), channel_id=1, source_target_pairs={{0,2},{1,3},{2,0},{3,1},{4,6},{5,7},{6,4},{7,5},{8,10},{9,11},{10,... | collective-permute-start | bytes 786440 | tf_op jit(solution)/shard_map/ppermute | solution.py:65
  77.8 18.4 %collective-permute-start.20 = (bf16[384,512]{1,0:T(8,128)(2,1)}, bf16[384,512]{1,0:T(8,128)(2,1)}, u32[]{:S(2)}, u32[]{:S(2)}) collective-permute-start(bf16[384,512]{1,0:T(8,128)(2,1)} %copy-done.37), channel_id=1, source_target_pairs={{0,16},{1,17},{2,18},{3,19},{4,20},{5,21},{6,22},{7,23},{8,24},{9,... | collective-permute-start | bytes 1179656 | tf_op jit(solution)/shard_map/ppermute | solution.py:65
  78.9 16.8 %collective-permute-start.19 = (bf16[256,512]{1,0:T(8,128)(2,1)}, bf16[256,512]{1,0:T(8,128)(2,1)S(1)}, u32[]{:S(2)}, u32[]{:S(2)}) collective-permute-start(bf16[256,512]{1,0:T(8,128)(2,1)} %copy-done.38), channel_id=1, source_target_pairs={{0,16},{1,17},{2,18},{3,19},{4,20},{5,21},{6,22},{7,23},{8,24},{9,... | collective-permute-start | bytes 786440 | tf_op jit(solution)/shard_map/ppermute | solution.py:65
  83.2 12.0 %copy-start.18 = (bf16[256,512]{1,0:T(8,128)(2,1)}, bf16[256,512]{1,0:T(8,128)(2,1)S(1)}, u32[]{:S(2)}) copy-start(bf16[256,512]{1,0:T(8,128)(2,1)S(1)} %get-tuple-element.46.token_ref.refs_2_) | copy-start | bytes 786436
  84.3 17.0 %collective-permute-start.17 = (bf16[256,512]{1,0:T(8,128)(2,1)S(1)}, bf16[256,512]{1,0:T(8,128)(2,1)S(1)}, u32[]{:S(2)}, u32[]{:S(2)}) collective-permute-start(bf16[256,512]{1,0:T(8,128)(2,1)S(1)} %cut_last.2.token_ref), channel_id=1, source_target_pairs={{0,16},{1,17},{2,18},{3,19},{4,20},{5,21},{6,22},{7,23},{8,24},{9,... | collective-permute-start | bytes 786440 | tf_op jit(solution)/shard_map/ppermute | solution.py:65
  85.4 25.2 %collective-permute-start.27 = (bf16[384,512]{1,0:T(8,128)(2,1)}, bf16[384,512]{1,0:T(8,128)(2,1)}, u32[]{:S(2)}, u32[]{:S(2)}) collective-permute-start(bf16[384,512]{1,0:T(8,128)(2,1)} %copy-done.27), channel_id=1, source_target_pairs={{0,16},{1,17},{2,18},{3,19},{4,20},{5,21},{6,22},{7,23},{8,24},{9,... | collective-permute-start | bytes 1179656 | tf_op jit(solution)/shard_map/ppermute | solution.py:65
  87.1 19.3 %collective-permute-start.23 = (bf16[256,512]{1,0:T(8,128)(2,1)S(1)}, bf16[256,512]{1,0:T(8,128)(2,1)S(1)}, u32[]{:S(2)}, u32[]{:S(2)}) collective-permute-start(bf16[256,512]{1,0:T(8,128)(2,1)S(1)} %get-tuple-element.46.token_ref.refs_2_), channel_id=1, source_target_pairs={{0,2},{1,3},{2,0},{3,1},{4,6},{5,7},{6,4},{7,5},{8,10},{9,11},{10,... | collective-permute-start | bytes 786440 | tf_op jit(solution)/shard_map/ppermute | solution.py:65
  91.5 4.6 %copy-start.13 = (bf16[384,512]{1,0:T(8,128)(2,1)S(1)}, bf16[384,512]{1,0:T(8,128)(2,1)}, u32[]{:S(2)}) copy-start(bf16[384,512]{1,0:T(8,128)(2,1)} %copy-done.12) | copy-start | bytes 1179652
  95.7 24.9 %collective-permute-start.26 = (bf16[384,512]{1,0:T(8,128)(2,1)}, bf16[384,512]{1,0:T(8,128)(2,1)}, u32[]{:S(2)}, u32[]{:S(2)}) collective-permute-start(bf16[384,512]{1,0:T(8,128)(2,1)} %get-tuple-element.58), channel_id=1, source_target_pairs={{0,16},{1,17},{2,18},{3,19},{4,20},{5,21},{6,22},{7,23},{8,24},{9,... | collective-permute-start | bytes 1179656 | tf_op jit(solution)/shard_map/ppermute | solution.py:65
  101.3 3.0 %copy-start.46 = (f32[64]{0:T(128)S(1)}, f32[64]{0:T(128)}, u32[]{:S(2)}) copy-start(f32[64]{0:T(128)} %copy-done.45) | copy-start | bytes 772
  101.3 4.3 %copy-start.39 = (f32[160,64]{1,0:T(8,128)S(1)}, f32[160,64]{1,0:T(8,128)}, u32[]{:S(2)}) copy-start(f32[160,64]{1,0:T(8,128)} %get-tuple-element.70) | copy-start | bytes 122884
  101.3 4.3 %copy-start.40 = (f32[160,64]{1,0:T(8,128)S(1)}, f32[160,64]{1,0:T(8,128)}, u32[]{:S(2)}) copy-start(f32[160,64]{1,0:T(8,128)} %get-tuple-element.71) | copy-start | bytes 122884
  101.3 4.3 %copy-start.41 = (f32[160,64]{1,0:T(8,128)S(1)}, f32[160,64]{1,0:T(8,128)}, u32[]{:S(2)}) copy-start(f32[160,64]{1,0:T(8,128)} %get-tuple-element.72) | copy-start | bytes 122884
  101.3 9.3 %copy-start.6 = (bf16[384,512]{1,0:T(8,128)(2,1)S(1)}, bf16[384,512]{1,0:T(8,128)(2,1)}, u32[]{:S(2)}) copy-start(bf16[384,512]{1,0:T(8,128)(2,1)} %copy-done.5) | copy-start | bytes 1179652
  104.3 5.0 %copy-start.22 = (f32[320,512]{1,0:T(8,128)}, f32[320,512]{1,0:T(8,128)S(1)}, u32[]{:S(2)}) copy-start(f32[320,512]{1,0:T(8,128)S(1)} %get-tuple-element.55.refs_0_) | copy-start | bytes 1966084
  104.3 22.6 %collective-permute-start.22 = (f32[320,512]{1,0:T(8,128)}, f32[320,512]{1,0:T(8,128)}, u32[]{:S(2)}, u32[]{:S(2)}) collective-permute-start(f32[320,512]{1,0:T(8,128)} %get-tuple-element.56), channel_id=1, source_target_pairs={{0,1},{1,0},{2,3},{3,2},{4,5},{5,4},{6,7},{7,6},{8,9},{9,8},{10,11... | collective-permute-start | bytes 1966088 | tf_op jit(solution)/shard_map/ppermute | solution.py:65
  105.2 15.4 %collective-permute-start.25 = (bf16[256,512]{1,0:T(8,128)(2,1)}, bf16[256,512]{1,0:T(8,128)(2,1)}, u32[]{:S(2)}, u32[]{:S(2)}) collective-permute-start(bf16[256,512]{1,0:T(8,128)(2,1)} %get-tuple-element.57), channel_id=1, source_target_pairs={{0,16},{1,17},{2,18},{3,19},{4,20},{5,21},{6,22},{7,23},{8,24},{9,... | collective-permute-start | bytes 786440 | tf_op jit(solution)/shard_map/ppermute | solution.py:65
  106.4 1.3 copy-start.20
  107.7 16.1 %collective-permute-start.24 = (bf16[256,512]{1,0:T(8,128)(2,1)}, bf16[256,512]{1,0:T(8,128)(2,1)}, u32[]{:S(2)}, u32[]{:S(2)}) collective-permute-start(bf16[256,512]{1,0:T(8,128)(2,1)} %cut_last.3.token_ref), channel_id=1, source_target_pairs={{0,16},{1,17},{2,18},{3,19},{4,20},{5,21},{6,22},{7,23},{8,24},{9,... | collective-permute-start | bytes 786440 | tf_op jit(solution)/shard_map/ppermute | solution.py:65
  112.6 8.0 %copy-start.19 = (bf16[256,512]{1,0:T(8,128)(2,1)S(1)}, bf16[256,512]{1,0:T(8,128)(2,1)}, u32[]{:S(2)}) copy-start(bf16[256,512]{1,0:T(8,128)(2,1)} %copy-done.18) | copy-start | bytes 786436
  112.6 8.0 %copy-start.21 = (bf16[256,512]{1,0:T(8,128)(2,1)S(1)}, bf16[256,512]{1,0:T(8,128)(2,1)}, u32[]{:S(2)}) copy-start(bf16[256,512]{1,0:T(8,128)(2,1)} %copy-done.20) | copy-start | bytes 786436
  123.8 3.1 %copy-start.23 = (f32[320,512]{1,0:T(8,128)S(1)}, f32[320,512]{1,0:T(8,128)}, u32[]{:S(2)}) copy-start(f32[320,512]{1,0:T(8,128)} %copy-done.22) | copy-start | bytes 1966084
  123.8 3.1 %copy-start.33 = (f32[160,128]{1,0:T(8,128)S(1)}, f32[160,128]{1,0:T(8,128)}, u32[]{:S(2)}) copy-start(f32[160,128]{1,0:T(8,128)} %get-tuple-element.79.refs_2_) | copy-start | bytes 245764
  123.8 3.1 %copy-start.34 = (f32[160,128]{1,0:T(8,128)S(1)}, f32[160,128]{1,0:T(8,128)}, u32[]{:S(2)}) copy-start(f32[160,128]{1,0:T(8,128)} %get-tuple-element.80.refs_3_) | copy-start | bytes 245764
  123.8 3.1 %copy-start.36 = (s32[8]{0:T(128)S(1)}, s32[8]{0:T(128)}, u32[]{:S(2)}) copy-start(s32[8]{0:T(128)} %owner.3) | copy-start | bytes 100
  123.8 10.7 %copy-start.42 = (f32[1,4,8,128]{3,1,2,0:T(4,128)S(1)}, f32[1,4,8,128]{3,1,2,0:T(4,128)}, u32[]{:S(2)}) copy-start(f32[1,4,8,128]{3,1,2,0:T(4,128)} %convert_bitcast_fusion) | copy-start | bytes 49156
  123.9 11.4 %copy-start.43 = (f32[4,64]{1,0:T(4,128)S(1)}, f32[4,64]{1,0:T(4,128)}, u32[]{:S(2)}) copy-start(f32[4,64]{1,0:T(4,128)} %get-tuple-element.73) | copy-start | bytes 3076
  123.9 11.4 %copy-start.44 = (f32[4,64]{1,0:T(4,128)S(1)}, f32[4,64]{1,0:T(4,128)}, u32[]{:S(2)}) copy-start(f32[4,64]{1,0:T(4,128)} %get-tuple-element.74) | copy-start | bytes 3076
  123.9 11.5 %copy-start.47 = (bf16[4,64]{1,0:T(4,128)(2,1)S(1)}, bf16[4,64]{1,0:T(4,128)(2,1)}, u32[]{:S(2)}) copy-start(bf16[4,64]{1,0:T(4,128)(2,1)} %get-tuple-element.68) | copy-start | bytes 1540
  123.9 11.4 %copy-start.48 = (bf16[4,64]{1,0:T(4,128)(2,1)S(1)}, bf16[4,64]{1,0:T(4,128)(2,1)}, u32[]{:S(2)}) copy-start(bf16[4,64]{1,0:T(4,128)(2,1)} %get-tuple-element.69) | copy-start | bytes 1540
  126.9 8.7 %collective-permute-start.28 = (f32[320,512]{1,0:T(8,128)}, f32[320,512]{1,0:T(8,128)S(1)}, u32[]{:S(2)}, u32[]{:S(2)}) collective-permute-start(f32[320,512]{1,0:T(8,128)} %get-tuple-element.65), channel_id=1, source_target_pairs={{0,1},{1,0},{2,3},{3,2},{4,5},{5,4},{6,7},{7,6},{8,9},{9,8},{10,11... | collective-permute-start | bytes 1966088 | tf_op jit(solution)/shard_map/ppermute | solution.py:65
  129.6 16.0 %all-to-all-start = ((bf16[16,80,128]{2,1,0:T(8,128)(2,1)}), bf16[16,80,128]{2,1,0:T(8,128)(2,1)S(1)}, u32[]{:S(2)}, u32[]{:S(2)}) async-start(bf16[16,80,128]{2,1,0:T(8,128)(2,1)} %cache_rows.2), calls=%async_computation | async-start | bytes 655360 | tf_op jit(solution)/shard_map/all_to_all | solution.py:442
  145.7 14.6 %all-to-all-start.1 = ((bf16[16,80,128]{2,1,0:T(8,128)(2,1)}), bf16[16,80,128]{2,1,0:T(8,128)(2,1)S(1)}, u32[]{:S(2)}, u32[]{:S(2)}) async-start(bf16[16,80,128]{2,1,0:T(8,128)(2,1)} %cache_rows.3), calls=%async_computation.1 | async-start | bytes 655360 | tf_op jit(solution)/shard_map/all_to_all | solution.py:442
  149.6 1.2 collective-permute-start.29
  151.0 1.2 collective-permute-start.30
  160.5 1.2 collective-permute-start.31
  (19 other events, 17.2 us)

commit v4 on v1

--- a/solution.py
+++ b/solution.py
@@ -1,6 +1,11 @@
+import functools
+
 import jax
 import jax.numpy as jnp
+import numpy as np
 from jax import lax
+from jax.experimental import pallas as pl
+from jax.experimental.pallas import tpu as pltpu
 from jax.sharding import PartitionSpec as P
 
 HEAD_SIZE = 128
@@ -23,8 +28,8 @@
 
 
 def rope_table(positions, head_dim):
-    freq = ROPE_BASE ** (-(jnp.arange(head_dim // 2, dtype=jnp.float32) * 2.0) / head_dim)
-    angle = positions.astype(jnp.float32)[:, None] * freq[None, :]
+    freq = ROPE_BASE ** (-(np.arange(head_dim // 2, dtype=np.float64) * 2.0) / head_dim)
+    angle = positions.astype(jnp.float32)[:, None] * jnp.asarray(freq, jnp.float32)[None, :]
     return (jnp.cos(angle), jnp.sin(angle))
 
 
@@ -54,10 +59,8 @@
     route = []
     for g in range(groups):
         for s in range(seq):
-            place = rule(g, s // 2 // low, s // 2 % low, s % 2)
-            if place is not None:
-                tg, tz, ty, tc = place
-                route.append((g * seq + s, tg * seq + (tz * low + ty) * 2 + tc))
+            tg, tz, ty, tc = rule(g, s // 2 // low, s // 2 % low, s % 2)
+            route.append((g * seq + s, tg * seq + (tz * low + ty) * 2 + tc))
     return lax.ppermute(block, ("groups", "seq"), route)
 
 
@@ -73,50 +76,238 @@
     return (1 - g, z, y, c)
 
 
-def to_pair(g, z, y, c):
-    return (g, z ^ 1, y, c)
-
-
-def to_middle(g, z, y, c):
-    return (g, 3 - z, y, c) if z in (1, 2) else None
-
-
-def to_end(g, z, y, c):
-    return (g, 0 if z == 1 else 3, y, c) if z in (1, 2) else None
-
-
-def mirrored(block, axis, flag):
-    quarter = block.shape[axis] // 4
-    parts = [lax.slice_in_dim(block, i * quarter, (i + 1) * quarter, axis=axis) for i in range(4)]
-    return jnp.where(flag, jnp.concatenate(parts[::-1], axis), block)
-
-
-def gathered_blocks(weight, z, y, g):
-    quarter = weight.shape[0] // 4
-    own = mirrored(weight, 0, g == 1)
-    is_end = (z == 0) | (z == 3)
-    main = own[: 3 * quarter]
-    near = moved(main, to_pair)
-    mid_b = moved(main, to_middle)
-    mid_c = moved(near, to_middle)
-    end_b = moved(mid_b, to_end)
-    end_c = moved(mid_c, to_end)
-    slot_b = jnp.where(is_end, end_b, mid_b)
-    slot_c = jnp.where(is_end, end_c, mid_c)
-    z_a, z_b, z_c = z ^ 1, jnp.where(z < 2, 2, 1), jnp.where(z < 2, 3, 0)
-    pieces = [(z, y, 0, own)]
-    for zz, block, share in ((z, main, 2), (z_a, near, 2), (z_b, slot_b, 3), (z_c, slot_c, 3)):
-        if block is not main:
-            pieces.append((zz, y, 0, block))
-            pieces.append((zz, y, 3 * quarter, moved(block[:quarter], to_group)))
-        across = moved(block[: share * quarter], to_row)
-        pieces.append((zz, 1 - y, 0, across))
-        if share == 2:
-            onward = jnp.concatenate([across[quarter:], across[:quarter]], 0)
+def along(bits):
+    return lambda g, z, y, c: (g, z ^ bits, y, c)
+
+
+VMEM_REF = pl.BlockSpec(memory_space=pltpu.VMEM)
+SMEM_REF = pl.BlockSpec(memory_space=pltpu.SMEM)
+ANY_REF = pl.BlockSpec(memory_space=pl.ANY)
+PARAMS = pltpu.CompilerParams(vmem_limit_bytes=56 << 20)
+
+
+def cost(flops, moved_bytes):
+    return pl.CostEstimate(flops=flops, bytes_accessed=moved_bytes, transcendentals=0)
+
+
+def halves_kernel(place, *refs):
+    sems = refs[-1]
+    count = (len(refs) - 1) // 3
+    rows = refs[count].shape[0]
+    copies = []
+    for k, weight in enumerate(refs[:count]):
+        for part in range(2):
+            first = (place[0] if part == 0 else 1 - place[0]) * rows
+            source = weight.at[pl.ds(pl.multiple_of(first, rows), rows)]
+            target = refs[count + 2 * k + part]
+            copies.append(pltpu.make_async_copy(source, target, sems.at[2 * k + part]))
+    for copy in copies:
+        copy.start()
+    for copy in copies:
+        copy.wait()
+
+
+def weight_halves(place, weights):
+    rows, columns = weights[0].shape
+    out = jax.ShapeDtypeStruct((rows // 2, columns), weights[0].dtype)
+    outs = pl.pallas_call(
+        halves_kernel,
+        in_specs=[SMEM_REF] + [ANY_REF] * len(weights),
+        out_specs=[ANY_REF] * (2 * len(weights)),
+        out_shape=[out] * (2 * len(weights)),
+        scratch_shapes=[pltpu.SemaphoreType.DMA((2 * len(weights),))],
+        compiler_params=PARAMS,
+        cost_estimate=cost(1000, 1000),
+        name="weight_halves",
+    )(place, *weights)
+    return [outs[2 * k : 2 * k + 2] for k in range(len(weights))]
+
+
+def prepare_kernel(place, rows_in, token, mine, other):
+    depth = mine.shape[2]
+    wide = rows_in[...].astype(jnp.float32)
+    scale = lax.rsqrt(jnp.mean(wide * wide, -1, keepdims=True) + 1e-05)
+    for core in range(2):
+
+        @pl.when(place[1] == core)
+        def _():
+            for j in range(mine.shape[0] // 2):
+                for c in range(2):
+                    target = mine if c == core else other
+                    for h in range(2):
+                        first = (4 * j + 2 * c + h) * depth
+                        part = rows_in[:, first : first + depth].astype(jnp.float32)
+                        target[2 * j + h] = (part * scale).astype(jnp.bfloat16)
+
+
+def prepared(flat, place, token, blocks):
+    rows, width = flat.shape
+    depth = width // (4 * blocks)
+    tile = 64 if rows % 64 == 0 else rows
+    out = jax.ShapeDtypeStruct((2 * blocks, rows, depth), jnp.bfloat16)
+    spec = pl.BlockSpec((2 * blocks, tile, depth), lambda i, place: (0, i, 0))
+    return pl.pallas_call(
+        prepare_kernel,
+        grid_spec=pltpu.PrefetchScalarGridSpec(
+            num_scalar_prefetch=1,
+            grid=(rows // tile,),
+            in_specs=[pl.BlockSpec((tile, width), lambda i, place: (i, 0)), ANY_REF],
+            out_specs=[spec, spec],
+        ),
+        out_shape=[out, out],
+        compiler_params=PARAMS,
+        cost_estimate=cost(1 << 36, 4 * rows * width),
+        name="normed_halves",
+    )(place, flat, token)
+
+
+def fetch(source, target, sem):
+    copy = pltpu.make_async_copy(source, target, sem)
+    copy.start()
+    return copy
+
+
+def product_kernel(plan, group, with_total, place, mine, other, *refs):
+    count = len(plan)
+    pieces = refs[:count]
+    totals_in = refs[count : count + 2 * with_total]
+    outs = refs[count + 2 * with_total : count + 2 * with_total + 2]
+    left, right, total, sems, total_sems = refs[-5:]
+    rows, depth = mine.shape[1], mine.shape[2]
+    waits = []
+    for k, (entry, flipped, first) in enumerate(plan):
+        half = (1 - place[0]) if flipped == 1 else place[0]
+        half = first // depth if flipped is None else half
+        index = place[entry] * 2 + half
+        area = pl.ds((k % group) * depth, depth)
+        slot = k // group
+        waits.append(
+            [
+                fetch(mine.at[index], left.at[slot, pl.ds(0, rows), area], sems.at[3 * k]),
+                fetch(other.at[index], left.at[slot, pl.ds(rows, rows), area], sems.at[3 * k + 1]),
+                fetch(pieces[k].at[pl.ds(first, depth)], right.at[slot, area], sems.at[3 * k + 2]),
+            ]
+        )
+    carried = [
+        fetch(ref, total.at[pl.ds(k * rows, rows)], total_sems.at[k])
+        for k, ref in enumerate(totals_in)
+    ]
+    for slot in range(count // group):
+        for copies in waits[slot * group : (slot + 1) * group]:
+            for copy in copies:
+                copy.wait()
+        value = jnp.dot(left[slot], right[slot], preferred_element_type=jnp.float32)
+        if slot == 0:
+            for copy in carried:
+                copy.wait()
+        if slot or with_total:
+            value += total[...]
+        if slot + 1 < count // group:
+            total[...] = value
         else:
-            onward = across[:quarter]
-        pieces.append((zz, 1 - y, share * quarter, moved(onward, to_group)))
-    return pieces
+            outs[0][...] = value[:rows]
+            outs[1][...] = value[rows:]
+
+
+def product(place, mine, other, plan, pieces, totals, group, token):
+    _, rows, depth = mine.shape
+    columns = pieces[0].shape[1]
+    count = len(plan)
+    out = jax.ShapeDtypeStruct((rows, columns), jnp.float32)
+
+    def kernel(place_ref, token_ref, *refs):
+        product_kernel(plan, group, len(totals) // 2, place_ref, *refs)
+
+    return pl.pallas_call(
+        kernel,
+        in_specs=[SMEM_REF] + [ANY_REF] * (3 + count + len(totals)),
+        out_specs=[VMEM_REF] * 2,
+        out_shape=[out, out],
+        scratch_shapes=[
+            pltpu.VMEM((count // group, 2 * rows, group * depth), mine.dtype),
+            pltpu.VMEM((count // group, group * depth, columns), mine.dtype),
+            pltpu.VMEM((2 * rows, columns), jnp.float32),
+            pltpu.SemaphoreType.DMA((3 * count,)),
+            pltpu.SemaphoreType.DMA((2,)),
+        ],
+        compiler_params=PARAMS,
+        cost_estimate=cost(64 * rows * columns * depth * count, 1 << 22),
+        name="add_product",
+    )(place, token, mine, other, *pieces, *totals)
+
+
+def rows_kernel(plan, rotated, place, lengths, owner, mine, kept, *refs):
+    count = len(plan)
+    pieces = refs[: 2 * count]
+    total_in, came_in = refs[2 * count : 2 * count + 2]
+    turn = refs[2 * count + 2 : 4 * count]
+    out, left, right, total, came, scratch, sems = refs[-7:]
+    rows, depth = mine.shape[1], mine.shape[2]
+    waits = [fetch(total_in, total, sems.at[0]), fetch(came_in, came, sems.at[1])]
+    sem = 2
+    for k in range(2 * count):
+        entry, flipped, first = plan[k // 2]
+        half = (1 - place[0]) if flipped else place[0]
+        source = (mine, kept)[k % 2]
+        area = pl.ds(k * depth, depth)
+        waits.append(fetch(source.at[place[entry] * 2 + half], left.at[:, area], sems.at[sem]))
+        waits.append(fetch(pieces[k], right.at[area], sems.at[sem + 1]))
+        sem += 2
+    for copy in waits:
+        copy.wait()
+    total[...] += came[...]
+    total[...] += jnp.dot(left[...], right[...], preferred_element_type=jnp.float32)
+    count_requests, count_rows = lengths.shape[0], scratch.shape[0]
+    index = place[2] * count_rows + lax.broadcasted_iota(jnp.int32, scratch.shape, 0)
+    for r in range(count_requests):
+        live = index < lengths[r]
+        for h in range(KEY_VALUE_HEADS):
+            part = total[
+                r * count_rows : (r + 1) * count_rows, h * HEAD_SIZE : (h + 1) * HEAD_SIZE
+            ]
+            if rotated:
+                turned = jnp.concatenate([part[:, HEAD_SIZE // 2 :], part[:, : HEAD_SIZE // 2]], 1)
+                part = part * turn[0][...] + turned * turn[1][...]
+            scratch[...] = jnp.where(live, part, 0.0)
+            peer = owner[r * KEY_VALUE_HEADS + h]
+            for b in range(2):
+                picked = scratch[pl.ds(b, count_rows // 2, stride=2), :]
+                out[peer * 2 + b] = picked.astype(jnp.bfloat16)
+
+
+def outgoing_rows(place, lengths, owner, mine, kept, plan, pieces, total, came, turn, token):
+    _, rows, depth = mine.shape
+    columns = total.shape[1]
+    count = len(plan)
+    count_rows = rows // lengths.shape[0]
+    out = jax.ShapeDtypeStruct((owner.shape[0] * 2, count_rows // 2, HEAD_SIZE), jnp.bfloat16)
+
+    def kernel(place_ref, lengths_ref, owner_ref, token_ref, *refs):
+        rows_kernel(plan, bool(turn), place_ref, lengths_ref, owner_ref, *refs)
+
+    operands = [mine, kept, *pieces, total, came]
+    return pl.pallas_call(
+        kernel,
+        in_specs=[SMEM_REF] * 3
+        + [ANY_REF] * (1 + len(operands))
+        + [VMEM_REF] * len(turn),
+        out_specs=VMEM_REF,
+        out_shape=out,
+        scratch_shapes=[
+            pltpu.VMEM((rows, 2 * count * depth), mine.dtype),
+            pltpu.VMEM((2 * count * depth, columns), mine.dtype),
+            pltpu.VMEM((rows, columns), jnp.float32),
+            pltpu.VMEM((rows, columns), jnp.float32),
+            pltpu.VMEM((count_rows, HEAD_SIZE), jnp.float32),
+            pltpu.SemaphoreType.DMA((2 + 4 * count,)),
+        ],
+        compiler_params=PARAMS,
+        cost_estimate=cost(4 * rows * columns * depth * count, 1 << 22),
+        name="cache_rows",
+    )(place, lengths, owner, token, *operands, *turn)
+
+
+HERE, THERE = 3, 7
 
 
 def body(hidden, key_weight, value_weight, lengths, owner, dec_query, dec_key, dec_value):
@@ -132,34 +323,22 @@
     positions = device_id * count_rows + jnp.arange(count_rows, dtype=jnp.int32)
     total_rows = count_requests * count_rows
     flat = hidden.reshape(total_rows, width)
-    widened = flat.astype(jnp.float32)
-    row_scale = lax.rsqrt(jnp.mean(widened * widened, -1, keepdims=True) + 1e-05)
-
     if planned:
         core = device_id % 2
         z, y = device_id // 4, device_id // 2 % 2
-        blocks = seq // 2
-        depth = width // seq
-        split_cols = flat.reshape(total_rows, blocks, 2, depth)
-        ordered = mirrored(split_cols, 3, group_id == 1)
-        mine = jnp.where(core == 0, ordered[:, :, 0], ordered[:, :, 1])
-        other = jnp.where(core == 0, ordered[:, :, 1], ordered[:, :, 0])
-        mine = jnp.transpose(mine, (1, 0, 2))
-        other = moved(jnp.transpose(other, (1, 0, 2)), to_core)
-        left = jnp.concatenate([mine, other], 1)
-
-        def project(weight):
-            total = jnp.zeros((2 * total_rows, weight.shape[1]), jnp.float32)
-            for zz, yy, first, piece in gathered_blocks(weight, z, y, group_id):
-                part = lax.dynamic_index_in_dim(left, zz * 2 + yy, 0, keepdims=False)
-                part = part[:, first : first + piece.shape[0]]
-                total = total + jnp.dot(part, piece, preferred_element_type=jnp.float32)
-            return total[:total_rows] + moved(total[total_rows:], to_core)
+        place = [group_id, core, device_id]
+        place += [(z ^ bits) * 2 + y for bits in range(4)]
+        place += [(z ^ bits) * 2 + 1 - y for bits in range(4)]
+        place = jnp.stack([jnp.asarray(entry, jnp.int32) for entry in place])
     else:
+        widened = flat.astype(jnp.float32)
+        normed = (
+            widened * lax.rsqrt(jnp.mean(widened * widened, -1, keepdims=True) + 1e-05)
+        ).astype(jnp.bfloat16)
 
         def project(weight):
             whole = lax.all_gather(weight, "seq", axis=0, tiled=True)
-            return jnp.dot(flat, whole, preferred_element_type=jnp.float32)
+            return jnp.dot(normed, whole, preferred_element_type=jnp.float32)
 
     pair_ids = jnp.arange(decode_peers, dtype=jnp.int32)
     matches = owner[None, :] == pair_ids[:, None]
@@ -177,13 +356,58 @@
         )
         return lax.all_to_all(outgoing, "seq", split_axis=0, concat_axis=1, tiled=True)[0]
 
-    shape = (count_requests, count_rows, KEY_VALUE_HEADS, HEAD_SIZE)
-    unrotated_key = (project(key_weight) * row_scale).reshape(shape)
     cosine, sine_part = rope_table(positions, HEAD_SIZE)
-    key_rows = rotate(unrotated_key, cosine[:, None, :], sine_part[:, None, :]).astype(jnp.bfloat16)
-    cache_keys = handed_over(key_rows)
-    value_rows = (project(value_weight) * row_scale).astype(jnp.bfloat16).reshape(shape)
-    cache_values = handed_over(value_rows)
+    if planned:
+        turn = (
+            jnp.concatenate([cosine, cosine], 1),
+            jnp.concatenate([-sine_part, sine_part], 1),
+        )
+        weights = (key_weight, value_weight)
+        halves = weight_halves(place, weights)
+        near = [moved(half, along(1)) for half, _ in halves]
+        across = [moved(half, to_row) for half, _ in halves]
+        far = [[moved(half, along(bits)) for bits in (2, 3)] for half, _ in halves]
+        near_rest = [moved(rest, along(1)) for _, rest in halves]
+        mine, kept = prepared(flat, place, halves[0][0], seq // 2)
+        other = moved(kept, to_core)
+        across_x = [moved(block, to_group) for block in across]
+        near_y = [moved(block, to_row) for block in near]
+        near_xy = [moved(block, to_group) for block in near_y]
+        far_y = [[moved(block, to_row) for block in blocks] for blocks in far]
+        far_x = [[moved(block, to_group) for block in blocks] for blocks in far]
+        depth = key_weight.shape[0] // 2
+        early = [(HERE, None, 0), (HERE, None, depth), (THERE, 0, 0), (THERE, 1, 0)]
+        early += [(HERE + 1, 0, 0), (HERE + 1, 1, 0), (THERE + 1, 0, 0), (THERE + 1, 1, 0)]
+        late = [(HERE + 2, 0, 0), (HERE + 2, 1, 0), (HERE + 3, 0, 0), (HERE + 3, 1, 0)]
+        late += [(THERE + 2, 0, 0), (THERE + 3, 0, 0)]
+        last = [(THERE + 2, 1, 0), (THERE + 3, 1, 0)]
+        caches = []
+        token = key_weight
+        for k, turned in enumerate((turn, ())):
+            pieces = [weights[k], weights[k], across[k], across_x[k]]
+            pieces += [near[k], near_rest[k], near_y[k], near_xy[k]]
+            totals = product(place, mine, other, early, pieces, (), 4, place)
+            pieces = [far[k][0], far_x[k][0], far[k][1], far_x[k][1], *far_y[k]]
+            total, sent = product(place, mine, other, late, pieces, totals, 6, place)
+            came = moved(sent, to_core)
+            ends = [moved(far_y[k][0], to_group), moved(far_x[k][1], to_row)]
+            pieces = [piece for end in ends for piece in (end, moved(end, to_core))]
+            outgoing = outgoing_rows(
+                place, lengths, owner, mine, kept, last, pieces, total, came, turned, token
+            )
+            caches.append(
+                lax.all_to_all(outgoing, "seq", split_axis=0, concat_axis=1, tiled=True)[0]
+            )
+            token = caches[0]
+        cache_keys, cache_values = caches
+    else:
+        shape = (count_requests, count_rows, KEY_VALUE_HEADS, HEAD_SIZE)
+        unrotated_key = project(key_weight).reshape(shape)
+        key_rows = rotate(
+            unrotated_key, cosine[:, None, :], sine_part[:, None, :]
+        ).astype(jnp.bfloat16)
+        cache_keys = handed_over(key_rows)
+        cache_values = handed_over(project(value_weight).astype(jnp.bfloat16).reshape(shape))
     slot_count = cache_keys.shape[0]
     decode_peer = device_id // split_point
     block = device_id % split_point

time: 245 us -> 188 us (0.77)
  Pallas kernels: 0 us -> 71.2 us
  other arithmetic: 61.4 us -> 8.05 us
  waiting for transfers between devices: 82.3 us -> 41 us
  local copies, waits for them, and re-layouts: 34.2 us -> 3.03 us
  matrix products: 15.4 us -> 1.99 us
  starting transfers between devices: 46.9 us -> 57.6 us
    pallas_call x0 -> x8, Pallas kernels: none -> 71.2 us  [the longest x1 33.6 us: weight_halves(): pl.pallas_call(halves_kernel, in_specs=[SMEM_REF] + [ANY_REF] * len(weigh...]
    ppermute x35, waiting for transfers between devices: 64 us -> 24.1 us  [moved(): return lax.ppermute(block, ('groups', 'seq'), route)]
    concatenate x6 -> x1, other arithmetic: 24.2 us -> 0.77 us  [body(): jnp.concatenate([cosine, cosine], 1)]
    select_n x10 -> x0, other arithmetic: 23.1 us -> none  [the longest x1 13.2 us: body(): other = jnp.where(core == 0, ordered[:, :, 1], ordered[:, :, 0])]
    dot_general x30 -> x0, matrix products: 14.4 us -> none  [project(): total = total + jnp.dot(part, piece, preferred_element_type=jnp.float32)]
    slice x26 -> x0, local copies, waits for them, and re-layouts: 12.3 us -> none  [the longest x3 6.62 us: mirrored(): lax.slice_in_dim(block, i * quarter, (i + 1) * quarter, axis=axis)]
    another operation x1, local copies, waits for them, and re-layouts: 9.45 us -> 0.63 us  [body(): place = jnp.stack([jnp.asarray(entry, jnp.int32) for entry in place])]
    ppermute x35, starting transfers between devices: 39.1 us -> 45 us  [moved(): return lax.ppermute(block, ('groups', 'seq'), route)]
  transfers between devices with their start and end apart: 40 -> 40, of which waited for: 18 -> 14; matrix products, arithmetic and copies ran while one was open for 42% -> 5% of each run, Pallas kernels for 0% -> 14%
where the time goes in v4:
time: 188 us; the launch traced here: 187 us
  Pallas kernels  71.2 us (38%)
  starting transfers between devices  57.6 us (31%)
  waiting for transfers between devices  41 us (22%)
  other arithmetic  8.05 us (4%)
  between operations  3.74 us (2%)
  local copies, waits for them, and re-layouts  3.03 us (2%)
  matrix products  1.99 us (1%)
    ppermute x35, starting transfers between devices, moved(): return lax.ppermute(block, ('groups', 'seq'), route)  45 us
    pallas_call x1, Pallas kernels, weight_halves(): pl.pallas_call(halves_kernel, in_specs=[SMEM_REF] + [ANY_REF] * len(weigh...  33.6 us
    ppermute x35, waiting for transfers between devices, moved(): return lax.ppermute(block, ('groups', 'seq'), route)  24.1 us
    pallas_call x4, Pallas kernels, product(): pl.pallas_call(kernel, in_specs=[SMEM_REF] + [ANY_REF] * (3 + count + len...  21.1 us
    all_to_all x2, waiting for transfers between devices, body(): lax.all_to_all(outgoing, 'seq', split_axis=0, concat_axis=1, tiled=True)[0]  15.2 us
    all_to_all x2, starting transfers between devices, body(): lax.all_to_all(outgoing, 'seq', split_axis=0, concat_axis=1, tiled=True)[0]  11.9 us
    pallas_call x1, Pallas kernels, prepared(): pl.pallas_call(prepare_kernel, grid_spec=pltpu.PrefetchScalarGridSpec(num...  8.46 us
    pallas_call x2, Pallas kernels, outgoing_rows(): pl.pallas_call(kernel, in_specs=[SMEM_REF] * 3 + [ANY_REF] * (1 + len(ope...  8.11 us
  transfers between devices with their start and end apart: 40, of which 14 were waited for; matrix products, arithmetic and copies ran while one was open for 5% of the time, Pallas kernels for 14%

profile of v4, /device:TPU:0, one launch (start us, length us, event | category | flops | bytes accessed | tf_op | source)
XLA Modules:
  0.0 186.7 jit_solution(4472980940864681175)
XLA Ops:
  0.7 0.6 stack.47.place.place_ref.token_ref
  1.3 33.6 %weight_halves.1 = (bf16[256,512]{1,0:T(8,128)(2,1)}, bf16[256,512]{1,0:T(8,128)(2,1)}, bf16[256,512]{1,0:T(8,128)(2,1)}, bf16[256,512]{1,0:T(8,128)(2,1)}) custom-call(s32[11]{0:T(128)} %stack.47.place.place_ref.token_ref, bf16[512,512]{1,0:T(8,128)(2,1)} %token_ref.1, bf16[512,512]{1,0:T(8,128)(2,1)} %refs_3_.3), custom_call_target="tpu_custom_call" | custom-call | flops 1000 | bytes 1000 | tf_op jit(solution)/shard_map/weight_halves/pallas_call | solution.py:113
  35.0 8.5 %normed_halves.1 = (bf16[16,320,256]{2,1,0:T(8,128)(2,1)}, bf16[16,320,256]{2,1,0:T(8,128)(2,1)}) custom-call(s32[11]{0:T(128)} %stack.47.place.place_ref.token_ref, bf16[320,8192]{1,0:T(8,128)(2,1)} %bitcast.55, bf16[256,512]{1,0:T(8,128)(2,1)} %get-tuple-element.16.token), custom_call_target="tpu_custom_call" | custom-call | flops 68719476736 | bytes 10485760 | tf_op jit(solution)/shard_map/normed_halves/pallas_call | solution.py:149
  43.4 0.5 collective-permute-start.8
  43.9 2.6 %collective-permute-start.13 = (bf16[256,512]{1,0:T(8,128)(2,1)S(1)}, bf16[256,512]{1,0:T(8,128)(2,1)S(1)}, u32[]{:S(2)}, u32[]{:S(2)}) collective-permute-start(bf16[256,512]{1,0:T(8,128)(2,1)S(1)} %copy-done.28), channel_id=1, source_target_pairs={{0,4},{1,5},{2,6},{3,7},{4,0},{5,1},{6,2},{7,3},{8,12},{9,13},{10,... | collective-permute-start | bytes 786440 | tf_op jit(solution)/shard_map/ppermute | solution.py:64
  46.5 1.5 collective-permute-start.11
  48.1 2.6 %collective-permute-start = (bf16[256,512]{1,0:T(8,128)(2,1)S(1)}, bf16[256,512]{1,0:T(8,128)(2,1)S(1)}, u32[]{:S(2)}, u32[]{:S(2)}) collective-permute-start(bf16[256,512]{1,0:T(8,128)(2,1)S(1)} %copy-done.28), channel_id=1, source_target_pairs={{0,8},{1,9},{2,10},{3,11},{4,12},{5,13},{6,14},{7,15},{8,0},{9,1},... | collective-permute-start | bytes 786440 | tf_op jit(solution)/shard_map/ppermute | solution.py:64
  50.7 0.4 collective-permute-start.14
  51.1 0.6 fusion.19
  54.4 0.6 fusion.20
  55.4 2.6 %collective-permute-done.13.refs_6_ = bf16[256,512]{1,0:T(8,128)(2,1)S(1)} collective-permute-done((bf16[256,512]{1,0:T(8,128)(2,1)S(1)}, bf16[256,512]{1,0:T(8,128)(2,1)S(1)}, u32[]{:S(2)}, u32[]{:S(2)}) %collective-permute-start.13) | collective-permute-done | bytes 262176 | tf_op jit(solution)/shard_map/ppermute | solution.py:64
  58.0 2.9 %collective-permute-start.4 = (bf16[256,512]{1,0:T(8,128)(2,1)S(1)}, bf16[256,512]{1,0:T(8,128)(2,1)S(1)}, u32[]{:S(2)}, u32[]{:S(2)}) collective-permute-start(bf16[256,512]{1,0:T(8,128)(2,1)S(1)} %copy-done.28), channel_id=1, source_target_pairs={{0,12},{1,13},{2,14},{3,15},{4,8},{5,9},{6,10},{7,11},{8,4},{9,5},... | collective-permute-start | bytes 786440 | tf_op jit(solution)/shard_map/ppermute | solution.py:64
  60.9 4.0 %collective-permute-done.14.refs_7_ = bf16[256,512]{1,0:T(8,128)(2,1)S(1)} collective-permute-done((bf16[256,512]{1,0:T(8,128)(2,1)S(1)}, bf16[256,512]{1,0:T(8,128)(2,1)S(1)}, u32[]{:S(2)}, u32[]{:S(2)}) %collective-permute-start.14) | collective-permute-done | bytes 262176 | tf_op jit(solution)/shard_map/ppermute | solution.py:64
  64.9 1.9 %collective-permute-start.15 = (bf16[256,512]{1,0:T(8,128)(2,1)S(1)}, bf16[256,512]{1,0:T(8,128)(2,1)S(1)}, u32[]{:S(2)}, u32[]{:S(2)}) collective-permute-start(bf16[256,512]{1,0:T(8,128)(2,1)S(1)} %collective-permute-done.13.refs_6_), channel_id=1, source_target_pairs={{0,2},{1,3},{2,0},{3,1},{4,6},{5,7},{6,4},{7,5},{8,10},{9,11},{10,... | collective-permute-start | bytes 786440 | tf_op jit(solution)/shard_map/ppermute | solution.py:64
  66.8 0.7 fusion.14
  67.5 0.7 convert_bitcast_fusion
  68.2 0.8 pad_maximum_fusion
  69.1 3.9 %collective-permute-done.4.refs_4_ = bf16[256,512]{1,0:T(8,128)(2,1)S(1)} collective-permute-done((bf16[256,512]{1,0:T(8,128)(2,1)S(1)}, bf16[256,512]{1,0:T(8,128)(2,1)S(1)}, u32[]{:S(2)}, u32[]{:S(2)}) %collective-permute-start.4) | collective-permute-done | bytes 262176 | tf_op jit(solution)/shard_map/ppermute | solution.py:64
  73.1 1.5 collective-permute-start.12
  74.5 1.4 collective-permute-done.30.refs_6_
  75.9 1.7 collective-permute-start.32
  77.6 1.5 collective-permute-start.16
  79.1 0.6 add_convert_fusion.3
  79.9 3.6 %collective-permute-start.18 = (bf16[256,512]{1,0:T(8,128)(2,1)S(1)}, bf16[256,512]{1,0:T(8,128)(2,1)S(1)}, u32[]{:S(2)}, u32[]{:S(2)}) collective-permute-start(bf16[256,512]{1,0:T(8,128)(2,1)S(1)} %copy-done.16), channel_id=1, source_target_pairs={{0,8},{1,9},{2,10},{3,11},{4,12},{5,13},{6,14},{7,15},{8,0},{9,1},... | collective-permute-start | bytes 786440 | tf_op jit(solution)/shard_map/ppermute | solution.py:64
  83.5 3.8 %collective-permute-start.22 = (bf16[256,512]{1,0:T(8,128)(2,1)S(1)}, bf16[256,512]{1,0:T(8,128)(2,1)S(1)}, u32[]{:S(2)}, u32[]{:S(2)}) collective-permute-start(bf16[256,512]{1,0:T(8,128)(2,1)S(1)} %copy-done.16), channel_id=1, source_target_pairs={{0,12},{1,13},{2,14},{3,15},{4,8},{5,9},{6,10},{7,11},{8,4},{9,5},... | collective-permute-start | bytes 786440 | tf_op jit(solution)/shard_map/ppermute | solution.py:64
  87.3 0.6 collective-permute-start.31
  87.9 1.5 collective-permute-start.29
  89.4 0.5 collective-permute-start.33
  90.0 5.1 %add_product.4 = (f32[320,512]{1,0:T(8,128)}, f32[320,512]{1,0:T(8,128)}) custom-call(s32[11]{0:T(128)} %stack.47.place.place_ref.token_ref, s32[11]{0:T(128)} %stack.47.place.place_ref.token_ref, bf16[16,320,256]{2,1,0:T(8,128)(2,1)} %get-tuple-element.17.refs_0_, bf16[16,320,256]{2,1,0:T(8,128)(2,1)} %collective-permute-done.8.refs_1_, ...), custom_call_target="tpu_custom_call" | custom-call | flops 21474836480 | bytes 4194304 | tf_op jit(solution)/shard_map/add_product/pallas_call | solution.py:221
  95.2 6.1 %collective-permute-done.31.refs_7_ = bf16[256,512]{1,0:T(8,128)(2,1)S(1)} collective-permute-done((bf16[256,512]{1,0:T(8,128)(2,1)S(1)}, bf16[256,512]{1,0:T(8,128)(2,1)S(1)}, u32[]{:S(2)}, u32[]{:S(2)}) %collective-permute-start.31) | collective-permute-done | bytes 262176 | tf_op jit(solution)/shard_map/ppermute | solution.py:64
  101.3 1.2 collective-permute-start.10
  102.5 0.9 collective-permute-start.5
  103.4 1.2 collective-permute-start.1
  104.6 0.9 collective-permute-start.9
  105.5 1.2 collective-permute-start.19
  106.7 5.1 %add_product.6 = (f32[320,512]{1,0:T(8,128)}, f32[320,512]{1,0:T(8,128)}) custom-call(s32[11]{0:T(128)} %stack.47.place.place_ref.token_ref, s32[11]{0:T(128)} %stack.47.place.place_ref.token_ref, bf16[16,320,256]{2,1,0:T(8,128)(2,1)} %get-tuple-element.17.refs_0_, bf16[16,320,256]{2,1,0:T(8,128)(2,1)} %collective-permute-done.8.refs_1_, ...), custom_call_target="tpu_custom_call" | custom-call | flops 21474836480 | bytes 4194304 | tf_op jit(solution)/shard_map/add_product/pallas_call | solution.py:221
  111.8 3.0 %collective-permute-done.1.refs_6_ = bf16[256,512]{1,0:T(8,128)(2,1)S(1)} collective-permute-done((bf16[256,512]{1,0:T(8,128)(2,1)S(1)}, bf16[256,512]{1,0:T(8,128)(2,1)S(1)}, u32[]{:S(2)}, u32[]{:S(2)}) %collective-permute-start.1) | collective-permute-done | bytes 262176 | tf_op jit(solution)/shard_map/ppermute | solution.py:64
  114.8 2.5 %collective-permute-start.26 = (bf16[256,512]{1,0:T(8,128)(2,1)S(1)}, bf16[256,512]{1,0:T(8,128)(2,1)S(1)}, u32[]{:S(2)}, u32[]{:S(2)}) collective-permute-start(bf16[256,512]{1,0:T(8,128)(2,1)S(1)} %collective-permute-done.18.refs_2_), channel_id=1, source_target_pairs={{0,16},{1,17},{2,18},{3,19},{4,20},{5,21},{6,22},{7,23},{8,24},{9,... | collective-permute-start | bytes 786440 | tf_op jit(solution)/shard_map/ppermute | solution.py:64
  117.5 2.0 %collective-permute-start.27 = (bf16[256,512]{1,0:T(8,128)(2,1)S(1)}, bf16[256,512]{1,0:T(8,128)(2,1)S(1)}, u32[]{:S(2)}, u32[]{:S(2)}) collective-permute-start(bf16[256,512]{1,0:T(8,128)(2,1)S(1)} %collective-permute-done.22.refs_4_), channel_id=1, source_target_pairs={{0,2},{1,3},{2,0},{3,1},{4,6},{5,7},{6,4},{7,5},{8,10},{9,11},{10,... | collective-permute-start | bytes 786440 | tf_op jit(solution)/shard_map/ppermute | solution.py:64
  119.4 0.8 collective-permute-start.2
  120.5 2.5 %collective-permute-start.6 = (bf16[256,512]{1,0:T(8,128)(2,1)S(1)}, bf16[256,512]{1,0:T(8,128)(2,1)S(1)}, u32[]{:S(2)}, u32[]{:S(2)}) collective-permute-start(bf16[256,512]{1,0:T(8,128)(2,1)S(1)} %collective-permute-done.5.refs_5_), channel_id=1, source_target_pairs={{0,2},{1,3},{2,0},{3,1},{4,6},{5,7},{6,4},{7,5},{8,10},{9,11},{10,... | collective-permute-start | bytes 786440 | tf_op jit(solution)/shard_map/ppermute | solution.py:64
  122.9 5.4 %add_product.5 = (f32[320,512]{1,0:T(8,128)}, f32[320,512]{1,0:T(8,128)}) custom-call(s32[11]{0:T(128)} %stack.47.place.place_ref.token_ref, s32[11]{0:T(128)} %stack.47.place.place_ref.token_ref, bf16[16,320,256]{2,1,0:T(8,128)(2,1)} %get-tuple-element.17.refs_0_, bf16[16,320,256]{2,1,0:T(8,128)(2,1)} %collective-permute-done.8.refs_1_, ...), custom_call_target="tpu_custom_call" | custom-call | flops 16106127360 | bytes 4194304 | tf_op jit(solution)/shard_map/add_product/pallas_call | solution.py:221
  128.4 1.6 collective-permute-done.23.refs_5_
  130.0 1.6 collective-permute-start.20
  131.5 1.5 collective-permute-start.24
  133.1 0.5 collective-permute-start.7
  133.7 0.6 copy-done.36
  134.3 5.5 %add_product.7 = (f32[320,512]{1,0:T(8,128)}, f32[320,512]{1,0:T(8,128)}) custom-call(s32[11]{0:T(128)} %stack.47.place.place_ref.token_ref, s32[11]{0:T(128)} %stack.47.place.place_ref.token_ref, bf16[16,320,256]{2,1,0:T(8,128)(2,1)} %get-tuple-element.17.refs_0_, bf16[16,320,256]{2,1,0:T(8,128)(2,1)} %collective-permute-done.8.refs_1_, ...), custom_call_target="tpu_custom_call" | custom-call | flops 16106127360 | bytes 4194304 | tf_op jit(solution)/shard_map/add_product/pallas_call | solution.py:221
  139.9 0.5 copy-done.8
  140.9 4.3 %cache_rows.2 = bf16[16,80,128]{2,1,0:T(8,128)(2,1)} custom-call(s32[11]{0:T(128)} %stack.47.place.place_ref.token_ref, s32[2]{0:T(128)} %lengths_ref.3, s32[8]{0:T(128)} %owner_ref.3, bf16[512,512]{1,0:T(8,128)(2,1)} %token_ref.1, bf16[16,320,256]{2,1,0:T(8,128)(2,1)} %get-tuple-element.17.refs_0_, bf16[16,320,256]{2,1,0:T(8,128)(2,1)} %get-tuple-element.18.refs_1_, ...), custom_call_target="tpu_custom_call" | custom-call | flops 335544320 | bytes 4194304 | tf_op jit(solution)/shard_map/cache_rows/pallas_call | solution.py:289
  145.1 8.4 %all-to-all-start = ((bf16[16,80,128]{2,1,0:T(8,128)(2,1)}), bf16[16,80,128]{2,1,0:T(8,128)(2,1)S(1)}, u32[]{:S(2)}, u32[]{:S(2)}) async-start(bf16[16,80,128]{2,1,0:T(8,128)(2,1)} %cache_rows.2), calls=%async_computation | async-start | bytes 655360 | tf_op jit(solution)/shard_map/all_to_all | solution.py:399
  153.5 0.7 add_compare_fusion
  154.2 0.5 collective-permute-start.21
  155.1 0.8 collective-permute-done.21.refs_3_
  156.3 8.3 %all-to-all-done = bf16[16,80,128]{2,1,0:T(8,128)(2,1)S(1)} async-done(((bf16[16,80,128]{2,1,0:T(8,128)(2,1)}), bf16[16,80,128]{2,1,0:T(8,128)(2,1)S(1)}, u32[]{:S(2)}, u32[]{:S(2)}) %all-to-all-start) | async-done | bytes 327712 | tf_op jit(solution)/shard_map/all_to_all | solution.py:399
  164.6 0.7 copy-done.1
  165.3 3.9 %cache_rows.3 = bf16[16,80,128]{2,1,0:T(8,128)(2,1)} custom-call(s32[11]{0:T(128)} %stack.47.place.place_ref.token_ref, s32[2]{0:T(128)} %lengths_ref.3, s32[8]{0:T(128)} %owner_ref.3, bf16[1280,128]{1,0:T(8,128)(2,1)} %bitcast.47, bf16[16,320,256]{2,1,0:T(8,128)(2,1)} %get-tuple-element.17.refs_0_, bf16[16,320,256]{2,1,0:T(8,128)(2,1)} %get-tuple-element.18.refs_1_, ...), custom_call_target="tpu_custom_call" | custom-call | flops 335544320 | bytes 4194304 | tf_op jit(solution)/shard_map/cache_rows/pallas_call | solution.py:289
  169.2 3.6 %all-to-all-start.1 = ((bf16[16,80,128]{2,1,0:T(8,128)(2,1)}), bf16[16,80,128]{2,1,0:T(8,128)(2,1)S(1)}, u32[]{:S(2)}, u32[]{:S(2)}) async-start(bf16[16,80,128]{2,1,0:T(8,128)(2,1)} %cache_rows.3), calls=%async_computation.1 | async-start | bytes 655360 | tf_op jit(solution)/shard_map/all_to_all | solution.py:399
  172.7 1.3 fusion.23
  174.4 0.9 collective-permute-done.35
  175.8 0.9 collective-permute-done.36
  176.9 6.9 %all-to-all-done.1 = bf16[16,80,128]{2,1,0:T(8,128)(2,1)S(1)} async-done(((bf16[16,80,128]{2,1,0:T(8,128)(2,1)}), bf16[16,80,128]{2,1,0:T(8,128)(2,1)S(1)}, u32[]{:S(2)}, u32[]{:S(2)}) %all-to-all-start.1) | async-done | bytes 327712 | tf_op jit(solution)/shard_map/all_to_all | solution.py:399
  184.1 1.9 %maximum_bitcast_fusion = bf16[1,1280,256]{2,1,0:T(8,128)(2,1)} fusion(bf16[1280,128]{1,0:T(8,128)(2,1)S(1)} %bitcast.51, bf16[1280,128]{1,0:T(8,128)(2,1)} %bitcast.49), kind=kLoop, calls=%fused_computation.6 | loop fusion | flops 1310720 | bytes 1310720 | tf_op jit(solution)/shard_map/broadcast_in_dim | solution.py:467
  186.1 0.6 fusion.7
  (137 shorter events, 4.0 us)
Async XLA Ops:
  0.6 176.1 %copy-start = (bf16[8,4,128]{2,1,0:T(4,128)(2,1)S(1)}, bf16[8,4,128]{2,1,0:T(4,128)(2,1)}, u32[]{:S(2)}) copy-start(bf16[8,4,128]{2,1,0:T(4,128)(2,1)} %param.17) | copy-start | bytes 24580
  34.9 9.0 %copy-start.28 = (bf16[256,512]{1,0:T(8,128)(2,1)S(1)}, bf16[256,512]{1,0:T(8,128)(2,1)}, u32[]{:S(2)}) copy-start(bf16[256,512]{1,0:T(8,128)(2,1)} %get-tuple-element.16.token) | copy-start | bytes 786436
  34.9 15.7 %copy-start.31 = (bf16[256,512]{1,0:T(8,128)(2,1)S(1)}, bf16[256,512]{1,0:T(8,128)(2,1)}, u32[]{:S(2)}) copy-start(bf16[256,512]{1,0:T(8,128)(2,1)} %get-tuple-element.19) | copy-start | bytes 786436
  34.9 16.2 %copy-start.13 = (s32[8]{0:T(128)S(1)}, s32[8]{0:T(128)}, u32[]{:S(2)}) copy-start(s32[8]{0:T(128)} %owner_ref.3) | copy-start | bytes 100
  34.9 19.4 %copy-start.12 = (s32[2]{0:T(128)S(1)}, s32[2]{0:T(128)}, u32[]{:S(2)}) copy-start(s32[2]{0:T(128)} %lengths_ref.3) | copy-start | bytes 28
  35.0 20.0 %copy-start.14 = (f32[64]{0:T(128)S(1)}, f32[64]{0:T(128)}, u32[]{:S(2)}) copy-start(f32[64]{0:T(128)} %constant.90.clone) | copy-start | bytes 772
  35.0 25.9 %copy-start.16 = (bf16[256,512]{1,0:T(8,128)(2,1)S(1)}, bf16[256,512]{1,0:T(8,128)(2,1)}, u32[]{:S(2)}) copy-start(bf16[256,512]{1,0:T(8,128)(2,1)} %get-tuple-element.24) | copy-start | bytes 786436
  35.0 52.4 %copy-start.18 = (bf16[256,512]{1,0:T(8,128)(2,1)S(1)}, bf16[256,512]{1,0:T(8,128)(2,1)}, u32[]{:S(2)}) copy-start(bf16[256,512]{1,0:T(8,128)(2,1)} %get-tuple-element.25) | copy-start | bytes 786436
  43.4 46.0 %collective-permute-start.8 = (bf16[16,320,256]{2,1,0:T(8,128)(2,1)}, bf16[16,320,256]{2,1,0:T(8,128)(2,1)}, u32[]{:S(2)}, u32[]{:S(2)}) collective-permute-start(bf16[16,320,256]{2,1,0:T(8,128)(2,1)} %get-tuple-element.18.refs_1_), channel_id=1, source_target_pairs={{0,1},{1,0},{2,3},{3,2},{4,5},{5,4},{6,7},{7,6},{8,9},{9,8},{10,11... | collective-permute-start | bytes 7864328 | tf_op jit(solution)/shard_map/ppermute | solution.py:64
  43.9 14.0 %collective-permute-start.13 = (bf16[256,512]{1,0:T(8,128)(2,1)S(1)}, bf16[256,512]{1,0:T(8,128)(2,1)S(1)}, u32[]{:S(2)}, u32[]{:S(2)}) collective-permute-start(bf16[256,512]{1,0:T(8,128)(2,1)S(1)} %copy-done.28), channel_id=1, source_target_pairs={{0,4},{1,5},{2,6},{3,7},{4,0},{5,1},{6,2},{7,3},{8,12},{9,13},{10,... | collective-permute-start | bytes 786440 | tf_op jit(solution)/shard_map/ppermute | solution.py:64
  46.5 14.3 %collective-permute-start.11 = (bf16[256,512]{1,0:T(8,128)(2,1)S(1)}, bf16[256,512]{1,0:T(8,128)(2,1)S(1)}, u32[]{:S(2)}, u32[]{:S(2)}) collective-permute-start(bf16[256,512]{1,0:T(8,128)(2,1)S(1)} %copy-done.28), channel_id=1, source_target_pairs={{0,2},{1,3},{2,0},{3,1},{4,6},{5,7},{6,4},{7,5},{8,10},{9,11},{10,... | collective-permute-start | bytes 786440 | tf_op jit(solution)/shard_map/ppermute | solution.py:64
  48.1 20.9 %collective-permute-start = (bf16[256,512]{1,0:T(8,128)(2,1)S(1)}, bf16[256,512]{1,0:T(8,128)(2,1)S(1)}, u32[]{:S(2)}, u32[]{:S(2)}) collective-permute-start(bf16[256,512]{1,0:T(8,128)(2,1)S(1)} %copy-done.28), channel_id=1, source_target_pairs={{0,8},{1,9},{2,10},{3,11},{4,12},{5,13},{6,14},{7,15},{8,0},{9,1},... | collective-permute-start | bytes 786440 | tf_op jit(solution)/shard_map/ppermute | solution.py:64
  50.7 14.3 %collective-permute-start.14 = (bf16[256,512]{1,0:T(8,128)(2,1)S(1)}, bf16[256,512]{1,0:T(8,128)(2,1)S(1)}, u32[]{:S(2)}, u32[]{:S(2)}) collective-permute-start(bf16[256,512]{1,0:T(8,128)(2,1)S(1)} %copy-done.31), channel_id=1, source_target_pairs={{0,4},{1,5},{2,6},{3,7},{4,0},{5,1},{6,2},{7,3},{8,12},{9,13},{10,... | collective-permute-start | bytes 786440 | tf_op jit(solution)/shard_map/ppermute | solution.py:64
  58.0 32.0 %copy-start.19 = (bf16[256,512]{1,0:T(8,128)(2,1)}, bf16[256,512]{1,0:T(8,128)(2,1)S(1)}, u32[]{:S(2)}) copy-start(bf16[256,512]{1,0:T(8,128)(2,1)S(1)} %collective-permute-done.13.refs_6_) | copy-start | bytes 786436
  58.0 15.1 %collective-permute-start.4 = (bf16[256,512]{1,0:T(8,128)(2,1)S(1)}, bf16[256,512]{1,0:T(8,128)(2,1)S(1)}, u32[]{:S(2)}, u32[]{:S(2)}) collective-permute-start(bf16[256,512]{1,0:T(8,128)(2,1)S(1)} %copy-done.28), channel_id=1, source_target_pairs={{0,12},{1,13},{2,14},{3,15},{4,8},{5,9},{6,10},{7,11},{8,4},{9,5},... | collective-permute-start | bytes 786440 | tf_op jit(solution)/shard_map/ppermute | solution.py:64
  60.8 29.1 %copy-start.21 = (bf16[256,512]{1,0:T(8,128)(2,1)}, bf16[256,512]{1,0:T(8,128)(2,1)S(1)}, u32[]{:S(2)}) copy-start(bf16[256,512]{1,0:T(8,128)(2,1)S(1)} %collective-permute-done.11.refs_4_) | copy-start | bytes 786436
  60.8 15.1 %collective-permute-start.30 = (bf16[256,512]{1,0:T(8,128)(2,1)S(1)}, bf16[256,512]{1,0:T(8,128)(2,1)S(1)}, u32[]{:S(2)}, u32[]{:S(2)}) collective-permute-start(bf16[256,512]{1,0:T(8,128)(2,1)S(1)} %copy-done.16), channel_id=1, source_target_pairs={{0,4},{1,5},{2,6},{3,7},{4,0},{5,1},{6,2},{7,3},{8,12},{9,13},{10,... | collective-permute-start | bytes 786440 | tf_op jit(solution)/shard_map/ppermute | solution.py:64
  64.9 25.0 %copy-start.23 = (bf16[256,512]{1,0:T(8,128)(2,1)}, bf16[256,512]{1,0:T(8,128)(2,1)S(1)}, u32[]{:S(2)}) copy-start(bf16[256,512]{1,0:T(8,128)(2,1)S(1)} %collective-permute-done.14.refs_7_) | copy-start | bytes 786436
  64.9 12.7 %collective-permute-start.15 = (bf16[256,512]{1,0:T(8,128)(2,1)S(1)}, bf16[256,512]{1,0:T(8,128)(2,1)S(1)}, u32[]{:S(2)}, u32[]{:S(2)}) collective-permute-start(bf16[256,512]{1,0:T(8,128)(2,1)S(1)} %collective-permute-done.13.refs_6_), channel_id=1, source_target_pairs={{0,2},{1,3},{2,0},{3,1},{4,6},{5,7},{6,4},{7,5},{8,10},{9,11},{10,... | collective-permute-start | bytes 786440 | tf_op jit(solution)/shard_map/ppermute | solution.py:64
  69.0 35.6 %copy-start.15 = (bf16[256,512]{1,0:T(8,128)(2,1)}, bf16[256,512]{1,0:T(8,128)(2,1)S(1)}, u32[]{:S(2)}) copy-start(bf16[256,512]{1,0:T(8,128)(2,1)S(1)} %collective-permute-done.refs_2_) | copy-start | bytes 786436
  69.0 10.9 %collective-permute-start.28 = (bf16[256,512]{1,0:T(8,128)(2,1)S(1)}, bf16[256,512]{1,0:T(8,128)(2,1)S(1)}, u32[]{:S(2)}, u32[]{:S(2)}) collective-permute-start(bf16[256,512]{1,0:T(8,128)(2,1)S(1)} %copy-done.16), channel_id=1, source_target_pairs={{0,2},{1,3},{2,0},{3,1},{4,6},{5,7},{6,4},{7,5},{8,10},{9,11},{10,... | collective-permute-start | bytes 786440 | tf_op jit(solution)/shard_map/ppermute | solution.py:64
  73.0 29.4 %copy-start.17 = (bf16[256,512]{1,0:T(8,128)(2,1)}, bf16[256,512]{1,0:T(8,128)(2,1)S(1)}, u32[]{:S(2)}) copy-start(bf16[256,512]{1,0:T(8,128)(2,1)S(1)} %collective-permute-done.4.refs_4_) | copy-start | bytes 786436
  73.1 10.5 %collective-permute-start.12 = (bf16[256,512]{1,0:T(8,128)(2,1)S(1)}, bf16[256,512]{1,0:T(8,128)(2,1)S(1)}, u32[]{:S(2)}, u32[]{:S(2)}) collective-permute-start(bf16[256,512]{1,0:T(8,128)(2,1)S(1)} %collective-permute-done.11.refs_4_), channel_id=1, source_target_pairs={{0,16},{1,17},{2,18},{3,19},{4,20},{5,21},{6,22},{7,23},{8,24},{9,... | collective-permute-start | bytes 786440 | tf_op jit(solution)/shard_map/ppermute | solution.py:64
  75.9 19.2 %copy-start.25 = (bf16[256,512]{1,0:T(8,128)(2,1)}, bf16[256,512]{1,0:T(8,128)(2,1)S(1)}, u32[]{:S(2)}) copy-start(bf16[256,512]{1,0:T(8,128)(2,1)S(1)} %collective-permute-done.30.refs_6_) | copy-start | bytes 786436
  75.9 11.4 %collective-permute-start.32 = (bf16[256,512]{1,0:T(8,128)(2,1)S(1)}, bf16[256,512]{1,0:T(8,128)(2,1)S(1)}, u32[]{:S(2)}, u32[]{:S(2)}) collective-permute-start(bf16[256,512]{1,0:T(8,128)(2,1)S(1)} %collective-permute-done.30.refs_6_), channel_id=1, source_target_pairs={{0,2},{1,3},{2,0},{3,1},{4,6},{5,7},{6,4},{7,5},{8,10},{9,11},{10,... | collective-permute-start | bytes 786440 | tf_op jit(solution)/shard_map/ppermute | solution.py:64
  77.6 12.3 %copy-start.32 = (bf16[256,512]{1,0:T(8,128)(2,1)}, bf16[256,512]{1,0:T(8,128)(2,1)S(1)}, u32[]{:S(2)}) copy-start(bf16[256,512]{1,0:T(8,128)(2,1)S(1)} %collective-permute-done.15.refs_8_) | copy-start | bytes 786436
  77.6 10.3 %collective-permute-start.16 = (bf16[256,512]{1,0:T(8,128)(2,1)S(1)}, bf16[256,512]{1,0:T(8,128)(2,1)S(1)}, u32[]{:S(2)}, u32[]{:S(2)}) collective-permute-start(bf16[256,512]{1,0:T(8,128)(2,1)S(1)} %collective-permute-done.15.refs_8_), channel_id=1, source_target_pairs={{0,16},{1,17},{2,18},{3,19},{4,20},{5,21},{6,22},{7,23},{8,24},{9,... | collective-permute-start | bytes 786440 | tf_op jit(solution)/shard_map/ppermute | solution.py:64
  79.9 15.2 %copy-start.27 = (bf16[256,512]{1,0:T(8,128)(2,1)}, bf16[256,512]{1,0:T(8,128)(2,1)S(1)}, u32[]{:S(2)}) copy-start(bf16[256,512]{1,0:T(8,128)(2,1)S(1)} %collective-permute-done.28.refs_4_) | copy-start | bytes 786436
  79.9 22.6 %collective-permute-start.18 = (bf16[256,512]{1,0:T(8,128)(2,1)S(1)}, bf16[256,512]{1,0:T(8,128)(2,1)S(1)}, u32[]{:S(2)}, u32[]{:S(2)}) collective-permute-start(bf16[256,512]{1,0:T(8,128)(2,1)S(1)} %copy-done.16), channel_id=1, source_target_pairs={{0,8},{1,9},{2,10},{3,11},{4,12},{5,13},{6,14},{7,15},{8,0},{9,1},... | collective-permute-start | bytes 786440 | tf_op jit(solution)/shard_map/ppermute | solution.py:64
  83.5 19.8 %collective-permute-start.22 = (bf16[256,512]{1,0:T(8,128)(2,1)S(1)}, bf16[256,512]{1,0:T(8,128)(2,1)S(1)}, u32[]{:S(2)}, u32[]{:S(2)}) collective-permute-start(bf16[256,512]{1,0:T(8,128)(2,1)S(1)} %copy-done.16), channel_id=1, source_target_pairs={{0,12},{1,13},{2,14},{3,15},{4,8},{5,9},{6,10},{7,11},{8,4},{9,5},... | collective-permute-start | bytes 786440 | tf_op jit(solution)/shard_map/ppermute | solution.py:64
  87.3 13.9 %collective-permute-start.31 = (bf16[256,512]{1,0:T(8,128)(2,1)S(1)}, bf16[256,512]{1,0:T(8,128)(2,1)S(1)}, u32[]{:S(2)}, u32[]{:S(2)}) collective-permute-start(bf16[256,512]{1,0:T(8,128)(2,1)S(1)} %copy-done.18), channel_id=1, source_target_pairs={{0,4},{1,5},{2,6},{3,7},{4,0},{5,1},{6,2},{7,3},{8,12},{9,13},{10,... | collective-permute-start | bytes 786440 | tf_op jit(solution)/shard_map/ppermute | solution.py:64
  87.9 16.7 %collective-permute-start.29 = (bf16[256,512]{1,0:T(8,128)(2,1)S(1)}, bf16[256,512]{1,0:T(8,128)(2,1)S(1)}, u32[]{:S(2)}, u32[]{:S(2)}) collective-permute-start(bf16[256,512]{1,0:T(8,128)(2,1)S(1)} %collective-permute-done.28.refs_4_), channel_id=1, source_target_pairs={{0,16},{1,17},{2,18},{3,19},{4,20},{5,21},{6,22},{7,23},{8,24},{9,... | collective-permute-start | bytes 786440 | tf_op jit(solution)/shard_map/ppermute | solution.py:64
  89.4 16.1 %collective-permute-start.33 = (bf16[256,512]{1,0:T(8,128)(2,1)S(1)}, bf16[256,512]{1,0:T(8,128)(2,1)S(1)}, u32[]{:S(2)}, u32[]{:S(2)}) collective-permute-start(bf16[256,512]{1,0:T(8,128)(2,1)S(1)} %collective-permute-done.32.refs_8_), channel_id=1, source_target_pairs={{0,16},{1,17},{2,18},{3,19},{4,20},{5,21},{6,22},{7,23},{8,24},{9,... | collective-permute-start | bytes 786440 | tf_op jit(solution)/shard_map/ppermute | solution.py:64
  101.3 16.1 %collective-permute-start.10 = (bf16[256,512]{1,0:T(8,128)(2,1)S(1)}, bf16[256,512]{1,0:T(8,128)(2,1)S(1)}, u32[]{:S(2)}, u32[]{:S(2)}) collective-permute-start(bf16[256,512]{1,0:T(8,128)(2,1)S(1)} %collective-permute-done.4.refs_4_), channel_id=1, source_target_pairs={{0,2},{1,3},{2,0},{3,1},{4,6},{5,7},{6,4},{7,5},{8,10},{9,11},{10,... | collective-permute-start | bytes 786440 | tf_op jit(solution)/shard_map/ppermute | solution.py:64
  102.5 12.3 %copy-start.20 = (bf16[256,512]{1,0:T(8,128)(2,1)}, bf16[256,512]{1,0:T(8,128)(2,1)S(1)}, u32[]{:S(2)}) copy-start(bf16[256,512]{1,0:T(8,128)(2,1)S(1)} %collective-permute-done.18.refs_2_) | copy-start | bytes 786436
  102.5 14.9 %collective-permute-start.5 = (bf16[256,512]{1,0:T(8,128)(2,1)S(1)}, bf16[256,512]{1,0:T(8,128)(2,1)S(1)}, u32[]{:S(2)}, u32[]{:S(2)}) collective-permute-start(bf16[256,512]{1,0:T(8,128)(2,1)S(1)} %collective-permute-done.4.refs_4_), channel_id=1, source_target_pairs={{0,16},{1,17},{2,18},{3,19},{4,20},{5,21},{6,22},{7,23},{8,24},{9,... | collective-permute-start | bytes 786440 | tf_op jit(solution)/shard_map/ppermute | solution.py:64
  103.4 14.1 %copy-start.22 = (bf16[256,512]{1,0:T(8,128)(2,1)}, bf16[256,512]{1,0:T(8,128)(2,1)S(1)}, u32[]{:S(2)}) copy-start(bf16[256,512]{1,0:T(8,128)(2,1)S(1)} %collective-permute-done.22.refs_4_) | copy-start | bytes 786436
  103.4 11.5 %collective-permute-start.1 = (bf16[256,512]{1,0:T(8,128)(2,1)S(1)}, bf16[256,512]{1,0:T(8,128)(2,1)S(1)}, u32[]{:S(2)}, u32[]{:S(2)}) collective-permute-start(bf16[256,512]{1,0:T(8,128)(2,1)S(1)} %collective-permute-done.refs_2_), channel_id=1, source_target_pairs={{0,2},{1,3},{2,0},{3,1},{4,6},{5,7},{6,4},{7,5},{8,10},{9,11},{10,... | collective-permute-start | bytes 786440 | tf_op jit(solution)/shard_map/ppermute | solution.py:64
  104.6 14.8 %collective-permute-start.9 = (bf16[256,512]{1,0:T(8,128)(2,1)S(1)}, bf16[256,512]{1,0:T(8,128)(2,1)S(1)}, u32[]{:S(2)}, u32[]{:S(2)}) collective-permute-start(bf16[256,512]{1,0:T(8,128)(2,1)S(1)} %collective-permute-done.refs_2_), channel_id=1, source_target_pairs={{0,16},{1,17},{2,18},{3,19},{4,20},{5,21},{6,22},{7,23},{8,24},{9,... | collective-permute-start | bytes 786440 | tf_op jit(solution)/shard_map/ppermute | solution.py:64
  105.5 15.0 %collective-permute-start.19 = (bf16[256,512]{1,0:T(8,128)(2,1)S(1)}, bf16[256,512]{1,0:T(8,128)(2,1)S(1)}, u32[]{:S(2)}, u32[]{:S(2)}) collective-permute-start(bf16[256,512]{1,0:T(8,128)(2,1)S(1)} %collective-permute-done.18.refs_2_), channel_id=1, source_target_pairs={{0,2},{1,3},{2,0},{3,1},{4,6},{5,7},{6,4},{7,5},{8,10},{9,11},{10,... | collective-permute-start | bytes 786440 | tf_op jit(solution)/shard_map/ppermute | solution.py:64
  114.8 16.7 %collective-permute-start.26 = (bf16[256,512]{1,0:T(8,128)(2,1)S(1)}, bf16[256,512]{1,0:T(8,128)(2,1)S(1)}, u32[]{:S(2)}, u32[]{:S(2)}) collective-permute-start(bf16[256,512]{1,0:T(8,128)(2,1)S(1)} %collective-permute-done.18.refs_2_), channel_id=1, source_target_pairs={{0,16},{1,17},{2,18},{3,19},{4,20},{5,21},{6,22},{7,23},{8,24},{9,... | collective-permute-start | bytes 786440 | tf_op jit(solution)/shard_map/ppermute | solution.py:64
  117.4 12.6 %collective-permute-start.23 = (bf16[256,512]{1,0:T(8,128)(2,1)S(1)}, bf16[256,512]{1,0:T(8,128)(2,1)S(1)}, u32[]{:S(2)}, u32[]{:S(2)}) collective-permute-start(bf16[256,512]{1,0:T(8,128)(2,1)S(1)} %collective-permute-done.22.refs_4_), channel_id=1, source_target_pairs={{0,16},{1,17},{2,18},{3,19},{4,20},{5,21},{6,22},{7,23},{8,24},{9,... | collective-permute-start | bytes 786440 | tf_op jit(solution)/shard_map/ppermute | solution.py:64
  117.5 16.1 %collective-permute-start.27 = (bf16[256,512]{1,0:T(8,128)(2,1)S(1)}, bf16[256,512]{1,0:T(8,128)(2,1)S(1)}, u32[]{:S(2)}, u32[]{:S(2)}) collective-permute-start(bf16[256,512]{1,0:T(8,128)(2,1)S(1)} %collective-permute-done.22.refs_4_), channel_id=1, source_target_pairs={{0,2},{1,3},{2,0},{3,1},{4,6},{5,7},{6,4},{7,5},{8,10},{9,11},{10,... | collective-permute-start | bytes 786440 | tf_op jit(solution)/shard_map/ppermute | solution.py:64
  119.4 13.6 %collective-permute-start.2 = (bf16[256,512]{1,0:T(8,128)(2,1)S(1)}, bf16[256,512]{1,0:T(8,128)(2,1)S(1)}, u32[]{:S(2)}, u32[]{:S(2)}) collective-permute-start(bf16[256,512]{1,0:T(8,128)(2,1)S(1)} %collective-permute-done.1.refs_6_), channel_id=1, source_target_pairs={{0,16},{1,17},{2,18},{3,19},{4,20},{5,21},{6,22},{7,23},{8,24},{9,... | collective-permute-start | bytes 786440 | tf_op jit(solution)/shard_map/ppermute | solution.py:64
  120.4 9.5 %copy-start.24 = (bf16[256,512]{1,0:T(8,128)(2,1)}, bf16[256,512]{1,0:T(8,128)(2,1)S(1)}, u32[]{:S(2)}) copy-start(bf16[256,512]{1,0:T(8,128)(2,1)S(1)} %collective-permute-done.19.refs_6_) | copy-start | bytes 786436
  120.5 12.6 %collective-permute-start.6 = (bf16[256,512]{1,0:T(8,128)(2,1)S(1)}, bf16[256,512]{1,0:T(8,128)(2,1)S(1)}, u32[]{:S(2)}, u32[]{:S(2)}) collective-permute-start(bf16[256,512]{1,0:T(8,128)(2,1)S(1)} %collective-permute-done.5.refs_5_), channel_id=1, source_target_pairs={{0,2},{1,3},{2,0},{3,1},{4,6},{5,7},{6,4},{7,5},{8,10},{9,11},{10,... | collective-permute-start | bytes 786440 | tf_op jit(solution)/shard_map/ppermute | solution.py:64
  130.0 24.3 %collective-permute-start.20 = (bf16[256,512]{1,0:T(8,128)(2,1)S(1)}, bf16[256,512]{1,0:T(8,128)(2,1)S(1)}, u32[]{:S(2)}, u32[]{:S(2)}) collective-permute-start(bf16[256,512]{1,0:T(8,128)(2,1)S(1)} %collective-permute-done.19.refs_6_), channel_id=1, source_target_pairs={{0,16},{1,17},{2,18},{3,19},{4,20},{5,21},{6,22},{7,23},{8,24},{9,... | collective-permute-start | bytes 786440 | tf_op jit(solution)/shard_map/ppermute | solution.py:64
  131.5 23.2 %collective-permute-start.24 = (bf16[256,512]{1,0:T(8,128)(2,1)S(1)}, bf16[256,512]{1,0:T(8,128)(2,1)S(1)}, u32[]{:S(2)}, u32[]{:S(2)}) collective-permute-start(bf16[256,512]{1,0:T(8,128)(2,1)S(1)} %collective-permute-done.23.refs_5_), channel_id=1, source_target_pairs={{0,2},{1,3},{2,0},{3,1},{4,6},{5,7},{6,4},{7,5},{8,10},{9,11},{10,... | collective-permute-start | bytes 786440 | tf_op jit(solution)/shard_map/ppermute | solution.py:64
  133.0 6.7 %collective-permute-start.3 = (bf16[256,512]{1,0:T(8,128)(2,1)S(1)}, bf16[256,512]{1,0:T(8,128)(2,1)S(1)}, u32[]{:S(2)}, u32[]{:S(2)}) collective-permute-start(bf16[256,512]{1,0:T(8,128)(2,1)S(1)} %collective-permute-done.2.refs_2_), channel_id=1, source_target_pairs={{0,1},{1,0},{2,3},{3,2},{4,5},{5,4},{6,7},{7,6},{8,9},{9,8},{10,11... | collective-permute-start | bytes 786440 | tf_op jit(solution)/shard_map/ppermute | solution.py:64
  133.1 6.9 %collective-permute-start.7 = (bf16[256,512]{1,0:T(8,128)(2,1)S(1)}, bf16[256,512]{1,0:T(8,128)(2,1)S(1)}, u32[]{:S(2)}, u32[]{:S(2)}) collective-permute-start(bf16[256,512]{1,0:T(8,128)(2,1)S(1)} %collective-permute-done.6.refs_4_), channel_id=1, source_target_pairs={{0,1},{1,0},{2,3},{3,2},{4,5},{5,4},{6,7},{7,6},{8,9},{9,8},{10,11... | collective-permute-start | bytes 786440 | tf_op jit(solution)/shard_map/ppermute | solution.py:64
  133.6 6.4 %collective-permute-start.17 = (f32[320,512]{1,0:T(8,128)}, f32[320,512]{1,0:T(8,128)S(1)}, u32[]{:S(2)}, u32[]{:S(2)}) collective-permute-start(f32[320,512]{1,0:T(8,128)} %get-tuple-element.23), channel_id=1, source_target_pairs={{0,1},{1,0},{2,3},{3,2},{4,5},{5,4},{6,7},{7,6},{8,9},{9,8},{10,11... | collective-permute-start | bytes 1966088 | tf_op jit(solution)/shard_map/ppermute | solution.py:64
  139.8 16.5 %collective-permute-start.34 = (f32[320,512]{1,0:T(8,128)}, f32[320,512]{1,0:T(8,128)S(1)}, u32[]{:S(2)}, u32[]{:S(2)}) collective-permute-start(f32[320,512]{1,0:T(8,128)} %get-tuple-element.29), channel_id=1, source_target_pairs={{0,1},{1,0},{2,3},{3,2},{4,5},{5,4},{6,7},{7,6},{8,9},{9,8},{10,11... | collective-permute-start | bytes 1966088 | tf_op jit(solution)/shard_map/ppermute | solution.py:64
  145.1 19.5 %all-to-all-start = ((bf16[16,80,128]{2,1,0:T(8,128)(2,1)}), bf16[16,80,128]{2,1,0:T(8,128)(2,1)S(1)}, u32[]{:S(2)}, u32[]{:S(2)}) async-start(bf16[16,80,128]{2,1,0:T(8,128)(2,1)} %cache_rows.2), calls=%async_computation | async-start | bytes 655360 | tf_op jit(solution)/shard_map/all_to_all | solution.py:399
  154.2 10.3 %copy-start.4 = (bf16[256,512]{1,0:T(8,128)(2,1)}, bf16[256,512]{1,0:T(8,128)(2,1)S(1)}, u32[]{:S(2)}) copy-start(bf16[256,512]{1,0:T(8,128)(2,1)S(1)} %collective-permute-done.20.refs_2_) | copy-start | bytes 786436
  154.2 1.6 collective-permute-start.21
  154.7 9.9 %copy-start.5 = (bf16[256,512]{1,0:T(8,128)(2,1)}, bf16[256,512]{1,0:T(8,128)(2,1)S(1)}, u32[]{:S(2)}) copy-start(bf16[256,512]{1,0:T(8,128)(2,1)S(1)} %collective-permute-done.24.refs_4_) | copy-start | bytes 786436
  154.7 1.5 collective-permute-start.25
  155.9 8.7 %copy-start.9 = (bf16[256,512]{1,0:T(8,128)(2,1)}, bf16[256,512]{1,0:T(8,128)(2,1)S(1)}, u32[]{:S(2)}) copy-start(bf16[256,512]{1,0:T(8,128)(2,1)S(1)} %collective-permute-done.21.refs_3_) | copy-start | bytes 786436
  156.3 8.3 %copy-start.11 = (bf16[256,512]{1,0:T(8,128)(2,1)}, bf16[256,512]{1,0:T(8,128)(2,1)S(1)}, u32[]{:S(2)}) copy-start(bf16[256,512]{1,0:T(8,128)(2,1)S(1)} %collective-permute-done.25.refs_5_) | copy-start | bytes 786436
  156.3 8.3 %copy-start.2 = (f32[320,512]{1,0:T(8,128)}, f32[320,512]{1,0:T(8,128)S(1)}, u32[]{:S(2)}) copy-start(f32[320,512]{1,0:T(8,128)S(1)} %collective-permute-done.34.refs_7_) | copy-start | bytes 1966084
  169.2 14.6 %all-to-all-start.1 = ((bf16[16,80,128]{2,1,0:T(8,128)(2,1)}), bf16[16,80,128]{2,1,0:T(8,128)(2,1)S(1)}, u32[]{:S(2)}, u32[]{:S(2)}) async-start(bf16[16,80,128]{2,1,0:T(8,128)(2,1)} %cache_rows.3), calls=%async_computation.1 | async-start | bytes 655360 | tf_op jit(solution)/shard_map/all_to_all | solution.py:399
  174.1 1.2 collective-permute-start.35
  175.5 1.2 collective-permute-start.36
  184.0 2.0 %collective-permute-start.37 = (f32[4,1024]{1,0:T(4,128)S(1)}, f32[4,1024]{1,0:T(4,128)S(1)}, u32[]{:S(2)}, u32[]{:S(2)}) collective-permute-start(f32[4,1024]{1,0:T(4,128)S(1)} %bitcast.53), channel_id=1, source_target_pairs={{0,1},{1,0},{2,3},{3,2},{4,5},{5,4},{6,7},{7,6},{8,9},{9,8},{10,11... | collective-permute-start | bytes 49160 | tf_op jit(solution)/shard_map/ppermute | solution.py:27
  (19 other events, 70.7 us)

commit v5 on v2

--- a/solution.py
+++ b/solution.py
@@ -2,6 +2,7 @@
 
 import jax
 import jax.numpy as jnp
+import numpy as np
 from jax import lax
 from jax.experimental import pallas as pl
 from jax.experimental.pallas import tpu as pltpu
@@ -27,8 +28,8 @@
 
 
 def rope_table(positions, head_dim):
-    freq = ROPE_BASE ** (-(jnp.arange(head_dim // 2, dtype=jnp.float32) * 2.0) / head_dim)
-    angle = positions.astype(jnp.float32)[:, None] * freq[None, :]
+    freq = ROPE_BASE ** (-(np.arange(head_dim // 2, dtype=np.float64) * 2.0) / head_dim)
+    angle = positions.astype(jnp.float32)[:, None] * jnp.asarray(freq, jnp.float32)[None, :]
     return (jnp.cos(angle), jnp.sin(angle))
 
 
@@ -45,58 +46,27 @@
     )
 
 
-def spread(count):
-    side = 1
-    while side * side < count:
-        side *= 2
-    return (side, count // side)
-
-
-def moved(block, rule):
+def swapped_core(block):
+    count = lax.axis_size("seq")
+    return lax.ppermute(block, "seq", [(i, i ^ 1) for i in range(count)])
+
+
+def plane_gather(block):
     groups, seq = lax.axis_size("groups"), lax.axis_size("seq")
-    low = spread(seq // 2)[1]
-    route = []
-    for g in range(groups):
-        for s in range(seq):
-            place = rule(g, s // 2 // low, s // 2 % low, s % 2)
-            if place is not None:
-                tg, tz, ty, tc = place
-                route.append((g * seq + s, tg * seq + (tz * low + ty) * 2 + tc))
-    return lax.ppermute(block, ("groups", "seq"), route)
-
-
-def to_core(g, z, y, c):
-    return (g, z, y, 1 - c)
-
-
-def to_row(g, z, y, c):
-    return (g, z, 1 - y, c)
-
-
-def to_group(g, z, y, c):
-    return (1 - g, z, y, c)
-
-
-def to_pair(g, z, y, c):
-    return (g, z ^ 1, y, c)
-
-
-def to_middle(g, z, y, c):
-    return (g, 3 - z, y, c) if z in (1, 2) else None
-
-
-def to_end(g, z, y, c):
-    return (g, 0 if z == 1 else 3, y, c) if z in (1, 2) else None
-
-
-def mirrored(block, axis, flag):
-    quarter = block.shape[axis] // 4
-    parts = [lax.slice_in_dim(block, i * quarter, (i + 1) * quarter, axis=axis) for i in range(4)]
-    return jnp.where(flag, jnp.concatenate(parts[::-1], axis), block)
-
-
-def small_cost():
-    return pl.CostEstimate(flops=1000, bytes_accessed=1000, transcendentals=0)
+    planes = [[d for d in range(groups * seq) if d % 2 == core] for core in range(2)]
+    return lax.all_gather(
+        block, ("groups", "seq"), axis=0, tiled=True, axis_index_groups=planes
+    )
+
+
+VMEM_REF = pl.BlockSpec(memory_space=pltpu.VMEM)
+SMEM_REF = pl.BlockSpec(memory_space=pltpu.SMEM)
+ANY_REF = pl.BlockSpec(memory_space=pl.ANY)
+PARAMS = pltpu.CompilerParams(vmem_limit_bytes=56 << 20)
+
+
+def cost(flops, moved_bytes):
+    return pl.CostEstimate(flops=flops, bytes_accessed=moved_bytes, transcendentals=0)
 
 
 def whole_block(array):
@@ -104,33 +74,34 @@
 
 
 def prepare_kernel(place, rows_in, mine, other):
-    blocks, _, depth = mine.shape
-    quarter = depth // 4
-    wide = rows_in[...].astype(jnp.float32)
-    scale = lax.rsqrt(jnp.mean(wide * wide, -1, keepdims=True) + 1e-05)
-    for g in range(2):
-        for core in range(2):
-
-            @pl.when((place[0] == g) & (place[1] == core))
-            def _():
-                for j in range(blocks):
-                    for c in range(2):
-                        target = mine if c == core else other
-                        for q in range(4):
-                            first = (2 * j + c) * depth + q * quarter
-                            part = rows_in[:, first : first + quarter].astype(jnp.float32)
-                            spot = 3 - q if g else q
-                            target[j, :, spot * quarter : (spot + 1) * quarter] = (
-                                part * scale
-                            ).astype(jnp.bfloat16)
-
-
-def prepared(flat, group_id, core, blocks):
+    steps, rows, depth = mine.shape
+    half = depth // 2
+    width = rows_in.shape[1]
+    square = jnp.zeros((rows, half), jnp.float32)
+    for first in range(0, width, half):
+        part = rows_in[:, first : first + half].astype(jnp.float32)
+        square += part * part
+    scale = lax.rsqrt(jnp.sum(square, -1, keepdims=True) / width + 1e-05)
+    for core in range(2):
+
+        @pl.when(place[0] == core)
+        def _():
+            for first in range(0, width, half):
+                j, c, h = first // (2 * depth), first // depth % 2, first // half % 2
+                spot = h * steps + j
+                target = mine if c == core else other
+                part = rows_in[:, first : first + half].astype(jnp.float32)
+                target[spot // 2, :, (spot % 2) * half : (spot % 2 + 1) * half] = (
+                    part * scale
+                ).astype(jnp.bfloat16)
+
+
+def prepared(flat, place, steps):
     rows, width = flat.shape
-    depth = width // (2 * blocks)
-    tile = 64 if rows % 64 == 0 else rows
-    out = jax.ShapeDtypeStruct((blocks, rows, depth), jnp.bfloat16)
-    spec = pl.BlockSpec((blocks, tile, depth), lambda i, place: (0, i, 0))
+    depth = width // (2 * steps)
+    tile = 32 if rows % 32 == 0 else rows
+    out = jax.ShapeDtypeStruct((steps, rows, depth), jnp.bfloat16)
+    spec = pl.BlockSpec((steps, tile, depth), lambda i, place: (0, i, 0))
     return pl.pallas_call(
         prepare_kernel,
         grid_spec=pltpu.PrefetchScalarGridSpec(
@@ -140,49 +111,40 @@
             out_specs=[spec, spec],
         ),
         out_shape=[out, out],
-        compiler_params=pltpu.CompilerParams(vmem_limit_bytes=32 << 20),
-        cost_estimate=small_cost(),
+        compiler_params=PARAMS,
+        cost_estimate=cost(8 * rows * width, 4 * rows * width),
         name="normed_halves",
-    )(jnp.stack([group_id, core]).astype(jnp.int32), flat)
-
-
-def product_kernel(count_near, has_total, which, *refs):
-    left = refs[:4]
-    pieces = [ref[...] for ref in refs[4 : -2 - 2 * has_total]]
-    near = jnp.concatenate(pieces[:count_near], 0) if count_near > 1 else pieces[0]
-    far = jnp.concatenate(pieces[count_near:], 0)
-    for half in range(2):
-        total = jnp.dot(left[2 * half][0], near, preferred_element_type=jnp.float32)
-        total += jnp.dot(left[2 * half + 1][0], far, preferred_element_type=jnp.float32)
-        if has_total:
-            total += refs[half - 4][...]
-        refs[half - 2][...] = total
-
-
-def product(which, mine, other, near, far, totals):
-    _, rows, depth = mine.shape
-    columns = near[0].shape[1]
-    operands = [*near, *far, *totals]
-    left_specs = [
-        pl.BlockSpec((1, rows, depth), functools.partial(lambda k, _, which: (which[k], 0, 0), k))
-        for k in (0, 1)
-    ]
+    )(place, flat)
+
+
+def product_kernel(token, mine, other, weight, *totals):
+    for left, total in zip((mine, other), totals):
+        part = jnp.dot(left[0], weight[...], preferred_element_type=jnp.float32)
+
+        @pl.when(pl.program_id(0) == 0)
+        def _():
+            total[...] = part
+
+        @pl.when(pl.program_id(0) > 0)
+        def _():
+            total[...] += part
+
+
+def product(mine, other, weight, token):
+    steps, rows, depth = mine.shape
+    columns = weight.shape[1]
     out = jax.ShapeDtypeStruct((rows, columns), jnp.float32)
-    first_total = 1 + 4 + len(near) + len(far)
+    left = pl.BlockSpec((1, rows, depth), lambda i: (i, 0, 0))
     return pl.pallas_call(
-        functools.partial(product_kernel, len(near), len(totals) // 2),
-        grid_spec=pltpu.PrefetchScalarGridSpec(
-            num_scalar_prefetch=1,
-            grid=(1,),
-            in_specs=left_specs * 2 + [whole_block(piece) for piece in operands],
-            out_specs=[whole_block(out)] * 2,
-        ),
+        product_kernel,
+        grid=(steps,),
+        in_specs=[ANY_REF, left, left, pl.BlockSpec((depth, columns), lambda i: (i, 0))],
+        out_specs=[whole_block(out)] * 2,
         out_shape=[out, out],
-        input_output_aliases={first_total + i: i for i in range(len(totals))},
-        compiler_params=pltpu.CompilerParams(vmem_limit_bytes=32 << 20),
-        cost_estimate=small_cost(),
-        name="add_product",
-    )(which, mine, mine, other, other, *operands)
+        compiler_params=PARAMS,
+        cost_estimate=cost(4 * rows * columns * depth * steps, 1 << 22),
+        name="product",
+    )(token, mine, other, weight)
 
 
 def rows_kernel(rotated, place, lengths, owner, *refs):
@@ -224,39 +186,10 @@
             scratch_shapes=[pltpu.VMEM((count_rows, HEAD_SIZE), jnp.float32)],
         ),
         out_shape=out,
-        compiler_params=pltpu.CompilerParams(vmem_limit_bytes=32 << 20),
-        cost_estimate=small_cost(),
+        compiler_params=pltpu.CompilerParams(vmem_limit_bytes=56 << 20),
+        cost_estimate=cost(1 << 20, 1 << 21),
         name="cache_rows",
     )(place, lengths, owner, *operands)
-
-
-def planned_totals(weight, mine, other, z, y, g):
-    quarter = weight.shape[0] // 4
-    own = mirrored(weight, 0, g == 1)
-    is_end = (z == 0) | (z == 3)
-    main = own[: 3 * quarter]
-    near = moved(main, to_pair)
-    mid_b = moved(main, to_middle)
-    mid_c = moved(near, to_middle)
-    end_b = moved(mid_b, to_end)
-    end_c = moved(mid_c, to_end)
-    slot_b = jnp.where(is_end, end_b, mid_b)
-    slot_c = jnp.where(is_end, end_c, mid_c)
-    z_a, z_b, z_c = z ^ 1, jnp.where(z < 2, 2, 1), jnp.where(z < 2, 3, 0)
-    totals = []
-    for zz, block, share in ((z, own, 2), (z_a, near, 2), (z_b, slot_b, 3), (z_c, slot_c, 3)):
-        here = [block]
-        if block is not own:
-            here.append(moved(block[:quarter], to_group))
-        across = moved(block[: share * quarter], to_row)
-        if share == 2:
-            onward = jnp.concatenate([across[quarter:], across[:quarter]], 0)
-        else:
-            onward = across[:quarter]
-        there = [across, moved(onward, to_group)]
-        which = jnp.stack([zz * 2 + y, zz * 2 + 1 - y]).astype(jnp.int32)
-        totals = product(which, mine, other, here, there, totals)
-    return totals
 
 
 def body(hidden, key_weight, value_weight, lengths, owner, dec_query, dec_key, dec_value):
@@ -272,12 +205,7 @@
     positions = device_id * count_rows + jnp.arange(count_rows, dtype=jnp.int32)
     total_rows = count_requests * count_rows
     flat = hidden.reshape(total_rows, width)
-    if planned:
-        core = device_id % 2
-        z, y = device_id // 4, device_id // 2 % 2
-        mine, other = prepared(flat, group_id, core, seq // 2)
-        other = moved(other, to_core)
-    else:
+    if not planned:
         widened = flat.astype(jnp.float32)
         normed = (
             widened * lax.rsqrt(jnp.mean(widened * widened, -1, keepdims=True) + 1e-05)
@@ -309,16 +237,26 @@
             jnp.concatenate([cosine, cosine], 1),
             jnp.concatenate([-sine_part, sine_part], 1),
         )
-        place = device_id.astype(jnp.int32).reshape(1)
-
-        def cached(weight, turn):
-            total, came = planned_totals(weight, mine, other, z, y, group_id)
-            came = moved(came, to_core)
-            outgoing = outgoing_rows(total, came, place, lengths, owner, turn)
-            return lax.all_to_all(outgoing, "seq", split_axis=0, concat_axis=1, tiled=True)[0]
-
-        cache_keys = cached(key_weight, turn)
-        cache_values = cached(value_weight, ())
+        depth = key_weight.shape[0] // 2
+        halves = [
+            lax.dynamic_slice_in_dim(weight, group_id * depth, depth, 0)
+            for weight in (key_weight, value_weight)
+        ]
+        gathered = [plane_gather(half) for half in halves]
+        mine, kept = prepared(flat, (device_id % 2).reshape(1), seq // 2)
+        other = swapped_core(kept)
+        caches = []
+        token = mine
+        for weight, turned in zip(gathered, (turn, ())):
+            total, sent = product(mine, other, weight, token)
+            outgoing = outgoing_rows(
+                total, swapped_core(sent), device_id.reshape(1), lengths, owner, turned
+            )
+            caches.append(
+                lax.all_to_all(outgoing, "seq", split_axis=0, concat_axis=1, tiled=True)[0]
+            )
+            token = caches[0]
+        cache_keys, cache_values = caches
     else:
         shape = (count_requests, count_rows, KEY_VALUE_HEADS, HEAD_SIZE)
         unrotated_key = project(key_weight).reshape(shape)

time: 174 us -> 210 us (1.21)
  waiting for transfers between devices: 53.8 us -> 132 us
  starting transfers between devices: 46.7 us -> 9.97 us
  between operations: 3.64 us -> 16.8 us
  local copies, waits for them, and re-layouts: 17.4 us -> 5.81 us
  other arithmetic: 13.6 us -> 7.06 us
    all_gather x0 -> x2, waiting for transfers between devices: none -> 116 us  [plane_gather(): lax.all_gather(block, ('groups', 'seq'), axis=0, tiled=True, axis_index_g...]
    ppermute x35 -> x3, starting transfers between devices: 38.9 us -> 0.45 us  [swapped_core(): return lax.ppermute(block, 'seq', [(i, i ^ 1) for i in range(count)])]
    ppermute x35 -> x3, waiting for transfers between devices: 35.4 us -> 7 us  [swapped_core(): return lax.ppermute(block, 'seq', [(i, i ^ 1) for i in range(count)])]
    all_to_all x2, waiting for transfers between devices: 16.4 us -> 7.15 us  [body(): lax.all_to_all(outgoing, 'seq', split_axis=0, concat_axis=1, tiled=True)[0]]
    slice x22 -> x0, local copies, waits for them, and re-layouts: 9.13 us -> none  [the longest x4 2.01 us: planned_totals(): onward = jnp.concatenate([across[quarter:], across[:quarter]], 0)]
    pallas_call x8 -> x2, Pallas kernels: 28.3 us -> 20.4 us  [product(): pl.pallas_call(product_kernel, grid=(steps,), in_specs=[ANY_REF, left, le...]
    unnamed x88 -> x20, local copies, waits for them, and re-layouts: 8.31 us -> 3.42 us
    pallas_call x1, Pallas kernels: 4.59 us -> 8.83 us  [prepared(): pl.pallas_call(prepare_kernel, grid_spec=pltpu.PrefetchScalarGridSpec(num...]
  transfers between devices with their start and end apart: 40 -> 10, of which waited for: 13 -> 9; matrix products, arithmetic and copies ran while one was open for 11% -> 5% of each run, Pallas kernels for 21% -> 11%
where the time goes in v5:
time: 210 us; the launch traced here: 209 us
  waiting for transfers between devices  132 us (63%)
  Pallas kernels  35.2 us (17%)
  between operations  16.8 us (8%)
  starting transfers between devices  9.97 us (5%)
  other arithmetic  7.06 us (3%)
  local copies, waits for them, and re-layouts  5.81 us (3%)
    all_gather x2, waiting for transfers between devices, plane_gather(): lax.all_gather(block, ('groups', 'seq'), axis=0, tiled=True, axis_index_g...  116 us
    pallas_call x2, Pallas kernels, product(): pl.pallas_call(product_kernel, grid=(steps,), in_specs=[ANY_REF, left, le...  20.4 us
    pallas_call x1, Pallas kernels, prepared(): pl.pallas_call(prepare_kernel, grid_spec=pltpu.PrefetchScalarGridSpec(num...  8.83 us
    all_to_all x2, starting transfers between devices, body(): lax.all_to_all(outgoing, 'seq', split_axis=0, concat_axis=1, tiled=True)[0]  8.43 us
    all_to_all x2, waiting for transfers between devices, body(): lax.all_to_all(outgoing, 'seq', split_axis=0, concat_axis=1, tiled=True)[0]  7.15 us
    ppermute x3, waiting for transfers between devices, swapped_core(): return lax.ppermute(block, 'seq', [(i, i ^ 1) for i in range(count)])  7 us
    pallas_call x2, Pallas kernels, outgoing_rows(): pl.pallas_call(functools.partial(rows_kernel, bool(turn)), grid_spec=pltp...  5.91 us
  transfers between devices with their start and end apart: 10, of which 9 were waited for; matrix products, arithmetic and copies ran while one was open for 5% of the time, Pallas kernels for 11%

profile of v5, /device:TPU:0, one launch (start us, length us, event | category | flops | bytes accessed | tf_op | source)
XLA Modules:
  0.0 208.5 jit_solution(18100567932641681555)
XLA Ops:
  7.2 0.0 copy-start
  7.2 0.0 all-gather.3.cloned.1.call-start
  7.2 1.0 copy-done
  8.2 0.7 constant_dynamic-slice_fusion.3
  8.9 0.0 all-gather.3.cloned.1.call-update
  9.0 0.0 all-gather.5.cloned.1.call-start
  9.0 1.7 constant_dynamic-slice_fusion.2
  10.7 0.0 all-gather.5.cloned.1.call-update
  10.7 8.8 %normed_halves.1 = (bf16[8,320,512]{2,1,0:T(8,128)(2,1)}, bf16[8,320,512]{2,1,0:T(8,128)(2,1)}) custom-call(s32[1]{0:T(128)} %bitcast.1.place, bf16[320,8192]{1,0:T(8,128)(2,1)} %bitcast.38), custom_call_target="tpu_custom_call" | custom-call | flops 20971520 | bytes 10485760 | tf_op jit(solution)/shard_map/normed_halves/pallas_call | solution.py:105
  19.5 0.4 collective-permute-start
  20.0 4.7 %collective-permute-done.other = bf16[8,320,512]{2,1,0:T(8,128)(2,1)S(1)} collective-permute-done((bf16[8,320,512]{2,1,0:T(8,128)(2,1)}, bf16[8,320,512]{2,1,0:T(8,128)(2,1)S(1)}, u32[]{:S(2)}, u32[]{:S(2)}) %collective-permute-start) | collective-permute-done | bytes 2621472 | tf_op jit(solution)/shard_map/ppermute | solution.py:51
  24.7 0.0 copy-start.3
  24.7 65.3 %all-gather.3.cloned.1.call-done.weight = bf16[4096,512]{1,0:T(8,128)(2,1)} async-done(((bf16[256,512]{1,0:T(8,128)(2,1)}), bf16[4096,512]{1,0:T(8,128)(2,1)}) %all-gather.3.cloned.1.call-update) | async-done | bytes 4194320 | tf_op jit(solution)/shard_map/all_gather | solution.py:57
  90.0 0.0 copy-done.3
  90.0 0.0 copy-start.6
  90.0 10.2 %product.2 = (f32[320,512]{1,0:T(8,128)}, f32[320,512]{1,0:T(8,128)}) custom-call(bf16[8,320,512]{2,1,0:T(8,128)(2,1)} %get-tuple-element.8.token.mine, bf16[8,320,512]{2,1,0:T(8,128)(2,1)} %get-tuple-element.8.token.mine, bf16[8,320,512]{2,1,0:T(8,128)(2,1)} %copy-done.3, bf16[4096,512]{1,0:T(8,128)(2,1)} %all-gather.3.cloned.1.call-done.weight), custom_call_target="tpu_custom_call" | custom-call | flops 2684354560 | bytes 4194304 | tf_op jit(solution)/shard_map/product/pallas_call | solution.py:138
  100.2 0.0 copy-start.8
  100.2 0.0 copy-start.7
  100.2 0.0 collective-permute-start.1
  100.3 0.7 convert_bitcast_fusion
  101.0 0.0 copy-done.6
  101.0 0.4 fusion.6
  101.4 0.8 pad_maximum_fusion
  102.2 0.4 collective-permute-done.1.refs_1_
  102.5 0.0 copy-start.5
  102.6 0.8 copy-done.5
  103.4 3.0 %cache_rows.2 = bf16[16,80,128]{2,1,0:T(8,128)(2,1)} custom-call(s32[1]{0:T(128)} %bitcast.place, s32[2]{0:T(128)} %lengths.3, s32[8]{0:T(128)} %owner.3, f32[320,512]{1,0:T(8,128)} %get-tuple-element.10.refs_0_, f32[320,512]{1,0:T(8,128)} %copy-done.5, f32[160,128]{1,0:T(8,128)} %get-tuple-element.27.refs_2_, f32[160,128]{1,0:T(8,128)} %get-tuple-element.28.refs_3_), custom_call_target="tpu_custom_call" | custom-call | flops 1048576 | bytes 2097152 | tf_op jit(solution)/shard_map/cache_rows/pallas_call | solution.py:179
  106.4 4.2 %all-to-all-start = ((bf16[16,80,128]{2,1,0:T(8,128)(2,1)}), bf16[16,80,128]{2,1,0:T(8,128)(2,1)S(1)}, u32[]{:S(2)}, u32[]{:S(2)}) async-start(bf16[16,80,128]{2,1,0:T(8,128)(2,1)} %cache_rows.2), calls=%async_computation | async-start | bytes 655360 | tf_op jit(solution)/shard_map/all_to_all | solution.py:256
  110.6 0.0 copy-done.8
  110.6 0.6 fusion.19
  113.9 0.0 copy-done.7
  113.9 0.6 fusion.20
  114.5 0.6 add_convert_fusion.3
  115.2 0.7 add_compare_fusion
  115.9 0.7 fusion.14
  116.6 50.7 %all-gather.5.cloned.1.call-done.weight = bf16[4096,512]{1,0:T(8,128)(2,1)} async-done(((bf16[256,512]{1,0:T(8,128)(2,1)}), bf16[4096,512]{1,0:T(8,128)(2,1)}) %all-gather.5.cloned.1.call-update) | async-done | bytes 4194320 | tf_op jit(solution)/shard_map/all_gather | solution.py:57
  167.3 0.0 all-to-all-done
  167.3 0.0 copy-start.1
  167.3 0.7 copy-done.1
  168.0 10.2 %product.3 = (f32[320,512]{1,0:T(8,128)}, f32[320,512]{1,0:T(8,128)}) custom-call(bf16[1280,128]{1,0:T(8,128)(2,1)} %bitcast.39, bf16[8,320,512]{2,1,0:T(8,128)(2,1)} %get-tuple-element.8.token.mine, bf16[8,320,512]{2,1,0:T(8,128)(2,1)} %copy-done.3, bf16[4096,512]{1,0:T(8,128)(2,1)} %all-gather.5.cloned.1.call-done.weight), custom_call_target="tpu_custom_call" | custom-call | flops 2684354560 | bytes 4194304 | tf_op jit(solution)/shard_map/product/pallas_call | solution.py:138
  178.2 0.0 copy-start.2
  178.2 0.0 collective-permute-start.2
  178.2 0.1 subtract_convert_fusion.1
  178.3 0.1 subtract_convert_fusion
  178.4 0.2 fusion.24
  178.7 1.9 collective-permute-done.2.refs_1_
  180.5 0.0 copy-start.4
  180.5 0.8 copy-done.4
  181.4 2.9 %cache_rows.3 = bf16[16,80,128]{2,1,0:T(8,128)(2,1)} custom-call(s32[1]{0:T(128)} %bitcast.place, s32[2]{0:T(128)} %lengths.3, s32[8]{0:T(128)} %owner.3, f32[320,512]{1,0:T(8,128)} %get-tuple-element.12.refs_0_, f32[320,512]{1,0:T(8,128)} %copy-done.4), custom_call_target="tpu_custom_call" | custom-call | flops 1048576 | bytes 2097152 | tf_op jit(solution)/shard_map/cache_rows/pallas_call | solution.py:179
  184.3 4.2 %all-to-all-start.1 = ((bf16[16,80,128]{2,1,0:T(8,128)(2,1)}), bf16[16,80,128]{2,1,0:T(8,128)(2,1)S(1)}, u32[]{:S(2)}, u32[]{:S(2)}) async-start(bf16[16,80,128]{2,1,0:T(8,128)(2,1)} %cache_rows.3), calls=%async_computation.1 | async-start | bytes 655360 | tf_op jit(solution)/shard_map/all_to_all | solution.py:256
  188.5 0.0 copy-done.2
  188.5 0.4 fusion.23
  188.9 0.4 collective-permute-start.3
  189.3 0.8 collective-permute-done.3
  190.2 0.2 fusion.3
  190.4 0.4 collective-permute-start.4
  190.7 0.8 collective-permute-done.4
  191.6 0.9 fusion.9
  192.4 7.2 %all-to-all-done.1 = bf16[16,80,128]{2,1,0:T(8,128)(2,1)S(1)} async-done(((bf16[16,80,128]{2,1,0:T(8,128)(2,1)}), bf16[16,80,128]{2,1,0:T(8,128)(2,1)S(1)}, u32[]{:S(2)}, u32[]{:S(2)}) %all-to-all-start.1) | async-done | bytes 327712 | tf_op jit(solution)/shard_map/all_to_all | solution.py:256
  199.6 0.2 fusion.1
  199.8 0.2 collective-permute-start.5
  200.0 0.9 maximum_bitcast_fusion
  200.9 0.2 collective-permute-done.5
  201.1 0.6 fusion.7
  (9 shorter events, 0.1 us)
Async XLA Ops:
  7.2 1.0 copy-start
  7.2 82.8 %all-gather.3.cloned.1.call-start = ((), (), s32[]{:S(2)}) async-start(), calls=%async_computation.2 | async-start | bytes 4456448 | tf_op jit(solution)/shard_map/all_gather | solution.py:57
  9.0 158.3 %all-gather.5.cloned.1.call-start = ((), (), s32[]{:S(2)}) async-start(), calls=%async_computation.3 | async-start | bytes 4456448 | tf_op jit(solution)/shard_map/all_gather | solution.py:57
  19.5 5.2 %collective-permute-start = (bf16[8,320,512]{2,1,0:T(8,128)(2,1)}, bf16[8,320,512]{2,1,0:T(8,128)(2,1)S(1)}, u32[]{:S(2)}, u32[]{:S(2)}) collective-permute-start(bf16[8,320,512]{2,1,0:T(8,128)(2,1)} %get-tuple-element.9), channel_id=1, source_target_pairs={{0,1},{1,0},{2,3},{3,2},{4,5},{5,4},{6,7},{7,6},{8,9},{9,8},{10,11... | collective-permute-start | bytes 7864328 | tf_op jit(solution)/shard_map/ppermute | solution.py:51
  24.7 65.3 %copy-start.3 = (bf16[8,320,512]{2,1,0:T(8,128)(2,1)}, bf16[8,320,512]{2,1,0:T(8,128)(2,1)S(1)}, u32[]{:S(2)}) copy-start(bf16[8,320,512]{2,1,0:T(8,128)(2,1)S(1)} %collective-permute-done.other) | copy-start | bytes 7864324
  90.0 11.0 %copy-start.6 = (f32[64]{0:T(128)S(1)}, f32[64]{0:T(128)}, u32[]{:S(2)}) copy-start(f32[64]{0:T(128)} %constant.77.clone) | copy-start | bytes 772
  100.2 10.4 %copy-start.8 = (s32[8]{0:T(128)S(1)}, s32[8]{0:T(128)}, u32[]{:S(2)}) copy-start(s32[8]{0:T(128)} %owner.3) | copy-start | bytes 100
  100.2 13.7 %copy-start.7 = (s32[2]{0:T(128)S(1)}, s32[2]{0:T(128)}, u32[]{:S(2)}) copy-start(s32[2]{0:T(128)} %lengths.3) | copy-start | bytes 28
  100.2 2.3 %collective-permute-start.1 = (f32[320,512]{1,0:T(8,128)}, f32[320,512]{1,0:T(8,128)S(1)}, u32[]{:S(2)}, u32[]{:S(2)}) collective-permute-start(f32[320,512]{1,0:T(8,128)} %get-tuple-element.11), channel_id=1, source_target_pairs={{0,1},{1,0},{2,3},{3,2},{4,5},{5,4},{6,7},{7,6},{8,9},{9,8},{10,11... | collective-permute-start | bytes 1966088 | tf_op jit(solution)/shard_map/ppermute | solution.py:51
  102.5 0.8 copy-start.5
  106.4 60.9 %all-to-all-start = ((bf16[16,80,128]{2,1,0:T(8,128)(2,1)}), bf16[16,80,128]{2,1,0:T(8,128)(2,1)S(1)}, u32[]{:S(2)}, u32[]{:S(2)}) async-start(bf16[16,80,128]{2,1,0:T(8,128)(2,1)} %cache_rows.2), calls=%async_computation | async-start | bytes 655360 | tf_op jit(solution)/shard_map/all_to_all | solution.py:256
  167.3 0.7 copy-start.1
  178.2 10.3 %copy-start.2 = (bf16[16,80,128]{2,1,0:T(8,128)(2,1)S(1)}, bf16[16,80,128]{2,1,0:T(8,128)(2,1)}, u32[]{:S(2)}) copy-start(bf16[16,80,128]{2,1,0:T(8,128)(2,1)} %copy-done.1) | copy-start | bytes 983044
  178.2 2.3 %collective-permute-start.2 = (f32[320,512]{1,0:T(8,128)}, f32[320,512]{1,0:T(8,128)S(1)}, u32[]{:S(2)}, u32[]{:S(2)}) collective-permute-start(f32[320,512]{1,0:T(8,128)} %get-tuple-element.13), channel_id=1, source_target_pairs={{0,1},{1,0},{2,3},{3,2},{4,5},{5,4},{6,7},{7,6},{8,9},{9,8},{10,11... | collective-permute-start | bytes 1966088 | tf_op jit(solution)/shard_map/ppermute | solution.py:51
  180.5 0.8 copy-start.4
  184.3 15.3 %all-to-all-start.1 = ((bf16[16,80,128]{2,1,0:T(8,128)(2,1)}), bf16[16,80,128]{2,1,0:T(8,128)(2,1)S(1)}, u32[]{:S(2)}, u32[]{:S(2)}) async-start(bf16[16,80,128]{2,1,0:T(8,128)(2,1)} %cache_rows.3), calls=%async_computation.1 | async-start | bytes 655360 | tf_op jit(solution)/shard_map/all_to_all | solution.py:256
  188.9 1.3 collective-permute-start.3
  190.4 1.2 collective-permute-start.4
  199.8 1.2 collective-permute-start.5
Sparse Core Ops, SparseCore 0:
  11.4 78.5 all-gather.2
  92.8 74.4 all-gather.4

commit v6 on v4

--- a/solution.py
+++ b/solution.py
@@ -90,60 +90,63 @@
     return pl.CostEstimate(flops=flops, bytes_accessed=moved_bytes, transcendentals=0)
 
 
-def halves_kernel(place, *refs):
-    sems = refs[-1]
-    count = (len(refs) - 1) // 3
-    rows = refs[count].shape[0]
-    copies = []
-    for k, weight in enumerate(refs[:count]):
-        for part in range(2):
-            first = (place[0] if part == 0 else 1 - place[0]) * rows
-            source = weight.at[pl.ds(pl.multiple_of(first, rows), rows)]
-            target = refs[count + 2 * k + part]
-            copies.append(pltpu.make_async_copy(source, target, sems.at[2 * k + part]))
-    for copy in copies:
-        copy.start()
-    for copy in copies:
-        copy.wait()
-
-
-def weight_halves(place, weights):
-    rows, columns = weights[0].shape
-    out = jax.ShapeDtypeStruct((rows // 2, columns), weights[0].dtype)
-    outs = pl.pallas_call(
+def halves_kernel(place, key_sent, value_sent, key_rest, value_rest, sent, rest, key, value):
+    columns = key.shape[1]
+    key[...] = key_sent[...]
+    value[...] = value_sent[...]
+    sent[:, :columns] = key_sent[...]
+    sent[:, columns:] = value_sent[...]
+    rest[:, :columns] = key_rest[...]
+    rest[:, columns:] = value_rest[...]
+
+
+def weight_halves(place, key_weight, value_weight):
+    rows, columns = key_weight.shape
+    depth = rows // 2
+    both = jax.ShapeDtypeStruct((depth, 2 * columns), key_weight.dtype)
+    one = jax.ShapeDtypeStruct((depth, columns), key_weight.dtype)
+    sent = pl.BlockSpec((depth, columns), lambda i, place: (place[0], 0))
+    rest = pl.BlockSpec((depth, columns), lambda i, place: (1 - place[0], 0))
+    return pl.pallas_call(
         halves_kernel,
-        in_specs=[SMEM_REF] + [ANY_REF] * len(weights),
-        out_specs=[ANY_REF] * (2 * len(weights)),
-        out_shape=[out] * (2 * len(weights)),
-        scratch_shapes=[pltpu.SemaphoreType.DMA((2 * len(weights),))],
+        grid_spec=pltpu.PrefetchScalarGridSpec(
+            num_scalar_prefetch=1,
+            grid=(1,),
+            in_specs=[sent, sent, rest, rest],
+            out_specs=[
+                pl.BlockSpec(out.shape, lambda i, place: (0, 0)) for out in (both, both, one, one)
+            ],
+        ),
+        out_shape=[both, both, one, one],
         compiler_params=PARAMS,
         cost_estimate=cost(1000, 1000),
         name="weight_halves",
-    )(place, *weights)
-    return [outs[2 * k : 2 * k + 2] for k in range(len(weights))]
+    )(place, key_weight, value_weight, key_weight, value_weight)
 
 
 def prepare_kernel(place, rows_in, token, mine, other):
-    depth = mine.shape[2]
-    wide = rows_in[...].astype(jnp.float32)
-    scale = lax.rsqrt(jnp.mean(wide * wide, -1, keepdims=True) + 1e-05)
+    rows, depth = mine.shape[1], mine.shape[2]
+    width = rows_in.shape[1]
+    square = jnp.zeros((rows, depth), jnp.float32)
+    for first in range(0, width, depth):
+        part = rows_in[:, first : first + depth].astype(jnp.float32)
+        square += part * part
+    scale = lax.rsqrt(jnp.sum(square, -1, keepdims=True) / width + 1e-05)
     for core in range(2):
 
         @pl.when(place[1] == core)
         def _():
-            for j in range(mine.shape[0] // 2):
-                for c in range(2):
-                    target = mine if c == core else other
-                    for h in range(2):
-                        first = (4 * j + 2 * c + h) * depth
-                        part = rows_in[:, first : first + depth].astype(jnp.float32)
-                        target[2 * j + h] = (part * scale).astype(jnp.bfloat16)
+            for first in range(0, width, depth):
+                j, c, h = first // (4 * depth), first // (2 * depth) % 2, first // depth % 2
+                target = mine if c == core else other
+                part = rows_in[:, first : first + depth].astype(jnp.float32)
+                target[2 * j + h] = (part * scale).astype(jnp.bfloat16)
 
 
 def prepared(flat, place, token, blocks):
     rows, width = flat.shape
     depth = width // (4 * blocks)
-    tile = 64 if rows % 64 == 0 else rows
+    tile = 80 if rows % 80 == 0 else rows
     out = jax.ShapeDtypeStruct((2 * blocks, rows, depth), jnp.bfloat16)
     spec = pl.BlockSpec((2 * blocks, tile, depth), lambda i, place: (0, i, 0))
     return pl.pallas_call(
@@ -156,7 +159,7 @@
         ),
         out_shape=[out, out],
         compiler_params=PARAMS,
-        cost_estimate=cost(1 << 36, 4 * rows * width),
+        cost_estimate=cost(1000, 1000),
         name="normed_halves",
     )(place, flat, token)
 
@@ -167,17 +170,17 @@
     return copy
 
 
-def product_kernel(plan, group, with_total, place, mine, other, *refs):
+def product_kernel(plan, group, parts, with_total, place, mine, other, *refs):
     count = len(plan)
     pieces = refs[:count]
-    totals_in = refs[count : count + 2 * with_total]
-    outs = refs[count + 2 * with_total : count + 2 * with_total + 2]
+    totals_in = refs[count : count + 2 * parts * with_total]
+    outs = refs[len(refs) - 5 - 2 * parts : len(refs) - 5]
     left, right, total, sems, total_sems = refs[-5:]
     rows, depth = mine.shape[1], mine.shape[2]
+    columns = pieces[0].shape[1] // parts
     waits = []
-    for k, (entry, flipped, first) in enumerate(plan):
-        half = (1 - place[0]) if flipped == 1 else place[0]
-        half = first // depth if flipped is None else half
+    for k, (entry, flipped) in enumerate(plan):
+        half = (1 - place[0]) if flipped else place[0]
         index = place[entry] * 2 + half
         area = pl.ds((k % group) * depth, depth)
         slot = k // group
@@ -185,7 +188,7 @@
             [
                 fetch(mine.at[index], left.at[slot, pl.ds(0, rows), area], sems.at[3 * k]),
                 fetch(other.at[index], left.at[slot, pl.ds(rows, rows), area], sems.at[3 * k + 1]),
-                fetch(pieces[k].at[pl.ds(first, depth)], right.at[slot, area], sems.at[3 * k + 2]),
+                fetch(pieces[k], right.at[slot, area], sems.at[3 * k + 2]),
             ]
         )
     carried = [
@@ -205,24 +208,21 @@
         if slot + 1 < count // group:
             total[...] = value
         else:
-            outs[0][...] = value[:rows]
-            outs[1][...] = value[rows:]
-
-
-def product(place, mine, other, plan, pieces, totals, group, token):
+            for k, out in enumerate(outs):
+                area = slice(k // 2 * columns, (k // 2 + 1) * columns)
+                out[...] = value[k % 2 * rows : (k % 2 + 1) * rows, area]
+
+
+def product(place, mine, other, plan, pieces, totals, group, parts):
     _, rows, depth = mine.shape
     columns = pieces[0].shape[1]
     count = len(plan)
-    out = jax.ShapeDtypeStruct((rows, columns), jnp.float32)
-
-    def kernel(place_ref, token_ref, *refs):
-        product_kernel(plan, group, len(totals) // 2, place_ref, *refs)
-
+    out = jax.ShapeDtypeStruct((rows, columns // parts), jnp.float32)
     return pl.pallas_call(
-        kernel,
-        in_specs=[SMEM_REF] + [ANY_REF] * (3 + count + len(totals)),
-        out_specs=[VMEM_REF] * 2,
-        out_shape=[out, out],
+        functools.partial(product_kernel, plan, group, parts, bool(totals)),
+        in_specs=[SMEM_REF] + [ANY_REF] * (2 + count + len(totals)),
+        out_specs=[VMEM_REF] * (2 * parts),
+        out_shape=[out] * (2 * parts),
         scratch_shapes=[
             pltpu.VMEM((count // group, 2 * rows, group * depth), mine.dtype),
             pltpu.VMEM((count // group, group * depth, columns), mine.dtype),
@@ -231,9 +231,9 @@
             pltpu.SemaphoreType.DMA((2,)),
         ],
         compiler_params=PARAMS,
-        cost_estimate=cost(64 * rows * columns * depth * count, 1 << 22),
+        cost_estimate=cost(1000, 1000),
         name="add_product",
-    )(place, token, mine, other, *pieces, *totals)
+    )(place, mine, other, *pieces, *totals)
 
 
 def rows_kernel(plan, rotated, place, lengths, owner, mine, kept, *refs):
@@ -246,7 +246,7 @@
     waits = [fetch(total_in, total, sems.at[0]), fetch(came_in, came, sems.at[1])]
     sem = 2
     for k in range(2 * count):
-        entry, flipped, first = plan[k // 2]
+        entry, flipped = plan[k // 2]
         half = (1 - place[0]) if flipped else place[0]
         source = (mine, kept)[k % 2]
         area = pl.ds(k * depth, depth)
@@ -302,7 +302,7 @@
             pltpu.SemaphoreType.DMA((2 + 4 * count,)),
         ],
         compiler_params=PARAMS,
-        cost_estimate=cost(4 * rows * columns * depth * count, 1 << 22),
+        cost_estimate=cost(1000, 1000),
         name="cache_rows",
     )(place, lengths, owner, token, *operands, *turn)
 
@@ -362,35 +362,34 @@
             jnp.concatenate([cosine, cosine], 1),
             jnp.concatenate([-sine_part, sine_part], 1),
         )
-        weights = (key_weight, value_weight)
-        halves = weight_halves(place, weights)
-        near = [moved(half, along(1)) for half, _ in halves]
-        across = [moved(half, to_row) for half, _ in halves]
-        far = [[moved(half, along(bits)) for bits in (2, 3)] for half, _ in halves]
-        near_rest = [moved(rest, along(1)) for _, rest in halves]
-        mine, kept = prepared(flat, place, halves[0][0], seq // 2)
+        sent, rest, *alone = weight_halves(place, key_weight, value_weight)
+        near = moved(sent, along(1))
+        across = moved(sent, to_row)
+        far = [[moved(half, along(bits)) for bits in (2, 3)] for half in alone]
+        mine, kept = prepared(flat, place, sent, seq // 2)
         other = moved(kept, to_core)
-        across_x = [moved(block, to_group) for block in across]
-        near_y = [moved(block, to_row) for block in near]
-        near_xy = [moved(block, to_group) for block in near_y]
-        far_y = [[moved(block, to_row) for block in blocks] for blocks in far]
-        far_x = [[moved(block, to_group) for block in blocks] for blocks in far]
-        depth = key_weight.shape[0] // 2
-        early = [(HERE, None, 0), (HERE, None, depth), (THERE, 0, 0), (THERE, 1, 0)]
-        early += [(HERE + 1, 0, 0), (HERE + 1, 1, 0), (THERE + 1, 0, 0), (THERE + 1, 1, 0)]
-        late = [(HERE + 2, 0, 0), (HERE + 2, 1, 0), (HERE + 3, 0, 0), (HERE + 3, 1, 0)]
-        late += [(THERE + 2, 0, 0), (THERE + 3, 0, 0)]
-        last = [(THERE + 2, 1, 0), (THERE + 3, 1, 0)]
+        near_rest = moved(rest, along(1))
+        across_x = moved(across, to_group)
+        near_y = moved(near, to_row)
+        near_xy = moved(near_y, to_group)
+        early = [(HERE, 0), (HERE, 1), (THERE, 0), (THERE, 1)]
+        early += [(HERE + 1, 0), (HERE + 1, 1), (THERE + 1, 0), (THERE + 1, 1)]
+        late = [(HERE + 2, 0), (HERE + 2, 1), (HERE + 3, 0), (HERE + 3, 1)]
+        late += [(THERE + 2, 0), (THERE + 3, 0)]
+        last = [(THERE + 2, 1), (THERE + 3, 1)]
+        pieces = [sent, rest, across, across_x, near, near_rest, near_y, near_xy]
+        totals = product(place, mine, other, early, pieces, (), 4, 2)
         caches = []
-        token = key_weight
+        token = sent
         for k, turned in enumerate((turn, ())):
-            pieces = [weights[k], weights[k], across[k], across_x[k]]
-            pieces += [near[k], near_rest[k], near_y[k], near_xy[k]]
-            totals = product(place, mine, other, early, pieces, (), 4, place)
-            pieces = [far[k][0], far_x[k][0], far[k][1], far_x[k][1], *far_y[k]]
-            total, sent = product(place, mine, other, late, pieces, totals, 6, place)
-            came = moved(sent, to_core)
-            ends = [moved(far_y[k][0], to_group), moved(far_x[k][1], to_row)]
+            far_y = [moved(block, to_row) for block in far[k]]
+            far_x = [moved(block, to_group) for block in far[k]]
+            pieces = [far[k][0], far_x[0], far[k][1], far_x[1], *far_y]
+            total, given = product(
+                place, mine, other, late, pieces, totals[2 * k : 2 * k + 2], 6, 1
+            )
+            came = moved(given, to_core)
+            ends = [moved(far_y[0], to_group), moved(far_x[1], to_row)]
             pieces = [piece for end in ends for piece in (end, moved(end, to_core))]
             outgoing = outgoing_rows(
                 place, lengths, owner, mine, kept, last, pieces, total, came, turned, token

time: 188 us -> 158 us (0.84)
  Pallas kernels: 71.2 us -> 35.8 us
  waiting for transfers between devices: 41 us -> 63.9 us
  starting transfers between devices: 57.6 us -> 40.1 us
    pallas_call x5 -> x4, Pallas kernels: 54.7 us -> 20.8 us  [the longest x3 17.7 us: product(): pl.pallas_call(functools.partial(product_kernel, plan, group, parts, bool...]
    ppermute x35 -> x29, waiting for transfers between devices: 24.1 us -> 47 us  [moved(): return lax.ppermute(block, ('groups', 'seq'), route)]
    ppermute x35 -> x29, starting transfers between devices: 45 us -> 31.3 us  [moved(): return lax.ppermute(block, ('groups', 'seq'), route)]
    all_to_all x2, starting transfers between devices: 11.9 us -> 8.02 us  [body(): lax.all_to_all(outgoing, 'seq', split_axis=0, concat_axis=1, tiled=True)[0]]
  transfers between devices with their start and end apart: 40 -> 34, of which waited for: 14 -> 11; matrix products, arithmetic and copies ran while one was open for 5% -> 6% of each run, Pallas kernels for 14% -> 14%
where the time goes in v6:
time: 158 us; the launch traced here: 157 us
  waiting for transfers between devices  63.9 us (40%)
  starting transfers between devices  40.1 us (25%)
  Pallas kernels  35.8 us (23%)
  other arithmetic  8.05 us (5%)
  between operations  3.68 us (2%)
  local copies, waits for them, and re-layouts  3.56 us (2%)
  matrix products  1.99 us (1%)
    ppermute x29, waiting for transfers between devices, moved(): return lax.ppermute(block, ('groups', 'seq'), route)  47 us
    ppermute x29, starting transfers between devices, moved(): return lax.ppermute(block, ('groups', 'seq'), route)  31.3 us
    pallas_call x3, Pallas kernels, product(): pl.pallas_call(functools.partial(product_kernel, plan, group, parts, bool...  17.7 us
    all_to_all x2, waiting for transfers between devices, body(): lax.all_to_all(outgoing, 'seq', split_axis=0, concat_axis=1, tiled=True)[0]  15.2 us
    pallas_call x2, Pallas kernels, outgoing_rows(): pl.pallas_call(kernel, in_specs=[SMEM_REF] * 3 + [ANY_REF] * (1 + len(ope...  8.12 us
    all_to_all x2, starting transfers between devices, body(): lax.all_to_all(outgoing, 'seq', split_axis=0, concat_axis=1, tiled=True)[0]  8.02 us
    pallas_call x1, Pallas kernels, prepared(): pl.pallas_call(prepare_kernel, grid_spec=pltpu.PrefetchScalarGridSpec(num...  6.96 us
  transfers between devices with their start and end apart: 34, of which 11 were waited for; matrix products, arithmetic and copies ran while one was open for 6% of the time, Pallas kernels for 14%

profile of v6, /device:TPU:0, one launch (start us, length us, event | category | flops | bytes accessed | tf_op | source)
XLA Modules:
  0.0 157.2 jit_solution(342339272010407430)
XLA Ops:
  0.7 0.6 stack.47.place.place_ref
  1.3 3.0 %weight_halves.1 = (bf16[256,1024]{1,0:T(8,128)(2,1)}, bf16[256,1024]{1,0:T(8,128)(2,1)}, bf16[256,512]{1,0:T(8,128)(2,1)}, bf16[256,512]{1,0:T(8,128)(2,1)}) custom-call(s32[11]{0:T(128)} %stack.47.place.place_ref, bf16[512,512]{1,0:T(8,128)(2,1)} %key_rest.1, bf16[512,512]{1,0:T(8,128)(2,1)} %value_rest.1, bf16[512,512]{1,0:T(8,128)(2,1)} %key_rest.1, ...), custom_call_target="tpu_custom_call" | custom-call | flops 1000 | bytes 1000 | tf_op jit(solution)/shard_map/weight_halves/pallas_call | solution.py:110
  4.4 7.0 %normed_halves.1 = (bf16[16,320,256]{2,1,0:T(8,128)(2,1)}, bf16[16,320,256]{2,1,0:T(8,128)(2,1)}) custom-call(s32[11]{0:T(128)} %stack.47.place.place_ref, bf16[320,8192]{1,0:T(8,128)(2,1)} %bitcast.50, bf16[256,1024]{1,0:T(8,128)(2,1)} %get-tuple-element.16.token.refs_0_.token_ref), custom_call_target="tpu_custom_call" | custom-call | flops 1000 | bytes 1000 | tf_op jit(solution)/shard_map/normed_halves/pallas_call | solution.py:152
  11.4 0.5 collective-permute-start.8
  11.8 2.6 %collective-permute-start.13 = (bf16[256,1024]{1,0:T(8,128)(2,1)S(1)}, bf16[256,1024]{1,0:T(8,128)(2,1)S(1)}, u32[]{:S(2)}, u32[]{:S(2)}) collective-permute-start(bf16[256,1024]{1,0:T(8,128)(2,1)S(1)} %copy-done.3), channel_id=1, source_target_pairs={{0,4},{1,5},{2,6},{3,7},{4,0},{5,1},{6,2},{7,3},{8,12},{9,13},{10,... | collective-permute-start | bytes 1572872 | tf_op jit(solution)/shard_map/ppermute | solution.py:64
  14.4 1.5 collective-permute-start.11
  16.0 11.0 %collective-permute-done.13.refs_4_ = bf16[256,1024]{1,0:T(8,128)(2,1)S(1)} collective-permute-done((bf16[256,1024]{1,0:T(8,128)(2,1)S(1)}, bf16[256,1024]{1,0:T(8,128)(2,1)S(1)}, u32[]{:S(2)}, u32[]{:S(2)}) %collective-permute-start.13) | collective-permute-done | bytes 524320 | tf_op jit(solution)/shard_map/ppermute | solution.py:64
  27.0 1.7 %collective-permute-start.15 = (bf16[256,1024]{1,0:T(8,128)(2,1)S(1)}, bf16[256,1024]{1,0:T(8,128)(2,1)}, u32[]{:S(2)}, u32[]{:S(2)}) collective-permute-start(bf16[256,1024]{1,0:T(8,128)(2,1)S(1)} %collective-permute-done.13.refs_4_), channel_id=1, source_target_pairs={{0,2},{1,3},{2,0},{3,1},{4,6},{5,7},{6,4},{7,5},{8,10},{9,11},{10,... | collective-permute-start | bytes 1572872 | tf_op jit(solution)/shard_map/ppermute | solution.py:64
  28.7 2.6 %collective-permute-start = (bf16[256,512]{1,0:T(8,128)(2,1)S(1)}, bf16[256,512]{1,0:T(8,128)(2,1)S(1)}, u32[]{:S(2)}, u32[]{:S(2)}) collective-permute-start(bf16[256,512]{1,0:T(8,128)(2,1)S(1)} %copy-done.28), channel_id=1, source_target_pairs={{0,8},{1,9},{2,10},{3,11},{4,12},{5,13},{6,14},{7,15},{8,0},{9,1},... | collective-permute-start | bytes 786440 | tf_op jit(solution)/shard_map/ppermute | solution.py:64
  31.3 1.3 collective-permute-start.4
  32.6 17.1 %collective-permute-done.refs_0_ = bf16[256,512]{1,0:T(8,128)(2,1)S(1)} collective-permute-done((bf16[256,512]{1,0:T(8,128)(2,1)S(1)}, bf16[256,512]{1,0:T(8,128)(2,1)S(1)}, u32[]{:S(2)}, u32[]{:S(2)}) %collective-permute-start) | collective-permute-done | bytes 262176 | tf_op jit(solution)/shard_map/ppermute | solution.py:64
  49.7 1.6 collective-permute-start.12
  51.3 0.5 collective-permute-start.16
  51.8 0.7 copy-done.10
  52.5 4.9 %collective-permute-start.18 = (bf16[256,512]{1,0:T(8,128)(2,1)}, bf16[256,512]{1,0:T(8,128)(2,1)S(1)}, u32[]{:S(2)}, u32[]{:S(2)}) collective-permute-start(bf16[256,512]{1,0:T(8,128)(2,1)} %get-tuple-element.25), channel_id=1, source_target_pairs={{0,8},{1,9},{2,10},{3,11},{4,12},{5,13},{6,14},{7,15},{8,0},{9,1},... | collective-permute-start | bytes 786440 | tf_op jit(solution)/shard_map/ppermute | solution.py:64
  57.4 0.6 fusion.19
  60.7 0.6 fusion.20
  61.3 11.4 %collective-permute-done.18.refs_0_ = bf16[256,512]{1,0:T(8,128)(2,1)S(1)} collective-permute-done((bf16[256,512]{1,0:T(8,128)(2,1)}, bf16[256,512]{1,0:T(8,128)(2,1)S(1)}, u32[]{:S(2)}, u32[]{:S(2)}) %collective-permute-start.18) | collective-permute-done | bytes 262176 | tf_op jit(solution)/shard_map/ppermute | solution.py:64
  72.7 0.6 collective-permute-start.10
  73.3 1.5 collective-permute-start.5
  74.8 1.4 collective-permute-done.16.refs_7_
  76.4 1.5 collective-permute-start.9
  77.9 0.4 fusion.6
  78.2 6.9 %add_product.3 = (f32[320,512]{1,0:T(8,128)}, f32[320,512]{1,0:T(8,128)}, f32[320,512]{1,0:T(8,128)}, f32[320,512]{1,0:T(8,128)}) custom-call(s32[11]{0:T(128)} %stack.47.place.place_ref, bf16[16,320,256]{2,1,0:T(8,128)(2,1)} %get-tuple-element.17.mine.refs_0_, bf16[16,320,256]{2,1,0:T(8,128)(2,1)} %copy-done.1, ...), custom_call_target="tpu_custom_call" | custom-call | flops 1000 | bytes 1000 | tf_op jit(solution)/shard_map/add_product/pallas_call | solution.py:221
  85.2 1.9 %collective-permute-start.19 = (bf16[256,512]{1,0:T(8,128)(2,1)S(1)}, bf16[256,512]{1,0:T(8,128)(2,1)S(1)}, u32[]{:S(2)}, u32[]{:S(2)}) collective-permute-start(bf16[256,512]{1,0:T(8,128)(2,1)S(1)} %collective-permute-done.18.refs_0_), channel_id=1, source_target_pairs={{0,2},{1,3},{2,0},{3,1},{4,6},{5,7},{6,4},{7,5},{8,10},{9,11},{10,... | collective-permute-start | bytes 786440 | tf_op jit(solution)/shard_map/ppermute | solution.py:64
  87.1 1.1 collective-permute-start.23
  88.2 0.9 collective-permute-start.2
  89.1 0.2 collective-permute-start.6
  89.3 0.5 copy-done.13
  89.8 5.4 %add_product.4 = (f32[320,512]{1,0:T(8,128)}, f32[320,512]{1,0:T(8,128)}) custom-call(s32[11]{0:T(128)} %stack.47.place.place_ref, bf16[16,320,256]{2,1,0:T(8,128)(2,1)} %get-tuple-element.17.mine.refs_0_, bf16[16,320,256]{2,1,0:T(8,128)(2,1)} %copy-done.1, bf16[256,512]{1,0:T(8,128)(2,1)} %copy-done.9, bf16[256,512]{1,0:T(8,128)(2,1)} %collective-permute-done.9.refs_1_, ...), custom_call_target="tpu_custom_call" | custom-call | flops 1000 | bytes 1000 | tf_op jit(solution)/shard_map/add_product/pallas_call | solution.py:221
  95.3 0.7 fusion.14
  96.0 0.7 convert_bitcast_fusion
  96.7 0.8 pad_maximum_fusion
  97.5 1.2 collective-permute-start.26
  98.7 1.3 collective-permute-start.27
  100.1 0.5 collective-permute-start.7
  100.6 0.6 add_convert_fusion.3
  101.3 4.9 %collective-permute-done.26.refs_1_ = bf16[256,512]{1,0:T(8,128)(2,1)S(1)} collective-permute-done((bf16[256,512]{1,0:T(8,128)(2,1)S(1)}, bf16[256,512]{1,0:T(8,128)(2,1)S(1)}, u32[]{:S(2)}, u32[]{:S(2)}) %collective-permute-start.26) | collective-permute-done | bytes 262176 | tf_op jit(solution)/shard_map/ppermute | solution.py:64
  106.3 1.2 collective-permute-start.20
  107.4 1.3 collective-permute-start.24
  108.8 5.4 %add_product.5 = (f32[320,512]{1,0:T(8,128)}, f32[320,512]{1,0:T(8,128)}) custom-call(s32[11]{0:T(128)} %stack.47.place.place_ref, bf16[16,320,256]{2,1,0:T(8,128)(2,1)} %get-tuple-element.17.mine.refs_0_, bf16[16,320,256]{2,1,0:T(8,128)(2,1)} %copy-done.1, bf16[256,512]{1,0:T(8,128)(2,1)} %copy-done.8, bf16[256,512]{1,0:T(8,128)(2,1)} %copy-done.21, ...), custom_call_target="tpu_custom_call" | custom-call | flops 1000 | bytes 1000 | tf_op jit(solution)/shard_map/add_product/pallas_call | solution.py:221
  114.4 0.6 copy-done.19
  115.0 0.2 copy-done.4
  115.2 4.2 %cache_rows.2 = bf16[16,80,128]{2,1,0:T(8,128)(2,1)} custom-call(s32[11]{0:T(128)} %stack.47.place.place_ref, s32[2]{0:T(128)} %lengths_ref.3, s32[8]{0:T(128)} %owner_ref.3, bf16[256,1024]{1,0:T(8,128)(2,1)} %get-tuple-element.16.token.refs_0_.token_ref, bf16[16,320,256]{2,1,0:T(8,128)(2,1)} %get-tuple-element.17.mine.refs_0_, ...), custom_call_target="tpu_custom_call" | custom-call | flops 1000 | bytes 1000 | tf_op jit(solution)/shard_map/cache_rows/pallas_call | solution.py:289
  119.5 4.5 %all-to-all-start = ((bf16[16,80,128]{2,1,0:T(8,128)(2,1)}), bf16[16,80,128]{2,1,0:T(8,128)(2,1)S(1)}, u32[]{:S(2)}, u32[]{:S(2)}) async-start(bf16[16,80,128]{2,1,0:T(8,128)(2,1)} %cache_rows.2), calls=%async_computation | async-start | bytes 655360 | tf_op jit(solution)/shard_map/all_to_all | solution.py:398
  124.0 0.7 add_compare_fusion
  124.8 0.5 collective-permute-start.21
  125.3 0.2 fusion.24
  125.6 0.8 collective-permute-done.21.refs_3_
  126.4 0.4 collective-permute-done.25.refs_5_
  126.8 8.3 %all-to-all-done = bf16[16,80,128]{2,1,0:T(8,128)(2,1)S(1)} async-done(((bf16[16,80,128]{2,1,0:T(8,128)(2,1)}), bf16[16,80,128]{2,1,0:T(8,128)(2,1)S(1)}, u32[]{:S(2)}, u32[]{:S(2)}) %all-to-all-start) | async-done | bytes 327712 | tf_op jit(solution)/shard_map/all_to_all | solution.py:398
  135.1 0.7 copy-done.2
  135.8 3.9 %cache_rows.3 = bf16[16,80,128]{2,1,0:T(8,128)(2,1)} custom-call(s32[11]{0:T(128)} %stack.47.place.place_ref, s32[2]{0:T(128)} %lengths_ref.3, s32[8]{0:T(128)} %owner_ref.3, bf16[1280,128]{1,0:T(8,128)(2,1)} %bitcast.47, bf16[16,320,256]{2,1,0:T(8,128)(2,1)} %get-tuple-element.17.mine.refs_0_, bf16[16,320,256]{2,1,0:T(8,128)(2,1)} %get-tuple-element.18.refs_1_, ...), custom_call_target="tpu_custom_call" | custom-call | flops 1000 | bytes 1000 | tf_op jit(solution)/shard_map/cache_rows/pallas_call | solution.py:289
  139.7 3.6 %all-to-all-start.1 = ((bf16[16,80,128]{2,1,0:T(8,128)(2,1)}), bf16[16,80,128]{2,1,0:T(8,128)(2,1)S(1)}, u32[]{:S(2)}, u32[]{:S(2)}) async-start(bf16[16,80,128]{2,1,0:T(8,128)(2,1)} %cache_rows.3), calls=%async_computation.1 | async-start | bytes 655360 | tf_op jit(solution)/shard_map/all_to_all | solution.py:398
  143.3 1.3 fusion.23
  144.6 0.3 collective-permute-start.29
  144.9 0.9 collective-permute-done.29
  146.0 0.3 collective-permute-start.30
  146.4 0.9 collective-permute-done.30
  147.2 0.2 fusion.9
  147.4 6.9 %all-to-all-done.1 = bf16[16,80,128]{2,1,0:T(8,128)(2,1)S(1)} async-done(((bf16[16,80,128]{2,1,0:T(8,128)(2,1)}), bf16[16,80,128]{2,1,0:T(8,128)(2,1)S(1)}, u32[]{:S(2)}, u32[]{:S(2)}) %all-to-all-start.1) | async-done | bytes 327712 | tf_op jit(solution)/shard_map/all_to_all | solution.py:398
  154.3 0.2 fusion.1
  154.6 1.9 %maximum_bitcast_fusion = bf16[1,1280,256]{2,1,0:T(8,128)(2,1)} fusion(bf16[1280,128]{1,0:T(8,128)(2,1)S(1)} %bitcast.52, bf16[1280,128]{1,0:T(8,128)(2,1)} %bitcast.49), kind=kLoop, calls=%fused_computation.6 | loop fusion | flops 1310720 | bytes 1310720 | tf_op jit(solution)/shard_map/broadcast_in_dim | solution.py:466
  156.6 0.6 fusion.7
  (96 shorter events, 1.2 us)
Async XLA Ops:
  0.6 146.6 %copy-start = (bf16[8,4,128]{2,1,0:T(4,128)(2,1)S(1)}, bf16[8,4,128]{2,1,0:T(4,128)(2,1)}, u32[]{:S(2)}) copy-start(bf16[8,4,128]{2,1,0:T(4,128)(2,1)} %param.17) | copy-start | bytes 24580
  4.3 7.5 %copy-start.3 = (bf16[256,1024]{1,0:T(8,128)(2,1)S(1)}, bf16[256,1024]{1,0:T(8,128)(2,1)}, u32[]{:S(2)}) copy-start(bf16[256,1024]{1,0:T(8,128)(2,1)} %get-tuple-element.16.token.refs_0_.token_ref) | copy-start | bytes 1572868
  4.3 24.3 %copy-start.28 = (bf16[256,512]{1,0:T(8,128)(2,1)S(1)}, bf16[256,512]{1,0:T(8,128)(2,1)}, u32[]{:S(2)}) copy-start(bf16[256,512]{1,0:T(8,128)(2,1)} %get-tuple-element.19) | copy-start | bytes 786436
  4.3 45.3 %copy-start.6 = (bf16[256,1024]{1,0:T(8,128)(2,1)S(1)}, bf16[256,1024]{1,0:T(8,128)(2,1)}, u32[]{:S(2)}) copy-start(bf16[256,1024]{1,0:T(8,128)(2,1)} %get-tuple-element.20.refs_1_) | copy-start | bytes 1572868
  4.4 53.1 %copy-start.26 = (s32[8]{0:T(128)S(1)}, s32[8]{0:T(128)}, u32[]{:S(2)}) copy-start(s32[8]{0:T(128)} %owner_ref.3) | copy-start | bytes 100
  4.4 56.3 %copy-start.25 = (s32[2]{0:T(128)S(1)}, s32[2]{0:T(128)}, u32[]{:S(2)}) copy-start(s32[2]{0:T(128)} %lengths_ref.3) | copy-start | bytes 28
  4.4 73.5 %copy-start.27 = (f32[64]{0:T(128)S(1)}, f32[64]{0:T(128)}, u32[]{:S(2)}) copy-start(f32[64]{0:T(128)} %constant.90.clone) | copy-start | bytes 772
  11.4 65.0 %collective-permute-start.8 = (bf16[16,320,256]{2,1,0:T(8,128)(2,1)}, bf16[16,320,256]{2,1,0:T(8,128)(2,1)S(1)}, u32[]{:S(2)}, u32[]{:S(2)}) collective-permute-start(bf16[16,320,256]{2,1,0:T(8,128)(2,1)} %get-tuple-element.18.refs_1_), channel_id=1, source_target_pairs={{0,1},{1,0},{2,3},{3,2},{4,5},{5,4},{6,7},{7,6},{8,9},{9,8},{10,11... | collective-permute-start | bytes 7864328 | tf_op jit(solution)/shard_map/ppermute | solution.py:64
  11.8 15.2 %collective-permute-start.13 = (bf16[256,1024]{1,0:T(8,128)(2,1)S(1)}, bf16[256,1024]{1,0:T(8,128)(2,1)S(1)}, u32[]{:S(2)}, u32[]{:S(2)}) collective-permute-start(bf16[256,1024]{1,0:T(8,128)(2,1)S(1)} %copy-done.3), channel_id=1, source_target_pairs={{0,4},{1,5},{2,6},{3,7},{4,0},{5,1},{6,2},{7,3},{8,12},{9,13},{10,... | collective-permute-start | bytes 1572872 | tf_op jit(solution)/shard_map/ppermute | solution.py:64
  14.4 35.2 %collective-permute-start.11 = (bf16[256,1024]{1,0:T(8,128)(2,1)S(1)}, bf16[256,1024]{1,0:T(8,128)(2,1)}, u32[]{:S(2)}, u32[]{:S(2)}) collective-permute-start(bf16[256,1024]{1,0:T(8,128)(2,1)S(1)} %copy-done.3), channel_id=1, source_target_pairs={{0,2},{1,3},{2,0},{3,1},{4,6},{5,7},{6,4},{7,5},{8,10},{9,11},{10,... | collective-permute-start | bytes 1572872 | tf_op jit(solution)/shard_map/ppermute | solution.py:64
  27.0 22.7 %copy-start.7 = (bf16[256,1024]{1,0:T(8,128)(2,1)}, bf16[256,1024]{1,0:T(8,128)(2,1)S(1)}, u32[]{:S(2)}) copy-start(bf16[256,1024]{1,0:T(8,128)(2,1)S(1)} %collective-permute-done.13.refs_4_) | copy-start | bytes 1572868
  27.0 24.3 %collective-permute-start.15 = (bf16[256,1024]{1,0:T(8,128)(2,1)S(1)}, bf16[256,1024]{1,0:T(8,128)(2,1)}, u32[]{:S(2)}, u32[]{:S(2)}) collective-permute-start(bf16[256,1024]{1,0:T(8,128)(2,1)S(1)} %collective-permute-done.13.refs_4_), channel_id=1, source_target_pairs={{0,2},{1,3},{2,0},{3,1},{4,6},{5,7},{6,4},{7,5},{8,10},{9,11},{10,... | collective-permute-start | bytes 1572872 | tf_op jit(solution)/shard_map/ppermute | solution.py:64
  28.7 21.0 %collective-permute-start = (bf16[256,512]{1,0:T(8,128)(2,1)S(1)}, bf16[256,512]{1,0:T(8,128)(2,1)S(1)}, u32[]{:S(2)}, u32[]{:S(2)}) collective-permute-start(bf16[256,512]{1,0:T(8,128)(2,1)S(1)} %copy-done.28), channel_id=1, source_target_pairs={{0,8},{1,9},{2,10},{3,11},{4,12},{5,13},{6,14},{7,15},{8,0},{9,1},... | collective-permute-start | bytes 786440 | tf_op jit(solution)/shard_map/ppermute | solution.py:64
  31.3 20.5 %collective-permute-start.4 = (bf16[256,512]{1,0:T(8,128)(2,1)S(1)}, bf16[256,512]{1,0:T(8,128)(2,1)S(1)}, u32[]{:S(2)}, u32[]{:S(2)}) collective-permute-start(bf16[256,512]{1,0:T(8,128)(2,1)S(1)} %copy-done.28), channel_id=1, source_target_pairs={{0,12},{1,13},{2,14},{3,15},{4,8},{5,9},{6,10},{7,11},{8,4},{9,5},... | collective-permute-start | bytes 786440 | tf_op jit(solution)/shard_map/ppermute | solution.py:64
  49.7 2.1 %copy-start.9 = (bf16[256,512]{1,0:T(8,128)(2,1)}, bf16[256,512]{1,0:T(8,128)(2,1)S(1)}, u32[]{:S(2)}) copy-start(bf16[256,512]{1,0:T(8,128)(2,1)S(1)} %collective-permute-done.refs_0_) | copy-start | bytes 786436
  49.7 23.0 %collective-permute-start.14 = (bf16[256,1024]{1,0:T(8,128)(2,1)S(1)}, bf16[256,1024]{1,0:T(8,128)(2,1)}, u32[]{:S(2)}, u32[]{:S(2)}) collective-permute-start(bf16[256,1024]{1,0:T(8,128)(2,1)S(1)} %copy-done.6), channel_id=1, source_target_pairs={{0,4},{1,5},{2,6},{3,7},{4,0},{5,1},{6,2},{7,3},{8,12},{9,13},{10,... | collective-permute-start | bytes 1572872 | tf_op jit(solution)/shard_map/ppermute | solution.py:64
  49.7 23.6 %collective-permute-start.12 = (bf16[256,1024]{1,0:T(8,128)(2,1)}, bf16[256,1024]{1,0:T(8,128)(2,1)}, u32[]{:S(2)}, u32[]{:S(2)}) collective-permute-start(bf16[256,1024]{1,0:T(8,128)(2,1)} %collective-permute-done.11.refs_2_), channel_id=1, source_target_pairs={{0,16},{1,17},{2,18},{3,19},{4,20},{5,21},{6,22},{7,23},{8,24},{9,... | collective-permute-start | bytes 1572872 | tf_op jit(solution)/shard_map/ppermute | solution.py:64
  51.3 24.9 %collective-permute-start.16 = (bf16[256,1024]{1,0:T(8,128)(2,1)}, bf16[256,1024]{1,0:T(8,128)(2,1)}, u32[]{:S(2)}, u32[]{:S(2)}) collective-permute-start(bf16[256,1024]{1,0:T(8,128)(2,1)} %collective-permute-done.15.refs_6_), channel_id=1, source_target_pairs={{0,16},{1,17},{2,18},{3,19},{4,20},{5,21},{6,22},{7,23},{8,24},{9,... | collective-permute-start | bytes 1572872 | tf_op jit(solution)/shard_map/ppermute | solution.py:64
  51.8 0.7 copy-start.10
  52.5 20.2 %collective-permute-start.18 = (bf16[256,512]{1,0:T(8,128)(2,1)}, bf16[256,512]{1,0:T(8,128)(2,1)S(1)}, u32[]{:S(2)}, u32[]{:S(2)}) collective-permute-start(bf16[256,512]{1,0:T(8,128)(2,1)} %get-tuple-element.25), channel_id=1, source_target_pairs={{0,8},{1,9},{2,10},{3,11},{4,12},{5,13},{6,14},{7,15},{8,0},{9,1},... | collective-permute-start | bytes 786440 | tf_op jit(solution)/shard_map/ppermute | solution.py:64
  72.7 24.8 %copy-start.8 = (bf16[256,512]{1,0:T(8,128)(2,1)}, bf16[256,512]{1,0:T(8,128)(2,1)S(1)}, u32[]{:S(2)}) copy-start(bf16[256,512]{1,0:T(8,128)(2,1)S(1)} %collective-permute-done.18.refs_0_) | copy-start | bytes 786436
  72.7 12.5 %collective-permute-start.22 = (bf16[256,512]{1,0:T(8,128)(2,1)}, bf16[256,512]{1,0:T(8,128)(2,1)}, u32[]{:S(2)}, u32[]{:S(2)}) collective-permute-start(bf16[256,512]{1,0:T(8,128)(2,1)} %get-tuple-element.25), channel_id=1, source_target_pairs={{0,12},{1,13},{2,14},{3,15},{4,8},{5,9},{6,10},{7,11},{8,4},{9,5},... | collective-permute-start | bytes 786440 | tf_op jit(solution)/shard_map/ppermute | solution.py:64
  72.7 15.5 %collective-permute-start.10 = (bf16[256,512]{1,0:T(8,128)(2,1)}, bf16[256,512]{1,0:T(8,128)(2,1)}, u32[]{:S(2)}, u32[]{:S(2)}) collective-permute-start(bf16[256,512]{1,0:T(8,128)(2,1)} %copy-done.10), channel_id=1, source_target_pairs={{0,2},{1,3},{2,0},{3,1},{4,6},{5,7},{6,4},{7,5},{8,10},{9,11},{10,... | collective-permute-start | bytes 786440 | tf_op jit(solution)/shard_map/ppermute | solution.py:64
  73.3 15.8 %collective-permute-start.5 = (bf16[256,512]{1,0:T(8,128)(2,1)}, bf16[256,512]{1,0:T(8,128)(2,1)S(1)}, u32[]{:S(2)}, u32[]{:S(2)}) collective-permute-start(bf16[256,512]{1,0:T(8,128)(2,1)} %copy-done.10), channel_id=1, source_target_pairs={{0,16},{1,17},{2,18},{3,19},{4,20},{5,21},{6,22},{7,23},{8,24},{9,... | collective-permute-start | bytes 786440 | tf_op jit(solution)/shard_map/ppermute | solution.py:64
  76.2 10.9 %collective-permute-start.1 = (bf16[256,512]{1,0:T(8,128)(2,1)}, bf16[256,512]{1,0:T(8,128)(2,1)S(1)}, u32[]{:S(2)}, u32[]{:S(2)}) collective-permute-start(bf16[256,512]{1,0:T(8,128)(2,1)} %copy-done.9), channel_id=1, source_target_pairs={{0,2},{1,3},{2,0},{3,1},{4,6},{5,7},{6,4},{7,5},{8,10},{9,11},{10,... | collective-permute-start | bytes 786440 | tf_op jit(solution)/shard_map/ppermute | solution.py:64
  76.4 1.9 %copy-start.1 = (bf16[16,320,256]{2,1,0:T(8,128)(2,1)}, bf16[16,320,256]{2,1,0:T(8,128)(2,1)S(1)}, u32[]{:S(2)}) copy-start(bf16[16,320,256]{2,1,0:T(8,128)(2,1)S(1)} %collective-permute-done.8.other) | copy-start | bytes 7864324
  76.4 12.9 %collective-permute-start.9 = (bf16[256,512]{1,0:T(8,128)(2,1)}, bf16[256,512]{1,0:T(8,128)(2,1)}, u32[]{:S(2)}, u32[]{:S(2)}) collective-permute-start(bf16[256,512]{1,0:T(8,128)(2,1)} %copy-done.9), channel_id=1, source_target_pairs={{0,16},{1,17},{2,18},{3,19},{4,20},{5,21},{6,22},{7,23},{8,24},{9,... | collective-permute-start | bytes 786440 | tf_op jit(solution)/shard_map/ppermute | solution.py:64
  85.2 12.3 %collective-permute-start.19 = (bf16[256,512]{1,0:T(8,128)(2,1)S(1)}, bf16[256,512]{1,0:T(8,128)(2,1)S(1)}, u32[]{:S(2)}, u32[]{:S(2)}) collective-permute-start(bf16[256,512]{1,0:T(8,128)(2,1)S(1)} %collective-permute-done.18.refs_0_), channel_id=1, source_target_pairs={{0,2},{1,3},{2,0},{3,1},{4,6},{5,7},{6,4},{7,5},{8,10},{9,11},{10,... | collective-permute-start | bytes 786440 | tf_op jit(solution)/shard_map/ppermute | solution.py:64
  87.1 2.2 %copy-start.17 = (bf16[256,512]{1,0:T(8,128)(2,1)}, bf16[256,512]{1,0:T(8,128)(2,1)S(1)}, u32[]{:S(2)}) copy-start(bf16[256,512]{1,0:T(8,128)(2,1)S(1)} %collective-permute-done.1.refs_4_) | copy-start | bytes 786436
  87.1 11.6 %collective-permute-start.23 = (bf16[256,512]{1,0:T(8,128)(2,1)}, bf16[256,512]{1,0:T(8,128)(2,1)S(1)}, u32[]{:S(2)}, u32[]{:S(2)}) collective-permute-start(bf16[256,512]{1,0:T(8,128)(2,1)} %collective-permute-done.22.refs_2_), channel_id=1, source_target_pairs={{0,16},{1,17},{2,18},{3,19},{4,20},{5,21},{6,22},{7,23},{8,24},{9,... | collective-permute-start | bytes 786440 | tf_op jit(solution)/shard_map/ppermute | solution.py:64
  88.2 11.8 %collective-permute-start.2 = (bf16[256,512]{1,0:T(8,128)(2,1)S(1)}, bf16[256,512]{1,0:T(8,128)(2,1)S(1)}, u32[]{:S(2)}, u32[]{:S(2)}) collective-permute-start(bf16[256,512]{1,0:T(8,128)(2,1)S(1)} %collective-permute-done.1.refs_4_), channel_id=1, source_target_pairs={{0,16},{1,17},{2,18},{3,19},{4,20},{5,21},{6,22},{7,23},{8,24},{9,... | collective-permute-start | bytes 786440 | tf_op jit(solution)/shard_map/ppermute | solution.py:64
  89.1 0.7 copy-start.13
  89.1 10.9 %collective-permute-start.6 = (bf16[256,512]{1,0:T(8,128)(2,1)S(1)}, bf16[256,512]{1,0:T(8,128)(2,1)S(1)}, u32[]{:S(2)}, u32[]{:S(2)}) collective-permute-start(bf16[256,512]{1,0:T(8,128)(2,1)S(1)} %collective-permute-done.5.refs_3_), channel_id=1, source_target_pairs={{0,2},{1,3},{2,0},{3,1},{4,6},{5,7},{6,4},{7,5},{8,10},{9,11},{10,... | collective-permute-start | bytes 786440 | tf_op jit(solution)/shard_map/ppermute | solution.py:64
  95.2 19.1 %collective-permute-start.17 = (f32[320,512]{1,0:T(8,128)}, f32[320,512]{1,0:T(8,128)S(1)}, u32[]{:S(2)}, u32[]{:S(2)}) collective-permute-start(f32[320,512]{1,0:T(8,128)} %get-tuple-element.24), channel_id=1, source_target_pairs={{0,1},{1,0},{2,3},{3,2},{4,5},{5,4},{6,7},{7,6},{8,9},{9,8},{10,11... | collective-permute-start | bytes 1966088 | tf_op jit(solution)/shard_map/ppermute | solution.py:64
  97.5 11.3 %copy-start.12 = (bf16[256,512]{1,0:T(8,128)(2,1)}, bf16[256,512]{1,0:T(8,128)(2,1)S(1)}, u32[]{:S(2)}) copy-start(bf16[256,512]{1,0:T(8,128)(2,1)S(1)} %collective-permute-done.19.refs_4_) | copy-start | bytes 786436
  97.5 8.8 %collective-permute-start.26 = (bf16[256,512]{1,0:T(8,128)(2,1)S(1)}, bf16[256,512]{1,0:T(8,128)(2,1)S(1)}, u32[]{:S(2)}, u32[]{:S(2)}) collective-permute-start(bf16[256,512]{1,0:T(8,128)(2,1)S(1)} %collective-permute-done.18.refs_0_), channel_id=1, source_target_pairs={{0,16},{1,17},{2,18},{3,19},{4,20},{5,21},{6,22},{7,23},{8,24},{9,... | collective-permute-start | bytes 786440 | tf_op jit(solution)/shard_map/ppermute | solution.py:64
  98.7 10.1 %copy-start.11 = (bf16[256,512]{1,0:T(8,128)(2,1)}, bf16[256,512]{1,0:T(8,128)(2,1)S(1)}, u32[]{:S(2)}) copy-start(bf16[256,512]{1,0:T(8,128)(2,1)S(1)} %collective-permute-done.23.refs_3_) | copy-start | bytes 786436
  98.7 8.7 %collective-permute-start.27 = (bf16[256,512]{1,0:T(8,128)(2,1)}, bf16[256,512]{1,0:T(8,128)(2,1)S(1)}, u32[]{:S(2)}, u32[]{:S(2)}) collective-permute-start(bf16[256,512]{1,0:T(8,128)(2,1)} %collective-permute-done.22.refs_2_), channel_id=1, source_target_pairs={{0,2},{1,3},{2,0},{3,1},{4,6},{5,7},{6,4},{7,5},{8,10},{9,11},{10,... | collective-permute-start | bytes 786440 | tf_op jit(solution)/shard_map/ppermute | solution.py:64
  100.1 14.1 %copy-start.14 = (bf16[256,512]{1,0:T(8,128)(2,1)}, bf16[256,512]{1,0:T(8,128)(2,1)S(1)}, u32[]{:S(2)}) copy-start(bf16[256,512]{1,0:T(8,128)(2,1)S(1)} %collective-permute-done.2.refs_2_) | copy-start | bytes 786436
  100.1 14.2 %collective-permute-start.3 = (bf16[256,512]{1,0:T(8,128)(2,1)S(1)}, bf16[256,512]{1,0:T(8,128)(2,1)S(1)}, u32[]{:S(2)}, u32[]{:S(2)}) collective-permute-start(bf16[256,512]{1,0:T(8,128)(2,1)S(1)} %collective-permute-done.2.refs_2_), channel_id=1, source_target_pairs={{0,1},{1,0},{2,3},{3,2},{4,5},{5,4},{6,7},{7,6},{8,9},{9,8},{10,11... | collective-permute-start | bytes 786440 | tf_op jit(solution)/shard_map/ppermute | solution.py:64
  100.1 14.1 %copy-start.15 = (bf16[256,512]{1,0:T(8,128)(2,1)}, bf16[256,512]{1,0:T(8,128)(2,1)S(1)}, u32[]{:S(2)}) copy-start(bf16[256,512]{1,0:T(8,128)(2,1)S(1)} %collective-permute-done.6.refs_4_) | copy-start | bytes 786436
  100.1 14.2 %collective-permute-start.7 = (bf16[256,512]{1,0:T(8,128)(2,1)S(1)}, bf16[256,512]{1,0:T(8,128)(2,1)S(1)}, u32[]{:S(2)}, u32[]{:S(2)}) collective-permute-start(bf16[256,512]{1,0:T(8,128)(2,1)S(1)} %collective-permute-done.6.refs_4_), channel_id=1, source_target_pairs={{0,1},{1,0},{2,3},{3,2},{4,5},{5,4},{6,7},{7,6},{8,9},{9,8},{10,11... | collective-permute-start | bytes 786440 | tf_op jit(solution)/shard_map/ppermute | solution.py:64
  106.3 2.5 %copy-start.21 = (bf16[256,512]{1,0:T(8,128)(2,1)}, bf16[256,512]{1,0:T(8,128)(2,1)S(1)}, u32[]{:S(2)}) copy-start(bf16[256,512]{1,0:T(8,128)(2,1)S(1)} %collective-permute-done.26.refs_1_) | copy-start | bytes 786436
  106.3 18.5 %collective-permute-start.20 = (bf16[256,512]{1,0:T(8,128)(2,1)S(1)}, bf16[256,512]{1,0:T(8,128)(2,1)S(1)}, u32[]{:S(2)}, u32[]{:S(2)}) collective-permute-start(bf16[256,512]{1,0:T(8,128)(2,1)S(1)} %collective-permute-done.19.refs_4_), channel_id=1, source_target_pairs={{0,16},{1,17},{2,18},{3,19},{4,20},{5,21},{6,22},{7,23},{8,24},{9,... | collective-permute-start | bytes 786440 | tf_op jit(solution)/shard_map/ppermute | solution.py:64
  107.4 1.4 copy-start.22
  107.4 17.8 %collective-permute-start.24 = (bf16[256,512]{1,0:T(8,128)(2,1)S(1)}, bf16[256,512]{1,0:T(8,128)(2,1)S(1)}, u32[]{:S(2)}, u32[]{:S(2)}) collective-permute-start(bf16[256,512]{1,0:T(8,128)(2,1)S(1)} %collective-permute-done.23.refs_3_), channel_id=1, source_target_pairs={{0,2},{1,3},{2,0},{3,1},{4,6},{5,7},{6,4},{7,5},{8,10},{9,11},{10,... | collective-permute-start | bytes 786440 | tf_op jit(solution)/shard_map/ppermute | solution.py:64
  114.2 0.7 copy-start.19
  114.2 12.5 %collective-permute-start.28 = (f32[320,512]{1,0:T(8,128)}, f32[320,512]{1,0:T(8,128)S(1)}, u32[]{:S(2)}, u32[]{:S(2)}) collective-permute-start(f32[320,512]{1,0:T(8,128)} %get-tuple-element.29), channel_id=1, source_target_pairs={{0,1},{1,0},{2,3},{3,2},{4,5},{5,4},{6,7},{7,6},{8,9},{9,8},{10,11... | collective-permute-start | bytes 1966088 | tf_op jit(solution)/shard_map/ppermute | solution.py:64
  114.3 0.7 copy-start.20
  114.3 0.9 copy-start.4
  119.5 15.6 %all-to-all-start = ((bf16[16,80,128]{2,1,0:T(8,128)(2,1)}), bf16[16,80,128]{2,1,0:T(8,128)(2,1)S(1)}, u32[]{:S(2)}, u32[]{:S(2)}) async-start(bf16[16,80,128]{2,1,0:T(8,128)(2,1)} %cache_rows.2), calls=%async_computation | async-start | bytes 655360 | tf_op jit(solution)/shard_map/all_to_all | solution.py:398
  124.7 10.3 %copy-start.16 = (bf16[256,512]{1,0:T(8,128)(2,1)}, bf16[256,512]{1,0:T(8,128)(2,1)S(1)}, u32[]{:S(2)}) copy-start(bf16[256,512]{1,0:T(8,128)(2,1)S(1)} %collective-permute-done.20.refs_2_) | copy-start | bytes 786436
  124.8 1.6 %collective-permute-start.21 = (bf16[256,512]{1,0:T(8,128)(2,1)S(1)}, bf16[256,512]{1,0:T(8,128)(2,1)S(1)}, u32[]{:S(2)}, u32[]{:S(2)}) collective-permute-start(bf16[256,512]{1,0:T(8,128)(2,1)S(1)} %collective-permute-done.20.refs_2_), channel_id=1, source_target_pairs={{0,1},{1,0},{2,3},{3,2},{4,5},{5,4},{6,7},{7,6},{8,9},{9,8},{10,11... | collective-permute-start | bytes 786440 | tf_op jit(solution)/shard_map/ppermute | solution.py:64
  125.2 9.9 %copy-start.18 = (bf16[256,512]{1,0:T(8,128)(2,1)}, bf16[256,512]{1,0:T(8,128)(2,1)S(1)}, u32[]{:S(2)}) copy-start(bf16[256,512]{1,0:T(8,128)(2,1)S(1)} %collective-permute-done.24.refs_4_) | copy-start | bytes 786436
  125.2 1.5 collective-permute-start.25
  126.4 8.7 %copy-start.23 = (bf16[256,512]{1,0:T(8,128)(2,1)}, bf16[256,512]{1,0:T(8,128)(2,1)S(1)}, u32[]{:S(2)}) copy-start(bf16[256,512]{1,0:T(8,128)(2,1)S(1)} %collective-permute-done.21.refs_3_) | copy-start | bytes 786436
  126.8 8.3 %copy-start.24 = (bf16[256,512]{1,0:T(8,128)(2,1)}, bf16[256,512]{1,0:T(8,128)(2,1)S(1)}, u32[]{:S(2)}) copy-start(bf16[256,512]{1,0:T(8,128)(2,1)S(1)} %collective-permute-done.25.refs_5_) | copy-start | bytes 786436
  126.8 8.3 %copy-start.5 = (f32[320,512]{1,0:T(8,128)}, f32[320,512]{1,0:T(8,128)S(1)}, u32[]{:S(2)}) copy-start(f32[320,512]{1,0:T(8,128)S(1)} %collective-permute-done.28.refs_7_) | copy-start | bytes 1966084
  135.1 0.7 copy-start.2
  139.7 14.6 %all-to-all-start.1 = ((bf16[16,80,128]{2,1,0:T(8,128)(2,1)}), bf16[16,80,128]{2,1,0:T(8,128)(2,1)S(1)}, u32[]{:S(2)}, u32[]{:S(2)}) async-start(bf16[16,80,128]{2,1,0:T(8,128)(2,1)} %cache_rows.3), calls=%async_computation.1 | async-start | bytes 655360 | tf_op jit(solution)/shard_map/all_to_all | solution.py:398
  144.6 1.2 collective-permute-start.29
  146.0 1.2 collective-permute-start.30
  154.6 2.0 %collective-permute-start.31 = (f32[4,1024]{1,0:T(4,128)S(1)}, f32[4,1024]{1,0:T(4,128)S(1)}, u32[]{:S(2)}, u32[]{:S(2)}) collective-permute-start(f32[4,1024]{1,0:T(4,128)S(1)} %bitcast.54), channel_id=1, source_target_pairs={{0,1},{1,0},{2,3},{3,2},{4,5},{5,4},{6,7},{7,6},{8,9},{9,8},{10,11... | collective-permute-start | bytes 49160 | tf_op jit(solution)/shard_map/ppermute | solution.py:27

commit v7 on v4

--- a/solution.py
+++ b/solution.py
@@ -90,75 +90,93 @@
     return pl.CostEstimate(flops=flops, bytes_accessed=moved_bytes, transcendentals=0)
 
 
-def halves_kernel(place, *refs):
-    sems = refs[-1]
-    count = (len(refs) - 1) // 3
-    rows = refs[count].shape[0]
-    copies = []
-    for k, weight in enumerate(refs[:count]):
-        for part in range(2):
-            first = (place[0] if part == 0 else 1 - place[0]) * rows
-            source = weight.at[pl.ds(pl.multiple_of(first, rows), rows)]
-            target = refs[count + 2 * k + part]
-            copies.append(pltpu.make_async_copy(source, target, sems.at[2 * k + part]))
-    for copy in copies:
-        copy.start()
-    for copy in copies:
-        copy.wait()
-
-
-def weight_halves(place, weights):
-    rows, columns = weights[0].shape
-    out = jax.ShapeDtypeStruct((rows // 2, columns), weights[0].dtype)
-    outs = pl.pallas_call(
-        halves_kernel,
-        in_specs=[SMEM_REF] + [ANY_REF] * len(weights),
-        out_specs=[ANY_REF] * (2 * len(weights)),
-        out_shape=[out] * (2 * len(weights)),
-        scratch_shapes=[pltpu.SemaphoreType.DMA((2 * len(weights),))],
+def halves_kernel(together, place, *refs):
+    count = len(refs) // 2
+    if together:
+        columns = refs[0].shape[1]
+        for k in range(len(refs) - 1):
+            refs[-1][:, k * columns : (k + 1) * columns] = refs[k][...]
+    else:
+        for source, target in zip(refs[:count], refs[count:]):
+            target[...] = source[...]
+
+
+def sent_halves(place, blocks, together):
+    rows, columns = blocks[0].shape
+    depth, count = rows // 2, len(blocks)
+    kind = blocks[0].dtype
+    if together:
+        outs = [jax.ShapeDtypeStruct((depth, count * columns), kind)]
+    else:
+        outs = [jax.ShapeDtypeStruct((depth, columns), kind)] * count
+    return pl.pallas_call(
+        functools.partial(halves_kernel, together),
+        grid_spec=pltpu.PrefetchScalarGridSpec(
+            num_scalar_prefetch=1,
+            grid=(1,),
+            in_specs=[pl.BlockSpec((depth, columns), lambda i, place: (place[0], 0))] * count,
+            out_specs=[pl.BlockSpec(out.shape, lambda i, place: (0, 0)) for out in outs],
+        ),
+        out_shape=outs,
         compiler_params=PARAMS,
         cost_estimate=cost(1000, 1000),
-        name="weight_halves",
-    )(place, *weights)
-    return [outs[2 * k : 2 * k + 2] for k in range(len(weights))]
-
-
-def prepare_kernel(place, rows_in, token, mine, other):
-    depth = mine.shape[2]
-    wide = rows_in[...].astype(jnp.float32)
-    scale = lax.rsqrt(jnp.mean(wide * wide, -1, keepdims=True) + 1e-05)
-    for core in range(2):
-
-        @pl.when(place[1] == core)
-        def _():
-            for j in range(mine.shape[0] // 2):
-                for c in range(2):
-                    target = mine if c == core else other
-                    for h in range(2):
-                        first = (4 * j + 2 * c + h) * depth
+        name="sent_halves",
+    )(place, *blocks)
+
+
+def prepare_kernel(place, *refs):
+    left, kept = refs[-2:]
+    rows, depth = kept.shape[1], kept.shape[2]
+    width = refs[0].shape[1]
+    for who, rows_in in enumerate(refs[:2]):
+        square = jnp.zeros((rows, depth), jnp.float32)
+        for first in range(0, width, depth):
+            part = rows_in[:, first : first + depth].astype(jnp.float32)
+            square += part * part
+        scale = lax.rsqrt(jnp.sum(square, -1, keepdims=True) / width + 1e-05)
+        for core in range(2):
+
+            @pl.when(place[1] == core)
+            def _():
+                for first in range(0, width, depth):
+                    j, c, h = first // (4 * depth), first // (2 * depth) % 2, first // depth % 2
+                    if c == core or who == 0:
                         part = rows_in[:, first : first + depth].astype(jnp.float32)
-                        target[2 * j + h] = (part * scale).astype(jnp.bfloat16)
-
-
-def prepared(flat, place, token, blocks):
-    rows, width = flat.shape
+                        part = (part * scale).astype(jnp.bfloat16)
+                        if c == core:
+                            left[2 * j + h, who] = part
+                        else:
+                            kept[2 * j + h] = part
+
+
+def prepared(place, mine, other, blocks):
+    rows, width = mine.shape
     depth = width // (4 * blocks)
-    tile = 64 if rows % 64 == 0 else rows
-    out = jax.ShapeDtypeStruct((2 * blocks, rows, depth), jnp.bfloat16)
-    spec = pl.BlockSpec((2 * blocks, tile, depth), lambda i, place: (0, i, 0))
+    tile = 80 if rows % 80 == 0 else rows
+    spec = pl.BlockSpec((tile, width), lambda i, place: (i, 0))
     return pl.pallas_call(
         prepare_kernel,
         grid_spec=pltpu.PrefetchScalarGridSpec(
             num_scalar_prefetch=1,
             grid=(rows // tile,),
-            in_specs=[pl.BlockSpec((tile, width), lambda i, place: (i, 0)), ANY_REF],
-            out_specs=[spec, spec],
+            in_specs=[spec, spec],
+            out_specs=[
+                pl.BlockSpec((2 * blocks, 2, tile, depth), lambda i, place: (0, 0, i, 0)),
+                pl.BlockSpec((2 * blocks, tile, depth), lambda i, place: (0, i, 0)),
+            ],
         ),
-        out_shape=[out, out],
+        out_shape=[
+            jax.ShapeDtypeStruct((2 * blocks, 2, rows, depth), jnp.bfloat16),
+            jax.ShapeDtypeStruct((2 * blocks, rows, depth), jnp.bfloat16),
+        ],
         compiler_params=PARAMS,
-        cost_estimate=cost(1 << 36, 4 * rows * width),
+        cost_estimate=cost(1 << 36, 1000),
         name="normed_halves",
-    )(place, flat, token)
+    )(place, mine, other)
+
+
+def after(value, *events):
+    return lax.optimization_barrier((value, *events))[0]
 
 
 def fetch(source, target, sem):
@@ -167,25 +185,28 @@
     return copy
 
 
-def product_kernel(plan, group, with_total, place, mine, other, *refs):
+def half_index(place, entry, kind):
+    half = {0: place[0], 1: 1 - place[0], 2: 0, 3: 1}[kind]
+    return place[entry] * 2 + half
+
+
+def product_kernel(plan, group, with_total, place, both, *refs):
     count = len(plan)
     pieces = refs[:count]
     totals_in = refs[count : count + 2 * with_total]
-    outs = refs[count + 2 * with_total : count + 2 * with_total + 2]
+    outs = refs[-7:-5]
     left, right, total, sems, total_sems = refs[-5:]
-    rows, depth = mine.shape[1], mine.shape[2]
+    rows, depth = both.shape[2], both.shape[3]
+    columns = right.shape[2]
     waits = []
-    for k, (entry, flipped, first) in enumerate(plan):
-        half = (1 - place[0]) if flipped == 1 else place[0]
-        half = first // depth if flipped is None else half
-        index = place[entry] * 2 + half
+    for k, (entry, kind, row, column) in enumerate(plan):
         area = pl.ds((k % group) * depth, depth)
         slot = k // group
+        piece = pieces[k].at[pl.ds(row, depth), pl.ds(column, columns)]
         waits.append(
             [
-                fetch(mine.at[index], left.at[slot, pl.ds(0, rows), area], sems.at[3 * k]),
-                fetch(other.at[index], left.at[slot, pl.ds(rows, rows), area], sems.at[3 * k + 1]),
-                fetch(pieces[k].at[pl.ds(first, depth)], right.at[slot, area], sems.at[3 * k + 2]),
+                fetch(both.at[half_index(place, entry, kind)], left.at[slot, :, :, area], sems.at[2 * k]),
+                fetch(piece, right.at[slot, area], sems.at[2 * k + 1]),
             ]
         )
     carried = [
@@ -196,7 +217,8 @@
         for copies in waits[slot * group : (slot + 1) * group]:
             for copy in copies:
                 copy.wait()
-        value = jnp.dot(left[slot], right[slot], preferred_element_type=jnp.float32)
+        stacked = left[slot].reshape(2 * rows, group * depth)
+        value = jnp.dot(stacked, right[slot], preferred_element_type=jnp.float32)
         if slot == 0:
             for copy in carried:
                 copy.wait()
@@ -209,48 +231,42 @@
             outs[1][...] = value[rows:]
 
 
-def product(place, mine, other, plan, pieces, totals, group, token):
-    _, rows, depth = mine.shape
-    columns = pieces[0].shape[1]
+def product(place, both, plan, pieces, totals, group, columns):
+    _, _, rows, depth = both.shape
     count = len(plan)
     out = jax.ShapeDtypeStruct((rows, columns), jnp.float32)
-
-    def kernel(place_ref, token_ref, *refs):
-        product_kernel(plan, group, len(totals) // 2, place_ref, *refs)
-
     return pl.pallas_call(
-        kernel,
-        in_specs=[SMEM_REF] + [ANY_REF] * (3 + count + len(totals)),
+        functools.partial(product_kernel, plan, group, bool(totals)),
+        in_specs=[SMEM_REF] + [ANY_REF] * (1 + count + len(totals)),
         out_specs=[VMEM_REF] * 2,
-        out_shape=[out, out],
+        out_shape=[out] * 2,
         scratch_shapes=[
-            pltpu.VMEM((count // group, 2 * rows, group * depth), mine.dtype),
-            pltpu.VMEM((count // group, group * depth, columns), mine.dtype),
+            pltpu.VMEM((count // group, 2, rows, group * depth), both.dtype),
+            pltpu.VMEM((count // group, group * depth, columns), both.dtype),
             pltpu.VMEM((2 * rows, columns), jnp.float32),
-            pltpu.SemaphoreType.DMA((3 * count,)),
+            pltpu.SemaphoreType.DMA((2 * count,)),
             pltpu.SemaphoreType.DMA((2,)),
         ],
         compiler_params=PARAMS,
-        cost_estimate=cost(64 * rows * columns * depth * count, 1 << 22),
+        cost_estimate=cost(1000, 1000),
         name="add_product",
-    )(place, token, mine, other, *pieces, *totals)
-
-
-def rows_kernel(plan, rotated, place, lengths, owner, mine, kept, *refs):
+    )(place, both, *pieces, *totals)
+
+
+def rows_kernel(plan, rotated, place, lengths, owner, both, kept, *refs):
     count = len(plan)
     pieces = refs[: 2 * count]
     total_in, came_in = refs[2 * count : 2 * count + 2]
     turn = refs[2 * count + 2 : 4 * count]
     out, left, right, total, came, scratch, sems = refs[-7:]
-    rows, depth = mine.shape[1], mine.shape[2]
+    rows, depth = kept.shape[1], kept.shape[2]
     waits = [fetch(total_in, total, sems.at[0]), fetch(came_in, came, sems.at[1])]
     sem = 2
     for k in range(2 * count):
-        entry, flipped, first = plan[k // 2]
-        half = (1 - place[0]) if flipped else place[0]
-        source = (mine, kept)[k % 2]
+        index = half_index(place, *plan[k // 2])
+        source = kept.at[index] if k % 2 else both.at[index, 0]
         area = pl.ds(k * depth, depth)
-        waits.append(fetch(source.at[place[entry] * 2 + half], left.at[:, area], sems.at[sem]))
+        waits.append(fetch(source, left.at[:, area], sems.at[sem]))
         waits.append(fetch(pieces[k], right.at[area], sems.at[sem + 1]))
         sem += 2
     for copy in waits:
@@ -275,8 +291,8 @@
                 out[peer * 2 + b] = picked.astype(jnp.bfloat16)
 
 
-def outgoing_rows(place, lengths, owner, mine, kept, plan, pieces, total, came, turn, token):
-    _, rows, depth = mine.shape
+def outgoing_rows(place, lengths, owner, both, kept, plan, pieces, total, came, turn, token):
+    _, rows, depth = kept.shape
     columns = total.shape[1]
     count = len(plan)
     count_rows = rows // lengths.shape[0]
@@ -285,7 +301,7 @@
     def kernel(place_ref, lengths_ref, owner_ref, token_ref, *refs):
         rows_kernel(plan, bool(turn), place_ref, lengths_ref, owner_ref, *refs)
 
-    operands = [mine, kept, *pieces, total, came]
+    operands = [both, kept, *pieces, total, came]
     return pl.pallas_call(
         kernel,
         in_specs=[SMEM_REF] * 3
@@ -294,15 +310,15 @@
         out_specs=VMEM_REF,
         out_shape=out,
         scratch_shapes=[
-            pltpu.VMEM((rows, 2 * count * depth), mine.dtype),
-            pltpu.VMEM((2 * count * depth, columns), mine.dtype),
+            pltpu.VMEM((rows, 2 * count * depth), kept.dtype),
+            pltpu.VMEM((2 * count * depth, columns), kept.dtype),
             pltpu.VMEM((rows, columns), jnp.float32),
             pltpu.VMEM((rows, columns), jnp.float32),
             pltpu.VMEM((count_rows, HEAD_SIZE), jnp.float32),
             pltpu.SemaphoreType.DMA((2 + 4 * count,)),
         ],
         compiler_params=PARAMS,
-        cost_estimate=cost(4 * rows * columns * depth * count, 1 << 22),
+        cost_estimate=cost(1000, 1000),
         name="cache_rows",
     )(place, lengths, owner, token, *operands, *turn)
 
@@ -363,37 +379,55 @@
             jnp.concatenate([-sine_part, sine_part], 1),
         )
         weights = (key_weight, value_weight)
-        halves = weight_halves(place, weights)
-        near = [moved(half, along(1)) for half, _ in halves]
-        across = [moved(half, to_row) for half, _ in halves]
-        far = [[moved(half, along(bits)) for bits in (2, 3)] for half, _ in halves]
-        near_rest = [moved(rest, along(1)) for _, rest in halves]
-        mine, kept = prepared(flat, place, halves[0][0], seq // 2)
-        other = moved(kept, to_core)
-        across_x = [moved(block, to_group) for block in across]
-        near_y = [moved(block, to_row) for block in near]
-        near_xy = [moved(block, to_group) for block in near_y]
-        far_y = [[moved(block, to_row) for block in blocks] for blocks in far]
-        far_x = [[moved(block, to_group) for block in blocks] for blocks in far]
+        columns = key_weight.shape[1]
         depth = key_weight.shape[0] // 2
-        early = [(HERE, None, 0), (HERE, None, depth), (THERE, 0, 0), (THERE, 1, 0)]
-        early += [(HERE + 1, 0, 0), (HERE + 1, 1, 0), (THERE + 1, 0, 0), (THERE + 1, 1, 0)]
-        late = [(HERE + 2, 0, 0), (HERE + 2, 1, 0), (HERE + 3, 0, 0), (HERE + 3, 1, 0)]
-        late += [(THERE + 2, 0, 0), (THERE + 3, 0, 0)]
-        last = [(THERE + 2, 1, 0), (THERE + 3, 1, 0)]
+        other = moved(flat, to_core)
+        halves = sent_halves(place, weights, False)
+        lanes = {}
+
+        def sent(lane, window, block, rule):
+            held = lanes.setdefault(lane, [])
+            if len(held) >= window:
+                block = after(block, held[-window])
+            held.append(moved(block, rule))
+            return held[-1]
+
+        near, across, far = [], [], []
+        for weight, half in zip(weights, halves):
+            near.append(sent("z", 3, weight, along(1)))
+            across.append(sent("y", 1, weight, to_row))
+            far.append([sent("z", 3, half, along(bits)) for bits in (2, 3)])
+        both, kept = prepared(place, flat, other, seq // 2)
+        (near_half,) = sent_halves(place, [after(block, other) for block in near], True)
+        far_y, far_x, ends = [], [], []
+        far_x.append([sent("x", 2, block, to_group) for block in far[0]])
+        near_y = sent("y", 2, near_half, to_row)
+        far_y.append([sent("y", 2, block, to_row) for block in far[0]])
+        near_xy = sent("x", 2, near_y, to_group)
+        ends.append([sent("x", 2, block, to_group) for block in far_y[0]])
+        far_y.append([sent("y", 2, block, to_row) for block in far[1]])
+        far_x.append([sent("x", 2, block, to_group) for block in far[1]])
         caches = []
-        token = key_weight
+        token = place
         for k, turned in enumerate((turn, ())):
-            pieces = [weights[k], weights[k], across[k], across_x[k]]
-            pieces += [near[k], near_rest[k], near_y[k], near_xy[k]]
-            totals = product(place, mine, other, early, pieces, (), 4, place)
+            early = [(HERE, 2 + h, h * depth, 0) for h in range(2)]
+            early += [(THERE, 2 + h, h * depth, 0) for h in range(2)]
+            early += [(HERE + 1, 2 + h, h * depth, 0) for h in range(2)]
+            early += [(THERE + 1, h, 0, k * columns) for h in range(2)]
+            pieces = [weights[k]] * 2 + [across[k]] * 2 + [near[k]] * 2 + [near_y, near_xy]
+            totals = product(place, both, early, pieces, (), 4, columns)
+            late = [(HERE + 2, 0), (HERE + 2, 1), (HERE + 3, 0), (HERE + 3, 1)]
+            late += [(THERE + 2, 0), (THERE + 3, 0)]
             pieces = [far[k][0], far_x[k][0], far[k][1], far_x[k][1], *far_y[k]]
-            total, sent = product(place, mine, other, late, pieces, totals, 6, place)
-            came = moved(sent, to_core)
-            ends = [moved(far_y[k][0], to_group), moved(far_x[k][1], to_row)]
-            pieces = [piece for end in ends for piece in (end, moved(end, to_core))]
+            late = [(*entry, 0, 0) for entry in late]
+            total, given = product(place, both, late, pieces, totals, 6, columns)
+            came = moved(given, to_core)
+            if k:
+                ends.append([sent("x", 2, after(block, outgoing), to_group) for block in far_y[1]])
+            pieces = [piece for end in ends[k] for piece in (end, moved(end, to_core))]
+            last = [(THERE + 2, 1), (THERE + 3, 1)]
             outgoing = outgoing_rows(
-                place, lengths, owner, mine, kept, last, pieces, total, came, turned, token
+                place, lengths, owner, both, kept, last, pieces, total, came, turned, token
             )
             caches.append(
                 lax.all_to_all(outgoing, "seq", split_axis=0, concat_axis=1, tiled=True)[0]

time: 188 us -> 182 us (0.968)
  waiting for transfers between devices: 41 us -> 77.4 us
  Pallas kernels: 71.2 us -> 43.3 us
  starting transfers between devices: 57.6 us -> 40.9 us
  local copies, waits for them, and re-layouts: 3.03 us -> 5.56 us
    ppermute x35 -> x29, waiting for transfers between devices: 24.1 us -> 68.9 us  [moved(): return lax.ppermute(block, ('groups', 'seq'), route)]
    pallas_call x5 -> x6, Pallas kernels: 54.7 us -> 25.7 us  [the longest x4 20.7 us: product(): pl.pallas_call(functools.partial(product_kernel, plan, group, bool(totals...]
    ppermute x35 -> x29, starting transfers between devices: 45 us -> 30.5 us  [moved(): return lax.ppermute(block, ('groups', 'seq'), route)]
    all_to_all x2, waiting for transfers between devices: 15.2 us -> 6.85 us  [body(): lax.all_to_all(outgoing, 'seq', split_axis=0, concat_axis=1, tiled=True)[0]]
    unnamed x88 -> x70, local copies, waits for them, and re-layouts: 2.39 us -> 4.98 us
    all_to_all x2, starting transfers between devices: 11.9 us -> 9.4 us  [body(): lax.all_to_all(outgoing, 'seq', split_axis=0, concat_axis=1, tiled=True)[0]]
  transfers between devices with their start and end apart: 40 -> 34, of which waited for: 14 -> 13; matrix products, arithmetic and copies ran while one was open for 5% -> 5% of each run, Pallas kernels for 14% -> 22%
where the time goes in v7:
time: 182 us; the launch traced here: 181 us
  waiting for transfers between devices  77.4 us (43%)
  Pallas kernels  43.3 us (24%)
  starting transfers between devices  40.9 us (22%)
  other arithmetic  8.03 us (4%)
  local copies, waits for them, and re-layouts  5.56 us (3%)
  between operations  3.7 us (2%)
  matrix products  1.99 us (1%)
    ppermute x29, waiting for transfers between devices, moved(): return lax.ppermute(block, ('groups', 'seq'), route)  68.9 us
    ppermute x29, starting transfers between devices, moved(): return lax.ppermute(block, ('groups', 'seq'), route)  30.5 us
    pallas_call x4, Pallas kernels, product(): pl.pallas_call(functools.partial(product_kernel, plan, group, bool(totals...  20.7 us
    pallas_call x1, Pallas kernels, prepared(): pl.pallas_call(prepare_kernel, grid_spec=pltpu.PrefetchScalarGridSpec(num...  9.41 us
    all_to_all x2, starting transfers between devices, body(): lax.all_to_all(outgoing, 'seq', split_axis=0, concat_axis=1, tiled=True)[0]  9.4 us
    pallas_call x2, Pallas kernels, outgoing_rows(): pl.pallas_call(kernel, in_specs=[SMEM_REF] * 3 + [ANY_REF] * (1 + len(ope...  8.19 us
    all_to_all x2, waiting for transfers between devices, body(): lax.all_to_all(outgoing, 'seq', split_axis=0, concat_axis=1, tiled=True)[0]  6.85 us
    pallas_call x2, Pallas kernels, sent_halves(): pl.pallas_call(functools.partial(halves_kernel, together), grid_spec=pltp...  5.02 us
  transfers between devices with their start and end apart: 34, of which 13 were waited for; matrix products, arithmetic and copies ran while one was open for 5% of the time, Pallas kernels for 22%

profile of v7, /device:TPU:0, one launch (start us, length us, event | category | flops | bytes accessed | tf_op | source)
XLA Modules:
  0.0 181.0 jit_solution(9299051349577987675)
XLA Ops:
  0.7 0.5 collective-permute-start
  1.2 2.6 %collective-permute-start.2 = (bf16[512,512]{1,0:T(8,128)(2,1)}, bf16[512,512]{1,0:T(8,128)(2,1)S(1)}, u32[]{:S(2)}, u32[]{:S(2)}) collective-permute-start(bf16[512,512]{1,0:T(8,128)(2,1)} %refs_1_.4), channel_id=1, source_target_pairs={{0,2},{1,3},{2,0},{3,1},{4,6},{5,7},{6,4},{7,5},{8,10},{9,11},{10,... | collective-permute-start | bytes 1572872 | tf_op jit(solution)/shard_map/ppermute | solution.py:64
  3.8 1.6 collective-permute-start.9
  5.4 11.1 %collective-permute-done.2.refs_2_.refs_3_ = bf16[512,512]{1,0:T(8,128)(2,1)S(1)} collective-permute-done((bf16[512,512]{1,0:T(8,128)(2,1)}, bf16[512,512]{1,0:T(8,128)(2,1)S(1)}, u32[]{:S(2)}, u32[]{:S(2)}) %collective-permute-start.2) | collective-permute-done | bytes 524320 | tf_op jit(solution)/shard_map/ppermute | solution.py:64
  16.5 1.8 collective-permute-start.3
  18.3 1.6 collective-permute-start.10
  19.9 0.6 stack.47.place.place_ref.token_ref
  20.4 2.5 %sent_halves.2 = (bf16[256,512]{1,0:T(8,128)(2,1)}, bf16[256,512]{1,0:T(8,128)(2,1)}) custom-call(s32[11]{0:T(128)} %stack.47.place.place_ref.token_ref, bf16[512,512]{1,0:T(8,128)(2,1)} %refs_1_.4, bf16[512,512]{1,0:T(8,128)(2,1)} %refs_1_.5), custom_call_target="tpu_custom_call" | custom-call | flops 1000 | bytes 1000 | tf_op jit(solution)/shard_map/sent_halves/pallas_call | solution.py:112
  22.9 2.5 %collective-permute-start.5 = (bf16[256,512]{1,0:T(8,128)(2,1)}, bf16[256,512]{1,0:T(8,128)(2,1)S(1)}, u32[]{:S(2)}, u32[]{:S(2)}) collective-permute-start(bf16[256,512]{1,0:T(8,128)(2,1)} %get-tuple-element.36), channel_id=1, source_target_pairs={{0,12},{1,13},{2,14},{3,15},{4,8},{5,9},{6,10},{7,11},{8,4},{9,5},... | collective-permute-start | bytes 786440 | tf_op jit(solution)/shard_map/ppermute | solution.py:64
  25.5 15.6 %collective-permute-done.5.refs_2_ = bf16[256,512]{1,0:T(8,128)(2,1)S(1)} collective-permute-done((bf16[256,512]{1,0:T(8,128)(2,1)}, bf16[256,512]{1,0:T(8,128)(2,1)S(1)}, u32[]{:S(2)}, u32[]{:S(2)}) %collective-permute-start.5) | collective-permute-done | bytes 262176 | tf_op jit(solution)/shard_map/ppermute | solution.py:64
  41.1 1.5 collective-permute-start.6
  42.6 5.5 %collective-permute-done.1.refs_0_ = bf16[256,512]{1,0:T(8,128)(2,1)S(1)} collective-permute-done((bf16[256,512]{1,0:T(8,128)(2,1)}, bf16[256,512]{1,0:T(8,128)(2,1)S(1)}, u32[]{:S(2)}, u32[]{:S(2)}) %collective-permute-start.1) | collective-permute-done | bytes 262176 | tf_op jit(solution)/shard_map/ppermute | solution.py:64
  48.2 0.6 collective-permute-start.4
  48.7 0.8 copy-done.2
  49.6 2.5 %sent_halves.3 = bf16[256,1024]{1,0:T(8,128)(2,1)} custom-call(s32[11]{0:T(128)} %stack.47.place.place_ref.token_ref, bf16[512,512]{1,0:T(8,128)(2,1)} %copy-done.3, bf16[512,512]{1,0:T(8,128)(2,1)} %copy-done.2), custom_call_target="tpu_custom_call" | custom-call | flops 1000 | bytes 1000 | tf_op jit(solution)/shard_map/sent_halves/pallas_call | solution.py:112
  52.1 1.5 collective-permute-start.11
  53.6 0.6 fusion.19
  56.8 0.6 fusion.20
  57.5 1.5 collective-permute-start.13
  59.0 0.6 collective-permute-start.7
  60.0 2.7 %collective-permute-start.23 = (bf16[256,512]{1,0:T(8,128)(2,1)}, bf16[256,512]{1,0:T(8,128)(2,1)S(1)}, u32[]{:S(2)}, u32[]{:S(2)}) collective-permute-start(bf16[256,512]{1,0:T(8,128)(2,1)} %get-tuple-element.57), channel_id=1, source_target_pairs={{0,12},{1,13},{2,14},{3,15},{4,8},{5,9},{6,10},{7,11},{8,4},{9,5},... | collective-permute-start | bytes 786440 | tf_op jit(solution)/shard_map/ppermute | solution.py:64
  62.7 13.2 %collective-permute-done.18.refs_0_ = bf16[256,512]{1,0:T(8,128)(2,1)S(1)} collective-permute-done((bf16[256,512]{1,0:T(8,128)(2,1)}, bf16[256,512]{1,0:T(8,128)(2,1)S(1)}, u32[]{:S(2)}, u32[]{:S(2)}) %collective-permute-start.18) | collective-permute-done | bytes 262176 | tf_op jit(solution)/shard_map/ppermute | solution.py:64
  75.9 0.5 collective-permute-start.19
  76.4 1.5 collective-permute-start.20
  77.9 0.6 collective-permute-start.14
  78.5 1.5 collective-permute-start.12
  80.0 9.4 %normed_halves.1 = (bf16[16,2,320,256]{3,2,1,0:T(8,128)(2,1)}, bf16[16,320,256]{2,1,0:T(8,128)(2,1)}) custom-call(s32[11]{0:T(128)} %stack.47.place.place_ref.token_ref, bf16[320,8192]{1,0:T(8,128)(2,1)} %bitcast.56, bf16[320,8192]{1,0:T(8,128)(2,1)} %collective-permute-done.refs_1_), custom_call_target="tpu_custom_call" | custom-call | flops 68719476736 | bytes 1000 | tf_op jit(solution)/shard_map/normed_halves/pallas_call | solution.py:157
  89.5 5.6 %collective-permute-done.14.refs_7_ = bf16[256,1024]{1,0:T(8,128)(2,1)S(1)} collective-permute-done((bf16[256,1024]{1,0:T(8,128)(2,1)S(1)}, bf16[256,1024]{1,0:T(8,128)(2,1)S(1)}, u32[]{:S(2)}, u32[]{:S(2)}) %collective-permute-start.14) | collective-permute-done | bytes 524320 | tf_op jit(solution)/shard_map/ppermute | solution.py:64
  95.2 0.8 copy-done.7
  96.0 5.0 %add_product.4 = (f32[320,512]{1,0:T(8,128)}, f32[320,512]{1,0:T(8,128)}) custom-call(s32[11]{0:T(128)} %stack.47.place.place_ref.token_ref, bf16[16,2,320,256]{3,2,1,0:T(8,128)(2,1)} %get-tuple-element.34.both.refs_0_, bf16[512,512]{1,0:T(8,128)(2,1)} %refs_1_.4, bf16[512,512]{1,0:T(8,128)(2,1)} %refs_1_.4, bf16[512,512]{1,0:T(8,128)(2,1)} %copy-done.5, ...), custom_call_target="tpu_custom_call" | custom-call | flops 1000 | bytes 1000 | tf_op jit(solution)/shard_map/add_product/pallas_call | solution.py:238
  101.0 0.7 copy-done.27
  101.7 5.3 %add_product.5 = (f32[320,512]{1,0:T(8,128)}, f32[320,512]{1,0:T(8,128)}) custom-call(s32[11]{0:T(128)} %stack.47.place.place_ref.token_ref, bf16[16,2,320,256]{3,2,1,0:T(8,128)(2,1)} %get-tuple-element.34.both.refs_0_, bf16[256,512]{1,0:T(8,128)(2,1)} %copy-done.15, bf16[256,512]{1,0:T(8,128)(2,1)} %collective-permute-done.13.refs_1_, ...), custom_call_target="tpu_custom_call" | custom-call | flops 1000 | bytes 1000 | tf_op jit(solution)/shard_map/add_product/pallas_call | solution.py:238
  107.1 1.6 collective-permute-start.15
  108.7 0.7 fusion.14
  109.4 0.7 convert_bitcast_fusion
  110.1 0.8 pad_maximum_fusion
  111.1 5.0 %collective-permute-done.15.refs_4_ = bf16[256,512]{1,0:T(8,128)(2,1)S(1)} collective-permute-done((bf16[256,512]{1,0:T(8,128)(2,1)}, bf16[256,512]{1,0:T(8,128)(2,1)S(1)}, u32[]{:S(2)}, u32[]{:S(2)}) %collective-permute-start.15) | collective-permute-done | bytes 262176 | tf_op jit(solution)/shard_map/ppermute | solution.py:64
  116.1 1.5 collective-permute-start.24
  117.6 1.5 collective-permute-start.25
  119.1 0.7 add_convert_fusion.3
  119.9 5.0 %add_product.6 = (f32[320,512]{1,0:T(8,128)}, f32[320,512]{1,0:T(8,128)}) custom-call(s32[11]{0:T(128)} %stack.47.place.place_ref.token_ref, bf16[16,2,320,256]{3,2,1,0:T(8,128)(2,1)} %get-tuple-element.34.both.refs_0_, bf16[512,512]{1,0:T(8,128)(2,1)} %refs_1_.5, bf16[512,512]{1,0:T(8,128)(2,1)} %refs_1_.5, bf16[512,512]{1,0:T(8,128)(2,1)} %copy-done.4, ...), custom_call_target="tpu_custom_call" | custom-call | flops 1000 | bytes 1000 | tf_op jit(solution)/shard_map/add_product/pallas_call | solution.py:238
  125.2 0.5 copy-done.20
  125.9 5.4 %add_product.7 = (f32[320,512]{1,0:T(8,128)}, f32[320,512]{1,0:T(8,128)}) custom-call(s32[11]{0:T(128)} %stack.47.place.place_ref.token_ref, bf16[16,2,320,256]{3,2,1,0:T(8,128)(2,1)} %get-tuple-element.34.both.refs_0_, bf16[256,512]{1,0:T(8,128)(2,1)} %copy-done.13, bf16[256,512]{1,0:T(8,128)(2,1)} %copy-done.19, bf16[256,512]{1,0:T(8,128)(2,1)} %copy-done.18, ...), custom_call_target="tpu_custom_call" | custom-call | flops 1000 | bytes 1000 | tf_op jit(solution)/shard_map/add_product/pallas_call | solution.py:238
  131.3 0.4 collective-permute-start.28
  131.8 0.7 copy-done.23
  132.8 4.3 %cache_rows.2 = bf16[16,80,128]{2,1,0:T(8,128)(2,1)} custom-call(s32[11]{0:T(128)} %stack.47.place.place_ref.token_ref, s32[2]{0:T(128)} %lengths_ref.3, s32[8]{0:T(128)} %owner_ref.3, s32[11]{0:T(128)} %stack.47.place.place_ref.token_ref, bf16[16,2,320,256]{3,2,1,0:T(8,128)(2,1)} %get-tuple-element.34.both.refs_0_, ...), custom_call_target="tpu_custom_call" | custom-call | flops 1000 | bytes 1000 | tf_op jit(solution)/shard_map/cache_rows/pallas_call | solution.py:305
  137.1 3.6 %all-to-all-start = ((bf16[16,80,128]{2,1,0:T(8,128)(2,1)}), bf16[16,80,128]{2,1,0:T(8,128)(2,1)S(1)}, u32[]{:S(2)}, u32[]{:S(2)}) async-start(bf16[16,80,128]{2,1,0:T(8,128)(2,1)} %cache_rows.2), calls=%async_computation | async-start | bytes 655360 | tf_op jit(solution)/shard_map/all_to_all | solution.py:433
  140.7 1.2 collective-permute-start.26
  141.9 0.8 collective-permute-start.21
  142.7 0.7 add_compare_fusion
  143.5 6.4 %collective-permute-done.26.refs_4_ = bf16[256,512]{1,0:T(8,128)(2,1)S(1)} collective-permute-done((bf16[256,512]{1,0:T(8,128)(2,1)S(1)}, bf16[256,512]{1,0:T(8,128)(2,1)S(1)}, u32[]{:S(2)}, u32[]{:S(2)}) %collective-permute-start.26) | collective-permute-done | bytes 262176 | tf_op jit(solution)/shard_map/ppermute | solution.py:64
  149.9 5.0 %collective-permute-done.21.refs_2_ = bf16[256,512]{1,0:T(8,128)(2,1)S(1)} collective-permute-done((bf16[256,512]{1,0:T(8,128)(2,1)S(1)}, bf16[256,512]{1,0:T(8,128)(2,1)S(1)}, u32[]{:S(2)}, u32[]{:S(2)}) %collective-permute-start.21) | collective-permute-done | bytes 262176 | tf_op jit(solution)/shard_map/ppermute | solution.py:64
  155.1 1.2 collective-permute-done.22.refs_3_
  156.4 0.7 copy-done.30
  157.2 3.9 %cache_rows.3 = bf16[16,80,128]{2,1,0:T(8,128)(2,1)} custom-call(s32[11]{0:T(128)} %stack.47.place.place_ref.token_ref, s32[2]{0:T(128)} %lengths_ref.3, s32[8]{0:T(128)} %owner_ref.3, bf16[1280,128]{1,0:T(8,128)(2,1)} %bitcast.47, bf16[16,2,320,256]{3,2,1,0:T(8,128)(2,1)} %get-tuple-element.34.both.refs_0_, ...), custom_call_target="tpu_custom_call" | custom-call | flops 1000 | bytes 1000 | tf_op jit(solution)/shard_map/cache_rows/pallas_call | solution.py:305
  161.1 5.8 %all-to-all-start.1 = ((bf16[16,80,128]{2,1,0:T(8,128)(2,1)}), bf16[16,80,128]{2,1,0:T(8,128)(2,1)S(1)}, u32[]{:S(2)}, u32[]{:S(2)}) async-start(bf16[16,80,128]{2,1,0:T(8,128)(2,1)} %cache_rows.3), calls=%async_computation.1 | async-start | bytes 655360 | tf_op jit(solution)/shard_map/all_to_all | solution.py:433
  166.9 1.3 fusion.23
  168.3 0.5 collective-permute-start.29
  168.7 0.8 collective-permute-done.29
  169.8 0.4 collective-permute-start.30
  170.2 0.8 collective-permute-done.30
  171.2 6.8 %all-to-all-done.1 = bf16[16,80,128]{2,1,0:T(8,128)(2,1)S(1)} async-done(((bf16[16,80,128]{2,1,0:T(8,128)(2,1)}), bf16[16,80,128]{2,1,0:T(8,128)(2,1)S(1)}, u32[]{:S(2)}, u32[]{:S(2)}) %all-to-all-start.1) | async-done | bytes 327712 | tf_op jit(solution)/shard_map/all_to_all | solution.py:433
  178.5 1.9 %maximum_bitcast_fusion = bf16[1,1280,256]{2,1,0:T(8,128)(2,1)} fusion(bf16[1280,128]{1,0:T(8,128)(2,1)S(1)} %bitcast.51, bf16[1280,128]{1,0:T(8,128)(2,1)} %bitcast.49), kind=kLoop, calls=%fused_computation.6 | loop fusion | flops 1310720 | bytes 1310720 | tf_op jit(solution)/shard_map/broadcast_in_dim | solution.py:501
  180.4 0.6 fusion.7
  (108 shorter events, 3.0 us)
Async XLA Ops:
  0.6 170.4 %copy-start = (bf16[8,4,128]{2,1,0:T(4,128)(2,1)S(1)}, bf16[8,4,128]{2,1,0:T(4,128)(2,1)}, u32[]{:S(2)}) copy-start(bf16[8,4,128]{2,1,0:T(4,128)(2,1)} %param.17) | copy-start | bytes 24580
  0.6 59.0 %copy-start.33 = (f32[64]{0:T(128)S(1)}, f32[64]{0:T(128)}, u32[]{:S(2)}) copy-start(f32[64]{0:T(128)} %constant.90.clone) | copy-start | bytes 772
  0.7 52.9 %copy-start.32 = (s32[8]{0:T(128)S(1)}, s32[8]{0:T(128)}, u32[]{:S(2)}) copy-start(s32[8]{0:T(128)} %owner_ref.3) | copy-start | bytes 100
  0.7 56.2 %copy-start.31 = (s32[2]{0:T(128)S(1)}, s32[2]{0:T(128)}, u32[]{:S(2)}) copy-start(s32[2]{0:T(128)} %lengths_ref.3) | copy-start | bytes 28
  0.7 48.0 %collective-permute-start = (bf16[320,8192]{1,0:T(8,128)(2,1)}, bf16[320,8192]{1,0:T(8,128)(2,1)}, u32[]{:S(2)}, u32[]{:S(2)}) collective-permute-start(bf16[320,8192]{1,0:T(8,128)(2,1)} %bitcast.55), channel_id=1, source_target_pairs={{0,1},{1,0},{2,3},{3,2},{4,5},{5,4},{6,7},{7,6},{8,9},{9,8},{10,11... | collective-permute-start | bytes 15728648 | tf_op jit(solution)/shard_map/ppermute | solution.py:64
  1.2 15.3 %collective-permute-start.2 = (bf16[512,512]{1,0:T(8,128)(2,1)}, bf16[512,512]{1,0:T(8,128)(2,1)S(1)}, u32[]{:S(2)}, u32[]{:S(2)}) collective-permute-start(bf16[512,512]{1,0:T(8,128)(2,1)} %refs_1_.4), channel_id=1, source_target_pairs={{0,2},{1,3},{2,0},{3,1},{4,6},{5,7},{6,4},{7,5},{8,10},{9,11},{10,... | collective-permute-start | bytes 1572872 | tf_op jit(solution)/shard_map/ppermute | solution.py:64
  3.8 14.5 %collective-permute-start.9 = (bf16[512,512]{1,0:T(8,128)(2,1)}, bf16[512,512]{1,0:T(8,128)(2,1)S(1)}, u32[]{:S(2)}, u32[]{:S(2)}) collective-permute-start(bf16[512,512]{1,0:T(8,128)(2,1)} %refs_1_.4), channel_id=1, source_target_pairs={{0,4},{1,5},{2,6},{3,7},{4,0},{5,1},{6,2},{7,3},{8,12},{9,13},{10,... | collective-permute-start | bytes 1572872 | tf_op jit(solution)/shard_map/ppermute | solution.py:64
  16.5 72.9 %copy-start.5 = (bf16[512,512]{1,0:T(8,128)(2,1)}, bf16[512,512]{1,0:T(8,128)(2,1)S(1)}, u32[]{:S(2)}) copy-start(bf16[512,512]{1,0:T(8,128)(2,1)S(1)} %collective-permute-done.2.refs_2_.refs_3_) | copy-start | bytes 1572868
  16.5 31.6 %collective-permute-start.3 = (bf16[512,512]{1,0:T(8,128)(2,1)}, bf16[512,512]{1,0:T(8,128)(2,1)S(1)}, u32[]{:S(2)}, u32[]{:S(2)}) collective-permute-start(bf16[512,512]{1,0:T(8,128)(2,1)} %refs_1_.5), channel_id=1, source_target_pairs={{0,2},{1,3},{2,0},{3,1},{4,6},{5,7},{6,4},{7,5},{8,10},{9,11},{10,... | collective-permute-start | bytes 1572872 | tf_op jit(solution)/shard_map/ppermute | solution.py:64
  18.3 30.4 %copy-start.3 = (bf16[512,512]{1,0:T(8,128)(2,1)}, bf16[512,512]{1,0:T(8,128)(2,1)S(1)}, u32[]{:S(2)}) copy-start(bf16[512,512]{1,0:T(8,128)(2,1)S(1)} %collective-permute-done.9.refs_0_.refs_4_.refs_5_) | copy-start | bytes 1572868
  18.3 30.4 %collective-permute-start.10 = (bf16[512,512]{1,0:T(8,128)(2,1)}, bf16[512,512]{1,0:T(8,128)(2,1)S(1)}, u32[]{:S(2)}, u32[]{:S(2)}) collective-permute-start(bf16[512,512]{1,0:T(8,128)(2,1)} %refs_1_.5), channel_id=1, source_target_pairs={{0,4},{1,5},{2,6},{3,7},{4,0},{5,1},{6,2},{7,3},{8,12},{9,13},{10,... | collective-permute-start | bytes 1572872 | tf_op jit(solution)/shard_map/ppermute | solution.py:64
  22.9 18.2 %collective-permute-start.5 = (bf16[256,512]{1,0:T(8,128)(2,1)}, bf16[256,512]{1,0:T(8,128)(2,1)S(1)}, u32[]{:S(2)}, u32[]{:S(2)}) collective-permute-start(bf16[256,512]{1,0:T(8,128)(2,1)} %get-tuple-element.36), channel_id=1, source_target_pairs={{0,12},{1,13},{2,14},{3,15},{4,8},{5,9},{6,10},{7,11},{8,4},{9,5},... | collective-permute-start | bytes 786440 | tf_op jit(solution)/shard_map/ppermute | solution.py:64
  25.4 22.7 %collective-permute-start.1 = (bf16[256,512]{1,0:T(8,128)(2,1)}, bf16[256,512]{1,0:T(8,128)(2,1)S(1)}, u32[]{:S(2)}, u32[]{:S(2)}) collective-permute-start(bf16[256,512]{1,0:T(8,128)(2,1)} %get-tuple-element.36), channel_id=1, source_target_pairs={{0,8},{1,9},{2,10},{3,11},{4,12},{5,13},{6,14},{7,15},{8,0},{9,1},... | collective-permute-start | bytes 786440 | tf_op jit(solution)/shard_map/ppermute | solution.py:64
  41.1 48.4 %copy-start.14 = (bf16[256,512]{1,0:T(8,128)(2,1)}, bf16[256,512]{1,0:T(8,128)(2,1)S(1)}, u32[]{:S(2)}) copy-start(bf16[256,512]{1,0:T(8,128)(2,1)S(1)} %collective-permute-done.5.refs_2_) | copy-start | bytes 786436
  41.1 17.9 %collective-permute-start.6 = (bf16[256,512]{1,0:T(8,128)(2,1)S(1)}, bf16[256,512]{1,0:T(8,128)(2,1)S(1)}, u32[]{:S(2)}, u32[]{:S(2)}) collective-permute-start(bf16[256,512]{1,0:T(8,128)(2,1)S(1)} %collective-permute-done.5.refs_2_), channel_id=1, source_target_pairs={{0,16},{1,17},{2,18},{3,19},{4,20},{5,21},{6,22},{7,23},{8,24},{9,... | collective-permute-start | bytes 786440 | tf_op jit(solution)/shard_map/ppermute | solution.py:64
  48.1 41.3 %copy-start.15 = (bf16[256,512]{1,0:T(8,128)(2,1)}, bf16[256,512]{1,0:T(8,128)(2,1)S(1)}, u32[]{:S(2)}) copy-start(bf16[256,512]{1,0:T(8,128)(2,1)S(1)} %collective-permute-done.1.refs_0_) | copy-start | bytes 786436
  48.1 41.3 %copy-start.4 = (bf16[512,512]{1,0:T(8,128)(2,1)}, bf16[512,512]{1,0:T(8,128)(2,1)S(1)}, u32[]{:S(2)}) copy-start(bf16[512,512]{1,0:T(8,128)(2,1)S(1)} %collective-permute-done.3.refs_2_.refs_3_) | copy-start | bytes 1572868
  48.2 10.8 %collective-permute-start.4 = (bf16[256,512]{1,0:T(8,128)(2,1)S(1)}, bf16[256,512]{1,0:T(8,128)(2,1)S(1)}, u32[]{:S(2)}, u32[]{:S(2)}) collective-permute-start(bf16[256,512]{1,0:T(8,128)(2,1)S(1)} %collective-permute-done.1.refs_0_), channel_id=1, source_target_pairs={{0,2},{1,3},{2,0},{3,1},{4,6},{5,7},{6,4},{7,5},{8,10},{9,11},{10,... | collective-permute-start | bytes 786440 | tf_op jit(solution)/shard_map/ppermute | solution.py:64
  48.7 0.8 copy-start.2
  52.1 25.8 %collective-permute-start.11 = (bf16[256,1024]{1,0:T(8,128)(2,1)}, bf16[256,1024]{1,0:T(8,128)(2,1)S(1)}, u32[]{:S(2)}, u32[]{:S(2)}) collective-permute-start(bf16[256,1024]{1,0:T(8,128)(2,1)} %sent_halves.3), channel_id=1, source_target_pairs={{0,2},{1,3},{2,0},{3,1},{4,6},{5,7},{6,4},{7,5},{8,10},{9,11},{10,... | collective-permute-start | bytes 1572872 | tf_op jit(solution)/shard_map/ppermute | solution.py:64
  57.5 18.4 %collective-permute-start.18 = (bf16[256,512]{1,0:T(8,128)(2,1)}, bf16[256,512]{1,0:T(8,128)(2,1)S(1)}, u32[]{:S(2)}, u32[]{:S(2)}) collective-permute-start(bf16[256,512]{1,0:T(8,128)(2,1)} %get-tuple-element.57), channel_id=1, source_target_pairs={{0,8},{1,9},{2,10},{3,11},{4,12},{5,13},{6,14},{7,15},{8,0},{9,1},... | collective-permute-start | bytes 786440 | tf_op jit(solution)/shard_map/ppermute | solution.py:64
  57.5 20.4 %collective-permute-start.13 = (bf16[256,512]{1,0:T(8,128)(2,1)S(1)}, bf16[256,512]{1,0:T(8,128)(2,1)}, u32[]{:S(2)}, u32[]{:S(2)}) collective-permute-start(bf16[256,512]{1,0:T(8,128)(2,1)S(1)} %collective-permute-done.1.refs_0_), channel_id=1, source_target_pairs={{0,16},{1,17},{2,18},{3,19},{4,20},{5,21},{6,22},{7,23},{8,24},{9,... | collective-permute-start | bytes 786440 | tf_op jit(solution)/shard_map/ppermute | solution.py:64
  59.0 30.5 %copy-start.16 = (bf16[256,512]{1,0:T(8,128)(2,1)}, bf16[256,512]{1,0:T(8,128)(2,1)S(1)}, u32[]{:S(2)}) copy-start(bf16[256,512]{1,0:T(8,128)(2,1)S(1)} %collective-permute-done.6.refs_3_) | copy-start | bytes 786436
  59.0 30.5 %copy-start.17 = (bf16[256,512]{1,0:T(8,128)(2,1)}, bf16[256,512]{1,0:T(8,128)(2,1)S(1)}, u32[]{:S(2)}) copy-start(bf16[256,512]{1,0:T(8,128)(2,1)S(1)} %collective-permute-done.4.refs_4_) | copy-start | bytes 786436
  59.0 17.4 %collective-permute-start.7 = (bf16[256,512]{1,0:T(8,128)(2,1)S(1)}, bf16[256,512]{1,0:T(8,128)(2,1)S(1)}, u32[]{:S(2)}, u32[]{:S(2)}) collective-permute-start(bf16[256,512]{1,0:T(8,128)(2,1)S(1)} %collective-permute-done.4.refs_4_), channel_id=1, source_target_pairs={{0,16},{1,17},{2,18},{3,19},{4,20},{5,21},{6,22},{7,23},{8,24},{9,... | collective-permute-start | bytes 786440 | tf_op jit(solution)/shard_map/ppermute | solution.py:64
  60.0 50.9 %collective-permute-start.23 = (bf16[256,512]{1,0:T(8,128)(2,1)}, bf16[256,512]{1,0:T(8,128)(2,1)S(1)}, u32[]{:S(2)}, u32[]{:S(2)}) collective-permute-start(bf16[256,512]{1,0:T(8,128)(2,1)} %get-tuple-element.57), channel_id=1, source_target_pairs={{0,12},{1,13},{2,14},{3,15},{4,8},{5,9},{6,10},{7,11},{8,4},{9,5},... | collective-permute-start | bytes 786440 | tf_op jit(solution)/shard_map/ppermute | solution.py:64
  75.9 13.6 %copy-start.13 = (bf16[256,512]{1,0:T(8,128)(2,1)}, bf16[256,512]{1,0:T(8,128)(2,1)S(1)}, u32[]{:S(2)}) copy-start(bf16[256,512]{1,0:T(8,128)(2,1)S(1)} %collective-permute-done.18.refs_0_) | copy-start | bytes 786436
  75.9 41.7 %collective-permute-start.19 = (bf16[256,512]{1,0:T(8,128)(2,1)S(1)}, bf16[256,512]{1,0:T(8,128)(2,1)S(1)}, u32[]{:S(2)}, u32[]{:S(2)}) collective-permute-start(bf16[256,512]{1,0:T(8,128)(2,1)S(1)} %collective-permute-done.18.refs_0_), channel_id=1, source_target_pairs={{0,2},{1,3},{2,0},{3,1},{4,6},{5,7},{6,4},{7,5},{8,10},{9,11},{10,... | collective-permute-start | bytes 786440 | tf_op jit(solution)/shard_map/ppermute | solution.py:64
  76.4 34.4 %copy-start.12 = (bf16[256,512]{1,0:T(8,128)(2,1)}, bf16[256,512]{1,0:T(8,128)(2,1)S(1)}, u32[]{:S(2)}) copy-start(bf16[256,512]{1,0:T(8,128)(2,1)S(1)} %collective-permute-done.7.refs_2_) | copy-start | bytes 786436
  76.4 42.6 %collective-permute-start.20 = (bf16[256,512]{1,0:T(8,128)(2,1)S(1)}, bf16[256,512]{1,0:T(8,128)(2,1)S(1)}, u32[]{:S(2)}, u32[]{:S(2)}) collective-permute-start(bf16[256,512]{1,0:T(8,128)(2,1)S(1)} %collective-permute-done.18.refs_0_), channel_id=1, source_target_pairs={{0,16},{1,17},{2,18},{3,19},{4,20},{5,21},{6,22},{7,23},{8,24},{9,... | collective-permute-start | bytes 786440 | tf_op jit(solution)/shard_map/ppermute | solution.py:64
  77.9 11.6 %copy-start.6 = (bf16[256,1024]{1,0:T(8,128)(2,1)}, bf16[256,1024]{1,0:T(8,128)(2,1)S(1)}, u32[]{:S(2)}) copy-start(bf16[256,1024]{1,0:T(8,128)(2,1)S(1)} %collective-permute-done.11.refs_6_) | copy-start | bytes 1572868
  77.9 17.2 %collective-permute-start.14 = (bf16[256,1024]{1,0:T(8,128)(2,1)S(1)}, bf16[256,1024]{1,0:T(8,128)(2,1)S(1)}, u32[]{:S(2)}, u32[]{:S(2)}) collective-permute-start(bf16[256,1024]{1,0:T(8,128)(2,1)S(1)} %collective-permute-done.11.refs_6_), channel_id=1, source_target_pairs={{0,16},{1,17},{2,18},{3,19},{4,20},{5,21},{6,22},{7,23},{8,24},{9,... | collective-permute-start | bytes 1572872 | tf_op jit(solution)/shard_map/ppermute | solution.py:64
  78.5 22.4 %collective-permute-start.12 = (bf16[256,512]{1,0:T(8,128)(2,1)S(1)}, bf16[256,512]{1,0:T(8,128)(2,1)S(1)}, u32[]{:S(2)}, u32[]{:S(2)}) collective-permute-start(bf16[256,512]{1,0:T(8,128)(2,1)S(1)} %collective-permute-done.5.refs_2_), channel_id=1, source_target_pairs={{0,2},{1,3},{2,0},{3,1},{4,6},{5,7},{6,4},{7,5},{8,10},{9,11},{10,... | collective-permute-start | bytes 786440 | tf_op jit(solution)/shard_map/ppermute | solution.py:64
  95.2 0.8 copy-start.7
  107.0 24.7 %collective-permute-start.17 = (f32[320,512]{1,0:T(8,128)}, f32[320,512]{1,0:T(8,128)S(1)}, u32[]{:S(2)}, u32[]{:S(2)}) collective-permute-start(f32[320,512]{1,0:T(8,128)} %get-tuple-element.50), channel_id=1, source_target_pairs={{0,1},{1,0},{2,3},{3,2},{4,5},{5,4},{6,7},{7,6},{8,9},{9,8},{10,11... | collective-permute-start | bytes 1966088 | tf_op jit(solution)/shard_map/ppermute | solution.py:64
  107.1 8.9 %collective-permute-start.15 = (bf16[256,512]{1,0:T(8,128)(2,1)}, bf16[256,512]{1,0:T(8,128)(2,1)S(1)}, u32[]{:S(2)}, u32[]{:S(2)}) collective-permute-start(bf16[256,512]{1,0:T(8,128)(2,1)} %copy-done.27), channel_id=1, source_target_pairs={{0,16},{1,17},{2,18},{3,19},{4,20},{5,21},{6,22},{7,23},{8,24},{9,... | collective-permute-start | bytes 786440 | tf_op jit(solution)/shard_map/ppermute | solution.py:64
  110.8 14.1 %copy-start.18 = (bf16[256,512]{1,0:T(8,128)(2,1)}, bf16[256,512]{1,0:T(8,128)(2,1)S(1)}, u32[]{:S(2)}) copy-start(bf16[256,512]{1,0:T(8,128)(2,1)S(1)} %collective-permute-done.23.refs_2_) | copy-start | bytes 786436
  110.9 20.9 %collective-permute-start.8 = (bf16[256,512]{1,0:T(8,128)(2,1)S(1)}, bf16[256,512]{1,0:T(8,128)(2,1)S(1)}, u32[]{:S(2)}, u32[]{:S(2)}) collective-permute-start(bf16[256,512]{1,0:T(8,128)(2,1)S(1)} %collective-permute-done.7.refs_2_), channel_id=1, source_target_pairs={{0,1},{1,0},{2,3},{3,2},{4,5},{5,4},{6,7},{7,6},{8,9},{9,8},{10,11... | collective-permute-start | bytes 786440 | tf_op jit(solution)/shard_map/ppermute | solution.py:64
  116.1 8.9 %copy-start.22 = (bf16[256,512]{1,0:T(8,128)(2,1)}, bf16[256,512]{1,0:T(8,128)(2,1)S(1)}, u32[]{:S(2)}) copy-start(bf16[256,512]{1,0:T(8,128)(2,1)S(1)} %collective-permute-done.15.refs_4_) | copy-start | bytes 786436
  116.1 8.9 %collective-permute-start.24 = (bf16[256,512]{1,0:T(8,128)(2,1)S(1)}, bf16[256,512]{1,0:T(8,128)(2,1)S(1)}, u32[]{:S(2)}, u32[]{:S(2)}) collective-permute-start(bf16[256,512]{1,0:T(8,128)(2,1)S(1)} %collective-permute-done.23.refs_2_), channel_id=1, source_target_pairs={{0,2},{1,3},{2,0},{3,1},{4,6},{5,7},{6,4},{7,5},{8,10},{9,11},{10,... | collective-permute-start | bytes 786440 | tf_op jit(solution)/shard_map/ppermute | solution.py:64
  117.6 7.4 %copy-start.10 = (bf16[256,512]{1,0:T(8,128)(2,1)}, bf16[256,512]{1,0:T(8,128)(2,1)S(1)}, u32[]{:S(2)}) copy-start(bf16[256,512]{1,0:T(8,128)(2,1)S(1)} %collective-permute-done.19.refs_4_) | copy-start | bytes 786436
  117.6 7.6 %collective-permute-start.25 = (bf16[256,512]{1,0:T(8,128)(2,1)S(1)}, bf16[256,512]{1,0:T(8,128)(2,1)S(1)}, u32[]{:S(2)}, u32[]{:S(2)}) collective-permute-start(bf16[256,512]{1,0:T(8,128)(2,1)S(1)} %collective-permute-done.23.refs_2_), channel_id=1, source_target_pairs={{0,16},{1,17},{2,18},{3,19},{4,20},{5,21},{6,22},{7,23},{8,24},{9,... | collective-permute-start | bytes 786440 | tf_op jit(solution)/shard_map/ppermute | solution.py:64
  119.1 5.9 %copy-start.19 = (bf16[256,512]{1,0:T(8,128)(2,1)}, bf16[256,512]{1,0:T(8,128)(2,1)S(1)}, u32[]{:S(2)}) copy-start(bf16[256,512]{1,0:T(8,128)(2,1)S(1)} %collective-permute-done.20.refs_1_) | copy-start | bytes 786436
  119.1 12.7 %collective-permute-start.16 = (bf16[256,512]{1,0:T(8,128)(2,1)S(1)}, bf16[256,512]{1,0:T(8,128)(2,1)S(1)}, u32[]{:S(2)}, u32[]{:S(2)}) collective-permute-start(bf16[256,512]{1,0:T(8,128)(2,1)S(1)} %collective-permute-done.15.refs_4_), channel_id=1, source_target_pairs={{0,1},{1,0},{2,3},{3,2},{4,5},{5,4},{6,7},{7,6},{8,9},{9,8},{10,11... | collective-permute-start | bytes 786440 | tf_op jit(solution)/shard_map/ppermute | solution.py:64
  131.3 23.8 %collective-permute-start.28 = (f32[320,512]{1,0:T(8,128)}, f32[320,512]{1,0:T(8,128)S(1)}, u32[]{:S(2)}, u32[]{:S(2)}) collective-permute-start(f32[320,512]{1,0:T(8,128)} %get-tuple-element.65), channel_id=1, source_target_pairs={{0,1},{1,0},{2,3},{3,2},{4,5},{5,4},{6,7},{7,6},{8,9},{9,8},{10,11... | collective-permute-start | bytes 1966088 | tf_op jit(solution)/shard_map/ppermute | solution.py:64
  131.8 0.9 copy-start.26
  131.8 1.0 copy-start.8
  132.8 7.9 %copy-start.21 = (bf16[256,512]{1,0:T(8,128)(2,1)S(1)}, bf16[256,512]{1,0:T(8,128)(2,1)}, u32[]{:S(2)}) copy-start(bf16[256,512]{1,0:T(8,128)(2,1)} %copy-done.20) | copy-start | bytes 786436
  132.8 9.1 %copy-start.11 = (bf16[256,512]{1,0:T(8,128)(2,1)S(1)}, bf16[256,512]{1,0:T(8,128)(2,1)}, u32[]{:S(2)}) copy-start(bf16[256,512]{1,0:T(8,128)(2,1)} %copy-done.10) | copy-start | bytes 786436
  137.1 19.3 %all-to-all-start = ((bf16[16,80,128]{2,1,0:T(8,128)(2,1)}), bf16[16,80,128]{2,1,0:T(8,128)(2,1)S(1)}, u32[]{:S(2)}, u32[]{:S(2)}) async-start(bf16[16,80,128]{2,1,0:T(8,128)(2,1)} %cache_rows.2), calls=%async_computation | async-start | bytes 655360 | tf_op jit(solution)/shard_map/all_to_all | solution.py:433
  140.7 9.2 %collective-permute-start.26 = (bf16[256,512]{1,0:T(8,128)(2,1)S(1)}, bf16[256,512]{1,0:T(8,128)(2,1)S(1)}, u32[]{:S(2)}, u32[]{:S(2)}) collective-permute-start(bf16[256,512]{1,0:T(8,128)(2,1)S(1)} %copy-done.21), channel_id=1, source_target_pairs={{0,16},{1,17},{2,18},{3,19},{4,20},{5,21},{6,22},{7,23},{8,24},{9,... | collective-permute-start | bytes 786440 | tf_op jit(solution)/shard_map/ppermute | solution.py:64
  141.9 12.9 %collective-permute-start.21 = (bf16[256,512]{1,0:T(8,128)(2,1)S(1)}, bf16[256,512]{1,0:T(8,128)(2,1)S(1)}, u32[]{:S(2)}, u32[]{:S(2)}) collective-permute-start(bf16[256,512]{1,0:T(8,128)(2,1)S(1)} %copy-done.11), channel_id=1, source_target_pairs={{0,16},{1,17},{2,18},{3,19},{4,20},{5,21},{6,22},{7,23},{8,24},{9,... | collective-permute-start | bytes 786440 | tf_op jit(solution)/shard_map/ppermute | solution.py:64
  149.9 6.5 %copy-start.24 = (bf16[256,512]{1,0:T(8,128)(2,1)}, bf16[256,512]{1,0:T(8,128)(2,1)S(1)}, u32[]{:S(2)}) copy-start(bf16[256,512]{1,0:T(8,128)(2,1)S(1)} %collective-permute-done.26.refs_4_) | copy-start | bytes 786436
  149.9 5.3 %collective-permute-start.27 = (bf16[256,512]{1,0:T(8,128)(2,1)S(1)}, bf16[256,512]{1,0:T(8,128)(2,1)S(1)}, u32[]{:S(2)}, u32[]{:S(2)}) collective-permute-start(bf16[256,512]{1,0:T(8,128)(2,1)S(1)} %collective-permute-done.26.refs_4_), channel_id=1, source_target_pairs={{0,1},{1,0},{2,3},{3,2},{4,5},{5,4},{6,7},{7,6},{8,9},{9,8},{10,11... | collective-permute-start | bytes 786440 | tf_op jit(solution)/shard_map/ppermute | solution.py:64
  154.8 1.6 copy-start.25
  154.8 1.5 collective-permute-start.22
  155.1 1.3 copy-start.9
  155.1 1.3 copy-start.28
  156.4 0.8 copy-start.30
  156.4 0.8 copy-start.1
  161.1 17.0 %all-to-all-start.1 = ((bf16[16,80,128]{2,1,0:T(8,128)(2,1)}), bf16[16,80,128]{2,1,0:T(8,128)(2,1)S(1)}, u32[]{:S(2)}, u32[]{:S(2)}) async-start(bf16[16,80,128]{2,1,0:T(8,128)(2,1)} %cache_rows.3), calls=%async_computation.1 | async-start | bytes 655360 | tf_op jit(solution)/shard_map/all_to_all | solution.py:433
  168.3 1.3 collective-permute-start.29
  169.8 1.2 collective-permute-start.30
  178.3 2.1 %collective-permute-start.31 = (f32[4,1024]{1,0:T(4,128)S(1)}, f32[4,1024]{1,0:T(4,128)S(1)}, u32[]{:S(2)}, u32[]{:S(2)}) collective-permute-start(f32[4,1024]{1,0:T(4,128)S(1)} %bitcast.53), channel_id=1, source_target_pairs={{0,1},{1,0},{2,3},{3,2},{4,5},{5,4},{6,7},{7,6},{8,9},{9,8},{10,11... | collective-permute-start | bytes 49160 | tf_op jit(solution)/shard_map/ppermute | solution.py:27
  (4 other events, 2.9 us)

commit v8 on v7

--- a/solution.py
+++ b/solution.py
@@ -59,8 +59,10 @@
     route = []
     for g in range(groups):
         for s in range(seq):
-            tg, tz, ty, tc = rule(g, s // 2 // low, s // 2 % low, s % 2)
-            route.append((g * seq + s, tg * seq + (tz * low + ty) * 2 + tc))
+            place = rule(g, s // 2 // low, s // 2 % low, s % 2)
+            if place is not None:
+                tg, tz, ty, tc = place
+                route.append((g * seq + s, tg * seq + (tz * low + ty) * 2 + tc))
     return lax.ppermute(block, ("groups", "seq"), route)
 
 
@@ -76,8 +78,16 @@
     return (1 - g, z, y, c)
 
 
-def along(bits):
-    return lambda g, z, y, c: (g, z ^ bits, y, c)
+def to_pair(g, z, y, c):
+    return (g, z ^ 1, y, c)
+
+
+def to_middle(g, z, y, c):
+    return (g, 3 - z, y, c) if z in (1, 2) else None
+
+
+def to_end(g, z, y, c):
+    return (g, 0 if z == 1 else 3, y, c) if z in (1, 2) else None
 
 
 VMEM_REF = pl.BlockSpec(memory_space=pltpu.VMEM)
@@ -90,38 +100,33 @@
     return pl.CostEstimate(flops=flops, bytes_accessed=moved_bytes, transcendentals=0)
 
 
-def halves_kernel(together, place, *refs):
-    count = len(refs) // 2
-    if together:
-        columns = refs[0].shape[1]
-        for k in range(len(refs) - 1):
-            refs[-1][:, k * columns : (k + 1) * columns] = refs[k][...]
-    else:
-        for source, target in zip(refs[:count], refs[count:]):
-            target[...] = source[...]
-
-
-def sent_halves(place, blocks, together):
-    rows, columns = blocks[0].shape
-    depth, count = rows // 2, len(blocks)
-    kind = blocks[0].dtype
-    if together:
-        outs = [jax.ShapeDtypeStruct((depth, count * columns), kind)]
-    else:
-        outs = [jax.ShapeDtypeStruct((depth, columns), kind)] * count
+def halves_kernel(place, key_sent, value_sent, key_rest, value_rest, sent, rest):
+    columns = key_sent.shape[1]
+    sent[:, :columns] = key_sent[...]
+    sent[:, columns:] = value_sent[...]
+    rest[:, :columns] = key_rest[...]
+    rest[:, columns:] = value_rest[...]
+
+
+def weight_halves(place, key_weight, value_weight):
+    rows, columns = key_weight.shape
+    depth = rows // 2
+    out = jax.ShapeDtypeStruct((depth, 2 * columns), key_weight.dtype)
+    sent = pl.BlockSpec((depth, columns), lambda i, place: (place[0], 0))
+    rest = pl.BlockSpec((depth, columns), lambda i, place: (1 - place[0], 0))
     return pl.pallas_call(
-        functools.partial(halves_kernel, together),
+        halves_kernel,
         grid_spec=pltpu.PrefetchScalarGridSpec(
             num_scalar_prefetch=1,
             grid=(1,),
-            in_specs=[pl.BlockSpec((depth, columns), lambda i, place: (place[0], 0))] * count,
-            out_specs=[pl.BlockSpec(out.shape, lambda i, place: (0, 0)) for out in outs],
+            in_specs=[sent, sent, rest, rest],
+            out_specs=[pl.BlockSpec(out.shape, lambda i, place: (0, 0))] * 2,
         ),
-        out_shape=outs,
+        out_shape=[out, out],
         compiler_params=PARAMS,
         cost_estimate=cost(1000, 1000),
-        name="sent_halves",
-    )(place, *blocks)
+        name="weight_halves",
+    )(place, key_weight, value_weight, key_weight, value_weight)
 
 
 def prepare_kernel(place, *refs):
@@ -170,7 +175,7 @@
             jax.ShapeDtypeStruct((2 * blocks, rows, depth), jnp.bfloat16),
         ],
         compiler_params=PARAMS,
-        cost_estimate=cost(1 << 36, 1000),
+        cost_estimate=cost(1000, 1000),
         name="normed_halves",
     )(place, mine, other)
 
@@ -190,27 +195,32 @@
     return place[entry] * 2 + half
 
 
-def product_kernel(plan, group, with_total, place, both, *refs):
+def product_kernel(plan, group, parts, with_total, place, both, *refs):
     count = len(plan)
     pieces = refs[:count]
-    totals_in = refs[count : count + 2 * with_total]
-    outs = refs[-7:-5]
+    totals_in = refs[count : count + 2 * with_total * parts]
+    outs = refs[-5 - 2 * parts : -5]
     left, right, total, sems, total_sems = refs[-5:]
     rows, depth = both.shape[2], both.shape[3]
     columns = right.shape[2]
     waits = []
-    for k, (entry, kind, row, column) in enumerate(plan):
+    for k, (entry, kind, column) in enumerate(plan):
         area = pl.ds((k % group) * depth, depth)
         slot = k // group
-        piece = pieces[k].at[pl.ds(row, depth), pl.ds(column, columns)]
+        piece = pieces[k].at[:, pl.ds(column, columns)]
         waits.append(
             [
                 fetch(both.at[half_index(place, entry, kind)], left.at[slot, :, :, area], sems.at[2 * k]),
                 fetch(piece, right.at[slot, area], sems.at[2 * k + 1]),
             ]
         )
+    width = columns // parts
     carried = [
-        fetch(ref, total.at[pl.ds(k * rows, rows)], total_sems.at[k])
+        fetch(
+            ref,
+            total.at[pl.ds(k % 2 * rows, rows), pl.ds(k // 2 * width, width)],
+            total_sems.at[k],
+        )
         for k, ref in enumerate(totals_in)
     ]
     for slot in range(count // group):
@@ -227,25 +237,27 @@
         if slot + 1 < count // group:
             total[...] = value
         else:
-            outs[0][...] = value[:rows]
-            outs[1][...] = value[rows:]
-
-
-def product(place, both, plan, pieces, totals, group, columns):
+            for k, out in enumerate(outs):
+                out[...] = value[
+                    k % 2 * rows : (k % 2 + 1) * rows, k // 2 * width : (k // 2 + 1) * width
+                ]
+
+
+def product(place, both, plan, pieces, totals, group, columns, parts):
     _, _, rows, depth = both.shape
     count = len(plan)
-    out = jax.ShapeDtypeStruct((rows, columns), jnp.float32)
+    out = jax.ShapeDtypeStruct((rows, columns // parts), jnp.float32)
     return pl.pallas_call(
-        functools.partial(product_kernel, plan, group, bool(totals)),
+        functools.partial(product_kernel, plan, group, parts, bool(totals)),
         in_specs=[SMEM_REF] + [ANY_REF] * (1 + count + len(totals)),
-        out_specs=[VMEM_REF] * 2,
-        out_shape=[out] * 2,
+        out_specs=[VMEM_REF] * (2 * parts),
+        out_shape=[out] * (2 * parts),
         scratch_shapes=[
             pltpu.VMEM((count // group, 2, rows, group * depth), both.dtype),
             pltpu.VMEM((count // group, group * depth, columns), both.dtype),
             pltpu.VMEM((2 * rows, columns), jnp.float32),
             pltpu.SemaphoreType.DMA((2 * count,)),
-            pltpu.SemaphoreType.DMA((2,)),
+            pltpu.SemaphoreType.DMA((2 * parts,)),
         ],
         compiler_params=PARAMS,
         cost_estimate=cost(1000, 1000),
@@ -257,7 +269,7 @@
     count = len(plan)
     pieces = refs[: 2 * count]
     total_in, came_in = refs[2 * count : 2 * count + 2]
-    turn = refs[2 * count + 2 : 4 * count]
+    turn = refs[2 * count + 2 : 2 * count + 2 + 2 * rotated]
     out, left, right, total, came, scratch, sems = refs[-7:]
     rows, depth = kept.shape[1], kept.shape[2]
     waits = [fetch(total_in, total, sems.at[0]), fetch(came_in, came, sems.at[1])]
@@ -342,9 +354,11 @@
     if planned:
         core = device_id % 2
         z, y = device_id // 4, device_id // 2 % 2
+        layers = [z, z ^ 1, jnp.where(z < 2, 2, 1), jnp.where(z < 2, 3, 0)]
+        is_end = (z == 0) | (z == 3)
         place = [group_id, core, device_id]
-        place += [(z ^ bits) * 2 + y for bits in range(4)]
-        place += [(z ^ bits) * 2 + 1 - y for bits in range(4)]
+        place += [layer * 2 + y for layer in layers]
+        place += [layer * 2 + 1 - y for layer in layers]
         place = jnp.stack([jnp.asarray(entry, jnp.int32) for entry in place])
     else:
         widened = flat.astype(jnp.float32)
@@ -378,62 +392,77 @@
             jnp.concatenate([cosine, cosine], 1),
             jnp.concatenate([-sine_part, sine_part], 1),
         )
-        weights = (key_weight, value_weight)
         columns = key_weight.shape[1]
-        depth = key_weight.shape[0] // 2
+
+        def parts_of(block):
+            return [block[:, k * columns : (k + 1) * columns] for k in range(2)]
+
+        sent, rest = weight_halves(place, key_weight, value_weight)
+        near = moved(sent, to_pair)
+        middle = moved(sent, to_middle)
+        across = moved(sent, to_row)
         other = moved(flat, to_core)
-        halves = sent_halves(place, weights, False)
-        lanes = {}
-
-        def sent(lane, window, block, rule):
-            held = lanes.setdefault(lane, [])
-            if len(held) >= window:
-                block = after(block, held[-window])
-            held.append(moved(block, rule))
-            return held[-1]
-
-        near, across, far = [], [], []
-        for weight, half in zip(weights, halves):
-            near.append(sent("z", 3, weight, along(1)))
-            across.append(sent("y", 1, weight, to_row))
-            far.append([sent("z", 3, half, along(bits)) for bits in (2, 3)])
-        both, kept = prepared(place, flat, other, seq // 2)
-        (near_half,) = sent_halves(place, [after(block, other) for block in near], True)
-        far_y, far_x, ends = [], [], []
-        far_x.append([sent("x", 2, block, to_group) for block in far[0]])
-        near_y = sent("y", 2, near_half, to_row)
-        far_y.append([sent("y", 2, block, to_row) for block in far[0]])
-        near_xy = sent("x", 2, near_y, to_group)
-        ends.append([sent("x", 2, block, to_group) for block in far_y[0]])
-        far_y.append([sent("y", 2, block, to_row) for block in far[1]])
-        far_x.append([sent("x", 2, block, to_group) for block in far[1]])
-        caches = []
-        token = place
-        for k, turned in enumerate((turn, ())):
-            early = [(HERE, 2 + h, h * depth, 0) for h in range(2)]
-            early += [(THERE, 2 + h, h * depth, 0) for h in range(2)]
-            early += [(HERE + 1, 2 + h, h * depth, 0) for h in range(2)]
-            early += [(THERE + 1, h, 0, k * columns) for h in range(2)]
-            pieces = [weights[k]] * 2 + [across[k]] * 2 + [near[k]] * 2 + [near_y, near_xy]
-            totals = product(place, both, early, pieces, (), 4, columns)
-            late = [(HERE + 2, 0), (HERE + 2, 1), (HERE + 3, 0), (HERE + 3, 1)]
-            late += [(THERE + 2, 0), (THERE + 3, 0)]
-            pieces = [far[k][0], far_x[k][0], far[k][1], far_x[k][1], *far_y[k]]
-            late = [(*entry, 0, 0) for entry in late]
-            total, given = product(place, both, late, pieces, totals, 6, columns)
-            came = moved(given, to_core)
-            if k:
-                ends.append([sent("x", 2, after(block, outgoing), to_group) for block in far_y[1]])
-            pieces = [piece for end in ends[k] for piece in (end, moved(end, to_core))]
-            last = [(THERE + 2, 1), (THERE + 3, 1)]
-            outgoing = outgoing_rows(
-                place, lengths, owner, both, kept, last, pieces, total, came, turned, token
-            )
-            caches.append(
-                lax.all_to_all(outgoing, "seq", split_axis=0, concat_axis=1, tiled=True)[0]
-            )
-            token = caches[0]
-        cache_keys, cache_values = caches
+        came = (near, middle, across, other)
+        end_b = moved(after(middle, *came), to_end)
+        middle_c = moved(after(near, *came), to_middle)
+        near_y = moved(after(near, *came), to_row)
+        across_x = moved(after(across, *came), to_group)
+        both, kept = prepared(place, after(flat, *came), other, seq // 2)
+        came = (end_b, middle_c, near_y, across_x, both)
+        end_c = moved(after(middle_c, *came), to_end)
+        near_xy = moved(after(near_y, *came), to_group)
+        block_b = jnp.where(is_end, after(end_b, *came), middle)
+        block_yb = moved(block_b, to_row)
+        plan = [(HERE, 0, 0), (HERE, 1, 0), (THERE, 0, 0), (THERE, 1, 0)]
+        plan += [(HERE + 1, 0, 0), (THERE + 1, 0, 0)]
+        pieces = [sent, rest, across, across_x, near, near_y]
+        totals = product(place, after(both, *came), plan, pieces, (), 3, 2 * columns, 2)
+        key_b, value_b = parts_of(block_b)
+        came = (end_c, near_xy, block_yb, totals[0], key_b, value_b)
+        near_rest = moved(after(rest, *came), to_pair)
+        key_xb = moved(after(key_b, *came), to_group)
+        key_c, value_c = parts_of(jnp.where(is_end, after(end_c, *came), middle_c))
+        key_yc, value_yc = moved(key_c, to_row), moved(value_c, to_row)
+        key_xc = moved(key_c, to_group)
+        plan = [(THERE + 1, 1, 0), (HERE + 2, 0, 0), (THERE + 2, 0, 0)]
+        pieces = [near_xy, block_b, block_yb]
+        totals = product(place, after(both, *came), plan, pieces, totals, 3, 2 * columns, 2)
+        came = (near_rest, key_xb, key_yc, value_yc, key_xc, totals[0])
+        key_xyc = moved(after(key_yc, *came), to_group)
+        key_yxb = moved(after(key_xb, *came), to_row)
+        value_xb = moved(after(value_b, *came), to_group)
+        plan = [(HERE + 1, 1, 0), (HERE + 2, 1, 0), (HERE + 3, 0, 0), (HERE + 3, 1, 0)]
+        plan += [(THERE + 3, 0, 0)]
+        pieces = [near_rest, key_xb, key_c, key_xc, key_yc]
+        total, given = product(
+            place, after(both, *came), plan, pieces, totals[:2], 5, columns, 1
+        )
+        came = (key_xyc, key_yxb, value_xb, total)
+        value_yxb = moved(after(value_xb, *came), to_row)
+        value_xc = moved(after(value_c, *came), to_group)
+        value_xyc = moved(after(value_yc, *came), to_group)
+        given = moved(after(given, *came), to_core)
+        ends = [after(key_yxb, *came), after(key_xyc, *came)]
+        pieces = [piece for end in ends for piece in (end, moved(end, to_core))]
+        plan = [(THERE + 2, 1), (THERE + 3, 1)]
+        outgoing = outgoing_rows(
+            place, lengths, owner, both, kept, plan, pieces, total, given, turn, place
+        )
+        cache_keys = lax.all_to_all(outgoing, "seq", split_axis=0, concat_axis=1, tiled=True)[0]
+        plan = [(HERE + 1, 1, columns), (HERE + 2, 1, 0), (HERE + 3, 0, 0), (THERE + 3, 0, 0)]
+        pieces = [near_rest, value_xb, value_c, value_yc]
+        total, given = product(
+            place, after(both, outgoing), plan, pieces, totals[2:], 4, columns, 1
+        )
+        given = moved(given, to_core)
+        came = (value_yxb, value_xc, value_xyc, total)
+        ends = [after(end, *came) for end in came[:3]]
+        pieces = [piece for end in ends for piece in (end, moved(end, to_core))]
+        plan = [(THERE + 2, 1), (HERE + 3, 1), (THERE + 3, 1)]
+        outgoing = outgoing_rows(
+            place, lengths, owner, both, kept, plan, pieces, total, given, (), cache_keys
+        )
+        cache_values = lax.all_to_all(outgoing, "seq", split_axis=0, concat_axis=1, tiled=True)[0]
     else:
         shape = (count_requests, count_rows, KEY_VALUE_HEADS, HEAD_SIZE)
         unrotated_key = project(key_weight).reshape(shape)

time: 182 us -> 133 us (0.73)
  waiting for transfers between devices: 77.4 us -> 35.2 us
  starting transfers between devices: 40.9 us -> 37.1 us
  local copies, waits for them, and re-layouts: 5.56 us -> 3.45 us
    ppermute x29, waiting for transfers between devices: 68.9 us -> 23.7 us  [moved(): return lax.ppermute(block, ('groups', 'seq'), route)]
    unnamed x70 -> x66, local copies, waits for them, and re-layouts: 4.98 us -> 1.94 us
    all_to_all x2, waiting for transfers between devices: 6.85 us -> 9.76 us  [body(): lax.all_to_all(outgoing, 'seq', split_axis=0, concat_axis=1, tiled=True)[0]]
    all_to_all x2, starting transfers between devices: 9.4 us -> 7.17 us  [body(): lax.all_to_all(outgoing, 'seq', split_axis=0, concat_axis=1, tiled=True)[0]]
    pallas_call x6 -> x5, Pallas kernels: 25.7 us -> 24.2 us  [the longest x4 21.3 us: product(): pl.pallas_call(functools.partial(product_kernel, plan, group, parts, bool...]
  transfers between devices with their start and end apart: 34 -> 34, of which waited for: 13 -> 13; matrix products, arithmetic and copies ran while one was open for 5% -> 8% of each run, Pallas kernels for 22% -> 29%
where the time goes in v8:
time: 133 us; the launch traced here: 132 us
  Pallas kernels  42.2 us (32%)
  starting transfers between devices  37.1 us (28%)
  waiting for transfers between devices  35.2 us (26%)
  other arithmetic  8.21 us (6%)
  between operations  3.79 us (3%)
  local copies, waits for them, and re-layouts  3.45 us (3%)
  matrix products  1.99 us (1%)
    ppermute x29, starting transfers between devices, moved(): return lax.ppermute(block, ('groups', 'seq'), route)  29.1 us
    ppermute x29, waiting for transfers between devices, moved(): return lax.ppermute(block, ('groups', 'seq'), route)  23.7 us
    pallas_call x4, Pallas kernels, product(): pl.pallas_call(functools.partial(product_kernel, plan, group, parts, bool...  21.3 us
    all_to_all x2, waiting for transfers between devices, body(): lax.all_to_all(outgoing, 'seq', split_axis=0, concat_axis=1, tiled=True)[0]  9.76 us
    pallas_call x1, Pallas kernels, prepared(): pl.pallas_call(prepare_kernel, grid_spec=pltpu.PrefetchScalarGridSpec(num...  9.41 us
    pallas_call x2, Pallas kernels, outgoing_rows(): pl.pallas_call(kernel, in_specs=[SMEM_REF] * 3 + [ANY_REF] * (1 + len(ope...  8.6 us
    all_to_all x2, starting transfers between devices, body(): lax.all_to_all(outgoing, 'seq', split_axis=0, concat_axis=1, tiled=True)[0]  7.17 us
    pallas_call x1, Pallas kernels, weight_halves(): pl.pallas_call(halves_kernel, grid_spec=pltpu.PrefetchScalarGridSpec(num_...  2.87 us
  transfers between devices with their start and end apart: 34, of which 13 were waited for; matrix products, arithmetic and copies ran while one was open for 8% of the time, Pallas kernels for 29%

profile of v8, /device:TPU:0, one launch (start us, length us, event | category | flops | bytes accessed | tf_op | source)
XLA Modules:
  0.0 131.9 jit_solution(15252462727069636508)
XLA Ops:
  0.6 0.5 collective-permute-start.3
  1.2 0.6 stack.47.place.place_ref.token_ref
  1.8 2.9 %weight_halves.1 = (bf16[256,1024]{1,0:T(8,128)(2,1)}, bf16[256,1024]{1,0:T(8,128)(2,1)}) custom-call(s32[11]{0:T(128)} %stack.47.place.place_ref.token_ref, bf16[512,512]{1,0:T(8,128)(2,1)} %key_rest.1, bf16[512,512]{1,0:T(8,128)(2,1)} %value_rest.1, bf16[512,512]{1,0:T(8,128)(2,1)} %key_rest.1, bf16[512,512]{1,0:T(8,128)(2,1)} %value_rest.1), custom_call_target="tpu_custom_call" | custom-call | flops 1000 | bytes 1000 | tf_op jit(solution)/shard_map/weight_halves/pallas_call | solution.py:117
  4.7 2.7 %collective-permute-start = (bf16[256,1024]{1,0:T(8,128)(2,1)}, bf16[256,1024]{1,0:T(8,128)(2,1)S(1)}, u32[]{:S(2)}, u32[]{:S(2)}) collective-permute-start(bf16[256,1024]{1,0:T(8,128)(2,1)} %get-tuple-element.44.refs_0_), channel_id=1, source_target_pairs={{0,4},{1,5},{2,6},{3,7},{4,0},{5,1},{6,2},{7,3},{8,12},{9,13},{10,... | collective-permute-start | bytes 1572872 | tf_op jit(solution)/shard_map/ppermute | solution.py:66
  7.3 0.7 collective-permute-start.1
  8.0 1.6 %collective-permute-start.2 = (bf16[256,1024]{1,0:T(8,128)(2,1)}, bf16[256,1024]{1,0:T(8,128)(2,1)S(1)}, u32[]{:S(2)}, u32[]{:S(2)}) collective-permute-start(bf16[256,1024]{1,0:T(8,128)(2,1)} %get-tuple-element.44.refs_0_), channel_id=1, source_target_pairs={{0,2},{1,3},{2,0},{3,1},{4,6},{5,7},{6,4},{7,5},{8,10},{9,11},{10,... | collective-permute-start | bytes 1572872 | tf_op jit(solution)/shard_map/ppermute | solution.py:66
  9.6 10.5 %collective-permute-done.refs_4_ = bf16[256,1024]{1,0:T(8,128)(2,1)S(1)} collective-permute-done((bf16[256,1024]{1,0:T(8,128)(2,1)}, bf16[256,1024]{1,0:T(8,128)(2,1)S(1)}, u32[]{:S(2)}, u32[]{:S(2)}) %collective-permute-start) | collective-permute-done | bytes 524320 | tf_op jit(solution)/shard_map/ppermute | solution.py:66
  20.1 2.2 %collective-permute-done.2.refs_2_ = bf16[256,1024]{1,0:T(8,128)(2,1)S(1)} collective-permute-done((bf16[256,1024]{1,0:T(8,128)(2,1)}, bf16[256,1024]{1,0:T(8,128)(2,1)S(1)}, u32[]{:S(2)}, u32[]{:S(2)}) %collective-permute-start.2) | collective-permute-done | bytes 524320 | tf_op jit(solution)/shard_map/ppermute | solution.py:66
  22.3 1.5 %collective-permute-start.5 = (bf16[256,1024]{1,0:T(8,128)(2,1)S(1)}, bf16[256,1024]{1,0:T(8,128)(2,1)}, u32[]{:S(2)}, u32[]{:S(2)}) collective-permute-start(bf16[256,1024]{1,0:T(8,128)(2,1)S(1)} %collective-permute-done.refs_4_), channel_id=1, source_target_pairs={{4,8},{5,9},{6,10},{7,11},{8,4},{9,5},{10,6},{11,7},{20,24},{21,25... | collective-permute-start | bytes 1572872 | tf_op jit(solution)/shard_map/ppermute | solution.py:66
  23.8 1.5 %collective-permute-start.6 = (bf16[256,1024]{1,0:T(8,128)(2,1)S(1)}, bf16[256,1024]{1,0:T(8,128)(2,1)S(1)}, u32[]{:S(2)}, u32[]{:S(2)}) collective-permute-start(bf16[256,1024]{1,0:T(8,128)(2,1)S(1)} %collective-permute-done.refs_4_), channel_id=1, source_target_pairs={{0,2},{1,3},{2,0},{3,1},{4,6},{5,7},{6,4},{7,5},{8,10},{9,11},{10,... | collective-permute-start | bytes 1572872 | tf_op jit(solution)/shard_map/ppermute | solution.py:66
  25.3 1.3 collective-permute-start.4
  26.6 1.6 %collective-permute-start.7 = (bf16[256,1024]{1,0:T(8,128)(2,1)S(1)}, bf16[256,1024]{1,0:T(8,128)(2,1)S(1)}, u32[]{:S(2)}, u32[]{:S(2)}) collective-permute-start(bf16[256,1024]{1,0:T(8,128)(2,1)S(1)} %collective-permute-done.2.refs_2_), channel_id=1, source_target_pairs={{0,16},{1,17},{2,18},{3,19},{4,20},{5,21},{6,22},{7,23},{8,24},{9,... | collective-permute-start | bytes 1572872 | tf_op jit(solution)/shard_map/ppermute | solution.py:66
  28.1 9.4 %normed_halves.1 = (bf16[16,2,320,256]{3,2,1,0:T(8,128)(2,1)}, bf16[16,320,256]{2,1,0:T(8,128)(2,1)}) custom-call(s32[11]{0:T(128)} %stack.47.place.place_ref.token_ref, bf16[320,8192]{1,0:T(8,128)(2,1)} %bitcast.51, bf16[320,8192]{1,0:T(8,128)(2,1)} %collective-permute-done.3.refs_1_), custom_call_target="tpu_custom_call" | custom-call | flops 1000 | bytes 1000 | tf_op jit(solution)/shard_map/normed_halves/pallas_call | solution.py:162
  37.6 4.7 %collective-permute-done.4 = bf16[256,1024]{1,0:T(8,128)(2,1)S(1)} collective-permute-done((bf16[256,1024]{1,0:T(8,128)(2,1)S(1)}, bf16[256,1024]{1,0:T(8,128)(2,1)S(1)}, u32[]{:S(2)}, u32[]{:S(2)}) %collective-permute-start.4) | collective-permute-done | bytes 524320 | tf_op jit(solution)/shard_map/ppermute | solution.py:66
  42.3 1.3 collective-permute-start.8
  43.6 1.6 %collective-permute-start.9 = (bf16[256,1024]{1,0:T(8,128)(2,1)S(1)}, bf16[256,1024]{1,0:T(8,128)(2,1)S(1)}, u32[]{:S(2)}, u32[]{:S(2)}) collective-permute-start(bf16[256,1024]{1,0:T(8,128)(2,1)S(1)} %collective-permute-done.6.refs_5_), channel_id=1, source_target_pairs={{0,16},{1,17},{2,18},{3,19},{4,20},{5,21},{6,22},{7,23},{8,24},{9,... | collective-permute-start | bytes 1572872 | tf_op jit(solution)/shard_map/ppermute | solution.py:66
  45.2 0.6 collective-permute-start.10
  45.8 6.1 %add_product.4 = (f32[320,512]{1,0:T(8,128)}, f32[320,512]{1,0:T(8,128)}, f32[320,512]{1,0:T(8,128)}, f32[320,512]{1,0:T(8,128)}) custom-call(s32[11]{0:T(128)} %stack.47.place.place_ref.token_ref, bf16[16,2,320,256]{3,2,1,0:T(8,128)(2,1)} %get-tuple-element.78.both.refs_0_, bf16[256,1024]{1,0:T(8,128)(2,1)} %get-tuple-element.44.refs_0_, ...), custom_call_target="tpu_custom_call" | custom-call | flops 1000 | bytes 1000 | tf_op jit(solution)/shard_map/add_product/pallas_call | solution.py:250
  51.9 0.8 fusion.24
  52.8 3.6 %collective-permute-done.8 = bf16[256,1024]{1,0:T(8,128)(2,1)S(1)} collective-permute-done((bf16[256,1024]{1,0:T(8,128)(2,1)}, bf16[256,1024]{1,0:T(8,128)(2,1)S(1)}, u32[]{:S(2)}, u32[]{:S(2)}) %collective-permute-start.8) | collective-permute-done | bytes 524320 | tf_op jit(solution)/shard_map/ppermute | solution.py:66
  56.4 0.6 collective-permute-done.10.refs_2_
  57.0 1.0 collective-permute-start.11
  58.0 2.0 %collective-permute-start.12 = (bf16[256,1024]{1,0:T(8,128)(2,1)S(1)}, bf16[256,1024]{1,0:T(8,128)(2,1)S(1)}, u32[]{:S(2)}, u32[]{:S(2)}) collective-permute-start(bf16[256,1024]{1,0:T(8,128)(2,1)S(1)} %copy-done.8), channel_id=1, source_target_pairs={{0,4},{1,5},{2,6},{3,7},{4,0},{5,1},{6,2},{7,3},{8,12},{9,13},{10,... | collective-permute-start | bytes 1572872 | tf_op jit(solution)/shard_map/ppermute | solution.py:66
  60.1 0.6 collective-permute-start.13
  60.6 1.5 %collective-permute-start.14 = (bf16[256,512]{1,0:T(8,128)(2,1)S(1)}, bf16[256,512]{1,0:T(8,128)(2,1)S(1)}, u32[]{:S(2)}, u32[]{:S(2)}) collective-permute-start(bf16[256,512]{1,0:T(8,128)(2,1)S(1)} %get-tuple-element.76.refs_2_), channel_id=1, source_target_pairs={{0,2},{1,3},{2,0},{3,1},{4,6},{5,7},{6,4},{7,5},{8,10},{9,11},{10,... | collective-permute-start | bytes 786440 | tf_op jit(solution)/shard_map/ppermute | solution.py:66
  62.2 1.5 %collective-permute-start.15 = (bf16[256,512]{1,0:T(8,128)(2,1)S(1)}, bf16[256,512]{1,0:T(8,128)(2,1)}, u32[]{:S(2)}, u32[]{:S(2)}) collective-permute-start(bf16[256,512]{1,0:T(8,128)(2,1)S(1)} %get-tuple-element.87.refs_2_), channel_id=1, source_target_pairs={{0,16},{1,17},{2,18},{3,19},{4,20},{5,21},{6,22},{7,23},{8,24},{9,... | collective-permute-start | bytes 786440 | tf_op jit(solution)/shard_map/ppermute | solution.py:66
  63.7 0.7 fusion.14
  64.3 0.6 fusion.19
  65.0 5.7 %add_product.5 = (f32[320,512]{1,0:T(8,128)}, f32[320,512]{1,0:T(8,128)}, f32[320,512]{1,0:T(8,128)}, f32[320,512]{1,0:T(8,128)}) custom-call(s32[11]{0:T(128)} %stack.47.place.place_ref.token_ref, bf16[16,2,320,256]{3,2,1,0:T(8,128)(2,1)} %get-tuple-element.78.both.refs_0_, bf16[256,1024]{1,0:T(8,128)(2,1)} %copy-done.10, bf16[256,1024]{1,0:T(8,128)(2,1)} %copy-done.2, ...), custom_call_target="tpu_custom_call" | custom-call | flops 1000 | bytes 1000 | tf_op jit(solution)/shard_map/add_product/pallas_call | solution.py:250
  70.7 0.7 collective-permute-done.14.refs_3_
  71.4 0.6 collective-permute-start.16
  72.0 1.4 %collective-permute-start.17 = (bf16[256,512]{1,0:T(8,128)(2,1)S(1)}, bf16[256,512]{1,0:T(8,128)(2,1)S(1)}, u32[]{:S(2)}, u32[]{:S(2)}) collective-permute-start(bf16[256,512]{1,0:T(8,128)(2,1)S(1)} %collective-permute-done.13.refs_4_), channel_id=1, source_target_pairs={{0,16},{1,17},{2,18},{3,19},{4,20},{5,21},{6,22},{7,23},{8,24},{9,... | collective-permute-start | bytes 786440 | tf_op jit(solution)/shard_map/ppermute | solution.py:66
  73.4 0.6 collective-permute-start.18
  76.6 0.6 fusion.20
  77.2 0.7 convert_bitcast_fusion
  78.0 4.9 %add_product.6 = (f32[320,512]{1,0:T(8,128)}, f32[320,512]{1,0:T(8,128)}) custom-call(s32[11]{0:T(128)} %stack.47.place.place_ref.token_ref, bf16[16,2,320,256]{3,2,1,0:T(8,128)(2,1)} %get-tuple-element.78.both.refs_0_, bf16[256,1024]{1,0:T(8,128)(2,1)} %copy-done.3, bf16[256,512]{1,0:T(8,128)(2,1)} %copy-done.18, bf16[256,512]{1,0:T(8,128)(2,1)} %copy-done.5, ...), custom_call_target="tpu_custom_call" | custom-call | flops 1000 | bytes 1000 | tf_op jit(solution)/shard_map/add_product/pallas_call | solution.py:250
  83.1 0.4 fusion.6
  83.5 0.8 pad_maximum_fusion
  84.2 0.5 collective-permute-start.19
  84.7 0.6 add_convert_fusion.3
  85.5 1.6 %collective-permute-start.22 = (bf16[256,512]{1,0:T(8,128)(2,1)S(1)}, bf16[256,512]{1,0:T(8,128)(2,1)S(1)}, u32[]{:S(2)}, u32[]{:S(2)}) collective-permute-start(bf16[256,512]{1,0:T(8,128)(2,1)S(1)} %collective-permute-done.18.refs_1_), channel_id=1, source_target_pairs={{0,2},{1,3},{2,0},{3,1},{4,6},{5,7},{6,4},{7,5},{8,10},{9,11},{10,... | collective-permute-start | bytes 786440 | tf_op jit(solution)/shard_map/ppermute | solution.py:66
  87.1 1.4 %collective-permute-start.23 = (bf16[256,512]{1,0:T(8,128)(2,1)S(1)}, bf16[256,512]{1,0:T(8,128)(2,1)S(1)}, u32[]{:S(2)}, u32[]{:S(2)}) collective-permute-start(bf16[256,512]{1,0:T(8,128)(2,1)S(1)} %get-tuple-element.76.refs_2_), channel_id=1, source_target_pairs={{0,16},{1,17},{2,18},{3,19},{4,20},{5,21},{6,22},{7,23},{8,24},{9,... | collective-permute-start | bytes 786440 | tf_op jit(solution)/shard_map/ppermute | solution.py:66
  88.6 0.6 collective-permute-start.24
  89.3 0.6 copy-done.27
  90.1 4.3 %cache_rows.2 = bf16[16,80,128]{2,1,0:T(8,128)(2,1)} custom-call(s32[11]{0:T(128)} %stack.47.place.place_ref.token_ref, s32[2]{0:T(128)} %lengths_ref.3, s32[8]{0:T(128)} %owner_ref.3, s32[11]{0:T(128)} %stack.47.place.place_ref.token_ref, bf16[16,2,320,256]{3,2,1,0:T(8,128)(2,1)} %get-tuple-element.78.both.refs_0_, ...), custom_call_target="tpu_custom_call" | custom-call | flops 1000 | bytes 1000 | tf_op jit(solution)/shard_map/cache_rows/pallas_call | solution.py:317
  94.4 3.6 %all-to-all-start = ((bf16[16,80,128]{2,1,0:T(8,128)(2,1)}), bf16[16,80,128]{2,1,0:T(8,128)(2,1)S(1)}, u32[]{:S(2)}, u32[]{:S(2)}) async-start(bf16[16,80,128]{2,1,0:T(8,128)(2,1)} %cache_rows.2), calls=%async_computation | async-start | bytes 655360 | tf_op jit(solution)/shard_map/all_to_all | solution.py:451
  98.0 4.6 %add_product.7 = (f32[320,512]{1,0:T(8,128)}, f32[320,512]{1,0:T(8,128)}) custom-call(s32[11]{0:T(128)} %stack.47.place.place_ref.token_ref, bf16[16,2,320,256]{3,2,1,0:T(8,128)(2,1)} %get-tuple-element.78.both.refs_0_, bf16[256,1024]{1,0:T(8,128)(2,1)} %copy-done.3, bf16[256,512]{1,0:T(8,128)(2,1)} %copy-done.16, bf16[256,512]{1,0:T(8,128)(2,1)} %copy-done.4, ...), custom_call_target="tpu_custom_call" | custom-call | flops 1000 | bytes 1000 | tf_op jit(solution)/shard_map/add_product/pallas_call | solution.py:250
  102.6 0.5 collective-permute-start.28
  103.1 0.7 add_compare_fusion
  104.0 0.4 collective-permute-start.26
  104.8 0.7 collective-permute-done.25.refs_3_
  105.5 0.4 collective-permute-done.26.refs_5_
  105.8 0.4 collective-permute-done.27.refs_7_
  106.2 2.9 %all-to-all-done = bf16[16,80,128]{2,1,0:T(8,128)(2,1)S(1)} async-done(((bf16[16,80,128]{2,1,0:T(8,128)(2,1)}), bf16[16,80,128]{2,1,0:T(8,128)(2,1)S(1)}, u32[]{:S(2)}, u32[]{:S(2)}) %all-to-all-start) | async-done | bytes 327712 | tf_op jit(solution)/shard_map/all_to_all | solution.py:451
  109.2 0.7 copy-done.1
  110.1 4.3 %cache_rows.3 = bf16[16,80,128]{2,1,0:T(8,128)(2,1)} custom-call(s32[11]{0:T(128)} %stack.47.place.place_ref.token_ref, s32[2]{0:T(128)} %lengths_ref.3, s32[8]{0:T(128)} %owner_ref.3, bf16[1280,128]{1,0:T(8,128)(2,1)} %bitcast.47, bf16[16,2,320,256]{3,2,1,0:T(8,128)(2,1)} %get-tuple-element.78.both.refs_0_, ...), custom_call_target="tpu_custom_call" | custom-call | flops 1000 | bytes 1000 | tf_op jit(solution)/shard_map/cache_rows/pallas_call | solution.py:317
  114.4 3.6 %all-to-all-start.1 = ((bf16[16,80,128]{2,1,0:T(8,128)(2,1)}), bf16[16,80,128]{2,1,0:T(8,128)(2,1)S(1)}, u32[]{:S(2)}, u32[]{:S(2)}) async-start(bf16[16,80,128]{2,1,0:T(8,128)(2,1)} %cache_rows.3), calls=%async_computation.1 | async-start | bytes 655360 | tf_op jit(solution)/shard_map/all_to_all | solution.py:465
  118.0 1.3 %fusion.25 = (f32[4,8]{1,0:T(4,128)S(1)}, f32[4,8,1280]{2,1,0:T(8,128)S(1)}) fusion(bf16[1280,128,1]{1,0,2:T(8,128)(2,1)} %bitcast.48, bf16[4,8,64]{2,1,0:T(8,128)(2,1)S(1)} %get-tuple-element.91, bf16[4,8,64]{2,1,0:T(8,128)(2,1)S(1)} %get-tuple-element.90, pred[1280]{0:T(1024)(128)(4,1)S(1)} %add_compare_fusion), kind=kOutput, calls=%fused_computation.58 | convolution fusion | flops 10624992 | bytes 501120 | tf_op jit(solution)/shard_map/sjd,id->sji/dot_general | solution.py:495
  119.3 0.3 collective-permute-start.29
  119.7 0.9 collective-permute-done.29
  121.1 0.9 collective-permute-done.30
  122.2 6.9 %all-to-all-done.1 = bf16[16,80,128]{2,1,0:T(8,128)(2,1)S(1)} async-done(((bf16[16,80,128]{2,1,0:T(8,128)(2,1)}), bf16[16,80,128]{2,1,0:T(8,128)(2,1)S(1)}, u32[]{:S(2)}, u32[]{:S(2)}) %all-to-all-start.1) | async-done | bytes 327712 | tf_op jit(solution)/shard_map/all_to_all | solution.py:465
  129.4 1.9 %maximum_bitcast_fusion = bf16[1,1280,256]{2,1,0:T(8,128)(2,1)} fusion(bf16[1280,128]{1,0:T(8,128)(2,1)S(1)} %bitcast.53, bf16[1280,128]{1,0:T(8,128)(2,1)} %bitcast.49), kind=kLoop, calls=%fused_computation.6 | loop fusion | flops 1310720 | bytes 1310720 | tf_op jit(solution)/shard_map/broadcast_in_dim | solution.py:530
  131.3 0.6 fusion.7
  (107 shorter events, 2.8 us)
Async XLA Ops:
  0.6 121.3 %copy-start = (bf16[8,4,128]{2,1,0:T(4,128)(2,1)S(1)}, bf16[8,4,128]{2,1,0:T(4,128)(2,1)}, u32[]{:S(2)}) copy-start(bf16[8,4,128]{2,1,0:T(4,128)(2,1)} %param.17) | copy-start | bytes 24580
  0.6 21.6 %collective-permute-start.3 = (bf16[320,8192]{1,0:T(8,128)(2,1)}, bf16[320,8192]{1,0:T(8,128)(2,1)}, u32[]{:S(2)}, u32[]{:S(2)}) collective-permute-start(bf16[320,8192]{1,0:T(8,128)(2,1)} %bitcast.50), channel_id=1, source_target_pairs={{0,1},{1,0},{2,3},{3,2},{4,5},{5,4},{6,7},{7,6},{8,9},{9,8},{10,11... | collective-permute-start | bytes 15728648 | tf_op jit(solution)/shard_map/ppermute | solution.py:66
  4.7 15.4 %collective-permute-start = (bf16[256,1024]{1,0:T(8,128)(2,1)}, bf16[256,1024]{1,0:T(8,128)(2,1)S(1)}, u32[]{:S(2)}, u32[]{:S(2)}) collective-permute-start(bf16[256,1024]{1,0:T(8,128)(2,1)} %get-tuple-element.44.refs_0_), channel_id=1, source_target_pairs={{0,4},{1,5},{2,6},{3,7},{4,0},{5,1},{6,2},{7,3},{8,12},{9,13},{10,... | collective-permute-start | bytes 1572872 | tf_op jit(solution)/shard_map/ppermute | solution.py:66
  7.3 12.7 %collective-permute-start.1 = (bf16[256,1024]{1,0:T(8,128)(2,1)}, bf16[256,1024]{1,0:T(8,128)(2,1)S(1)}, u32[]{:S(2)}, u32[]{:S(2)}) collective-permute-start(bf16[256,1024]{1,0:T(8,128)(2,1)} %get-tuple-element.44.refs_0_), channel_id=1, source_target_pairs={{4,8},{5,9},{6,10},{7,11},{8,4},{9,5},{10,6},{11,7},{20,24},{21,25... | collective-permute-start | bytes 1572872 | tf_op jit(solution)/shard_map/ppermute | solution.py:66
  8.0 14.3 %collective-permute-start.2 = (bf16[256,1024]{1,0:T(8,128)(2,1)}, bf16[256,1024]{1,0:T(8,128)(2,1)S(1)}, u32[]{:S(2)}, u32[]{:S(2)}) collective-permute-start(bf16[256,1024]{1,0:T(8,128)(2,1)} %get-tuple-element.44.refs_0_), channel_id=1, source_target_pairs={{0,2},{1,3},{2,0},{3,1},{4,6},{5,7},{6,4},{7,5},{8,10},{9,11},{10,... | collective-permute-start | bytes 1572872 | tf_op jit(solution)/shard_map/ppermute | solution.py:66
  20.0 17.5 %copy-start.9 = (bf16[256,1024]{1,0:T(8,128)(2,1)}, bf16[256,1024]{1,0:T(8,128)(2,1)S(1)}, u32[]{:S(2)}) copy-start(bf16[256,1024]{1,0:T(8,128)(2,1)S(1)} %collective-permute-done.refs_4_) | copy-start | bytes 1572868
  22.3 15.3 %copy-start.11 = (bf16[256,1024]{1,0:T(8,128)(2,1)}, bf16[256,1024]{1,0:T(8,128)(2,1)S(1)}, u32[]{:S(2)}) copy-start(bf16[256,1024]{1,0:T(8,128)(2,1)S(1)} %collective-permute-done.2.refs_2_) | copy-start | bytes 1572868
  22.3 20.0 %collective-permute-start.5 = (bf16[256,1024]{1,0:T(8,128)(2,1)S(1)}, bf16[256,1024]{1,0:T(8,128)(2,1)}, u32[]{:S(2)}, u32[]{:S(2)}) collective-permute-start(bf16[256,1024]{1,0:T(8,128)(2,1)S(1)} %collective-permute-done.refs_4_), channel_id=1, source_target_pairs={{4,8},{5,9},{6,10},{7,11},{8,4},{9,5},{10,6},{11,7},{20,24},{21,25... | collective-permute-start | bytes 1572872 | tf_op jit(solution)/shard_map/ppermute | solution.py:66
  23.8 18.5 %collective-permute-start.6 = (bf16[256,1024]{1,0:T(8,128)(2,1)S(1)}, bf16[256,1024]{1,0:T(8,128)(2,1)S(1)}, u32[]{:S(2)}, u32[]{:S(2)}) collective-permute-start(bf16[256,1024]{1,0:T(8,128)(2,1)S(1)} %collective-permute-done.refs_4_), channel_id=1, source_target_pairs={{0,2},{1,3},{2,0},{3,1},{4,6},{5,7},{6,4},{7,5},{8,10},{9,11},{10,... | collective-permute-start | bytes 1572872 | tf_op jit(solution)/shard_map/ppermute | solution.py:66
  25.3 17.0 %collective-permute-start.4 = (bf16[256,1024]{1,0:T(8,128)(2,1)S(1)}, bf16[256,1024]{1,0:T(8,128)(2,1)S(1)}, u32[]{:S(2)}, u32[]{:S(2)}) collective-permute-start(bf16[256,1024]{1,0:T(8,128)(2,1)S(1)} %collective-permute-done.1), channel_id=1, source_target_pairs={{4,0},{5,1},{6,2},{7,3},{8,12},{9,13},{10,14},{11,15},{20,16},{21,... | collective-permute-start | bytes 1572872 | tf_op jit(solution)/shard_map/ppermute | solution.py:66
  26.6 15.7 %collective-permute-start.7 = (bf16[256,1024]{1,0:T(8,128)(2,1)S(1)}, bf16[256,1024]{1,0:T(8,128)(2,1)S(1)}, u32[]{:S(2)}, u32[]{:S(2)}) collective-permute-start(bf16[256,1024]{1,0:T(8,128)(2,1)S(1)} %collective-permute-done.2.refs_2_), channel_id=1, source_target_pairs={{0,16},{1,17},{2,18},{3,19},{4,20},{5,21},{6,22},{7,23},{8,24},{9,... | collective-permute-start | bytes 1572872 | tf_op jit(solution)/shard_map/ppermute | solution.py:66
  42.3 3.5 %copy-start.13 = (bf16[256,1024]{1,0:T(8,128)(2,1)}, bf16[256,1024]{1,0:T(8,128)(2,1)S(1)}, u32[]{:S(2)}) copy-start(bf16[256,1024]{1,0:T(8,128)(2,1)S(1)} %collective-permute-done.6.refs_5_) | copy-start | bytes 1572868
  42.3 3.5 %copy-start.14 = (bf16[256,1024]{1,0:T(8,128)(2,1)}, bf16[256,1024]{1,0:T(8,128)(2,1)S(1)}, u32[]{:S(2)}) copy-start(bf16[256,1024]{1,0:T(8,128)(2,1)S(1)} %collective-permute-done.7.refs_3_) | copy-start | bytes 1572868
  42.3 14.1 %collective-permute-start.8 = (bf16[256,1024]{1,0:T(8,128)(2,1)}, bf16[256,1024]{1,0:T(8,128)(2,1)S(1)}, u32[]{:S(2)}, u32[]{:S(2)}) collective-permute-start(bf16[256,1024]{1,0:T(8,128)(2,1)} %collective-permute-done.5), channel_id=1, source_target_pairs={{4,0},{5,1},{6,2},{7,3},{8,12},{9,13},{10,14},{11,15},{20,16},{21,... | collective-permute-start | bytes 1572872 | tf_op jit(solution)/shard_map/ppermute | solution.py:66
  43.6 12.8 %collective-permute-start.9 = (bf16[256,1024]{1,0:T(8,128)(2,1)S(1)}, bf16[256,1024]{1,0:T(8,128)(2,1)S(1)}, u32[]{:S(2)}, u32[]{:S(2)}) collective-permute-start(bf16[256,1024]{1,0:T(8,128)(2,1)S(1)} %collective-permute-done.6.refs_5_), channel_id=1, source_target_pairs={{0,16},{1,17},{2,18},{3,19},{4,20},{5,21},{6,22},{7,23},{8,24},{9,... | collective-permute-start | bytes 1572872 | tf_op jit(solution)/shard_map/ppermute | solution.py:66
  45.2 6.7 %copy-start.2 = (bf16[256,1024]{1,0:T(8,128)(2,1)}, bf16[256,1024]{1,0:T(8,128)(2,1)S(1)}, u32[]{:S(2)}) copy-start(bf16[256,1024]{1,0:T(8,128)(2,1)S(1)} %broadcast_select_fusion.1.refs_1_) | copy-start | bytes 1572868
  45.2 11.7 %collective-permute-start.10 = (bf16[256,1024]{1,0:T(8,128)(2,1)S(1)}, bf16[256,1024]{1,0:T(8,128)(2,1)S(1)}, u32[]{:S(2)}, u32[]{:S(2)}) collective-permute-start(bf16[256,1024]{1,0:T(8,128)(2,1)S(1)} %broadcast_select_fusion.1.refs_1_), channel_id=1, source_target_pairs={{0,2},{1,3},{2,0},{3,1},{4,6},{5,7},{6,4},{7,5},{8,10},{9,11},{10,... | collective-permute-start | bytes 1572872 | tf_op jit(solution)/shard_map/ppermute | solution.py:66
  45.8 12.1 %copy-start.8 = (bf16[256,1024]{1,0:T(8,128)(2,1)S(1)}, bf16[256,1024]{1,0:T(8,128)(2,1)}, u32[]{:S(2)}) copy-start(bf16[256,1024]{1,0:T(8,128)(2,1)} %get-tuple-element.58.refs_1_) | copy-start | bytes 1572868
  51.9 12.4 %copy-start.30 = (s32[8]{0:T(128)S(1)}, s32[8]{0:T(128)}, u32[]{:S(2)}) copy-start(s32[8]{0:T(128)} %owner_ref.3) | copy-start | bytes 100
  56.4 8.6 %copy-start.10 = (bf16[256,1024]{1,0:T(8,128)(2,1)}, bf16[256,1024]{1,0:T(8,128)(2,1)S(1)}, u32[]{:S(2)}) copy-start(bf16[256,1024]{1,0:T(8,128)(2,1)S(1)} %collective-permute-done.9.refs_0_) | copy-start | bytes 1572868
  57.0 8.0 %copy-start.12 = (bf16[256,1024]{1,0:T(8,128)(2,1)}, bf16[256,1024]{1,0:T(8,128)(2,1)S(1)}, u32[]{:S(2)}) copy-start(bf16[256,1024]{1,0:T(8,128)(2,1)S(1)} %collective-permute-done.10.refs_2_) | copy-start | bytes 1572868
  57.0 13.7 %collective-permute-start.11 = (bf16[256,512]{1,0:T(8,128)(2,1)}, bf16[256,512]{1,0:T(8,128)(2,1)S(1)}, u32[]{:S(2)}, u32[]{:S(2)}) collective-permute-start(bf16[256,512]{1,0:T(8,128)(2,1)} %get-tuple-element.57), channel_id=1, source_target_pairs={{0,16},{1,17},{2,18},{3,19},{4,20},{5,21},{6,22},{7,23},{8,24},{9,... | collective-permute-start | bytes 786440 | tf_op jit(solution)/shard_map/ppermute | solution.py:66
  58.0 13.4 %collective-permute-start.12 = (bf16[256,1024]{1,0:T(8,128)(2,1)S(1)}, bf16[256,1024]{1,0:T(8,128)(2,1)S(1)}, u32[]{:S(2)}, u32[]{:S(2)}) collective-permute-start(bf16[256,1024]{1,0:T(8,128)(2,1)S(1)} %copy-done.8), channel_id=1, source_target_pairs={{0,4},{1,5},{2,6},{3,7},{4,0},{5,1},{6,2},{7,3},{8,12},{9,13},{10,... | collective-permute-start | bytes 1572872 | tf_op jit(solution)/shard_map/ppermute | solution.py:66
  60.1 10.6 %copy-start.5 = (bf16[256,512]{1,0:T(8,128)(2,1)}, bf16[256,512]{1,0:T(8,128)(2,1)S(1)}, u32[]{:S(2)}) copy-start(bf16[256,512]{1,0:T(8,128)(2,1)S(1)} %get-tuple-element.87.refs_2_) | copy-start | bytes 786436
  60.1 27.0 %copy-start.4 = (bf16[256,512]{1,0:T(8,128)(2,1)}, bf16[256,512]{1,0:T(8,128)(2,1)S(1)}, u32[]{:S(2)}) copy-start(bf16[256,512]{1,0:T(8,128)(2,1)S(1)} %get-tuple-element.76.refs_2_) | copy-start | bytes 786436
  60.1 10.6 %collective-permute-start.13 = (bf16[256,512]{1,0:T(8,128)(2,1)S(1)}, bf16[256,512]{1,0:T(8,128)(2,1)S(1)}, u32[]{:S(2)}, u32[]{:S(2)}) collective-permute-start(bf16[256,512]{1,0:T(8,128)(2,1)S(1)} %get-tuple-element.87.refs_2_), channel_id=1, source_target_pairs={{0,2},{1,3},{2,0},{3,1},{4,6},{5,7},{6,4},{7,5},{8,10},{9,11},{10,... | collective-permute-start | bytes 786440 | tf_op jit(solution)/shard_map/ppermute | solution.py:66
  60.6 10.7 %collective-permute-start.14 = (bf16[256,512]{1,0:T(8,128)(2,1)S(1)}, bf16[256,512]{1,0:T(8,128)(2,1)S(1)}, u32[]{:S(2)}, u32[]{:S(2)}) collective-permute-start(bf16[256,512]{1,0:T(8,128)(2,1)S(1)} %get-tuple-element.76.refs_2_), channel_id=1, source_target_pairs={{0,2},{1,3},{2,0},{3,1},{4,6},{5,7},{6,4},{7,5},{8,10},{9,11},{10,... | collective-permute-start | bytes 786440 | tf_op jit(solution)/shard_map/ppermute | solution.py:66
  62.2 9.2 %collective-permute-start.15 = (bf16[256,512]{1,0:T(8,128)(2,1)S(1)}, bf16[256,512]{1,0:T(8,128)(2,1)}, u32[]{:S(2)}, u32[]{:S(2)}) collective-permute-start(bf16[256,512]{1,0:T(8,128)(2,1)S(1)} %get-tuple-element.87.refs_2_), channel_id=1, source_target_pairs={{0,16},{1,17},{2,18},{3,19},{4,20},{5,21},{6,22},{7,23},{8,24},{9,... | collective-permute-start | bytes 786440 | tf_op jit(solution)/shard_map/ppermute | solution.py:66
  65.0 11.6 %copy-start.29 = (s32[2]{0:T(128)S(1)}, s32[2]{0:T(128)}, u32[]{:S(2)}) copy-start(s32[2]{0:T(128)} %lengths_ref.3) | copy-start | bytes 28
  70.7 7.3 %copy-start.18 = (bf16[256,512]{1,0:T(8,128)(2,1)}, bf16[256,512]{1,0:T(8,128)(2,1)S(1)}, u32[]{:S(2)}) copy-start(bf16[256,512]{1,0:T(8,128)(2,1)S(1)} %collective-permute-done.11.refs_1_) | copy-start | bytes 786436
  70.7 7.2 %copy-start.21 = (bf16[256,512]{1,0:T(8,128)(2,1)}, bf16[256,512]{1,0:T(8,128)(2,1)S(1)}, u32[]{:S(2)}) copy-start(bf16[256,512]{1,0:T(8,128)(2,1)S(1)} %collective-permute-done.13.refs_4_) | copy-start | bytes 786436
  71.4 23.0 %copy-start.15 = (bf16[256,512]{1,0:T(8,128)(2,1)}, bf16[256,512]{1,0:T(8,128)(2,1)S(1)}, u32[]{:S(2)}) copy-start(bf16[256,512]{1,0:T(8,128)(2,1)S(1)} %collective-permute-done.14.refs_3_) | copy-start | bytes 786436
  71.4 6.6 %copy-start.3 = (bf16[256,1024]{1,0:T(8,128)(2,1)}, bf16[256,1024]{1,0:T(8,128)(2,1)S(1)}, u32[]{:S(2)}) copy-start(bf16[256,1024]{1,0:T(8,128)(2,1)S(1)} %collective-permute-done.12.refs_0_) | copy-start | bytes 1572868
  71.4 11.5 %collective-permute-start.16 = (bf16[256,512]{1,0:T(8,128)(2,1)S(1)}, bf16[256,512]{1,0:T(8,128)(2,1)S(1)}, u32[]{:S(2)}, u32[]{:S(2)}) collective-permute-start(bf16[256,512]{1,0:T(8,128)(2,1)S(1)} %collective-permute-done.11.refs_1_), channel_id=1, source_target_pairs={{0,2},{1,3},{2,0},{3,1},{4,6},{5,7},{6,4},{7,5},{8,10},{9,11},{10,... | collective-permute-start | bytes 786440 | tf_op jit(solution)/shard_map/ppermute | solution.py:66
  72.0 11.0 %collective-permute-start.17 = (bf16[256,512]{1,0:T(8,128)(2,1)S(1)}, bf16[256,512]{1,0:T(8,128)(2,1)S(1)}, u32[]{:S(2)}, u32[]{:S(2)}) collective-permute-start(bf16[256,512]{1,0:T(8,128)(2,1)S(1)} %collective-permute-done.13.refs_4_), channel_id=1, source_target_pairs={{0,16},{1,17},{2,18},{3,19},{4,20},{5,21},{6,22},{7,23},{8,24},{9,... | collective-permute-start | bytes 786440 | tf_op jit(solution)/shard_map/ppermute | solution.py:66
  73.4 9.6 %collective-permute-start.18 = (bf16[256,512]{1,0:T(8,128)(2,1)}, bf16[256,512]{1,0:T(8,128)(2,1)S(1)}, u32[]{:S(2)}, u32[]{:S(2)}) collective-permute-start(bf16[256,512]{1,0:T(8,128)(2,1)} %get-tuple-element.67), channel_id=1, source_target_pairs={{0,16},{1,17},{2,18},{3,19},{4,20},{5,21},{6,22},{7,23},{8,24},{9,... | collective-permute-start | bytes 786440 | tf_op jit(solution)/shard_map/ppermute | solution.py:66
  78.0 5.1 %copy-start.31 = (f32[64]{0:T(128)S(1)}, f32[64]{0:T(128)}, u32[]{:S(2)}) copy-start(f32[64]{0:T(128)} %constant.90.clone) | copy-start | bytes 772
  82.9 6.2 %copy-start.17 = (bf16[256,512]{1,0:T(8,128)(2,1)}, bf16[256,512]{1,0:T(8,128)(2,1)S(1)}, u32[]{:S(2)}) copy-start(bf16[256,512]{1,0:T(8,128)(2,1)S(1)} %collective-permute-done.16.refs_2_) | copy-start | bytes 786436
  83.0 6.2 %copy-start.19 = (bf16[256,512]{1,0:T(8,128)(2,1)}, bf16[256,512]{1,0:T(8,128)(2,1)S(1)}, u32[]{:S(2)}) copy-start(bf16[256,512]{1,0:T(8,128)(2,1)S(1)} %collective-permute-done.17.refs_4_) | copy-start | bytes 786436
  83.0 11.4 %copy-start.16 = (bf16[256,512]{1,0:T(8,128)(2,1)}, bf16[256,512]{1,0:T(8,128)(2,1)S(1)}, u32[]{:S(2)}) copy-start(bf16[256,512]{1,0:T(8,128)(2,1)S(1)} %collective-permute-done.18.refs_1_) | copy-start | bytes 786436
  83.0 6.2 %collective-permute-start.21 = (f32[320,512]{1,0:T(8,128)}, f32[320,512]{1,0:T(8,128)S(1)}, u32[]{:S(2)}, u32[]{:S(2)}) collective-permute-start(f32[320,512]{1,0:T(8,128)} %get-tuple-element.74), channel_id=1, source_target_pairs={{0,1},{1,0},{2,3},{3,2},{4,5},{5,4},{6,7},{7,6},{8,9},{9,8},{10,11... | collective-permute-start | bytes 1966088 | tf_op jit(solution)/shard_map/ppermute | solution.py:66
  84.2 4.3 %collective-permute-start.19 = (bf16[256,512]{1,0:T(8,128)(2,1)S(1)}, bf16[256,512]{1,0:T(8,128)(2,1)S(1)}, u32[]{:S(2)}, u32[]{:S(2)}) collective-permute-start(bf16[256,512]{1,0:T(8,128)(2,1)S(1)} %collective-permute-done.16.refs_2_), channel_id=1, source_target_pairs={{0,1},{1,0},{2,3},{3,2},{4,5},{5,4},{6,7},{7,6},{8,9},{9,8},{10,11... | collective-permute-start | bytes 786440 | tf_op jit(solution)/shard_map/ppermute | solution.py:66
  84.7 4.4 %collective-permute-start.20 = (bf16[256,512]{1,0:T(8,128)(2,1)S(1)}, bf16[256,512]{1,0:T(8,128)(2,1)S(1)}, u32[]{:S(2)}, u32[]{:S(2)}) collective-permute-start(bf16[256,512]{1,0:T(8,128)(2,1)S(1)} %collective-permute-done.17.refs_4_), channel_id=1, source_target_pairs={{0,1},{1,0},{2,3},{3,2},{4,5},{5,4},{6,7},{7,6},{8,9},{9,8},{10,11... | collective-permute-start | bytes 786440 | tf_op jit(solution)/shard_map/ppermute | solution.py:66
  85.5 18.3 %collective-permute-start.22 = (bf16[256,512]{1,0:T(8,128)(2,1)S(1)}, bf16[256,512]{1,0:T(8,128)(2,1)S(1)}, u32[]{:S(2)}, u32[]{:S(2)}) collective-permute-start(bf16[256,512]{1,0:T(8,128)(2,1)S(1)} %collective-permute-done.18.refs_1_), channel_id=1, source_target_pairs={{0,2},{1,3},{2,0},{3,1},{4,6},{5,7},{6,4},{7,5},{8,10},{9,11},{10,... | collective-permute-start | bytes 786440 | tf_op jit(solution)/shard_map/ppermute | solution.py:66
  87.1 16.7 %collective-permute-start.23 = (bf16[256,512]{1,0:T(8,128)(2,1)S(1)}, bf16[256,512]{1,0:T(8,128)(2,1)S(1)}, u32[]{:S(2)}, u32[]{:S(2)}) collective-permute-start(bf16[256,512]{1,0:T(8,128)(2,1)S(1)} %get-tuple-element.76.refs_2_), channel_id=1, source_target_pairs={{0,16},{1,17},{2,18},{3,19},{4,20},{5,21},{6,22},{7,23},{8,24},{9,... | collective-permute-start | bytes 786440 | tf_op jit(solution)/shard_map/ppermute | solution.py:66
  88.6 15.3 %collective-permute-start.24 = (bf16[256,512]{1,0:T(8,128)(2,1)S(1)}, bf16[256,512]{1,0:T(8,128)(2,1)S(1)}, u32[]{:S(2)}, u32[]{:S(2)}) collective-permute-start(bf16[256,512]{1,0:T(8,128)(2,1)S(1)} %collective-permute-done.14.refs_3_), channel_id=1, source_target_pairs={{0,16},{1,17},{2,18},{3,19},{4,20},{5,21},{6,22},{7,23},{8,24},{9,... | collective-permute-start | bytes 786440 | tf_op jit(solution)/shard_map/ppermute | solution.py:66
  89.2 0.9 copy-start.7
  94.4 14.7 %all-to-all-start = ((bf16[16,80,128]{2,1,0:T(8,128)(2,1)}), bf16[16,80,128]{2,1,0:T(8,128)(2,1)S(1)}, u32[]{:S(2)}, u32[]{:S(2)}) async-start(bf16[16,80,128]{2,1,0:T(8,128)(2,1)} %cache_rows.2), calls=%async_computation | async-start | bytes 655360 | tf_op jit(solution)/shard_map/all_to_all | solution.py:451
  102.6 6.5 %collective-permute-start.28 = (f32[320,512]{1,0:T(8,128)}, f32[320,512]{1,0:T(8,128)S(1)}, u32[]{:S(2)}, u32[]{:S(2)}) collective-permute-start(f32[320,512]{1,0:T(8,128)} %get-tuple-element.85), channel_id=1, source_target_pairs={{0,1},{1,0},{2,3},{3,2},{4,5},{5,4},{6,7},{7,6},{8,9},{9,8},{10,11... | collective-permute-start | bytes 1966088 | tf_op jit(solution)/shard_map/ppermute | solution.py:66
  103.8 5.3 %copy-start.20 = (bf16[256,512]{1,0:T(8,128)(2,1)}, bf16[256,512]{1,0:T(8,128)(2,1)S(1)}, u32[]{:S(2)}) copy-start(bf16[256,512]{1,0:T(8,128)(2,1)S(1)} %collective-permute-done.22.refs_2_) | copy-start | bytes 786436
  103.8 5.3 %copy-start.22 = (bf16[256,512]{1,0:T(8,128)(2,1)}, bf16[256,512]{1,0:T(8,128)(2,1)S(1)}, u32[]{:S(2)}) copy-start(bf16[256,512]{1,0:T(8,128)(2,1)S(1)} %collective-permute-done.23.refs_4_) | copy-start | bytes 786436
  103.9 5.3 %copy-start.23 = (bf16[256,512]{1,0:T(8,128)(2,1)}, bf16[256,512]{1,0:T(8,128)(2,1)S(1)}, u32[]{:S(2)}) copy-start(bf16[256,512]{1,0:T(8,128)(2,1)S(1)} %collective-permute-done.24.refs_6_) | copy-start | bytes 786436
  103.9 1.6 %collective-permute-start.25 = (bf16[256,512]{1,0:T(8,128)(2,1)S(1)}, bf16[256,512]{1,0:T(8,128)(2,1)S(1)}, u32[]{:S(2)}, u32[]{:S(2)}) collective-permute-start(bf16[256,512]{1,0:T(8,128)(2,1)S(1)} %collective-permute-done.22.refs_2_), channel_id=1, source_target_pairs={{0,1},{1,0},{2,3},{3,2},{4,5},{5,4},{6,7},{7,6},{8,9},{9,8},{10,11... | collective-permute-start | bytes 786440 | tf_op jit(solution)/shard_map/ppermute | solution.py:66
  104.0 1.8 %collective-permute-start.26 = (bf16[256,512]{1,0:T(8,128)(2,1)S(1)}, bf16[256,512]{1,0:T(8,128)(2,1)S(1)}, u32[]{:S(2)}, u32[]{:S(2)}) collective-permute-start(bf16[256,512]{1,0:T(8,128)(2,1)S(1)} %collective-permute-done.23.refs_4_), channel_id=1, source_target_pairs={{0,1},{1,0},{2,3},{3,2},{4,5},{5,4},{6,7},{7,6},{8,9},{9,8},{10,11... | collective-permute-start | bytes 786440 | tf_op jit(solution)/shard_map/ppermute | solution.py:66
  104.4 1.8 %collective-permute-start.27 = (bf16[256,512]{1,0:T(8,128)(2,1)S(1)}, bf16[256,512]{1,0:T(8,128)(2,1)S(1)}, u32[]{:S(2)}, u32[]{:S(2)}) collective-permute-start(bf16[256,512]{1,0:T(8,128)(2,1)S(1)} %collective-permute-done.24.refs_6_), channel_id=1, source_target_pairs={{0,1},{1,0},{2,3},{3,2},{4,5},{5,4},{6,7},{7,6},{8,9},{9,8},{10,11... | collective-permute-start | bytes 786440 | tf_op jit(solution)/shard_map/ppermute | solution.py:66
  105.5 3.7 %copy-start.24 = (bf16[256,512]{1,0:T(8,128)(2,1)}, bf16[256,512]{1,0:T(8,128)(2,1)S(1)}, u32[]{:S(2)}) copy-start(bf16[256,512]{1,0:T(8,128)(2,1)S(1)} %collective-permute-done.25.refs_3_) | copy-start | bytes 786436
  105.8 3.3 %copy-start.26 = (bf16[256,512]{1,0:T(8,128)(2,1)}, bf16[256,512]{1,0:T(8,128)(2,1)S(1)}, u32[]{:S(2)}) copy-start(bf16[256,512]{1,0:T(8,128)(2,1)S(1)} %collective-permute-done.26.refs_5_) | copy-start | bytes 786436
  106.2 2.9 %copy-start.28 = (bf16[256,512]{1,0:T(8,128)(2,1)}, bf16[256,512]{1,0:T(8,128)(2,1)S(1)}, u32[]{:S(2)}) copy-start(bf16[256,512]{1,0:T(8,128)(2,1)S(1)} %collective-permute-done.27.refs_7_) | copy-start | bytes 786436
  109.1 0.7 copy-start.1
  109.1 1.0 copy-start.6
  114.4 14.6 %all-to-all-start.1 = ((bf16[16,80,128]{2,1,0:T(8,128)(2,1)}), bf16[16,80,128]{2,1,0:T(8,128)(2,1)S(1)}, u32[]{:S(2)}, u32[]{:S(2)}) async-start(bf16[16,80,128]{2,1,0:T(8,128)(2,1)} %cache_rows.3), calls=%async_computation.1 | async-start | bytes 655360 | tf_op jit(solution)/shard_map/all_to_all | solution.py:465
  119.3 1.2 collective-permute-start.29
  120.8 1.2 collective-permute-start.30
  129.3 2.0 %collective-permute-start.31 = (f32[4,1024]{1,0:T(4,128)S(1)}, f32[4,1024]{1,0:T(4,128)S(1)}, u32[]{:S(2)}, u32[]{:S(2)}) collective-permute-start(f32[4,1024]{1,0:T(4,128)S(1)} %bitcast.55), channel_id=1, source_target_pairs={{0,1},{1,0},{2,3},{3,2},{4,5},{5,4},{6,7},{7,6},{8,9},{9,8},{10,11... | collective-permute-start | bytes 49160 | tf_op jit(solution)/shard_map/ppermute | solution.py:27
  (2 other events, 1.4 us)

commit v9 on v8

--- a/solution.py
+++ b/solution.py
@@ -100,33 +100,36 @@
     return pl.CostEstimate(flops=flops, bytes_accessed=moved_bytes, transcendentals=0)
 
 
-def halves_kernel(place, key_sent, value_sent, key_rest, value_rest, sent, rest):
-    columns = key_sent.shape[1]
-    sent[:, :columns] = key_sent[...]
-    sent[:, columns:] = value_sent[...]
-    rest[:, :columns] = key_rest[...]
-    rest[:, columns:] = value_rest[...]
-
-
-def weight_halves(place, key_weight, value_weight):
+def fetch(source, target, sem):
+    copy = pltpu.make_async_copy(source, target, sem)
+    copy.start()
+    return copy
+
+
+def halves_kernel(kind, place, key_weight, value_weight, out, sems):
+    depth, columns = out.shape[0], out.shape[1] // 2
+    half = 1 - place[0] if kind else place[0]
+    rows = pl.ds(pl.multiple_of(half * depth, depth), depth)
+    copies = [
+        fetch(weight.at[rows], out.at[:, pl.ds(k * columns, columns)], sems.at[k])
+        for k, weight in enumerate((key_weight, value_weight))
+    ]
+    for copy in copies:
+        copy.wait()
+
+
+def weight_half(place, kind, key_weight, value_weight):
     rows, columns = key_weight.shape
-    depth = rows // 2
-    out = jax.ShapeDtypeStruct((depth, 2 * columns), key_weight.dtype)
-    sent = pl.BlockSpec((depth, columns), lambda i, place: (place[0], 0))
-    rest = pl.BlockSpec((depth, columns), lambda i, place: (1 - place[0], 0))
     return pl.pallas_call(
-        halves_kernel,
-        grid_spec=pltpu.PrefetchScalarGridSpec(
-            num_scalar_prefetch=1,
-            grid=(1,),
-            in_specs=[sent, sent, rest, rest],
-            out_specs=[pl.BlockSpec(out.shape, lambda i, place: (0, 0))] * 2,
-        ),
-        out_shape=[out, out],
+        functools.partial(halves_kernel, kind),
+        in_specs=[SMEM_REF, ANY_REF, ANY_REF],
+        out_specs=VMEM_REF,
+        out_shape=jax.ShapeDtypeStruct((rows // 2, 2 * columns), key_weight.dtype),
+        scratch_shapes=[pltpu.SemaphoreType.DMA((2,))],
         compiler_params=PARAMS,
         cost_estimate=cost(1000, 1000),
-        name="weight_halves",
-    )(place, key_weight, value_weight, key_weight, value_weight)
+        name="weight_half",
+    )(place, key_weight, value_weight)
 
 
 def prepare_kernel(place, *refs):
@@ -184,12 +187,6 @@
     return lax.optimization_barrier((value, *events))[0]
 
 
-def fetch(source, target, sem):
-    copy = pltpu.make_async_copy(source, target, sem)
-    copy.start()
-    return copy
-
-
 def half_index(place, entry, kind):
     half = {0: place[0], 1: 1 - place[0], 2: 0, 3: 1}[kind]
     return place[entry] * 2 + half
@@ -197,24 +194,23 @@
 
 def product_kernel(plan, group, parts, with_total, place, both, *refs):
     count = len(plan)
-    pieces = refs[:count]
-    totals_in = refs[count : count + 2 * with_total * parts]
+    taken = sum(pair for _, _, pair in plan)
+    totals_in = refs[taken : taken + 2 * with_total * parts]
+    next_ref = iter(refs)
     outs = refs[-5 - 2 * parts : -5]
     left, right, total, sems, total_sems = refs[-5:]
     rows, depth = both.shape[2], both.shape[3]
     columns = right.shape[2]
     waits = []
-    for k, (entry, kind, column) in enumerate(plan):
+    width = columns // parts
+    for k, (entry, kind, pair) in enumerate(plan):
         area = pl.ds((k % group) * depth, depth)
         slot = k // group
-        piece = pieces[k].at[:, pl.ds(column, columns)]
-        waits.append(
-            [
-                fetch(both.at[half_index(place, entry, kind)], left.at[slot, :, :, area], sems.at[2 * k]),
-                fetch(piece, right.at[slot, area], sems.at[2 * k + 1]),
-            ]
-        )
-    width = columns // parts
+        index = half_index(place, entry, kind)
+        waits.append([fetch(both.at[index], left.at[slot, :, :, area], sems.at[3 * k])])
+        for p in range(pair):
+            target = right.at[slot, area, pl.ds(p * columns // pair, columns // pair)]
+            waits[-1].append(fetch(next(next_ref), target, sems.at[3 * k + 1 + p]))
     carried = [
         fetch(
             ref,
@@ -243,26 +239,28 @@
                 ]
 
 
-def product(place, both, plan, pieces, totals, group, columns, parts):
+def product(place, both, pieces, totals, group, columns, parts):
     _, _, rows, depth = both.shape
+    plan = [(entry, kind, len(arrays)) for entry, kind, *arrays in pieces]
+    pieces_flat = [array for _, _, *arrays in pieces for array in arrays]
     count = len(plan)
     out = jax.ShapeDtypeStruct((rows, columns // parts), jnp.float32)
     return pl.pallas_call(
         functools.partial(product_kernel, plan, group, parts, bool(totals)),
-        in_specs=[SMEM_REF] + [ANY_REF] * (1 + count + len(totals)),
+        in_specs=[SMEM_REF] + [ANY_REF] * (1 + len(pieces_flat) + len(totals)),
         out_specs=[VMEM_REF] * (2 * parts),
         out_shape=[out] * (2 * parts),
         scratch_shapes=[
             pltpu.VMEM((count // group, 2, rows, group * depth), both.dtype),
             pltpu.VMEM((count // group, group * depth, columns), both.dtype),
             pltpu.VMEM((2 * rows, columns), jnp.float32),
-            pltpu.SemaphoreType.DMA((2 * count,)),
+            pltpu.SemaphoreType.DMA((3 * count,)),
             pltpu.SemaphoreType.DMA((2 * parts,)),
         ],
         compiler_params=PARAMS,
         cost_estimate=cost(1000, 1000),
         name="add_product",
-    )(place, both, *pieces, *totals)
+    )(place, both, *pieces_flat, *totals)
 
 
 def rows_kernel(plan, rotated, place, lengths, owner, both, kept, *refs):
@@ -386,92 +384,6 @@
         )
         return lax.all_to_all(outgoing, "seq", split_axis=0, concat_axis=1, tiled=True)[0]
 
-    cosine, sine_part = rope_table(positions, HEAD_SIZE)
-    if planned:
-        turn = (
-            jnp.concatenate([cosine, cosine], 1),
-            jnp.concatenate([-sine_part, sine_part], 1),
-        )
-        columns = key_weight.shape[1]
-
-        def parts_of(block):
-            return [block[:, k * columns : (k + 1) * columns] for k in range(2)]
-
-        sent, rest = weight_halves(place, key_weight, value_weight)
-        near = moved(sent, to_pair)
-        middle = moved(sent, to_middle)
-        across = moved(sent, to_row)
-        other = moved(flat, to_core)
-        came = (near, middle, across, other)
-        end_b = moved(after(middle, *came), to_end)
-        middle_c = moved(after(near, *came), to_middle)
-        near_y = moved(after(near, *came), to_row)
-        across_x = moved(after(across, *came), to_group)
-        both, kept = prepared(place, after(flat, *came), other, seq // 2)
-        came = (end_b, middle_c, near_y, across_x, both)
-        end_c = moved(after(middle_c, *came), to_end)
-        near_xy = moved(after(near_y, *came), to_group)
-        block_b = jnp.where(is_end, after(end_b, *came), middle)
-        block_yb = moved(block_b, to_row)
-        plan = [(HERE, 0, 0), (HERE, 1, 0), (THERE, 0, 0), (THERE, 1, 0)]
-        plan += [(HERE + 1, 0, 0), (THERE + 1, 0, 0)]
-        pieces = [sent, rest, across, across_x, near, near_y]
-        totals = product(place, after(both, *came), plan, pieces, (), 3, 2 * columns, 2)
-        key_b, value_b = parts_of(block_b)
-        came = (end_c, near_xy, block_yb, totals[0], key_b, value_b)
-        near_rest = moved(after(rest, *came), to_pair)
-        key_xb = moved(after(key_b, *came), to_group)
-        key_c, value_c = parts_of(jnp.where(is_end, after(end_c, *came), middle_c))
-        key_yc, value_yc = moved(key_c, to_row), moved(value_c, to_row)
-        key_xc = moved(key_c, to_group)
-        plan = [(THERE + 1, 1, 0), (HERE + 2, 0, 0), (THERE + 2, 0, 0)]
-        pieces = [near_xy, block_b, block_yb]
-        totals = product(place, after(both, *came), plan, pieces, totals, 3, 2 * columns, 2)
-        came = (near_rest, key_xb, key_yc, value_yc, key_xc, totals[0])
-        key_xyc = moved(after(key_yc, *came), to_group)
-        key_yxb = moved(after(key_xb, *came), to_row)
-        value_xb = moved(after(value_b, *came), to_group)
-        plan = [(HERE + 1, 1, 0), (HERE + 2, 1, 0), (HERE + 3, 0, 0), (HERE + 3, 1, 0)]
-        plan += [(THERE + 3, 0, 0)]
-        pieces = [near_rest, key_xb, key_c, key_xc, key_yc]
-        total, given = product(
-            place, after(both, *came), plan, pieces, totals[:2], 5, columns, 1
-        )
-        came = (key_xyc, key_yxb, value_xb, total)
-        value_yxb = moved(after(value_xb, *came), to_row)
-        value_xc = moved(after(value_c, *came), to_group)
-        value_xyc = moved(after(value_yc, *came), to_group)
-        given = moved(after(given, *came), to_core)
-        ends = [after(key_yxb, *came), after(key_xyc, *came)]
-        pieces = [piece for end in ends for piece in (end, moved(end, to_core))]
-        plan = [(THERE + 2, 1), (THERE + 3, 1)]
-        outgoing = outgoing_rows(
-            place, lengths, owner, both, kept, plan, pieces, total, given, turn, place
-        )
-        cache_keys = lax.all_to_all(outgoing, "seq", split_axis=0, concat_axis=1, tiled=True)[0]
-        plan = [(HERE + 1, 1, columns), (HERE + 2, 1, 0), (HERE + 3, 0, 0), (THERE + 3, 0, 0)]
-        pieces = [near_rest, value_xb, value_c, value_yc]
-        total, given = product(
-            place, after(both, outgoing), plan, pieces, totals[2:], 4, columns, 1
-        )
-        given = moved(given, to_core)
-        came = (value_yxb, value_xc, value_xyc, total)
-        ends = [after(end, *came) for end in came[:3]]
-        pieces = [piece for end in ends for piece in (end, moved(end, to_core))]
-        plan = [(THERE + 2, 1), (HERE + 3, 1), (THERE + 3, 1)]
-        outgoing = outgoing_rows(
-            place, lengths, owner, both, kept, plan, pieces, total, given, (), cache_keys
-        )
-        cache_values = lax.all_to_all(outgoing, "seq", split_axis=0, concat_axis=1, tiled=True)[0]
-    else:
-        shape = (count_requests, count_rows, KEY_VALUE_HEADS, HEAD_SIZE)
-        unrotated_key = project(key_weight).reshape(shape)
-        key_rows = rotate(
-            unrotated_key, cosine[:, None, :], sine_part[:, None, :]
-        ).astype(jnp.bfloat16)
-        cache_keys = handed_over(key_rows)
-        cache_values = handed_over(project(value_weight).astype(jnp.bfloat16).reshape(shape))
-    slot_count = cache_keys.shape[0]
     decode_peer = device_id // split_point
     block = device_id % split_point
     source_pair = jnp.sum(jnp.where(owner == decode_peer, pair_ids, 0))
@@ -490,6 +402,81 @@
         step_sin[:, None, :],
     ).astype(jnp.bfloat16)
     new_keys = rotate(new_key.astype(jnp.float32), step_cos, step_sin).astype(jnp.bfloat16)
+    cosine, sine_part = rope_table(positions, HEAD_SIZE)
+    if planned:
+        turn = (
+            jnp.concatenate([cosine, cosine], 1),
+            jnp.concatenate([-sine_part, sine_part], 1),
+        )
+        columns = key_weight.shape[1]
+
+        def parts_of(block):
+            return [block[:, k * columns : (k + 1) * columns] for k in range(2)]
+
+        sent = weight_half(place, 0, key_weight, value_weight)
+        near = moved(sent, to_pair)
+        middle = moved(sent, to_middle)
+        across = moved(sent, to_row)
+        other = moved(flat, to_core)
+        rest = weight_half(place, 1, key_weight, after(value_weight, sent))
+        came = (near, middle, across, other, rest, *turn, query_rot, new_keys)
+        end_b = moved(after(middle, *came), to_end)
+        middle_c = moved(after(near, *came), to_middle)
+        near_y = moved(after(near, *came), to_row)
+        across_x = moved(after(across, *came), to_group)
+        both, kept = prepared(place, after(flat, *came), other, seq // 2)
+        came = (end_b, middle_c, near_y, across_x, both)
+        end_c = moved(after(middle_c, *came), to_end)
+        block_b = jnp.where(is_end, after(end_b, *came), middle)
+        block_yb = moved(block_b, to_row)
+        block_xb = moved(block_b, to_group)
+        pieces = [(HERE, 0, sent), (HERE, 1, rest), (THERE, 0, across), (THERE, 1, across_x)]
+        pieces += [(HERE + 1, 0, near), (THERE + 1, 0, near_y)]
+        totals = product(place, after(both, *came), pieces, (), 3, 2 * columns, 2)
+        ends_x = parts_of(after(across_x, *came))
+        came = (end_c, block_yb, block_xb, totals[0], *ends_x)
+        near_rest = moved(after(rest, *came), to_pair)
+        block_c = parts_of(jnp.where(is_end, after(end_c, *came), middle_c))
+        block_xc = [moved(block_c[0], to_group)]
+        block_yc = [moved(block_c[0], to_row)]
+        block_xc.append(moved(block_c[1], to_group))
+        block_yc.append(moved(block_c[1], to_row))
+        pieces = [(HERE + 2, 0, block_b), (HERE + 2, 1, block_xb)]
+        pieces += [(THERE + 2, 0, block_yb), (HERE + 3, 0, *block_c)]
+        totals = product(place, after(both, *came), pieces, totals, 4, 2 * columns, 2)
+        ends_yb = parts_of(after(block_yb, *came))
+        came = (near_rest, *block_xc, *block_yc, totals[0], *ends_yb)
+        ends = []
+        for k in range(2):
+            near_xy = moved(after(ends_x[k], *came), to_pair)
+            ends.append([near_xy, moved(after(ends_yb[k], *came), to_group)])
+            ends[k].append(moved(after(block_xc[k], *came), to_row))
+        pieces = [(HERE + 1, 1, near_rest), (HERE + 3, 1, *block_xc), (THERE + 3, 0, *block_yc)]
+        totals = product(place, after(both, ends[0][1]), pieces, totals, 3, 2 * columns, 2)
+        plan = [(THERE + 1, 1), (THERE + 2, 1), (THERE + 3, 1)]
+        caches = []
+        token = place
+        for k, turned in enumerate((turn, ())):
+            given = moved(after(totals[2 * k + 1], token), to_core)
+            swapped_ends = [moved(end, to_core) for end in ends[k]]
+            pieces = [piece for pair in zip(ends[k], swapped_ends) for piece in pair]
+            outgoing = outgoing_rows(
+                place, lengths, owner, both, kept, plan, pieces, totals[2 * k], given, turned, token
+            )
+            caches.append(
+                lax.all_to_all(outgoing, "seq", split_axis=0, concat_axis=1, tiled=True)[0]
+            )
+            token = outgoing
+        cache_keys, cache_values = caches
+    else:
+        shape = (count_requests, count_rows, KEY_VALUE_HEADS, HEAD_SIZE)
+        unrotated_key = project(key_weight).reshape(shape)
+        key_rows = rotate(
+            unrotated_key, cosine[:, None, :], sine_part[:, None, :]
+        ).astype(jnp.bfloat16)
+        cache_keys = handed_over(key_rows)
+        cache_values = handed_over(project(value_weight).astype(jnp.bfloat16).reshape(shape))
+    slot_count = cache_keys.shape[0]
     score_scale = 1.0 / HEAD_SIZE**0.5
     old_scores = (
         jnp.einsum(

time: 133 us -> 143 us (1.075)
  waiting for transfers between devices: 35.2 us -> 44.4 us
  starting transfers between devices: 37.1 us -> 38.7 us
    ppermute x29 -> x30, waiting for transfers between devices: 23.7 us -> 34.7 us  [moved(): return lax.ppermute(block, ('groups', 'seq'), route)]
    pallas_call x4 -> x3, Pallas kernels: 21.3 us -> 17.3 us  [product(): pl.pallas_call(functools.partial(product_kernel, plan, group, parts, bool...]
    all_to_all x2, starting transfers between devices: 7.17 us -> 9.52 us  [body(): lax.all_to_all(outgoing, 'seq', split_axis=0, concat_axis=1, tiled=True)[0]]
    pallas_call x1 -> x2, Pallas kernels: 2.87 us -> 5.01 us  [weight_half(): pl.pallas_call(functools.partial(halves_kernel, kind), in_specs=[SMEM_REF...]
    all_to_all x2, waiting for transfers between devices: 9.76 us -> 7.88 us  [body(): lax.all_to_all(outgoing, 'seq', split_axis=0, concat_axis=1, tiled=True)[0]]
    ppermute x29 -> x30, starting transfers between devices: 29.1 us -> 28.2 us  [moved(): return lax.ppermute(block, ('groups', 'seq'), route)]
  transfers between devices with their start and end apart: 34 -> 35, of which waited for: 13 -> 18; matrix products, arithmetic and copies ran while one was open for 8% -> 7% of each run, Pallas kernels for 29% -> 22%
where the time goes in v9:
time: 143 us; the launch traced here: 142 us
  waiting for transfers between devices  44.4 us (31%)
  Pallas kernels  40.9 us (29%)
  starting transfers between devices  38.7 us (27%)
  other arithmetic  8.57 us (6%)
  local copies, waits for them, and re-layouts  4.7 us (3%)
  between operations  3.8 us (3%)
    ppermute x30, waiting for transfers between devices, moved(): return lax.ppermute(block, ('groups', 'seq'), route)  34.7 us
    ppermute x30, starting transfers between devices, moved(): return lax.ppermute(block, ('groups', 'seq'), route)  28.2 us
    pallas_call x3, Pallas kernels, product(): pl.pallas_call(functools.partial(product_kernel, plan, group, parts, bool...  17.3 us
    all_to_all x2, starting transfers between devices, body(): lax.all_to_all(outgoing, 'seq', split_axis=0, concat_axis=1, tiled=True)[0]  9.52 us
    pallas_call x1, Pallas kernels, prepared(): pl.pallas_call(prepare_kernel, grid_spec=pltpu.PrefetchScalarGridSpec(num...  9.37 us
    pallas_call x2, Pallas kernels, outgoing_rows(): pl.pallas_call(kernel, in_specs=[SMEM_REF] * 3 + [ANY_REF] * (1 + len(ope...  9.15 us
    all_to_all x2, waiting for transfers between devices, body(): lax.all_to_all(outgoing, 'seq', split_axis=0, concat_axis=1, tiled=True)[0]  7.88 us
    pallas_call x2, Pallas kernels, weight_half(): pl.pallas_call(functools.partial(halves_kernel, kind), in_specs=[SMEM_REF...  5.01 us
  transfers between devices with their start and end apart: 35, of which 18 were waited for; matrix products, arithmetic and copies ran while one was open for 7% of the time, Pallas kernels for 22%

profile of v9, /device:TPU:0, one launch (start us, length us, event | category | flops | bytes accessed | tf_op | source)
XLA Modules:
  0.0 142.0 jit_solution(3275948525857860462)
XLA Ops:
  0.7 0.5 collective-permute-start.3
  1.2 0.6 stack.47.place.place_ref.token_ref
  1.8 2.5 %weight_half.2.refs_0_ = bf16[256,1024]{1,0:T(8,128)(2,1)} custom-call(s32[11]{0:T(128)} %stack.47.place.place_ref.token_ref, bf16[512,512]{1,0:T(8,128)(2,1)} %key_weight.3, bf16[512,512]{1,0:T(8,128)(2,1)} %value_weight.2), custom_call_target="tpu_custom_call" | custom-call | flops 1000 | bytes 1000 | tf_op jit(solution)/shard_map/weight_half/pallas_call | solution.py:123
  4.3 2.7 %collective-permute-start = (bf16[256,1024]{1,0:T(8,128)(2,1)}, bf16[256,1024]{1,0:T(8,128)(2,1)S(1)}, u32[]{:S(2)}, u32[]{:S(2)}) collective-permute-start(bf16[256,1024]{1,0:T(8,128)(2,1)} %weight_half.2.refs_0_), channel_id=1, source_target_pairs={{0,4},{1,5},{2,6},{3,7},{4,0},{5,1},{6,2},{7,3},{8,12},{9,13},{10,... | collective-permute-start | bytes 1572872 | tf_op jit(solution)/shard_map/ppermute | solution.py:66
  7.1 0.7 collective-permute-start.1
  7.7 1.6 %collective-permute-start.2 = (bf16[256,1024]{1,0:T(8,128)(2,1)}, bf16[256,1024]{1,0:T(8,128)(2,1)S(1)}, u32[]{:S(2)}, u32[]{:S(2)}) collective-permute-start(bf16[256,1024]{1,0:T(8,128)(2,1)} %weight_half.2.refs_0_), channel_id=1, source_target_pairs={{0,2},{1,3},{2,0},{3,1},{4,6},{5,7},{6,4},{7,5},{8,10},{9,11},{10,... | collective-permute-start | bytes 1572872 | tf_op jit(solution)/shard_map/ppermute | solution.py:66
  9.3 2.5 %weight_half.3.refs_1_ = bf16[256,1024]{1,0:T(8,128)(2,1)} custom-call(s32[11]{0:T(128)} %stack.47.place.place_ref.token_ref, bf16[512,512]{1,0:T(8,128)(2,1)} %key_weight.3, bf16[512,512]{1,0:T(8,128)(2,1)} %value_weight.2), custom_call_target="tpu_custom_call" | custom-call | flops 1000 | bytes 1000 | tf_op jit(solution)/shard_map/weight_half/pallas_call | solution.py:123
  11.8 0.6 fusion.18
  15.1 0.7 convert_bitcast_fusion
  15.8 0.6 fusion.19
  16.4 0.6 add_convert_fusion.3
  17.1 0.7 fusion.14
  18.1 0.4 fusion.6
  18.5 0.8 pad_maximum_fusion
  19.3 0.5 collective-permute-done.refs_4_
  19.8 2.2 %collective-permute-done.2.refs_2_ = bf16[256,1024]{1,0:T(8,128)(2,1)S(1)} collective-permute-done((bf16[256,1024]{1,0:T(8,128)(2,1)}, bf16[256,1024]{1,0:T(8,128)(2,1)S(1)}, u32[]{:S(2)}, u32[]{:S(2)}) %collective-permute-start.2) | collective-permute-done | bytes 524320 | tf_op jit(solution)/shard_map/ppermute | solution.py:66
  22.0 1.5 %collective-permute-start.4 = (bf16[256,1024]{1,0:T(8,128)(2,1)S(1)}, bf16[256,1024]{1,0:T(8,128)(2,1)S(1)}, u32[]{:S(2)}, u32[]{:S(2)}) collective-permute-start(bf16[256,1024]{1,0:T(8,128)(2,1)S(1)} %collective-permute-done.2.refs_2_), channel_id=1, source_target_pairs={{0,16},{1,17},{2,18},{3,19},{4,20},{5,21},{6,22},{7,23},{8,24},{9,... | collective-permute-start | bytes 1572872 | tf_op jit(solution)/shard_map/ppermute | solution.py:66
  23.5 1.3 collective-permute-start.5
  24.8 0.7 collective-permute-start.6
  25.5 1.6 %collective-permute-start.7 = (bf16[256,1024]{1,0:T(8,128)(2,1)S(1)}, bf16[256,1024]{1,0:T(8,128)(2,1)S(1)}, u32[]{:S(2)}, u32[]{:S(2)}) collective-permute-start(bf16[256,1024]{1,0:T(8,128)(2,1)S(1)} %collective-permute-done.refs_4_), channel_id=1, source_target_pairs={{0,2},{1,3},{2,0},{3,1},{4,6},{5,7},{6,4},{7,5},{8,10},{9,11},{10,... | collective-permute-start | bytes 1572872 | tf_op jit(solution)/shard_map/ppermute | solution.py:66
  27.1 9.4 %normed_halves.1 = (bf16[16,2,320,256]{3,2,1,0:T(8,128)(2,1)}, bf16[16,320,256]{2,1,0:T(8,128)(2,1)}) custom-call(s32[11]{0:T(128)} %stack.47.place.place_ref.token_ref, bf16[320,8192]{1,0:T(8,128)(2,1)} %bitcast.50, bf16[320,8192]{1,0:T(8,128)(2,1)} %collective-permute-done.3.refs_1_), custom_call_target="tpu_custom_call" | custom-call | flops 1000 | bytes 1000 | tf_op jit(solution)/shard_map/normed_halves/pallas_call | solution.py:165
  36.5 3.3 %collective-permute-done.5 = bf16[256,1024]{1,0:T(8,128)(2,1)} collective-permute-done((bf16[256,1024]{1,0:T(8,128)(2,1)S(1)}, bf16[256,1024]{1,0:T(8,128)(2,1)}, u32[]{:S(2)}, u32[]{:S(2)}) %collective-permute-start.5) | collective-permute-done | bytes 524320 | tf_op jit(solution)/shard_map/ppermute | solution.py:66
  39.8 1.3 broadcast_select_fusion.1.refs_0_
  41.1 0.6 collective-permute-start.10
  41.7 1.5 %collective-permute-start.9 = (bf16[256,1024]{1,0:T(8,128)(2,1)S(1)}, bf16[256,1024]{1,0:T(8,128)(2,1)S(1)}, u32[]{:S(2)}, u32[]{:S(2)}) collective-permute-start(bf16[256,1024]{1,0:T(8,128)(2,1)S(1)} %broadcast_select_fusion.1.refs_0_), channel_id=1, source_target_pairs={{0,2},{1,3},{2,0},{3,1},{4,6},{5,7},{6,4},{7,5},{8,10},{9,11},{10,... | collective-permute-start | bytes 1572872 | tf_op jit(solution)/shard_map/ppermute | solution.py:66
  43.3 1.3 collective-permute-start.8
  44.6 5.9 %add_product.3 = (f32[320,512]{1,0:T(8,128)}, f32[320,512]{1,0:T(8,128)}, f32[320,512]{1,0:T(8,128)}, f32[320,512]{1,0:T(8,128)}) custom-call(s32[11]{0:T(128)} %stack.47.place.place_ref.token_ref, bf16[16,2,320,256]{3,2,1,0:T(8,128)(2,1)} %get-tuple-element.61.both.refs_0_, bf16[256,1024]{1,0:T(8,128)(2,1)} %weight_half.2.refs_0_, ...), custom_call_target="tpu_custom_call" | custom-call | flops 1000 | bytes 1000 | tf_op jit(solution)/shard_map/add_product/pallas_call | solution.py:248
  50.5 1.1 fusion.22
  51.6 1.6 %collective-permute-done.10.refs_1_ = bf16[256,1024]{1,0:T(8,128)(2,1)S(1)} collective-permute-done((bf16[256,1024]{1,0:T(8,128)(2,1)S(1)}, bf16[256,1024]{1,0:T(8,128)(2,1)S(1)}, u32[]{:S(2)}, u32[]{:S(2)}) %collective-permute-start.10) | collective-permute-done | bytes 524320 | tf_op jit(solution)/shard_map/ppermute | solution.py:66
  53.4 4.7 %collective-permute-done.8 = bf16[256,1024]{1,0:T(8,128)(2,1)S(1)} collective-permute-done((bf16[256,1024]{1,0:T(8,128)(2,1)S(1)}, bf16[256,1024]{1,0:T(8,128)(2,1)S(1)}, u32[]{:S(2)}, u32[]{:S(2)}) %collective-permute-start.8) | collective-permute-done | bytes 524320 | tf_op jit(solution)/shard_map/ppermute | solution.py:66
  58.3 1.6 %collective-permute-start.12 = (bf16[256,512]{1,0:T(8,128)(2,1)S(1)}, bf16[256,512]{1,0:T(8,128)(2,1)S(1)}, u32[]{:S(2)}, u32[]{:S(2)}) collective-permute-start(bf16[256,512]{1,0:T(8,128)(2,1)S(1)} %get-tuple-element.77.refs_3_), channel_id=1, source_target_pairs={{0,16},{1,17},{2,18},{3,19},{4,20},{5,21},{6,22},{7,23},{8,24},{9,... | collective-permute-start | bytes 786440 | tf_op jit(solution)/shard_map/ppermute | solution.py:66
  59.8 0.5 collective-permute-start.13
  60.3 0.5 collective-permute-start.14
  60.9 1.5 %collective-permute-start.15 = (bf16[256,512]{1,0:T(8,128)(2,1)S(1)}, bf16[256,512]{1,0:T(8,128)(2,1)S(1)}, u32[]{:S(2)}, u32[]{:S(2)}) collective-permute-start(bf16[256,512]{1,0:T(8,128)(2,1)S(1)} %get-tuple-element.76.refs_4_), channel_id=1, source_target_pairs={{0,2},{1,3},{2,0},{3,1},{4,6},{5,7},{6,4},{7,5},{8,10},{9,11},{10,... | collective-permute-start | bytes 786440 | tf_op jit(solution)/shard_map/ppermute | solution.py:66
  62.4 6.1 %add_product.4 = (f32[320,512]{1,0:T(8,128)}, f32[320,512]{1,0:T(8,128)}, f32[320,512]{1,0:T(8,128)}, f32[320,512]{1,0:T(8,128)}) custom-call(s32[11]{0:T(128)} %stack.47.place.place_ref.token_ref, bf16[16,2,320,256]{3,2,1,0:T(8,128)(2,1)} %get-tuple-element.61.both.refs_0_, bf16[256,1024]{1,0:T(8,128)(2,1)} %copy-done.2, bf16[256,1024]{1,0:T(8,128)(2,1)} %copy-done.12, ...), custom_call_target="tpu_custom_call" | custom-call | flops 1000 | bytes 1000 | tf_op jit(solution)/shard_map/add_product/pallas_call | solution.py:248
  68.5 1.1 fusion.20
  69.6 1.6 %collective-permute-start.18 = (bf16[256,512]{1,0:T(8,128)(2,1)S(1)}, bf16[256,512]{1,0:T(8,128)(2,1)S(1)}, u32[]{:S(2)}, u32[]{:S(2)}) collective-permute-start(bf16[256,512]{1,0:T(8,128)(2,1)S(1)} %get-tuple-element.59), channel_id=1, source_target_pairs={{0,16},{1,17},{2,18},{3,19},{4,20},{5,21},{6,22},{7,23},{8,24},{9,... | collective-permute-start | bytes 786440 | tf_op jit(solution)/shard_map/ppermute | solution.py:66
  71.2 4.9 %collective-permute-done.18.refs_4_ = bf16[256,512]{1,0:T(8,128)(2,1)S(1)} collective-permute-done((bf16[256,512]{1,0:T(8,128)(2,1)S(1)}, bf16[256,512]{1,0:T(8,128)(2,1)S(1)}, u32[]{:S(2)}, u32[]{:S(2)}) %collective-permute-start.18) | collective-permute-done | bytes 262176 | tf_op jit(solution)/shard_map/ppermute | solution.py:66
  76.1 5.4 %add_product.5 = (f32[320,512]{1,0:T(8,128)}, f32[320,512]{1,0:T(8,128)}, f32[320,512]{1,0:T(8,128)}, f32[320,512]{1,0:T(8,128)}) custom-call(s32[11]{0:T(128)} %stack.47.place.place_ref.token_ref, bf16[16,2,320,256]{3,2,1,0:T(8,128)(2,1)} %get-tuple-element.61.both.refs_0_, bf16[256,1024]{1,0:T(8,128)(2,1)} %copy-done.11, bf16[256,512]{1,0:T(8,128)(2,1)} %copy-done.16, ...), custom_call_target="tpu_custom_call" | custom-call | flops 1000 | bytes 1000 | tf_op jit(solution)/shard_map/add_product/pallas_call | solution.py:248
  81.6 0.6 collective-permute-start.20
  82.2 2.0 %collective-permute-start.16 = (bf16[256,512]{1,0:T(8,128)(2,1)S(1)}, bf16[256,512]{1,0:T(8,128)(2,1)S(1)}, u32[]{:S(2)}, u32[]{:S(2)}) collective-permute-start(bf16[256,512]{1,0:T(8,128)(2,1)S(1)} %get-tuple-element.58), channel_id=1, source_target_pairs={{0,4},{1,5},{2,6},{3,7},{4,0},{5,1},{6,2},{7,3},{8,12},{9,13},{10,... | collective-permute-start | bytes 786440 | tf_op jit(solution)/shard_map/ppermute | solution.py:66
  84.2 6.3 %collective-permute-done.20.refs_6_ = bf16[256,512]{1,0:T(8,128)(2,1)S(1)} collective-permute-done((bf16[256,512]{1,0:T(8,128)(2,1)}, bf16[256,512]{1,0:T(8,128)(2,1)S(1)}, u32[]{:S(2)}, u32[]{:S(2)}) %collective-permute-start.20) | collective-permute-done | bytes 262176 | tf_op jit(solution)/shard_map/ppermute | solution.py:66
  91.0 1.0 collective-permute-done.21.refs_7_
  92.0 0.4 collective-permute-done.17.refs_3_
  93.4 4.8 %cache_rows.2.token_ref = bf16[16,80,128]{2,1,0:T(8,128)(2,1)} custom-call(s32[11]{0:T(128)} %stack.47.place.place_ref.token_ref, s32[2]{0:T(128)} %lengths_ref.3, s32[8]{0:T(128)} %owner_ref.3, s32[11]{0:T(128)} %stack.47.place.place_ref.token_ref, bf16[16,2,320,256]{3,2,1,0:T(8,128)(2,1)} %get-tuple-element.61.both.refs_0_, ...), custom_call_target="tpu_custom_call" | custom-call | flops 1000 | bytes 1000 | tf_op jit(solution)/shard_map/cache_rows/pallas_call | solution.py:315
  98.4 4.9 %all-to-all-start = ((bf16[16,80,128]{2,1,0:T(8,128)(2,1)}), bf16[16,80,128]{2,1,0:T(8,128)(2,1)S(1)}, u32[]{:S(2)}, u32[]{:S(2)}) async-start(bf16[16,80,128]{2,1,0:T(8,128)(2,1)} %cache_rows.2.token_ref), calls=%async_computation | async-start | bytes 655360 | tf_op jit(solution)/shard_map/all_to_all | solution.py:467
  103.3 2.0 %collective-permute-start.27 = (bf16[256,512]{1,0:T(8,128)(2,1)S(1)}, bf16[256,512]{1,0:T(8,128)(2,1)S(1)}, u32[]{:S(2)}, u32[]{:S(2)}) collective-permute-start(bf16[256,512]{1,0:T(8,128)(2,1)S(1)} %copy-done.15), channel_id=1, source_target_pairs={{0,2},{1,3},{2,0},{3,1},{4,6},{5,7},{6,4},{7,5},{8,10},{9,11},{10,... | collective-permute-start | bytes 786440 | tf_op jit(solution)/shard_map/ppermute | solution.py:66
  105.3 1.5 %collective-permute-start.25 = (bf16[256,512]{1,0:T(8,128)(2,1)S(1)}, bf16[256,512]{1,0:T(8,128)(2,1)S(1)}, u32[]{:S(2)}, u32[]{:S(2)}) collective-permute-start(bf16[256,512]{1,0:T(8,128)(2,1)S(1)} %get-tuple-element.69), channel_id=1, source_target_pairs={{0,16},{1,17},{2,18},{3,19},{4,20},{5,21},{6,22},{7,23},{8,24},{9,... | collective-permute-start | bytes 786440 | tf_op jit(solution)/shard_map/ppermute | solution.py:66
  106.8 1.5 %collective-permute-start.23 = (bf16[256,512]{1,0:T(8,128)(2,1)S(1)}, bf16[256,512]{1,0:T(8,128)(2,1)S(1)}, u32[]{:S(2)}, u32[]{:S(2)}) collective-permute-start(bf16[256,512]{1,0:T(8,128)(2,1)S(1)} %get-tuple-element.68), channel_id=1, source_target_pairs={{0,4},{1,5},{2,6},{3,7},{4,0},{5,1},{6,2},{7,3},{8,12},{9,13},{10,... | collective-permute-start | bytes 786440 | tf_op jit(solution)/shard_map/ppermute | solution.py:66
  108.2 0.7 add_compare_fusion
  108.9 6.6 %collective-permute-done.27.refs_6_ = bf16[256,512]{1,0:T(8,128)(2,1)S(1)} collective-permute-done((bf16[256,512]{1,0:T(8,128)(2,1)S(1)}, bf16[256,512]{1,0:T(8,128)(2,1)S(1)}, u32[]{:S(2)}, u32[]{:S(2)}) %collective-permute-start.27) | collective-permute-done | bytes 262176 | tf_op jit(solution)/shard_map/ppermute | solution.py:66
  115.6 0.5 collective-permute-start.26
  116.1 1.2 collective-permute-done.23.refs_2_
  117.5 1.3 collective-permute-done.24.refs_3_
  118.9 0.6 copy-done.28
  119.8 4.3 %cache_rows.3 = bf16[16,80,128]{2,1,0:T(8,128)(2,1)} custom-call(s32[11]{0:T(128)} %stack.47.place.place_ref.token_ref, s32[2]{0:T(128)} %lengths_ref.3, s32[8]{0:T(128)} %owner_ref.3, bf16[16,80,128]{2,1,0:T(8,128)(2,1)} %cache_rows.2.token_ref, bf16[16,2,320,256]{3,2,1,0:T(8,128)(2,1)} %get-tuple-element.61.both.refs_0_, ...), custom_call_target="tpu_custom_call" | custom-call | flops 1000 | bytes 1000 | tf_op jit(solution)/shard_map/cache_rows/pallas_call | solution.py:315
  124.1 4.7 %all-to-all-start.1 = ((bf16[16,80,128]{2,1,0:T(8,128)(2,1)}), bf16[16,80,128]{2,1,0:T(8,128)(2,1)S(1)}, u32[]{:S(2)}, u32[]{:S(2)}) async-start(bf16[16,80,128]{2,1,0:T(8,128)(2,1)} %cache_rows.3), calls=%async_computation.1 | async-start | bytes 655360 | tf_op jit(solution)/shard_map/all_to_all | solution.py:467
  129.1 0.4 collective-permute-start.30
  129.5 0.8 collective-permute-done.30
  130.6 0.4 collective-permute-start.31
  131.0 0.8 collective-permute-done.31
  132.0 7.9 %all-to-all-done.1 = bf16[16,80,128]{2,1,0:T(8,128)(2,1)S(1)} async-done(((bf16[16,80,128]{2,1,0:T(8,128)(2,1)}), bf16[16,80,128]{2,1,0:T(8,128)(2,1)S(1)}, u32[]{:S(2)}, u32[]{:S(2)}) %all-to-all-start.1) | async-done | bytes 327712 | tf_op jit(solution)/shard_map/all_to_all | solution.py:467
  140.3 0.9 maximum_bitcast_fusion
  141.4 0.6 fusion.7
  (118 shorter events, 4.3 us)
Async XLA Ops:
  0.6 131.2 %copy-start = (bf16[8,4,128]{2,1,0:T(4,128)(2,1)S(1)}, bf16[8,4,128]{2,1,0:T(4,128)(2,1)}, u32[]{:S(2)}) copy-start(bf16[8,4,128]{2,1,0:T(4,128)(2,1)} %param.17) | copy-start | bytes 24580
  0.6 17.1 %copy-start.33 = (f32[64]{0:T(128)S(1)}, f32[64]{0:T(128)}, u32[]{:S(2)}) copy-start(f32[64]{0:T(128)} %constant.90.clone) | copy-start | bytes 772
  0.7 11.2 %copy-start.32 = (s32[8]{0:T(128)S(1)}, s32[8]{0:T(128)}, u32[]{:S(2)}) copy-start(s32[8]{0:T(128)} %owner_ref.3) | copy-start | bytes 100
  0.7 15.1 %copy-start.31 = (s32[2]{0:T(128)S(1)}, s32[2]{0:T(128)}, u32[]{:S(2)}) copy-start(s32[2]{0:T(128)} %lengths_ref.3) | copy-start | bytes 28
  0.7 21.3 %collective-permute-start.3 = (bf16[320,8192]{1,0:T(8,128)(2,1)}, bf16[320,8192]{1,0:T(8,128)(2,1)}, u32[]{:S(2)}, u32[]{:S(2)}) collective-permute-start(bf16[320,8192]{1,0:T(8,128)(2,1)} %bitcast.49), channel_id=1, source_target_pairs={{0,1},{1,0},{2,3},{3,2},{4,5},{5,4},{6,7},{7,6},{8,9},{9,8},{10,11... | collective-permute-start | bytes 15728648 | tf_op jit(solution)/shard_map/ppermute | solution.py:66
  4.3 15.4 %collective-permute-start = (bf16[256,1024]{1,0:T(8,128)(2,1)}, bf16[256,1024]{1,0:T(8,128)(2,1)S(1)}, u32[]{:S(2)}, u32[]{:S(2)}) collective-permute-start(bf16[256,1024]{1,0:T(8,128)(2,1)} %weight_half.2.refs_0_), channel_id=1, source_target_pairs={{0,4},{1,5},{2,6},{3,7},{4,0},{5,1},{6,2},{7,3},{8,12},{9,13},{10,... | collective-permute-start | bytes 1572872 | tf_op jit(solution)/shard_map/ppermute | solution.py:66
  7.1 12.7 %collective-permute-start.1 = (bf16[256,1024]{1,0:T(8,128)(2,1)}, bf16[256,1024]{1,0:T(8,128)(2,1)S(1)}, u32[]{:S(2)}, u32[]{:S(2)}) collective-permute-start(bf16[256,1024]{1,0:T(8,128)(2,1)} %weight_half.2.refs_0_), channel_id=1, source_target_pairs={{4,8},{5,9},{6,10},{7,11},{8,4},{9,5},{10,6},{11,7},{20,24},{21,25... | collective-permute-start | bytes 1572872 | tf_op jit(solution)/shard_map/ppermute | solution.py:66
  7.7 14.3 %collective-permute-start.2 = (bf16[256,1024]{1,0:T(8,128)(2,1)}, bf16[256,1024]{1,0:T(8,128)(2,1)S(1)}, u32[]{:S(2)}, u32[]{:S(2)}) collective-permute-start(bf16[256,1024]{1,0:T(8,128)(2,1)} %weight_half.2.refs_0_), channel_id=1, source_target_pairs={{0,2},{1,3},{2,0},{3,1},{4,6},{5,7},{6,4},{7,5},{8,10},{9,11},{10,... | collective-permute-start | bytes 1572872 | tf_op jit(solution)/shard_map/ppermute | solution.py:66
  19.8 16.7 %copy-start.9 = (bf16[256,1024]{1,0:T(8,128)(2,1)}, bf16[256,1024]{1,0:T(8,128)(2,1)S(1)}, u32[]{:S(2)}) copy-start(bf16[256,1024]{1,0:T(8,128)(2,1)S(1)} %collective-permute-done.refs_4_) | copy-start | bytes 1572868
  22.0 14.5 %copy-start.10 = (bf16[256,1024]{1,0:T(8,128)(2,1)}, bf16[256,1024]{1,0:T(8,128)(2,1)S(1)}, u32[]{:S(2)}) copy-start(bf16[256,1024]{1,0:T(8,128)(2,1)S(1)} %collective-permute-done.2.refs_2_) | copy-start | bytes 1572868
  22.0 14.5 %collective-permute-start.4 = (bf16[256,1024]{1,0:T(8,128)(2,1)S(1)}, bf16[256,1024]{1,0:T(8,128)(2,1)S(1)}, u32[]{:S(2)}, u32[]{:S(2)}) collective-permute-start(bf16[256,1024]{1,0:T(8,128)(2,1)S(1)} %collective-permute-done.2.refs_2_), channel_id=1, source_target_pairs={{0,16},{1,17},{2,18},{3,19},{4,20},{5,21},{6,22},{7,23},{8,24},{9,... | collective-permute-start | bytes 1572872 | tf_op jit(solution)/shard_map/ppermute | solution.py:66
  23.5 16.3 %collective-permute-start.5 = (bf16[256,1024]{1,0:T(8,128)(2,1)S(1)}, bf16[256,1024]{1,0:T(8,128)(2,1)}, u32[]{:S(2)}, u32[]{:S(2)}) collective-permute-start(bf16[256,1024]{1,0:T(8,128)(2,1)S(1)} %collective-permute-done.1), channel_id=1, source_target_pairs={{4,0},{5,1},{6,2},{7,3},{8,12},{9,13},{10,14},{11,15},{20,16},{21,... | collective-permute-start | bytes 1572872 | tf_op jit(solution)/shard_map/ppermute | solution.py:66
  24.8 15.0 %collective-permute-start.6 = (bf16[256,1024]{1,0:T(8,128)(2,1)S(1)}, bf16[256,1024]{1,0:T(8,128)(2,1)S(1)}, u32[]{:S(2)}, u32[]{:S(2)}) collective-permute-start(bf16[256,1024]{1,0:T(8,128)(2,1)S(1)} %collective-permute-done.refs_4_), channel_id=1, source_target_pairs={{4,8},{5,9},{6,10},{7,11},{8,4},{9,5},{10,6},{11,7},{20,24},{21,25... | collective-permute-start | bytes 1572872 | tf_op jit(solution)/shard_map/ppermute | solution.py:66
  25.5 14.3 %collective-permute-start.7 = (bf16[256,1024]{1,0:T(8,128)(2,1)S(1)}, bf16[256,1024]{1,0:T(8,128)(2,1)S(1)}, u32[]{:S(2)}, u32[]{:S(2)}) collective-permute-start(bf16[256,1024]{1,0:T(8,128)(2,1)S(1)} %collective-permute-done.refs_4_), channel_id=1, source_target_pairs={{0,2},{1,3},{2,0},{3,1},{4,6},{5,7},{6,4},{7,5},{8,10},{9,11},{10,... | collective-permute-start | bytes 1572872 | tf_op jit(solution)/shard_map/ppermute | solution.py:66
  36.5 8.1 %copy-start.4 = (bf16[256,1024]{1,0:T(8,128)(2,1)}, bf16[256,1024]{1,0:T(8,128)(2,1)S(1)}, u32[]{:S(2)}) copy-start(bf16[256,1024]{1,0:T(8,128)(2,1)S(1)} %collective-permute-done.4.refs_3_) | copy-start | bytes 1572868
  39.8 4.8 %copy-start.13 = (bf16[256,1024]{1,0:T(8,128)(2,1)}, bf16[256,1024]{1,0:T(8,128)(2,1)S(1)}, u32[]{:S(2)}) copy-start(bf16[256,1024]{1,0:T(8,128)(2,1)S(1)} %collective-permute-done.7.refs_5_) | copy-start | bytes 1572868
  41.1 9.3 %copy-start.2 = (bf16[256,1024]{1,0:T(8,128)(2,1)}, bf16[256,1024]{1,0:T(8,128)(2,1)S(1)}, u32[]{:S(2)}) copy-start(bf16[256,1024]{1,0:T(8,128)(2,1)S(1)} %broadcast_select_fusion.1.refs_0_) | copy-start | bytes 1572868
  41.1 17.0 %copy-start.1 = (bf16[256,1024]{1,0:T(8,128)(2,1)S(1)}, bf16[256,1024]{1,0:T(8,128)(2,1)}, u32[]{:S(2)}) copy-start(bf16[256,1024]{1,0:T(8,128)(2,1)} %weight_half.3.refs_1_) | copy-start | bytes 1572868
  41.1 12.0 %collective-permute-start.10 = (bf16[256,1024]{1,0:T(8,128)(2,1)S(1)}, bf16[256,1024]{1,0:T(8,128)(2,1)S(1)}, u32[]{:S(2)}, u32[]{:S(2)}) collective-permute-start(bf16[256,1024]{1,0:T(8,128)(2,1)S(1)} %broadcast_select_fusion.1.refs_0_), channel_id=1, source_target_pairs={{0,16},{1,17},{2,18},{3,19},{4,20},{5,21},{6,22},{7,23},{8,24},{9,... | collective-permute-start | bytes 1572872 | tf_op jit(solution)/shard_map/ppermute | solution.py:66
  41.7 11.6 %collective-permute-start.9 = (bf16[256,1024]{1,0:T(8,128)(2,1)S(1)}, bf16[256,1024]{1,0:T(8,128)(2,1)S(1)}, u32[]{:S(2)}, u32[]{:S(2)}) collective-permute-start(bf16[256,1024]{1,0:T(8,128)(2,1)S(1)} %broadcast_select_fusion.1.refs_0_), channel_id=1, source_target_pairs={{0,2},{1,3},{2,0},{3,1},{4,6},{5,7},{6,4},{7,5},{8,10},{9,11},{10,... | collective-permute-start | bytes 1572872 | tf_op jit(solution)/shard_map/ppermute | solution.py:66
  43.3 14.9 %collective-permute-start.8 = (bf16[256,1024]{1,0:T(8,128)(2,1)S(1)}, bf16[256,1024]{1,0:T(8,128)(2,1)S(1)}, u32[]{:S(2)}, u32[]{:S(2)}) collective-permute-start(bf16[256,1024]{1,0:T(8,128)(2,1)S(1)} %collective-permute-done.6), channel_id=1, source_target_pairs={{4,0},{5,1},{6,2},{7,3},{8,12},{9,13},{10,14},{11,15},{20,16},{21,... | collective-permute-start | bytes 1572872 | tf_op jit(solution)/shard_map/ppermute | solution.py:66
  53.1 9.2 %copy-start.12 = (bf16[256,1024]{1,0:T(8,128)(2,1)}, bf16[256,1024]{1,0:T(8,128)(2,1)S(1)}, u32[]{:S(2)}) copy-start(bf16[256,1024]{1,0:T(8,128)(2,1)S(1)} %collective-permute-done.10.refs_1_) | copy-start | bytes 1572868
  53.4 9.0 %copy-start.3 = (bf16[256,1024]{1,0:T(8,128)(2,1)}, bf16[256,1024]{1,0:T(8,128)(2,1)S(1)}, u32[]{:S(2)}) copy-start(bf16[256,1024]{1,0:T(8,128)(2,1)S(1)} %collective-permute-done.9.refs_2_) | copy-start | bytes 1572868
  58.1 11.5 %collective-permute-start.11 = (bf16[256,1024]{1,0:T(8,128)(2,1)S(1)}, bf16[256,1024]{1,0:T(8,128)(2,1)S(1)}, u32[]{:S(2)}, u32[]{:S(2)}) collective-permute-start(bf16[256,1024]{1,0:T(8,128)(2,1)S(1)} %copy-done.1), channel_id=1, source_target_pairs={{0,4},{1,5},{2,6},{3,7},{4,0},{5,1},{6,2},{7,3},{8,12},{9,13},{10,... | collective-permute-start | bytes 1572872 | tf_op jit(solution)/shard_map/ppermute | solution.py:66
  58.2 4.1 %copy-start.5 = (bf16[256,512]{1,0:T(8,128)(2,1)}, bf16[256,512]{1,0:T(8,128)(2,1)S(1)}, u32[]{:S(2)}) copy-start(bf16[256,512]{1,0:T(8,128)(2,1)S(1)} %get-tuple-element.76.refs_4_) | copy-start | bytes 786436
  58.2 4.1 %copy-start.6 = (bf16[256,512]{1,0:T(8,128)(2,1)}, bf16[256,512]{1,0:T(8,128)(2,1)S(1)}, u32[]{:S(2)}) copy-start(bf16[256,512]{1,0:T(8,128)(2,1)S(1)} %get-tuple-element.77.refs_3_) | copy-start | bytes 786436
  58.3 11.3 %collective-permute-start.12 = (bf16[256,512]{1,0:T(8,128)(2,1)S(1)}, bf16[256,512]{1,0:T(8,128)(2,1)S(1)}, u32[]{:S(2)}, u32[]{:S(2)}) collective-permute-start(bf16[256,512]{1,0:T(8,128)(2,1)S(1)} %get-tuple-element.77.refs_3_), channel_id=1, source_target_pairs={{0,16},{1,17},{2,18},{3,19},{4,20},{5,21},{6,22},{7,23},{8,24},{9,... | collective-permute-start | bytes 786440 | tf_op jit(solution)/shard_map/ppermute | solution.py:66
  59.8 9.7 %collective-permute-start.13 = (bf16[256,512]{1,0:T(8,128)(2,1)S(1)}, bf16[256,512]{1,0:T(8,128)(2,1)S(1)}, u32[]{:S(2)}, u32[]{:S(2)}) collective-permute-start(bf16[256,512]{1,0:T(8,128)(2,1)S(1)} %get-tuple-element.76.refs_4_), channel_id=1, source_target_pairs={{0,16},{1,17},{2,18},{3,19},{4,20},{5,21},{6,22},{7,23},{8,24},{9,... | collective-permute-start | bytes 786440 | tf_op jit(solution)/shard_map/ppermute | solution.py:66
  60.3 9.2 %collective-permute-start.14 = (bf16[256,512]{1,0:T(8,128)(2,1)S(1)}, bf16[256,512]{1,0:T(8,128)(2,1)S(1)}, u32[]{:S(2)}, u32[]{:S(2)}) collective-permute-start(bf16[256,512]{1,0:T(8,128)(2,1)S(1)} %get-tuple-element.77.refs_3_), channel_id=1, source_target_pairs={{0,2},{1,3},{2,0},{3,1},{4,6},{5,7},{6,4},{7,5},{8,10},{9,11},{10,... | collective-permute-start | bytes 786440 | tf_op jit(solution)/shard_map/ppermute | solution.py:66
  60.9 8.7 %collective-permute-start.15 = (bf16[256,512]{1,0:T(8,128)(2,1)S(1)}, bf16[256,512]{1,0:T(8,128)(2,1)S(1)}, u32[]{:S(2)}, u32[]{:S(2)}) collective-permute-start(bf16[256,512]{1,0:T(8,128)(2,1)S(1)} %get-tuple-element.76.refs_4_), channel_id=1, source_target_pairs={{0,2},{1,3},{2,0},{3,1},{4,6},{5,7},{6,4},{7,5},{8,10},{9,11},{10,... | collective-permute-start | bytes 786440 | tf_op jit(solution)/shard_map/ppermute | solution.py:66
  69.5 6.5 %copy-start.16 = (bf16[256,512]{1,0:T(8,128)(2,1)}, bf16[256,512]{1,0:T(8,128)(2,1)S(1)}, u32[]{:S(2)}) copy-start(bf16[256,512]{1,0:T(8,128)(2,1)S(1)} %collective-permute-done.12.refs_1_) | copy-start | bytes 786436
  69.6 6.5 %copy-start.14 = (bf16[256,512]{1,0:T(8,128)(2,1)}, bf16[256,512]{1,0:T(8,128)(2,1)S(1)}, u32[]{:S(2)}) copy-start(bf16[256,512]{1,0:T(8,128)(2,1)S(1)} %collective-permute-done.13.refs_2_) | copy-start | bytes 786436
  69.6 6.5 %copy-start.21 = (bf16[256,512]{1,0:T(8,128)(2,1)}, bf16[256,512]{1,0:T(8,128)(2,1)S(1)}, u32[]{:S(2)}) copy-start(bf16[256,512]{1,0:T(8,128)(2,1)S(1)} %collective-permute-done.14.refs_3_) | copy-start | bytes 786436
  69.6 6.5 %copy-start.22 = (bf16[256,512]{1,0:T(8,128)(2,1)}, bf16[256,512]{1,0:T(8,128)(2,1)S(1)}, u32[]{:S(2)}) copy-start(bf16[256,512]{1,0:T(8,128)(2,1)S(1)} %collective-permute-done.15.refs_4_) | copy-start | bytes 786436
  69.6 6.5 %copy-start.11 = (bf16[256,1024]{1,0:T(8,128)(2,1)}, bf16[256,1024]{1,0:T(8,128)(2,1)S(1)}, u32[]{:S(2)}) copy-start(bf16[256,1024]{1,0:T(8,128)(2,1)S(1)} %collective-permute-done.11.refs_0_) | copy-start | bytes 1572868
  69.6 6.4 %collective-permute-start.18 = (bf16[256,512]{1,0:T(8,128)(2,1)S(1)}, bf16[256,512]{1,0:T(8,128)(2,1)S(1)}, u32[]{:S(2)}, u32[]{:S(2)}) collective-permute-start(bf16[256,512]{1,0:T(8,128)(2,1)S(1)} %get-tuple-element.59), channel_id=1, source_target_pairs={{0,16},{1,17},{2,18},{3,19},{4,20},{5,21},{6,22},{7,23},{8,24},{9,... | collective-permute-start | bytes 786440 | tf_op jit(solution)/shard_map/ppermute | solution.py:66
  76.1 8.1 %copy-start.17 = (bf16[256,512]{1,0:T(8,128)(2,1)}, bf16[256,512]{1,0:T(8,128)(2,1)S(1)}, u32[]{:S(2)}) copy-start(bf16[256,512]{1,0:T(8,128)(2,1)S(1)} %collective-permute-done.18.refs_4_) | copy-start | bytes 786436
  81.5 10.9 %collective-permute-start.22 = (f32[320,512]{1,0:T(8,128)}, f32[320,512]{1,0:T(8,128)S(1)}, u32[]{:S(2)}, u32[]{:S(2)}) collective-permute-start(f32[320,512]{1,0:T(8,128)} %get-tuple-element.67), channel_id=1, source_target_pairs={{0,1},{1,0},{2,3},{3,2},{4,5},{5,4},{6,7},{7,6},{8,9},{9,8},{10,11... | collective-permute-start | bytes 1966088 | tf_op jit(solution)/shard_map/ppermute | solution.py:66
  81.6 8.9 %collective-permute-start.20 = (bf16[256,512]{1,0:T(8,128)(2,1)}, bf16[256,512]{1,0:T(8,128)(2,1)S(1)}, u32[]{:S(2)}, u32[]{:S(2)}) collective-permute-start(bf16[256,512]{1,0:T(8,128)(2,1)} %copy-done.16), channel_id=1, source_target_pairs={{0,2},{1,3},{2,0},{3,1},{4,6},{5,7},{6,4},{7,5},{8,10},{9,11},{10,... | collective-permute-start | bytes 786440 | tf_op jit(solution)/shard_map/ppermute | solution.py:66
  82.2 8.6 %collective-permute-start.16 = (bf16[256,512]{1,0:T(8,128)(2,1)S(1)}, bf16[256,512]{1,0:T(8,128)(2,1)S(1)}, u32[]{:S(2)}, u32[]{:S(2)}) collective-permute-start(bf16[256,512]{1,0:T(8,128)(2,1)S(1)} %get-tuple-element.58), channel_id=1, source_target_pairs={{0,4},{1,5},{2,6},{3,7},{4,0},{5,1},{6,2},{7,3},{8,12},{9,13},{10,... | collective-permute-start | bytes 786440 | tf_op jit(solution)/shard_map/ppermute | solution.py:66
  84.2 7.9 %collective-permute-start.19 = (bf16[256,512]{1,0:T(8,128)(2,1)S(1)}, bf16[256,512]{1,0:T(8,128)(2,1)S(1)}, u32[]{:S(2)}, u32[]{:S(2)}) collective-permute-start(bf16[256,512]{1,0:T(8,128)(2,1)S(1)} %collective-permute-done.18.refs_4_), channel_id=1, source_target_pairs={{0,1},{1,0},{2,3},{3,2},{4,5},{5,4},{6,7},{7,6},{8,9},{9,8},{10,11... | collective-permute-start | bytes 786440 | tf_op jit(solution)/shard_map/ppermute | solution.py:66
  90.5 1.9 %copy-start.24 = (bf16[256,512]{1,0:T(8,128)(2,1)}, bf16[256,512]{1,0:T(8,128)(2,1)S(1)}, u32[]{:S(2)}) copy-start(bf16[256,512]{1,0:T(8,128)(2,1)S(1)} %collective-permute-done.20.refs_6_) | copy-start | bytes 786436
  90.5 1.5 %collective-permute-start.21 = (bf16[256,512]{1,0:T(8,128)(2,1)S(1)}, bf16[256,512]{1,0:T(8,128)(2,1)S(1)}, u32[]{:S(2)}, u32[]{:S(2)}) collective-permute-start(bf16[256,512]{1,0:T(8,128)(2,1)S(1)} %collective-permute-done.20.refs_6_), channel_id=1, source_target_pairs={{0,1},{1,0},{2,3},{3,2},{4,5},{5,4},{6,7},{7,6},{8,9},{9,8},{10,11... | collective-permute-start | bytes 786440 | tf_op jit(solution)/shard_map/ppermute | solution.py:66
  90.8 1.6 %copy-start.25 = (bf16[256,512]{1,0:T(8,128)(2,1)}, bf16[256,512]{1,0:T(8,128)(2,1)S(1)}, u32[]{:S(2)}) copy-start(bf16[256,512]{1,0:T(8,128)(2,1)S(1)} %collective-permute-done.16.refs_2_) | copy-start | bytes 786436
  90.8 1.6 %collective-permute-start.17 = (bf16[256,512]{1,0:T(8,128)(2,1)S(1)}, bf16[256,512]{1,0:T(8,128)(2,1)S(1)}, u32[]{:S(2)}, u32[]{:S(2)}) collective-permute-start(bf16[256,512]{1,0:T(8,128)(2,1)S(1)} %collective-permute-done.16.refs_2_), channel_id=1, source_target_pairs={{0,1},{1,0},{2,3},{3,2},{4,5},{5,4},{6,7},{7,6},{8,9},{9,8},{10,11... | collective-permute-start | bytes 786440 | tf_op jit(solution)/shard_map/ppermute | solution.py:66
  93.4 4.8 %copy-start.34 = (f32[320,512]{1,0:T(8,128)S(1)}, f32[320,512]{1,0:T(8,128)}, u32[]{:S(2)}) copy-start(f32[320,512]{1,0:T(8,128)} %get-tuple-element.73) | copy-start | bytes 1966084
  93.4 9.9 %copy-start.15 = (bf16[256,512]{1,0:T(8,128)(2,1)S(1)}, bf16[256,512]{1,0:T(8,128)(2,1)}, u32[]{:S(2)}) copy-start(bf16[256,512]{1,0:T(8,128)(2,1)} %copy-done.14) | copy-start | bytes 786436
  98.2 20.6 %collective-permute-start.29 = (f32[320,512]{1,0:T(8,128)S(1)}, f32[320,512]{1,0:T(8,128)S(1)}, u32[]{:S(2)}, u32[]{:S(2)}) collective-permute-start(f32[320,512]{1,0:T(8,128)S(1)} %copy-done.34), channel_id=1, source_target_pairs={{0,1},{1,0},{2,3},{3,2},{4,5},{5,4},{6,7},{7,6},{8,9},{9,8},{10,11... | collective-permute-start | bytes 1966088 | tf_op jit(solution)/shard_map/ppermute | solution.py:66
  98.4 25.7 %all-to-all-start = ((bf16[16,80,128]{2,1,0:T(8,128)(2,1)}), bf16[16,80,128]{2,1,0:T(8,128)(2,1)S(1)}, u32[]{:S(2)}, u32[]{:S(2)}) async-start(bf16[16,80,128]{2,1,0:T(8,128)(2,1)} %cache_rows.2.token_ref), calls=%async_computation | async-start | bytes 655360 | tf_op jit(solution)/shard_map/all_to_all | solution.py:467
  103.3 12.2 %collective-permute-start.27 = (bf16[256,512]{1,0:T(8,128)(2,1)S(1)}, bf16[256,512]{1,0:T(8,128)(2,1)S(1)}, u32[]{:S(2)}, u32[]{:S(2)}) collective-permute-start(bf16[256,512]{1,0:T(8,128)(2,1)S(1)} %copy-done.15), channel_id=1, source_target_pairs={{0,2},{1,3},{2,0},{3,1},{4,6},{5,7},{6,4},{7,5},{8,10},{9,11},{10,... | collective-permute-start | bytes 786440 | tf_op jit(solution)/shard_map/ppermute | solution.py:66
  105.3 10.3 %collective-permute-start.25 = (bf16[256,512]{1,0:T(8,128)(2,1)S(1)}, bf16[256,512]{1,0:T(8,128)(2,1)S(1)}, u32[]{:S(2)}, u32[]{:S(2)}) collective-permute-start(bf16[256,512]{1,0:T(8,128)(2,1)S(1)} %get-tuple-element.69), channel_id=1, source_target_pairs={{0,16},{1,17},{2,18},{3,19},{4,20},{5,21},{6,22},{7,23},{8,24},{9,... | collective-permute-start | bytes 786440 | tf_op jit(solution)/shard_map/ppermute | solution.py:66
  106.8 10.5 %collective-permute-start.23 = (bf16[256,512]{1,0:T(8,128)(2,1)S(1)}, bf16[256,512]{1,0:T(8,128)(2,1)S(1)}, u32[]{:S(2)}, u32[]{:S(2)}) collective-permute-start(bf16[256,512]{1,0:T(8,128)(2,1)S(1)} %get-tuple-element.68), channel_id=1, source_target_pairs={{0,4},{1,5},{2,6},{3,7},{4,0},{5,1},{6,2},{7,3},{8,12},{9,13},{10,... | collective-permute-start | bytes 786440 | tf_op jit(solution)/shard_map/ppermute | solution.py:66
  115.5 3.3 %copy-start.18 = (bf16[256,512]{1,0:T(8,128)(2,1)}, bf16[256,512]{1,0:T(8,128)(2,1)S(1)}, u32[]{:S(2)}) copy-start(bf16[256,512]{1,0:T(8,128)(2,1)S(1)} %collective-permute-done.27.refs_6_) | copy-start | bytes 786436
  115.5 1.9 %collective-permute-start.28 = (bf16[256,512]{1,0:T(8,128)(2,1)S(1)}, bf16[256,512]{1,0:T(8,128)(2,1)S(1)}, u32[]{:S(2)}, u32[]{:S(2)}) collective-permute-start(bf16[256,512]{1,0:T(8,128)(2,1)S(1)} %collective-permute-done.27.refs_6_), channel_id=1, source_target_pairs={{0,1},{1,0},{2,3},{3,2},{4,5},{5,4},{6,7},{7,6},{8,9},{9,8},{10,11... | collective-permute-start | bytes 786440 | tf_op jit(solution)/shard_map/ppermute | solution.py:66
  115.5 3.3 %copy-start.19 = (bf16[256,512]{1,0:T(8,128)(2,1)}, bf16[256,512]{1,0:T(8,128)(2,1)S(1)}, u32[]{:S(2)}) copy-start(bf16[256,512]{1,0:T(8,128)(2,1)S(1)} %collective-permute-done.25.refs_4_) | copy-start | bytes 786436
  115.6 1.9 %collective-permute-start.26 = (bf16[256,512]{1,0:T(8,128)(2,1)S(1)}, bf16[256,512]{1,0:T(8,128)(2,1)S(1)}, u32[]{:S(2)}, u32[]{:S(2)}) collective-permute-start(bf16[256,512]{1,0:T(8,128)(2,1)S(1)} %collective-permute-done.25.refs_4_), channel_id=1, source_target_pairs={{0,1},{1,0},{2,3},{3,2},{4,5},{5,4},{6,7},{7,6},{8,9},{9,8},{10,11... | collective-permute-start | bytes 786440 | tf_op jit(solution)/shard_map/ppermute | solution.py:66
  117.3 1.6 %copy-start.20 = (bf16[256,512]{1,0:T(8,128)(2,1)}, bf16[256,512]{1,0:T(8,128)(2,1)S(1)}, u32[]{:S(2)}) copy-start(bf16[256,512]{1,0:T(8,128)(2,1)S(1)} %collective-permute-done.23.refs_2_) | copy-start | bytes 786436
  117.3 1.5 %collective-permute-start.24 = (bf16[256,512]{1,0:T(8,128)(2,1)S(1)}, bf16[256,512]{1,0:T(8,128)(2,1)S(1)}, u32[]{:S(2)}, u32[]{:S(2)}) collective-permute-start(bf16[256,512]{1,0:T(8,128)(2,1)S(1)} %collective-permute-done.23.refs_2_), channel_id=1, source_target_pairs={{0,1},{1,0},{2,3},{3,2},{4,5},{5,4},{6,7},{7,6},{8,9},{9,8},{10,11... | collective-permute-start | bytes 786440 | tf_op jit(solution)/shard_map/ppermute | solution.py:66
  117.5 1.4 copy-start.23
  117.5 1.4 copy-start.26
  124.1 15.8 %all-to-all-start.1 = ((bf16[16,80,128]{2,1,0:T(8,128)(2,1)}), bf16[16,80,128]{2,1,0:T(8,128)(2,1)S(1)}, u32[]{:S(2)}, u32[]{:S(2)}) async-start(bf16[16,80,128]{2,1,0:T(8,128)(2,1)} %cache_rows.3), calls=%async_computation.1 | async-start | bytes 655360 | tf_op jit(solution)/shard_map/all_to_all | solution.py:467
  129.1 1.3 collective-permute-start.30
  130.6 1.2 collective-permute-start.31
  140.1 1.2 collective-permute-start.32
  (6 other events, 4.8 us)

commit v10 on v9

--- a/solution.py
+++ b/solution.py
@@ -258,30 +258,78 @@
             pltpu.SemaphoreType.DMA((2 * parts,)),
         ],
         compiler_params=PARAMS,
-        cost_estimate=cost(1000, 1000),
+        cost_estimate=cost(1 << 36, 1000),
         name="add_product",
     )(place, both, *pieces_flat, *totals)
 
 
-def rows_kernel(plan, rotated, place, lengths, owner, both, kept, *refs):
+def own_product_kernel(plan, place, both, kept, *refs):
     count = len(plan)
-    pieces = refs[: 2 * count]
-    total_in, came_in = refs[2 * count : 2 * count + 2]
-    turn = refs[2 * count + 2 : 2 * count + 2 + 2 * rotated]
-    out, left, right, total, came, scratch, sems = refs[-7:]
-    rows, depth = kept.shape[1], kept.shape[2]
-    waits = [fetch(total_in, total, sems.at[0]), fetch(came_in, came, sems.at[1])]
-    sem = 2
+    pieces, sums_in = refs[: 2 * count], refs[2 * count : 2 * count + 2]
+    outs = refs[2 * count + 2 : 2 * count + 4]
+    left, right, total, came, sems = refs[-5:]
+    depth, columns = kept.shape[2], outs[0].shape[1]
+    waits = []
+    for k in range(2 * count):
+        index = half_index(place, *plan[k // 2])
+        source = kept.at[index] if k % 2 else both.at[index, 0]
+        area = pl.ds(k * depth, depth)
+        waits.append(fetch(source, left.at[:, area], sems.at[2 * k]))
+        waits.append(fetch(pieces[k], right.at[area], sems.at[2 * k + 1]))
+    waits.append(fetch(sums_in[0], total, sems.at[4 * count]))
+    waits.append(fetch(sums_in[1], came, sems.at[4 * count + 1]))
+    for copy in waits:
+        copy.wait()
+    for k, out in enumerate(outs):
+        area = slice(k * columns, (k + 1) * columns)
+        out[...] = (total[:, area] + came[:, area]) + jnp.dot(
+            left[...], right[:, area], preferred_element_type=jnp.float32
+        )
+
+
+def own_product(place, both, kept, pieces, sums):
+    _, rows, depth = kept.shape
+    columns = sums[0].shape[1]
+    count = len(pieces)
+    plan = [(entry, kind) for entry, kind, _, _ in pieces]
+    operands = [block for _, _, *blocks in pieces for block in blocks]
+    out = jax.ShapeDtypeStruct((rows, columns // 2), jnp.float32)
+    return pl.pallas_call(
+        functools.partial(own_product_kernel, plan),
+        in_specs=[SMEM_REF] + [ANY_REF] * (4 + 2 * count),
+        out_specs=[VMEM_REF] * 2,
+        out_shape=[out] * 2,
+        scratch_shapes=[
+            pltpu.VMEM((rows, 2 * count * depth), kept.dtype),
+            pltpu.VMEM((2 * count * depth, columns), kept.dtype),
+            pltpu.VMEM((rows, columns), jnp.float32),
+            pltpu.VMEM((rows, columns), jnp.float32),
+            pltpu.SemaphoreType.DMA((4 * count + 2,)),
+        ],
+        compiler_params=PARAMS,
+        cost_estimate=cost(1 << 36, 1000),
+        name="own_product",
+    )(place, both, kept, *operands, *sums)
+
+
+def rows_kernel(plan, part, rotated, place, lengths, owner, both, kept, *refs):
+    count = len(plan)
+    pieces, refs = refs[: 2 * count], refs[2 * count :]
+    turn = refs[1 : 1 + 2 * rotated]
+    out, left, right, total, scratch, sems = refs[-6:]
+    depth, columns = kept.shape[2], total.shape[1]
+    waits, sem = [], 0
     for k in range(2 * count):
         index = half_index(place, *plan[k // 2])
         source = kept.at[index] if k % 2 else both.at[index, 0]
         area = pl.ds(k * depth, depth)
         waits.append(fetch(source, left.at[:, area], sems.at[sem]))
-        waits.append(fetch(pieces[k], right.at[area], sems.at[sem + 1]))
+        piece = pieces[k].at[:, pl.ds(part * columns, columns)]
+        waits.append(fetch(piece, right.at[area], sems.at[sem + 1]))
         sem += 2
+    waits.append(fetch(refs[0], total, sems.at[sem]))
     for copy in waits:
         copy.wait()
-    total[...] += came[...]
     total[...] += jnp.dot(left[...], right[...], preferred_element_type=jnp.float32)
     count_requests, count_rows = lengths.shape[0], scratch.shape[0]
     index = place[2] * count_rows + lax.broadcasted_iota(jnp.int32, scratch.shape, 0)
@@ -301,7 +349,7 @@
                 out[peer * 2 + b] = picked.astype(jnp.bfloat16)
 
 
-def outgoing_rows(place, lengths, owner, both, kept, plan, pieces, total, came, turn, token):
+def outgoing_rows(place, lengths, owner, both, kept, plan, pieces, part, total, turn, token):
     _, rows, depth = kept.shape
     columns = total.shape[1]
     count = len(plan)
@@ -309,9 +357,9 @@
     out = jax.ShapeDtypeStruct((owner.shape[0] * 2, count_rows // 2, HEAD_SIZE), jnp.bfloat16)
 
     def kernel(place_ref, lengths_ref, owner_ref, token_ref, *refs):
-        rows_kernel(plan, bool(turn), place_ref, lengths_ref, owner_ref, *refs)
-
-    operands = [both, kept, *pieces, total, came]
+        rows_kernel(plan, part, bool(turn), place_ref, lengths_ref, owner_ref, *refs)
+
+    operands = [both, kept, *pieces, total]
     return pl.pallas_call(
         kernel,
         in_specs=[SMEM_REF] * 3
@@ -323,9 +371,8 @@
             pltpu.VMEM((rows, 2 * count * depth), kept.dtype),
             pltpu.VMEM((2 * count * depth, columns), kept.dtype),
             pltpu.VMEM((rows, columns), jnp.float32),
-            pltpu.VMEM((rows, columns), jnp.float32),
             pltpu.VMEM((count_rows, HEAD_SIZE), jnp.float32),
-            pltpu.SemaphoreType.DMA((2 + 4 * count,)),
+            pltpu.SemaphoreType.DMA((4 * count + 1,)),
         ],
         compiler_params=PARAMS,
         cost_estimate=cost(1000, 1000),
@@ -410,9 +457,6 @@
         )
         columns = key_weight.shape[1]
 
-        def parts_of(block):
-            return [block[:, k * columns : (k + 1) * columns] for k in range(2)]
-
         sent = weight_half(place, 0, key_weight, value_weight)
         near = moved(sent, to_pair)
         middle = moved(sent, to_middle)
@@ -432,36 +476,36 @@
         block_xb = moved(block_b, to_group)
         pieces = [(HERE, 0, sent), (HERE, 1, rest), (THERE, 0, across), (THERE, 1, across_x)]
         pieces += [(HERE + 1, 0, near), (THERE + 1, 0, near_y)]
-        totals = product(place, after(both, *came), pieces, (), 3, 2 * columns, 2)
-        ends_x = parts_of(after(across_x, *came))
-        came = (end_c, block_yb, block_xb, totals[0], *ends_x)
+        totals = product(place, after(both, *came), pieces, (), 3, 2 * columns, 1)
+        came = (end_c, block_yb, block_xb, totals[0])
         near_rest = moved(after(rest, *came), to_pair)
-        block_c = parts_of(jnp.where(is_end, after(end_c, *came), middle_c))
-        block_xc = [moved(block_c[0], to_group)]
-        block_yc = [moved(block_c[0], to_row)]
-        block_xc.append(moved(block_c[1], to_group))
-        block_yc.append(moved(block_c[1], to_row))
+        block_c = jnp.where(is_end, after(end_c, *came), middle_c)
+        block_xc = moved(block_c, to_group)
+        block_yc = moved(block_c, to_row)
         pieces = [(HERE + 2, 0, block_b), (HERE + 2, 1, block_xb)]
-        pieces += [(THERE + 2, 0, block_yb), (HERE + 3, 0, *block_c)]
-        totals = product(place, after(both, *came), pieces, totals, 4, 2 * columns, 2)
-        ends_yb = parts_of(after(block_yb, *came))
-        came = (near_rest, *block_xc, *block_yc, totals[0], *ends_yb)
-        ends = []
-        for k in range(2):
-            near_xy = moved(after(ends_x[k], *came), to_pair)
-            ends.append([near_xy, moved(after(ends_yb[k], *came), to_group)])
-            ends[k].append(moved(after(block_xc[k], *came), to_row))
-        pieces = [(HERE + 1, 1, near_rest), (HERE + 3, 1, *block_xc), (THERE + 3, 0, *block_yc)]
-        totals = product(place, after(both, ends[0][1]), pieces, totals, 3, 2 * columns, 2)
+        pieces += [(THERE + 2, 0, block_yb), (HERE + 3, 0, block_c)]
+        total, given = product(place, after(both, *came), pieces, totals, 4, 2 * columns, 1)
+        came = (near_rest, block_xc, block_yc, total)
+        ends = [moved(after(across_x, *came), to_pair), moved(after(block_yb, *came), to_group)]
+        ends.append(moved(after(block_xc, *came), to_row))
+        pieces = [(HERE + 1, 1, near_rest), (HERE + 3, 1, block_xc), (THERE + 3, 0, block_yc)]
+        pieces = [
+            (entry, kind, after(block, *came), moved(after(block, *came), to_core))
+            for entry, kind, block in pieces
+        ]
+        given = moved(after(given, *came), to_core)
+        sums = own_product(place, both, kept, pieces, (total, given))
+        came = (*ends, *sums)
+        pieces = []
+        for end in ends:
+            end = after(end, *came)
+            pieces += [end, moved(end, to_core)]
         plan = [(THERE + 1, 1), (THERE + 2, 1), (THERE + 3, 1)]
         caches = []
         token = place
         for k, turned in enumerate((turn, ())):
-            given = moved(after(totals[2 * k + 1], token), to_core)
-            swapped_ends = [moved(end, to_core) for end in ends[k]]
-            pieces = [piece for pair in zip(ends[k], swapped_ends) for piece in pair]
             outgoing = outgoing_rows(
-                place, lengths, owner, both, kept, plan, pieces, totals[2 * k], given, turned, token
+                place, lengths, owner, both, kept, plan, pieces, k, sums[k], turned, token
             )
             caches.append(
                 lax.all_to_all(outgoing, "seq", split_axis=0, concat_axis=1, tiled=True)[0]

time: 143 us -> 129 us (0.902)
  starting transfers between devices: 38.7 us -> 28.4 us
  waiting for transfers between devices: 44.4 us -> 42 us
  local copies, waits for them, and re-layouts: 4.7 us -> 2.79 us
    ppermute x30 -> x24, waiting for transfers between devices: 34.7 us -> 26.1 us  [moved(): return lax.ppermute(block, ('groups', 'seq'), route)]
    ppermute x30 -> x24, starting transfers between devices: 28.2 us -> 20.1 us  [moved(): return lax.ppermute(block, ('groups', 'seq'), route)]
    all_to_all x2, waiting for transfers between devices: 7.88 us -> 13.9 us  [body(): lax.all_to_all(outgoing, 'seq', split_axis=0, concat_axis=1, tiled=True)[0]]
    pallas_call x0 -> x1, Pallas kernels: none -> 5.88 us  [own_product(): pl.pallas_call(functools.partial(own_product_kernel, plan), in_specs=[SME...]
    pallas_call x3 -> x2, Pallas kernels: 17.3 us -> 13 us  [product(): pl.pallas_call(functools.partial(product_kernel, plan, group, parts, bool...]
    slice x3 -> x0, local copies, waits for them, and re-layouts: 2.17 us -> none  [parts_of(): return [block[:, k * columns:(k + 1) * columns] for k in range(2)]]
    all_to_all x2, starting transfers between devices: 9.52 us -> 7.57 us  [body(): lax.all_to_all(outgoing, 'seq', split_axis=0, concat_axis=1, tiled=True)[0]]
  transfers between devices with their start and end apart: 35 -> 29, of which waited for: 18 -> 22; matrix products, arithmetic and copies ran while one was open for 7% -> 7% of each run, Pallas kernels for 22% -> 29%
where the time goes in v10:
time: 129 us
  Pallas kernels  42.3 us (33%)
  waiting for transfers between devices  42 us (33%)
  starting transfers between devices  28.4 us (22%)
  other arithmetic  8.63 us (7%)
  between operations  3.65 us (3%)
  local copies, waits for them, and re-layouts  2.79 us (2%)
    ppermute x24, waiting for transfers between devices, moved(): return lax.ppermute(block, ('groups', 'seq'), route)  26.1 us
    ppermute x24, starting transfers between devices, moved(): return lax.ppermute(block, ('groups', 'seq'), route)  20.1 us
    all_to_all x2, waiting for transfers between devices, body(): lax.all_to_all(outgoing, 'seq', split_axis=0, concat_axis=1, tiled=True)[0]  13.9 us
    pallas_call x2, Pallas kernels, product(): pl.pallas_call(functools.partial(product_kernel, plan, group, parts, bool...  13 us
    pallas_call x1, Pallas kernels, prepared(): pl.pallas_call(prepare_kernel, grid_spec=pltpu.PrefetchScalarGridSpec(num...  9.41 us
    pallas_call x2, Pallas kernels, outgoing_rows(): pl.pallas_call(kernel, in_specs=[SMEM_REF] * 3 + [ANY_REF] * (1 + len(ope...  8.82 us
    all_to_all x2, starting transfers between devices, body(): lax.all_to_all(outgoing, 'seq', split_axis=0, concat_axis=1, tiled=True)[0]  7.57 us
    pallas_call x1, Pallas kernels, own_product(): pl.pallas_call(functools.partial(own_product_kernel, plan), in_specs=[SME...  5.88 us
  transfers between devices with their start and end apart: 29, of which 22 were waited for; matrix products, arithmetic and copies ran while one was open for 7% of the time, Pallas kernels for 29%

profile of v10, /device:TPU:0, one launch (start us, length us, event | category | flops | bytes accessed | tf_op | source)
XLA Modules:
  0.0 128.7 jit_solution(3900900717780407491)
XLA Ops:
  0.6 0.5 collective-permute-start.3
  1.2 0.6 stack.47.place.place_ref.token_ref
  1.8 2.6 %weight_half.2.refs_0_ = bf16[256,1024]{1,0:T(8,128)(2,1)} custom-call(s32[11]{0:T(128)} %stack.47.place.place_ref.token_ref, bf16[512,512]{1,0:T(8,128)(2,1)} %key_weight.3, bf16[512,512]{1,0:T(8,128)(2,1)} %value_weight.2), custom_call_target="tpu_custom_call" | custom-call | flops 1000 | bytes 1000 | tf_op jit(solution)/shard_map/weight_half/pallas_call | solution.py:123
  4.4 2.7 %collective-permute-start = (bf16[256,1024]{1,0:T(8,128)(2,1)}, bf16[256,1024]{1,0:T(8,128)(2,1)S(1)}, u32[]{:S(2)}, u32[]{:S(2)}) collective-permute-start(bf16[256,1024]{1,0:T(8,128)(2,1)} %weight_half.2.refs_0_), channel_id=1, source_target_pairs={{0,4},{1,5},{2,6},{3,7},{4,0},{5,1},{6,2},{7,3},{8,12},{9,13},{10,... | collective-permute-start | bytes 1572872 | tf_op jit(solution)/shard_map/ppermute | solution.py:66
  7.1 0.7 collective-permute-start.1
  7.8 1.6 %collective-permute-start.2 = (bf16[256,1024]{1,0:T(8,128)(2,1)}, bf16[256,1024]{1,0:T(8,128)(2,1)S(1)}, u32[]{:S(2)}, u32[]{:S(2)}) collective-permute-start(bf16[256,1024]{1,0:T(8,128)(2,1)} %weight_half.2.refs_0_), channel_id=1, source_target_pairs={{0,2},{1,3},{2,0},{3,1},{4,6},{5,7},{6,4},{7,5},{8,10},{9,11},{10,... | collective-permute-start | bytes 1572872 | tf_op jit(solution)/shard_map/ppermute | solution.py:66
  9.4 2.5 %weight_half.3.refs_1_ = bf16[256,1024]{1,0:T(8,128)(2,1)} custom-call(s32[11]{0:T(128)} %stack.47.place.place_ref.token_ref, bf16[512,512]{1,0:T(8,128)(2,1)} %key_weight.3, bf16[512,512]{1,0:T(8,128)(2,1)} %value_weight.2), custom_call_target="tpu_custom_call" | custom-call | flops 1000 | bytes 1000 | tf_op jit(solution)/shard_map/weight_half/pallas_call | solution.py:123
  11.9 0.6 fusion.18
  15.2 0.7 convert_bitcast_fusion
  15.9 0.7 fusion.19
  16.6 0.7 add_convert_fusion.3
  17.3 0.7 fusion.14
  18.2 0.6 pad_maximum_fusion.3
  18.8 0.7 pad_maximum_fusion.2
  19.5 0.4 fusion.6
  19.9 0.8 pad_maximum_fusion
  20.7 1.4 %collective-permute-done.2.refs_2_ = bf16[256,1024]{1,0:T(8,128)(2,1)S(1)} collective-permute-done((bf16[256,1024]{1,0:T(8,128)(2,1)}, bf16[256,1024]{1,0:T(8,128)(2,1)S(1)}, u32[]{:S(2)}, u32[]{:S(2)}) %collective-permute-start.2) | collective-permute-done | bytes 524320 | tf_op jit(solution)/shard_map/ppermute | solution.py:66
  22.1 1.5 %collective-permute-start.4 = (bf16[256,1024]{1,0:T(8,128)(2,1)S(1)}, bf16[256,1024]{1,0:T(8,128)(2,1)S(1)}, u32[]{:S(2)}, u32[]{:S(2)}) collective-permute-start(bf16[256,1024]{1,0:T(8,128)(2,1)S(1)} %collective-permute-done.2.refs_2_), channel_id=1, source_target_pairs={{0,16},{1,17},{2,18},{3,19},{4,20},{5,21},{6,22},{7,23},{8,24},{9,... | collective-permute-start | bytes 1572872 | tf_op jit(solution)/shard_map/ppermute | solution.py:66
  23.6 0.7 collective-permute-start.5
  24.3 1.3 %collective-permute-start.6 = (bf16[256,1024]{1,0:T(8,128)(2,1)S(1)}, bf16[256,1024]{1,0:T(8,128)(2,1)S(1)}, u32[]{:S(2)}, u32[]{:S(2)}) collective-permute-start(bf16[256,1024]{1,0:T(8,128)(2,1)S(1)} %collective-permute-done.1), channel_id=1, source_target_pairs={{4,0},{5,1},{6,2},{7,3},{8,12},{9,13},{10,14},{11,15},{20,16},{21,... | collective-permute-start | bytes 1572872 | tf_op jit(solution)/shard_map/ppermute | solution.py:66
  25.6 1.6 %collective-permute-start.7 = (bf16[256,1024]{1,0:T(8,128)(2,1)S(1)}, bf16[256,1024]{1,0:T(8,128)(2,1)}, u32[]{:S(2)}, u32[]{:S(2)}) collective-permute-start(bf16[256,1024]{1,0:T(8,128)(2,1)S(1)} %collective-permute-done.refs_4_), channel_id=1, source_target_pairs={{0,2},{1,3},{2,0},{3,1},{4,6},{5,7},{6,4},{7,5},{8,10},{9,11},{10,... | collective-permute-start | bytes 1572872 | tf_op jit(solution)/shard_map/ppermute | solution.py:66
  27.2 9.4 %normed_halves.1 = (bf16[16,2,320,256]{3,2,1,0:T(8,128)(2,1)}, bf16[16,320,256]{2,1,0:T(8,128)(2,1)}) custom-call(s32[11]{0:T(128)} %stack.47.place.place_ref.token_ref, bf16[320,8192]{1,0:T(8,128)(2,1)} %bitcast.50, bf16[320,8192]{1,0:T(8,128)(2,1)} %collective-permute-done.3.refs_1_), custom_call_target="tpu_custom_call" | custom-call | flops 1000 | bytes 1000 | tf_op jit(solution)/shard_map/normed_halves/pallas_call | solution.py:165
  36.6 5.4 %collective-permute-done.6 = bf16[256,1024]{1,0:T(8,128)(2,1)S(1)} collective-permute-done((bf16[256,1024]{1,0:T(8,128)(2,1)S(1)}, bf16[256,1024]{1,0:T(8,128)(2,1)S(1)}, u32[]{:S(2)}, u32[]{:S(2)}) %collective-permute-start.6) | collective-permute-done | bytes 524320 | tf_op jit(solution)/shard_map/ppermute | solution.py:66
  42.1 0.6 collective-permute-start.10
  42.7 1.5 %collective-permute-start.9 = (bf16[256,1024]{1,0:T(8,128)(2,1)S(1)}, bf16[256,1024]{1,0:T(8,128)(2,1)S(1)}, u32[]{:S(2)}, u32[]{:S(2)}) collective-permute-start(bf16[256,1024]{1,0:T(8,128)(2,1)S(1)} %broadcast_select_fusion.1.refs_0_), channel_id=1, source_target_pairs={{0,2},{1,3},{2,0},{3,1},{4,6},{5,7},{6,4},{7,5},{8,10},{9,11},{10,... | collective-permute-start | bytes 1572872 | tf_op jit(solution)/shard_map/ppermute | solution.py:66
  44.2 1.3 collective-permute-start.8
  45.5 6.4 %add_product.2 = (f32[320,1024]{1,0:T(8,128)}, f32[320,1024]{1,0:T(8,128)}) custom-call(s32[11]{0:T(128)} %stack.47.place.place_ref.token_ref, bf16[16,2,320,256]{3,2,1,0:T(8,128)(2,1)} %get-tuple-element.43.both.refs_0_, bf16[256,1024]{1,0:T(8,128)(2,1)} %weight_half.2.refs_0_, bf16[256,1024]{1,0:T(8,128)(2,1)} %weight_half.3.refs_1_, ...), custom_call_target="tpu_custom_call" | custom-call | flops 68719476736 | bytes 1000 | tf_op jit(solution)/shard_map/add_product/pallas_call | solution.py:248
  51.9 2.2 %collective-permute-done.10.refs_1_ = bf16[256,1024]{1,0:T(8,128)(2,1)S(1)} collective-permute-done((bf16[256,1024]{1,0:T(8,128)(2,1)S(1)}, bf16[256,1024]{1,0:T(8,128)(2,1)S(1)}, u32[]{:S(2)}, u32[]{:S(2)}) %collective-permute-start.10) | collective-permute-done | bytes 524320 | tf_op jit(solution)/shard_map/ppermute | solution.py:66
  54.4 3.1 %collective-permute-done.8 = bf16[256,1024]{1,0:T(8,128)(2,1)S(1)} collective-permute-done((bf16[256,1024]{1,0:T(8,128)(2,1)S(1)}, bf16[256,1024]{1,0:T(8,128)(2,1)S(1)}, u32[]{:S(2)}, u32[]{:S(2)}) %collective-permute-start.8) | collective-permute-done | bytes 524320 | tf_op jit(solution)/shard_map/ppermute | solution.py:66
  57.6 1.6 %collective-permute-start.12 = (bf16[256,1024]{1,0:T(8,128)(2,1)S(1)}, bf16[256,1024]{1,0:T(8,128)(2,1)S(1)}, u32[]{:S(2)}, u32[]{:S(2)}) collective-permute-start(bf16[256,1024]{1,0:T(8,128)(2,1)S(1)} %broadcast_select_fusion.refs_3_), channel_id=1, source_target_pairs={{0,16},{1,17},{2,18},{3,19},{4,20},{5,21},{6,22},{7,23},{8,24},{9,... | collective-permute-start | bytes 1572872 | tf_op jit(solution)/shard_map/ppermute | solution.py:66
  59.2 0.4 collective-permute-start.13
  59.7 6.7 %add_product.3 = (f32[320,1024]{1,0:T(8,128)}, f32[320,1024]{1,0:T(8,128)}) custom-call(s32[11]{0:T(128)} %stack.47.place.place_ref.token_ref, bf16[16,2,320,256]{3,2,1,0:T(8,128)(2,1)} %get-tuple-element.43.both.refs_0_, bf16[256,1024]{1,0:T(8,128)(2,1)} %copy-done.8, bf16[256,1024]{1,0:T(8,128)(2,1)} %copy-done.24, bf16[256,1024]{1,0:T(8,128)(2,1)} %copy-done.20, ...), custom_call_target="tpu_custom_call" | custom-call | flops 68719476736 | bytes 1000 | tf_op jit(solution)/shard_map/add_product/pallas_call | solution.py:248
  66.3 1.8 %collective-permute-done.12.refs_2_ = bf16[256,1024]{1,0:T(8,128)(2,1)S(1)} collective-permute-done((bf16[256,1024]{1,0:T(8,128)(2,1)S(1)}, bf16[256,1024]{1,0:T(8,128)(2,1)S(1)}, u32[]{:S(2)}, u32[]{:S(2)}) %collective-permute-start.12) | collective-permute-done | bytes 524320 | tf_op jit(solution)/shard_map/ppermute | solution.py:66
  68.1 1.2 collective-permute-done.13.refs_4_
  69.5 0.5 collective-permute-start.19
  70.1 0.5 collective-permute-start.18
  70.6 1.5 %collective-permute-start.16 = (bf16[256,1024]{1,0:T(8,128)(2,1)S(1)}, bf16[256,1024]{1,0:T(8,128)(2,1)S(1)}, u32[]{:S(2)}, u32[]{:S(2)}) collective-permute-start(bf16[256,1024]{1,0:T(8,128)(2,1)S(1)} %collective-permute-done.12.refs_2_), channel_id=1, source_target_pairs={{0,2},{1,3},{2,0},{3,1},{4,6},{5,7},{6,4},{7,5},{8,10},{9,11},{10,... | collective-permute-start | bytes 1572872 | tf_op jit(solution)/shard_map/ppermute | solution.py:66
  72.1 0.9 collective-permute-done.19.refs_5_
  73.0 0.7 collective-permute-start.15
  74.0 0.8 collective-permute-done.18.refs_3_
  74.9 0.8 copy-done.27
  75.6 0.5 copy-done.15
  76.1 5.9 %own_product.1 = (f32[320,512]{1,0:T(8,128)}, f32[320,512]{1,0:T(8,128)}) custom-call(s32[11]{0:T(128)} %stack.47.place.place_ref.token_ref, bf16[16,2,320,256]{3,2,1,0:T(8,128)(2,1)} %get-tuple-element.43.both.refs_0_, bf16[16,320,256]{2,1,0:T(8,128)(2,1)} %get-tuple-element.33.kept.refs_1_, bf16[256,1024]{1,0:T(8,128)(2,1)} %copy-done.23, ...), custom_call_target="tpu_custom_call" | custom-call | flops 68719476736 | bytes 1000 | tf_op jit(solution)/shard_map/own_product/pallas_call | solution.py:297
  82.0 2.4 %collective-permute-done.16.refs_6_ = bf16[256,1024]{1,0:T(8,128)(2,1)S(1)} collective-permute-done((bf16[256,1024]{1,0:T(8,128)(2,1)S(1)}, bf16[256,1024]{1,0:T(8,128)(2,1)S(1)}, u32[]{:S(2)}, u32[]{:S(2)}) %collective-permute-start.16) | collective-permute-done | bytes 524320 | tf_op jit(solution)/shard_map/ppermute | solution.py:66
  84.4 3.0 %collective-permute-done.15.refs_4_ = bf16[256,1024]{1,0:T(8,128)(2,1)S(1)} collective-permute-done((bf16[256,1024]{1,0:T(8,128)(2,1)}, bf16[256,1024]{1,0:T(8,128)(2,1)S(1)}, u32[]{:S(2)}, u32[]{:S(2)}) %collective-permute-start.15) | collective-permute-done | bytes 524320 | tf_op jit(solution)/shard_map/ppermute | solution.py:66
  87.4 0.5 collective-permute-done.14.refs_2_
  87.9 0.5 collective-permute-start.22
  88.5 1.3 %collective-permute-done.23.refs_7_ = bf16[256,1024]{1,0:T(8,128)(2,1)S(1)} collective-permute-done((bf16[256,1024]{1,0:T(8,128)(2,1)S(1)}, bf16[256,1024]{1,0:T(8,128)(2,1)S(1)}, u32[]{:S(2)}, u32[]{:S(2)}) %collective-permute-start.23) | collective-permute-done | bytes 524320 | tf_op jit(solution)/shard_map/ppermute | solution.py:66
  89.8 0.7 collective-permute-done.22.refs_5_
  90.6 0.7 collective-permute-done.21.refs_3_
  91.4 0.8 copy-done.6
  92.2 4.6 %cache_rows.2.token_ref = bf16[16,80,128]{2,1,0:T(8,128)(2,1)} custom-call(s32[11]{0:T(128)} %stack.47.place.place_ref.token_ref, s32[2]{0:T(128)} %lengths_ref.3, s32[8]{0:T(128)} %owner_ref.3, s32[11]{0:T(128)} %stack.47.place.place_ref.token_ref, bf16[16,2,320,256]{3,2,1,0:T(8,128)(2,1)} %get-tuple-element.43.both.refs_0_, ...), custom_call_target="tpu_custom_call" | custom-call | flops 1000 | bytes 1000 | tf_op jit(solution)/shard_map/cache_rows/pallas_call | solution.py:363
  96.8 4.0 %all-to-all-start = ((bf16[16,80,128]{2,1,0:T(8,128)(2,1)}), bf16[16,80,128]{2,1,0:T(8,128)(2,1)S(1)}, u32[]{:S(2)}, u32[]{:S(2)}) async-start(bf16[16,80,128]{2,1,0:T(8,128)(2,1)} %cache_rows.2.token_ref), calls=%async_computation | async-start | bytes 655360 | tf_op jit(solution)/shard_map/all_to_all | solution.py:511
  100.9 0.7 add_compare_fusion
  101.8 4.2 %cache_rows.3 = bf16[16,80,128]{2,1,0:T(8,128)(2,1)} custom-call(s32[11]{0:T(128)} %stack.47.place.place_ref.token_ref, s32[2]{0:T(128)} %lengths_ref.3, s32[8]{0:T(128)} %owner_ref.3, bf16[16,80,128]{2,1,0:T(8,128)(2,1)} %cache_rows.2.token_ref, bf16[16,2,320,256]{3,2,1,0:T(8,128)(2,1)} %get-tuple-element.43.both.refs_0_, ...), custom_call_target="tpu_custom_call" | custom-call | flops 1000 | bytes 1000 | tf_op jit(solution)/shard_map/cache_rows/pallas_call | solution.py:363
  106.0 6.0 %all-to-all-done = bf16[16,80,128]{2,1,0:T(8,128)(2,1)S(1)} async-done(((bf16[16,80,128]{2,1,0:T(8,128)(2,1)}), bf16[16,80,128]{2,1,0:T(8,128)(2,1)S(1)}, u32[]{:S(2)}, u32[]{:S(2)}) %all-to-all-start) | async-done | bytes 327712 | tf_op jit(solution)/shard_map/all_to_all | solution.py:511
  112.0 3.5 %all-to-all-start.1 = ((bf16[16,80,128]{2,1,0:T(8,128)(2,1)}), bf16[16,80,128]{2,1,0:T(8,128)(2,1)S(1)}, u32[]{:S(2)}, u32[]{:S(2)}) async-start(bf16[16,80,128]{2,1,0:T(8,128)(2,1)} %cache_rows.3), calls=%async_computation.1 | async-start | bytes 655360 | tf_op jit(solution)/shard_map/all_to_all | solution.py:511
  115.8 0.3 collective-permute-start.24
  116.2 0.9 collective-permute-done.24
  117.2 0.3 collective-permute-start.25
  117.6 0.9 collective-permute-done.25
  118.7 7.9 %all-to-all-done.1 = bf16[16,80,128]{2,1,0:T(8,128)(2,1)S(1)} async-done(((bf16[16,80,128]{2,1,0:T(8,128)(2,1)}), bf16[16,80,128]{2,1,0:T(8,128)(2,1)S(1)}, u32[]{:S(2)}, u32[]{:S(2)}) %all-to-all-start.1) | async-done | bytes 327712 | tf_op jit(solution)/shard_map/all_to_all | solution.py:511
  126.9 0.9 maximum_bitcast_fusion
  128.1 0.6 fusion.7
  (89 shorter events, 2.9 us)
Async XLA Ops:
  0.6 117.8 %copy-start = (bf16[8,4,128]{2,1,0:T(4,128)(2,1)S(1)}, bf16[8,4,128]{2,1,0:T(4,128)(2,1)}, u32[]{:S(2)}) copy-start(bf16[8,4,128]{2,1,0:T(4,128)(2,1)} %param.17) | copy-start | bytes 24580
  0.6 21.4 %collective-permute-start.3 = (bf16[320,8192]{1,0:T(8,128)(2,1)}, bf16[320,8192]{1,0:T(8,128)(2,1)}, u32[]{:S(2)}, u32[]{:S(2)}) collective-permute-start(bf16[320,8192]{1,0:T(8,128)(2,1)} %bitcast.49), channel_id=1, source_target_pairs={{0,1},{1,0},{2,3},{3,2},{4,5},{5,4},{6,7},{7,6},{8,9},{9,8},{10,11... | collective-permute-start | bytes 15728648 | tf_op jit(solution)/shard_map/ppermute | solution.py:66
  1.8 10.2 %copy-start.12 = (s32[8]{0:T(128)S(1)}, s32[8]{0:T(128)}, u32[]{:S(2)}) copy-start(s32[8]{0:T(128)} %owner_ref.3) | copy-start | bytes 100
  1.8 14.1 %copy-start.11 = (s32[2]{0:T(128)S(1)}, s32[2]{0:T(128)}, u32[]{:S(2)}) copy-start(s32[2]{0:T(128)} %lengths_ref.3) | copy-start | bytes 28
  1.8 16.3 %copy-start.13 = (f32[64]{0:T(128)S(1)}, f32[64]{0:T(128)}, u32[]{:S(2)}) copy-start(f32[64]{0:T(128)} %constant.90.clone) | copy-start | bytes 772
  4.4 16.3 %collective-permute-start = (bf16[256,1024]{1,0:T(8,128)(2,1)}, bf16[256,1024]{1,0:T(8,128)(2,1)S(1)}, u32[]{:S(2)}, u32[]{:S(2)}) collective-permute-start(bf16[256,1024]{1,0:T(8,128)(2,1)} %weight_half.2.refs_0_), channel_id=1, source_target_pairs={{0,4},{1,5},{2,6},{3,7},{4,0},{5,1},{6,2},{7,3},{8,12},{9,13},{10,... | collective-permute-start | bytes 1572872 | tf_op jit(solution)/shard_map/ppermute | solution.py:66
  7.1 13.5 %collective-permute-start.1 = (bf16[256,1024]{1,0:T(8,128)(2,1)}, bf16[256,1024]{1,0:T(8,128)(2,1)S(1)}, u32[]{:S(2)}, u32[]{:S(2)}) collective-permute-start(bf16[256,1024]{1,0:T(8,128)(2,1)} %weight_half.2.refs_0_), channel_id=1, source_target_pairs={{4,8},{5,9},{6,10},{7,11},{8,4},{9,5},{10,6},{11,7},{20,24},{21,25... | collective-permute-start | bytes 1572872 | tf_op jit(solution)/shard_map/ppermute | solution.py:66
  7.8 14.3 %collective-permute-start.2 = (bf16[256,1024]{1,0:T(8,128)(2,1)}, bf16[256,1024]{1,0:T(8,128)(2,1)S(1)}, u32[]{:S(2)}, u32[]{:S(2)}) collective-permute-start(bf16[256,1024]{1,0:T(8,128)(2,1)} %weight_half.2.refs_0_), channel_id=1, source_target_pairs={{0,2},{1,3},{2,0},{3,1},{4,6},{5,7},{6,4},{7,5},{8,10},{9,11},{10,... | collective-permute-start | bytes 1572872 | tf_op jit(solution)/shard_map/ppermute | solution.py:66
  20.7 15.9 %copy-start.16 = (bf16[256,1024]{1,0:T(8,128)(2,1)}, bf16[256,1024]{1,0:T(8,128)(2,1)S(1)}, u32[]{:S(2)}) copy-start(bf16[256,1024]{1,0:T(8,128)(2,1)S(1)} %collective-permute-done.refs_4_) | copy-start | bytes 1572868
  22.1 14.5 %copy-start.19 = (bf16[256,1024]{1,0:T(8,128)(2,1)}, bf16[256,1024]{1,0:T(8,128)(2,1)S(1)}, u32[]{:S(2)}) copy-start(bf16[256,1024]{1,0:T(8,128)(2,1)S(1)} %collective-permute-done.2.refs_2_) | copy-start | bytes 1572868
  22.1 14.5 %collective-permute-start.4 = (bf16[256,1024]{1,0:T(8,128)(2,1)S(1)}, bf16[256,1024]{1,0:T(8,128)(2,1)S(1)}, u32[]{:S(2)}, u32[]{:S(2)}) collective-permute-start(bf16[256,1024]{1,0:T(8,128)(2,1)S(1)} %collective-permute-done.2.refs_2_), channel_id=1, source_target_pairs={{0,16},{1,17},{2,18},{3,19},{4,20},{5,21},{6,22},{7,23},{8,24},{9,... | collective-permute-start | bytes 1572872 | tf_op jit(solution)/shard_map/ppermute | solution.py:66
  23.6 13.0 %collective-permute-start.5 = (bf16[256,1024]{1,0:T(8,128)(2,1)S(1)}, bf16[256,1024]{1,0:T(8,128)(2,1)S(1)}, u32[]{:S(2)}, u32[]{:S(2)}) collective-permute-start(bf16[256,1024]{1,0:T(8,128)(2,1)S(1)} %collective-permute-done.refs_4_), channel_id=1, source_target_pairs={{4,8},{5,9},{6,10},{7,11},{8,4},{9,5},{10,6},{11,7},{20,24},{21,25... | collective-permute-start | bytes 1572872 | tf_op jit(solution)/shard_map/ppermute | solution.py:66
  24.3 17.7 %collective-permute-start.6 = (bf16[256,1024]{1,0:T(8,128)(2,1)S(1)}, bf16[256,1024]{1,0:T(8,128)(2,1)S(1)}, u32[]{:S(2)}, u32[]{:S(2)}) collective-permute-start(bf16[256,1024]{1,0:T(8,128)(2,1)S(1)} %collective-permute-done.1), channel_id=1, source_target_pairs={{4,0},{5,1},{6,2},{7,3},{8,12},{9,13},{10,14},{11,15},{20,16},{21,... | collective-permute-start | bytes 1572872 | tf_op jit(solution)/shard_map/ppermute | solution.py:66
  25.6 16.4 %collective-permute-start.7 = (bf16[256,1024]{1,0:T(8,128)(2,1)S(1)}, bf16[256,1024]{1,0:T(8,128)(2,1)}, u32[]{:S(2)}, u32[]{:S(2)}) collective-permute-start(bf16[256,1024]{1,0:T(8,128)(2,1)S(1)} %collective-permute-done.refs_4_), channel_id=1, source_target_pairs={{0,2},{1,3},{2,0},{3,1},{4,6},{5,7},{6,4},{7,5},{8,10},{9,11},{10,... | collective-permute-start | bytes 1572872 | tf_op jit(solution)/shard_map/ppermute | solution.py:66
  36.6 8.9 %copy-start.17 = (bf16[256,1024]{1,0:T(8,128)(2,1)}, bf16[256,1024]{1,0:T(8,128)(2,1)S(1)}, u32[]{:S(2)}) copy-start(bf16[256,1024]{1,0:T(8,128)(2,1)S(1)} %collective-permute-done.4.refs_3_) | copy-start | bytes 1572868
  42.1 9.8 %copy-start.8 = (bf16[256,1024]{1,0:T(8,128)(2,1)}, bf16[256,1024]{1,0:T(8,128)(2,1)S(1)}, u32[]{:S(2)}) copy-start(bf16[256,1024]{1,0:T(8,128)(2,1)S(1)} %broadcast_select_fusion.1.refs_0_) | copy-start | bytes 1572868
  42.1 12.0 %collective-permute-start.10 = (bf16[256,1024]{1,0:T(8,128)(2,1)S(1)}, bf16[256,1024]{1,0:T(8,128)(2,1)S(1)}, u32[]{:S(2)}, u32[]{:S(2)}) collective-permute-start(bf16[256,1024]{1,0:T(8,128)(2,1)S(1)} %broadcast_select_fusion.1.refs_0_), channel_id=1, source_target_pairs={{0,16},{1,17},{2,18},{3,19},{4,20},{5,21},{6,22},{7,23},{8,24},{9,... | collective-permute-start | bytes 1572872 | tf_op jit(solution)/shard_map/ppermute | solution.py:66
  42.7 11.7 %collective-permute-start.9 = (bf16[256,1024]{1,0:T(8,128)(2,1)S(1)}, bf16[256,1024]{1,0:T(8,128)(2,1)S(1)}, u32[]{:S(2)}, u32[]{:S(2)}) collective-permute-start(bf16[256,1024]{1,0:T(8,128)(2,1)S(1)} %broadcast_select_fusion.1.refs_0_), channel_id=1, source_target_pairs={{0,2},{1,3},{2,0},{3,1},{4,6},{5,7},{6,4},{7,5},{8,10},{9,11},{10,... | collective-permute-start | bytes 1572872 | tf_op jit(solution)/shard_map/ppermute | solution.py:66
  44.2 13.3 %collective-permute-start.8 = (bf16[256,1024]{1,0:T(8,128)(2,1)S(1)}, bf16[256,1024]{1,0:T(8,128)(2,1)S(1)}, u32[]{:S(2)}, u32[]{:S(2)}) collective-permute-start(bf16[256,1024]{1,0:T(8,128)(2,1)S(1)} %collective-permute-done.5), channel_id=1, source_target_pairs={{4,0},{5,1},{6,2},{7,3},{8,12},{9,13},{10,14},{11,15},{20,16},{21,... | collective-permute-start | bytes 1572872 | tf_op jit(solution)/shard_map/ppermute | solution.py:66
  51.9 7.7 %copy-start.7 = (bf16[256,1024]{1,0:T(8,128)(2,1)S(1)}, bf16[256,1024]{1,0:T(8,128)(2,1)}, u32[]{:S(2)}) copy-start(bf16[256,1024]{1,0:T(8,128)(2,1)} %weight_half.3.refs_1_) | copy-start | bytes 1572868
  54.1 5.5 %copy-start.24 = (bf16[256,1024]{1,0:T(8,128)(2,1)}, bf16[256,1024]{1,0:T(8,128)(2,1)S(1)}, u32[]{:S(2)}) copy-start(bf16[256,1024]{1,0:T(8,128)(2,1)S(1)} %collective-permute-done.10.refs_1_) | copy-start | bytes 1572868
  54.4 5.3 %copy-start.20 = (bf16[256,1024]{1,0:T(8,128)(2,1)}, bf16[256,1024]{1,0:T(8,128)(2,1)S(1)}, u32[]{:S(2)}) copy-start(bf16[256,1024]{1,0:T(8,128)(2,1)S(1)} %collective-permute-done.9.refs_2_) | copy-start | bytes 1572868
  57.5 2.1 %copy-start.9 = (bf16[256,1024]{1,0:T(8,128)(2,1)}, bf16[256,1024]{1,0:T(8,128)(2,1)S(1)}, u32[]{:S(2)}) copy-start(bf16[256,1024]{1,0:T(8,128)(2,1)S(1)} %broadcast_select_fusion.refs_3_) | copy-start | bytes 1572868
  57.6 10.5 %collective-permute-start.12 = (bf16[256,1024]{1,0:T(8,128)(2,1)S(1)}, bf16[256,1024]{1,0:T(8,128)(2,1)S(1)}, u32[]{:S(2)}, u32[]{:S(2)}) collective-permute-start(bf16[256,1024]{1,0:T(8,128)(2,1)S(1)} %broadcast_select_fusion.refs_3_), channel_id=1, source_target_pairs={{0,16},{1,17},{2,18},{3,19},{4,20},{5,21},{6,22},{7,23},{8,24},{9,... | collective-permute-start | bytes 1572872 | tf_op jit(solution)/shard_map/ppermute | solution.py:66
  59.2 10.1 %collective-permute-start.13 = (bf16[256,1024]{1,0:T(8,128)(2,1)S(1)}, bf16[256,1024]{1,0:T(8,128)(2,1)S(1)}, u32[]{:S(2)}, u32[]{:S(2)}) collective-permute-start(bf16[256,1024]{1,0:T(8,128)(2,1)S(1)} %broadcast_select_fusion.refs_3_), channel_id=1, source_target_pairs={{0,2},{1,3},{2,0},{3,1},{4,6},{5,7},{6,4},{7,5},{8,10},{9,11},{10,... | collective-permute-start | bytes 1572872 | tf_op jit(solution)/shard_map/ppermute | solution.py:66
  59.6 9.9 %collective-permute-start.11 = (bf16[256,1024]{1,0:T(8,128)(2,1)S(1)}, bf16[256,1024]{1,0:T(8,128)(2,1)S(1)}, u32[]{:S(2)}, u32[]{:S(2)}) collective-permute-start(bf16[256,1024]{1,0:T(8,128)(2,1)S(1)} %copy-done.7), channel_id=1, source_target_pairs={{0,4},{1,5},{2,6},{3,7},{4,0},{5,1},{6,2},{7,3},{8,12},{9,13},{10,... | collective-permute-start | bytes 1572872 | tf_op jit(solution)/shard_map/ppermute | solution.py:66
  59.6 14.1 %copy-start.18 = (bf16[256,1024]{1,0:T(8,128)(2,1)S(1)}, bf16[256,1024]{1,0:T(8,128)(2,1)}, u32[]{:S(2)}) copy-start(bf16[256,1024]{1,0:T(8,128)(2,1)} %copy-done.17) | copy-start | bytes 1572868
  68.1 6.7 %copy-start.21 = (bf16[256,1024]{1,0:T(8,128)(2,1)}, bf16[256,1024]{1,0:T(8,128)(2,1)S(1)}, u32[]{:S(2)}) copy-start(bf16[256,1024]{1,0:T(8,128)(2,1)S(1)} %collective-permute-done.12.refs_2_) | copy-start | bytes 1572868
  69.3 5.5 %copy-start.22 = (bf16[256,1024]{1,0:T(8,128)(2,1)}, bf16[256,1024]{1,0:T(8,128)(2,1)S(1)}, u32[]{:S(2)}) copy-start(bf16[256,1024]{1,0:T(8,128)(2,1)S(1)} %collective-permute-done.13.refs_4_) | copy-start | bytes 1572868
  69.5 5.3 %copy-start.23 = (bf16[256,1024]{1,0:T(8,128)(2,1)}, bf16[256,1024]{1,0:T(8,128)(2,1)S(1)}, u32[]{:S(2)}) copy-start(bf16[256,1024]{1,0:T(8,128)(2,1)S(1)} %collective-permute-done.11.refs_0_) | copy-start | bytes 1572868
  69.5 5.3 %collective-permute-start.20 = (f32[320,1024]{1,0:T(8,128)}, f32[320,1024]{1,0:T(8,128)S(1)}, u32[]{:S(2)}, u32[]{:S(2)}) collective-permute-start(f32[320,1024]{1,0:T(8,128)} %get-tuple-element.52), channel_id=1, source_target_pairs={{0,1},{1,0},{2,3},{3,2},{4,5},{5,4},{6,7},{7,6},{8,9},{9,8},{10,11... | collective-permute-start | bytes 3932168 | tf_op jit(solution)/shard_map/ppermute | solution.py:66
  69.5 3.4 %collective-permute-start.19 = (bf16[256,1024]{1,0:T(8,128)(2,1)S(1)}, bf16[256,1024]{1,0:T(8,128)(2,1)S(1)}, u32[]{:S(2)}, u32[]{:S(2)}) collective-permute-start(bf16[256,1024]{1,0:T(8,128)(2,1)S(1)} %collective-permute-done.13.refs_4_), channel_id=1, source_target_pairs={{0,1},{1,0},{2,3},{3,2},{4,5},{5,4},{6,7},{7,6},{8,9},{9,8},{10,11... | collective-permute-start | bytes 1572872 | tf_op jit(solution)/shard_map/ppermute | solution.py:66
  70.1 3.7 %collective-permute-start.17 = (bf16[256,1024]{1,0:T(8,128)(2,1)S(1)}, bf16[256,1024]{1,0:T(8,128)(2,1)S(1)}, u32[]{:S(2)}, u32[]{:S(2)}) collective-permute-start(bf16[256,1024]{1,0:T(8,128)(2,1)S(1)} %collective-permute-done.11.refs_0_), channel_id=1, source_target_pairs={{0,1},{1,0},{2,3},{3,2},{4,5},{5,4},{6,7},{7,6},{8,9},{9,8},{10,11... | collective-permute-start | bytes 1572872 | tf_op jit(solution)/shard_map/ppermute | solution.py:66
  70.1 4.8 %collective-permute-start.18 = (bf16[256,1024]{1,0:T(8,128)(2,1)S(1)}, bf16[256,1024]{1,0:T(8,128)(2,1)S(1)}, u32[]{:S(2)}, u32[]{:S(2)}) collective-permute-start(bf16[256,1024]{1,0:T(8,128)(2,1)S(1)} %collective-permute-done.12.refs_2_), channel_id=1, source_target_pairs={{0,1},{1,0},{2,3},{3,2},{4,5},{5,4},{6,7},{7,6},{8,9},{9,8},{10,11... | collective-permute-start | bytes 1572872 | tf_op jit(solution)/shard_map/ppermute | solution.py:66
  70.6 13.8 %collective-permute-start.16 = (bf16[256,1024]{1,0:T(8,128)(2,1)S(1)}, bf16[256,1024]{1,0:T(8,128)(2,1)S(1)}, u32[]{:S(2)}, u32[]{:S(2)}) collective-permute-start(bf16[256,1024]{1,0:T(8,128)(2,1)S(1)} %collective-permute-done.12.refs_2_), channel_id=1, source_target_pairs={{0,2},{1,3},{2,0},{3,1},{4,6},{5,7},{6,4},{7,5},{8,10},{9,11},{10,... | collective-permute-start | bytes 1572872 | tf_op jit(solution)/shard_map/ppermute | solution.py:66
  73.0 1.9 %copy-start.25 = (bf16[256,1024]{1,0:T(8,128)(2,1)}, bf16[256,1024]{1,0:T(8,128)(2,1)S(1)}, u32[]{:S(2)}) copy-start(bf16[256,1024]{1,0:T(8,128)(2,1)S(1)} %collective-permute-done.19.refs_5_) | copy-start | bytes 1572868
  73.0 14.4 %collective-permute-start.15 = (bf16[256,1024]{1,0:T(8,128)(2,1)}, bf16[256,1024]{1,0:T(8,128)(2,1)S(1)}, u32[]{:S(2)}, u32[]{:S(2)}) collective-permute-start(bf16[256,1024]{1,0:T(8,128)(2,1)} %copy-done.20), channel_id=1, source_target_pairs={{0,16},{1,17},{2,18},{3,19},{4,20},{5,21},{6,22},{7,23},{8,24},{9,... | collective-permute-start | bytes 1572872 | tf_op jit(solution)/shard_map/ppermute | solution.py:66
  73.7 1.1 copy-start.26
  73.7 14.2 %collective-permute-start.14 = (bf16[256,1024]{1,0:T(8,128)(2,1)S(1)}, bf16[256,1024]{1,0:T(8,128)(2,1)S(1)}, u32[]{:S(2)}, u32[]{:S(2)}) collective-permute-start(bf16[256,1024]{1,0:T(8,128)(2,1)S(1)} %copy-done.18), channel_id=1, source_target_pairs={{0,4},{1,5},{2,6},{3,7},{4,0},{5,1},{6,2},{7,3},{8,12},{9,13},{10,... | collective-permute-start | bytes 1572872 | tf_op jit(solution)/shard_map/ppermute | solution.py:66
  74.8 0.8 copy-start.27
  74.8 1.3 %copy-start.15 = (f32[320,1024]{1,0:T(8,128)}, f32[320,1024]{1,0:T(8,128)S(1)}, u32[]{:S(2)}) copy-start(f32[320,1024]{1,0:T(8,128)S(1)} %collective-permute-done.20.refs_7_) | copy-start | bytes 3932164
  84.4 6.9 %copy-start.1 = (bf16[256,1024]{1,0:T(8,128)(2,1)}, bf16[256,1024]{1,0:T(8,128)(2,1)S(1)}, u32[]{:S(2)}) copy-start(bf16[256,1024]{1,0:T(8,128)(2,1)S(1)} %collective-permute-done.16.refs_6_) | copy-start | bytes 1572868
  87.4 4.0 %copy-start.2 = (bf16[256,1024]{1,0:T(8,128)(2,1)}, bf16[256,1024]{1,0:T(8,128)(2,1)S(1)}, u32[]{:S(2)}) copy-start(bf16[256,1024]{1,0:T(8,128)(2,1)S(1)} %collective-permute-done.15.refs_4_) | copy-start | bytes 1572868
  87.9 3.4 %copy-start.3 = (bf16[256,1024]{1,0:T(8,128)(2,1)}, bf16[256,1024]{1,0:T(8,128)(2,1)S(1)}, u32[]{:S(2)}) copy-start(bf16[256,1024]{1,0:T(8,128)(2,1)S(1)} %collective-permute-done.14.refs_2_) | copy-start | bytes 1572868
  87.9 13.7 %copy-start.10 = (bf16[4,8,128]{2,1,0:T(8,128)(2,1)S(1)}, bf16[4,8,128]{2,1,0:T(8,128)(2,1)}, u32[]{:S(2)}) copy-start(bf16[4,8,128]{2,1,0:T(8,128)(2,1)} %pad_maximum_fusion.2) | copy-start | bytes 24580
  87.9 13.7 %copy-start.14 = (bf16[4,128]{1,0:T(4,128)(2,1)S(1)}, bf16[4,128]{1,0:T(4,128)(2,1)}, u32[]{:S(2)}) copy-start(bf16[4,128]{1,0:T(4,128)(2,1)} %pad_maximum_fusion.3) | copy-start | bytes 3076
  87.9 1.9 %collective-permute-start.23 = (bf16[256,1024]{1,0:T(8,128)(2,1)S(1)}, bf16[256,1024]{1,0:T(8,128)(2,1)S(1)}, u32[]{:S(2)}, u32[]{:S(2)}) collective-permute-start(bf16[256,1024]{1,0:T(8,128)(2,1)S(1)} %collective-permute-done.16.refs_6_), channel_id=1, source_target_pairs={{0,1},{1,0},{2,3},{3,2},{4,5},{5,4},{6,7},{7,6},{8,9},{9,8},{10,11... | collective-permute-start | bytes 1572872 | tf_op jit(solution)/shard_map/ppermute | solution.py:66
  87.9 2.7 %collective-permute-start.22 = (bf16[256,1024]{1,0:T(8,128)(2,1)S(1)}, bf16[256,1024]{1,0:T(8,128)(2,1)S(1)}, u32[]{:S(2)}, u32[]{:S(2)}) collective-permute-start(bf16[256,1024]{1,0:T(8,128)(2,1)S(1)} %collective-permute-done.15.refs_4_), channel_id=1, source_target_pairs={{0,1},{1,0},{2,3},{3,2},{4,5},{5,4},{6,7},{7,6},{8,9},{9,8},{10,11... | collective-permute-start | bytes 1572872 | tf_op jit(solution)/shard_map/ppermute | solution.py:66
  88.4 2.9 %collective-permute-start.21 = (bf16[256,1024]{1,0:T(8,128)(2,1)S(1)}, bf16[256,1024]{1,0:T(8,128)(2,1)S(1)}, u32[]{:S(2)}, u32[]{:S(2)}) collective-permute-start(bf16[256,1024]{1,0:T(8,128)(2,1)S(1)} %collective-permute-done.14.refs_2_), channel_id=1, source_target_pairs={{0,1},{1,0},{2,3},{3,2},{4,5},{5,4},{6,7},{7,6},{8,9},{9,8},{10,11... | collective-permute-start | bytes 1572872 | tf_op jit(solution)/shard_map/ppermute | solution.py:66
  89.8 1.5 %copy-start.4 = (bf16[256,1024]{1,0:T(8,128)(2,1)}, bf16[256,1024]{1,0:T(8,128)(2,1)S(1)}, u32[]{:S(2)}) copy-start(bf16[256,1024]{1,0:T(8,128)(2,1)S(1)} %collective-permute-done.23.refs_7_) | copy-start | bytes 1572868
  90.6 0.8 copy-start.5
  91.4 0.8 copy-start.6
  96.8 15.1 %all-to-all-start = ((bf16[16,80,128]{2,1,0:T(8,128)(2,1)}), bf16[16,80,128]{2,1,0:T(8,128)(2,1)S(1)}, u32[]{:S(2)}, u32[]{:S(2)}) async-start(bf16[16,80,128]{2,1,0:T(8,128)(2,1)} %cache_rows.2.token_ref), calls=%async_computation | async-start | bytes 655360 | tf_op jit(solution)/shard_map/all_to_all | solution.py:511
  112.0 14.6 %all-to-all-start.1 = ((bf16[16,80,128]{2,1,0:T(8,128)(2,1)}), bf16[16,80,128]{2,1,0:T(8,128)(2,1)S(1)}, u32[]{:S(2)}, u32[]{:S(2)}) async-start(bf16[16,80,128]{2,1,0:T(8,128)(2,1)} %cache_rows.3), calls=%async_computation.1 | async-start | bytes 655360 | tf_op jit(solution)/shard_map/all_to_all | solution.py:511
  115.8 1.2 collective-permute-start.24
  117.2 1.2 collective-permute-start.25
  126.8 1.2 collective-permute-start.26

commit v11 on v9

--- a/solution.py
+++ b/solution.py
@@ -94,6 +94,7 @@
 SMEM_REF = pl.BlockSpec(memory_space=pltpu.SMEM)
 ANY_REF = pl.BlockSpec(memory_space=pl.ANY)
 PARAMS = pltpu.CompilerParams(vmem_limit_bytes=56 << 20)
+SMALL = pltpu.CompilerParams(vmem_limit_bytes=16 << 20)
 
 
 def cost(flops, moved_bytes):
@@ -106,30 +107,11 @@
     return copy
 
 
-def halves_kernel(kind, place, key_weight, value_weight, out, sems):
-    depth, columns = out.shape[0], out.shape[1] // 2
-    half = 1 - place[0] if kind else place[0]
-    rows = pl.ds(pl.multiple_of(half * depth, depth), depth)
-    copies = [
-        fetch(weight.at[rows], out.at[:, pl.ds(k * columns, columns)], sems.at[k])
-        for k, weight in enumerate((key_weight, value_weight))
-    ]
-    for copy in copies:
-        copy.wait()
-
-
-def weight_half(place, kind, key_weight, value_weight):
-    rows, columns = key_weight.shape
-    return pl.pallas_call(
-        functools.partial(halves_kernel, kind),
-        in_specs=[SMEM_REF, ANY_REF, ANY_REF],
-        out_specs=VMEM_REF,
-        out_shape=jax.ShapeDtypeStruct((rows // 2, 2 * columns), key_weight.dtype),
-        scratch_shapes=[pltpu.SemaphoreType.DMA((2,))],
-        compiler_params=PARAMS,
-        cost_estimate=cost(1000, 1000),
-        name="weight_half",
-    )(place, key_weight, value_weight)
+def weight_half(half, *weights):
+    depth = weights[0].shape[0] // 2
+    return jnp.concatenate(
+        [lax.dynamic_slice_in_dim(weight, half * depth, depth, 0) for weight in weights], 1
+    )
 
 
 def prepare_kernel(place, *refs):
@@ -239,7 +221,7 @@
                 ]
 
 
-def product(place, both, pieces, totals, group, columns, parts):
+def product(place, both, pieces, totals, group, columns, parts, params=PARAMS):
     _, _, rows, depth = both.shape
     plan = [(entry, kind, len(arrays)) for entry, kind, *arrays in pieces]
     pieces_flat = [array for _, _, *arrays in pieces for array in arrays]
@@ -257,80 +239,108 @@
             pltpu.SemaphoreType.DMA((3 * count,)),
             pltpu.SemaphoreType.DMA((2 * parts,)),
         ],
-        compiler_params=PARAMS,
-        cost_estimate=cost(1000, 1000),
+        compiler_params=params,
+        cost_estimate=cost(1 << 36, 1000),
         name="add_product",
     )(place, both, *pieces_flat, *totals)
 
 
-def rows_kernel(plan, rotated, place, lengths, owner, both, kept, *refs):
-    count = len(plan)
-    pieces = refs[: 2 * count]
-    total_in, came_in = refs[2 * count : 2 * count + 2]
-    turn = refs[2 * count + 2 : 2 * count + 2 + 2 * rotated]
-    out, left, right, total, came, scratch, sems = refs[-7:]
-    rows, depth = kept.shape[1], kept.shape[2]
-    waits = [fetch(total_in, total, sems.at[0]), fetch(came_in, came, sems.at[1])]
-    sem = 2
-    for k in range(2 * count):
-        index = half_index(place, *plan[k // 2])
-        source = kept.at[index] if k % 2 else both.at[index, 0]
-        area = pl.ds(k * depth, depth)
-        waits.append(fetch(source, left.at[:, area], sems.at[sem]))
-        waits.append(fetch(pieces[k], right.at[area], sems.at[sem + 1]))
-        sem += 2
-    for copy in waits:
-        copy.wait()
-    total[...] += came[...]
-    total[...] += jnp.dot(left[...], right[...], preferred_element_type=jnp.float32)
+def rows_kernel(place, lengths, owner, total, came, cosine, sine, out, scratch):
+    columns = total.shape[1] // 2
     count_requests, count_rows = lengths.shape[0], scratch.shape[0]
     index = place[2] * count_rows + lax.broadcasted_iota(jnp.int32, scratch.shape, 0)
     for r in range(count_requests):
         live = index < lengths[r]
         for h in range(KEY_VALUE_HEADS):
-            part = total[
-                r * count_rows : (r + 1) * count_rows, h * HEAD_SIZE : (h + 1) * HEAD_SIZE
-            ]
-            if rotated:
-                turned = jnp.concatenate([part[:, HEAD_SIZE // 2 :], part[:, : HEAD_SIZE // 2]], 1)
-                part = part * turn[0][...] + turned * turn[1][...]
-            scratch[...] = jnp.where(live, part, 0.0)
-            peer = owner[r * KEY_VALUE_HEADS + h]
-            for b in range(2):
-                picked = scratch[pl.ds(b, count_rows // 2, stride=2), :]
-                out[peer * 2 + b] = picked.astype(jnp.bfloat16)
-
-
-def outgoing_rows(place, lengths, owner, both, kept, plan, pieces, total, came, turn, token):
-    _, rows, depth = kept.shape
-    columns = total.shape[1]
-    count = len(plan)
-    count_rows = rows // lengths.shape[0]
-    out = jax.ShapeDtypeStruct((owner.shape[0] * 2, count_rows // 2, HEAD_SIZE), jnp.bfloat16)
-
-    def kernel(place_ref, lengths_ref, owner_ref, token_ref, *refs):
-        rows_kernel(plan, bool(turn), place_ref, lengths_ref, owner_ref, *refs)
-
-    operands = [both, kept, *pieces, total, came]
+            for part in range(2):
+                first = part * columns + h * HEAD_SIZE
+                area = (
+                    slice(r * count_rows, (r + 1) * count_rows),
+                    slice(first, first + HEAD_SIZE),
+                )
+                rows = total[area] + came[area]
+                if part == 0:
+                    half = HEAD_SIZE // 2
+                    turned = jnp.concatenate([rows[:, half:], rows[:, :half]], 1)
+                    rows = rows * cosine[...] + turned * sine[...]
+                scratch[...] = jnp.where(live, rows, 0.0)
+                peer = owner[r * KEY_VALUE_HEADS + h]
+                lanes = slice(part * HEAD_SIZE, (part + 1) * HEAD_SIZE)
+                for b in range(2):
+                    picked = scratch[pl.ds(b, count_rows // 2, stride=2), :]
+                    out[peer * 2 + b, :, lanes] = picked.astype(jnp.bfloat16)
+
+
+def outgoing_rows(place, lengths, owner, total, came, turn):
+    count_rows = total.shape[0] // lengths.shape[0]
+    out = (owner.shape[0] * 2, count_rows // 2, 2 * HEAD_SIZE)
     return pl.pallas_call(
-        kernel,
-        in_specs=[SMEM_REF] * 3
-        + [ANY_REF] * (1 + len(operands))
-        + [VMEM_REF] * len(turn),
+        rows_kernel,
+        in_specs=[SMEM_REF] * 3 + [VMEM_REF] * 4,
         out_specs=VMEM_REF,
-        out_shape=out,
-        scratch_shapes=[
-            pltpu.VMEM((rows, 2 * count * depth), kept.dtype),
-            pltpu.VMEM((2 * count * depth, columns), kept.dtype),
-            pltpu.VMEM((rows, columns), jnp.float32),
-            pltpu.VMEM((rows, columns), jnp.float32),
-            pltpu.VMEM((count_rows, HEAD_SIZE), jnp.float32),
-            pltpu.SemaphoreType.DMA((2 + 4 * count,)),
-        ],
-        compiler_params=PARAMS,
+        out_shape=jax.ShapeDtypeStruct(out, jnp.bfloat16),
+        scratch_shapes=[pltpu.VMEM((count_rows, HEAD_SIZE), jnp.float32)],
+        compiler_params=SMALL,
         cost_estimate=cost(1000, 1000),
         name="cache_rows",
-    )(place, lengths, owner, token, *operands, *turn)
+    )(place, lengths, owner, total, came, *turn)
+
+
+def decode_kernel(place, cache, query, new_keys, new_value, out):
+    slots, queries = cache.shape[0], query.shape[0]
+    block, length = place[0], place[1]
+    contract = (((1,), (1,)), ((), ()))
+    scale = 1.0 / HEAD_SIZE**0.5
+    old = lax.dot_general(
+        query[...], cache[:, :HEAD_SIZE], contract, preferred_element_type=jnp.float32
+    )
+    slot = lax.broadcasted_iota(jnp.int32, old.shape, 1) * 2 + block
+    old = jnp.where(slot < length, old * scale, -1e30)
+    new = lax.dot_general(query[...], new_keys[...], contract, preferred_element_type=jnp.float32)
+    step = lax.broadcasted_iota(jnp.int32, new.shape, 0) // QPK
+    token = lax.broadcasted_iota(jnp.int32, new.shape, 1)
+    new = jnp.where((token <= step) & (block == 0), new * scale, -1e30)
+    top = jnp.maximum(jnp.max(old, 1, keepdims=True), jnp.max(new, 1, keepdims=True))
+    old, new = jnp.exp(old - top), jnp.exp(new - top)
+    total = jnp.sum(old, 1, keepdims=True) + jnp.sum(new, 1, keepdims=True)
+    sums = jnp.dot(
+        old.astype(jnp.bfloat16), cache[:, HEAD_SIZE:], preferred_element_type=jnp.float32
+    )
+    out[:, :HEAD_SIZE] = sums + jnp.dot(
+        new.astype(jnp.bfloat16), new_value[...], preferred_element_type=jnp.float32
+    )
+    half = (queries, HEAD_SIZE // 2)
+    out[:, HEAD_SIZE : HEAD_SIZE + half[1]] = jnp.broadcast_to(top, half)
+    out[:, HEAD_SIZE + half[1] :] = jnp.broadcast_to(total, half)
+
+
+def decoded(block, length, cache, query, new_keys, new_value):
+    pad = ((0, 16 - STEPS), (0, 0))
+    new_keys, new_value = jnp.pad(new_keys, pad), jnp.pad(new_value, pad)
+    mine = pl.pallas_call(
+        decode_kernel,
+        in_specs=[SMEM_REF] + [VMEM_REF] * 4,
+        out_specs=VMEM_REF,
+        out_shape=jax.ShapeDtypeStruct((STEPS * QPK, 2 * HEAD_SIZE), jnp.float32),
+        compiler_params=SMALL,
+        cost_estimate=cost(1000, 1000),
+        name="decode",
+    )(jnp.stack([block, length]), cache, query, new_keys, new_value)
+    theirs = moved(mine, to_core)
+    share = QPK // 2
+
+    def heads(array):
+        array = array.reshape(STEPS, QPK, 2 * HEAD_SIZE)
+        array = lax.dynamic_slice_in_dim(array, block * share, share, 1)
+        last = HEAD_SIZE + HEAD_SIZE // 2
+        return array[..., :HEAD_SIZE], array[..., HEAD_SIZE : HEAD_SIZE + 1], array[..., last : last + 1]
+
+    sums_a, top_a, total_a = heads(mine)
+    sums_b, top_b, total_b = heads(theirs)
+    top = jnp.maximum(top_a, top_b)
+    scale_a, scale_b = jnp.exp(top_a - top), jnp.exp(top_b - top)
+    sums = sums_a * scale_a + sums_b * scale_b
+    return (sums / (total_a * scale_a + total_b * scale_b)).reshape(STEPS, share * HEAD_SIZE)
 
 
 HERE, THERE = 3, 7
@@ -410,15 +420,12 @@
         )
         columns = key_weight.shape[1]
 
-        def parts_of(block):
-            return [block[:, k * columns : (k + 1) * columns] for k in range(2)]
-
-        sent = weight_half(place, 0, key_weight, value_weight)
+        sent = weight_half(group_id, key_weight, value_weight)
         near = moved(sent, to_pair)
         middle = moved(sent, to_middle)
         across = moved(sent, to_row)
         other = moved(flat, to_core)
-        rest = weight_half(place, 1, key_weight, after(value_weight, sent))
+        rest = weight_half(1 - group_id, key_weight, after(value_weight, sent))
         came = (near, middle, across, other, rest, *turn, query_rot, new_keys)
         end_b = moved(after(middle, *came), to_end)
         middle_c = moved(after(near, *came), to_middle)
@@ -432,42 +439,31 @@
         block_xb = moved(block_b, to_group)
         pieces = [(HERE, 0, sent), (HERE, 1, rest), (THERE, 0, across), (THERE, 1, across_x)]
         pieces += [(HERE + 1, 0, near), (THERE + 1, 0, near_y)]
-        totals = product(place, after(both, *came), pieces, (), 3, 2 * columns, 2)
-        ends_x = parts_of(after(across_x, *came))
-        came = (end_c, block_yb, block_xb, totals[0], *ends_x)
+        totals = product(place, after(both, *came), pieces, (), 3, 2 * columns, 1)
+        came = (end_c, block_yb, block_xb, totals[0])
         near_rest = moved(after(rest, *came), to_pair)
-        block_c = parts_of(jnp.where(is_end, after(end_c, *came), middle_c))
-        block_xc = [moved(block_c[0], to_group)]
-        block_yc = [moved(block_c[0], to_row)]
-        block_xc.append(moved(block_c[1], to_group))
-        block_yc.append(moved(block_c[1], to_row))
+        block_c = jnp.where(is_end, after(end_c, *came), middle_c)
+        block_xc = moved(block_c, to_group)
+        block_yc = moved(block_c, to_row)
         pieces = [(HERE + 2, 0, block_b), (HERE + 2, 1, block_xb)]
-        pieces += [(THERE + 2, 0, block_yb), (HERE + 3, 0, *block_c)]
-        totals = product(place, after(both, *came), pieces, totals, 4, 2 * columns, 2)
-        ends_yb = parts_of(after(block_yb, *came))
-        came = (near_rest, *block_xc, *block_yc, totals[0], *ends_yb)
-        ends = []
-        for k in range(2):
-            near_xy = moved(after(ends_x[k], *came), to_pair)
-            ends.append([near_xy, moved(after(ends_yb[k], *came), to_group)])
-            ends[k].append(moved(after(block_xc[k], *came), to_row))
-        pieces = [(HERE + 1, 1, near_rest), (HERE + 3, 1, *block_xc), (THERE + 3, 0, *block_yc)]
-        totals = product(place, after(both, ends[0][1]), pieces, totals, 3, 2 * columns, 2)
-        plan = [(THERE + 1, 1), (THERE + 2, 1), (THERE + 3, 1)]
-        caches = []
-        token = place
-        for k, turned in enumerate((turn, ())):
-            given = moved(after(totals[2 * k + 1], token), to_core)
-            swapped_ends = [moved(end, to_core) for end in ends[k]]
-            pieces = [piece for pair in zip(ends[k], swapped_ends) for piece in pair]
-            outgoing = outgoing_rows(
-                place, lengths, owner, both, kept, plan, pieces, totals[2 * k], given, turned, token
-            )
-            caches.append(
-                lax.all_to_all(outgoing, "seq", split_axis=0, concat_axis=1, tiled=True)[0]
-            )
-            token = outgoing
-        cache_keys, cache_values = caches
+        pieces += [(THERE + 2, 0, block_yb), (HERE + 3, 0, block_c)]
+        total, given = product(place, after(both, *came), pieces, totals, 4, 2 * columns, 1)
+        came = (near_rest, block_xc, block_yc, total)
+        ends = [moved(after(across_x, *came), to_pair), moved(after(block_yb, *came), to_group)]
+        ends.append(moved(after(block_xc, *came), to_row))
+        pieces = [(HERE + 1, 1, near_rest), (HERE + 3, 1, block_xc), (THERE + 3, 0, block_yc)]
+        totals = product(place, after(both, *came), pieces, (total, given), 3, 2 * columns, 1)
+        came = (*ends, *totals)
+        spots = (THERE + 1, THERE + 2, THERE + 3)
+        pieces = [(spot, 1, after(end, *came)) for spot, end in zip(spots, ends)]
+        total, given = product(place, both, pieces, totals, 3, 2 * columns, 1, SMALL)
+        outgoing = outgoing_rows(place, lengths, owner, total, moved(given, to_core), turn)
+        incoming = lax.all_to_all(outgoing, "seq", split_axis=0, concat_axis=1, tiled=True)
+        mine = decoded(
+            device_id % 2, length, incoming[0], query_rot.reshape(STEPS * QPK, HEAD_SIZE),
+            new_keys, new_value,
+        )
+        return (incoming, mine.astype(jnp.bfloat16))
     else:
         shape = (count_requests, count_rows, KEY_VALUE_HEADS, HEAD_SIZE)
         unrotated_key = project(key_weight).reshape(shape)

time: 143 us -> 118 us (0.83)
  starting transfers between devices: 38.7 us -> 23.3 us
  Pallas kernels: 40.9 us -> 33.4 us
  local copies, waits for them, and re-layouts: 4.7 us -> 8.57 us
  waiting for transfers between devices: 44.4 us -> 41.2 us
    pallas_call x4 -> x2, Pallas kernels: 14.2 us -> 2.91 us  [the longest x1 1.88 us: outgoing_rows(): pl.pallas_call(rows_kernel, in_specs=[SMEM_REF] * 3 + [VMEM_REF] * 4, out...]
    ppermute x30 -> x19, starting transfers between devices: 28.2 us -> 18.4 us  [moved(): return lax.ppermute(block, ('groups', 'seq'), route)]
    ppermute x30 -> x19, waiting for transfers between devices: 34.7 us -> 25.5 us  [moved(): return lax.ppermute(block, ('groups', 'seq'), route)]
    all_to_all x2 -> x1, waiting for transfers between devices: 7.88 us -> 15.8 us  [body(): lax.all_to_all(outgoing, 'seq', split_axis=0, concat_axis=1, tiled=True)]
    unnamed x72 -> x51, local copies, waits for them, and re-layouts: 1.93 us -> 6.65 us
    all_to_all x2 -> x1, starting transfers between devices: 9.52 us -> 4.95 us  [body(): lax.all_to_all(outgoing, 'seq', split_axis=0, concat_axis=1, tiled=True)]
    pallas_call x3 -> x4, Pallas kernels: 17.3 us -> 21.1 us  [product(): pl.pallas_call(functools.partial(product_kernel, plan, group, parts, bool...]
    slice x3 -> x0, local copies, waits for them, and re-layouts: 2.17 us -> none  [parts_of(): return [block[:, k * columns:(k + 1) * columns] for k in range(2)]]
  transfers between devices with their start and end apart: 35 -> 20, of which waited for: 18 -> 11; matrix products, arithmetic and copies ran while one was open for 7% -> 8% of each run, Pallas kernels for 22% -> 24%
where the time goes in v11:
time: 118 us; the launch traced here: 117 us
  waiting for transfers between devices  41.2 us (35%)
  Pallas kernels  33.4 us (28%)
  starting transfers between devices  23.3 us (20%)
  local copies, waits for them, and re-layouts  8.57 us (7%)
  other arithmetic  7.29 us (6%)
  between operations  3.62 us (3%)
    ppermute x19, waiting for transfers between devices, moved(): return lax.ppermute(block, ('groups', 'seq'), route)  25.5 us
    pallas_call x4, Pallas kernels, product(): pl.pallas_call(functools.partial(product_kernel, plan, group, parts, bool...  21.1 us
    ppermute x19, starting transfers between devices, moved(): return lax.ppermute(block, ('groups', 'seq'), route)  18.4 us
    all_to_all x1, waiting for transfers between devices, body(): lax.all_to_all(outgoing, 'seq', split_axis=0, concat_axis=1, tiled=True)  15.8 us
    pallas_call x1, Pallas kernels, prepared(): pl.pallas_call(prepare_kernel, grid_spec=pltpu.PrefetchScalarGridSpec(num...  9.4 us
    unnamed x51, local copies, waits for them, and re-layouts  6.65 us
    all_to_all x1, starting transfers between devices, body(): lax.all_to_all(outgoing, 'seq', split_axis=0, concat_axis=1, tiled=True)  4.95 us
  transfers between devices with their start and end apart: 20, of which 11 were waited for; matrix products, arithmetic and copies ran while one was open for 8% of the time, Pallas kernels for 24%

profile of v11, /device:TPU:0, one launch (start us, length us, event | category | flops | bytes accessed | tf_op | source)
XLA Modules:
  0.0 117.4 jit_solution(4292539339337511981)
XLA Ops:
  0.6 0.0 copy-start
  0.6 0.5 collective-permute-start.3
  1.2 1.2 %constant_dynamic-slice_fusion.3 = (bf16[256,512]{1,0:T(8,128)(2,1)S(1)}, bf16[256,512]{1,0:T(8,128)(2,1)S(1)}, bf16[256,512]{1,0:T(8,128)(2,1)S(1)}) fusion(bf16[512,512]{1,0:T(8,128)(2,1)} %param.11, s32[]{:T(128)S(6)} %select_n.77, s32[]{:T(128)S(6)} %select_n.76, bf16[512,512]{1,0:T(8,128)(2,1)} %param.12), kind=kLoop, calls=%fused_computation.33 | loop fusion | bytes 1572872 | tf_op jit(solution)/shard_map/dynamic_slice | solution.py:113
  2.4 0.0 copy-start.9
  2.4 0.1 pad_maximum_fusion.refs_0_
  2.5 2.7 %collective-permute-start = (bf16[256,1024]{1,0:T(8,128)(2,1)S(1)}, bf16[256,1024]{1,0:T(8,128)(2,1)S(1)}, u32[]{:S(2)}, u32[]{:S(2)}) collective-permute-start(bf16[256,1024]{1,0:T(8,128)(2,1)S(1)} %pad_maximum_fusion.refs_0_), channel_id=1, source_target_pairs={{0,4},{1,5},{2,6},{3,7},{4,0},{5,1},{6,2},{7,3},{8,12},{9,13},{10,... | collective-permute-start | bytes 1572872 | tf_op jit(solution)/shard_map/ppermute | solution.py:66
  5.1 0.7 collective-permute-start.1
  5.8 1.6 %collective-permute-start.2 = (bf16[256,1024]{1,0:T(8,128)(2,1)S(1)}, bf16[256,1024]{1,0:T(8,128)(2,1)}, u32[]{:S(2)}, u32[]{:S(2)}) collective-permute-start(bf16[256,1024]{1,0:T(8,128)(2,1)S(1)} %pad_maximum_fusion.refs_0_), channel_id=1, source_target_pairs={{0,2},{1,3},{2,0},{3,1},{4,6},{5,7},{6,4},{7,5},{8,10},{9,11},{10,... | collective-permute-start | bytes 1572872 | tf_op jit(solution)/shard_map/ppermute | solution.py:66
  7.4 0.6 fusion.12
  10.0 0.7 convert_bitcast_fusion
  11.4 0.6 fusion.13
  12.0 0.6 add_convert_fusion.3
  12.7 0.7 fusion.10
  13.4 0.1 subtract_convert_fusion.1
  13.5 0.7 subtract_convert_fusion
  14.1 0.4 fusion
  14.5 0.6 pad_maximum_fusion.6
  15.2 0.1 pad_maximum_fusion.2
  15.3 0.9 pad_maximum_fusion.1.refs_1_
  16.2 1.5 %collective-permute-done.refs_4_ = bf16[256,1024]{1,0:T(8,128)(2,1)S(1)} collective-permute-done((bf16[256,1024]{1,0:T(8,128)(2,1)S(1)}, bf16[256,1024]{1,0:T(8,128)(2,1)S(1)}, u32[]{:S(2)}, u32[]{:S(2)}) %collective-permute-start) | collective-permute-done | bytes 524320 | tf_op jit(solution)/shard_map/ppermute | solution.py:66
  17.7 2.3 %collective-permute-done.2.refs_2_ = bf16[256,1024]{1,0:T(8,128)(2,1)} collective-permute-done((bf16[256,1024]{1,0:T(8,128)(2,1)S(1)}, bf16[256,1024]{1,0:T(8,128)(2,1)}, u32[]{:S(2)}, u32[]{:S(2)}) %collective-permute-start.2) | collective-permute-done | bytes 524320 | tf_op jit(solution)/shard_map/ppermute | solution.py:66
  20.0 1.5 %collective-permute-start.4 = (bf16[256,1024]{1,0:T(8,128)(2,1)}, bf16[256,1024]{1,0:T(8,128)(2,1)}, u32[]{:S(2)}, u32[]{:S(2)}) collective-permute-start(bf16[256,1024]{1,0:T(8,128)(2,1)} %collective-permute-done.2.refs_2_), channel_id=1, source_target_pairs={{0,16},{1,17},{2,18},{3,19},{4,20},{5,21},{6,22},{7,23},{8,24},{9,... | collective-permute-start | bytes 1572872 | tf_op jit(solution)/shard_map/ppermute | solution.py:66
  21.5 0.7 collective-permute-start.5
  22.2 1.3 %collective-permute-start.6 = (bf16[256,1024]{1,0:T(8,128)(2,1)S(1)}, bf16[256,1024]{1,0:T(8,128)(2,1)S(1)}, u32[]{:S(2)}, u32[]{:S(2)}) collective-permute-start(bf16[256,1024]{1,0:T(8,128)(2,1)S(1)} %collective-permute-done.1), channel_id=1, source_target_pairs={{4,0},{5,1},{6,2},{7,3},{8,12},{9,13},{10,14},{11,15},{20,16},{21,... | collective-permute-start | bytes 1572872 | tf_op jit(solution)/shard_map/ppermute | solution.py:66
  23.5 1.6 %collective-permute-start.7 = (bf16[256,1024]{1,0:T(8,128)(2,1)S(1)}, bf16[256,1024]{1,0:T(8,128)(2,1)}, u32[]{:S(2)}, u32[]{:S(2)}) collective-permute-start(bf16[256,1024]{1,0:T(8,128)(2,1)S(1)} %collective-permute-done.refs_4_), channel_id=1, source_target_pairs={{0,2},{1,3},{2,0},{3,1},{4,6},{5,7},{6,4},{7,5},{8,10},{9,11},{10,... | collective-permute-start | bytes 1572872 | tf_op jit(solution)/shard_map/ppermute | solution.py:66
  25.1 0.7 stack.54.place
  25.8 9.4 %normed_halves.1 = (bf16[16,2,320,256]{3,2,1,0:T(8,128)(2,1)}, bf16[16,320,256]{2,1,0:T(8,128)(2,1)}) custom-call(s32[11]{0:T(128)} %stack.54.place, bf16[320,8192]{1,0:T(8,128)(2,1)} %bitcast.42, bf16[320,8192]{1,0:T(8,128)(2,1)} %collective-permute-done.3.refs_1_), custom_call_target="tpu_custom_call" | custom-call | flops 1000 | bytes 1000 | tf_op jit(solution)/shard_map/normed_halves/pallas_call | solution.py:147
  35.2 4.8 %collective-permute-done.6 = bf16[256,1024]{1,0:T(8,128)(2,1)S(1)} collective-permute-done((bf16[256,1024]{1,0:T(8,128)(2,1)S(1)}, bf16[256,1024]{1,0:T(8,128)(2,1)S(1)}, u32[]{:S(2)}, u32[]{:S(2)}) %collective-permute-start.6) | collective-permute-done | bytes 524320 | tf_op jit(solution)/shard_map/ppermute | solution.py:66
  40.0 0.1 broadcast_select_fusion.1.refs_0_
  40.1 1.6 %collective-permute-start.9 = (bf16[256,1024]{1,0:T(8,128)(2,1)S(1)}, bf16[256,1024]{1,0:T(8,128)(2,1)S(1)}, u32[]{:S(2)}, u32[]{:S(2)}) collective-permute-start(bf16[256,1024]{1,0:T(8,128)(2,1)S(1)} %broadcast_select_fusion.1.refs_0_), channel_id=1, source_target_pairs={{0,2},{1,3},{2,0},{3,1},{4,6},{5,7},{6,4},{7,5},{8,10},{9,11},{10,... | collective-permute-start | bytes 1572872 | tf_op jit(solution)/shard_map/ppermute | solution.py:66
  41.6 0.5 collective-permute-start.10
  42.2 1.3 %collective-permute-start.8 = (bf16[256,1024]{1,0:T(8,128)(2,1)S(1)}, bf16[256,1024]{1,0:T(8,128)(2,1)S(1)}, u32[]{:S(2)}, u32[]{:S(2)}) collective-permute-start(bf16[256,1024]{1,0:T(8,128)(2,1)S(1)} %collective-permute-done.5), channel_id=1, source_target_pairs={{4,0},{5,1},{6,2},{7,3},{8,12},{9,13},{10,14},{11,15},{20,16},{21,... | collective-permute-start | bytes 1572872 | tf_op jit(solution)/shard_map/ppermute | solution.py:66
  43.5 6.3 %add_product.4 = (f32[320,1024]{1,0:T(8,128)}, f32[320,1024]{1,0:T(8,128)}) custom-call(s32[11]{0:T(128)} %stack.54.place, bf16[16,2,320,256]{3,2,1,0:T(8,128)(2,1)} %get-tuple-element.47.both, bf16[256,1024]{1,0:T(8,128)(2,1)} %copy-done.10, bf16[256,1024]{1,0:T(8,128)(2,1)} %pad_maximum_fusion.1.refs_1_, bf16[256,1024]{1,0:T(8,128)(2,1)} %collective-permute-done.2.refs_2_, ...), custom_call_target="tpu_custom_call" | custom-call | flops 68719476736 | bytes 1000 | tf_op jit(solution)/shard_map/add_product/pallas_call | solution.py:230
  49.8 5.7 %collective-permute-done.8 = bf16[256,1024]{1,0:T(8,128)(2,1)S(1)} collective-permute-done((bf16[256,1024]{1,0:T(8,128)(2,1)S(1)}, bf16[256,1024]{1,0:T(8,128)(2,1)S(1)}, u32[]{:S(2)}, u32[]{:S(2)}) %collective-permute-start.8) | collective-permute-done | bytes 524320 | tf_op jit(solution)/shard_map/ppermute | solution.py:66
  55.5 0.1 broadcast_select_fusion.refs_3_
  55.6 1.6 %collective-permute-start.12 = (bf16[256,1024]{1,0:T(8,128)(2,1)S(1)}, bf16[256,1024]{1,0:T(8,128)(2,1)S(1)}, u32[]{:S(2)}, u32[]{:S(2)}) collective-permute-start(bf16[256,1024]{1,0:T(8,128)(2,1)S(1)} %broadcast_select_fusion.refs_3_), channel_id=1, source_target_pairs={{0,16},{1,17},{2,18},{3,19},{4,20},{5,21},{6,22},{7,23},{8,24},{9,... | collective-permute-start | bytes 1572872 | tf_op jit(solution)/shard_map/ppermute | solution.py:66
  57.2 0.5 collective-permute-start.13
  57.7 6.5 %add_product.5 = (f32[320,1024]{1,0:T(8,128)}, f32[320,1024]{1,0:T(8,128)}) custom-call(s32[11]{0:T(128)} %stack.54.place, bf16[16,2,320,256]{3,2,1,0:T(8,128)(2,1)} %get-tuple-element.47.both, bf16[256,1024]{1,0:T(8,128)(2,1)} %copy-done.12, bf16[256,1024]{1,0:T(8,128)(2,1)} %copy-done.21, bf16[256,1024]{1,0:T(8,128)(2,1)} %copy-done.19, ...), custom_call_target="tpu_custom_call" | custom-call | flops 68719476736 | bytes 1000 | tf_op jit(solution)/shard_map/add_product/pallas_call | solution.py:230
  64.2 5.3 %collective-permute-done.11.refs_0_ = bf16[256,1024]{1,0:T(8,128)(2,1)S(1)} collective-permute-done((bf16[256,1024]{1,0:T(8,128)(2,1)S(1)}, bf16[256,1024]{1,0:T(8,128)(2,1)S(1)}, u32[]{:S(2)}, u32[]{:S(2)}) %collective-permute-start.11) | collective-permute-done | bytes 524320 | tf_op jit(solution)/shard_map/ppermute | solution.py:66
  69.5 0.1 collective-permute-start.14
  69.6 0.6 collective-permute-start.15
  70.2 1.5 %collective-permute-start.16 = (bf16[256,1024]{1,0:T(8,128)(2,1)S(1)}, bf16[256,1024]{1,0:T(8,128)(2,1)S(1)}, u32[]{:S(2)}, u32[]{:S(2)}) collective-permute-start(bf16[256,1024]{1,0:T(8,128)(2,1)S(1)} %collective-permute-done.12.refs_1_), channel_id=1, source_target_pairs={{0,2},{1,3},{2,0},{3,1},{4,6},{5,7},{6,4},{7,5},{8,10},{9,11},{10,... | collective-permute-start | bytes 1572872 | tf_op jit(solution)/shard_map/ppermute | solution.py:66
  71.7 5.9 %add_product.6 = (f32[320,1024]{1,0:T(8,128)}, f32[320,1024]{1,0:T(8,128)}) custom-call(s32[11]{0:T(128)} %stack.54.place, bf16[16,2,320,256]{3,2,1,0:T(8,128)(2,1)} %get-tuple-element.47.both, bf16[256,1024]{1,0:T(8,128)(2,1)} %copy-done.23, bf16[256,1024]{1,0:T(8,128)(2,1)} %copy-done.20, bf16[256,1024]{1,0:T(8,128)(2,1)} %copy-done.22, ...), custom_call_target="tpu_custom_call" | custom-call | flops 68719476736 | bytes 1000 | tf_op jit(solution)/shard_map/add_product/pallas_call | solution.py:230
  77.7 1.3 %collective-permute-done.14.refs_0_ = bf16[256,1024]{1,0:T(8,128)(2,1)S(1)} collective-permute-done((bf16[256,1024]{1,0:T(8,128)(2,1)}, bf16[256,1024]{1,0:T(8,128)(2,1)S(1)}, u32[]{:S(2)}, u32[]{:S(2)}) %collective-permute-start.14) | collective-permute-done | bytes 524320 | tf_op jit(solution)/shard_map/ppermute | solution.py:66
  78.9 0.1 collective-permute-done.15.refs_1_
  79.0 0.3 collective-permute-done.16.refs_2_
  79.4 2.5 %copy-done.6 = bf16[16,2,320,256]{3,2,1,0:T(8,128)(2,1)S(1)} copy-done((bf16[16,2,320,256]{3,2,1,0:T(8,128)(2,1)S(1)}, bf16[16,2,320,256]{3,2,1,0:T(8,128)(2,1)}, u32[]{:S(2)}) %copy-start.6) | copy-done | bytes 5242904
  81.8 1.3 %copy-done.7 = f32[320,1024]{1,0:T(8,128)S(1)} copy-done((f32[320,1024]{1,0:T(8,128)S(1)}, f32[320,1024]{1,0:T(8,128)}, u32[]{:S(2)}) %copy-start.7) | copy-done | bytes 1310744
  83.2 1.3 %copy-done.8 = f32[320,1024]{1,0:T(8,128)S(1)} copy-done((f32[320,1024]{1,0:T(8,128)S(1)}, f32[320,1024]{1,0:T(8,128)}, u32[]{:S(2)}) %copy-start.8) | copy-done | bytes 1310744
  84.5 2.4 %add_product.7 = (f32[320,1024]{1,0:T(8,128)S(1)}, f32[320,1024]{1,0:T(8,128)S(1)}) custom-call(s32[11]{0:T(128)S(1)} %copy-done.1, bf16[16,2,320,256]{3,2,1,0:T(8,128)(2,1)S(1)} %copy-done.6, bf16[256,1024]{1,0:T(8,128)(2,1)S(1)} %collective-permute-done.14.refs_0_, bf16[256,1024]{1,0:T(8,128)(2,1)S(1)} %collective-permute-done.15.refs_1_, ...), custom_call_target="tpu_custom_call" | custom-call | flops 68719476736 | bytes 1000 | tf_op jit(solution)/shard_map/add_product/pallas_call | solution.py:230
  86.8 0.1 collective-permute-start.17
  86.9 3.0 %collective-permute-done.17.came = f32[320,1024]{1,0:T(8,128)S(1)} collective-permute-done((f32[320,1024]{1,0:T(8,128)S(1)}, f32[320,1024]{1,0:T(8,128)S(1)}, u32[]{:S(2)}, u32[]{:S(2)}) %collective-permute-start.17) | collective-permute-done | bytes 1310752 | tf_op jit(solution)/shard_map/ppermute | solution.py:66
  90.0 1.9 %cache_rows.1 = bf16[16,80,256]{2,1,0:T(8,128)(2,1)} custom-call(s32[11]{0:T(128)S(1)} %copy-done.1, s32[2]{0:T(128)S(1)} %copy-done.3, s32[8]{0:T(128)S(1)} %copy-done.5, f32[320,1024]{1,0:T(8,128)S(1)} %get-tuple-element.54.total, f32[320,1024]{1,0:T(8,128)S(1)} %collective-permute-done.17.came, f32[160,128]{1,0:T(8,128)S(1)} %get-tuple-element.71.cosine, ...), custom_call_target="tpu_custom_call" | custom-call | flops 1000 | bytes 1000 | tf_op jit(solution)/shard_map/cache_rows/pallas_call | solution.py:277
  91.8 4.9 %all-to-all-start = ((bf16[16,80,256]{2,1,0:T(8,128)(2,1)}), bf16[16,80,256]{2,1,0:T(8,128)(2,1)S(1)}, u32[]{:S(2)}, u32[]{:S(2)}) async-start(bf16[16,80,256]{2,1,0:T(8,128)(2,1)} %cache_rows.1), calls=%async_computation | async-start | bytes 1310720 | tf_op jit(solution)/shard_map/all_to_all | solution.py:461
  96.9 0.7 pad_add_fusion.place
  97.6 0.1 pad_maximum_fusion.5.query
  97.6 15.8 %all-to-all-done = bf16[16,80,256]{2,1,0:T(8,128)(2,1)S(1)} async-done(((bf16[16,80,256]{2,1,0:T(8,128)(2,1)}), bf16[16,80,256]{2,1,0:T(8,128)(2,1)S(1)}, u32[]{:S(2)}, u32[]{:S(2)}) %all-to-all-start) | async-done | bytes 655392 | tf_op jit(solution)/shard_map/all_to_all | solution.py:461
  113.4 1.0 decode.1
  114.4 0.1 collective-permute-start.18
  114.6 1.1 collective-permute-done.18
  115.7 0.2 fusion.15
  115.9 0.1 fusion.8
  116.0 0.6 copy.20
  116.6 0.8 copy.22
  (59 shorter events, 0.2 us)
Async XLA Ops:
  0.6 96.2 %copy-start = (bf16[8,4,128]{2,1,0:T(4,128)(2,1)S(1)}, bf16[8,4,128]{2,1,0:T(4,128)(2,1)}, u32[]{:S(2)}) copy-start(bf16[8,4,128]{2,1,0:T(4,128)(2,1)} %param.17) | copy-start | bytes 24580
  0.6 19.4 %collective-permute-start.3 = (bf16[320,8192]{1,0:T(8,128)(2,1)}, bf16[320,8192]{1,0:T(8,128)(2,1)}, u32[]{:S(2)}, u32[]{:S(2)}) collective-permute-start(bf16[320,8192]{1,0:T(8,128)(2,1)} %bitcast.41), channel_id=1, source_target_pairs={{0,1},{1,0},{2,3},{3,2},{4,5},{5,4},{6,7},{7,6},{8,9},{9,8},{10,11... | collective-permute-start | bytes 15728648 | tf_op jit(solution)/shard_map/ppermute | solution.py:66
  1.2 6.2 %copy-start.4 = (s32[8]{0:T(128)S(1)}, s32[8]{0:T(128)}, u32[]{:S(2)}) copy-start(s32[8]{0:T(128)} %owner.1) | copy-start | bytes 100
  1.2 10.2 %copy-start.2 = (s32[2]{0:T(128)S(1)}, s32[2]{0:T(128)}, u32[]{:S(2)}) copy-start(s32[2]{0:T(128)} %lengths.1) | copy-start | bytes 28
  1.2 12.2 %copy-start.17 = (f32[64]{0:T(128)S(1)}, f32[64]{0:T(128)}, u32[]{:S(2)}) copy-start(f32[64]{0:T(128)} %constant.84.clone) | copy-start | bytes 772
  2.4 12.9 %copy-start.9 = (bf16[512,512]{1,0:T(8,128)(2,1)S(1)}, bf16[512,512]{1,0:T(8,128)(2,1)}, u32[]{:S(2)}) copy-start(bf16[512,512]{1,0:T(8,128)(2,1)} %param.12) | copy-start | bytes 1572868
  2.4 32.7 %copy-start.10 = (bf16[256,1024]{1,0:T(8,128)(2,1)}, bf16[256,1024]{1,0:T(8,128)(2,1)S(1)}, u32[]{:S(2)}) copy-start(bf16[256,1024]{1,0:T(8,128)(2,1)S(1)} %pad_maximum_fusion.refs_0_) | copy-start | bytes 1572868
  2.5 15.2 %collective-permute-start = (bf16[256,1024]{1,0:T(8,128)(2,1)S(1)}, bf16[256,1024]{1,0:T(8,128)(2,1)S(1)}, u32[]{:S(2)}, u32[]{:S(2)}) collective-permute-start(bf16[256,1024]{1,0:T(8,128)(2,1)S(1)} %pad_maximum_fusion.refs_0_), channel_id=1, source_target_pairs={{0,4},{1,5},{2,6},{3,7},{4,0},{5,1},{6,2},{7,3},{8,12},{9,13},{10,... | collective-permute-start | bytes 1572872 | tf_op jit(solution)/shard_map/ppermute | solution.py:66
  5.1 12.6 %collective-permute-start.1 = (bf16[256,1024]{1,0:T(8,128)(2,1)S(1)}, bf16[256,1024]{1,0:T(8,128)(2,1)S(1)}, u32[]{:S(2)}, u32[]{:S(2)}) collective-permute-start(bf16[256,1024]{1,0:T(8,128)(2,1)S(1)} %pad_maximum_fusion.refs_0_), channel_id=1, source_target_pairs={{4,8},{5,9},{6,10},{7,11},{8,4},{9,5},{10,6},{11,7},{20,24},{21,25... | collective-permute-start | bytes 1572872 | tf_op jit(solution)/shard_map/ppermute | solution.py:66
  5.8 14.2 %collective-permute-start.2 = (bf16[256,1024]{1,0:T(8,128)(2,1)S(1)}, bf16[256,1024]{1,0:T(8,128)(2,1)}, u32[]{:S(2)}, u32[]{:S(2)}) collective-permute-start(bf16[256,1024]{1,0:T(8,128)(2,1)S(1)} %pad_maximum_fusion.refs_0_), channel_id=1, source_target_pairs={{0,2},{1,3},{2,0},{3,1},{4,6},{5,7},{6,4},{7,5},{8,10},{9,11},{10,... | collective-permute-start | bytes 1572872 | tf_op jit(solution)/shard_map/ppermute | solution.py:66
  17.7 17.5 %copy-start.18 = (bf16[256,1024]{1,0:T(8,128)(2,1)}, bf16[256,1024]{1,0:T(8,128)(2,1)S(1)}, u32[]{:S(2)}) copy-start(bf16[256,1024]{1,0:T(8,128)(2,1)S(1)} %collective-permute-done.refs_4_) | copy-start | bytes 1572868
  20.0 15.1 %collective-permute-start.4 = (bf16[256,1024]{1,0:T(8,128)(2,1)}, bf16[256,1024]{1,0:T(8,128)(2,1)}, u32[]{:S(2)}, u32[]{:S(2)}) collective-permute-start(bf16[256,1024]{1,0:T(8,128)(2,1)} %collective-permute-done.2.refs_2_), channel_id=1, source_target_pairs={{0,16},{1,17},{2,18},{3,19},{4,20},{5,21},{6,22},{7,23},{8,24},{9,... | collective-permute-start | bytes 1572872 | tf_op jit(solution)/shard_map/ppermute | solution.py:66
  21.5 13.7 %collective-permute-start.5 = (bf16[256,1024]{1,0:T(8,128)(2,1)S(1)}, bf16[256,1024]{1,0:T(8,128)(2,1)S(1)}, u32[]{:S(2)}, u32[]{:S(2)}) collective-permute-start(bf16[256,1024]{1,0:T(8,128)(2,1)S(1)} %collective-permute-done.refs_4_), channel_id=1, source_target_pairs={{4,8},{5,9},{6,10},{7,11},{8,4},{9,5},{10,6},{11,7},{20,24},{21,25... | collective-permute-start | bytes 1572872 | tf_op jit(solution)/shard_map/ppermute | solution.py:66
  22.2 17.8 %collective-permute-start.6 = (bf16[256,1024]{1,0:T(8,128)(2,1)S(1)}, bf16[256,1024]{1,0:T(8,128)(2,1)S(1)}, u32[]{:S(2)}, u32[]{:S(2)}) collective-permute-start(bf16[256,1024]{1,0:T(8,128)(2,1)S(1)} %collective-permute-done.1), channel_id=1, source_target_pairs={{4,0},{5,1},{6,2},{7,3},{8,12},{9,13},{10,14},{11,15},{20,16},{21,... | collective-permute-start | bytes 1572872 | tf_op jit(solution)/shard_map/ppermute | solution.py:66
  23.5 16.5 %collective-permute-start.7 = (bf16[256,1024]{1,0:T(8,128)(2,1)S(1)}, bf16[256,1024]{1,0:T(8,128)(2,1)}, u32[]{:S(2)}, u32[]{:S(2)}) collective-permute-start(bf16[256,1024]{1,0:T(8,128)(2,1)S(1)} %collective-permute-done.refs_4_), channel_id=1, source_target_pairs={{0,2},{1,3},{2,0},{3,1},{4,6},{5,7},{6,4},{7,5},{8,10},{9,11},{10,... | collective-permute-start | bytes 1572872 | tf_op jit(solution)/shard_map/ppermute | solution.py:66
  40.0 9.7 %copy-start.12 = (bf16[256,1024]{1,0:T(8,128)(2,1)}, bf16[256,1024]{1,0:T(8,128)(2,1)S(1)}, u32[]{:S(2)}) copy-start(bf16[256,1024]{1,0:T(8,128)(2,1)S(1)} %broadcast_select_fusion.1.refs_0_) | copy-start | bytes 1572868
  40.1 15.5 %collective-permute-start.9 = (bf16[256,1024]{1,0:T(8,128)(2,1)S(1)}, bf16[256,1024]{1,0:T(8,128)(2,1)S(1)}, u32[]{:S(2)}, u32[]{:S(2)}) collective-permute-start(bf16[256,1024]{1,0:T(8,128)(2,1)S(1)} %broadcast_select_fusion.1.refs_0_), channel_id=1, source_target_pairs={{0,2},{1,3},{2,0},{3,1},{4,6},{5,7},{6,4},{7,5},{8,10},{9,11},{10,... | collective-permute-start | bytes 1572872 | tf_op jit(solution)/shard_map/ppermute | solution.py:66
  41.6 13.9 %collective-permute-start.10 = (bf16[256,1024]{1,0:T(8,128)(2,1)S(1)}, bf16[256,1024]{1,0:T(8,128)(2,1)S(1)}, u32[]{:S(2)}, u32[]{:S(2)}) collective-permute-start(bf16[256,1024]{1,0:T(8,128)(2,1)S(1)} %broadcast_select_fusion.1.refs_0_), channel_id=1, source_target_pairs={{0,16},{1,17},{2,18},{3,19},{4,20},{5,21},{6,22},{7,23},{8,24},{9,... | collective-permute-start | bytes 1572872 | tf_op jit(solution)/shard_map/ppermute | solution.py:66
  42.2 13.3 %collective-permute-start.8 = (bf16[256,1024]{1,0:T(8,128)(2,1)S(1)}, bf16[256,1024]{1,0:T(8,128)(2,1)S(1)}, u32[]{:S(2)}, u32[]{:S(2)}) collective-permute-start(bf16[256,1024]{1,0:T(8,128)(2,1)S(1)} %collective-permute-done.5), channel_id=1, source_target_pairs={{4,0},{5,1},{6,2},{7,3},{8,12},{9,13},{10,14},{11,15},{20,16},{21,... | collective-permute-start | bytes 1572872 | tf_op jit(solution)/shard_map/ppermute | solution.py:66
  49.8 7.9 %copy-start.11 = (bf16[256,1024]{1,0:T(8,128)(2,1)S(1)}, bf16[256,1024]{1,0:T(8,128)(2,1)}, u32[]{:S(2)}) copy-start(bf16[256,1024]{1,0:T(8,128)(2,1)} %pad_maximum_fusion.1.refs_1_) | copy-start | bytes 1572868
  55.5 2.2 %copy-start.19 = (bf16[256,1024]{1,0:T(8,128)(2,1)}, bf16[256,1024]{1,0:T(8,128)(2,1)S(1)}, u32[]{:S(2)}) copy-start(bf16[256,1024]{1,0:T(8,128)(2,1)S(1)} %collective-permute-done.9.refs_2_) | copy-start | bytes 1572868
  55.5 2.2 %copy-start.21 = (bf16[256,1024]{1,0:T(8,128)(2,1)}, bf16[256,1024]{1,0:T(8,128)(2,1)S(1)}, u32[]{:S(2)}) copy-start(bf16[256,1024]{1,0:T(8,128)(2,1)S(1)} %collective-permute-done.10.refs_1_) | copy-start | bytes 1572868
  55.6 2.1 %copy-start.13 = (bf16[256,1024]{1,0:T(8,128)(2,1)}, bf16[256,1024]{1,0:T(8,128)(2,1)S(1)}, u32[]{:S(2)}) copy-start(bf16[256,1024]{1,0:T(8,128)(2,1)S(1)} %broadcast_select_fusion.refs_3_) | copy-start | bytes 1572868
  55.6 13.9 %collective-permute-start.12 = (bf16[256,1024]{1,0:T(8,128)(2,1)S(1)}, bf16[256,1024]{1,0:T(8,128)(2,1)S(1)}, u32[]{:S(2)}, u32[]{:S(2)}) collective-permute-start(bf16[256,1024]{1,0:T(8,128)(2,1)S(1)} %broadcast_select_fusion.refs_3_), channel_id=1, source_target_pairs={{0,16},{1,17},{2,18},{3,19},{4,20},{5,21},{6,22},{7,23},{8,24},{9,... | collective-permute-start | bytes 1572872 | tf_op jit(solution)/shard_map/ppermute | solution.py:66
  57.2 12.3 %collective-permute-start.13 = (bf16[256,1024]{1,0:T(8,128)(2,1)S(1)}, bf16[256,1024]{1,0:T(8,128)(2,1)S(1)}, u32[]{:S(2)}, u32[]{:S(2)}) collective-permute-start(bf16[256,1024]{1,0:T(8,128)(2,1)S(1)} %broadcast_select_fusion.refs_3_), channel_id=1, source_target_pairs={{0,2},{1,3},{2,0},{3,1},{4,6},{5,7},{6,4},{7,5},{8,10},{9,11},{10,... | collective-permute-start | bytes 1572872 | tf_op jit(solution)/shard_map/ppermute | solution.py:66
  57.7 11.8 %collective-permute-start.11 = (bf16[256,1024]{1,0:T(8,128)(2,1)S(1)}, bf16[256,1024]{1,0:T(8,128)(2,1)S(1)}, u32[]{:S(2)}, u32[]{:S(2)}) collective-permute-start(bf16[256,1024]{1,0:T(8,128)(2,1)S(1)} %copy-done.11), channel_id=1, source_target_pairs={{0,4},{1,5},{2,6},{3,7},{4,0},{5,1},{6,2},{7,3},{8,12},{9,13},{10,... | collective-permute-start | bytes 1572872 | tf_op jit(solution)/shard_map/ppermute | solution.py:66
  69.5 2.2 %copy-start.23 = (bf16[256,1024]{1,0:T(8,128)(2,1)}, bf16[256,1024]{1,0:T(8,128)(2,1)S(1)}, u32[]{:S(2)}) copy-start(bf16[256,1024]{1,0:T(8,128)(2,1)S(1)} %collective-permute-done.11.refs_0_) | copy-start | bytes 1572868
  69.5 2.2 %copy-start.20 = (bf16[256,1024]{1,0:T(8,128)(2,1)}, bf16[256,1024]{1,0:T(8,128)(2,1)S(1)}, u32[]{:S(2)}) copy-start(bf16[256,1024]{1,0:T(8,128)(2,1)S(1)} %collective-permute-done.12.refs_1_) | copy-start | bytes 1572868
  69.5 2.2 %copy-start.22 = (bf16[256,1024]{1,0:T(8,128)(2,1)}, bf16[256,1024]{1,0:T(8,128)(2,1)S(1)}, u32[]{:S(2)}) copy-start(bf16[256,1024]{1,0:T(8,128)(2,1)S(1)} %collective-permute-done.13.refs_2_) | copy-start | bytes 1572868
  69.5 9.5 %collective-permute-start.14 = (bf16[256,1024]{1,0:T(8,128)(2,1)}, bf16[256,1024]{1,0:T(8,128)(2,1)S(1)}, u32[]{:S(2)}, u32[]{:S(2)}) collective-permute-start(bf16[256,1024]{1,0:T(8,128)(2,1)} %collective-permute-done.4.refs_3_), channel_id=1, source_target_pairs={{0,4},{1,5},{2,6},{3,7},{4,0},{5,1},{6,2},{7,3},{8,12},{9,13},{10,... | collective-permute-start | bytes 1572872 | tf_op jit(solution)/shard_map/ppermute | solution.py:66
  69.6 9.5 %collective-permute-start.15 = (bf16[256,1024]{1,0:T(8,128)(2,1)}, bf16[256,1024]{1,0:T(8,128)(2,1)S(1)}, u32[]{:S(2)}, u32[]{:S(2)}) collective-permute-start(bf16[256,1024]{1,0:T(8,128)(2,1)} %copy-done.19), channel_id=1, source_target_pairs={{0,16},{1,17},{2,18},{3,19},{4,20},{5,21},{6,22},{7,23},{8,24},{9,... | collective-permute-start | bytes 1572872 | tf_op jit(solution)/shard_map/ppermute | solution.py:66
  70.2 9.2 %collective-permute-start.16 = (bf16[256,1024]{1,0:T(8,128)(2,1)S(1)}, bf16[256,1024]{1,0:T(8,128)(2,1)S(1)}, u32[]{:S(2)}, u32[]{:S(2)}) collective-permute-start(bf16[256,1024]{1,0:T(8,128)(2,1)S(1)} %collective-permute-done.12.refs_1_), channel_id=1, source_target_pairs={{0,2},{1,3},{2,0},{3,1},{4,6},{5,7},{6,4},{7,5},{8,10},{9,11},{10,... | collective-permute-start | bytes 1572872 | tf_op jit(solution)/shard_map/ppermute | solution.py:66
  71.7 7.7 %copy-start.1 = (s32[11]{0:T(128)S(1)}, s32[11]{0:T(128)}, u32[]{:S(2)}) copy-start(s32[11]{0:T(128)} %stack.54.place) | copy-start | bytes 136
  79.4 2.5 %copy-start.6 = (bf16[16,2,320,256]{3,2,1,0:T(8,128)(2,1)S(1)}, bf16[16,2,320,256]{3,2,1,0:T(8,128)(2,1)}, u32[]{:S(2)}) copy-start(bf16[16,2,320,256]{3,2,1,0:T(8,128)(2,1)} %get-tuple-element.47.both) | copy-start | bytes 15728644
  81.8 1.3 %copy-start.7 = (f32[320,1024]{1,0:T(8,128)S(1)}, f32[320,1024]{1,0:T(8,128)}, u32[]{:S(2)}) copy-start(f32[320,1024]{1,0:T(8,128)} %get-tuple-element.49.refs_3_) | copy-start | bytes 3932164
  83.2 1.3 %copy-start.8 = (f32[320,1024]{1,0:T(8,128)S(1)}, f32[320,1024]{1,0:T(8,128)}, u32[]{:S(2)}) copy-start(f32[320,1024]{1,0:T(8,128)} %get-tuple-element.50.refs_4_) | copy-start | bytes 3932164
  84.5 5.5 %copy-start.3 = (s32[2]{0:T(128)S(1)}, s32[2]{0:T(128)}, u32[]{:S(2)}) copy-start(s32[2]{0:T(128)} %lengths.1) | copy-start | bytes 28
  84.5 5.5 %copy-start.5 = (s32[8]{0:T(128)S(1)}, s32[8]{0:T(128)}, u32[]{:S(2)}) copy-start(s32[8]{0:T(128)} %owner.1) | copy-start | bytes 100
  86.8 3.1 %collective-permute-start.17 = (f32[320,1024]{1,0:T(8,128)S(1)}, f32[320,1024]{1,0:T(8,128)S(1)}, u32[]{:S(2)}, u32[]{:S(2)}) collective-permute-start(f32[320,1024]{1,0:T(8,128)S(1)} %get-tuple-element.55), channel_id=1, source_target_pairs={{0,1},{1,0},{2,3},{3,2},{4,5},{5,4},{6,7},{7,6},{8,9},{9,8},{10,11... | collective-permute-start | bytes 3932168 | tf_op jit(solution)/shard_map/ppermute | solution.py:66
  91.8 5.0 %copy-start.16 = (bf16[4,128]{1,0:T(4,128)(2,1)S(1)}, bf16[4,128]{1,0:T(4,128)(2,1)}, u32[]{:S(2)}) copy-start(bf16[4,128]{1,0:T(4,128)(2,1)} %pad_maximum_fusion.6) | copy-start | bytes 3076
  91.8 5.7 %copy-start.14 = (bf16[4,8,64]{2,1,0:T(8,128)(2,1)S(1)}, bf16[4,8,64]{2,1,0:T(8,128)(2,1)}, u32[]{:S(2)}) copy-start(bf16[4,8,64]{2,1,0:T(8,128)(2,1)} %get-tuple-element.61) | copy-start | bytes 12292
  91.8 5.7 %copy-start.15 = (bf16[4,8,64]{2,1,0:T(8,128)(2,1)S(1)}, bf16[4,8,64]{2,1,0:T(8,128)(2,1)}, u32[]{:S(2)}) copy-start(bf16[4,8,64]{2,1,0:T(8,128)(2,1)} %get-tuple-element.62) | copy-start | bytes 12292
  91.8 21.6 %all-to-all-start = ((bf16[16,80,256]{2,1,0:T(8,128)(2,1)}), bf16[16,80,256]{2,1,0:T(8,128)(2,1)S(1)}, u32[]{:S(2)}, u32[]{:S(2)}) async-start(bf16[16,80,256]{2,1,0:T(8,128)(2,1)} %cache_rows.1), calls=%async_computation | async-start | bytes 1310720 | tf_op jit(solution)/shard_map/all_to_all | solution.py:461
  114.4 1.3 %collective-permute-start.18 = (f32[32,256]{1,0:T(8,128)S(1)}, f32[32,256]{1,0:T(8,128)S(1)}, u32[]{:S(2)}, u32[]{:S(2)}) collective-permute-start(f32[32,256]{1,0:T(8,128)S(1)} %decode.1), channel_id=1, source_target_pairs={{0,1},{1,0},{2,3},{3,2},{4,5},{5,4},{6,7},{7,6},{8,9},{9,8},{10,11... | collective-permute-start | bytes 98312 | tf_op jit(solution)/shard_map/ppermute | solution.py:66

commit v12 on v11

--- a/solution.py
+++ b/solution.py
@@ -93,7 +93,7 @@
 VMEM_REF = pl.BlockSpec(memory_space=pltpu.VMEM)
 SMEM_REF = pl.BlockSpec(memory_space=pltpu.SMEM)
 ANY_REF = pl.BlockSpec(memory_space=pl.ANY)
-PARAMS = pltpu.CompilerParams(vmem_limit_bytes=56 << 20)
+PARAMS = pltpu.CompilerParams(vmem_limit_bytes=20 << 20)
 SMALL = pltpu.CompilerParams(vmem_limit_bytes=16 << 20)
 
 

time: 118 us -> 115 us (0.975)
  Pallas kernels: 33.4 us -> 21.3 us
  waiting for transfers between devices: 41.2 us -> 50.9 us
  local copies, waits for them, and re-layouts: 8.57 us -> 5.31 us
  starting transfers between devices: 23.3 us -> 25.6 us
    pallas_call x4, Pallas kernels: 21.1 us -> 11.1 us  [product(): pl.pallas_call(functools.partial(product_kernel, plan, group, parts, bool...]
    ppermute x19, waiting for transfers between devices: 25.5 us -> 35.1 us  [moved(): return lax.ppermute(block, ('groups', 'seq'), route)]
    ppermute x19, starting transfers between devices: 18.4 us -> 21.3 us  [moved(): return lax.ppermute(block, ('groups', 'seq'), route)]
    unnamed x51 -> x25, local copies, waits for them, and re-layouts: 6.65 us -> 3.97 us
    pallas_call x1, Pallas kernels: 9.4 us -> 7.21 us  [prepared(): pl.pallas_call(prepare_kernel, grid_spec=pltpu.PrefetchScalarGridSpec(num...]
  transfers between devices with their start and end apart: 20 -> 20, of which waited for: 11 -> 11; matrix products, arithmetic and copies ran while one was open for 8% -> 7% of each run, Pallas kernels for 24% -> 14%
where the time goes in v12:
time: 115 us; the launch traced here: 114 us
  waiting for transfers between devices  50.9 us (44%)
  starting transfers between devices  25.6 us (22%)
  Pallas kernels  21.3 us (19%)
  other arithmetic  7.54 us (7%)
  local copies, waits for them, and re-layouts  5.31 us (5%)
  between operations  3.5 us (3%)
    ppermute x19, waiting for transfers between devices, moved(): return lax.ppermute(block, ('groups', 'seq'), route)  35.1 us
    ppermute x19, starting transfers between devices, moved(): return lax.ppermute(block, ('groups', 'seq'), route)  21.3 us
    all_to_all x1, waiting for transfers between devices, body(): lax.all_to_all(outgoing, 'seq', split_axis=0, concat_axis=1, tiled=True)  15.8 us
    pallas_call x4, Pallas kernels, product(): pl.pallas_call(functools.partial(product_kernel, plan, group, parts, bool...  11.1 us
    pallas_call x1, Pallas kernels, prepared(): pl.pallas_call(prepare_kernel, grid_spec=pltpu.PrefetchScalarGridSpec(num...  7.21 us
    all_to_all x1, starting transfers between devices, body(): lax.all_to_all(outgoing, 'seq', split_axis=0, concat_axis=1, tiled=True)  4.32 us
    unnamed x25, local copies, waits for them, and re-layouts  3.97 us
  transfers between devices with their start and end apart: 20, of which 11 were waited for; matrix products, arithmetic and copies ran while one was open for 7% of the time, Pallas kernels for 14%

profile of v12, /device:TPU:0, one launch (start us, length us, event | category | flops | bytes accessed | tf_op | source)
XLA Modules:
  0.0 114.0 jit_solution(340311737951725772)
XLA Ops:
  0.6 0.0 copy-start
  0.6 0.5 collective-permute-start.3
  1.2 1.2 %constant_dynamic-slice_fusion.3 = (bf16[256,512]{1,0:T(8,128)(2,1)S(1)}, bf16[256,512]{1,0:T(8,128)(2,1)S(1)}, bf16[256,512]{1,0:T(8,128)(2,1)S(1)}) fusion(bf16[512,512]{1,0:T(8,128)(2,1)} %param.11, s32[]{:T(128)S(6)} %select_n.77, s32[]{:T(128)S(6)} %select_n.76, bf16[512,512]{1,0:T(8,128)(2,1)} %param.12), kind=kLoop, calls=%fused_computation.33 | loop fusion | bytes 1572872 | tf_op jit(solution)/shard_map/dynamic_slice | solution.py:113
  2.4 0.0 copy-start.6
  2.4 0.1 pad_maximum_fusion.refs_0_
  2.4 2.7 %collective-permute-start = (bf16[256,1024]{1,0:T(8,128)(2,1)S(1)}, bf16[256,1024]{1,0:T(8,128)(2,1)S(1)}, u32[]{:S(2)}, u32[]{:S(2)}) collective-permute-start(bf16[256,1024]{1,0:T(8,128)(2,1)S(1)} %pad_maximum_fusion.refs_0_), channel_id=1, source_target_pairs={{0,4},{1,5},{2,6},{3,7},{4,0},{5,1},{6,2},{7,3},{8,12},{9,13},{10,... | collective-permute-start | bytes 1572872 | tf_op jit(solution)/shard_map/ppermute | solution.py:66
  5.1 1.5 %collective-permute-start.1 = (bf16[256,1024]{1,0:T(8,128)(2,1)S(1)}, bf16[256,1024]{1,0:T(8,128)(2,1)}, u32[]{:S(2)}, u32[]{:S(2)}) collective-permute-start(bf16[256,1024]{1,0:T(8,128)(2,1)S(1)} %pad_maximum_fusion.refs_0_), channel_id=1, source_target_pairs={{4,8},{5,9},{6,10},{7,11},{8,4},{9,5},{10,6},{11,7},{20,24},{21,25... | collective-permute-start | bytes 1572872 | tf_op jit(solution)/shard_map/ppermute | solution.py:66
  6.6 1.5 %collective-permute-start.2 = (bf16[256,1024]{1,0:T(8,128)(2,1)S(1)}, bf16[256,1024]{1,0:T(8,128)(2,1)S(1)}, u32[]{:S(2)}, u32[]{:S(2)}) collective-permute-start(bf16[256,1024]{1,0:T(8,128)(2,1)S(1)} %pad_maximum_fusion.refs_0_), channel_id=1, source_target_pairs={{0,2},{1,3},{2,0},{3,1},{4,6},{5,7},{6,4},{7,5},{8,10},{9,11},{10,... | collective-permute-start | bytes 1572872 | tf_op jit(solution)/shard_map/ppermute | solution.py:66
  8.2 0.6 fusion.12
  10.7 0.7 convert_bitcast_fusion
  12.1 0.7 fusion.13
  12.8 0.6 add_convert_fusion.3
  13.4 0.7 fusion.10
  14.1 0.1 subtract_convert_fusion.1
  14.3 0.7 subtract_convert_fusion
  14.9 0.4 fusion
  15.3 0.6 pad_maximum_fusion.6
  15.9 0.1 pad_maximum_fusion.2
  16.1 0.1 pad_maximum_fusion.1.refs_1_
  16.2 1.5 %collective-permute-done.refs_4_ = bf16[256,1024]{1,0:T(8,128)(2,1)S(1)} collective-permute-done((bf16[256,1024]{1,0:T(8,128)(2,1)S(1)}, bf16[256,1024]{1,0:T(8,128)(2,1)S(1)}, u32[]{:S(2)}, u32[]{:S(2)}) %collective-permute-start) | collective-permute-done | bytes 524320 | tf_op jit(solution)/shard_map/ppermute | solution.py:66
  17.7 0.0 collective-permute-done.1
  17.7 3.0 %collective-permute-done.2.refs_2_ = bf16[256,1024]{1,0:T(8,128)(2,1)S(1)} collective-permute-done((bf16[256,1024]{1,0:T(8,128)(2,1)S(1)}, bf16[256,1024]{1,0:T(8,128)(2,1)S(1)}, u32[]{:S(2)}, u32[]{:S(2)}) %collective-permute-start.2) | collective-permute-done | bytes 524320 | tf_op jit(solution)/shard_map/ppermute | solution.py:66
  20.7 1.5 %collective-permute-start.4 = (bf16[256,1024]{1,0:T(8,128)(2,1)S(1)}, bf16[256,1024]{1,0:T(8,128)(2,1)S(1)}, u32[]{:S(2)}, u32[]{:S(2)}) collective-permute-start(bf16[256,1024]{1,0:T(8,128)(2,1)S(1)} %collective-permute-done.2.refs_2_), channel_id=1, source_target_pairs={{0,16},{1,17},{2,18},{3,19},{4,20},{5,21},{6,22},{7,23},{8,24},{9,... | collective-permute-start | bytes 1572872 | tf_op jit(solution)/shard_map/ppermute | solution.py:66
  22.2 1.5 %collective-permute-start.5 = (bf16[256,1024]{1,0:T(8,128)(2,1)S(1)}, bf16[256,1024]{1,0:T(8,128)(2,1)}, u32[]{:S(2)}, u32[]{:S(2)}) collective-permute-start(bf16[256,1024]{1,0:T(8,128)(2,1)S(1)} %collective-permute-done.refs_4_), channel_id=1, source_target_pairs={{4,8},{5,9},{6,10},{7,11},{8,4},{9,5},{10,6},{11,7},{20,24},{21,25... | collective-permute-start | bytes 1572872 | tf_op jit(solution)/shard_map/ppermute | solution.py:66
  23.7 1.3 %collective-permute-start.6 = (bf16[256,1024]{1,0:T(8,128)(2,1)}, bf16[256,1024]{1,0:T(8,128)(2,1)}, u32[]{:S(2)}, u32[]{:S(2)}) collective-permute-start(bf16[256,1024]{1,0:T(8,128)(2,1)} %collective-permute-done.1), channel_id=1, source_target_pairs={{4,0},{5,1},{6,2},{7,3},{8,12},{9,13},{10,14},{11,15},{20,16},{21,... | collective-permute-start | bytes 1572872 | tf_op jit(solution)/shard_map/ppermute | solution.py:66
  25.0 1.6 %collective-permute-start.7 = (bf16[256,1024]{1,0:T(8,128)(2,1)S(1)}, bf16[256,1024]{1,0:T(8,128)(2,1)S(1)}, u32[]{:S(2)}, u32[]{:S(2)}) collective-permute-start(bf16[256,1024]{1,0:T(8,128)(2,1)S(1)} %collective-permute-done.refs_4_), channel_id=1, source_target_pairs={{0,2},{1,3},{2,0},{3,1},{4,6},{5,7},{6,4},{7,5},{8,10},{9,11},{10,... | collective-permute-start | bytes 1572872 | tf_op jit(solution)/shard_map/ppermute | solution.py:66
  26.6 0.1 stack.54.place
  26.6 2.5 %copy-done.1 = bf16[2,160,8192]{2,1,0:T(8,128)(2,1)S(1)} copy-done((bf16[2,160,8192]{2,1,0:T(8,128)(2,1)S(1)}, bf16[2,160,8192]{2,1,0:T(8,128)(2,1)}, u32[]{:S(2)}) %copy-start.1) | copy-done | bytes 5242904
  29.1 7.2 %normed_halves.1 = (bf16[16,2,320,256]{3,2,1,0:T(8,128)(2,1)S(1)}, bf16[16,320,256]{2,1,0:T(8,128)(2,1)}) custom-call(s32[11]{0:T(128)S(1)} %stack.54.place, bf16[320,8192]{1,0:T(8,128)(2,1)S(1)} %bitcast.40, bf16[320,8192]{1,0:T(8,128)(2,1)} %collective-permute-done.3.refs_1_), custom_call_target="tpu_custom_call" | custom-call | flops 1000 | bytes 1000 | tf_op jit(solution)/shard_map/normed_halves/pallas_call | solution.py:147
  36.4 3.9 %collective-permute-done.6 = bf16[256,1024]{1,0:T(8,128)(2,1)} collective-permute-done((bf16[256,1024]{1,0:T(8,128)(2,1)}, bf16[256,1024]{1,0:T(8,128)(2,1)}, u32[]{:S(2)}, u32[]{:S(2)}) %collective-permute-start.6) | collective-permute-done | bytes 524320 | tf_op jit(solution)/shard_map/ppermute | solution.py:66
  40.3 1.1 broadcast_select_fusion.1.refs_0_
  41.4 1.6 %collective-permute-start.9 = (bf16[256,1024]{1,0:T(8,128)(2,1)S(1)}, bf16[256,1024]{1,0:T(8,128)(2,1)S(1)}, u32[]{:S(2)}, u32[]{:S(2)}) collective-permute-start(bf16[256,1024]{1,0:T(8,128)(2,1)S(1)} %broadcast_select_fusion.1.refs_0_), channel_id=1, source_target_pairs={{0,2},{1,3},{2,0},{3,1},{4,6},{5,7},{6,4},{7,5},{8,10},{9,11},{10,... | collective-permute-start | bytes 1572872 | tf_op jit(solution)/shard_map/ppermute | solution.py:66
  43.0 0.5 collective-permute-start.10
  43.5 1.3 %collective-permute-start.8 = (bf16[256,1024]{1,0:T(8,128)(2,1)}, bf16[256,1024]{1,0:T(8,128)(2,1)S(1)}, u32[]{:S(2)}, u32[]{:S(2)}) collective-permute-start(bf16[256,1024]{1,0:T(8,128)(2,1)} %collective-permute-done.5), channel_id=1, source_target_pairs={{4,0},{5,1},{6,2},{7,3},{8,12},{9,13},{10,14},{11,15},{20,16},{21,... | collective-permute-start | bytes 1572872 | tf_op jit(solution)/shard_map/ppermute | solution.py:66
  44.8 3.5 %add_product.4 = (f32[320,1024]{1,0:T(8,128)S(1)}, f32[320,1024]{1,0:T(8,128)S(1)}) custom-call(s32[11]{0:T(128)S(1)} %stack.54.place, bf16[16,2,320,256]{3,2,1,0:T(8,128)(2,1)S(1)} %get-tuple-element.47.both, bf16[256,1024]{1,0:T(8,128)(2,1)S(1)} %pad_maximum_fusion.refs_0_, bf16[256,1024]{1,0:T(8,128)(2,1)S(1)} %pad_maximum_fusion.1.refs_1_, ...), custom_call_target="tpu_custom_call" | custom-call | flops 68719476736 | bytes 1000 | tf_op jit(solution)/shard_map/add_product/pallas_call | solution.py:230
  48.3 8.8 %collective-permute-done.8 = bf16[256,1024]{1,0:T(8,128)(2,1)S(1)} collective-permute-done((bf16[256,1024]{1,0:T(8,128)(2,1)}, bf16[256,1024]{1,0:T(8,128)(2,1)S(1)}, u32[]{:S(2)}, u32[]{:S(2)}) %collective-permute-start.8) | collective-permute-done | bytes 524320 | tf_op jit(solution)/shard_map/ppermute | solution.py:66
  57.2 0.1 broadcast_select_fusion.refs_3_
  57.2 1.6 %collective-permute-start.12 = (bf16[256,1024]{1,0:T(8,128)(2,1)S(1)}, bf16[256,1024]{1,0:T(8,128)(2,1)S(1)}, u32[]{:S(2)}, u32[]{:S(2)}) collective-permute-start(bf16[256,1024]{1,0:T(8,128)(2,1)S(1)} %broadcast_select_fusion.refs_3_), channel_id=1, source_target_pairs={{0,16},{1,17},{2,18},{3,19},{4,20},{5,21},{6,22},{7,23},{8,24},{9,... | collective-permute-start | bytes 1572872 | tf_op jit(solution)/shard_map/ppermute | solution.py:66
  58.8 0.5 collective-permute-start.13
  59.3 0.7 collective-permute-start.11
  60.0 2.9 %add_product.5 = (f32[320,1024]{1,0:T(8,128)S(1)}, f32[320,1024]{1,0:T(8,128)S(1)}) custom-call(s32[11]{0:T(128)S(1)} %stack.54.place, bf16[16,2,320,256]{3,2,1,0:T(8,128)(2,1)S(1)} %get-tuple-element.47.both, bf16[256,1024]{1,0:T(8,128)(2,1)S(1)} %broadcast_select_fusion.1.refs_0_, bf16[256,1024]{1,0:T(8,128)(2,1)S(1)} %collective-permute-done.10.refs_1_, ...), custom_call_target="tpu_custom_call" | custom-call | flops 68719476736 | bytes 1000 | tf_op jit(solution)/shard_map/add_product/pallas_call | solution.py:230
  62.9 8.4 %collective-permute-done.11.refs_0_ = bf16[256,1024]{1,0:T(8,128)(2,1)S(1)} collective-permute-done((bf16[256,1024]{1,0:T(8,128)(2,1)S(1)}, bf16[256,1024]{1,0:T(8,128)(2,1)S(1)}, u32[]{:S(2)}, u32[]{:S(2)}) %collective-permute-start.11) | collective-permute-done | bytes 524320 | tf_op jit(solution)/shard_map/ppermute | solution.py:66
  71.3 0.7 collective-permute-start.14
  72.0 0.5 collective-permute-start.15
  72.5 1.6 %collective-permute-start.16 = (bf16[256,1024]{1,0:T(8,128)(2,1)S(1)}, bf16[256,1024]{1,0:T(8,128)(2,1)S(1)}, u32[]{:S(2)}, u32[]{:S(2)}) collective-permute-start(bf16[256,1024]{1,0:T(8,128)(2,1)S(1)} %collective-permute-done.12.refs_1_), channel_id=1, source_target_pairs={{0,2},{1,3},{2,0},{3,1},{4,6},{5,7},{6,4},{7,5},{8,10},{9,11},{10,... | collective-permute-start | bytes 1572872 | tf_op jit(solution)/shard_map/ppermute | solution.py:66
  74.1 2.4 %add_product.6 = (f32[320,1024]{1,0:T(8,128)S(1)}, f32[320,1024]{1,0:T(8,128)S(1)}) custom-call(s32[11]{0:T(128)S(1)} %stack.54.place, bf16[16,2,320,256]{3,2,1,0:T(8,128)(2,1)S(1)} %get-tuple-element.47.both, bf16[256,1024]{1,0:T(8,128)(2,1)S(1)} %collective-permute-done.11.refs_0_, bf16[256,1024]{1,0:T(8,128)(2,1)S(1)} %collective-permute-done.12.refs_1_, ...), custom_call_target="tpu_custom_call" | custom-call | flops 68719476736 | bytes 1000 | tf_op jit(solution)/shard_map/add_product/pallas_call | solution.py:230
  76.5 4.1 %collective-permute-done.14.refs_0_ = bf16[256,1024]{1,0:T(8,128)(2,1)S(1)} collective-permute-done((bf16[256,1024]{1,0:T(8,128)(2,1)S(1)}, bf16[256,1024]{1,0:T(8,128)(2,1)S(1)}, u32[]{:S(2)}, u32[]{:S(2)}) %collective-permute-start.14) | collective-permute-done | bytes 524320 | tf_op jit(solution)/shard_map/ppermute | solution.py:66
  80.6 0.6 collective-permute-done.15.refs_1_
  81.2 0.5 collective-permute-done.16.refs_2_
  81.7 2.4 %add_product.7 = (f32[320,1024]{1,0:T(8,128)S(1)}, f32[320,1024]{1,0:T(8,128)S(1)}) custom-call(s32[11]{0:T(128)S(1)} %stack.54.place, bf16[16,2,320,256]{3,2,1,0:T(8,128)(2,1)S(1)} %get-tuple-element.47.both, bf16[256,1024]{1,0:T(8,128)(2,1)S(1)} %collective-permute-done.14.refs_0_, bf16[256,1024]{1,0:T(8,128)(2,1)S(1)} %collective-permute-done.15.refs_1_, ...), custom_call_target="tpu_custom_call" | custom-call | flops 68719476736 | bytes 1000 | tf_op jit(solution)/shard_map/add_product/pallas_call | solution.py:230
  84.1 0.1 collective-permute-start.17
  84.2 3.0 %collective-permute-done.17.came = f32[320,1024]{1,0:T(8,128)S(1)} collective-permute-done((f32[320,1024]{1,0:T(8,128)S(1)}, f32[320,1024]{1,0:T(8,128)S(1)}, u32[]{:S(2)}, u32[]{:S(2)}) %collective-permute-start.17) | collective-permute-done | bytes 1310752 | tf_op jit(solution)/shard_map/ppermute | solution.py:66
  87.2 1.9 %cache_rows.1 = bf16[16,80,256]{2,1,0:T(8,128)(2,1)} custom-call(s32[11]{0:T(128)S(1)} %stack.54.place, s32[2]{0:T(128)S(1)} %copy-done.3, s32[8]{0:T(128)S(1)} %copy-done.5, f32[320,1024]{1,0:T(8,128)S(1)} %get-tuple-element.54.total, f32[320,1024]{1,0:T(8,128)S(1)} %collective-permute-done.17.came, f32[160,128]{1,0:T(8,128)S(1)} %get-tuple-element.71.cosine, ...), custom_call_target="tpu_custom_call" | custom-call | flops 1000 | bytes 1000 | tf_op jit(solution)/shard_map/cache_rows/pallas_call | solution.py:277
  89.1 4.3 %all-to-all-start = ((bf16[16,80,256]{2,1,0:T(8,128)(2,1)}), bf16[16,80,256]{2,1,0:T(8,128)(2,1)S(1)}, u32[]{:S(2)}, u32[]{:S(2)}) async-start(bf16[16,80,256]{2,1,0:T(8,128)(2,1)} %cache_rows.1), calls=%async_computation | async-start | bytes 1310720 | tf_op jit(solution)/shard_map/all_to_all | solution.py:461
  93.5 0.7 pad_add_fusion.place
  94.2 0.1 pad_maximum_fusion.5.query
  94.3 15.8 %all-to-all-done = bf16[16,80,256]{2,1,0:T(8,128)(2,1)S(1)} async-done(((bf16[16,80,256]{2,1,0:T(8,128)(2,1)}), bf16[16,80,256]{2,1,0:T(8,128)(2,1)S(1)}, u32[]{:S(2)}, u32[]{:S(2)}) %all-to-all-start) | async-done | bytes 655392 | tf_op jit(solution)/shard_map/all_to_all | solution.py:461
  110.0 1.0 decode.1
  111.1 0.1 collective-permute-start.18
  111.2 1.1 collective-permute-done.18
  112.3 0.2 fusion.15
  112.5 0.1 fusion.8
  112.6 0.6 copy.20
  113.2 0.8 copy.22
  (33 shorter events, 0.1 us)
Async XLA Ops:
  0.6 92.8 %copy-start = (bf16[8,4,128]{2,1,0:T(4,128)(2,1)S(1)}, bf16[8,4,128]{2,1,0:T(4,128)(2,1)}, u32[]{:S(2)}) copy-start(bf16[8,4,128]{2,1,0:T(4,128)(2,1)} %param.17) | copy-start | bytes 24580
  0.6 20.0 %collective-permute-start.3 = (bf16[320,8192]{1,0:T(8,128)(2,1)}, bf16[320,8192]{1,0:T(8,128)(2,1)}, u32[]{:S(2)}, u32[]{:S(2)}) collective-permute-start(bf16[320,8192]{1,0:T(8,128)(2,1)} %bitcast.39), channel_id=1, source_target_pairs={{0,1},{1,0},{2,3},{3,2},{4,5},{5,4},{6,7},{7,6},{8,9},{9,8},{10,11... | collective-permute-start | bytes 15728648 | tf_op jit(solution)/shard_map/ppermute | solution.py:66
  1.2 7.0 %copy-start.4 = (s32[8]{0:T(128)S(1)}, s32[8]{0:T(128)}, u32[]{:S(2)}) copy-start(s32[8]{0:T(128)} %owner.1) | copy-start | bytes 100
  1.2 11.0 %copy-start.2 = (s32[2]{0:T(128)S(1)}, s32[2]{0:T(128)}, u32[]{:S(2)}) copy-start(s32[2]{0:T(128)} %lengths.1) | copy-start | bytes 28
  1.2 13.0 %copy-start.10 = (f32[64]{0:T(128)S(1)}, f32[64]{0:T(128)}, u32[]{:S(2)}) copy-start(f32[64]{0:T(128)} %constant.84.clone) | copy-start | bytes 772
  2.4 13.7 %copy-start.6 = (bf16[512,512]{1,0:T(8,128)(2,1)S(1)}, bf16[512,512]{1,0:T(8,128)(2,1)}, u32[]{:S(2)}) copy-start(bf16[512,512]{1,0:T(8,128)(2,1)} %param.12) | copy-start | bytes 1572868
  2.4 15.2 %collective-permute-start = (bf16[256,1024]{1,0:T(8,128)(2,1)S(1)}, bf16[256,1024]{1,0:T(8,128)(2,1)S(1)}, u32[]{:S(2)}, u32[]{:S(2)}) collective-permute-start(bf16[256,1024]{1,0:T(8,128)(2,1)S(1)} %pad_maximum_fusion.refs_0_), channel_id=1, source_target_pairs={{0,4},{1,5},{2,6},{3,7},{4,0},{5,1},{6,2},{7,3},{8,12},{9,13},{10,... | collective-permute-start | bytes 1572872 | tf_op jit(solution)/shard_map/ppermute | solution.py:66
  5.1 12.6 %collective-permute-start.1 = (bf16[256,1024]{1,0:T(8,128)(2,1)S(1)}, bf16[256,1024]{1,0:T(8,128)(2,1)}, u32[]{:S(2)}, u32[]{:S(2)}) collective-permute-start(bf16[256,1024]{1,0:T(8,128)(2,1)S(1)} %pad_maximum_fusion.refs_0_), channel_id=1, source_target_pairs={{4,8},{5,9},{6,10},{7,11},{8,4},{9,5},{10,6},{11,7},{20,24},{21,25... | collective-permute-start | bytes 1572872 | tf_op jit(solution)/shard_map/ppermute | solution.py:66
  6.6 14.0 %collective-permute-start.2 = (bf16[256,1024]{1,0:T(8,128)(2,1)S(1)}, bf16[256,1024]{1,0:T(8,128)(2,1)S(1)}, u32[]{:S(2)}, u32[]{:S(2)}) collective-permute-start(bf16[256,1024]{1,0:T(8,128)(2,1)S(1)} %pad_maximum_fusion.refs_0_), channel_id=1, source_target_pairs={{0,2},{1,3},{2,0},{3,1},{4,6},{5,7},{6,4},{7,5},{8,10},{9,11},{10,... | collective-permute-start | bytes 1572872 | tf_op jit(solution)/shard_map/ppermute | solution.py:66
  20.7 15.7 %collective-permute-start.4 = (bf16[256,1024]{1,0:T(8,128)(2,1)S(1)}, bf16[256,1024]{1,0:T(8,128)(2,1)S(1)}, u32[]{:S(2)}, u32[]{:S(2)}) collective-permute-start(bf16[256,1024]{1,0:T(8,128)(2,1)S(1)} %collective-permute-done.2.refs_2_), channel_id=1, source_target_pairs={{0,16},{1,17},{2,18},{3,19},{4,20},{5,21},{6,22},{7,23},{8,24},{9,... | collective-permute-start | bytes 1572872 | tf_op jit(solution)/shard_map/ppermute | solution.py:66
  22.2 14.2 %collective-permute-start.5 = (bf16[256,1024]{1,0:T(8,128)(2,1)S(1)}, bf16[256,1024]{1,0:T(8,128)(2,1)}, u32[]{:S(2)}, u32[]{:S(2)}) collective-permute-start(bf16[256,1024]{1,0:T(8,128)(2,1)S(1)} %collective-permute-done.refs_4_), channel_id=1, source_target_pairs={{4,8},{5,9},{6,10},{7,11},{8,4},{9,5},{10,6},{11,7},{20,24},{21,25... | collective-permute-start | bytes 1572872 | tf_op jit(solution)/shard_map/ppermute | solution.py:66
  23.7 16.6 %collective-permute-start.6 = (bf16[256,1024]{1,0:T(8,128)(2,1)}, bf16[256,1024]{1,0:T(8,128)(2,1)}, u32[]{:S(2)}, u32[]{:S(2)}) collective-permute-start(bf16[256,1024]{1,0:T(8,128)(2,1)} %collective-permute-done.1), channel_id=1, source_target_pairs={{4,0},{5,1},{6,2},{7,3},{8,12},{9,13},{10,14},{11,15},{20,16},{21,... | collective-permute-start | bytes 1572872 | tf_op jit(solution)/shard_map/ppermute | solution.py:66
  25.0 15.3 %collective-permute-start.7 = (bf16[256,1024]{1,0:T(8,128)(2,1)S(1)}, bf16[256,1024]{1,0:T(8,128)(2,1)S(1)}, u32[]{:S(2)}, u32[]{:S(2)}) collective-permute-start(bf16[256,1024]{1,0:T(8,128)(2,1)S(1)} %collective-permute-done.refs_4_), channel_id=1, source_target_pairs={{0,2},{1,3},{2,0},{3,1},{4,6},{5,7},{6,4},{7,5},{8,10},{9,11},{10,... | collective-permute-start | bytes 1572872 | tf_op jit(solution)/shard_map/ppermute | solution.py:66
  26.6 2.5 %copy-start.1 = (bf16[2,160,8192]{2,1,0:T(8,128)(2,1)S(1)}, bf16[2,160,8192]{2,1,0:T(8,128)(2,1)}, u32[]{:S(2)}) copy-start(bf16[2,160,8192]{2,1,0:T(8,128)(2,1)} %param.10) | copy-start | bytes 15728644
  41.4 15.8 %collective-permute-start.9 = (bf16[256,1024]{1,0:T(8,128)(2,1)S(1)}, bf16[256,1024]{1,0:T(8,128)(2,1)S(1)}, u32[]{:S(2)}, u32[]{:S(2)}) collective-permute-start(bf16[256,1024]{1,0:T(8,128)(2,1)S(1)} %broadcast_select_fusion.1.refs_0_), channel_id=1, source_target_pairs={{0,2},{1,3},{2,0},{3,1},{4,6},{5,7},{6,4},{7,5},{8,10},{9,11},{10,... | collective-permute-start | bytes 1572872 | tf_op jit(solution)/shard_map/ppermute | solution.py:66
  43.0 14.2 %collective-permute-start.10 = (bf16[256,1024]{1,0:T(8,128)(2,1)S(1)}, bf16[256,1024]{1,0:T(8,128)(2,1)S(1)}, u32[]{:S(2)}, u32[]{:S(2)}) collective-permute-start(bf16[256,1024]{1,0:T(8,128)(2,1)S(1)} %broadcast_select_fusion.1.refs_0_), channel_id=1, source_target_pairs={{0,16},{1,17},{2,18},{3,19},{4,20},{5,21},{6,22},{7,23},{8,24},{9,... | collective-permute-start | bytes 1572872 | tf_op jit(solution)/shard_map/ppermute | solution.py:66
  43.5 13.6 %collective-permute-start.8 = (bf16[256,1024]{1,0:T(8,128)(2,1)}, bf16[256,1024]{1,0:T(8,128)(2,1)S(1)}, u32[]{:S(2)}, u32[]{:S(2)}) collective-permute-start(bf16[256,1024]{1,0:T(8,128)(2,1)} %collective-permute-done.5), channel_id=1, source_target_pairs={{4,0},{5,1},{6,2},{7,3},{8,12},{9,13},{10,14},{11,15},{20,16},{21,... | collective-permute-start | bytes 1572872 | tf_op jit(solution)/shard_map/ppermute | solution.py:66
  57.2 14.1 %collective-permute-start.12 = (bf16[256,1024]{1,0:T(8,128)(2,1)S(1)}, bf16[256,1024]{1,0:T(8,128)(2,1)S(1)}, u32[]{:S(2)}, u32[]{:S(2)}) collective-permute-start(bf16[256,1024]{1,0:T(8,128)(2,1)S(1)} %broadcast_select_fusion.refs_3_), channel_id=1, source_target_pairs={{0,16},{1,17},{2,18},{3,19},{4,20},{5,21},{6,22},{7,23},{8,24},{9,... | collective-permute-start | bytes 1572872 | tf_op jit(solution)/shard_map/ppermute | solution.py:66
  58.8 12.5 %collective-permute-start.13 = (bf16[256,1024]{1,0:T(8,128)(2,1)S(1)}, bf16[256,1024]{1,0:T(8,128)(2,1)S(1)}, u32[]{:S(2)}, u32[]{:S(2)}) collective-permute-start(bf16[256,1024]{1,0:T(8,128)(2,1)S(1)} %broadcast_select_fusion.refs_3_), channel_id=1, source_target_pairs={{0,2},{1,3},{2,0},{3,1},{4,6},{5,7},{6,4},{7,5},{8,10},{9,11},{10,... | collective-permute-start | bytes 1572872 | tf_op jit(solution)/shard_map/ppermute | solution.py:66
  59.3 12.0 %collective-permute-start.11 = (bf16[256,1024]{1,0:T(8,128)(2,1)S(1)}, bf16[256,1024]{1,0:T(8,128)(2,1)S(1)}, u32[]{:S(2)}, u32[]{:S(2)}) collective-permute-start(bf16[256,1024]{1,0:T(8,128)(2,1)S(1)} %pad_maximum_fusion.1.refs_1_), channel_id=1, source_target_pairs={{0,4},{1,5},{2,6},{3,7},{4,0},{5,1},{6,2},{7,3},{8,12},{9,13},{10,... | collective-permute-start | bytes 1572872 | tf_op jit(solution)/shard_map/ppermute | solution.py:66
  71.3 9.3 %collective-permute-start.14 = (bf16[256,1024]{1,0:T(8,128)(2,1)S(1)}, bf16[256,1024]{1,0:T(8,128)(2,1)S(1)}, u32[]{:S(2)}, u32[]{:S(2)}) collective-permute-start(bf16[256,1024]{1,0:T(8,128)(2,1)S(1)} %collective-permute-done.4.refs_3_), channel_id=1, source_target_pairs={{0,4},{1,5},{2,6},{3,7},{4,0},{5,1},{6,2},{7,3},{8,12},{9,13},{10,... | collective-permute-start | bytes 1572872 | tf_op jit(solution)/shard_map/ppermute | solution.py:66
  72.0 9.2 %collective-permute-start.15 = (bf16[256,1024]{1,0:T(8,128)(2,1)S(1)}, bf16[256,1024]{1,0:T(8,128)(2,1)S(1)}, u32[]{:S(2)}, u32[]{:S(2)}) collective-permute-start(bf16[256,1024]{1,0:T(8,128)(2,1)S(1)} %collective-permute-done.9.refs_2_), channel_id=1, source_target_pairs={{0,16},{1,17},{2,18},{3,19},{4,20},{5,21},{6,22},{7,23},{8,24},{9,... | collective-permute-start | bytes 1572872 | tf_op jit(solution)/shard_map/ppermute | solution.py:66
  72.5 9.2 %collective-permute-start.16 = (bf16[256,1024]{1,0:T(8,128)(2,1)S(1)}, bf16[256,1024]{1,0:T(8,128)(2,1)S(1)}, u32[]{:S(2)}, u32[]{:S(2)}) collective-permute-start(bf16[256,1024]{1,0:T(8,128)(2,1)S(1)} %collective-permute-done.12.refs_1_), channel_id=1, source_target_pairs={{0,2},{1,3},{2,0},{3,1},{4,6},{5,7},{6,4},{7,5},{8,10},{9,11},{10,... | collective-permute-start | bytes 1572872 | tf_op jit(solution)/shard_map/ppermute | solution.py:66
  81.7 5.5 %copy-start.3 = (s32[2]{0:T(128)S(1)}, s32[2]{0:T(128)}, u32[]{:S(2)}) copy-start(s32[2]{0:T(128)} %lengths.1) | copy-start | bytes 28
  81.7 5.5 %copy-start.5 = (s32[8]{0:T(128)S(1)}, s32[8]{0:T(128)}, u32[]{:S(2)}) copy-start(s32[8]{0:T(128)} %owner.1) | copy-start | bytes 100
  84.1 3.1 %collective-permute-start.17 = (f32[320,1024]{1,0:T(8,128)S(1)}, f32[320,1024]{1,0:T(8,128)S(1)}, u32[]{:S(2)}, u32[]{:S(2)}) collective-permute-start(f32[320,1024]{1,0:T(8,128)S(1)} %get-tuple-element.55), channel_id=1, source_target_pairs={{0,1},{1,0},{2,3},{3,2},{4,5},{5,4},{6,7},{7,6},{8,9},{9,8},{10,11... | collective-permute-start | bytes 3932168 | tf_op jit(solution)/shard_map/ppermute | solution.py:66
  89.1 4.3 %copy-start.9 = (bf16[4,128]{1,0:T(4,128)(2,1)S(1)}, bf16[4,128]{1,0:T(4,128)(2,1)}, u32[]{:S(2)}) copy-start(bf16[4,128]{1,0:T(4,128)(2,1)} %pad_maximum_fusion.6) | copy-start | bytes 3076
  89.1 5.1 %copy-start.7 = (bf16[4,8,64]{2,1,0:T(8,128)(2,1)S(1)}, bf16[4,8,64]{2,1,0:T(8,128)(2,1)}, u32[]{:S(2)}) copy-start(bf16[4,8,64]{2,1,0:T(8,128)(2,1)} %get-tuple-element.61) | copy-start | bytes 12292
  89.1 5.1 %copy-start.8 = (bf16[4,8,64]{2,1,0:T(8,128)(2,1)S(1)}, bf16[4,8,64]{2,1,0:T(8,128)(2,1)}, u32[]{:S(2)}) copy-start(bf16[4,8,64]{2,1,0:T(8,128)(2,1)} %get-tuple-element.62) | copy-start | bytes 12292
  89.1 20.9 %all-to-all-start = ((bf16[16,80,256]{2,1,0:T(8,128)(2,1)}), bf16[16,80,256]{2,1,0:T(8,128)(2,1)S(1)}, u32[]{:S(2)}, u32[]{:S(2)}) async-start(bf16[16,80,256]{2,1,0:T(8,128)(2,1)} %cache_rows.1), calls=%async_computation | async-start | bytes 1310720 | tf_op jit(solution)/shard_map/all_to_all | solution.py:461
  111.1 1.3 %collective-permute-start.18 = (f32[32,256]{1,0:T(8,128)S(1)}, f32[32,256]{1,0:T(8,128)S(1)}, u32[]{:S(2)}, u32[]{:S(2)}) collective-permute-start(f32[32,256]{1,0:T(8,128)S(1)} %decode.1), channel_id=1, source_target_pairs={{0,1},{1,0},{2,3},{3,2},{4,5},{5,4},{6,7},{7,6},{8,9},{9,8},{10,11... | collective-permute-start | bytes 98312 | tf_op jit(solution)/shard_map/ppermute | solution.py:66

commit v13 on v12

v13 whole, which is shorter than its diff:
```python
import functools

import jax
import jax.numpy as jnp
import numpy as np
from jax import lax
from jax.experimental import pallas as pl
from jax.experimental.pallas import tpu as pltpu
from jax.sharding import PartitionSpec as P

HEAD_SIZE = 128
KEY_VALUE_HEADS = 4
QPK = 8
STEPS = 4


ROPE_BASE = 500000.0


def swapped(block, axis, bit):
    count = lax.axis_size(axis)
    route = []
    for low in range(count):
        high = low | 1 << bit
        if high != low and high < count:
            route += [(low, high), (high, low)]
    return lax.ppermute(block, axis, route)


def rope_table(positions, head_dim):
    freq = ROPE_BASE ** (-(np.arange(head_dim // 2, dtype=np.float64) * 2.0) / head_dim)
    angle = positions.astype(jnp.float32)[:, None] * jnp.asarray(freq, jnp.float32)[None, :]
    return (jnp.cos(angle), jnp.sin(angle))


def rotate(values_in, cosine, sine_part):
    half_dim = values_in.shape[-1] // 2
    lower_half = values_in[..., :half_dim]
    upper_half = values_in[..., half_dim:]
    return jnp.concatenate(
        [
            lower_half * cosine - upper_half * sine_part,
            upper_half * cosine + lower_half * sine_part,
        ],
        -1,
    )


def spread(count):
    side = 1
    while side * side < count:
        side *= 2
    return (side, count // side)


def moved(block, rule):
    groups, seq = lax.axis_size("groups"), lax.axis_size("seq")
    low = spread(seq // 2)[1]
    route = []
    for g in range(groups):
        for s in range(seq):
            place = rule(g, s // 2 // low, s // 2 % low, s % 2)
            if place is not None:
                tg, tz, ty, tc = place
                route.append((g * seq + s, tg * seq + (tz * low + ty) * 2 + tc))
    return lax.ppermute(block, ("groups", "seq"), route)


def to_core(g, z, y, c):
    return (g, z, y, 1 - c)


def to_row(g, z, y, c):
    return (g, z, 1 - y, c)


def to_group(g, z, y, c):
    return (1 - g, z, y, c)


def to_pair(g, z, y, c):
    return (g, z ^ 1, y, c)


def to_middle(g, z, y, c):
    return (g, 3 - z, y, c) if z in (1, 2) else None


def to_end(g, z, y, c):
    return (g, 0 if z == 1 else 3, y, c) if z in (1, 2) else None


VMEM_REF = pl.BlockSpec(memory_space=pltpu.VMEM)
SMEM_REF = pl.BlockSpec(memory_space=pltpu.SMEM)
ANY_REF = pl.BlockSpec(memory_space=pl.ANY)
PARAMS = pltpu.CompilerParams(vmem_limit_bytes=20 << 20)
SMALL = pltpu.CompilerParams(vmem_limit_bytes=16 << 20)


def cost(flops, moved_bytes):
    return pl.CostEstimate(flops=flops, bytes_accessed=moved_bytes, transcendentals=0)


def fetch(source, target, sem):
    copy = pltpu.make_async_copy(source, target, sem)
    copy.start()
    return copy


def prepare_kernel(place, rows_in, mine, kept):
    depth = mine.shape[2]
    rows, width = rows_in.shape
    square = jnp.zeros((rows, depth), jnp.float32)
    for first in range(0, width, depth):
        part = rows_in[:, first : first + depth].astype(jnp.float32)
        square += part * part
    scale = lax.rsqrt(jnp.sum(square, -1, keepdims=True) / width + 1e-05)
    for core in range(2):

        @pl.when(place[1] == core)
        def _():
            for first in range(0, width, depth):
                j, c, h = first // (4 * depth), first // (2 * depth) % 2, first // depth % 2
                target = mine if c == core else kept
                part = rows_in[:, first : first + depth].astype(jnp.float32)
                target[2 * j + h] = (part * scale).astype(jnp.bfloat16)


def prepared(place, flat, blocks):
    rows, width = flat.shape
    depth = width // (4 * blocks)
    tile = 80 if rows % 80 == 0 else rows
    out = jax.ShapeDtypeStruct((2 * blocks, rows, depth), jnp.bfloat16)
    spec = pl.BlockSpec((2 * blocks, tile, depth), lambda i, place: (0, i, 0))
    return pl.pallas_call(
        prepare_kernel,
        grid_spec=pltpu.PrefetchScalarGridSpec(
            num_scalar_prefetch=1,
            grid=(rows // tile,),
            in_specs=[pl.BlockSpec((tile, width), lambda i, place: (i, 0))],
            out_specs=[spec, spec],
        ),
        out_shape=[out, out],
        compiler_params=PARAMS,
        cost_estimate=cost(1000, 1000),
        name="normed_halves",
    )(place, flat)


def after(value, *events):
    return lax.optimization_barrier((value, *events))[0]


def half_index(place, entry, kind):
    half = {0: place[0], 1: 1 - place[0], 2: 0, 3: 1}[kind]
    return place[entry] * 2 + half


def product_kernel(plan, group, with_total, place, mine, other, *refs):
    count = len(plan)
    outs = refs[-7:-5]
    left, right, total, sems, total_sems = refs[-5:]
    rows, depth = mine.shape[1], mine.shape[2]
    waits = []
    for k, (entry, kind) in enumerate(plan):
        area = pl.ds((k % group) * depth, depth)
        slot = k // group
        index = half_index(place, entry, kind)
        sources = (mine.at[index], other.at[index], refs[k])
        targets = (left.at[slot, 0, :, area], left.at[slot, 1, :, area], right.at[slot, area])
        waits.append(
            [fetch(a, b, sems.at[3 * k + i]) for i, (a, b) in enumerate(zip(sources, targets))]
        )
    carried = [
        fetch(ref, total.at[pl.ds(k * rows, rows)], total_sems.at[k])
        for k, ref in enumerate(refs[count : count + 2 * with_total])
    ]
    for slot in range(count // group):
        for copies in waits[slot * group : (slot + 1) * group]:
            for copy in copies:
                copy.wait()
        stacked = left[slot].reshape(2 * rows, group * depth)
        value = jnp.dot(stacked, right[slot], preferred_element_type=jnp.float32)
        if slot == 0:
            for copy in carried:
                copy.wait()
        if slot or with_total:
            value += total[...]
        if slot + 1 < count // group:
            total[...] = value
        else:
            outs[0][...] = value[:rows]
            outs[1][...] = value[rows:]


def product(place, mine, other, pieces, totals, group, moved_bytes=1000):
    _, rows, depth = mine.shape
    columns = pieces[0][2].shape[1]
    plan = [(entry, kind) for entry, kind, _ in pieces]
    count = len(plan)
    out = jax.ShapeDtypeStruct((rows, columns), jnp.float32)
    return pl.pallas_call(
        functools.partial(product_kernel, plan, group, bool(totals)),
        in_specs=[SMEM_REF] + [ANY_REF] * (2 + count + len(totals)),
        out_specs=[VMEM_REF] * 2,
        out_shape=[out] * 2,
        scratch_shapes=[
            pltpu.VMEM((count // group, 2, rows, group * depth), mine.dtype),
            pltpu.VMEM((count // group, group * depth, columns), mine.dtype),
            pltpu.VMEM((2 * rows, columns), jnp.float32),
            pltpu.SemaphoreType.DMA((3 * count,)),
            pltpu.SemaphoreType.DMA((2,)),
        ],
        compiler_params=PARAMS,
        cost_estimate=cost(1000, moved_bytes),
        name="add_product",
    )(place, mine, other, *[array for _, _, array in pieces], *totals)


LOW = 64


def turn_tables(positions, rows):
    freq = ROPE_BASE ** (-(np.arange(HEAD_SIZE // 2) * 2.0) / HEAD_SIZE)
    tables = []
    for places in (np.arange(0, positions, LOW), np.arange(LOW), np.arange(rows)):
        angle = places[:, None] * freq[None, :]
        tables.append(np.concatenate([np.cos(angle), np.cos(angle)], 1))
        tables.append(np.concatenate([-np.sin(angle), np.sin(angle)], 1))
    return [jnp.asarray(table, jnp.float32) for table in tables]


def turned_by(start, tables, cosine, sine):
    high, low = pl.ds(start // LOW, 1), pl.ds(start % LOW, 1)
    for cos_row, sin_row in (
        (tables[0][high], tables[1][high]),
        (tables[2][low], tables[3][low]),
    ):
        cosine, sine = cosine * cos_row - sine * sin_row, sine * cos_row + cosine * sin_row
    return cosine, sine


def rotated(rows, cosine, sine):
    half = HEAD_SIZE // 2
    return rows * cosine + jnp.concatenate([rows[:, half:], rows[:, :half]], 1) * sine


def rows_kernel(place, lengths, owner, *refs):
    totals, came, tables, (out, scratch) = refs[:2], refs[2:4], refs[4:10], refs[10:]
    count_requests, count_rows = lengths.shape[0], scratch.shape[0]
    cosine, sine = turned_by(place[2] * count_rows, tables, tables[4][...], tables[5][...])
    index = place[2] * count_rows + lax.broadcasted_iota(jnp.int32, scratch.shape, 0)
    for r in range(count_requests):
        live = index < lengths[r]
        for h in range(KEY_VALUE_HEADS):
            for part in range(2):
                area = (
                    slice(r * count_rows, (r + 1) * count_rows),
                    slice(h * HEAD_SIZE, (h + 1) * HEAD_SIZE),
                )
                rows = totals[part][area] + came[part][area]
                if part == 0:
                    rows = rotated(rows, cosine, sine)
                scratch[...] = jnp.where(live, rows, 0.0)
                peer = owner[r * KEY_VALUE_HEADS + h]
                lanes = slice(part * HEAD_SIZE, (part + 1) * HEAD_SIZE)
                for b in range(2):
                    picked = scratch[pl.ds(b, count_rows // 2, stride=2), :]
                    out[peer * 2 + b, :, lanes] = picked.astype(jnp.bfloat16)


def outgoing_rows(place, lengths, owner, totals, came, tables):
    count_rows = totals[0].shape[0] // lengths.shape[0]
    out = (owner.shape[0] * 2, count_rows // 2, 2 * HEAD_SIZE)
    return pl.pallas_call(
        rows_kernel,
        in_specs=[SMEM_REF] * 3 + [VMEM_REF] * 10,
        out_specs=VMEM_REF,
        out_shape=jax.ShapeDtypeStruct(out, jnp.bfloat16),
        scratch_shapes=[pltpu.VMEM((count_rows, HEAD_SIZE), jnp.float32)],
        compiler_params=SMALL,
        cost_estimate=cost(1000, 1000),
        name="cache_rows",
    )(place, lengths, owner, *totals, *came, *tables)


def decode_kernel(place, lengths, owner, cache, dec_query, dec_key, dec_value, *refs):
    tables, out = refs[:4], refs[4]
    peer, block = place[2] // 2, place[2] % 2
    length = lengths[0]
    for pair in range(owner.shape[0]):
        length = jnp.where(owner[pair] == peer, lengths[pair // KEY_VALUE_HEADS], length)
    cosine, sine = turned_by(length, tables, tables[2][:STEPS], tables[3][:STEPS])

    def turned(rows):
        return rotated(rows.astype(jnp.float32), cosine, sine)

    def padded(rows):
        return jnp.concatenate([rows, jnp.zeros((16 - STEPS, HEAD_SIZE), jnp.float32)], 0)

    raw = dec_query[peer]
    heads = [raw[:, j * HEAD_SIZE : (j + 1) * HEAD_SIZE] for j in range(QPK)]
    query = jnp.concatenate([turned(head) for head in heads], 0).astype(jnp.bfloat16)
    new_keys = padded(turned(dec_key[peer])).astype(jnp.bfloat16)
    new_value = padded(dec_value[peer].astype(jnp.float32)).astype(jnp.bfloat16)
    contract = (((1,), (1,)), ((), ()))
    scale = 1.0 / HEAD_SIZE**0.5
    old = lax.dot_general(
        query, cache[:, :HEAD_SIZE], contract, preferred_element_type=jnp.float32
    )
    slot = lax.broadcasted_iota(jnp.int32, old.shape, 1) * 2 + block
    old = jnp.where(slot < length, old * scale, -1e30)
    new = lax.dot_general(query, new_keys, contract, preferred_element_type=jnp.float32)
    step = lax.broadcasted_iota(jnp.int32, new.shape, 0) % STEPS
    token = lax.broadcasted_iota(jnp.int32, new.shape, 1)
    new = jnp.where((token <= step) & (block == 0), new * scale, -1e30)
    top = jnp.maximum(jnp.max(old, 1, keepdims=True), jnp.max(new, 1, keepdims=True))
    old, new = jnp.exp(old - top), jnp.exp(new - top)
    total = jnp.sum(old, 1, keepdims=True) + jnp.sum(new, 1, keepdims=True)
    sums = jnp.dot(
        old.astype(jnp.bfloat16), cache[:, HEAD_SIZE:], preferred_element_type=jnp.float32
    )
    out[:, :HEAD_SIZE] = sums + jnp.dot(
        new.astype(jnp.bfloat16), new_value, preferred_element_type=jnp.float32
    )
    half = (QPK * STEPS, HEAD_SIZE // 2)
    out[:, HEAD_SIZE : HEAD_SIZE + half[1]] = jnp.broadcast_to(top, half)
    out[:, HEAD_SIZE + half[1] :] = jnp.broadcast_to(total, half)


def joined_kernel(place, mine, theirs, out):
    share = QPK // 2
    area = pl.ds(place[2] % 2 * share * STEPS, share * STEPS)
    last = HEAD_SIZE + HEAD_SIZE // 2
    sums, tops, totals = [], [], []
    for ref in (mine, theirs):
        sums.append(ref[area, :HEAD_SIZE])
        tops.append(ref[area, HEAD_SIZE : HEAD_SIZE + 1])
        totals.append(ref[area, last : last + 1])
    top = jnp.maximum(tops[0], tops[1])
    scales = [jnp.exp(one - top) for one in tops]
    total = totals[0] * scales[0] + totals[1] * scales[1]
    value = (sums[0] * scales[0] + sums[1] * scales[1]) / total
    for j in range(share):
        rows = value[j * STEPS : (j + 1) * STEPS]
        out[:, j * HEAD_SIZE : (j + 1) * HEAD_SIZE] = rows.astype(jnp.bfloat16)


def decoded(place, lengths, owner, cache, dec_query, dec_key, dec_value, tables):
    mine = pl.pallas_call(
        decode_kernel,
        in_specs=[SMEM_REF] * 3 + [VMEM_REF] * 8,
        out_specs=VMEM_REF,
        out_shape=jax.ShapeDtypeStruct((STEPS * QPK, 2 * HEAD_SIZE), jnp.float32),
        compiler_params=SMALL,
        cost_estimate=cost(1000, 1000),
        name="decode",
    )(place, lengths, owner, cache, dec_query, dec_key, dec_value, *tables[:4])
    return pl.pallas_call(
        joined_kernel,
        in_specs=[SMEM_REF] + [VMEM_REF] * 2,
        out_specs=VMEM_REF,
        out_shape=jax.ShapeDtypeStruct((STEPS, QPK // 2 * HEAD_SIZE), jnp.bfloat16),
        compiler_params=SMALL,
        cost_estimate=cost(1000, 1000),
        name="joined",
    )(place, mine, moved(mine, to_core))


HERE, THERE = 3, 7


def body(hidden, key_weight, value_weight, lengths, owner, dec_query, dec_key, dec_value):
    count_requests, count_rows, width = hidden.shape
    device_id = lax.axis_index("seq")
    group_id = lax.axis_index("groups")
    seq = lax.axis_size("seq")
    planned = seq == 16 and lax.axis_size("groups") == 2
    decode_peers = count_requests * KEY_VALUE_HEADS
    split_point = seq // decode_peers
    tree_levels = split_point.bit_length() - 1
    rows_per_peer = count_rows // split_point
    positions = device_id * count_rows + jnp.arange(count_rows, dtype=jnp.int32)
    total_rows = count_requests * count_rows
    flat = hidden.reshape(total_rows, width)
    if planned:
        core = device_id % 2
        z, y = device_id // 4, device_id // 2 % 2
        layers = [z, z ^ 1, jnp.where(z < 2, 2, 1), jnp.where(z < 2, 3, 0)]
        is_end = (z == 0) | (z == 3)
        place = [group_id, core, device_id]
        place += [layer * 2 + y for layer in layers]
        place += [layer * 2 + 1 - y for layer in layers]
        place = jnp.stack([jnp.asarray(entry, jnp.int32) for entry in place])
    else:
        widened = flat.astype(jnp.float32)
        normed = (
            widened * lax.rsqrt(jnp.mean(widened * widened, -1, keepdims=True) + 1e-05)
        ).astype(jnp.bfloat16)

        def project(weight):
            whole = lax.all_gather(weight, "seq", axis=0, tiled=True)
            return jnp.dot(normed, whole, preferred_element_type=jnp.float32)

    pair_ids = jnp.arange(decode_peers, dtype=jnp.int32)
    matches = owner[None, :] == pair_ids[:, None]
    inverse_order = jnp.sum(jnp.where(matches, pair_ids[None, :], 0), axis=1)
    live_rows = positions[None, :] < lengths[:, None]

    def handed_over(rows):
        rows = jnp.where(live_rows[:, :, None, None], rows, jnp.zeros_like(rows))
        pair_rows = jnp.transpose(rows, (0, 2, 1, 3)).reshape(decode_peers, count_rows, HEAD_SIZE)
        sorted_rows = pair_rows[inverse_order].reshape(
            decode_peers, rows_per_peer, split_point, HEAD_SIZE
        )
        outgoing = jnp.transpose(sorted_rows, (0, 2, 1, 3)).reshape(
            decode_peers * split_point, rows_per_peer, HEAD_SIZE
        )
        return lax.all_to_all(outgoing, "seq", split_axis=0, concat_axis=1, tiled=True)[0]

    if planned:
        weights = (key_weight, value_weight)
        depth = key_weight.shape[0] // 2
        sent = [lax.dynamic_slice_in_dim(w, group_id * depth, depth, 0) for w in weights]
        rest = [lax.dynamic_slice_in_dim(w, depth - group_id * depth, depth, 0) for w in weights]
        tables = turn_tables(count_rows * seq + STEPS, count_rows)
        steps = []

        def gated(value, k):
            return after(value, *steps[k]) if len(steps) > k else value

        near = [moved(block, to_pair) for block in sent]
        middle = [moved(block, to_middle) for block in sent]
        across = [moved(block, to_row) for block in sent]
        mine, kept = prepared(place, flat, seq // 2)
        steps = [[near[k], middle[k], across[k]] for k in range(2)]
        steps[0].append(mine)
        end_b = [moved(gated(middle[k], k), to_end) for k in range(2)]
        middle_c = [moved(gated(near[k], k), to_middle) for k in range(2)]
        near_y = [moved(gated(near[k], k), to_row) for k in range(2)]
        across_x = [moved(gated(across[k], k), to_group) for k in range(2)]
        other = moved(gated(kept, 0), to_core)
        steps = [[end_b[k], middle_c[k], near_y[k], across_x[k], other] for k in range(2)]
        end_c = [moved(gated(middle_c[k], k), to_end) for k in range(2)]
        block_b = [jnp.where(is_end, gated(end_b[k], k), middle[k]) for k in range(2)]
        block_yb = [moved(block, to_row) for block in block_b]
        block_xb = [moved(block, to_group) for block in block_b]
        totals = []
        for k in range(2):
            pieces = [(HERE, 0, sent[k]), (HERE, 1, rest[k]), (THERE, 0, across[k])]
            pieces += [(THERE, 1, across_x[k]), (HERE + 1, 0, near[k]), (THERE + 1, 0, near_y[k])]
            totals.append(product(place, gated(mine, k), other, pieces, (), 3))
        steps = [[end_c[k], block_yb[k], block_xb[k], totals[k][0]] for k in range(2)]
        near_rest = [moved(gated(rest[k], k), to_pair) for k in range(2)]
        block_c = [jnp.where(is_end, gated(end_c[k], k), middle_c[k]) for k in range(2)]
        block_xc = [moved(block, to_group) for block in block_c]
        block_yc = [moved(block, to_row) for block in block_c]
        for k in range(2):
            pieces = [(HERE + 2, 0, block_b[k]), (HERE + 2, 1, block_xb[k])]
            pieces += [(THERE + 2, 0, block_yb[k]), (HERE + 3, 0, block_c[k])]
            totals[k] = product(place, gated(mine, k), other, pieces, totals[k], 4)
        steps = [[near_rest[k], block_xc[k], block_yc[k], totals[k][0]] for k in range(2)]
        ends = []
        for k in range(2):
            ends.append([moved(gated(across_x[k], k), to_pair)])
            ends[k].append(moved(gated(block_yb[k], k), to_group))
            ends[k].append(moved(gated(block_xc[k], k), to_row))
            pieces = [(HERE + 1, 1, near_rest[k]), (HERE + 3, 1, block_xc[k])]
            pieces.append((THERE + 3, 0, block_yc[k]))
            totals[k] = product(place, gated(mine, k), other, pieces, totals[k], 3)
        steps = [[*ends[k], *totals[k]] for k in range(2)]
        sums, came = [], []
        spots = (THERE + 1, THERE + 2, THERE + 3)
        for k in range(2):
            pieces = [(spot, 1, gated(end, k)) for spot, end in zip(spots, ends[k])]
            left = after(mine, *sums)
            total, given = product(place, left, other, pieces, totals[k], 3, (1 - k) << 24)
            sums.append(total)
            came.append(moved(given, to_core))
        outgoing = outgoing_rows(place, lengths, owner, sums, came, tables)
        incoming = lax.all_to_all(outgoing, "seq", split_axis=0, concat_axis=1, tiled=True)
        attended = decoded(
            place, lengths, owner, incoming[0], dec_query, dec_key, dec_value, tables
        )
        return (incoming, attended)
    else:
        cosine, sine_part = rope_table(positions, HEAD_SIZE)
        shape = (count_requests, count_rows, KEY_VALUE_HEADS, HEAD_SIZE)
        unrotated_key = project(key_weight).reshape(shape)
        key_rows = rotate(
            unrotated_key, cosine[:, None, :], sine_part[:, None, :]
        ).astype(jnp.bfloat16)
        cache_keys = handed_over(key_rows)
        cache_values = handed_over(project(value_weight).astype(jnp.bfloat16).reshape(shape))
    slot_count = cache_keys.shape[0]
    decode_peer = device_id // split_point
    block = device_id % split_point
    source_pair = jnp.sum(jnp.where(owner == decode_peer, pair_ids, 0))
    source_request = source_pair // KEY_VALUE_HEADS
    length = jnp.sum(
        jnp.where(jnp.arange(count_requests, dtype=jnp.int32) == source_request, lengths, 0)
    )
    query = lax.dynamic_index_in_dim(dec_query, decode_peer, 0, keepdims=False)
    new_key = lax.dynamic_index_in_dim(dec_key, decode_peer, 0, keepdims=False)
    new_value = lax.dynamic_index_in_dim(dec_value, decode_peer, 0, keepdims=False)
    step_pos = length + jnp.arange(STEPS, dtype=jnp.int32)
    step_cos, step_sin = rope_table(step_pos, HEAD_SIZE)
    query_rot = rotate(
        query.astype(jnp.float32).reshape(STEPS, QPK, HEAD_SIZE),
        step_cos[:, None, :],
        step_sin[:, None, :],
    ).astype(jnp.bfloat16)
    new_keys = rotate(new_key.astype(jnp.float32), step_cos, step_sin).astype(jnp.bfloat16)
    score_scale = 1.0 / HEAD_SIZE**0.5
    old_scores = (
        jnp.einsum(
            "sjd,id->sji", query_rot, cache_keys, preferred_element_type=jnp.float32
        )
        * score_scale
    )
    new_scores = (
        jnp.einsum("sjd,td->sjt", query_rot, new_keys, preferred_element_type=jnp.float32)
        * score_scale
    )
    slot_ids = jnp.arange(slot_count, dtype=jnp.int32) * split_point + block
    old_live = slot_ids < length
    new_live = (jnp.arange(STEPS)[None, :] <= jnp.arange(STEPS)[:, None]) & (block == 0)
    old_scores = jnp.where(old_live[None, None, :], old_scores, -1e30)
    new_scores = jnp.where(new_live[:, None, :], new_scores, -1e30)
    row_max = jnp.maximum(jnp.max(old_scores, -1), jnp.max(new_scores, -1))
    for bit in range(tree_levels):
        row_max = jnp.maximum(row_max, swapped(row_max, "seq", bit))
    old_exp = jnp.exp(old_scores - row_max[..., None])
    new_exp = jnp.exp(new_scores - row_max[..., None])
    denom = jnp.sum(old_exp, -1) + jnp.sum(new_exp, -1)
    for bit in range(tree_levels):
        denom = denom + swapped(denom, "seq", bit)
    old_probs = (old_exp / denom[..., None]).astype(jnp.bfloat16)
    new_probs = (new_exp / denom[..., None]).astype(jnp.bfloat16)
    partial_sum = jnp.einsum(
        "sji,id->sjd", old_probs, cache_values, preferred_element_type=jnp.float32
    )
    partial_sum = partial_sum + jnp.einsum(
        "sjt,td->sjd", new_probs, new_value, preferred_element_type=jnp.float32
    )
    flat_rows = partial_sum.reshape(STEPS, QPK * HEAD_SIZE)
    for bit in range(tree_levels):
        flat_rows = flat_rows + swapped(flat_rows, "seq", bit)
    share = flat_rows.shape[1] // split_point
    mine = lax.dynamic_slice_in_dim(flat_rows, block * share, share, 1)
    cache = jnp.concatenate([cache_keys, cache_values], 1)[None]
    return (cache, mine.astype(jnp.bfloat16))


def solution(mesh):
    placed = (
        P("groups", "seq", None),
        P("seq", None),
        P("seq", None),
        P("groups"),
        P("groups"),
        P("groups", None, None),
        P("groups", None, None),
        P("groups", None, None),
    )
    return jax.shard_map(
        body,
        mesh=mesh,
        in_specs=placed,
        out_specs=(P(("groups", "seq"), None, None), P("groups", "seq")),
        check_vma=False,
    )
```

time: 115 us -> 126 us (1.096)
  waiting for transfers between devices: 50.9 us -> 18.1 us
  blocking collectives: 0 us -> 22.7 us
  starting transfers between devices: 25.6 us -> 41.2 us
  Pallas kernels: 21.3 us -> 29.5 us
  other arithmetic: 7.54 us -> 2.04 us
  local copies, waits for them, and re-layouts: 5.31 us -> 10.3 us
  between operations: 3.5 us -> 1.12 us
    all_to_all x0 -> x1, blocking collectives: none -> 22.7 us  [body(): lax.all_to_all(outgoing, 'seq', split_axis=0, concat_axis=1, tiled=True)]
    ppermute x19 -> x36, starting transfers between devices: 21.3 us -> 41.2 us  [moved(): return lax.ppermute(block, ('groups', 'seq'), route)]
    ppermute x19 -> x36, waiting for transfers between devices: 35.1 us -> 18.1 us  [moved(): return lax.ppermute(block, ('groups', 'seq'), route)]
    all_to_all x1 -> x0, waiting for transfers between devices: 15.8 us -> none  [body(): lax.all_to_all(outgoing, 'seq', split_axis=0, concat_axis=1, tiled=True)]
    pallas_call x6 -> x11, Pallas kernels: 14 us -> 25.6 us  [the longest x8 22.2 us: product(): pl.pallas_call(functools.partial(product_kernel, plan, group, bool(totals...]
    unnamed x25 -> x51, local copies, waits for them, and re-layouts: 3.97 us -> 9.1 us
    all_to_all x1 -> x0, starting transfers between devices: 4.32 us -> none  [body(): lax.all_to_all(outgoing, 'seq', split_axis=0, concat_axis=1, tiled=True)]
    pallas_call x1, Pallas kernels: 7.21 us -> 3.86 us  [prepared(): pl.pallas_call(prepare_kernel, grid_spec=pltpu.PrefetchScalarGridSpec(num...]
  transfers between devices with their start and end apart: 20 -> 36, of which waited for: 11 -> 11; matrix products, arithmetic and copies ran while one was open for 7% -> 2% of each run, Pallas kernels for 14% -> 21%
where the time goes in v13:
time: 126 us; the launch traced here: 125 us
  starting transfers between devices  41.2 us (33%)
  Pallas kernels  29.5 us (23%)
  blocking collectives  22.7 us (18%)
  waiting for transfers between devices  18.1 us (14%)
  local copies, waits for them, and re-layouts  10.3 us (8%)
  other arithmetic  2.04 us (2%)
    ppermute x36, starting transfers between devices, moved(): return lax.ppermute(block, ('groups', 'seq'), route)  41.2 us
    all_to_all x1, blocking collectives, body(): lax.all_to_all(outgoing, 'seq', split_axis=0, concat_axis=1, tiled=True)  22.7 us
    pallas_call x8, Pallas kernels, product(): pl.pallas_call(functools.partial(product_kernel, plan, group, bool(totals...  22.2 us
    ppermute x36, waiting for transfers between devices, moved(): return lax.ppermute(block, ('groups', 'seq'), route)  18.1 us
    unnamed x51, local copies, waits for them, and re-layouts  9.1 us
    pallas_call x1, Pallas kernels, prepared(): pl.pallas_call(prepare_kernel, grid_spec=pltpu.PrefetchScalarGridSpec(num...  3.86 us
  transfers between devices with their start and end apart: 36, of which 11 were waited for; matrix products, arithmetic and copies ran while one was open for 2% of the time, Pallas kernels for 21%

profile of v13, /device:TPU:0, one launch (start us, length us, event | category | flops | bytes accessed | tf_op | source)
XLA Modules:
  0.0 124.9 jit_solution(16664524406807915848)
XLA Ops:
  0.6 1.1 constant_dynamic-slice_fusion.2
  1.7 3.1 %collective-permute-start = (bf16[256,512]{1,0:T(8,128)(2,1)S(1)}, bf16[256,512]{1,0:T(8,128)(2,1)S(1)}, u32[]{:S(2)}, u32[]{:S(2)}) collective-permute-start(bf16[256,512]{1,0:T(8,128)(2,1)S(1)} %get-tuple-element.109.refs_0_), channel_id=1, source_target_pairs={{0,4},{1,5},{2,6},{3,7},{4,0},{5,1},{6,2},{7,3},{8,12},{9,13},{10,... | collective-permute-start | bytes 786440 | tf_op jit(solution)/shard_map/ppermute | solution.py:66
  4.8 1.4 %collective-permute-start.1 = (bf16[256,512]{1,0:T(8,128)(2,1)S(1)}, bf16[256,512]{1,0:T(8,128)(2,1)}, u32[]{:S(2)}, u32[]{:S(2)}) collective-permute-start(bf16[256,512]{1,0:T(8,128)(2,1)S(1)} %get-tuple-element.109.refs_0_), channel_id=1, source_target_pairs={{4,8},{5,9},{6,10},{7,11},{8,4},{9,5},{10,6},{11,7},{20,24},{21,25... | collective-permute-start | bytes 786440 | tf_op jit(solution)/shard_map/ppermute | solution.py:66
  6.2 1.5 %collective-permute-start.2 = (bf16[256,512]{1,0:T(8,128)(2,1)S(1)}, bf16[256,512]{1,0:T(8,128)(2,1)}, u32[]{:S(2)}, u32[]{:S(2)}) collective-permute-start(bf16[256,512]{1,0:T(8,128)(2,1)S(1)} %get-tuple-element.109.refs_0_), channel_id=1, source_target_pairs={{0,2},{1,3},{2,0},{3,1},{4,6},{5,7},{6,4},{7,5},{8,10},{9,11},{10,... | collective-permute-start | bytes 786440 | tf_op jit(solution)/shard_map/ppermute | solution.py:66
  7.8 2.5 %copy-done = bf16[2,160,8192]{2,1,0:T(8,128)(2,1)S(1)} copy-done((bf16[2,160,8192]{2,1,0:T(8,128)(2,1)S(1)}, bf16[2,160,8192]{2,1,0:T(8,128)(2,1)}, u32[]{:S(2)}) %copy-start) | copy-done | bytes 5242904
  10.3 3.9 %normed_halves.1 = (bf16[16,320,256]{2,1,0:T(8,128)(2,1)S(1)}, bf16[16,320,256]{2,1,0:T(8,128)(2,1)}) custom-call(s32[11]{0:T(128)S(1)} %stack.47.place, bf16[320,8192]{1,0:T(8,128)(2,1)S(1)} %bitcast.16), custom_call_target="tpu_custom_call" | custom-call | flops 1000 | bytes 1000 | tf_op jit(solution)/shard_map/normed_halves/pallas_call | solution.py:135
  14.1 0.7 copy-done.3
  14.9 0.8 collective-permute-start.17
  15.7 3.5 %collective-permute-start.18 = (bf16[256,512]{1,0:T(8,128)(2,1)S(1)}, bf16[256,512]{1,0:T(8,128)(2,1)}, u32[]{:S(2)}, u32[]{:S(2)}) collective-permute-start(bf16[256,512]{1,0:T(8,128)(2,1)S(1)} %get-tuple-element.107.refs_0_), channel_id=1, source_target_pairs={{0,4},{1,5},{2,6},{3,7},{4,0},{5,1},{6,2},{7,3},{8,12},{9,13},{10,... | collective-permute-start | bytes 786440 | tf_op jit(solution)/shard_map/ppermute | solution.py:66
  19.2 1.4 %collective-permute-start.19 = (bf16[256,512]{1,0:T(8,128)(2,1)S(1)}, bf16[256,512]{1,0:T(8,128)(2,1)}, u32[]{:S(2)}, u32[]{:S(2)}) collective-permute-start(bf16[256,512]{1,0:T(8,128)(2,1)S(1)} %get-tuple-element.107.refs_0_), channel_id=1, source_target_pairs={{4,8},{5,9},{6,10},{7,11},{8,4},{9,5},{10,6},{11,7},{20,24},{21,25... | collective-permute-start | bytes 786440 | tf_op jit(solution)/shard_map/ppermute | solution.py:66
  20.6 0.7 copy-done.1
  21.3 1.5 %collective-permute-start.4 = (bf16[256,512]{1,0:T(8,128)(2,1)}, bf16[256,512]{1,0:T(8,128)(2,1)S(1)}, u32[]{:S(2)}, u32[]{:S(2)}) collective-permute-start(bf16[256,512]{1,0:T(8,128)(2,1)} %collective-permute-done.2.refs_2_), channel_id=1, source_target_pairs={{0,16},{1,17},{2,18},{3,19},{4,20},{5,21},{6,22},{7,23},{8,24},{9,... | collective-permute-start | bytes 786440 | tf_op jit(solution)/shard_map/ppermute | solution.py:66
  22.8 0.9 collective-permute-done.17.refs_2_
  23.7 0.7 collective-permute-start.5
  24.4 1.6 %collective-permute-done.18.refs_4_ = bf16[256,512]{1,0:T(8,128)(2,1)} collective-permute-done((bf16[256,512]{1,0:T(8,128)(2,1)S(1)}, bf16[256,512]{1,0:T(8,128)(2,1)}, u32[]{:S(2)}, u32[]{:S(2)}) %collective-permute-start.18) | collective-permute-done | bytes 262176 | tf_op jit(solution)/shard_map/ppermute | solution.py:66
  26.0 1.3 %collective-permute-start.6 = (bf16[256,512]{1,0:T(8,128)(2,1)}, bf16[256,512]{1,0:T(8,128)(2,1)S(1)}, u32[]{:S(2)}, u32[]{:S(2)}) collective-permute-start(bf16[256,512]{1,0:T(8,128)(2,1)} %collective-permute-done.1), channel_id=1, source_target_pairs={{4,0},{5,1},{6,2},{7,3},{8,12},{9,13},{10,14},{11,15},{20,16},{21,... | collective-permute-start | bytes 786440 | tf_op jit(solution)/shard_map/ppermute | solution.py:66
  27.3 1.6 %collective-permute-start.7 = (bf16[256,512]{1,0:T(8,128)(2,1)}, bf16[256,512]{1,0:T(8,128)(2,1)S(1)}, u32[]{:S(2)}, u32[]{:S(2)}) collective-permute-start(bf16[256,512]{1,0:T(8,128)(2,1)} %copy-done.3), channel_id=1, source_target_pairs={{0,2},{1,3},{2,0},{3,1},{4,6},{5,7},{6,4},{7,5},{8,10},{9,11},{10,... | collective-permute-start | bytes 786440 | tf_op jit(solution)/shard_map/ppermute | solution.py:66
  28.9 0.8 collective-permute-done.4.refs_3_
  29.7 0.7 copy-done.5
  30.4 1.5 %collective-permute-start.20 = (bf16[256,512]{1,0:T(8,128)(2,1)}, bf16[256,512]{1,0:T(8,128)(2,1)}, u32[]{:S(2)}, u32[]{:S(2)}) collective-permute-start(bf16[256,512]{1,0:T(8,128)(2,1)} %collective-permute-done.17.refs_2_), channel_id=1, source_target_pairs={{0,16},{1,17},{2,18},{3,19},{4,20},{5,21},{6,22},{7,23},{8,24},{9,... | collective-permute-start | bytes 786440 | tf_op jit(solution)/shard_map/ppermute | solution.py:66
  31.9 1.4 %collective-permute-start.21 = (bf16[256,512]{1,0:T(8,128)(2,1)}, bf16[256,512]{1,0:T(8,128)(2,1)}, u32[]{:S(2)}, u32[]{:S(2)}) collective-permute-start(bf16[256,512]{1,0:T(8,128)(2,1)} %collective-permute-done.18.refs_4_), channel_id=1, source_target_pairs={{4,8},{5,9},{6,10},{7,11},{8,4},{9,5},{10,6},{11,7},{20,24},{21,25... | collective-permute-start | bytes 786440 | tf_op jit(solution)/shard_map/ppermute | solution.py:66
  33.2 3.9 %collective-permute-done.6 = bf16[256,512]{1,0:T(8,128)(2,1)S(1)} collective-permute-done((bf16[256,512]{1,0:T(8,128)(2,1)}, bf16[256,512]{1,0:T(8,128)(2,1)S(1)}, u32[]{:S(2)}, u32[]{:S(2)}) %collective-permute-start.6) | collective-permute-done | bytes 262176 | tf_op jit(solution)/shard_map/ppermute | solution.py:66
  37.1 1.3 %collective-permute-start.22 = (bf16[256,512]{1,0:T(8,128)(2,1)}, bf16[256,512]{1,0:T(8,128)(2,1)}, u32[]{:S(2)}, u32[]{:S(2)}) collective-permute-start(bf16[256,512]{1,0:T(8,128)(2,1)} %collective-permute-done.19), channel_id=1, source_target_pairs={{4,0},{5,1},{6,2},{7,3},{8,12},{9,13},{10,14},{11,15},{20,16},{21,... | collective-permute-start | bytes 786440 | tf_op jit(solution)/shard_map/ppermute | solution.py:66
  38.4 0.7 copy-done.8
  39.7 1.3 %collective-permute-start.8 = (bf16[256,512]{1,0:T(8,128)(2,1)}, bf16[256,512]{1,0:T(8,128)(2,1)S(1)}, u32[]{:S(2)}, u32[]{:S(2)}) collective-permute-start(bf16[256,512]{1,0:T(8,128)(2,1)} %copy-done.22), channel_id=1, source_target_pairs={{4,0},{5,1},{6,2},{7,3},{8,12},{9,13},{10,14},{11,15},{20,16},{21,... | collective-permute-start | bytes 786440 | tf_op jit(solution)/shard_map/ppermute | solution.py:66
  41.0 1.0 broadcast_select_fusion.3.refs_0_
  42.0 1.6 %collective-permute-start.9 = (bf16[256,512]{1,0:T(8,128)(2,1)S(1)}, bf16[256,512]{1,0:T(8,128)(2,1)S(1)}, u32[]{:S(2)}, u32[]{:S(2)}) collective-permute-start(bf16[256,512]{1,0:T(8,128)(2,1)S(1)} %broadcast_select_fusion.3.refs_0_), channel_id=1, source_target_pairs={{0,2},{1,3},{2,0},{3,1},{4,6},{5,7},{6,4},{7,5},{8,10},{9,11},{10,... | collective-permute-start | bytes 786440 | tf_op jit(solution)/shard_map/ppermute | solution.py:66
  43.6 1.5 %collective-permute-start.10 = (bf16[256,512]{1,0:T(8,128)(2,1)S(1)}, bf16[256,512]{1,0:T(8,128)(2,1)S(1)}, u32[]{:S(2)}, u32[]{:S(2)}) collective-permute-start(bf16[256,512]{1,0:T(8,128)(2,1)S(1)} %broadcast_select_fusion.3.refs_0_), channel_id=1, source_target_pairs={{0,16},{1,17},{2,18},{3,19},{4,20},{5,21},{6,22},{7,23},{8,24},{9,... | collective-permute-start | bytes 786440 | tf_op jit(solution)/shard_map/ppermute | solution.py:66
  45.0 3.5 %collective-permute-done.22 = bf16[256,512]{1,0:T(8,128)(2,1)} collective-permute-done((bf16[256,512]{1,0:T(8,128)(2,1)}, bf16[256,512]{1,0:T(8,128)(2,1)}, u32[]{:S(2)}, u32[]{:S(2)}) %collective-permute-start.22) | collective-permute-done | bytes 262176 | tf_op jit(solution)/shard_map/ppermute | solution.py:66
  48.7 1.3 %collective-permute-start.24 = (bf16[256,512]{1,0:T(8,128)(2,1)}, bf16[256,512]{1,0:T(8,128)(2,1)S(1)}, u32[]{:S(2)}, u32[]{:S(2)}) collective-permute-start(bf16[256,512]{1,0:T(8,128)(2,1)} %collective-permute-done.21), channel_id=1, source_target_pairs={{4,0},{5,1},{6,2},{7,3},{8,12},{9,13},{10,14},{11,15},{20,16},{21,... | collective-permute-start | bytes 786440 | tf_op jit(solution)/shard_map/ppermute | solution.py:66
  50.0 1.0 broadcast_select_fusion.1.refs_0_
  51.0 0.6 collective-permute-start.25
  51.6 2.5 %collective-permute-done.8 = bf16[256,512]{1,0:T(8,128)(2,1)S(1)} collective-permute-done((bf16[256,512]{1,0:T(8,128)(2,1)}, bf16[256,512]{1,0:T(8,128)(2,1)S(1)}, u32[]{:S(2)}, u32[]{:S(2)}) %collective-permute-start.8) | collective-permute-done | bytes 262176 | tf_op jit(solution)/shard_map/ppermute | solution.py:66
  54.1 1.5 %collective-permute-start.26 = (bf16[256,512]{1,0:T(8,128)(2,1)S(1)}, bf16[256,512]{1,0:T(8,128)(2,1)S(1)}, u32[]{:S(2)}, u32[]{:S(2)}) collective-permute-start(bf16[256,512]{1,0:T(8,128)(2,1)S(1)} %broadcast_select_fusion.1.refs_0_), channel_id=1, source_target_pairs={{0,16},{1,17},{2,18},{3,19},{4,20},{5,21},{6,22},{7,23},{8,24},{9,... | collective-permute-start | bytes 786440 | tf_op jit(solution)/shard_map/ppermute | solution.py:66
  55.6 0.9 copy-done.4
  56.5 0.9 copy-done.6
  57.5 0.9 copy-done.9
  58.4 3.2 %add_product.8 = (f32[320,512]{1,0:T(8,128)S(1)}, f32[320,512]{1,0:T(8,128)S(1)}) custom-call(s32[11]{0:T(128)S(1)} %stack.47.place, bf16[16,320,256]{2,1,0:T(8,128)(2,1)S(1)} %get-tuple-element.96.mine, bf16[16,320,256]{2,1,0:T(8,128)(2,1)} %collective-permute-done.3.other, bf16[256,512]{1,0:T(8,128)(2,1)S(1)} %get-tuple-element.109.refs_0_, ...), custom_call_target="tpu_custom_call" | custom-call | flops 1000 | bytes 1000 | tf_op jit(solution)/shard_map/add_product/pallas_call | solution.py:202
  61.6 0.5 collective-permute-start.11
  62.2 0.6 collective-permute-start.12
  62.8 1.9 %collective-permute-start.13 = (bf16[256,512]{1,0:T(8,128)(2,1)S(1)}, bf16[256,512]{1,0:T(8,128)(2,1)S(1)}, u32[]{:S(2)}, u32[]{:S(2)}) collective-permute-start(bf16[256,512]{1,0:T(8,128)(2,1)S(1)} %broadcast_select_fusion.2.refs_3_), channel_id=1, source_target_pairs={{0,2},{1,3},{2,0},{3,1},{4,6},{5,7},{6,4},{7,5},{8,10},{9,11},{10,... | collective-permute-start | bytes 786440 | tf_op jit(solution)/shard_map/ppermute | solution.py:66
  64.7 3.2 %add_product.12 = (f32[320,512]{1,0:T(8,128)S(1)}, f32[320,512]{1,0:T(8,128)S(1)}) custom-call(s32[11]{0:T(128)S(1)} %stack.47.place, bf16[16,320,256]{2,1,0:T(8,128)(2,1)S(1)} %get-tuple-element.96.mine, bf16[16,320,256]{2,1,0:T(8,128)(2,1)} %collective-permute-done.3.other, bf16[256,512]{1,0:T(8,128)(2,1)S(1)} %copy-done.2, ...), custom_call_target="tpu_custom_call" | custom-call | flops 1000 | bytes 1000 | tf_op jit(solution)/shard_map/add_product/pallas_call | solution.py:202
  68.0 1.6 %collective-permute-start.28 = (bf16[256,512]{1,0:T(8,128)(2,1)S(1)}, bf16[256,512]{1,0:T(8,128)(2,1)S(1)}, u32[]{:S(2)}, u32[]{:S(2)}) collective-permute-start(bf16[256,512]{1,0:T(8,128)(2,1)S(1)} %broadcast_select_fusion.refs_3_), channel_id=1, source_target_pairs={{0,16},{1,17},{2,18},{3,19},{4,20},{5,21},{6,22},{7,23},{8,24},{9,... | collective-permute-start | bytes 786440 | tf_op jit(solution)/shard_map/ppermute | solution.py:66
  69.6 1.2 collective-permute-done.11.refs_0_
  70.8 0.5 collective-permute-start.29
  71.3 2.9 %add_product.9 = (f32[320,512]{1,0:T(8,128)S(1)}, f32[320,512]{1,0:T(8,128)S(1)}) custom-call(s32[11]{0:T(128)S(1)} %stack.47.place, bf16[16,320,256]{2,1,0:T(8,128)(2,1)S(1)} %get-tuple-element.96.mine, bf16[16,320,256]{2,1,0:T(8,128)(2,1)} %collective-permute-done.3.other, bf16[256,512]{1,0:T(8,128)(2,1)S(1)} %broadcast_select_fusion.3.refs_0_, ...), custom_call_target="tpu_custom_call" | custom-call | flops 1000 | bytes 1000 | tf_op jit(solution)/shard_map/add_product/pallas_call | solution.py:202
  74.2 1.9 %collective-permute-start.14 = (bf16[256,512]{1,0:T(8,128)(2,1)S(1)}, bf16[256,512]{1,0:T(8,128)(2,1)S(1)}, u32[]{:S(2)}, u32[]{:S(2)}) collective-permute-start(bf16[256,512]{1,0:T(8,128)(2,1)S(1)} %copy-done.7), channel_id=1, source_target_pairs={{0,4},{1,5},{2,6},{3,7},{4,0},{5,1},{6,2},{7,3},{8,12},{9,13},{10,... | collective-permute-start | bytes 786440 | tf_op jit(solution)/shard_map/ppermute | solution.py:66
  76.2 0.8 collective-permute-done.27.refs_0_
  77.1 1.0 collective-permute-start.16
  78.1 2.9 %add_product.13 = (f32[320,512]{1,0:T(8,128)S(1)}, f32[320,512]{1,0:T(8,128)S(1)}) custom-call(s32[11]{0:T(128)S(1)} %stack.47.place, bf16[16,320,256]{2,1,0:T(8,128)(2,1)S(1)} %get-tuple-element.96.mine, bf16[16,320,256]{2,1,0:T(8,128)(2,1)} %collective-permute-done.3.other, bf16[256,512]{1,0:T(8,128)(2,1)S(1)} %broadcast_select_fusion.1.refs_0_, ...), custom_call_target="tpu_custom_call" | custom-call | flops 1000 | bytes 1000 | tf_op jit(solution)/shard_map/add_product/pallas_call | solution.py:202
  81.2 1.9 %collective-permute-start.31 = (bf16[256,512]{1,0:T(8,128)(2,1)S(1)}, bf16[256,512]{1,0:T(8,128)(2,1)S(1)}, u32[]{:S(2)}, u32[]{:S(2)}) collective-permute-start(bf16[256,512]{1,0:T(8,128)(2,1)S(1)} %collective-permute-done.25.refs_2_), channel_id=1, source_target_pairs={{0,16},{1,17},{2,18},{3,19},{4,20},{5,21},{6,22},{7,23},{8,24},{9,... | collective-permute-start | bytes 786440 | tf_op jit(solution)/shard_map/ppermute | solution.py:66
  83.1 0.8 collective-permute-start.32
  83.9 2.5 %add_product.10 = (f32[320,512]{1,0:T(8,128)S(1)}, f32[320,512]{1,0:T(8,128)S(1)}) custom-call(s32[11]{0:T(128)S(1)} %stack.47.place, bf16[16,320,256]{2,1,0:T(8,128)(2,1)S(1)} %get-tuple-element.96.mine, bf16[16,320,256]{2,1,0:T(8,128)(2,1)} %collective-permute-done.3.other, bf16[256,512]{1,0:T(8,128)(2,1)S(1)} %collective-permute-done.11.refs_0_, ...), custom_call_target="tpu_custom_call" | custom-call | flops 1000 | bytes 1000 | tf_op jit(solution)/shard_map/add_product/pallas_call | solution.py:202
  86.4 2.5 %add_product.14 = (f32[320,512]{1,0:T(8,128)S(1)}, f32[320,512]{1,0:T(8,128)S(1)}) custom-call(s32[11]{0:T(128)S(1)} %stack.47.place, bf16[16,320,256]{2,1,0:T(8,128)(2,1)S(1)} %get-tuple-element.96.mine, bf16[16,320,256]{2,1,0:T(8,128)(2,1)} %collective-permute-done.3.other, bf16[256,512]{1,0:T(8,128)(2,1)S(1)} %collective-permute-done.27.refs_0_, ...), custom_call_target="tpu_custom_call" | custom-call | flops 1000 | bytes 1000 | tf_op jit(solution)/shard_map/add_product/pallas_call | solution.py:202
  89.0 2.5 %add_product.11 = (f32[320,512]{1,0:T(8,128)S(1)}, f32[320,512]{1,0:T(8,128)S(1)}) custom-call(s32[11]{0:T(128)S(1)} %stack.47.place, bf16[16,320,256]{2,1,0:T(8,128)(2,1)S(1)} %get-tuple-element.96.mine, bf16[16,320,256]{2,1,0:T(8,128)(2,1)} %collective-permute-done.3.other, bf16[256,512]{1,0:T(8,128)(2,1)S(1)} %collective-permute-done.14.refs_0_, ...), custom_call_target="tpu_custom_call" | custom-call | flops 1000 | bytes 16777216 | tf_op jit(solution)/shard_map/add_product/pallas_call | solution.py:202
  91.7 2.5 %add_product.15 = (f32[320,512]{1,0:T(8,128)S(1)}, f32[320,512]{1,0:T(8,128)S(1)}) custom-call(s32[11]{0:T(128)S(1)} %stack.47.place, bf16[16,320,256]{2,1,0:T(8,128)(2,1)S(1)} %get-tuple-element.96.mine, bf16[16,320,256]{2,1,0:T(8,128)(2,1)} %collective-permute-done.3.other, bf16[256,512]{1,0:T(8,128)(2,1)S(1)} %collective-permute-done.30.refs_0_, ...), custom_call_target="tpu_custom_call" | custom-call | flops 1000 | tf_op jit(solution)/shard_map/add_product/pallas_call | solution.py:202
  94.3 0.6 collective-permute-start.34
  94.9 1.7 %collective-permute-done.34.refs_3_ = f32[320,512]{1,0:T(8,128)S(1)} collective-permute-done((f32[320,512]{1,0:T(8,128)S(1)}, f32[320,512]{1,0:T(8,128)S(1)}, u32[]{:S(2)}, u32[]{:S(2)}) %collective-permute-start.34) | collective-permute-done | bytes 655392 | tf_op jit(solution)/shard_map/ppermute | solution.py:66
  96.7 1.0 cache_rows.1
  97.7 22.7 %all_to_all.12 = bf16[16,80,256]{2,1,0:T(8,128)(2,1)S(1)} all-to-all(bf16[16,80,256]{2,1,0:T(8,128)(2,1)S(1)} %cache_rows.1), channel_id=1, replica_groups=mesh['groups'=2,'seq'=16] {'seq'}, dimensions={0} | all-to-all | bytes 1310720 | tf_op jit(solution)/shard_map/all_to_all | solution.py:481
  120.4 1.1 decode.1.mine
  121.9 0.9 collective-permute-done.35.theirs
  122.8 1.3 %joined.1 = bf16[4,512]{1,0:T(4,128)(2,1)} custom-call(s32[11]{0:T(128)S(1)} %stack.47.place, f32[32,256]{1,0:T(8,128)S(1)} %decode.1.mine, f32[32,256]{1,0:T(8,128)S(1)} %collective-permute-done.35.theirs), custom_call_target="tpu_custom_call" | custom-call | flops 1000 | bytes 1000 | tf_op jit(solution)/shard_map/joined/pallas_call | solution.py:359
  124.1 0.8 copy.17
  (79 shorter events, 1.9 us)
Async XLA Ops:
  1.7 12.4 %collective-permute-start = (bf16[256,512]{1,0:T(8,128)(2,1)S(1)}, bf16[256,512]{1,0:T(8,128)(2,1)S(1)}, u32[]{:S(2)}, u32[]{:S(2)}) collective-permute-start(bf16[256,512]{1,0:T(8,128)(2,1)S(1)} %get-tuple-element.109.refs_0_), channel_id=1, source_target_pairs={{0,4},{1,5},{2,6},{3,7},{4,0},{5,1},{6,2},{7,3},{8,12},{9,13},{10,... | collective-permute-start | bytes 786440 | tf_op jit(solution)/shard_map/ppermute | solution.py:66
  4.8 9.3 %collective-permute-start.1 = (bf16[256,512]{1,0:T(8,128)(2,1)S(1)}, bf16[256,512]{1,0:T(8,128)(2,1)}, u32[]{:S(2)}, u32[]{:S(2)}) collective-permute-start(bf16[256,512]{1,0:T(8,128)(2,1)S(1)} %get-tuple-element.109.refs_0_), channel_id=1, source_target_pairs={{4,8},{5,9},{6,10},{7,11},{8,4},{9,5},{10,6},{11,7},{20,24},{21,25... | collective-permute-start | bytes 786440 | tf_op jit(solution)/shard_map/ppermute | solution.py:66
  6.2 8.0 %collective-permute-start.2 = (bf16[256,512]{1,0:T(8,128)(2,1)S(1)}, bf16[256,512]{1,0:T(8,128)(2,1)}, u32[]{:S(2)}, u32[]{:S(2)}) collective-permute-start(bf16[256,512]{1,0:T(8,128)(2,1)S(1)} %get-tuple-element.109.refs_0_), channel_id=1, source_target_pairs={{0,2},{1,3},{2,0},{3,1},{4,6},{5,7},{6,4},{7,5},{8,10},{9,11},{10,... | collective-permute-start | bytes 786440 | tf_op jit(solution)/shard_map/ppermute | solution.py:66
  7.8 2.5 %copy-start = (bf16[2,160,8192]{2,1,0:T(8,128)(2,1)S(1)}, bf16[2,160,8192]{2,1,0:T(8,128)(2,1)}, u32[]{:S(2)}) copy-start(bf16[2,160,8192]{2,1,0:T(8,128)(2,1)} %param.14) | copy-start | bytes 15728644
  10.3 4.6 %copy-start.21 = (bf16[512,512]{1,0:T(8,128)(2,1)S(1)}, bf16[512,512]{1,0:T(8,128)(2,1)}, u32[]{:S(2)}) copy-start(bf16[512,512]{1,0:T(8,128)(2,1)} %param.16) | copy-start | bytes 1572868
  14.1 0.7 copy-start.3
  14.8 24.9 %collective-permute-start.3 = (bf16[16,320,256]{2,1,0:T(8,128)(2,1)}, bf16[16,320,256]{2,1,0:T(8,128)(2,1)}, u32[]{:S(2)}, u32[]{:S(2)}) collective-permute-start(bf16[16,320,256]{2,1,0:T(8,128)(2,1)} %get-tuple-element.56), channel_id=1, source_target_pairs={{0,1},{1,0},{2,3},{3,2},{4,5},{5,4},{6,7},{7,6},{8,9},{9,8},{10,11... | collective-permute-start | bytes 7864328 | tf_op jit(solution)/shard_map/ppermute | solution.py:66
  14.9 8.9 %collective-permute-start.17 = (bf16[256,512]{1,0:T(8,128)(2,1)S(1)}, bf16[256,512]{1,0:T(8,128)(2,1)}, u32[]{:S(2)}, u32[]{:S(2)}) collective-permute-start(bf16[256,512]{1,0:T(8,128)(2,1)S(1)} %get-tuple-element.107.refs_0_), channel_id=1, source_target_pairs={{0,2},{1,3},{2,0},{3,1},{4,6},{5,7},{6,4},{7,5},{8,10},{9,11},{10,... | collective-permute-start | bytes 786440 | tf_op jit(solution)/shard_map/ppermute | solution.py:66
  15.7 10.3 %collective-permute-start.18 = (bf16[256,512]{1,0:T(8,128)(2,1)S(1)}, bf16[256,512]{1,0:T(8,128)(2,1)}, u32[]{:S(2)}, u32[]{:S(2)}) collective-permute-start(bf16[256,512]{1,0:T(8,128)(2,1)S(1)} %get-tuple-element.107.refs_0_), channel_id=1, source_target_pairs={{0,4},{1,5},{2,6},{3,7},{4,0},{5,1},{6,2},{7,3},{8,12},{9,13},{10,... | collective-permute-start | bytes 786440 | tf_op jit(solution)/shard_map/ppermute | solution.py:66
  19.2 8.1 %collective-permute-start.19 = (bf16[256,512]{1,0:T(8,128)(2,1)S(1)}, bf16[256,512]{1,0:T(8,128)(2,1)}, u32[]{:S(2)}, u32[]{:S(2)}) collective-permute-start(bf16[256,512]{1,0:T(8,128)(2,1)S(1)} %get-tuple-element.107.refs_0_), channel_id=1, source_target_pairs={{4,8},{5,9},{6,10},{7,11},{8,4},{9,5},{10,6},{11,7},{20,24},{21,25... | collective-permute-start | bytes 786440 | tf_op jit(solution)/shard_map/ppermute | solution.py:66
  20.6 0.7 copy-start.1
  21.3 8.4 %collective-permute-start.4 = (bf16[256,512]{1,0:T(8,128)(2,1)}, bf16[256,512]{1,0:T(8,128)(2,1)S(1)}, u32[]{:S(2)}, u32[]{:S(2)}) collective-permute-start(bf16[256,512]{1,0:T(8,128)(2,1)} %collective-permute-done.2.refs_2_), channel_id=1, source_target_pairs={{0,16},{1,17},{2,18},{3,19},{4,20},{5,21},{6,22},{7,23},{8,24},{9,... | collective-permute-start | bytes 786440 | tf_op jit(solution)/shard_map/ppermute | solution.py:66
  23.7 8.1 %collective-permute-start.5 = (bf16[256,512]{1,0:T(8,128)(2,1)}, bf16[256,512]{1,0:T(8,128)(2,1)S(1)}, u32[]{:S(2)}, u32[]{:S(2)}) collective-permute-start(bf16[256,512]{1,0:T(8,128)(2,1)} %copy-done.3), channel_id=1, source_target_pairs={{4,8},{5,9},{6,10},{7,11},{8,4},{9,5},{10,6},{11,7},{20,24},{21,25... | collective-permute-start | bytes 786440 | tf_op jit(solution)/shard_map/ppermute | solution.py:66
  26.0 11.1 %collective-permute-start.6 = (bf16[256,512]{1,0:T(8,128)(2,1)}, bf16[256,512]{1,0:T(8,128)(2,1)S(1)}, u32[]{:S(2)}, u32[]{:S(2)}) collective-permute-start(bf16[256,512]{1,0:T(8,128)(2,1)} %collective-permute-done.1), channel_id=1, source_target_pairs={{4,0},{5,1},{6,2},{7,3},{8,12},{9,13},{10,14},{11,15},{20,16},{21,... | collective-permute-start | bytes 786440 | tf_op jit(solution)/shard_map/ppermute | solution.py:66
  27.3 11.1 %collective-permute-start.7 = (bf16[256,512]{1,0:T(8,128)(2,1)}, bf16[256,512]{1,0:T(8,128)(2,1)S(1)}, u32[]{:S(2)}, u32[]{:S(2)}) collective-permute-start(bf16[256,512]{1,0:T(8,128)(2,1)} %copy-done.3), channel_id=1, source_target_pairs={{0,2},{1,3},{2,0},{3,1},{4,6},{5,7},{6,4},{7,5},{8,10},{9,11},{10,... | collective-permute-start | bytes 786440 | tf_op jit(solution)/shard_map/ppermute | solution.py:66
  29.7 0.7 copy-start.5
  30.4 11.6 %collective-permute-start.20 = (bf16[256,512]{1,0:T(8,128)(2,1)}, bf16[256,512]{1,0:T(8,128)(2,1)}, u32[]{:S(2)}, u32[]{:S(2)}) collective-permute-start(bf16[256,512]{1,0:T(8,128)(2,1)} %collective-permute-done.17.refs_2_), channel_id=1, source_target_pairs={{0,16},{1,17},{2,18},{3,19},{4,20},{5,21},{6,22},{7,23},{8,24},{9,... | collective-permute-start | bytes 786440 | tf_op jit(solution)/shard_map/ppermute | solution.py:66
  31.9 6.5 %copy-start.22 = (bf16[256,512]{1,0:T(8,128)(2,1)}, bf16[256,512]{1,0:T(8,128)(2,1)S(1)}, u32[]{:S(2)}) copy-start(bf16[256,512]{1,0:T(8,128)(2,1)S(1)} %collective-permute-done.5) | copy-start | bytes 786436
  31.9 11.7 %collective-permute-start.21 = (bf16[256,512]{1,0:T(8,128)(2,1)}, bf16[256,512]{1,0:T(8,128)(2,1)}, u32[]{:S(2)}, u32[]{:S(2)}) collective-permute-start(bf16[256,512]{1,0:T(8,128)(2,1)} %collective-permute-done.18.refs_4_), channel_id=1, source_target_pairs={{4,8},{5,9},{6,10},{7,11},{8,4},{9,5},{10,6},{11,7},{20,24},{21,25... | collective-permute-start | bytes 786440 | tf_op jit(solution)/shard_map/ppermute | solution.py:66
  37.1 1.3 %copy-start.24 = (bf16[256,512]{1,0:T(8,128)(2,1)}, bf16[256,512]{1,0:T(8,128)(2,1)S(1)}, u32[]{:S(2)}) copy-start(bf16[256,512]{1,0:T(8,128)(2,1)S(1)} %collective-permute-done.6) | copy-start | bytes 786436
  37.1 11.5 %collective-permute-start.22 = (bf16[256,512]{1,0:T(8,128)(2,1)}, bf16[256,512]{1,0:T(8,128)(2,1)}, u32[]{:S(2)}, u32[]{:S(2)}) collective-permute-start(bf16[256,512]{1,0:T(8,128)(2,1)} %collective-permute-done.19), channel_id=1, source_target_pairs={{4,0},{5,1},{6,2},{7,3},{8,12},{9,13},{10,14},{11,15},{20,16},{21,... | collective-permute-start | bytes 786440 | tf_op jit(solution)/shard_map/ppermute | solution.py:66
  38.4 0.7 copy-start.8
  39.2 9.6 %collective-permute-start.23 = (bf16[256,512]{1,0:T(8,128)(2,1)}, bf16[256,512]{1,0:T(8,128)(2,1)}, u32[]{:S(2)}, u32[]{:S(2)}) collective-permute-start(bf16[256,512]{1,0:T(8,128)(2,1)} %collective-permute-done.18.refs_4_), channel_id=1, source_target_pairs={{0,2},{1,3},{2,0},{3,1},{4,6},{5,7},{6,4},{7,5},{8,10},{9,11},{10,... | collective-permute-start | bytes 786440 | tf_op jit(solution)/shard_map/ppermute | solution.py:66
  39.7 14.4 %collective-permute-start.8 = (bf16[256,512]{1,0:T(8,128)(2,1)}, bf16[256,512]{1,0:T(8,128)(2,1)S(1)}, u32[]{:S(2)}, u32[]{:S(2)}) collective-permute-start(bf16[256,512]{1,0:T(8,128)(2,1)} %copy-done.22), channel_id=1, source_target_pairs={{4,0},{5,1},{6,2},{7,3},{8,12},{9,13},{10,14},{11,15},{20,16},{21,... | collective-permute-start | bytes 786440 | tf_op jit(solution)/shard_map/ppermute | solution.py:66
  42.0 19.7 %collective-permute-start.9 = (bf16[256,512]{1,0:T(8,128)(2,1)S(1)}, bf16[256,512]{1,0:T(8,128)(2,1)S(1)}, u32[]{:S(2)}, u32[]{:S(2)}) collective-permute-start(bf16[256,512]{1,0:T(8,128)(2,1)S(1)} %broadcast_select_fusion.3.refs_0_), channel_id=1, source_target_pairs={{0,2},{1,3},{2,0},{3,1},{4,6},{5,7},{6,4},{7,5},{8,10},{9,11},{10,... | collective-permute-start | bytes 786440 | tf_op jit(solution)/shard_map/ppermute | solution.py:66
  43.6 18.1 %collective-permute-start.10 = (bf16[256,512]{1,0:T(8,128)(2,1)S(1)}, bf16[256,512]{1,0:T(8,128)(2,1)S(1)}, u32[]{:S(2)}, u32[]{:S(2)}) collective-permute-start(bf16[256,512]{1,0:T(8,128)(2,1)S(1)} %broadcast_select_fusion.3.refs_0_), channel_id=1, source_target_pairs={{0,16},{1,17},{2,18},{3,19},{4,20},{5,21},{6,22},{7,23},{8,24},{9,... | collective-permute-start | bytes 786440 | tf_op jit(solution)/shard_map/ppermute | solution.py:66
  48.7 14.1 %collective-permute-start.24 = (bf16[256,512]{1,0:T(8,128)(2,1)}, bf16[256,512]{1,0:T(8,128)(2,1)S(1)}, u32[]{:S(2)}, u32[]{:S(2)}) collective-permute-start(bf16[256,512]{1,0:T(8,128)(2,1)} %collective-permute-done.21), channel_id=1, source_target_pairs={{4,0},{5,1},{6,2},{7,3},{8,12},{9,13},{10,14},{11,15},{20,16},{21,... | collective-permute-start | bytes 786440 | tf_op jit(solution)/shard_map/ppermute | solution.py:66
  51.0 16.9 %collective-permute-start.25 = (bf16[256,512]{1,0:T(8,128)(2,1)S(1)}, bf16[256,512]{1,0:T(8,128)(2,1)S(1)}, u32[]{:S(2)}, u32[]{:S(2)}) collective-permute-start(bf16[256,512]{1,0:T(8,128)(2,1)S(1)} %broadcast_select_fusion.1.refs_0_), channel_id=1, source_target_pairs={{0,2},{1,3},{2,0},{3,1},{4,6},{5,7},{6,4},{7,5},{8,10},{9,11},{10,... | collective-permute-start | bytes 786440 | tf_op jit(solution)/shard_map/ppermute | solution.py:66
  54.1 13.8 %collective-permute-start.26 = (bf16[256,512]{1,0:T(8,128)(2,1)S(1)}, bf16[256,512]{1,0:T(8,128)(2,1)S(1)}, u32[]{:S(2)}, u32[]{:S(2)}) collective-permute-start(bf16[256,512]{1,0:T(8,128)(2,1)S(1)} %broadcast_select_fusion.1.refs_0_), channel_id=1, source_target_pairs={{0,16},{1,17},{2,18},{3,19},{4,20},{5,21},{6,22},{7,23},{8,24},{9,... | collective-permute-start | bytes 786440 | tf_op jit(solution)/shard_map/ppermute | solution.py:66
  55.6 0.9 copy-start.4
  56.5 0.9 copy-start.6
  57.5 0.9 copy-start.9
  58.4 3.8 %copy-start.23 = (bf16[256,512]{1,0:T(8,128)(2,1)S(1)}, bf16[256,512]{1,0:T(8,128)(2,1)}, u32[]{:S(2)}) copy-start(bf16[256,512]{1,0:T(8,128)(2,1)} %copy-done.22) | copy-start | bytes 786436
  58.4 6.3 %copy-start.2 = (bf16[256,512]{1,0:T(8,128)(2,1)S(1)}, bf16[256,512]{1,0:T(8,128)(2,1)}, u32[]{:S(2)}) copy-start(bf16[256,512]{1,0:T(8,128)(2,1)} %copy-done.1) | copy-start | bytes 786436
  61.6 9.1 %collective-permute-start.11 = (bf16[256,512]{1,0:T(8,128)(2,1)S(1)}, bf16[256,512]{1,0:T(8,128)(2,1)S(1)}, u32[]{:S(2)}, u32[]{:S(2)}) collective-permute-start(bf16[256,512]{1,0:T(8,128)(2,1)S(1)} %get-tuple-element.64.refs_1_), channel_id=1, source_target_pairs={{0,4},{1,5},{2,6},{3,7},{4,0},{5,1},{6,2},{7,3},{8,12},{9,13},{10,... | collective-permute-start | bytes 786440 | tf_op jit(solution)/shard_map/ppermute | solution.py:66
  62.2 11.9 %collective-permute-start.12 = (bf16[256,512]{1,0:T(8,128)(2,1)S(1)}, bf16[256,512]{1,0:T(8,128)(2,1)S(1)}, u32[]{:S(2)}, u32[]{:S(2)}) collective-permute-start(bf16[256,512]{1,0:T(8,128)(2,1)S(1)} %broadcast_select_fusion.2.refs_3_), channel_id=1, source_target_pairs={{0,16},{1,17},{2,18},{3,19},{4,20},{5,21},{6,22},{7,23},{8,24},{9,... | collective-permute-start | bytes 786440 | tf_op jit(solution)/shard_map/ppermute | solution.py:66
  62.8 11.4 %collective-permute-start.13 = (bf16[256,512]{1,0:T(8,128)(2,1)S(1)}, bf16[256,512]{1,0:T(8,128)(2,1)S(1)}, u32[]{:S(2)}, u32[]{:S(2)}) collective-permute-start(bf16[256,512]{1,0:T(8,128)(2,1)S(1)} %broadcast_select_fusion.2.refs_3_), channel_id=1, source_target_pairs={{0,2},{1,3},{2,0},{3,1},{4,6},{5,7},{6,4},{7,5},{8,10},{9,11},{10,... | collective-permute-start | bytes 786440 | tf_op jit(solution)/shard_map/ppermute | solution.py:66
  67.9 9.1 %collective-permute-start.27 = (bf16[256,512]{1,0:T(8,128)(2,1)S(1)}, bf16[256,512]{1,0:T(8,128)(2,1)S(1)}, u32[]{:S(2)}, u32[]{:S(2)}) collective-permute-start(bf16[256,512]{1,0:T(8,128)(2,1)S(1)} %get-tuple-element.88.refs_1_), channel_id=1, source_target_pairs={{0,4},{1,5},{2,6},{3,7},{4,0},{5,1},{6,2},{7,3},{8,12},{9,13},{10,... | collective-permute-start | bytes 786440 | tf_op jit(solution)/shard_map/ppermute | solution.py:66
  68.0 12.9 %collective-permute-start.28 = (bf16[256,512]{1,0:T(8,128)(2,1)S(1)}, bf16[256,512]{1,0:T(8,128)(2,1)S(1)}, u32[]{:S(2)}, u32[]{:S(2)}) collective-permute-start(bf16[256,512]{1,0:T(8,128)(2,1)S(1)} %broadcast_select_fusion.refs_3_), channel_id=1, source_target_pairs={{0,16},{1,17},{2,18},{3,19},{4,20},{5,21},{6,22},{7,23},{8,24},{9,... | collective-permute-start | bytes 786440 | tf_op jit(solution)/shard_map/ppermute | solution.py:66
  70.8 10.2 %collective-permute-start.29 = (bf16[256,512]{1,0:T(8,128)(2,1)S(1)}, bf16[256,512]{1,0:T(8,128)(2,1)S(1)}, u32[]{:S(2)}, u32[]{:S(2)}) collective-permute-start(bf16[256,512]{1,0:T(8,128)(2,1)S(1)} %broadcast_select_fusion.refs_3_), channel_id=1, source_target_pairs={{0,2},{1,3},{2,0},{3,1},{4,6},{5,7},{6,4},{7,5},{8,10},{9,11},{10,... | collective-permute-start | bytes 786440 | tf_op jit(solution)/shard_map/ppermute | solution.py:66
  71.3 2.9 %copy-start.7 = (bf16[256,512]{1,0:T(8,128)(2,1)S(1)}, bf16[256,512]{1,0:T(8,128)(2,1)}, u32[]{:S(2)}) copy-start(bf16[256,512]{1,0:T(8,128)(2,1)} %copy-done.5) | copy-start | bytes 786436
  74.2 8.9 %collective-permute-start.14 = (bf16[256,512]{1,0:T(8,128)(2,1)S(1)}, bf16[256,512]{1,0:T(8,128)(2,1)S(1)}, u32[]{:S(2)}, u32[]{:S(2)}) collective-permute-start(bf16[256,512]{1,0:T(8,128)(2,1)S(1)} %copy-done.7), channel_id=1, source_target_pairs={{0,4},{1,5},{2,6},{3,7},{4,0},{5,1},{6,2},{7,3},{8,12},{9,13},{10,... | collective-permute-start | bytes 786440 | tf_op jit(solution)/shard_map/ppermute | solution.py:66
  76.1 12.9 %collective-permute-start.15 = (bf16[256,512]{1,0:T(8,128)(2,1)S(1)}, bf16[256,512]{1,0:T(8,128)(2,1)S(1)}, u32[]{:S(2)}, u32[]{:S(2)}) collective-permute-start(bf16[256,512]{1,0:T(8,128)(2,1)S(1)} %collective-permute-done.9.refs_2_), channel_id=1, source_target_pairs={{0,16},{1,17},{2,18},{3,19},{4,20},{5,21},{6,22},{7,23},{8,24},{9,... | collective-permute-start | bytes 786440 | tf_op jit(solution)/shard_map/ppermute | solution.py:66
  77.1 11.9 %collective-permute-start.16 = (bf16[256,512]{1,0:T(8,128)(2,1)S(1)}, bf16[256,512]{1,0:T(8,128)(2,1)S(1)}, u32[]{:S(2)}, u32[]{:S(2)}) collective-permute-start(bf16[256,512]{1,0:T(8,128)(2,1)S(1)} %collective-permute-done.12.refs_1_), channel_id=1, source_target_pairs={{0,2},{1,3},{2,0},{3,1},{4,6},{5,7},{6,4},{7,5},{8,10},{9,11},{10,... | collective-permute-start | bytes 786440 | tf_op jit(solution)/shard_map/ppermute | solution.py:66
  81.0 10.6 %collective-permute-start.30 = (bf16[256,512]{1,0:T(8,128)(2,1)}, bf16[256,512]{1,0:T(8,128)(2,1)S(1)}, u32[]{:S(2)}, u32[]{:S(2)}) collective-permute-start(bf16[256,512]{1,0:T(8,128)(2,1)} %collective-permute-done.20.refs_3_), channel_id=1, source_target_pairs={{0,4},{1,5},{2,6},{3,7},{4,0},{5,1},{6,2},{7,3},{8,12},{9,13},{10,... | collective-permute-start | bytes 786440 | tf_op jit(solution)/shard_map/ppermute | solution.py:66
  81.2 10.3 %collective-permute-start.31 = (bf16[256,512]{1,0:T(8,128)(2,1)S(1)}, bf16[256,512]{1,0:T(8,128)(2,1)S(1)}, u32[]{:S(2)}, u32[]{:S(2)}) collective-permute-start(bf16[256,512]{1,0:T(8,128)(2,1)S(1)} %collective-permute-done.25.refs_2_), channel_id=1, source_target_pairs={{0,16},{1,17},{2,18},{3,19},{4,20},{5,21},{6,22},{7,23},{8,24},{9,... | collective-permute-start | bytes 786440 | tf_op jit(solution)/shard_map/ppermute | solution.py:66
  83.1 8.4 %collective-permute-start.32 = (bf16[256,512]{1,0:T(8,128)(2,1)S(1)}, bf16[256,512]{1,0:T(8,128)(2,1)S(1)}, u32[]{:S(2)}, u32[]{:S(2)}) collective-permute-start(bf16[256,512]{1,0:T(8,128)(2,1)S(1)} %collective-permute-done.28.refs_1_), channel_id=1, source_target_pairs={{0,2},{1,3},{2,0},{3,1},{4,6},{5,7},{6,4},{7,5},{8,10},{9,11},{10,... | collective-permute-start | bytes 786440 | tf_op jit(solution)/shard_map/ppermute | solution.py:66
  91.6 5.0 %copy-start.10 = (f32[64,128]{1,0:T(8,128)S(1)}, f32[64,128]{1,0:T(8,128)}, u32[]{:S(2)}) copy-start(f32[64,128]{1,0:T(8,128)} %constant.70.clone.refs_6_.refs_2_) | copy-start | bytes 98308
  91.6 5.0 %copy-start.11 = (f32[64,128]{1,0:T(8,128)S(1)}, f32[64,128]{1,0:T(8,128)}, u32[]{:S(2)}) copy-start(f32[64,128]{1,0:T(8,128)} %constant.71.clone.refs_7_.refs_3_) | copy-start | bytes 98308
  91.6 5.0 %copy-start.12 = (f32[41,128]{1,0:T(8,128)S(1)}, f32[41,128]{1,0:T(8,128)}, u32[]{:S(2)}) copy-start(f32[41,128]{1,0:T(8,128)} %constant.68.clone.refs_4_.refs_0_) | copy-start | bytes 62980
  91.6 5.0 %copy-start.13 = (f32[41,128]{1,0:T(8,128)S(1)}, f32[41,128]{1,0:T(8,128)}, u32[]{:S(2)}) copy-start(f32[41,128]{1,0:T(8,128)} %constant.69.clone.refs_5_.refs_1_) | copy-start | bytes 62980
  91.6 5.0 %copy-start.14 = (f32[160,128]{1,0:T(8,128)S(1)}, f32[160,128]{1,0:T(8,128)}, u32[]{:S(2)}) copy-start(f32[160,128]{1,0:T(8,128)} %constant.72.clone.refs_8_) | copy-start | bytes 245764
  91.6 5.0 %copy-start.15 = (f32[160,128]{1,0:T(8,128)S(1)}, f32[160,128]{1,0:T(8,128)}, u32[]{:S(2)}) copy-start(f32[160,128]{1,0:T(8,128)} %constant.73.clone.refs_9_) | copy-start | bytes 245764
  91.6 5.0 %copy-start.19 = (s32[2]{0:T(128)S(1)}, s32[2]{0:T(128)}, u32[]{:S(2)}) copy-start(s32[2]{0:T(128)} %lengths.3) | copy-start | bytes 28
  91.7 5.0 %copy-start.20 = (s32[8]{0:T(128)S(1)}, s32[8]{0:T(128)}, u32[]{:S(2)}) copy-start(s32[8]{0:T(128)} %owner.3) | copy-start | bytes 100
  91.7 3.2 %collective-permute-start.33 = (f32[320,512]{1,0:T(8,128)S(1)}, f32[320,512]{1,0:T(8,128)S(1)}, u32[]{:S(2)}, u32[]{:S(2)}) collective-permute-start(f32[320,512]{1,0:T(8,128)S(1)} %get-tuple-element.104), channel_id=1, source_target_pairs={{0,1},{1,0},{2,3},{3,2},{4,5},{5,4},{6,7},{7,6},{8,9},{9,8},{10,11... | collective-permute-start | bytes 1966088 | tf_op jit(solution)/shard_map/ppermute | solution.py:66
  94.3 26.1 %copy-start.16 = (bf16[8,4,1024]{2,1,0:T(4,128)(2,1)S(1)}, bf16[8,4,1024]{2,1,0:T(4,128)(2,1)}, u32[]{:S(2)}) copy-start(bf16[8,4,1024]{2,1,0:T(4,128)(2,1)} %dec_query.1) | copy-start | bytes 196612
  94.3 26.1 %copy-start.17 = (bf16[8,4,128]{2,1,0:T(4,128)(2,1)S(1)}, bf16[8,4,128]{2,1,0:T(4,128)(2,1)}, u32[]{:S(2)}) copy-start(bf16[8,4,128]{2,1,0:T(4,128)(2,1)} %dec_key.1) | copy-start | bytes 24580
  94.3 26.1 %copy-start.18 = (bf16[8,4,128]{2,1,0:T(4,128)(2,1)S(1)}, bf16[8,4,128]{2,1,0:T(4,128)(2,1)}, u32[]{:S(2)}) copy-start(bf16[8,4,128]{2,1,0:T(4,128)(2,1)} %dec_value.1) | copy-start | bytes 24580
  94.3 2.3 %collective-permute-start.34 = (f32[320,512]{1,0:T(8,128)S(1)}, f32[320,512]{1,0:T(8,128)S(1)}, u32[]{:S(2)}, u32[]{:S(2)}) collective-permute-start(f32[320,512]{1,0:T(8,128)S(1)} %get-tuple-element.105), channel_id=1, source_target_pairs={{0,1},{1,0},{2,3},{3,2},{4,5},{5,4},{6,7},{7,6},{8,9},{9,8},{10,11... | collective-permute-start | bytes 1966088 | tf_op jit(solution)/shard_map/ppermute | solution.py:66
  121.5 1.3 %collective-permute-start.35 = (f32[32,256]{1,0:T(8,128)S(1)}, f32[32,256]{1,0:T(8,128)S(1)}, u32[]{:S(2)}, u32[]{:S(2)}) collective-permute-start(f32[32,256]{1,0:T(8,128)S(1)} %decode.1.mine), channel_id=1, source_target_pairs={{0,1},{1,0},{2,3},{3,2},{4,5},{5,4},{6,7},{7,6},{8,9},{9,8},{10,11... | collective-permute-start | bytes 98312 | tf_op jit(solution)/shard_map/ppermute | solution.py:66

commit v14 on v13

--- a/solution.py
+++ b/solution.py
@@ -246,7 +246,8 @@
 
 
 def rows_kernel(place, lengths, owner, *refs):
-    totals, came, tables, (out, scratch) = refs[:2], refs[2:4], refs[4:10], refs[10:]
+    total, came, *tables, out, scratch = refs
+    columns = total.shape[1] // 2
     count_requests, count_rows = lengths.shape[0], scratch.shape[0]
     cosine, sine = turned_by(place[2] * count_rows, tables, tables[4][...], tables[5][...])
     index = place[2] * count_rows + lax.broadcasted_iota(jnp.int32, scratch.shape, 0)
@@ -254,11 +255,12 @@
         live = index < lengths[r]
         for h in range(KEY_VALUE_HEADS):
             for part in range(2):
+                first = part * columns + h * HEAD_SIZE
                 area = (
                     slice(r * count_rows, (r + 1) * count_rows),
-                    slice(h * HEAD_SIZE, (h + 1) * HEAD_SIZE),
+                    slice(first, first + HEAD_SIZE),
                 )
-                rows = totals[part][area] + came[part][area]
+                rows = total[area] + came[area]
                 if part == 0:
                     rows = rotated(rows, cosine, sine)
                 scratch[...] = jnp.where(live, rows, 0.0)
@@ -269,19 +271,19 @@
                     out[peer * 2 + b, :, lanes] = picked.astype(jnp.bfloat16)
 
 
-def outgoing_rows(place, lengths, owner, totals, came, tables):
-    count_rows = totals[0].shape[0] // lengths.shape[0]
+def outgoing_rows(place, lengths, owner, total, came, tables):
+    count_rows = total.shape[0] // lengths.shape[0]
     out = (owner.shape[0] * 2, count_rows // 2, 2 * HEAD_SIZE)
     return pl.pallas_call(
         rows_kernel,
-        in_specs=[SMEM_REF] * 3 + [VMEM_REF] * 10,
+        in_specs=[SMEM_REF] * 3 + [VMEM_REF] * 8,
         out_specs=VMEM_REF,
         out_shape=jax.ShapeDtypeStruct(out, jnp.bfloat16),
         scratch_shapes=[pltpu.VMEM((count_rows, HEAD_SIZE), jnp.float32)],
         compiler_params=SMALL,
         cost_estimate=cost(1000, 1000),
         name="cache_rows",
-    )(place, lengths, owner, *totals, *came, *tables)
+    )(place, lengths, owner, total, came, *tables)
 
 
 def decode_kernel(place, lengths, owner, cache, dec_query, dec_key, dec_value, *refs):
@@ -419,65 +421,53 @@
         return lax.all_to_all(outgoing, "seq", split_axis=0, concat_axis=1, tiled=True)[0]
 
     if planned:
-        weights = (key_weight, value_weight)
         depth = key_weight.shape[0] // 2
-        sent = [lax.dynamic_slice_in_dim(w, group_id * depth, depth, 0) for w in weights]
-        rest = [lax.dynamic_slice_in_dim(w, depth - group_id * depth, depth, 0) for w in weights]
+
+        def half_block(first):
+            halves = [
+                lax.dynamic_slice_in_dim(weight, first, depth, 0)
+                for weight in (key_weight, value_weight)
+            ]
+            return jnp.concatenate(halves, 1)
+
+        sent = half_block(group_id * depth)
         tables = turn_tables(count_rows * seq + STEPS, count_rows)
-        steps = []
-
-        def gated(value, k):
-            return after(value, *steps[k]) if len(steps) > k else value
-
-        near = [moved(block, to_pair) for block in sent]
-        middle = [moved(block, to_middle) for block in sent]
-        across = [moved(block, to_row) for block in sent]
+        near = moved(sent, to_pair)
+        middle = moved(sent, to_middle)
+        across = moved(sent, to_row)
+        rest = half_block(depth - group_id * depth)
         mine, kept = prepared(place, flat, seq // 2)
-        steps = [[near[k], middle[k], across[k]] for k in range(2)]
-        steps[0].append(mine)
-        end_b = [moved(gated(middle[k], k), to_end) for k in range(2)]
-        middle_c = [moved(gated(near[k], k), to_middle) for k in range(2)]
-        near_y = [moved(gated(near[k], k), to_row) for k in range(2)]
-        across_x = [moved(gated(across[k], k), to_group) for k in range(2)]
-        other = moved(gated(kept, 0), to_core)
-        steps = [[end_b[k], middle_c[k], near_y[k], across_x[k], other] for k in range(2)]
-        end_c = [moved(gated(middle_c[k], k), to_end) for k in range(2)]
-        block_b = [jnp.where(is_end, gated(end_b[k], k), middle[k]) for k in range(2)]
-        block_yb = [moved(block, to_row) for block in block_b]
-        block_xb = [moved(block, to_group) for block in block_b]
-        totals = []
-        for k in range(2):
-            pieces = [(HERE, 0, sent[k]), (HERE, 1, rest[k]), (THERE, 0, across[k])]
-            pieces += [(THERE, 1, across_x[k]), (HERE + 1, 0, near[k]), (THERE + 1, 0, near_y[k])]
-            totals.append(product(place, gated(mine, k), other, pieces, (), 3))
-        steps = [[end_c[k], block_yb[k], block_xb[k], totals[k][0]] for k in range(2)]
-        near_rest = [moved(gated(rest[k], k), to_pair) for k in range(2)]
-        block_c = [jnp.where(is_end, gated(end_c[k], k), middle_c[k]) for k in range(2)]
-        block_xc = [moved(block, to_group) for block in block_c]
-        block_yc = [moved(block, to_row) for block in block_c]
-        for k in range(2):
-            pieces = [(HERE + 2, 0, block_b[k]), (HERE + 2, 1, block_xb[k])]
-            pieces += [(THERE + 2, 0, block_yb[k]), (HERE + 3, 0, block_c[k])]
-            totals[k] = product(place, gated(mine, k), other, pieces, totals[k], 4)
-        steps = [[near_rest[k], block_xc[k], block_yc[k], totals[k][0]] for k in range(2)]
-        ends = []
-        for k in range(2):
-            ends.append([moved(gated(across_x[k], k), to_pair)])
-            ends[k].append(moved(gated(block_yb[k], k), to_group))
-            ends[k].append(moved(gated(block_xc[k], k), to_row))
-            pieces = [(HERE + 1, 1, near_rest[k]), (HERE + 3, 1, block_xc[k])]
-            pieces.append((THERE + 3, 0, block_yc[k]))
-            totals[k] = product(place, gated(mine, k), other, pieces, totals[k], 3)
-        steps = [[*ends[k], *totals[k]] for k in range(2)]
-        sums, came = [], []
-        spots = (THERE + 1, THERE + 2, THERE + 3)
-        for k in range(2):
-            pieces = [(spot, 1, gated(end, k)) for spot, end in zip(spots, ends[k])]
-            left = after(mine, *sums)
-            total, given = product(place, left, other, pieces, totals[k], 3, (1 - k) << 24)
-            sums.append(total)
-            came.append(moved(given, to_core))
-        outgoing = outgoing_rows(place, lengths, owner, sums, came, tables)
+        layers, rows = (near, middle), (across, mine, rest)
+        end_b = moved(after(middle, *layers), to_end)
+        middle_c = moved(after(near, *layers), to_middle)
+        near_y = moved(after(near, *layers, *rows), to_row)
+        across_x = moved(after(across, *layers, *rows), to_group)
+        other = moved(after(kept, *layers, *rows), to_core)
+        layers, rows, before = (end_b, middle_c), (near_y, across_x, other), rows
+        end_c = moved(after(middle_c, *layers, *before), to_end)
+        block_b = jnp.where(is_end, after(end_b, *layers), middle)
+        block_yb = moved(after(block_b, *rows), to_row)
+        block_xb = moved(after(block_b, *rows), to_group)
+        pieces = [(HERE, 0, sent), (HERE, 1, rest), (THERE, 0, across)]
+        pieces += [(THERE, 1, across_x), (HERE + 1, 0, near), (THERE + 1, 0, near_y)]
+        totals = product(place, after(mine, *rows, block_b), other, pieces, (), 3)
+        layers, rows, before = (end_c,), (block_yb, block_xb, totals[0]), rows
+        near_rest = moved(after(rest, *layers, *before), to_pair)
+        block_c = jnp.where(is_end, after(end_c, *layers), middle_c)
+        block_xc = moved(after(block_c, *rows), to_group)
+        block_yc = moved(after(block_c, *rows), to_row)
+        pieces = [(HERE + 2, 0, block_b), (HERE + 2, 1, block_xb)]
+        pieces += [(THERE + 2, 0, block_yb), (HERE + 3, 0, block_c)]
+        totals = product(place, after(mine, *rows, block_c), other, pieces, totals, 4)
+        layers, rows, before = (near_rest,), (block_xc, block_yc, totals[0]), rows
+        end_a = moved(after(across_x, *layers, *before), to_pair)
+        ends = [moved(after(block_yb, *rows), to_group), moved(after(block_xc, *rows), to_row)]
+        pieces = [(HERE + 1, 1, near_rest), (HERE + 3, 1, block_xc)]
+        pieces += [(THERE + 3, 0, block_yc), (THERE + 1, 1, end_a)]
+        totals = product(place, after(mine, *rows, end_a), other, pieces, totals, 4, 1 << 24)
+        pieces = [(THERE + 2, 1, ends[0]), (THERE + 3, 1, ends[1])]
+        total, given = product(place, after(mine, *ends, *totals), other, pieces, totals, 2)
+        outgoing = outgoing_rows(place, lengths, owner, total, moved(given, to_core), tables)
         incoming = lax.all_to_all(outgoing, "seq", split_axis=0, concat_axis=1, tiled=True)
         attended = decoded(
             place, lengths, owner, incoming[0], dec_query, dec_key, dec_value, tables

time: 126 us -> 121 us (0.960)
  waiting for transfers between devices: 18.1 us -> 44.6 us
  starting transfers between devices: 41.2 us -> 24.2 us
  Pallas kernels: 29.5 us -> 21.6 us
  local copies, waits for them, and re-layouts: 10.3 us -> 5.44 us
  blocking collectives: 22.7 us -> 21 us
    ppermute x36 -> x19, waiting for transfers between devices: 18.1 us -> 44.6 us  [moved(): return lax.ppermute(block, ('groups', 'seq'), route)]
    ppermute x36 -> x19, starting transfers between devices: 41.2 us -> 24.2 us  [moved(): return lax.ppermute(block, ('groups', 'seq'), route)]
    pallas_call x8 -> x4, Pallas kernels: 22.2 us -> 14.3 us  [product(): pl.pallas_call(functools.partial(product_kernel, plan, group, bool(totals...]
    unnamed x51 -> x29, local copies, waits for them, and re-layouts: 9.1 us -> 3.39 us
    all_to_all x1, blocking collectives: 22.7 us -> 21 us  [body(): lax.all_to_all(outgoing, 'seq', split_axis=0, concat_axis=1, tiled=True)]
  transfers between devices with their start and end apart: 36 -> 19, of which waited for: 11 -> 12; matrix products, arithmetic and copies ran while one was open for 2% -> 3% of each run, Pallas kernels for 21% -> 13%
where the time goes in v14:
time: 121 us
  waiting for transfers between devices  44.6 us (37%)
  starting transfers between devices  24.2 us (20%)
  Pallas kernels  21.6 us (18%)
  blocking collectives  21 us (17%)
  local copies, waits for them, and re-layouts  5.44 us (4%)
  other arithmetic  3.17 us (3%)
    ppermute x19, waiting for transfers between devices, moved(): return lax.ppermute(block, ('groups', 'seq'), route)  44.6 us
    ppermute x19, starting transfers between devices, moved(): return lax.ppermute(block, ('groups', 'seq'), route)  24.2 us
    all_to_all x1, blocking collectives, body(): lax.all_to_all(outgoing, 'seq', split_axis=0, concat_axis=1, tiled=True)  21 us
    pallas_call x4, Pallas kernels, product(): pl.pallas_call(functools.partial(product_kernel, plan, group, bool(totals...  14.3 us
    pallas_call x1, Pallas kernels, prepared(): pl.pallas_call(prepare_kernel, grid_spec=pltpu.PrefetchScalarGridSpec(num...  3.9 us
    unnamed x29, local copies, waits for them, and re-layouts  3.39 us
  transfers between devices with their start and end apart: 19, of which 12 were waited for; matrix products, arithmetic and copies ran while one was open for 3% of the time, Pallas kernels for 13%

profile of v14, /device:TPU:0, one launch (start us, length us, event | category | flops | bytes accessed | tf_op | source)
XLA Modules:
  0.0 121.0 jit_solution(15542863908330489541)
XLA Ops:
  0.6 2.0 %constant_dynamic-slice_fusion = (bf16[256,512]{1,0:T(8,128)(2,1)S(1)}, bf16[256,512]{1,0:T(8,128)(2,1)S(1)}, bf16[256,512]{1,0:T(8,128)(2,1)S(1)}, bf16[256,512]{1,0:T(8,128)(2,1)}) fusion(bf16[512,512]{1,0:T(8,128)(2,1)} %param.16, s32[]{:T(128)S(6)} %select_n.54, s32[]{:T(128)S(6)} %select_n.52, bf16[512,512]{1,0:T(8,128)(2,1)} %param.15), kind=kLoop, calls=%fused_computation.4 | loop fusion | bytes 2097160 | tf_op jit(solution)/shard_map/dynamic_slice | solution.py:428
  2.6 0.1 pad_maximum_fusion.refs_0_
  2.7 1.5 %collective-permute-start = (bf16[256,1024]{1,0:T(8,128)(2,1)S(1)}, bf16[256,1024]{1,0:T(8,128)(2,1)}, u32[]{:S(2)}, u32[]{:S(2)}) collective-permute-start(bf16[256,1024]{1,0:T(8,128)(2,1)S(1)} %pad_maximum_fusion.refs_0_), channel_id=1, source_target_pairs={{4,8},{5,9},{6,10},{7,11},{8,4},{9,5},{10,6},{11,7},{20,24},{21,25... | collective-permute-start | bytes 1572872 | tf_op jit(solution)/shard_map/ppermute | solution.py:66
  4.1 5.1 %collective-permute-start.1 = (bf16[256,1024]{1,0:T(8,128)(2,1)S(1)}, bf16[256,1024]{1,0:T(8,128)(2,1)}, u32[]{:S(2)}, u32[]{:S(2)}) collective-permute-start(bf16[256,1024]{1,0:T(8,128)(2,1)S(1)} %pad_maximum_fusion.refs_0_), channel_id=1, source_target_pairs={{0,4},{1,5},{2,6},{3,7},{4,0},{5,1},{6,2},{7,3},{8,12},{9,13},{10,... | collective-permute-start | bytes 1572872 | tf_op jit(solution)/shard_map/ppermute | solution.py:66
  9.2 1.5 %collective-permute-start.4 = (bf16[256,1024]{1,0:T(8,128)(2,1)S(1)}, bf16[256,1024]{1,0:T(8,128)(2,1)}, u32[]{:S(2)}, u32[]{:S(2)}) collective-permute-start(bf16[256,1024]{1,0:T(8,128)(2,1)S(1)} %pad_maximum_fusion.refs_0_), channel_id=1, source_target_pairs={{0,2},{1,3},{2,0},{3,1},{4,6},{5,7},{6,4},{7,5},{8,10},{9,11},{10,... | collective-permute-start | bytes 1572872 | tf_op jit(solution)/shard_map/ppermute | solution.py:66
  10.8 0.1 stack.47.place
  10.9 2.5 %copy-done = bf16[2,160,8192]{2,1,0:T(8,128)(2,1)S(1)} copy-done((bf16[2,160,8192]{2,1,0:T(8,128)(2,1)S(1)}, bf16[2,160,8192]{2,1,0:T(8,128)(2,1)}, u32[]{:S(2)}) %copy-start) | copy-done | bytes 5242904
  13.3 3.9 %normed_halves.1 = (bf16[16,320,256]{2,1,0:T(8,128)(2,1)S(1)}, bf16[16,320,256]{2,1,0:T(8,128)(2,1)}) custom-call(s32[11]{0:T(128)S(1)} %stack.47.place, bf16[320,8192]{1,0:T(8,128)(2,1)S(1)} %bitcast.16), custom_call_target="tpu_custom_call" | custom-call | flops 1000 | bytes 1000 | tf_op jit(solution)/shard_map/normed_halves/pallas_call | solution.py:135
  17.3 0.9 pad_maximum_fusion.1.refs_1_
  18.1 0.0 collective-permute-done
  18.1 2.9 %collective-permute-done.1.refs_4_ = bf16[256,1024]{1,0:T(8,128)(2,1)} collective-permute-done((bf16[256,1024]{1,0:T(8,128)(2,1)S(1)}, bf16[256,1024]{1,0:T(8,128)(2,1)}, u32[]{:S(2)}, u32[]{:S(2)}) %collective-permute-start.1) | collective-permute-done | bytes 524320 | tf_op jit(solution)/shard_map/ppermute | solution.py:66
  21.0 1.5 %collective-permute-done.4.refs_2_ = bf16[256,1024]{1,0:T(8,128)(2,1)} collective-permute-done((bf16[256,1024]{1,0:T(8,128)(2,1)S(1)}, bf16[256,1024]{1,0:T(8,128)(2,1)}, u32[]{:S(2)}, u32[]{:S(2)}) %collective-permute-start.4) | collective-permute-done | bytes 524320 | tf_op jit(solution)/shard_map/ppermute | solution.py:66
  22.5 0.0 collective-permute-start.7
  22.5 1.5 %collective-permute-start.3 = (bf16[256,1024]{1,0:T(8,128)(2,1)}, bf16[256,1024]{1,0:T(8,128)(2,1)}, u32[]{:S(2)}, u32[]{:S(2)}) collective-permute-start(bf16[256,1024]{1,0:T(8,128)(2,1)} %collective-permute-done.1.refs_4_), channel_id=1, source_target_pairs={{4,8},{5,9},{6,10},{7,11},{8,4},{9,5},{10,6},{11,7},{20,24},{21,25... | collective-permute-start | bytes 1572872 | tf_op jit(solution)/shard_map/ppermute | solution.py:66
  24.0 1.3 %collective-permute-start.2 = (bf16[256,1024]{1,0:T(8,128)(2,1)}, bf16[256,1024]{1,0:T(8,128)(2,1)}, u32[]{:S(2)}, u32[]{:S(2)}) collective-permute-start(bf16[256,1024]{1,0:T(8,128)(2,1)} %collective-permute-done), channel_id=1, source_target_pairs={{4,0},{5,1},{6,2},{7,3},{8,12},{9,13},{10,14},{11,15},{20,16},{21,... | collective-permute-start | bytes 1572872 | tf_op jit(solution)/shard_map/ppermute | solution.py:66
  25.2 1.6 %collective-permute-start.6 = (bf16[256,1024]{1,0:T(8,128)(2,1)}, bf16[256,1024]{1,0:T(8,128)(2,1)}, u32[]{:S(2)}, u32[]{:S(2)}) collective-permute-start(bf16[256,1024]{1,0:T(8,128)(2,1)} %collective-permute-done.4.refs_2_), channel_id=1, source_target_pairs={{0,16},{1,17},{2,18},{3,19},{4,20},{5,21},{6,22},{7,23},{8,24},{9,... | collective-permute-start | bytes 1572872 | tf_op jit(solution)/shard_map/ppermute | solution.py:66
  26.8 1.5 %collective-permute-start.5 = (bf16[256,1024]{1,0:T(8,128)(2,1)}, bf16[256,1024]{1,0:T(8,128)(2,1)}, u32[]{:S(2)}, u32[]{:S(2)}) collective-permute-start(bf16[256,1024]{1,0:T(8,128)(2,1)} %collective-permute-done.1.refs_4_), channel_id=1, source_target_pairs={{0,2},{1,3},{2,0},{3,1},{4,6},{5,7},{6,4},{7,5},{8,10},{9,11},{10,... | collective-permute-start | bytes 1572872 | tf_op jit(solution)/shard_map/ppermute | solution.py:66
  28.3 0.0 collective-permute-done.3
  28.3 12.2 %collective-permute-done.2 = bf16[256,1024]{1,0:T(8,128)(2,1)} collective-permute-done((bf16[256,1024]{1,0:T(8,128)(2,1)}, bf16[256,1024]{1,0:T(8,128)(2,1)}, u32[]{:S(2)}, u32[]{:S(2)}) %collective-permute-start.2) | collective-permute-done | bytes 524320 | tf_op jit(solution)/shard_map/ppermute | solution.py:66
  40.5 1.3 %collective-permute-start.9 = (bf16[256,1024]{1,0:T(8,128)(2,1)}, bf16[256,1024]{1,0:T(8,128)(2,1)}, u32[]{:S(2)}, u32[]{:S(2)}) collective-permute-start(bf16[256,1024]{1,0:T(8,128)(2,1)} %collective-permute-done.3), channel_id=1, source_target_pairs={{4,0},{5,1},{6,2},{7,3},{8,12},{9,13},{10,14},{11,15},{20,16},{21,... | collective-permute-start | bytes 1572872 | tf_op jit(solution)/shard_map/ppermute | solution.py:66
  41.8 0.0 copy-start.1
  41.8 1.2 broadcast_select_fusion.1.refs_0_
  43.0 0.0 collective-permute-done.6.refs_3_
  43.0 0.0 collective-permute-done.5.refs_5_
  43.0 0.0 collective-permute-done.7.other
  43.0 1.6 %collective-permute-start.10 = (bf16[256,1024]{1,0:T(8,128)(2,1)S(1)}, bf16[256,1024]{1,0:T(8,128)(2,1)S(1)}, u32[]{:S(2)}, u32[]{:S(2)}) collective-permute-start(bf16[256,1024]{1,0:T(8,128)(2,1)S(1)} %broadcast_select_fusion.1.refs_0_), channel_id=1, source_target_pairs={{0,16},{1,17},{2,18},{3,19},{4,20},{5,21},{6,22},{7,23},{8,24},{9,... | collective-permute-start | bytes 1572872 | tf_op jit(solution)/shard_map/ppermute | solution.py:66
  44.6 1.5 %collective-permute-start.8 = (bf16[256,1024]{1,0:T(8,128)(2,1)S(1)}, bf16[256,1024]{1,0:T(8,128)(2,1)S(1)}, u32[]{:S(2)}, u32[]{:S(2)}) collective-permute-start(bf16[256,1024]{1,0:T(8,128)(2,1)S(1)} %broadcast_select_fusion.1.refs_0_), channel_id=1, source_target_pairs={{0,2},{1,3},{2,0},{3,1},{4,6},{5,7},{6,4},{7,5},{8,10},{9,11},{10,... | collective-permute-start | bytes 1572872 | tf_op jit(solution)/shard_map/ppermute | solution.py:66
  46.1 10.2 %collective-permute-done.9 = bf16[256,1024]{1,0:T(8,128)(2,1)} collective-permute-done((bf16[256,1024]{1,0:T(8,128)(2,1)}, bf16[256,1024]{1,0:T(8,128)(2,1)}, u32[]{:S(2)}, u32[]{:S(2)}) %collective-permute-start.9) | collective-permute-done | bytes 524320 | tf_op jit(solution)/shard_map/ppermute | solution.py:66
  56.2 1.1 broadcast_select_fusion.refs_3_
  57.4 0.1 collective-permute-start.15
  57.4 4.4 %add_product.4 = (f32[320,1024]{1,0:T(8,128)S(1)}, f32[320,1024]{1,0:T(8,128)S(1)}) custom-call(s32[11]{0:T(128)S(1)} %stack.47.place, bf16[16,320,256]{2,1,0:T(8,128)(2,1)S(1)} %get-tuple-element.55.mine, bf16[16,320,256]{2,1,0:T(8,128)(2,1)} %collective-permute-done.7.other, bf16[256,1024]{1,0:T(8,128)(2,1)S(1)} %pad_maximum_fusion.refs_0_, ...), custom_call_target="tpu_custom_call" | custom-call | flops 1000 | bytes 1000 | tf_op jit(solution)/shard_map/add_product/pallas_call | solution.py:202
  61.9 0.0 collective-permute-done.10.refs_1_
  61.9 0.0 collective-permute-done.8.refs_2_
  61.9 1.6 %collective-permute-start.11 = (bf16[256,1024]{1,0:T(8,128)(2,1)S(1)}, bf16[256,1024]{1,0:T(8,128)(2,1)S(1)}, u32[]{:S(2)}, u32[]{:S(2)}) collective-permute-start(bf16[256,1024]{1,0:T(8,128)(2,1)S(1)} %broadcast_select_fusion.refs_3_), channel_id=1, source_target_pairs={{0,16},{1,17},{2,18},{3,19},{4,20},{5,21},{6,22},{7,23},{8,24},{9,... | collective-permute-start | bytes 1572872 | tf_op jit(solution)/shard_map/ppermute | solution.py:66
  63.5 1.5 %collective-permute-start.12 = (bf16[256,1024]{1,0:T(8,128)(2,1)S(1)}, bf16[256,1024]{1,0:T(8,128)(2,1)S(1)}, u32[]{:S(2)}, u32[]{:S(2)}) collective-permute-start(bf16[256,1024]{1,0:T(8,128)(2,1)S(1)} %broadcast_select_fusion.refs_3_), channel_id=1, source_target_pairs={{0,2},{1,3},{2,0},{3,1},{4,6},{5,7},{6,4},{7,5},{8,10},{9,11},{10,... | collective-permute-start | bytes 1572872 | tf_op jit(solution)/shard_map/ppermute | solution.py:66
  65.0 5.1 %collective-permute-done.15.refs_0_ = bf16[256,1024]{1,0:T(8,128)(2,1)S(1)} collective-permute-done((bf16[256,1024]{1,0:T(8,128)(2,1)S(1)}, bf16[256,1024]{1,0:T(8,128)(2,1)S(1)}, u32[]{:S(2)}, u32[]{:S(2)}) %collective-permute-start.15) | collective-permute-done | bytes 524320 | tf_op jit(solution)/shard_map/ppermute | solution.py:66
  70.1 0.3 collective-permute-start.16
  70.4 3.6 %add_product.5 = (f32[320,1024]{1,0:T(8,128)S(1)}, f32[320,1024]{1,0:T(8,128)S(1)}) custom-call(s32[11]{0:T(128)S(1)} %stack.47.place, bf16[16,320,256]{2,1,0:T(8,128)(2,1)S(1)} %get-tuple-element.55.mine, bf16[16,320,256]{2,1,0:T(8,128)(2,1)} %collective-permute-done.7.other, bf16[256,1024]{1,0:T(8,128)(2,1)S(1)} %broadcast_select_fusion.1.refs_0_, ...), custom_call_target="tpu_custom_call" | custom-call | flops 1000 | bytes 1000 | tf_op jit(solution)/shard_map/add_product/pallas_call | solution.py:202
  74.0 0.6 collective-permute-done.11.refs_1_
  74.6 1.2 %collective-permute-done.12.refs_2_ = bf16[256,1024]{1,0:T(8,128)(2,1)S(1)} collective-permute-done((bf16[256,1024]{1,0:T(8,128)(2,1)S(1)}, bf16[256,1024]{1,0:T(8,128)(2,1)S(1)}, u32[]{:S(2)}, u32[]{:S(2)}) %collective-permute-start.12) | collective-permute-done | bytes 524320 | tf_op jit(solution)/shard_map/ppermute | solution.py:66
  75.8 1.5 %collective-permute-start.14 = (bf16[256,1024]{1,0:T(8,128)(2,1)S(1)}, bf16[256,1024]{1,0:T(8,128)(2,1)S(1)}, u32[]{:S(2)}, u32[]{:S(2)}) collective-permute-start(bf16[256,1024]{1,0:T(8,128)(2,1)S(1)} %collective-permute-done.11.refs_1_), channel_id=1, source_target_pairs={{0,2},{1,3},{2,0},{3,1},{4,6},{5,7},{6,4},{7,5},{8,10},{9,11},{10,... | collective-permute-start | bytes 1572872 | tf_op jit(solution)/shard_map/ppermute | solution.py:66
  77.4 0.5 collective-permute-start.13
  77.9 4.1 %collective-permute-done.16.refs_3_ = bf16[256,1024]{1,0:T(8,128)(2,1)S(1)} collective-permute-done((bf16[256,1024]{1,0:T(8,128)(2,1)}, bf16[256,1024]{1,0:T(8,128)(2,1)S(1)}, u32[]{:S(2)}, u32[]{:S(2)}) %collective-permute-start.16) | collective-permute-done | bytes 524320 | tf_op jit(solution)/shard_map/ppermute | solution.py:66
  82.0 3.6 %add_product.6 = (f32[320,1024]{1,0:T(8,128)S(1)}, f32[320,1024]{1,0:T(8,128)S(1)}) custom-call(s32[11]{0:T(128)S(1)} %stack.47.place, bf16[16,320,256]{2,1,0:T(8,128)(2,1)S(1)} %get-tuple-element.55.mine, bf16[16,320,256]{2,1,0:T(8,128)(2,1)} %collective-permute-done.7.other, bf16[256,1024]{1,0:T(8,128)(2,1)S(1)} %collective-permute-done.15.refs_0_, ...), custom_call_target="tpu_custom_call" | custom-call | flops 1000 | bytes 16777216 | tf_op jit(solution)/shard_map/add_product/pallas_call | solution.py:202
  85.7 1.6 %collective-permute-done.14.refs_1_ = bf16[256,1024]{1,0:T(8,128)(2,1)S(1)} collective-permute-done((bf16[256,1024]{1,0:T(8,128)(2,1)S(1)}, bf16[256,1024]{1,0:T(8,128)(2,1)S(1)}, u32[]{:S(2)}, u32[]{:S(2)}) %collective-permute-start.14) | collective-permute-done | bytes 524320 | tf_op jit(solution)/shard_map/ppermute | solution.py:66
  87.3 1.2 %collective-permute-done.13.refs_0_ = bf16[256,1024]{1,0:T(8,128)(2,1)S(1)} collective-permute-done((bf16[256,1024]{1,0:T(8,128)(2,1)S(1)}, bf16[256,1024]{1,0:T(8,128)(2,1)S(1)}, u32[]{:S(2)}, u32[]{:S(2)}) %collective-permute-start.13) | collective-permute-done | bytes 524320 | tf_op jit(solution)/shard_map/ppermute | solution.py:66
  88.6 0.0 copy-start.6
  88.6 0.0 copy-start.7
  88.6 0.0 copy-start.11
  88.6 0.0 copy-start.12
  88.6 2.6 %add_product.7 = (f32[320,1024]{1,0:T(8,128)S(1)}, f32[320,1024]{1,0:T(8,128)S(1)}) custom-call(s32[11]{0:T(128)S(1)} %stack.47.place, bf16[16,320,256]{2,1,0:T(8,128)(2,1)S(1)} %get-tuple-element.55.mine, bf16[16,320,256]{2,1,0:T(8,128)(2,1)} %collective-permute-done.7.other, bf16[256,1024]{1,0:T(8,128)(2,1)S(1)} %collective-permute-done.13.refs_0_, ...), custom_call_target="tpu_custom_call" | custom-call | flops 1000 | bytes 1000 | tf_op jit(solution)/shard_map/add_product/pallas_call | solution.py:202
  91.2 0.1 collective-permute-start.17
  91.3 3.0 %collective-permute-done.17.refs_1_ = f32[320,1024]{1,0:T(8,128)S(1)} collective-permute-done((f32[320,1024]{1,0:T(8,128)S(1)}, f32[320,1024]{1,0:T(8,128)S(1)}, u32[]{:S(2)}, u32[]{:S(2)}) %collective-permute-start.17) | collective-permute-done | bytes 1310752 | tf_op jit(solution)/shard_map/ppermute | solution.py:66
  94.3 0.0 copy-done.5
  94.4 1.0 cache_rows.1
  95.4 0.0 copy-start.8
  95.4 0.0 copy-start.9
  95.4 0.0 copy-start.10
  95.5 21.0 %all_to_all.12 = bf16[16,80,256]{2,1,0:T(8,128)(2,1)S(1)} all-to-all(bf16[16,80,256]{2,1,0:T(8,128)(2,1)S(1)} %cache_rows.1), channel_id=1, replica_groups=mesh['groups'=2,'seq'=16] {'seq'}, dimensions={0} | all-to-all | bytes 1310720 | tf_op jit(solution)/shard_map/all_to_all | solution.py:471
  116.5 1.1 decode.1.mine
  117.6 0.4 collective-permute-start.18
  117.9 0.9 collective-permute-done.18.theirs
  118.8 1.3 %joined.1 = bf16[4,512]{1,0:T(4,128)(2,1)} custom-call(s32[11]{0:T(128)S(1)} %stack.47.place, f32[32,256]{1,0:T(8,128)S(1)} %decode.1.mine, f32[32,256]{1,0:T(8,128)S(1)} %collective-permute-done.18.theirs), custom_call_target="tpu_custom_call" | custom-call | flops 1000 | bytes 1000 | tf_op jit(solution)/shard_map/joined/pallas_call | solution.py:361
  120.1 0.8 copy.17
  (18 shorter events, 0.0 us)
Async XLA Ops:
  2.7 15.4 %collective-permute-start = (bf16[256,1024]{1,0:T(8,128)(2,1)S(1)}, bf16[256,1024]{1,0:T(8,128)(2,1)}, u32[]{:S(2)}, u32[]{:S(2)}) collective-permute-start(bf16[256,1024]{1,0:T(8,128)(2,1)S(1)} %pad_maximum_fusion.refs_0_), channel_id=1, source_target_pairs={{4,8},{5,9},{6,10},{7,11},{8,4},{9,5},{10,6},{11,7},{20,24},{21,25... | collective-permute-start | bytes 1572872 | tf_op jit(solution)/shard_map/ppermute | solution.py:66
  4.1 16.9 %collective-permute-start.1 = (bf16[256,1024]{1,0:T(8,128)(2,1)S(1)}, bf16[256,1024]{1,0:T(8,128)(2,1)}, u32[]{:S(2)}, u32[]{:S(2)}) collective-permute-start(bf16[256,1024]{1,0:T(8,128)(2,1)S(1)} %pad_maximum_fusion.refs_0_), channel_id=1, source_target_pairs={{0,4},{1,5},{2,6},{3,7},{4,0},{5,1},{6,2},{7,3},{8,12},{9,13},{10,... | collective-permute-start | bytes 1572872 | tf_op jit(solution)/shard_map/ppermute | solution.py:66
  9.2 13.2 %collective-permute-start.4 = (bf16[256,1024]{1,0:T(8,128)(2,1)S(1)}, bf16[256,1024]{1,0:T(8,128)(2,1)}, u32[]{:S(2)}, u32[]{:S(2)}) collective-permute-start(bf16[256,1024]{1,0:T(8,128)(2,1)S(1)} %pad_maximum_fusion.refs_0_), channel_id=1, source_target_pairs={{0,2},{1,3},{2,0},{3,1},{4,6},{5,7},{6,4},{7,5},{8,10},{9,11},{10,... | collective-permute-start | bytes 1572872 | tf_op jit(solution)/shard_map/ppermute | solution.py:66
  10.9 2.5 %copy-start = (bf16[2,160,8192]{2,1,0:T(8,128)(2,1)S(1)}, bf16[2,160,8192]{2,1,0:T(8,128)(2,1)}, u32[]{:S(2)}) copy-start(bf16[2,160,8192]{2,1,0:T(8,128)(2,1)} %param.14) | copy-start | bytes 15728644
  13.3 3.9 %copy-start.13 = (bf16[256,512]{1,0:T(8,128)(2,1)S(1)}, bf16[256,512]{1,0:T(8,128)(2,1)}, u32[]{:S(2)}) copy-start(bf16[256,512]{1,0:T(8,128)(2,1)} %get-tuple-element.63) | copy-start | bytes 786436
  22.5 20.5 %collective-permute-start.7 = (bf16[16,320,256]{2,1,0:T(8,128)(2,1)}, bf16[16,320,256]{2,1,0:T(8,128)(2,1)}, u32[]{:S(2)}, u32[]{:S(2)}) collective-permute-start(bf16[16,320,256]{2,1,0:T(8,128)(2,1)} %get-tuple-element.37), channel_id=1, source_target_pairs={{0,1},{1,0},{2,3},{3,2},{4,5},{5,4},{6,7},{7,6},{8,9},{9,8},{10,11... | collective-permute-start | bytes 7864328 | tf_op jit(solution)/shard_map/ppermute | solution.py:66
  22.5 5.9 %collective-permute-start.3 = (bf16[256,1024]{1,0:T(8,128)(2,1)}, bf16[256,1024]{1,0:T(8,128)(2,1)}, u32[]{:S(2)}, u32[]{:S(2)}) collective-permute-start(bf16[256,1024]{1,0:T(8,128)(2,1)} %collective-permute-done.1.refs_4_), channel_id=1, source_target_pairs={{4,8},{5,9},{6,10},{7,11},{8,4},{9,5},{10,6},{11,7},{20,24},{21,25... | collective-permute-start | bytes 1572872 | tf_op jit(solution)/shard_map/ppermute | solution.py:66
  24.0 16.5 %collective-permute-start.2 = (bf16[256,1024]{1,0:T(8,128)(2,1)}, bf16[256,1024]{1,0:T(8,128)(2,1)}, u32[]{:S(2)}, u32[]{:S(2)}) collective-permute-start(bf16[256,1024]{1,0:T(8,128)(2,1)} %collective-permute-done), channel_id=1, source_target_pairs={{4,0},{5,1},{6,2},{7,3},{8,12},{9,13},{10,14},{11,15},{20,16},{21,... | collective-permute-start | bytes 1572872 | tf_op jit(solution)/shard_map/ppermute | solution.py:66
  25.2 17.7 %collective-permute-start.6 = (bf16[256,1024]{1,0:T(8,128)(2,1)}, bf16[256,1024]{1,0:T(8,128)(2,1)}, u32[]{:S(2)}, u32[]{:S(2)}) collective-permute-start(bf16[256,1024]{1,0:T(8,128)(2,1)} %collective-permute-done.4.refs_2_), channel_id=1, source_target_pairs={{0,16},{1,17},{2,18},{3,19},{4,20},{5,21},{6,22},{7,23},{8,24},{9,... | collective-permute-start | bytes 1572872 | tf_op jit(solution)/shard_map/ppermute | solution.py:66
  26.8 16.2 %collective-permute-start.5 = (bf16[256,1024]{1,0:T(8,128)(2,1)}, bf16[256,1024]{1,0:T(8,128)(2,1)}, u32[]{:S(2)}, u32[]{:S(2)}) collective-permute-start(bf16[256,1024]{1,0:T(8,128)(2,1)} %collective-permute-done.1.refs_4_), channel_id=1, source_target_pairs={{0,2},{1,3},{2,0},{3,1},{4,6},{5,7},{6,4},{7,5},{8,10},{9,11},{10,... | collective-permute-start | bytes 1572872 | tf_op jit(solution)/shard_map/ppermute | solution.py:66
  40.5 15.8 %collective-permute-start.9 = (bf16[256,1024]{1,0:T(8,128)(2,1)}, bf16[256,1024]{1,0:T(8,128)(2,1)}, u32[]{:S(2)}, u32[]{:S(2)}) collective-permute-start(bf16[256,1024]{1,0:T(8,128)(2,1)} %collective-permute-done.3), channel_id=1, source_target_pairs={{4,0},{5,1},{6,2},{7,3},{8,12},{9,13},{10,14},{11,15},{20,16},{21,... | collective-permute-start | bytes 1572872 | tf_op jit(solution)/shard_map/ppermute | solution.py:66
  41.8 15.6 %copy-start.1 = (bf16[256,1024]{1,0:T(8,128)(2,1)S(1)}, bf16[256,1024]{1,0:T(8,128)(2,1)}, u32[]{:S(2)}) copy-start(bf16[256,1024]{1,0:T(8,128)(2,1)} %pad_maximum_fusion.1.refs_1_) | copy-start | bytes 1572868
  43.0 18.9 %collective-permute-start.10 = (bf16[256,1024]{1,0:T(8,128)(2,1)S(1)}, bf16[256,1024]{1,0:T(8,128)(2,1)S(1)}, u32[]{:S(2)}, u32[]{:S(2)}) collective-permute-start(bf16[256,1024]{1,0:T(8,128)(2,1)S(1)} %broadcast_select_fusion.1.refs_0_), channel_id=1, source_target_pairs={{0,16},{1,17},{2,18},{3,19},{4,20},{5,21},{6,22},{7,23},{8,24},{9,... | collective-permute-start | bytes 1572872 | tf_op jit(solution)/shard_map/ppermute | solution.py:66
  44.6 17.3 %collective-permute-start.8 = (bf16[256,1024]{1,0:T(8,128)(2,1)S(1)}, bf16[256,1024]{1,0:T(8,128)(2,1)S(1)}, u32[]{:S(2)}, u32[]{:S(2)}) collective-permute-start(bf16[256,1024]{1,0:T(8,128)(2,1)S(1)} %broadcast_select_fusion.1.refs_0_), channel_id=1, source_target_pairs={{0,2},{1,3},{2,0},{3,1},{4,6},{5,7},{6,4},{7,5},{8,10},{9,11},{10,... | collective-permute-start | bytes 1572872 | tf_op jit(solution)/shard_map/ppermute | solution.py:66
  57.4 12.7 %collective-permute-start.15 = (bf16[256,1024]{1,0:T(8,128)(2,1)S(1)}, bf16[256,1024]{1,0:T(8,128)(2,1)S(1)}, u32[]{:S(2)}, u32[]{:S(2)}) collective-permute-start(bf16[256,1024]{1,0:T(8,128)(2,1)S(1)} %copy-done.1), channel_id=1, source_target_pairs={{0,4},{1,5},{2,6},{3,7},{4,0},{5,1},{6,2},{7,3},{8,12},{9,13},{10,... | collective-permute-start | bytes 1572872 | tf_op jit(solution)/shard_map/ppermute | solution.py:66
  61.9 12.7 %collective-permute-start.11 = (bf16[256,1024]{1,0:T(8,128)(2,1)S(1)}, bf16[256,1024]{1,0:T(8,128)(2,1)S(1)}, u32[]{:S(2)}, u32[]{:S(2)}) collective-permute-start(bf16[256,1024]{1,0:T(8,128)(2,1)S(1)} %broadcast_select_fusion.refs_3_), channel_id=1, source_target_pairs={{0,16},{1,17},{2,18},{3,19},{4,20},{5,21},{6,22},{7,23},{8,24},{9,... | collective-permute-start | bytes 1572872 | tf_op jit(solution)/shard_map/ppermute | solution.py:66
  63.5 12.4 %collective-permute-start.12 = (bf16[256,1024]{1,0:T(8,128)(2,1)S(1)}, bf16[256,1024]{1,0:T(8,128)(2,1)S(1)}, u32[]{:S(2)}, u32[]{:S(2)}) collective-permute-start(bf16[256,1024]{1,0:T(8,128)(2,1)S(1)} %broadcast_select_fusion.refs_3_), channel_id=1, source_target_pairs={{0,2},{1,3},{2,0},{3,1},{4,6},{5,7},{6,4},{7,5},{8,10},{9,11},{10,... | collective-permute-start | bytes 1572872 | tf_op jit(solution)/shard_map/ppermute | solution.py:66
  70.1 12.0 %collective-permute-start.16 = (bf16[256,1024]{1,0:T(8,128)(2,1)}, bf16[256,1024]{1,0:T(8,128)(2,1)S(1)}, u32[]{:S(2)}, u32[]{:S(2)}) collective-permute-start(bf16[256,1024]{1,0:T(8,128)(2,1)} %collective-permute-done.6.refs_3_), channel_id=1, source_target_pairs={{0,4},{1,5},{2,6},{3,7},{4,0},{5,1},{6,2},{7,3},{8,12},{9,13},{10,... | collective-permute-start | bytes 1572872 | tf_op jit(solution)/shard_map/ppermute | solution.py:66
  75.8 11.5 %collective-permute-start.14 = (bf16[256,1024]{1,0:T(8,128)(2,1)S(1)}, bf16[256,1024]{1,0:T(8,128)(2,1)S(1)}, u32[]{:S(2)}, u32[]{:S(2)}) collective-permute-start(bf16[256,1024]{1,0:T(8,128)(2,1)S(1)} %collective-permute-done.11.refs_1_), channel_id=1, source_target_pairs={{0,2},{1,3},{2,0},{3,1},{4,6},{5,7},{6,4},{7,5},{8,10},{9,11},{10,... | collective-permute-start | bytes 1572872 | tf_op jit(solution)/shard_map/ppermute | solution.py:66
  77.4 11.2 %collective-permute-start.13 = (bf16[256,1024]{1,0:T(8,128)(2,1)S(1)}, bf16[256,1024]{1,0:T(8,128)(2,1)S(1)}, u32[]{:S(2)}, u32[]{:S(2)}) collective-permute-start(bf16[256,1024]{1,0:T(8,128)(2,1)S(1)} %collective-permute-done.8.refs_2_), channel_id=1, source_target_pairs={{0,16},{1,17},{2,18},{3,19},{4,20},{5,21},{6,22},{7,23},{8,24},{9,... | collective-permute-start | bytes 1572872 | tf_op jit(solution)/shard_map/ppermute | solution.py:66
  88.5 5.8 %copy-start.2 = (f32[64,128]{1,0:T(8,128)S(1)}, f32[64,128]{1,0:T(8,128)}, u32[]{:S(2)}) copy-start(f32[64,128]{1,0:T(8,128)} %constant.70.clone.refs_4_.refs_2_) | copy-start | bytes 98308
  88.5 5.8 %copy-start.3 = (f32[64,128]{1,0:T(8,128)S(1)}, f32[64,128]{1,0:T(8,128)}, u32[]{:S(2)}) copy-start(f32[64,128]{1,0:T(8,128)} %constant.71.clone.refs_5_.refs_3_) | copy-start | bytes 98308
  88.5 5.8 %copy-start.4 = (f32[41,128]{1,0:T(8,128)S(1)}, f32[41,128]{1,0:T(8,128)}, u32[]{:S(2)}) copy-start(f32[41,128]{1,0:T(8,128)} %constant.68.clone.refs_2_.refs_0_) | copy-start | bytes 62980
  88.6 5.8 %copy-start.5 = (f32[41,128]{1,0:T(8,128)S(1)}, f32[41,128]{1,0:T(8,128)}, u32[]{:S(2)}) copy-start(f32[41,128]{1,0:T(8,128)} %constant.69.clone.refs_3_.refs_1_) | copy-start | bytes 62980
  88.6 5.8 %copy-start.6 = (f32[160,128]{1,0:T(8,128)S(1)}, f32[160,128]{1,0:T(8,128)}, u32[]{:S(2)}) copy-start(f32[160,128]{1,0:T(8,128)} %constant.72.clone.refs_6_) | copy-start | bytes 245764
  88.6 5.8 %copy-start.7 = (f32[160,128]{1,0:T(8,128)S(1)}, f32[160,128]{1,0:T(8,128)}, u32[]{:S(2)}) copy-start(f32[160,128]{1,0:T(8,128)} %constant.73.clone.refs_7_) | copy-start | bytes 245764
  88.6 5.8 %copy-start.11 = (s32[2]{0:T(128)S(1)}, s32[2]{0:T(128)}, u32[]{:S(2)}) copy-start(s32[2]{0:T(128)} %lengths.3) | copy-start | bytes 28
  88.6 5.8 %copy-start.12 = (s32[8]{0:T(128)S(1)}, s32[8]{0:T(128)}, u32[]{:S(2)}) copy-start(s32[8]{0:T(128)} %owner.3) | copy-start | bytes 100
  91.2 3.1 %collective-permute-start.17 = (f32[320,1024]{1,0:T(8,128)S(1)}, f32[320,1024]{1,0:T(8,128)S(1)}, u32[]{:S(2)}, u32[]{:S(2)}) collective-permute-start(f32[320,1024]{1,0:T(8,128)S(1)} %get-tuple-element.57), channel_id=1, source_target_pairs={{0,1},{1,0},{2,3},{3,2},{4,5},{5,4},{6,7},{7,6},{8,9},{9,8},{10,11... | collective-permute-start | bytes 3932168 | tf_op jit(solution)/shard_map/ppermute | solution.py:66
  95.4 21.0 %copy-start.8 = (bf16[8,4,1024]{2,1,0:T(4,128)(2,1)S(1)}, bf16[8,4,1024]{2,1,0:T(4,128)(2,1)}, u32[]{:S(2)}) copy-start(bf16[8,4,1024]{2,1,0:T(4,128)(2,1)} %dec_query.1) | copy-start | bytes 196612
  95.4 21.0 %copy-start.9 = (bf16[8,4,128]{2,1,0:T(4,128)(2,1)S(1)}, bf16[8,4,128]{2,1,0:T(4,128)(2,1)}, u32[]{:S(2)}) copy-start(bf16[8,4,128]{2,1,0:T(4,128)(2,1)} %dec_key.1) | copy-start | bytes 24580
  95.4 21.0 %copy-start.10 = (bf16[8,4,128]{2,1,0:T(4,128)(2,1)S(1)}, bf16[8,4,128]{2,1,0:T(4,128)(2,1)}, u32[]{:S(2)}) copy-start(bf16[8,4,128]{2,1,0:T(4,128)(2,1)} %dec_value.1) | copy-start | bytes 24580
  117.6 1.3 %collective-permute-start.18 = (f32[32,256]{1,0:T(8,128)S(1)}, f32[32,256]{1,0:T(8,128)S(1)}, u32[]{:S(2)}, u32[]{:S(2)}) collective-permute-start(f32[32,256]{1,0:T(8,128)S(1)} %decode.1.mine), channel_id=1, source_target_pairs={{0,1},{1,0},{2,3},{3,2},{4,5},{5,4},{6,7},{7,6},{8,9},{9,8},{10,11... | collective-permute-start | bytes 98312 | tf_op jit(solution)/shard_map/ppermute | solution.py:66

commit v15 on v14

--- a/solution.py
+++ b/solution.py
@@ -59,10 +59,8 @@
     route = []
     for g in range(groups):
         for s in range(seq):
-            place = rule(g, s // 2 // low, s // 2 % low, s % 2)
-            if place is not None:
-                tg, tz, ty, tc = place
-                route.append((g * seq + s, tg * seq + (tz * low + ty) * 2 + tc))
+            tg, tz, ty, tc = rule(g, s // 2 // low, s // 2 % low, s % 2)
+            route.append((g * seq + s, tg * seq + (tz * low + ty) * 2 + tc))
     return lax.ppermute(block, ("groups", "seq"), route)
 
 
@@ -78,16 +76,8 @@
     return (1 - g, z, y, c)
 
 
-def to_pair(g, z, y, c):
-    return (g, z ^ 1, y, c)
-
-
-def to_middle(g, z, y, c):
-    return (g, 3 - z, y, c) if z in (1, 2) else None
-
-
-def to_end(g, z, y, c):
-    return (g, 0 if z == 1 else 3, y, c) if z in (1, 2) else None
+def along(bits):
+    return lambda g, z, y, c: (g, z ^ bits, y, c)
 
 
 VMEM_REF = pl.BlockSpec(memory_space=pltpu.VMEM)
@@ -388,11 +378,9 @@
     if planned:
         core = device_id % 2
         z, y = device_id // 4, device_id // 2 % 2
-        layers = [z, z ^ 1, jnp.where(z < 2, 2, 1), jnp.where(z < 2, 3, 0)]
-        is_end = (z == 0) | (z == 3)
         place = [group_id, core, device_id]
-        place += [layer * 2 + y for layer in layers]
-        place += [layer * 2 + 1 - y for layer in layers]
+        place += [(z ^ bits) * 2 + y for bits in range(4)]
+        place += [(z ^ bits) * 2 + 1 - y for bits in range(4)]
         place = jnp.stack([jnp.asarray(entry, jnp.int32) for entry in place])
     else:
         widened = flat.astype(jnp.float32)
@@ -432,41 +420,37 @@
 
         sent = half_block(group_id * depth)
         tables = turn_tables(count_rows * seq + STEPS, count_rows)
-        near = moved(sent, to_pair)
-        middle = moved(sent, to_middle)
-        across = moved(sent, to_row)
+        layer_1 = moved(sent, along(1))
+        layer_2 = moved(sent, along(2))
+        row_0 = moved(sent, to_row)
+        mine, kept = prepared(place, flat, seq // 2)
         rest = half_block(depth - group_id * depth)
-        mine, kept = prepared(place, flat, seq // 2)
-        layers, rows = (near, middle), (across, mine, rest)
-        end_b = moved(after(middle, *layers), to_end)
-        middle_c = moved(after(near, *layers), to_middle)
-        near_y = moved(after(near, *layers, *rows), to_row)
-        across_x = moved(after(across, *layers, *rows), to_group)
-        other = moved(after(kept, *layers, *rows), to_core)
-        layers, rows, before = (end_b, middle_c), (near_y, across_x, other), rows
-        end_c = moved(after(middle_c, *layers, *before), to_end)
-        block_b = jnp.where(is_end, after(end_b, *layers), middle)
-        block_yb = moved(after(block_b, *rows), to_row)
-        block_xb = moved(after(block_b, *rows), to_group)
-        pieces = [(HERE, 0, sent), (HERE, 1, rest), (THERE, 0, across)]
-        pieces += [(THERE, 1, across_x), (HERE + 1, 0, near), (THERE + 1, 0, near_y)]
-        totals = product(place, after(mine, *rows, block_b), other, pieces, (), 3)
-        layers, rows, before = (end_c,), (block_yb, block_xb, totals[0]), rows
-        near_rest = moved(after(rest, *layers, *before), to_pair)
-        block_c = jnp.where(is_end, after(end_c, *layers), middle_c)
-        block_xc = moved(after(block_c, *rows), to_group)
-        block_yc = moved(after(block_c, *rows), to_row)
-        pieces = [(HERE + 2, 0, block_b), (HERE + 2, 1, block_xb)]
-        pieces += [(THERE + 2, 0, block_yb), (HERE + 3, 0, block_c)]
-        totals = product(place, after(mine, *rows, block_c), other, pieces, totals, 4)
-        layers, rows, before = (near_rest,), (block_xc, block_yc, totals[0]), rows
-        end_a = moved(after(across_x, *layers, *before), to_pair)
-        ends = [moved(after(block_yb, *rows), to_group), moved(after(block_xc, *rows), to_row)]
-        pieces = [(HERE + 1, 1, near_rest), (HERE + 3, 1, block_xc)]
-        pieces += [(THERE + 3, 0, block_yc), (THERE + 1, 1, end_a)]
-        totals = product(place, after(mine, *rows, end_a), other, pieces, totals, 4, 1 << 24)
-        pieces = [(THERE + 2, 1, ends[0]), (THERE + 3, 1, ends[1])]
-        total, given = product(place, after(mine, *ends, *totals), other, pieces, totals, 2)
+        came = (layer_1, layer_2, row_0, mine, rest)
+        other = moved(after(kept, *came), to_core)
+        layer_3 = moved(after(sent, *came), along(3))
+        rest_1 = moved(after(rest, *came), along(1))
+        row_1 = moved(after(layer_1, *came), to_row)
+        group_0 = moved(after(row_0, *came), to_group)
+        row_2 = moved(after(layer_2, *came), to_row)
+        group_2 = moved(after(layer_2, *came), to_group)
+        pieces = [(HERE, 0, sent), (HERE, 1, rest), (THERE, 0, row_0)]
+        pieces += [(HERE + 1, 0, layer_1), (HERE + 2, 0, layer_2)]
+        totals = product(place, after(mine, *came), other, pieces, (), 5)
+        came = (layer_3, rest_1, row_1, group_0, row_2, group_2, totals[0])
+        row_3 = moved(after(layer_3, *came), to_row)
+        group_3 = moved(after(layer_3, *came), to_group)
+        pair_1 = moved(after(group_0, *came), along(1))
+        pieces = [(THERE, 1, group_0), (THERE + 1, 0, row_1), (HERE + 1, 1, rest_1)]
+        pieces += [(THERE + 2, 0, row_2), (HERE + 2, 1, group_2), (HERE + 3, 0, layer_3)]
+        totals = product(place, after(mine, *came), other, pieces, totals, 3)
+        came = (row_3, group_3, pair_1, totals[0])
+        end_2 = moved(after(row_2, *came), to_group)
+        end_3 = moved(after(group_3, *came), to_row)
+        pieces = [(THERE + 1, 1, pair_1), (THERE + 3, 0, row_3), (HERE + 3, 1, group_3)]
+        totals = product(place, after(mine, *came), other, pieces, totals, 3)
+        came = (end_2, end_3, *totals)
+        pieces = [(THERE + 2, 1, end_2), (THERE + 3, 1, end_3)]
+        total, given = product(place, after(mine, *came), other, pieces, totals, 2)
         outgoing = outgoing_rows(place, lengths, owner, total, moved(given, to_core), tables)
         incoming = lax.all_to_all(outgoing, "seq", split_axis=0, concat_axis=1, tiled=True)
         attended = decoded(

time: 121 us -> 118 us (0.975)
  waiting for transfers between devices: 44.6 us -> 49.6 us
  Pallas kernels: 21.6 us -> 17.3 us
  other arithmetic: 3.17 us -> 0.12 us
  starting transfers between devices: 24.2 us -> 22.9 us
    ppermute x19 -> x17, waiting for transfers between devices: 44.6 us -> 49.6 us  [moved(): return lax.ppermute(block, ('groups', 'seq'), route)]
    pallas_call x4, Pallas kernels: 14.3 us -> 11 us  [product(): pl.pallas_call(functools.partial(product_kernel, plan, group, bool(totals...]
    select_n x2 -> x0, other arithmetic: 2.27 us -> none  [the longest x1 1.16 us: body(): block_b = jnp.where(is_end, after(end_b, *layers), middle)]
    ppermute x19 -> x17, starting transfers between devices: 24.2 us -> 22.9 us  [moved(): return lax.ppermute(block, ('groups', 'seq'), route)]
    unnamed x29 -> x25, local copies, waits for them, and re-layouts: 3.39 us -> 3.38 us
  transfers between devices with their start and end apart: 19 -> 17, of which waited for: 12 -> 11; matrix products, arithmetic and copies ran while one was open for 3% -> 0% of each run, Pallas kernels for 13% -> 10%
where the time goes in v15:
time: 118 us; the launch traced here: 117 us
  waiting for transfers between devices  49.6 us (42%)
  starting transfers between devices  22.9 us (19%)
  blocking collectives  21.9 us (19%)
  Pallas kernels  17.3 us (15%)
  local copies, waits for them, and re-layouts  4.73 us (4%)
    ppermute x17, waiting for transfers between devices, moved(): return lax.ppermute(block, ('groups', 'seq'), route)  49.6 us
    ppermute x17, starting transfers between devices, moved(): return lax.ppermute(block, ('groups', 'seq'), route)  22.9 us
    all_to_all x1, blocking collectives, body(): lax.all_to_all(outgoing, 'seq', split_axis=0, concat_axis=1, tiled=True)  21.9 us
    pallas_call x4, Pallas kernels, product(): pl.pallas_call(functools.partial(product_kernel, plan, group, bool(totals...  11 us
    unnamed x25, local copies, waits for them, and re-layouts  3.38 us
    pallas_call x1, Pallas kernels, prepared(): pl.pallas_call(prepare_kernel, grid_spec=pltpu.PrefetchScalarGridSpec(num...  2.87 us
  transfers between devices with their start and end apart: 17, of which 11 were waited for; matrix products, arithmetic and copies ran while one was open for 0% of the time, Pallas kernels for 10%

profile of v15, /device:TPU:0, one launch (start us, length us, event | category | flops | bytes accessed | tf_op | source)
XLA Modules:
  0.0 117.4 jit_solution(4211405546302459199)
XLA Ops:
  0.6 1.3 %constant_dynamic-slice_fusion = (bf16[256,512]{1,0:T(8,128)(2,1)S(1)}, bf16[256,512]{1,0:T(8,128)(2,1)S(1)}, bf16[256,512]{1,0:T(8,128)(2,1)S(1)}, bf16[256,512]{1,0:T(8,128)(2,1)S(1)}) fusion(bf16[512,512]{1,0:T(8,128)(2,1)} %param.16, s32[]{:T(128)S(6)} %select_n.31, s32[]{:T(128)S(6)} %select_n.30, bf16[512,512]{1,0:T(8,128)(2,1)} %param.15), kind=kLoop, calls=%fused_computation.2 | loop fusion | bytes 2097160 | tf_op jit(solution)/shard_map/dynamic_slice | solution.py:416
  1.9 0.1 pad_maximum_fusion.refs_0_
  2.0 4.1 %collective-permute-start = (bf16[256,1024]{1,0:T(8,128)(2,1)S(1)}, bf16[256,1024]{1,0:T(8,128)(2,1)S(1)}, u32[]{:S(2)}, u32[]{:S(2)}) collective-permute-start(bf16[256,1024]{1,0:T(8,128)(2,1)S(1)} %pad_maximum_fusion.refs_0_), channel_id=1, source_target_pairs={{0,8},{1,9},{2,10},{3,11},{4,12},{5,13},{6,14},{7,15},{8,0},{9,1},... | collective-permute-start | bytes 1572872 | tf_op jit(solution)/shard_map/ppermute | solution.py:64
  6.1 1.6 %collective-permute-start.1 = (bf16[256,1024]{1,0:T(8,128)(2,1)S(1)}, bf16[256,1024]{1,0:T(8,128)(2,1)S(1)}, u32[]{:S(2)}, u32[]{:S(2)}) collective-permute-start(bf16[256,1024]{1,0:T(8,128)(2,1)S(1)} %pad_maximum_fusion.refs_0_), channel_id=1, source_target_pairs={{0,4},{1,5},{2,6},{3,7},{4,0},{5,1},{6,2},{7,3},{8,12},{9,13},{10,... | collective-permute-start | bytes 1572872 | tf_op jit(solution)/shard_map/ppermute | solution.py:64
  7.6 1.5 %collective-permute-start.2 = (bf16[256,1024]{1,0:T(8,128)(2,1)S(1)}, bf16[256,1024]{1,0:T(8,128)(2,1)S(1)}, u32[]{:S(2)}, u32[]{:S(2)}) collective-permute-start(bf16[256,1024]{1,0:T(8,128)(2,1)S(1)} %pad_maximum_fusion.refs_0_), channel_id=1, source_target_pairs={{0,2},{1,3},{2,0},{3,1},{4,6},{5,7},{6,4},{7,5},{8,10},{9,11},{10,... | collective-permute-start | bytes 1572872 | tf_op jit(solution)/shard_map/ppermute | solution.py:64
  9.2 0.1 stack.47.place
  9.3 2.5 %copy-done = bf16[2,160,8192]{2,1,0:T(8,128)(2,1)S(1)} copy-done((bf16[2,160,8192]{2,1,0:T(8,128)(2,1)S(1)}, bf16[2,160,8192]{2,1,0:T(8,128)(2,1)}, u32[]{:S(2)}) %copy-start) | copy-done | bytes 5242904
  11.7 2.9 %normed_halves.1 = (bf16[16,320,256]{2,1,0:T(8,128)(2,1)S(1)}, bf16[16,320,256]{2,1,0:T(8,128)(2,1)S(1)}) custom-call(s32[11]{0:T(128)S(1)} %stack.47.place, bf16[320,8192]{1,0:T(8,128)(2,1)S(1)} %bitcast.16), custom_call_target="tpu_custom_call" | custom-call | flops 1000 | bytes 1000 | tf_op jit(solution)/shard_map/normed_halves/pallas_call | solution.py:125
  14.6 0.1 pad_maximum_fusion.1.refs_1_
  14.7 14.6 %collective-permute-done.refs_4_ = bf16[256,1024]{1,0:T(8,128)(2,1)S(1)} collective-permute-done((bf16[256,1024]{1,0:T(8,128)(2,1)S(1)}, bf16[256,1024]{1,0:T(8,128)(2,1)S(1)}, u32[]{:S(2)}, u32[]{:S(2)}) %collective-permute-start) | collective-permute-done | bytes 524320 | tf_op jit(solution)/shard_map/ppermute | solution.py:64
  29.3 0.2 collective-permute-done.1.refs_3_
  29.5 0.0 collective-permute-done.2.refs_2_
  29.5 0.0 collective-permute-start.9
  29.5 1.5 %collective-permute-start.7 = (bf16[256,1024]{1,0:T(8,128)(2,1)S(1)}, bf16[256,1024]{1,0:T(8,128)(2,1)S(1)}, u32[]{:S(2)}, u32[]{:S(2)}) collective-permute-start(bf16[256,1024]{1,0:T(8,128)(2,1)S(1)} %collective-permute-done.2.refs_2_), channel_id=1, source_target_pairs={{0,16},{1,17},{2,18},{3,19},{4,20},{5,21},{6,22},{7,23},{8,24},{9,... | collective-permute-start | bytes 1572872 | tf_op jit(solution)/shard_map/ppermute | solution.py:64
  31.1 1.5 %collective-permute-start.6 = (bf16[256,1024]{1,0:T(8,128)(2,1)S(1)}, bf16[256,1024]{1,0:T(8,128)(2,1)S(1)}, u32[]{:S(2)}, u32[]{:S(2)}) collective-permute-start(bf16[256,1024]{1,0:T(8,128)(2,1)S(1)} %collective-permute-done.1.refs_3_), channel_id=1, source_target_pairs={{0,2},{1,3},{2,0},{3,1},{4,6},{5,7},{6,4},{7,5},{8,10},{9,11},{10,... | collective-permute-start | bytes 1572872 | tf_op jit(solution)/shard_map/ppermute | solution.py:64
  32.6 1.4 %collective-permute-start.5 = (bf16[256,1024]{1,0:T(8,128)(2,1)S(1)}, bf16[256,1024]{1,0:T(8,128)(2,1)S(1)}, u32[]{:S(2)}, u32[]{:S(2)}) collective-permute-start(bf16[256,1024]{1,0:T(8,128)(2,1)S(1)} %pad_maximum_fusion.1.refs_1_), channel_id=1, source_target_pairs={{0,4},{1,5},{2,6},{3,7},{4,0},{5,1},{6,2},{7,3},{8,12},{9,13},{10,... | collective-permute-start | bytes 1572872 | tf_op jit(solution)/shard_map/ppermute | solution.py:64
  34.0 1.8 %collective-permute-start.4 = (bf16[256,1024]{1,0:T(8,128)(2,1)S(1)}, bf16[256,1024]{1,0:T(8,128)(2,1)S(1)}, u32[]{:S(2)}, u32[]{:S(2)}) collective-permute-start(bf16[256,1024]{1,0:T(8,128)(2,1)S(1)} %pad_maximum_fusion.refs_0_), channel_id=1, source_target_pairs={{0,12},{1,13},{2,14},{3,15},{4,8},{5,9},{6,10},{7,11},{8,4},{9,5},... | collective-permute-start | bytes 1572872 | tf_op jit(solution)/shard_map/ppermute | solution.py:64
  35.9 8.0 %collective-permute-done.7.refs_0_ = bf16[256,1024]{1,0:T(8,128)(2,1)S(1)} collective-permute-done((bf16[256,1024]{1,0:T(8,128)(2,1)S(1)}, bf16[256,1024]{1,0:T(8,128)(2,1)S(1)}, u32[]{:S(2)}, u32[]{:S(2)}) %collective-permute-start.7) | collective-permute-done | bytes 524320 | tf_op jit(solution)/shard_map/ppermute | solution.py:64
  43.9 1.6 %collective-permute-start.3 = (bf16[256,1024]{1,0:T(8,128)(2,1)S(1)}, bf16[256,1024]{1,0:T(8,128)(2,1)S(1)}, u32[]{:S(2)}, u32[]{:S(2)}) collective-permute-start(bf16[256,1024]{1,0:T(8,128)(2,1)S(1)} %collective-permute-done.refs_4_), channel_id=1, source_target_pairs={{0,2},{1,3},{2,0},{3,1},{4,6},{5,7},{6,4},{7,5},{8,10},{9,11},{10,... | collective-permute-start | bytes 1572872 | tf_op jit(solution)/shard_map/ppermute | solution.py:64
  45.4 0.0 collective-permute-done.9.other
  45.4 1.5 %collective-permute-start.8 = (bf16[256,1024]{1,0:T(8,128)(2,1)S(1)}, bf16[256,1024]{1,0:T(8,128)(2,1)S(1)}, u32[]{:S(2)}, u32[]{:S(2)}) collective-permute-start(bf16[256,1024]{1,0:T(8,128)(2,1)S(1)} %collective-permute-done.refs_4_), channel_id=1, source_target_pairs={{0,16},{1,17},{2,18},{3,19},{4,20},{5,21},{6,22},{7,23},{8,24},{9,... | collective-permute-start | bytes 1572872 | tf_op jit(solution)/shard_map/ppermute | solution.py:64
  46.9 2.9 %add_product.4 = (f32[320,1024]{1,0:T(8,128)S(1)}, f32[320,1024]{1,0:T(8,128)S(1)}) custom-call(s32[11]{0:T(128)S(1)} %stack.47.place, bf16[16,320,256]{2,1,0:T(8,128)(2,1)S(1)} %get-tuple-element.47.mine, bf16[16,320,256]{2,1,0:T(8,128)(2,1)S(1)} %collective-permute-done.9.other, bf16[256,1024]{1,0:T(8,128)(2,1)S(1)} %pad_maximum_fusion.refs_0_, ...), custom_call_target="tpu_custom_call" | custom-call | flops 1000 | bytes 1000 | tf_op jit(solution)/shard_map/add_product/pallas_call | solution.py:192
  49.8 0.0 collective-permute-done.6.refs_1_
  49.9 0.0 collective-permute-done.5.refs_2_
  49.9 9.3 %collective-permute-done.4.refs_5_ = bf16[256,1024]{1,0:T(8,128)(2,1)S(1)} collective-permute-done((bf16[256,1024]{1,0:T(8,128)(2,1)S(1)}, bf16[256,1024]{1,0:T(8,128)(2,1)S(1)}, u32[]{:S(2)}, u32[]{:S(2)}) %collective-permute-start.4) | collective-permute-done | bytes 524320 | tf_op jit(solution)/shard_map/ppermute | solution.py:64
  59.2 0.0 collective-permute-done.3.refs_3_
  59.2 0.0 collective-permute-done.8.refs_4_
  59.2 1.0 collective-permute-start.12
  60.2 0.5 collective-permute-start.10
  60.7 1.5 %collective-permute-start.11 = (bf16[256,1024]{1,0:T(8,128)(2,1)S(1)}, bf16[256,1024]{1,0:T(8,128)(2,1)S(1)}, u32[]{:S(2)}, u32[]{:S(2)}) collective-permute-start(bf16[256,1024]{1,0:T(8,128)(2,1)S(1)} %collective-permute-done.4.refs_5_), channel_id=1, source_target_pairs={{0,16},{1,17},{2,18},{3,19},{4,20},{5,21},{6,22},{7,23},{8,24},{9,... | collective-permute-start | bytes 1572872 | tf_op jit(solution)/shard_map/ppermute | solution.py:64
  62.2 3.8 %add_product.5 = (f32[320,1024]{1,0:T(8,128)S(1)}, f32[320,1024]{1,0:T(8,128)S(1)}) custom-call(s32[11]{0:T(128)S(1)} %stack.47.place, bf16[16,320,256]{2,1,0:T(8,128)(2,1)S(1)} %get-tuple-element.47.mine, bf16[16,320,256]{2,1,0:T(8,128)(2,1)S(1)} %collective-permute-done.9.other, bf16[256,1024]{1,0:T(8,128)(2,1)S(1)} %collective-permute-done.7.refs_0_, ...), custom_call_target="tpu_custom_call" | custom-call | flops 1000 | bytes 1000 | tf_op jit(solution)/shard_map/add_product/pallas_call | solution.py:192
  66.0 6.3 %collective-permute-done.12.refs_0_ = bf16[256,1024]{1,0:T(8,128)(2,1)S(1)} collective-permute-done((bf16[256,1024]{1,0:T(8,128)(2,1)S(1)}, bf16[256,1024]{1,0:T(8,128)(2,1)S(1)}, u32[]{:S(2)}, u32[]{:S(2)}) %collective-permute-start.12) | collective-permute-done | bytes 524320 | tf_op jit(solution)/shard_map/ppermute | solution.py:64
  72.3 0.1 collective-permute-done.10.refs_1_
  72.3 0.2 collective-permute-done.11.refs_2_
  72.6 1.5 %collective-permute-start.14 = (bf16[256,1024]{1,0:T(8,128)(2,1)S(1)}, bf16[256,1024]{1,0:T(8,128)(2,1)S(1)}, u32[]{:S(2)}, u32[]{:S(2)}) collective-permute-start(bf16[256,1024]{1,0:T(8,128)(2,1)S(1)} %collective-permute-done.11.refs_2_), channel_id=1, source_target_pairs={{0,2},{1,3},{2,0},{3,1},{4,6},{5,7},{6,4},{7,5},{8,10},{9,11},{10,... | collective-permute-start | bytes 1572872 | tf_op jit(solution)/shard_map/ppermute | solution.py:64
  74.1 1.4 %collective-permute-start.13 = (bf16[256,1024]{1,0:T(8,128)(2,1)S(1)}, bf16[256,1024]{1,0:T(8,128)(2,1)S(1)}, u32[]{:S(2)}, u32[]{:S(2)}) collective-permute-start(bf16[256,1024]{1,0:T(8,128)(2,1)S(1)} %collective-permute-done.3.refs_3_), channel_id=1, source_target_pairs={{0,16},{1,17},{2,18},{3,19},{4,20},{5,21},{6,22},{7,23},{8,24},{9,... | collective-permute-start | bytes 1572872 | tf_op jit(solution)/shard_map/ppermute | solution.py:64
  75.5 2.4 %add_product.6 = (f32[320,1024]{1,0:T(8,128)S(1)}, f32[320,1024]{1,0:T(8,128)S(1)}) custom-call(s32[11]{0:T(128)S(1)} %stack.47.place, bf16[16,320,256]{2,1,0:T(8,128)(2,1)S(1)} %get-tuple-element.47.mine, bf16[16,320,256]{2,1,0:T(8,128)(2,1)S(1)} %collective-permute-done.9.other, bf16[256,1024]{1,0:T(8,128)(2,1)S(1)} %collective-permute-done.12.refs_0_, ...), custom_call_target="tpu_custom_call" | custom-call | flops 1000 | bytes 1000 | tf_op jit(solution)/shard_map/add_product/pallas_call | solution.py:192
  77.8 6.6 %collective-permute-done.14.refs_1_ = bf16[256,1024]{1,0:T(8,128)(2,1)S(1)} collective-permute-done((bf16[256,1024]{1,0:T(8,128)(2,1)S(1)}, bf16[256,1024]{1,0:T(8,128)(2,1)S(1)}, u32[]{:S(2)}, u32[]{:S(2)}) %collective-permute-start.14) | collective-permute-done | bytes 524320 | tf_op jit(solution)/shard_map/ppermute | solution.py:64
  84.5 0.3 collective-permute-done.13.refs_0_
  84.8 0.0 copy-start.5
  84.8 0.0 copy-start.6
  84.8 0.0 copy-start.10
  84.8 0.0 copy-start.11
  84.9 1.9 %add_product.7 = (f32[320,1024]{1,0:T(8,128)S(1)}, f32[320,1024]{1,0:T(8,128)S(1)}) custom-call(s32[11]{0:T(128)S(1)} %stack.47.place, bf16[16,320,256]{2,1,0:T(8,128)(2,1)S(1)} %get-tuple-element.47.mine, bf16[16,320,256]{2,1,0:T(8,128)(2,1)S(1)} %collective-permute-done.9.other, bf16[256,1024]{1,0:T(8,128)(2,1)S(1)} %collective-permute-done.13.refs_0_, ...), custom_call_target="tpu_custom_call" | custom-call | flops 1000 | bytes 1000 | tf_op jit(solution)/shard_map/add_product/pallas_call | solution.py:192
  86.7 0.1 collective-permute-start.15
  86.8 3.0 %collective-permute-done.15.refs_1_ = f32[320,1024]{1,0:T(8,128)S(1)} collective-permute-done((f32[320,1024]{1,0:T(8,128)S(1)}, f32[320,1024]{1,0:T(8,128)S(1)}, u32[]{:S(2)}, u32[]{:S(2)}) %collective-permute-start.15) | collective-permute-done | bytes 1310752 | tf_op jit(solution)/shard_map/ppermute | solution.py:64
  89.8 0.0 copy-done.1
  89.8 0.0 copy-done.2
  89.8 0.0 copy-done.3
  89.9 0.0 copy-done.4
  89.9 0.0 copy-done.5
  89.9 0.0 copy-done.6
  89.9 0.0 copy-done.10
  89.9 0.0 copy-done.11
  89.9 1.0 cache_rows.1
  91.0 0.0 copy-start.7
  91.0 0.0 copy-start.8
  91.0 0.0 copy-start.9
  91.0 21.9 %all_to_all.12 = bf16[16,80,256]{2,1,0:T(8,128)(2,1)S(1)} all-to-all(bf16[16,80,256]{2,1,0:T(8,128)(2,1)S(1)} %cache_rows.1), channel_id=1, replica_groups=mesh['groups'=2,'seq'=16] {'seq'}, dimensions={0} | all-to-all | bytes 1310720 | tf_op jit(solution)/shard_map/all_to_all | solution.py:455
  112.9 1.1 decode.1.mine
  114.0 0.4 collective-permute-start.16
  114.3 0.9 collective-permute-done.16.theirs
  115.2 1.3 %joined.1 = bf16[4,512]{1,0:T(4,128)(2,1)} custom-call(s32[11]{0:T(128)S(1)} %stack.47.place, f32[32,256]{1,0:T(8,128)S(1)} %decode.1.mine, f32[32,256]{1,0:T(8,128)S(1)} %collective-permute-done.16.theirs), custom_call_target="tpu_custom_call" | custom-call | flops 1000 | bytes 1000 | tf_op jit(solution)/shard_map/joined/pallas_call | solution.py:351
  116.5 0.8 copy.17
  (8 shorter events, 0.0 us)
Async XLA Ops:
  2.0 27.4 %collective-permute-start = (bf16[256,1024]{1,0:T(8,128)(2,1)S(1)}, bf16[256,1024]{1,0:T(8,128)(2,1)S(1)}, u32[]{:S(2)}, u32[]{:S(2)}) collective-permute-start(bf16[256,1024]{1,0:T(8,128)(2,1)S(1)} %pad_maximum_fusion.refs_0_), channel_id=1, source_target_pairs={{0,8},{1,9},{2,10},{3,11},{4,12},{5,13},{6,14},{7,15},{8,0},{9,1},... | collective-permute-start | bytes 1572872 | tf_op jit(solution)/shard_map/ppermute | solution.py:64
  6.1 23.5 %collective-permute-start.1 = (bf16[256,1024]{1,0:T(8,128)(2,1)S(1)}, bf16[256,1024]{1,0:T(8,128)(2,1)S(1)}, u32[]{:S(2)}, u32[]{:S(2)}) collective-permute-start(bf16[256,1024]{1,0:T(8,128)(2,1)S(1)} %pad_maximum_fusion.refs_0_), channel_id=1, source_target_pairs={{0,4},{1,5},{2,6},{3,7},{4,0},{5,1},{6,2},{7,3},{8,12},{9,13},{10,... | collective-permute-start | bytes 1572872 | tf_op jit(solution)/shard_map/ppermute | solution.py:64
  7.6 21.9 %collective-permute-start.2 = (bf16[256,1024]{1,0:T(8,128)(2,1)S(1)}, bf16[256,1024]{1,0:T(8,128)(2,1)S(1)}, u32[]{:S(2)}, u32[]{:S(2)}) collective-permute-start(bf16[256,1024]{1,0:T(8,128)(2,1)S(1)} %pad_maximum_fusion.refs_0_), channel_id=1, source_target_pairs={{0,2},{1,3},{2,0},{3,1},{4,6},{5,7},{6,4},{7,5},{8,10},{9,11},{10,... | collective-permute-start | bytes 1572872 | tf_op jit(solution)/shard_map/ppermute | solution.py:64
  9.3 2.5 %copy-start = (bf16[2,160,8192]{2,1,0:T(8,128)(2,1)S(1)}, bf16[2,160,8192]{2,1,0:T(8,128)(2,1)}, u32[]{:S(2)}) copy-start(bf16[2,160,8192]{2,1,0:T(8,128)(2,1)} %param.14) | copy-start | bytes 15728644
  29.5 15.9 %collective-permute-start.9 = (bf16[16,320,256]{2,1,0:T(8,128)(2,1)S(1)}, bf16[16,320,256]{2,1,0:T(8,128)(2,1)S(1)}, u32[]{:S(2)}, u32[]{:S(2)}) collective-permute-start(bf16[16,320,256]{2,1,0:T(8,128)(2,1)S(1)} %get-tuple-element.34), channel_id=1, source_target_pairs={{0,1},{1,0},{2,3},{3,2},{4,5},{5,4},{6,7},{7,6},{8,9},{9,8},{10,11... | collective-permute-start | bytes 7864328 | tf_op jit(solution)/shard_map/ppermute | solution.py:64
  29.5 14.3 %collective-permute-start.7 = (bf16[256,1024]{1,0:T(8,128)(2,1)S(1)}, bf16[256,1024]{1,0:T(8,128)(2,1)S(1)}, u32[]{:S(2)}, u32[]{:S(2)}) collective-permute-start(bf16[256,1024]{1,0:T(8,128)(2,1)S(1)} %collective-permute-done.2.refs_2_), channel_id=1, source_target_pairs={{0,16},{1,17},{2,18},{3,19},{4,20},{5,21},{6,22},{7,23},{8,24},{9,... | collective-permute-start | bytes 1572872 | tf_op jit(solution)/shard_map/ppermute | solution.py:64
  31.1 18.8 %collective-permute-start.6 = (bf16[256,1024]{1,0:T(8,128)(2,1)S(1)}, bf16[256,1024]{1,0:T(8,128)(2,1)S(1)}, u32[]{:S(2)}, u32[]{:S(2)}) collective-permute-start(bf16[256,1024]{1,0:T(8,128)(2,1)S(1)} %collective-permute-done.1.refs_3_), channel_id=1, source_target_pairs={{0,2},{1,3},{2,0},{3,1},{4,6},{5,7},{6,4},{7,5},{8,10},{9,11},{10,... | collective-permute-start | bytes 1572872 | tf_op jit(solution)/shard_map/ppermute | solution.py:64
  32.6 17.3 %collective-permute-start.5 = (bf16[256,1024]{1,0:T(8,128)(2,1)S(1)}, bf16[256,1024]{1,0:T(8,128)(2,1)S(1)}, u32[]{:S(2)}, u32[]{:S(2)}) collective-permute-start(bf16[256,1024]{1,0:T(8,128)(2,1)S(1)} %pad_maximum_fusion.1.refs_1_), channel_id=1, source_target_pairs={{0,4},{1,5},{2,6},{3,7},{4,0},{5,1},{6,2},{7,3},{8,12},{9,13},{10,... | collective-permute-start | bytes 1572872 | tf_op jit(solution)/shard_map/ppermute | solution.py:64
  34.0 25.1 %collective-permute-start.4 = (bf16[256,1024]{1,0:T(8,128)(2,1)S(1)}, bf16[256,1024]{1,0:T(8,128)(2,1)S(1)}, u32[]{:S(2)}, u32[]{:S(2)}) collective-permute-start(bf16[256,1024]{1,0:T(8,128)(2,1)S(1)} %pad_maximum_fusion.refs_0_), channel_id=1, source_target_pairs={{0,12},{1,13},{2,14},{3,15},{4,8},{5,9},{6,10},{7,11},{8,4},{9,5},... | collective-permute-start | bytes 1572872 | tf_op jit(solution)/shard_map/ppermute | solution.py:64
  43.9 15.3 %collective-permute-start.3 = (bf16[256,1024]{1,0:T(8,128)(2,1)S(1)}, bf16[256,1024]{1,0:T(8,128)(2,1)S(1)}, u32[]{:S(2)}, u32[]{:S(2)}) collective-permute-start(bf16[256,1024]{1,0:T(8,128)(2,1)S(1)} %collective-permute-done.refs_4_), channel_id=1, source_target_pairs={{0,2},{1,3},{2,0},{3,1},{4,6},{5,7},{6,4},{7,5},{8,10},{9,11},{10,... | collective-permute-start | bytes 1572872 | tf_op jit(solution)/shard_map/ppermute | solution.py:64
  45.4 13.7 %collective-permute-start.8 = (bf16[256,1024]{1,0:T(8,128)(2,1)S(1)}, bf16[256,1024]{1,0:T(8,128)(2,1)S(1)}, u32[]{:S(2)}, u32[]{:S(2)}) collective-permute-start(bf16[256,1024]{1,0:T(8,128)(2,1)S(1)} %collective-permute-done.refs_4_), channel_id=1, source_target_pairs={{0,16},{1,17},{2,18},{3,19},{4,20},{5,21},{6,22},{7,23},{8,24},{9,... | collective-permute-start | bytes 1572872 | tf_op jit(solution)/shard_map/ppermute | solution.py:64
  59.2 13.1 %collective-permute-start.12 = (bf16[256,1024]{1,0:T(8,128)(2,1)S(1)}, bf16[256,1024]{1,0:T(8,128)(2,1)S(1)}, u32[]{:S(2)}, u32[]{:S(2)}) collective-permute-start(bf16[256,1024]{1,0:T(8,128)(2,1)S(1)} %collective-permute-done.7.refs_0_), channel_id=1, source_target_pairs={{0,4},{1,5},{2,6},{3,7},{4,0},{5,1},{6,2},{7,3},{8,12},{9,13},{10,... | collective-permute-start | bytes 1572872 | tf_op jit(solution)/shard_map/ppermute | solution.py:64
  60.2 12.2 %collective-permute-start.10 = (bf16[256,1024]{1,0:T(8,128)(2,1)S(1)}, bf16[256,1024]{1,0:T(8,128)(2,1)S(1)}, u32[]{:S(2)}, u32[]{:S(2)}) collective-permute-start(bf16[256,1024]{1,0:T(8,128)(2,1)S(1)} %collective-permute-done.4.refs_5_), channel_id=1, source_target_pairs={{0,2},{1,3},{2,0},{3,1},{4,6},{5,7},{6,4},{7,5},{8,10},{9,11},{10,... | collective-permute-start | bytes 1572872 | tf_op jit(solution)/shard_map/ppermute | solution.py:64
  60.7 11.9 %collective-permute-start.11 = (bf16[256,1024]{1,0:T(8,128)(2,1)S(1)}, bf16[256,1024]{1,0:T(8,128)(2,1)S(1)}, u32[]{:S(2)}, u32[]{:S(2)}) collective-permute-start(bf16[256,1024]{1,0:T(8,128)(2,1)S(1)} %collective-permute-done.4.refs_5_), channel_id=1, source_target_pairs={{0,16},{1,17},{2,18},{3,19},{4,20},{5,21},{6,22},{7,23},{8,24},{9,... | collective-permute-start | bytes 1572872 | tf_op jit(solution)/shard_map/ppermute | solution.py:64
  72.6 11.9 %collective-permute-start.14 = (bf16[256,1024]{1,0:T(8,128)(2,1)S(1)}, bf16[256,1024]{1,0:T(8,128)(2,1)S(1)}, u32[]{:S(2)}, u32[]{:S(2)}) collective-permute-start(bf16[256,1024]{1,0:T(8,128)(2,1)S(1)} %collective-permute-done.11.refs_2_), channel_id=1, source_target_pairs={{0,2},{1,3},{2,0},{3,1},{4,6},{5,7},{6,4},{7,5},{8,10},{9,11},{10,... | collective-permute-start | bytes 1572872 | tf_op jit(solution)/shard_map/ppermute | solution.py:64
  74.1 10.7 %collective-permute-start.13 = (bf16[256,1024]{1,0:T(8,128)(2,1)S(1)}, bf16[256,1024]{1,0:T(8,128)(2,1)S(1)}, u32[]{:S(2)}, u32[]{:S(2)}) collective-permute-start(bf16[256,1024]{1,0:T(8,128)(2,1)S(1)} %collective-permute-done.3.refs_3_), channel_id=1, source_target_pairs={{0,16},{1,17},{2,18},{3,19},{4,20},{5,21},{6,22},{7,23},{8,24},{9,... | collective-permute-start | bytes 1572872 | tf_op jit(solution)/shard_map/ppermute | solution.py:64
  84.8 5.1 %copy-start.1 = (f32[64,128]{1,0:T(8,128)S(1)}, f32[64,128]{1,0:T(8,128)}, u32[]{:S(2)}) copy-start(f32[64,128]{1,0:T(8,128)} %constant.70.clone.refs_4_.refs_2_) | copy-start | bytes 98308
  84.8 5.1 %copy-start.2 = (f32[64,128]{1,0:T(8,128)S(1)}, f32[64,128]{1,0:T(8,128)}, u32[]{:S(2)}) copy-start(f32[64,128]{1,0:T(8,128)} %constant.71.clone.refs_5_.refs_3_) | copy-start | bytes 98308
  84.8 5.1 %copy-start.3 = (f32[41,128]{1,0:T(8,128)S(1)}, f32[41,128]{1,0:T(8,128)}, u32[]{:S(2)}) copy-start(f32[41,128]{1,0:T(8,128)} %constant.68.clone.refs_2_.refs_0_) | copy-start | bytes 62980
  84.8 5.1 %copy-start.4 = (f32[41,128]{1,0:T(8,128)S(1)}, f32[41,128]{1,0:T(8,128)}, u32[]{:S(2)}) copy-start(f32[41,128]{1,0:T(8,128)} %constant.69.clone.refs_3_.refs_1_) | copy-start | bytes 62980
  84.8 5.1 %copy-start.5 = (f32[160,128]{1,0:T(8,128)S(1)}, f32[160,128]{1,0:T(8,128)}, u32[]{:S(2)}) copy-start(f32[160,128]{1,0:T(8,128)} %constant.72.clone.refs_6_) | copy-start | bytes 245764
  84.8 5.1 %copy-start.6 = (f32[160,128]{1,0:T(8,128)S(1)}, f32[160,128]{1,0:T(8,128)}, u32[]{:S(2)}) copy-start(f32[160,128]{1,0:T(8,128)} %constant.73.clone.refs_7_) | copy-start | bytes 245764
  84.8 5.1 %copy-start.10 = (s32[2]{0:T(128)S(1)}, s32[2]{0:T(128)}, u32[]{:S(2)}) copy-start(s32[2]{0:T(128)} %lengths.3) | copy-start | bytes 28
  84.8 5.1 %copy-start.11 = (s32[8]{0:T(128)S(1)}, s32[8]{0:T(128)}, u32[]{:S(2)}) copy-start(s32[8]{0:T(128)} %owner.3) | copy-start | bytes 100
  86.7 3.1 %collective-permute-start.15 = (f32[320,1024]{1,0:T(8,128)S(1)}, f32[320,1024]{1,0:T(8,128)S(1)}, u32[]{:S(2)}, u32[]{:S(2)}) collective-permute-start(f32[320,1024]{1,0:T(8,128)S(1)} %get-tuple-element.49), channel_id=1, source_target_pairs={{0,1},{1,0},{2,3},{3,2},{4,5},{5,4},{6,7},{7,6},{8,9},{9,8},{10,11... | collective-permute-start | bytes 3932168 | tf_op jit(solution)/shard_map/ppermute | solution.py:64
  91.0 21.9 %copy-start.7 = (bf16[8,4,1024]{2,1,0:T(4,128)(2,1)S(1)}, bf16[8,4,1024]{2,1,0:T(4,128)(2,1)}, u32[]{:S(2)}) copy-start(bf16[8,4,1024]{2,1,0:T(4,128)(2,1)} %dec_query.1) | copy-start | bytes 196612
  91.0 21.9 %copy-start.8 = (bf16[8,4,128]{2,1,0:T(4,128)(2,1)S(1)}, bf16[8,4,128]{2,1,0:T(4,128)(2,1)}, u32[]{:S(2)}) copy-start(bf16[8,4,128]{2,1,0:T(4,128)(2,1)} %dec_key.1) | copy-start | bytes 24580
  91.0 21.9 %copy-start.9 = (bf16[8,4,128]{2,1,0:T(4,128)(2,1)S(1)}, bf16[8,4,128]{2,1,0:T(4,128)(2,1)}, u32[]{:S(2)}) copy-start(bf16[8,4,128]{2,1,0:T(4,128)(2,1)} %dec_value.1) | copy-start | bytes 24580
  114.0 1.3 %collective-permute-start.16 = (f32[32,256]{1,0:T(8,128)S(1)}, f32[32,256]{1,0:T(8,128)S(1)}, u32[]{:S(2)}, u32[]{:S(2)}) collective-permute-start(f32[32,256]{1,0:T(8,128)S(1)} %decode.1.mine), channel_id=1, source_target_pairs={{0,1},{1,0},{2,3},{3,2},{4,5},{5,4},{6,7},{7,6},{8,9},{9,8},{10,11... | collective-permute-start | bytes 98312 | tf_op jit(solution)/shard_map/ppermute | solution.py:64

commit v16 on v14

--- a/solution.py
+++ b/solution.py
@@ -83,11 +83,7 @@
 
 
 def to_middle(g, z, y, c):
-    return (g, 3 - z, y, c) if z in (1, 2) else None
-
-
-def to_end(g, z, y, c):
-    return (g, 0 if z == 1 else 3, y, c) if z in (1, 2) else None
+    return (g, 3 - z if z in (1, 2) else z, y, c)
 
 
 VMEM_REF = pl.BlockSpec(memory_space=pltpu.VMEM)
@@ -438,13 +434,13 @@
         rest = half_block(depth - group_id * depth)
         mine, kept = prepared(place, flat, seq // 2)
         layers, rows = (near, middle), (across, mine, rest)
-        end_b = moved(after(middle, *layers), to_end)
+        end_b = moved(after(middle, *layers), to_pair)
         middle_c = moved(after(near, *layers), to_middle)
         near_y = moved(after(near, *layers, *rows), to_row)
         across_x = moved(after(across, *layers, *rows), to_group)
         other = moved(after(kept, *layers, *rows), to_core)
         layers, rows, before = (end_b, middle_c), (near_y, across_x, other), rows
-        end_c = moved(after(middle_c, *layers, *before), to_end)
+        end_c = moved(after(middle_c, *layers, *before), to_pair)
         block_b = jnp.where(is_end, after(end_b, *layers), middle)
         block_yb = moved(after(block_b, *rows), to_row)
         block_xb = moved(after(block_b, *rows), to_group)

time: 121 us -> 122 us (level)
  starting transfers between devices: 24.2 us -> 26.7 us
  waiting for transfers between devices: 44.6 us -> 42.7 us
    ppermute x19, starting transfers between devices: 24.2 us -> 26.7 us  [moved(): return lax.ppermute(block, ('groups', 'seq'), route)]
    ppermute x19, waiting for transfers between devices: 44.6 us -> 42.7 us  [moved(): return lax.ppermute(block, ('groups', 'seq'), route)]
where the time goes in v16:
time: 122 us; the launch traced here: 121 us
  waiting for transfers between devices  42.7 us (35%)
  starting transfers between devices  26.7 us (22%)
  Pallas kernels  21.6 us (18%)
  blocking collectives  20.9 us (17%)
  local copies, waits for them, and re-layouts  5.44 us (4%)
  other arithmetic  3.17 us (3%)
    ppermute x19, waiting for transfers between devices, moved(): return lax.ppermute(block, ('groups', 'seq'), route)  42.7 us
    ppermute x19, starting transfers between devices, moved(): return lax.ppermute(block, ('groups', 'seq'), route)  26.7 us
    all_to_all x1, blocking collectives, body(): lax.all_to_all(outgoing, 'seq', split_axis=0, concat_axis=1, tiled=True)  20.9 us
    pallas_call x4, Pallas kernels, product(): pl.pallas_call(functools.partial(product_kernel, plan, group, bool(totals...  14.3 us
    pallas_call x1, Pallas kernels, prepared(): pl.pallas_call(prepare_kernel, grid_spec=pltpu.PrefetchScalarGridSpec(num...  3.9 us
    unnamed x29, local copies, waits for them, and re-layouts  3.39 us
  transfers between devices with their start and end apart: 19, of which 12 were waited for; matrix products, arithmetic and copies ran while one was open for 3% of the time, Pallas kernels for 13%

profile of v16, /device:TPU:0, one launch (start us, length us, event | category | flops | bytes accessed | tf_op | source)
XLA Modules:
  0.0 121.4 jit_solution(17929804399354634285)
XLA Ops:
  0.6 2.0 %constant_dynamic-slice_fusion = (bf16[256,512]{1,0:T(8,128)(2,1)S(1)}, bf16[256,512]{1,0:T(8,128)(2,1)S(1)}, bf16[256,512]{1,0:T(8,128)(2,1)S(1)}, bf16[256,512]{1,0:T(8,128)(2,1)}) fusion(bf16[512,512]{1,0:T(8,128)(2,1)} %param.16, s32[]{:T(128)S(6)} %select_n.54, s32[]{:T(128)S(6)} %select_n.52, bf16[512,512]{1,0:T(8,128)(2,1)} %param.15), kind=kLoop, calls=%fused_computation.4 | loop fusion | bytes 2097160 | tf_op jit(solution)/shard_map/dynamic_slice | solution.py:424
  2.6 0.1 pad_maximum_fusion.refs_0_
  2.7 1.5 %collective-permute-start = (bf16[256,1024]{1,0:T(8,128)(2,1)S(1)}, bf16[256,1024]{1,0:T(8,128)(2,1)}, u32[]{:S(2)}, u32[]{:S(2)}) collective-permute-start(bf16[256,1024]{1,0:T(8,128)(2,1)S(1)} %pad_maximum_fusion.refs_0_), channel_id=1, source_target_pairs={{0,0},{1,1},{2,2},{3,3},{4,8},{5,9},{6,10},{7,11},{8,4},{9,5},{10,... | collective-permute-start | bytes 1572872 | tf_op jit(solution)/shard_map/ppermute | solution.py:66
  4.1 5.1 %collective-permute-start.1 = (bf16[256,1024]{1,0:T(8,128)(2,1)S(1)}, bf16[256,1024]{1,0:T(8,128)(2,1)}, u32[]{:S(2)}, u32[]{:S(2)}) collective-permute-start(bf16[256,1024]{1,0:T(8,128)(2,1)S(1)} %pad_maximum_fusion.refs_0_), channel_id=1, source_target_pairs={{0,4},{1,5},{2,6},{3,7},{4,0},{5,1},{6,2},{7,3},{8,12},{9,13},{10,... | collective-permute-start | bytes 1572872 | tf_op jit(solution)/shard_map/ppermute | solution.py:66
  9.2 1.5 %collective-permute-start.4 = (bf16[256,1024]{1,0:T(8,128)(2,1)S(1)}, bf16[256,1024]{1,0:T(8,128)(2,1)}, u32[]{:S(2)}, u32[]{:S(2)}) collective-permute-start(bf16[256,1024]{1,0:T(8,128)(2,1)S(1)} %pad_maximum_fusion.refs_0_), channel_id=1, source_target_pairs={{0,2},{1,3},{2,0},{3,1},{4,6},{5,7},{6,4},{7,5},{8,10},{9,11},{10,... | collective-permute-start | bytes 1572872 | tf_op jit(solution)/shard_map/ppermute | solution.py:66
  10.8 0.1 stack.47.place
  10.9 2.5 %copy-done = bf16[2,160,8192]{2,1,0:T(8,128)(2,1)S(1)} copy-done((bf16[2,160,8192]{2,1,0:T(8,128)(2,1)S(1)}, bf16[2,160,8192]{2,1,0:T(8,128)(2,1)}, u32[]{:S(2)}) %copy-start) | copy-done | bytes 5242904
  13.3 3.9 %normed_halves.1 = (bf16[16,320,256]{2,1,0:T(8,128)(2,1)S(1)}, bf16[16,320,256]{2,1,0:T(8,128)(2,1)}) custom-call(s32[11]{0:T(128)S(1)} %stack.47.place, bf16[320,8192]{1,0:T(8,128)(2,1)S(1)} %bitcast.16), custom_call_target="tpu_custom_call" | custom-call | flops 1000 | bytes 1000 | tf_op jit(solution)/shard_map/normed_halves/pallas_call | solution.py:131
  17.3 0.9 pad_maximum_fusion.1.refs_1_
  18.1 0.0 collective-permute-done
  18.1 2.9 %collective-permute-done.1.refs_4_ = bf16[256,1024]{1,0:T(8,128)(2,1)} collective-permute-done((bf16[256,1024]{1,0:T(8,128)(2,1)S(1)}, bf16[256,1024]{1,0:T(8,128)(2,1)}, u32[]{:S(2)}, u32[]{:S(2)}) %collective-permute-start.1) | collective-permute-done | bytes 524320 | tf_op jit(solution)/shard_map/ppermute | solution.py:66
  21.0 1.5 %collective-permute-done.4.refs_2_ = bf16[256,1024]{1,0:T(8,128)(2,1)} collective-permute-done((bf16[256,1024]{1,0:T(8,128)(2,1)S(1)}, bf16[256,1024]{1,0:T(8,128)(2,1)}, u32[]{:S(2)}, u32[]{:S(2)}) %collective-permute-start.4) | collective-permute-done | bytes 524320 | tf_op jit(solution)/shard_map/ppermute | solution.py:66
  22.5 0.0 collective-permute-start.7
  22.5 5.4 %collective-permute-start.3 = (bf16[256,1024]{1,0:T(8,128)(2,1)}, bf16[256,1024]{1,0:T(8,128)(2,1)}, u32[]{:S(2)}, u32[]{:S(2)}) collective-permute-start(bf16[256,1024]{1,0:T(8,128)(2,1)} %collective-permute-done.1.refs_4_), channel_id=1, source_target_pairs={{0,0},{1,1},{2,2},{3,3},{4,8},{5,9},{6,10},{7,11},{8,4},{9,5},{10,... | collective-permute-start | bytes 1572872 | tf_op jit(solution)/shard_map/ppermute | solution.py:66
  27.8 0.0 collective-permute-start.2
  27.8 1.5 %collective-permute-start.6 = (bf16[256,1024]{1,0:T(8,128)(2,1)}, bf16[256,1024]{1,0:T(8,128)(2,1)}, u32[]{:S(2)}, u32[]{:S(2)}) collective-permute-start(bf16[256,1024]{1,0:T(8,128)(2,1)} %collective-permute-done.4.refs_2_), channel_id=1, source_target_pairs={{0,16},{1,17},{2,18},{3,19},{4,20},{5,21},{6,22},{7,23},{8,24},{9,... | collective-permute-start | bytes 1572872 | tf_op jit(solution)/shard_map/ppermute | solution.py:66
  29.3 1.5 %collective-permute-start.5 = (bf16[256,1024]{1,0:T(8,128)(2,1)}, bf16[256,1024]{1,0:T(8,128)(2,1)}, u32[]{:S(2)}, u32[]{:S(2)}) collective-permute-start(bf16[256,1024]{1,0:T(8,128)(2,1)} %collective-permute-done.1.refs_4_), channel_id=1, source_target_pairs={{0,2},{1,3},{2,0},{3,1},{4,6},{5,7},{6,4},{7,5},{8,10},{9,11},{10,... | collective-permute-start | bytes 1572872 | tf_op jit(solution)/shard_map/ppermute | solution.py:66
  30.9 0.0 collective-permute-done.3
  30.9 11.6 %collective-permute-done.2 = bf16[256,1024]{1,0:T(8,128)(2,1)} collective-permute-done((bf16[256,1024]{1,0:T(8,128)(2,1)}, bf16[256,1024]{1,0:T(8,128)(2,1)}, u32[]{:S(2)}, u32[]{:S(2)}) %collective-permute-start.2) | collective-permute-done | bytes 524320 | tf_op jit(solution)/shard_map/ppermute | solution.py:66
  42.5 0.3 collective-permute-start.9
  42.8 1.2 broadcast_select_fusion.1.refs_0_
  43.9 0.0 collective-permute-done.6.refs_3_
  43.9 0.0 collective-permute-done.5.refs_5_
  44.0 0.0 collective-permute-done.7.other
  44.0 1.6 %collective-permute-start.10 = (bf16[256,1024]{1,0:T(8,128)(2,1)S(1)}, bf16[256,1024]{1,0:T(8,128)(2,1)S(1)}, u32[]{:S(2)}, u32[]{:S(2)}) collective-permute-start(bf16[256,1024]{1,0:T(8,128)(2,1)S(1)} %broadcast_select_fusion.1.refs_0_), channel_id=1, source_target_pairs={{0,16},{1,17},{2,18},{3,19},{4,20},{5,21},{6,22},{7,23},{8,24},{9,... | collective-permute-start | bytes 1572872 | tf_op jit(solution)/shard_map/ppermute | solution.py:66
  45.5 1.5 %collective-permute-start.8 = (bf16[256,1024]{1,0:T(8,128)(2,1)S(1)}, bf16[256,1024]{1,0:T(8,128)(2,1)S(1)}, u32[]{:S(2)}, u32[]{:S(2)}) collective-permute-start(bf16[256,1024]{1,0:T(8,128)(2,1)S(1)} %broadcast_select_fusion.1.refs_0_), channel_id=1, source_target_pairs={{0,2},{1,3},{2,0},{3,1},{4,6},{5,7},{6,4},{7,5},{8,10},{9,11},{10,... | collective-permute-start | bytes 1572872 | tf_op jit(solution)/shard_map/ppermute | solution.py:66
  47.0 9.3 %collective-permute-done.9 = bf16[256,1024]{1,0:T(8,128)(2,1)} collective-permute-done((bf16[256,1024]{1,0:T(8,128)(2,1)}, bf16[256,1024]{1,0:T(8,128)(2,1)}, u32[]{:S(2)}, u32[]{:S(2)}) %collective-permute-start.9) | collective-permute-done | bytes 524320 | tf_op jit(solution)/shard_map/ppermute | solution.py:66
  56.4 1.1 broadcast_select_fusion.refs_3_
  57.5 0.5 collective-permute-start.15
  58.0 4.4 %add_product.4 = (f32[320,1024]{1,0:T(8,128)S(1)}, f32[320,1024]{1,0:T(8,128)S(1)}) custom-call(s32[11]{0:T(128)S(1)} %stack.47.place, bf16[16,320,256]{2,1,0:T(8,128)(2,1)S(1)} %get-tuple-element.55.mine, bf16[16,320,256]{2,1,0:T(8,128)(2,1)} %collective-permute-done.7.other, bf16[256,1024]{1,0:T(8,128)(2,1)S(1)} %pad_maximum_fusion.refs_0_, ...), custom_call_target="tpu_custom_call" | custom-call | flops 1000 | bytes 1000 | tf_op jit(solution)/shard_map/add_product/pallas_call | solution.py:198
  62.5 0.0 collective-permute-done.10.refs_1_
  62.5 0.0 collective-permute-done.8.refs_2_
  62.5 1.6 %collective-permute-start.11 = (bf16[256,1024]{1,0:T(8,128)(2,1)S(1)}, bf16[256,1024]{1,0:T(8,128)(2,1)S(1)}, u32[]{:S(2)}, u32[]{:S(2)}) collective-permute-start(bf16[256,1024]{1,0:T(8,128)(2,1)S(1)} %broadcast_select_fusion.refs_3_), channel_id=1, source_target_pairs={{0,16},{1,17},{2,18},{3,19},{4,20},{5,21},{6,22},{7,23},{8,24},{9,... | collective-permute-start | bytes 1572872 | tf_op jit(solution)/shard_map/ppermute | solution.py:66
  64.0 1.5 %collective-permute-start.12 = (bf16[256,1024]{1,0:T(8,128)(2,1)S(1)}, bf16[256,1024]{1,0:T(8,128)(2,1)S(1)}, u32[]{:S(2)}, u32[]{:S(2)}) collective-permute-start(bf16[256,1024]{1,0:T(8,128)(2,1)S(1)} %broadcast_select_fusion.refs_3_), channel_id=1, source_target_pairs={{0,2},{1,3},{2,0},{3,1},{4,6},{5,7},{6,4},{7,5},{8,10},{9,11},{10,... | collective-permute-start | bytes 1572872 | tf_op jit(solution)/shard_map/ppermute | solution.py:66
  65.6 4.6 %collective-permute-done.15.refs_0_ = bf16[256,1024]{1,0:T(8,128)(2,1)S(1)} collective-permute-done((bf16[256,1024]{1,0:T(8,128)(2,1)S(1)}, bf16[256,1024]{1,0:T(8,128)(2,1)S(1)}, u32[]{:S(2)}, u32[]{:S(2)}) %collective-permute-start.15) | collective-permute-done | bytes 524320 | tf_op jit(solution)/shard_map/ppermute | solution.py:66
  70.2 0.7 collective-permute-start.16
  70.9 3.6 %add_product.5 = (f32[320,1024]{1,0:T(8,128)S(1)}, f32[320,1024]{1,0:T(8,128)S(1)}) custom-call(s32[11]{0:T(128)S(1)} %stack.47.place, bf16[16,320,256]{2,1,0:T(8,128)(2,1)S(1)} %get-tuple-element.55.mine, bf16[16,320,256]{2,1,0:T(8,128)(2,1)} %collective-permute-done.7.other, bf16[256,1024]{1,0:T(8,128)(2,1)S(1)} %broadcast_select_fusion.1.refs_0_, ...), custom_call_target="tpu_custom_call" | custom-call | flops 1000 | bytes 1000 | tf_op jit(solution)/shard_map/add_product/pallas_call | solution.py:198
  74.5 0.6 collective-permute-done.11.refs_1_
  75.2 1.2 collective-permute-done.12.refs_2_
  76.4 1.5 %collective-permute-start.14 = (bf16[256,1024]{1,0:T(8,128)(2,1)S(1)}, bf16[256,1024]{1,0:T(8,128)(2,1)S(1)}, u32[]{:S(2)}, u32[]{:S(2)}) collective-permute-start(bf16[256,1024]{1,0:T(8,128)(2,1)S(1)} %collective-permute-done.11.refs_1_), channel_id=1, source_target_pairs={{0,2},{1,3},{2,0},{3,1},{4,6},{5,7},{6,4},{7,5},{8,10},{9,11},{10,... | collective-permute-start | bytes 1572872 | tf_op jit(solution)/shard_map/ppermute | solution.py:66
  77.9 0.5 collective-permute-start.13
  78.4 3.7 %collective-permute-done.16.refs_3_ = bf16[256,1024]{1,0:T(8,128)(2,1)S(1)} collective-permute-done((bf16[256,1024]{1,0:T(8,128)(2,1)}, bf16[256,1024]{1,0:T(8,128)(2,1)S(1)}, u32[]{:S(2)}, u32[]{:S(2)}) %collective-permute-start.16) | collective-permute-done | bytes 524320 | tf_op jit(solution)/shard_map/ppermute | solution.py:66
  82.2 3.6 %add_product.6 = (f32[320,1024]{1,0:T(8,128)S(1)}, f32[320,1024]{1,0:T(8,128)S(1)}) custom-call(s32[11]{0:T(128)S(1)} %stack.47.place, bf16[16,320,256]{2,1,0:T(8,128)(2,1)S(1)} %get-tuple-element.55.mine, bf16[16,320,256]{2,1,0:T(8,128)(2,1)} %collective-permute-done.7.other, bf16[256,1024]{1,0:T(8,128)(2,1)S(1)} %collective-permute-done.15.refs_0_, ...), custom_call_target="tpu_custom_call" | custom-call | flops 1000 | bytes 16777216 | tf_op jit(solution)/shard_map/add_product/pallas_call | solution.py:198
  85.8 2.0 %collective-permute-done.14.refs_1_ = bf16[256,1024]{1,0:T(8,128)(2,1)S(1)} collective-permute-done((bf16[256,1024]{1,0:T(8,128)(2,1)S(1)}, bf16[256,1024]{1,0:T(8,128)(2,1)S(1)}, u32[]{:S(2)}, u32[]{:S(2)}) %collective-permute-start.14) | collective-permute-done | bytes 524320 | tf_op jit(solution)/shard_map/ppermute | solution.py:66
  87.8 1.2 %collective-permute-done.13.refs_0_ = bf16[256,1024]{1,0:T(8,128)(2,1)S(1)} collective-permute-done((bf16[256,1024]{1,0:T(8,128)(2,1)S(1)}, bf16[256,1024]{1,0:T(8,128)(2,1)S(1)}, u32[]{:S(2)}, u32[]{:S(2)}) %collective-permute-start.13) | collective-permute-done | bytes 524320 | tf_op jit(solution)/shard_map/ppermute | solution.py:66
  89.0 0.0 copy-start.6
  89.1 0.0 copy-start.7
  89.1 0.0 copy-start.11
  89.1 0.0 copy-start.12
  89.1 2.6 %add_product.7 = (f32[320,1024]{1,0:T(8,128)S(1)}, f32[320,1024]{1,0:T(8,128)S(1)}) custom-call(s32[11]{0:T(128)S(1)} %stack.47.place, bf16[16,320,256]{2,1,0:T(8,128)(2,1)S(1)} %get-tuple-element.55.mine, bf16[16,320,256]{2,1,0:T(8,128)(2,1)} %collective-permute-done.7.other, bf16[256,1024]{1,0:T(8,128)(2,1)S(1)} %collective-permute-done.13.refs_0_, ...), custom_call_target="tpu_custom_call" | custom-call | flops 1000 | bytes 1000 | tf_op jit(solution)/shard_map/add_product/pallas_call | solution.py:198
  91.7 0.1 collective-permute-start.17
  91.8 3.0 %collective-permute-done.17.refs_1_ = f32[320,1024]{1,0:T(8,128)S(1)} collective-permute-done((f32[320,1024]{1,0:T(8,128)S(1)}, f32[320,1024]{1,0:T(8,128)S(1)}, u32[]{:S(2)}, u32[]{:S(2)}) %collective-permute-start.17) | collective-permute-done | bytes 1310752 | tf_op jit(solution)/shard_map/ppermute | solution.py:66
  94.8 0.0 copy-done.5
  94.8 0.0 copy-done.6
  94.9 1.0 cache_rows.1
  95.9 0.0 copy-start.8
  95.9 0.0 copy-start.9
  95.9 0.0 copy-start.10
  95.9 20.9 %all_to_all.12 = bf16[16,80,256]{2,1,0:T(8,128)(2,1)S(1)} all-to-all(bf16[16,80,256]{2,1,0:T(8,128)(2,1)S(1)} %cache_rows.1), channel_id=1, replica_groups=mesh['groups'=2,'seq'=16] {'seq'}, dimensions={0} | all-to-all | bytes 1310720 | tf_op jit(solution)/shard_map/all_to_all | solution.py:467
  116.9 1.1 decode.1.mine
  118.0 0.4 collective-permute-start.18
  118.4 0.9 collective-permute-done.18.theirs
  119.3 1.3 %joined.1 = bf16[4,512]{1,0:T(4,128)(2,1)} custom-call(s32[11]{0:T(128)S(1)} %stack.47.place, f32[32,256]{1,0:T(8,128)S(1)} %decode.1.mine, f32[32,256]{1,0:T(8,128)S(1)} %collective-permute-done.18.theirs), custom_call_target="tpu_custom_call" | custom-call | flops 1000 | bytes 1000 | tf_op jit(solution)/shard_map/joined/pallas_call | solution.py:357
  120.6 0.8 copy.17
  (18 shorter events, 0.0 us)
Async XLA Ops:
  2.7 15.4 %collective-permute-start = (bf16[256,1024]{1,0:T(8,128)(2,1)S(1)}, bf16[256,1024]{1,0:T(8,128)(2,1)}, u32[]{:S(2)}, u32[]{:S(2)}) collective-permute-start(bf16[256,1024]{1,0:T(8,128)(2,1)S(1)} %pad_maximum_fusion.refs_0_), channel_id=1, source_target_pairs={{0,0},{1,1},{2,2},{3,3},{4,8},{5,9},{6,10},{7,11},{8,4},{9,5},{10,... | collective-permute-start | bytes 1572872 | tf_op jit(solution)/shard_map/ppermute | solution.py:66
  4.1 16.9 %collective-permute-start.1 = (bf16[256,1024]{1,0:T(8,128)(2,1)S(1)}, bf16[256,1024]{1,0:T(8,128)(2,1)}, u32[]{:S(2)}, u32[]{:S(2)}) collective-permute-start(bf16[256,1024]{1,0:T(8,128)(2,1)S(1)} %pad_maximum_fusion.refs_0_), channel_id=1, source_target_pairs={{0,4},{1,5},{2,6},{3,7},{4,0},{5,1},{6,2},{7,3},{8,12},{9,13},{10,... | collective-permute-start | bytes 1572872 | tf_op jit(solution)/shard_map/ppermute | solution.py:66
  9.2 13.2 %collective-permute-start.4 = (bf16[256,1024]{1,0:T(8,128)(2,1)S(1)}, bf16[256,1024]{1,0:T(8,128)(2,1)}, u32[]{:S(2)}, u32[]{:S(2)}) collective-permute-start(bf16[256,1024]{1,0:T(8,128)(2,1)S(1)} %pad_maximum_fusion.refs_0_), channel_id=1, source_target_pairs={{0,2},{1,3},{2,0},{3,1},{4,6},{5,7},{6,4},{7,5},{8,10},{9,11},{10,... | collective-permute-start | bytes 1572872 | tf_op jit(solution)/shard_map/ppermute | solution.py:66
  10.9 2.5 %copy-start = (bf16[2,160,8192]{2,1,0:T(8,128)(2,1)S(1)}, bf16[2,160,8192]{2,1,0:T(8,128)(2,1)}, u32[]{:S(2)}) copy-start(bf16[2,160,8192]{2,1,0:T(8,128)(2,1)} %param.14) | copy-start | bytes 15728644
  13.3 3.9 %copy-start.13 = (bf16[256,512]{1,0:T(8,128)(2,1)S(1)}, bf16[256,512]{1,0:T(8,128)(2,1)}, u32[]{:S(2)}) copy-start(bf16[256,512]{1,0:T(8,128)(2,1)} %get-tuple-element.63) | copy-start | bytes 786436
  22.5 21.5 %collective-permute-start.7 = (bf16[16,320,256]{2,1,0:T(8,128)(2,1)}, bf16[16,320,256]{2,1,0:T(8,128)(2,1)}, u32[]{:S(2)}, u32[]{:S(2)}) collective-permute-start(bf16[16,320,256]{2,1,0:T(8,128)(2,1)} %get-tuple-element.37), channel_id=1, source_target_pairs={{0,1},{1,0},{2,3},{3,2},{4,5},{5,4},{6,7},{7,6},{8,9},{9,8},{10,11... | collective-permute-start | bytes 7864328 | tf_op jit(solution)/shard_map/ppermute | solution.py:66
  22.5 8.4 %collective-permute-start.3 = (bf16[256,1024]{1,0:T(8,128)(2,1)}, bf16[256,1024]{1,0:T(8,128)(2,1)}, u32[]{:S(2)}, u32[]{:S(2)}) collective-permute-start(bf16[256,1024]{1,0:T(8,128)(2,1)} %collective-permute-done.1.refs_4_), channel_id=1, source_target_pairs={{0,0},{1,1},{2,2},{3,3},{4,8},{5,9},{6,10},{7,11},{8,4},{9,5},{10,... | collective-permute-start | bytes 1572872 | tf_op jit(solution)/shard_map/ppermute | solution.py:66
  27.8 14.7 %collective-permute-start.2 = (bf16[256,1024]{1,0:T(8,128)(2,1)}, bf16[256,1024]{1,0:T(8,128)(2,1)}, u32[]{:S(2)}, u32[]{:S(2)}) collective-permute-start(bf16[256,1024]{1,0:T(8,128)(2,1)} %collective-permute-done), channel_id=1, source_target_pairs={{0,4},{1,5},{2,6},{3,7},{4,0},{5,1},{6,2},{7,3},{8,12},{9,13},{10,... | collective-permute-start | bytes 1572872 | tf_op jit(solution)/shard_map/ppermute | solution.py:66
  27.8 16.1 %collective-permute-start.6 = (bf16[256,1024]{1,0:T(8,128)(2,1)}, bf16[256,1024]{1,0:T(8,128)(2,1)}, u32[]{:S(2)}, u32[]{:S(2)}) collective-permute-start(bf16[256,1024]{1,0:T(8,128)(2,1)} %collective-permute-done.4.refs_2_), channel_id=1, source_target_pairs={{0,16},{1,17},{2,18},{3,19},{4,20},{5,21},{6,22},{7,23},{8,24},{9,... | collective-permute-start | bytes 1572872 | tf_op jit(solution)/shard_map/ppermute | solution.py:66
  29.3 14.6 %collective-permute-start.5 = (bf16[256,1024]{1,0:T(8,128)(2,1)}, bf16[256,1024]{1,0:T(8,128)(2,1)}, u32[]{:S(2)}, u32[]{:S(2)}) collective-permute-start(bf16[256,1024]{1,0:T(8,128)(2,1)} %collective-permute-done.1.refs_4_), channel_id=1, source_target_pairs={{0,2},{1,3},{2,0},{3,1},{4,6},{5,7},{6,4},{7,5},{8,10},{9,11},{10,... | collective-permute-start | bytes 1572872 | tf_op jit(solution)/shard_map/ppermute | solution.py:66
  42.5 13.9 %collective-permute-start.9 = (bf16[256,1024]{1,0:T(8,128)(2,1)}, bf16[256,1024]{1,0:T(8,128)(2,1)}, u32[]{:S(2)}, u32[]{:S(2)}) collective-permute-start(bf16[256,1024]{1,0:T(8,128)(2,1)} %collective-permute-done.3), channel_id=1, source_target_pairs={{0,4},{1,5},{2,6},{3,7},{4,0},{5,1},{6,2},{7,3},{8,12},{9,13},{10,... | collective-permute-start | bytes 1572872 | tf_op jit(solution)/shard_map/ppermute | solution.py:66
  42.8 14.7 %copy-start.1 = (bf16[256,1024]{1,0:T(8,128)(2,1)S(1)}, bf16[256,1024]{1,0:T(8,128)(2,1)}, u32[]{:S(2)}) copy-start(bf16[256,1024]{1,0:T(8,128)(2,1)} %pad_maximum_fusion.1.refs_1_) | copy-start | bytes 1572868
  44.0 18.5 %collective-permute-start.10 = (bf16[256,1024]{1,0:T(8,128)(2,1)S(1)}, bf16[256,1024]{1,0:T(8,128)(2,1)S(1)}, u32[]{:S(2)}, u32[]{:S(2)}) collective-permute-start(bf16[256,1024]{1,0:T(8,128)(2,1)S(1)} %broadcast_select_fusion.1.refs_0_), channel_id=1, source_target_pairs={{0,16},{1,17},{2,18},{3,19},{4,20},{5,21},{6,22},{7,23},{8,24},{9,... | collective-permute-start | bytes 1572872 | tf_op jit(solution)/shard_map/ppermute | solution.py:66
  45.5 16.9 %collective-permute-start.8 = (bf16[256,1024]{1,0:T(8,128)(2,1)S(1)}, bf16[256,1024]{1,0:T(8,128)(2,1)S(1)}, u32[]{:S(2)}, u32[]{:S(2)}) collective-permute-start(bf16[256,1024]{1,0:T(8,128)(2,1)S(1)} %broadcast_select_fusion.1.refs_0_), channel_id=1, source_target_pairs={{0,2},{1,3},{2,0},{3,1},{4,6},{5,7},{6,4},{7,5},{8,10},{9,11},{10,... | collective-permute-start | bytes 1572872 | tf_op jit(solution)/shard_map/ppermute | solution.py:66
  57.5 12.7 %collective-permute-start.15 = (bf16[256,1024]{1,0:T(8,128)(2,1)S(1)}, bf16[256,1024]{1,0:T(8,128)(2,1)S(1)}, u32[]{:S(2)}, u32[]{:S(2)}) collective-permute-start(bf16[256,1024]{1,0:T(8,128)(2,1)S(1)} %copy-done.1), channel_id=1, source_target_pairs={{0,4},{1,5},{2,6},{3,7},{4,0},{5,1},{6,2},{7,3},{8,12},{9,13},{10,... | collective-permute-start | bytes 1572872 | tf_op jit(solution)/shard_map/ppermute | solution.py:66
  62.5 12.7 %collective-permute-start.11 = (bf16[256,1024]{1,0:T(8,128)(2,1)S(1)}, bf16[256,1024]{1,0:T(8,128)(2,1)S(1)}, u32[]{:S(2)}, u32[]{:S(2)}) collective-permute-start(bf16[256,1024]{1,0:T(8,128)(2,1)S(1)} %broadcast_select_fusion.refs_3_), channel_id=1, source_target_pairs={{0,16},{1,17},{2,18},{3,19},{4,20},{5,21},{6,22},{7,23},{8,24},{9,... | collective-permute-start | bytes 1572872 | tf_op jit(solution)/shard_map/ppermute | solution.py:66
  64.0 12.3 %collective-permute-start.12 = (bf16[256,1024]{1,0:T(8,128)(2,1)S(1)}, bf16[256,1024]{1,0:T(8,128)(2,1)S(1)}, u32[]{:S(2)}, u32[]{:S(2)}) collective-permute-start(bf16[256,1024]{1,0:T(8,128)(2,1)S(1)} %broadcast_select_fusion.refs_3_), channel_id=1, source_target_pairs={{0,2},{1,3},{2,0},{3,1},{4,6},{5,7},{6,4},{7,5},{8,10},{9,11},{10,... | collective-permute-start | bytes 1572872 | tf_op jit(solution)/shard_map/ppermute | solution.py:66
  70.2 12.0 %collective-permute-start.16 = (bf16[256,1024]{1,0:T(8,128)(2,1)}, bf16[256,1024]{1,0:T(8,128)(2,1)S(1)}, u32[]{:S(2)}, u32[]{:S(2)}) collective-permute-start(bf16[256,1024]{1,0:T(8,128)(2,1)} %collective-permute-done.6.refs_3_), channel_id=1, source_target_pairs={{0,4},{1,5},{2,6},{3,7},{4,0},{5,1},{6,2},{7,3},{8,12},{9,13},{10,... | collective-permute-start | bytes 1572872 | tf_op jit(solution)/shard_map/ppermute | solution.py:66
  76.4 11.4 %collective-permute-start.14 = (bf16[256,1024]{1,0:T(8,128)(2,1)S(1)}, bf16[256,1024]{1,0:T(8,128)(2,1)S(1)}, u32[]{:S(2)}, u32[]{:S(2)}) collective-permute-start(bf16[256,1024]{1,0:T(8,128)(2,1)S(1)} %collective-permute-done.11.refs_1_), channel_id=1, source_target_pairs={{0,2},{1,3},{2,0},{3,1},{4,6},{5,7},{6,4},{7,5},{8,10},{9,11},{10,... | collective-permute-start | bytes 1572872 | tf_op jit(solution)/shard_map/ppermute | solution.py:66
  77.9 11.1 %collective-permute-start.13 = (bf16[256,1024]{1,0:T(8,128)(2,1)S(1)}, bf16[256,1024]{1,0:T(8,128)(2,1)S(1)}, u32[]{:S(2)}, u32[]{:S(2)}) collective-permute-start(bf16[256,1024]{1,0:T(8,128)(2,1)S(1)} %collective-permute-done.8.refs_2_), channel_id=1, source_target_pairs={{0,16},{1,17},{2,18},{3,19},{4,20},{5,21},{6,22},{7,23},{8,24},{9,... | collective-permute-start | bytes 1572872 | tf_op jit(solution)/shard_map/ppermute | solution.py:66
  89.0 5.8 %copy-start.2 = (f32[64,128]{1,0:T(8,128)S(1)}, f32[64,128]{1,0:T(8,128)}, u32[]{:S(2)}) copy-start(f32[64,128]{1,0:T(8,128)} %constant.70.clone.refs_4_.refs_2_) | copy-start | bytes 98308
  89.0 5.8 %copy-start.3 = (f32[64,128]{1,0:T(8,128)S(1)}, f32[64,128]{1,0:T(8,128)}, u32[]{:S(2)}) copy-start(f32[64,128]{1,0:T(8,128)} %constant.71.clone.refs_5_.refs_3_) | copy-start | bytes 98308
  89.0 5.8 %copy-start.4 = (f32[41,128]{1,0:T(8,128)S(1)}, f32[41,128]{1,0:T(8,128)}, u32[]{:S(2)}) copy-start(f32[41,128]{1,0:T(8,128)} %constant.68.clone.refs_2_.refs_0_) | copy-start | bytes 62980
  89.0 5.8 %copy-start.5 = (f32[41,128]{1,0:T(8,128)S(1)}, f32[41,128]{1,0:T(8,128)}, u32[]{:S(2)}) copy-start(f32[41,128]{1,0:T(8,128)} %constant.69.clone.refs_3_.refs_1_) | copy-start | bytes 62980
  89.0 5.8 %copy-start.6 = (f32[160,128]{1,0:T(8,128)S(1)}, f32[160,128]{1,0:T(8,128)}, u32[]{:S(2)}) copy-start(f32[160,128]{1,0:T(8,128)} %constant.72.clone.refs_6_) | copy-start | bytes 245764
  89.1 5.8 %copy-start.7 = (f32[160,128]{1,0:T(8,128)S(1)}, f32[160,128]{1,0:T(8,128)}, u32[]{:S(2)}) copy-start(f32[160,128]{1,0:T(8,128)} %constant.73.clone.refs_7_) | copy-start | bytes 245764
  89.1 5.8 %copy-start.11 = (s32[2]{0:T(128)S(1)}, s32[2]{0:T(128)}, u32[]{:S(2)}) copy-start(s32[2]{0:T(128)} %lengths.3) | copy-start | bytes 28
  89.1 5.8 %copy-start.12 = (s32[8]{0:T(128)S(1)}, s32[8]{0:T(128)}, u32[]{:S(2)}) copy-start(s32[8]{0:T(128)} %owner.3) | copy-start | bytes 100
  91.7 3.1 %collective-permute-start.17 = (f32[320,1024]{1,0:T(8,128)S(1)}, f32[320,1024]{1,0:T(8,128)S(1)}, u32[]{:S(2)}, u32[]{:S(2)}) collective-permute-start(f32[320,1024]{1,0:T(8,128)S(1)} %get-tuple-element.57), channel_id=1, source_target_pairs={{0,1},{1,0},{2,3},{3,2},{4,5},{5,4},{6,7},{7,6},{8,9},{9,8},{10,11... | collective-permute-start | bytes 3932168 | tf_op jit(solution)/shard_map/ppermute | solution.py:66
  95.9 21.0 %copy-start.8 = (bf16[8,4,1024]{2,1,0:T(4,128)(2,1)S(1)}, bf16[8,4,1024]{2,1,0:T(4,128)(2,1)}, u32[]{:S(2)}) copy-start(bf16[8,4,1024]{2,1,0:T(4,128)(2,1)} %dec_query.1) | copy-start | bytes 196612
  95.9 21.0 %copy-start.9 = (bf16[8,4,128]{2,1,0:T(4,128)(2,1)S(1)}, bf16[8,4,128]{2,1,0:T(4,128)(2,1)}, u32[]{:S(2)}) copy-start(bf16[8,4,128]{2,1,0:T(4,128)(2,1)} %dec_key.1) | copy-start | bytes 24580
  95.9 21.0 %copy-start.10 = (bf16[8,4,128]{2,1,0:T(4,128)(2,1)S(1)}, bf16[8,4,128]{2,1,0:T(4,128)(2,1)}, u32[]{:S(2)}) copy-start(bf16[8,4,128]{2,1,0:T(4,128)(2,1)} %dec_value.1) | copy-start | bytes 24580
  118.0 1.3 %collective-permute-start.18 = (f32[32,256]{1,0:T(8,128)S(1)}, f32[32,256]{1,0:T(8,128)S(1)}, u32[]{:S(2)}, u32[]{:S(2)}) collective-permute-start(f32[32,256]{1,0:T(8,128)S(1)} %decode.1.mine), channel_id=1, source_target_pairs={{0,1},{1,0},{2,3},{3,2},{4,5},{5,4},{6,7},{7,6},{8,9},{9,8},{10,11... | collective-permute-start | bytes 98312 | tf_op jit(solution)/shard_map/ppermute | solution.py:66

commit v17 on v14

--- a/solution.py
+++ b/solution.py
@@ -348,6 +348,22 @@
         out[:, j * HEAD_SIZE : (j + 1) * HEAD_SIZE] = rows.astype(jnp.bfloat16)
 
 
+def copied(cache):
+    def kernel(source, out, sem):
+        fetch(source, out, sem.at[0]).wait()
+
+    return pl.pallas_call(
+        kernel,
+        in_specs=[VMEM_REF],
+        out_specs=ANY_REF,
+        out_shape=jax.ShapeDtypeStruct(cache.shape, cache.dtype),
+        scratch_shapes=[pltpu.SemaphoreType.DMA((1,))],
+        compiler_params=SMALL,
+        cost_estimate=cost(1000, 1000),
+        name="copied",
+    )(cache)
+
+
 def decoded(place, lengths, owner, cache, dec_query, dec_key, dec_value, tables):
     mine = pl.pallas_call(
         decode_kernel,
@@ -435,44 +451,44 @@
         near = moved(sent, to_pair)
         middle = moved(sent, to_middle)
         across = moved(sent, to_row)
+        mine, kept = prepared(place, flat, seq // 2)
         rest = half_block(depth - group_id * depth)
-        mine, kept = prepared(place, flat, seq // 2)
-        layers, rows = (near, middle), (across, mine, rest)
-        end_b = moved(after(middle, *layers), to_end)
-        middle_c = moved(after(near, *layers), to_middle)
-        near_y = moved(after(near, *layers, *rows), to_row)
-        across_x = moved(after(across, *layers, *rows), to_group)
-        other = moved(after(kept, *layers, *rows), to_core)
-        layers, rows, before = (end_b, middle_c), (near_y, across_x, other), rows
-        end_c = moved(after(middle_c, *layers, *before), to_end)
-        block_b = jnp.where(is_end, after(end_b, *layers), middle)
-        block_yb = moved(after(block_b, *rows), to_row)
-        block_xb = moved(after(block_b, *rows), to_group)
+        came = (near, middle, across, mine, rest)
+        passed = moved(after(middle, *came), to_end)
+        middle_c = moved(after(near, *came), to_middle)
+        near_y = moved(after(near, *came), to_row)
+        across_x = moved(after(across, *came), to_group)
+        other = moved(after(kept, *came), to_core)
+        came = (passed, middle_c, near_y, across_x, other)
+        far = moved(after(middle_c, *came), to_end)
+        block_b = jnp.where(is_end, after(passed, *came), middle)
+        block_yb = moved(block_b, to_row)
+        block_xb = moved(block_b, to_group)
         pieces = [(HERE, 0, sent), (HERE, 1, rest), (THERE, 0, across)]
         pieces += [(THERE, 1, across_x), (HERE + 1, 0, near), (THERE + 1, 0, near_y)]
-        totals = product(place, after(mine, *rows, block_b), other, pieces, (), 3)
-        layers, rows, before = (end_c,), (block_yb, block_xb, totals[0]), rows
-        near_rest = moved(after(rest, *layers, *before), to_pair)
-        block_c = jnp.where(is_end, after(end_c, *layers), middle_c)
-        block_xc = moved(after(block_c, *rows), to_group)
-        block_yc = moved(after(block_c, *rows), to_row)
+        totals = product(place, after(mine, *came), other, pieces, (), 3)
+        came = (far, block_yb, block_xb, totals[0])
+        near_rest = moved(after(rest, *came), to_pair)
+        block_c = jnp.where(is_end, after(far, *came), middle_c)
+        block_xc = moved(block_c, to_group)
+        block_yc = moved(block_c, to_row)
         pieces = [(HERE + 2, 0, block_b), (HERE + 2, 1, block_xb)]
         pieces += [(THERE + 2, 0, block_yb), (HERE + 3, 0, block_c)]
-        totals = product(place, after(mine, *rows, block_c), other, pieces, totals, 4)
-        layers, rows, before = (near_rest,), (block_xc, block_yc, totals[0]), rows
-        end_a = moved(after(across_x, *layers, *before), to_pair)
-        ends = [moved(after(block_yb, *rows), to_group), moved(after(block_xc, *rows), to_row)]
-        pieces = [(HERE + 1, 1, near_rest), (HERE + 3, 1, block_xc)]
-        pieces += [(THERE + 3, 0, block_yc), (THERE + 1, 1, end_a)]
-        totals = product(place, after(mine, *rows, end_a), other, pieces, totals, 4, 1 << 24)
-        pieces = [(THERE + 2, 1, ends[0]), (THERE + 3, 1, ends[1])]
-        total, given = product(place, after(mine, *ends, *totals), other, pieces, totals, 2)
+        totals = product(place, after(mine, *came), other, pieces, totals, 4)
+        came = (near_rest, block_xc, block_yc, totals[0])
+        end_a = moved(after(across_x, *came), to_pair)
+        ends = [moved(after(block_yb, *came), to_group), moved(after(block_xc, *came), to_row)]
+        pieces = [(HERE + 1, 1, near_rest), (HERE + 3, 1, block_xc), (THERE + 3, 0, block_yc)]
+        totals = product(place, after(mine, *came), other, pieces, totals, 3)
+        came = (end_a, *ends, *totals)
+        pieces = [(THERE + 1, 1, end_a), (THERE + 2, 1, ends[0]), (THERE + 3, 1, ends[1])]
+        total, given = product(place, after(mine, *came), other, pieces, totals, 3)
         outgoing = outgoing_rows(place, lengths, owner, total, moved(given, to_core), tables)
         incoming = lax.all_to_all(outgoing, "seq", split_axis=0, concat_axis=1, tiled=True)
         attended = decoded(
             place, lengths, owner, incoming[0], dec_query, dec_key, dec_value, tables
         )
-        return (incoming, attended)
+        return (copied(incoming[0])[None], attended)
     else:
         cosine, sine_part = rope_table(positions, HEAD_SIZE)
         shape = (count_requests, count_rows, KEY_VALUE_HEADS, HEAD_SIZE)

time: 121 us -> 118 us (0.975)
  starting transfers between devices: 24.2 us -> 21.1 us
  waiting for transfers between devices: 44.6 us -> 45.9 us
    ppermute x19, starting transfers between devices: 24.2 us -> 21.1 us  [moved(): return lax.ppermute(block, ('groups', 'seq'), route)]
    ppermute x19, waiting for transfers between devices: 44.6 us -> 45.9 us  [moved(): return lax.ppermute(block, ('groups', 'seq'), route)]
    unnamed x29 -> x28, local copies, waits for them, and re-layouts: 3.39 us -> 2.56 us
  transfers between devices with their start and end apart: 19 -> 19, of which waited for: 12 -> 12; matrix products, arithmetic and copies ran while one was open for 3% -> 1% of each run, Pallas kernels for 13% -> 13%
where the time goes in v17:
time: 118 us
  waiting for transfers between devices  45.9 us (39%)
  Pallas kernels  22.4 us (19%)
  starting transfers between devices  21.1 us (18%)
  blocking collectives  20.9 us (18%)
  local copies, waits for them, and re-layouts  4.61 us (4%)
  other arithmetic  2.07 us (2%)
    ppermute x19, waiting for transfers between devices, moved(): return lax.ppermute(block, ('groups', 'seq'), route)  45.9 us
    ppermute x19, starting transfers between devices, moved(): return lax.ppermute(block, ('groups', 'seq'), route)  21.1 us
    all_to_all x1, blocking collectives, body(): lax.all_to_all(outgoing, 'seq', split_axis=0, concat_axis=1, tiled=True)  20.9 us
    pallas_call x4, Pallas kernels, product(): pl.pallas_call(functools.partial(product_kernel, plan, group, bool(totals...  14.2 us
    pallas_call x1, Pallas kernels, prepared(): pl.pallas_call(prepare_kernel, grid_spec=pltpu.PrefetchScalarGridSpec(num...  3.9 us
    unnamed x28, local copies, waits for them, and re-layouts  2.56 us
  transfers between devices with their start and end apart: 19, of which 12 were waited for; matrix products, arithmetic and copies ran while one was open for 1% of the time, Pallas kernels for 13%

profile of v17, /device:TPU:0, one launch (start us, length us, event | category | flops | bytes accessed | tf_op | source)
XLA Modules:
  0.0 117.9 jit_solution(17181851754753902110)
XLA Ops:
  0.6 2.0 %constant_dynamic-slice_fusion = (bf16[256,512]{1,0:T(8,128)(2,1)S(1)}, bf16[256,512]{1,0:T(8,128)(2,1)S(1)}, bf16[256,512]{1,0:T(8,128)(2,1)S(1)}, bf16[256,512]{1,0:T(8,128)(2,1)}) fusion(bf16[512,512]{1,0:T(8,128)(2,1)} %param.16, s32[]{:T(128)S(6)} %select_n.52, s32[]{:T(128)S(6)} %select_n.51, bf16[512,512]{1,0:T(8,128)(2,1)} %param.15), kind=kLoop, calls=%fused_computation.4 | loop fusion | bytes 2097160 | tf_op jit(solution)/shard_map/dynamic_slice | solution.py:444
  2.6 0.1 pad_maximum_fusion.refs_0_
  2.7 3.0 %collective-permute-start = (bf16[256,1024]{1,0:T(8,128)(2,1)S(1)}, bf16[256,1024]{1,0:T(8,128)(2,1)}, u32[]{:S(2)}, u32[]{:S(2)}) collective-permute-start(bf16[256,1024]{1,0:T(8,128)(2,1)S(1)} %pad_maximum_fusion.refs_0_), channel_id=1, source_target_pairs={{0,2},{1,3},{2,0},{3,1},{4,6},{5,7},{6,4},{7,5},{8,10},{9,11},{10,... | collective-permute-start | bytes 1572872 | tf_op jit(solution)/shard_map/ppermute | solution.py:66
  5.7 1.6 %collective-permute-start.1 = (bf16[256,1024]{1,0:T(8,128)(2,1)S(1)}, bf16[256,1024]{1,0:T(8,128)(2,1)}, u32[]{:S(2)}, u32[]{:S(2)}) collective-permute-start(bf16[256,1024]{1,0:T(8,128)(2,1)S(1)} %pad_maximum_fusion.refs_0_), channel_id=1, source_target_pairs={{0,4},{1,5},{2,6},{3,7},{4,0},{5,1},{6,2},{7,3},{8,12},{9,13},{10,... | collective-permute-start | bytes 1572872 | tf_op jit(solution)/shard_map/ppermute | solution.py:66
  7.3 1.5 %collective-permute-start.2 = (bf16[256,1024]{1,0:T(8,128)(2,1)S(1)}, bf16[256,1024]{1,0:T(8,128)(2,1)}, u32[]{:S(2)}, u32[]{:S(2)}) collective-permute-start(bf16[256,1024]{1,0:T(8,128)(2,1)S(1)} %pad_maximum_fusion.refs_0_), channel_id=1, source_target_pairs={{4,8},{5,9},{6,10},{7,11},{8,4},{9,5},{10,6},{11,7},{20,24},{21,25... | collective-permute-start | bytes 1572872 | tf_op jit(solution)/shard_map/ppermute | solution.py:66
  8.7 0.1 stack.47.place
  8.8 2.5 %copy-done = bf16[2,160,8192]{2,1,0:T(8,128)(2,1)S(1)} copy-done((bf16[2,160,8192]{2,1,0:T(8,128)(2,1)S(1)}, bf16[2,160,8192]{2,1,0:T(8,128)(2,1)}, u32[]{:S(2)}) %copy-start) | copy-done | bytes 5242904
  11.3 3.9 %normed_halves.1 = (bf16[16,320,256]{2,1,0:T(8,128)(2,1)S(1)}, bf16[16,320,256]{2,1,0:T(8,128)(2,1)}) custom-call(s32[11]{0:T(128)S(1)} %stack.47.place, bf16[320,8192]{1,0:T(8,128)(2,1)S(1)} %bitcast.16), custom_call_target="tpu_custom_call" | custom-call | flops 1000 | bytes 1000 | tf_op jit(solution)/shard_map/normed_halves/pallas_call | solution.py:135
  15.2 0.0 copy-done.13
  15.2 0.9 pad_maximum_fusion.1.refs_1_
  16.1 1.6 %collective-permute-done.refs_2_ = bf16[256,1024]{1,0:T(8,128)(2,1)} collective-permute-done((bf16[256,1024]{1,0:T(8,128)(2,1)S(1)}, bf16[256,1024]{1,0:T(8,128)(2,1)}, u32[]{:S(2)}, u32[]{:S(2)}) %collective-permute-start) | collective-permute-done | bytes 524320 | tf_op jit(solution)/shard_map/ppermute | solution.py:66
  17.7 1.5 %collective-permute-done.1.refs_4_ = bf16[256,1024]{1,0:T(8,128)(2,1)} collective-permute-done((bf16[256,1024]{1,0:T(8,128)(2,1)S(1)}, bf16[256,1024]{1,0:T(8,128)(2,1)}, u32[]{:S(2)}, u32[]{:S(2)}) %collective-permute-start.1) | collective-permute-done | bytes 524320 | tf_op jit(solution)/shard_map/ppermute | solution.py:66
  19.2 0.0 collective-permute-done.2
  19.2 0.0 collective-permute-start.7
  19.2 1.4 %collective-permute-start.4 = (bf16[256,1024]{1,0:T(8,128)(2,1)}, bf16[256,1024]{1,0:T(8,128)(2,1)}, u32[]{:S(2)}, u32[]{:S(2)}) collective-permute-start(bf16[256,1024]{1,0:T(8,128)(2,1)} %collective-permute-done.1.refs_4_), channel_id=1, source_target_pairs={{4,8},{5,9},{6,10},{7,11},{8,4},{9,5},{10,6},{11,7},{20,24},{21,25... | collective-permute-start | bytes 1572872 | tf_op jit(solution)/shard_map/ppermute | solution.py:66
  20.6 0.4 collective-permute-start.6
  21.0 1.3 %collective-permute-start.5 = (bf16[256,1024]{1,0:T(8,128)(2,1)}, bf16[256,1024]{1,0:T(8,128)(2,1)}, u32[]{:S(2)}, u32[]{:S(2)}) collective-permute-start(bf16[256,1024]{1,0:T(8,128)(2,1)} %collective-permute-done.2), channel_id=1, source_target_pairs={{4,0},{5,1},{6,2},{7,3},{8,12},{9,13},{10,14},{11,15},{20,16},{21,... | collective-permute-start | bytes 1572872 | tf_op jit(solution)/shard_map/ppermute | solution.py:66
  22.3 1.7 %collective-permute-start.3 = (bf16[256,1024]{1,0:T(8,128)(2,1)}, bf16[256,1024]{1,0:T(8,128)(2,1)}, u32[]{:S(2)}, u32[]{:S(2)}) collective-permute-start(bf16[256,1024]{1,0:T(8,128)(2,1)} %collective-permute-done.refs_2_), channel_id=1, source_target_pairs={{0,16},{1,17},{2,18},{3,19},{4,20},{5,21},{6,22},{7,23},{8,24},{9,... | collective-permute-start | bytes 1572872 | tf_op jit(solution)/shard_map/ppermute | solution.py:66
  24.0 17.6 %collective-permute-done.5 = bf16[256,1024]{1,0:T(8,128)(2,1)} collective-permute-done((bf16[256,1024]{1,0:T(8,128)(2,1)}, bf16[256,1024]{1,0:T(8,128)(2,1)}, u32[]{:S(2)}, u32[]{:S(2)}) %collective-permute-start.5) | collective-permute-done | bytes 524320 | tf_op jit(solution)/shard_map/ppermute | solution.py:66
  41.6 0.0 collective-permute-done.4
  41.6 0.0 collective-permute-done.6.refs_5_
  41.6 0.0 collective-permute-done.3.refs_3_
  41.6 0.0 collective-permute-done.7.other
  41.6 1.1 broadcast_select_fusion.1.refs_0_
  42.7 1.6 %collective-permute-start.10 = (bf16[256,1024]{1,0:T(8,128)(2,1)S(1)}, bf16[256,1024]{1,0:T(8,128)(2,1)S(1)}, u32[]{:S(2)}, u32[]{:S(2)}) collective-permute-start(bf16[256,1024]{1,0:T(8,128)(2,1)S(1)} %broadcast_select_fusion.1.refs_0_), channel_id=1, source_target_pairs={{0,16},{1,17},{2,18},{3,19},{4,20},{5,21},{6,22},{7,23},{8,24},{9,... | collective-permute-start | bytes 1572872 | tf_op jit(solution)/shard_map/ppermute | solution.py:66
  44.3 1.5 %collective-permute-start.9 = (bf16[256,1024]{1,0:T(8,128)(2,1)S(1)}, bf16[256,1024]{1,0:T(8,128)(2,1)S(1)}, u32[]{:S(2)}, u32[]{:S(2)}) collective-permute-start(bf16[256,1024]{1,0:T(8,128)(2,1)S(1)} %broadcast_select_fusion.1.refs_0_), channel_id=1, source_target_pairs={{0,2},{1,3},{2,0},{3,1},{4,6},{5,7},{6,4},{7,5},{8,10},{9,11},{10,... | collective-permute-start | bytes 1572872 | tf_op jit(solution)/shard_map/ppermute | solution.py:66
  45.8 1.3 %collective-permute-start.8 = (bf16[256,1024]{1,0:T(8,128)(2,1)}, bf16[256,1024]{1,0:T(8,128)(2,1)S(1)}, u32[]{:S(2)}, u32[]{:S(2)}) collective-permute-start(bf16[256,1024]{1,0:T(8,128)(2,1)} %collective-permute-done.4), channel_id=1, source_target_pairs={{4,0},{5,1},{6,2},{7,3},{8,12},{9,13},{10,14},{11,15},{20,16},{21,... | collective-permute-start | bytes 1572872 | tf_op jit(solution)/shard_map/ppermute | solution.py:66
  47.1 4.4 %add_product.4 = (f32[320,1024]{1,0:T(8,128)S(1)}, f32[320,1024]{1,0:T(8,128)S(1)}) custom-call(s32[11]{0:T(128)S(1)} %stack.47.place, bf16[16,320,256]{2,1,0:T(8,128)(2,1)S(1)} %get-tuple-element.49.mine, bf16[16,320,256]{2,1,0:T(8,128)(2,1)} %collective-permute-done.7.other, bf16[256,1024]{1,0:T(8,128)(2,1)S(1)} %pad_maximum_fusion.refs_0_, ...), custom_call_target="tpu_custom_call" | custom-call | flops 1000 | bytes 1000 | tf_op jit(solution)/shard_map/add_product/pallas_call | solution.py:202
  51.6 4.5 %collective-permute-done.10.refs_1_ = bf16[256,1024]{1,0:T(8,128)(2,1)S(1)} collective-permute-done((bf16[256,1024]{1,0:T(8,128)(2,1)S(1)}, bf16[256,1024]{1,0:T(8,128)(2,1)S(1)}, u32[]{:S(2)}, u32[]{:S(2)}) %collective-permute-start.10) | collective-permute-done | bytes 524320 | tf_op jit(solution)/shard_map/ppermute | solution.py:66
  56.1 1.2 %collective-permute-done.9.refs_2_ = bf16[256,1024]{1,0:T(8,128)(2,1)S(1)} collective-permute-done((bf16[256,1024]{1,0:T(8,128)(2,1)S(1)}, bf16[256,1024]{1,0:T(8,128)(2,1)S(1)}, u32[]{:S(2)}, u32[]{:S(2)}) %collective-permute-start.9) | collective-permute-done | bytes 524320 | tf_op jit(solution)/shard_map/ppermute | solution.py:66
  57.3 3.3 %collective-permute-done.8 = bf16[256,1024]{1,0:T(8,128)(2,1)S(1)} collective-permute-done((bf16[256,1024]{1,0:T(8,128)(2,1)}, bf16[256,1024]{1,0:T(8,128)(2,1)S(1)}, u32[]{:S(2)}, u32[]{:S(2)}) %collective-permute-start.8) | collective-permute-done | bytes 524320 | tf_op jit(solution)/shard_map/ppermute | solution.py:66
  60.6 0.1 broadcast_select_fusion.refs_3_
  60.7 0.6 collective-permute-start.12
  61.3 0.5 collective-permute-start.13
  61.8 1.0 collective-permute-start.11
  62.7 3.6 %add_product.5 = (f32[320,1024]{1,0:T(8,128)S(1)}, f32[320,1024]{1,0:T(8,128)S(1)}) custom-call(s32[11]{0:T(128)S(1)} %stack.47.place, bf16[16,320,256]{2,1,0:T(8,128)(2,1)S(1)} %get-tuple-element.49.mine, bf16[16,320,256]{2,1,0:T(8,128)(2,1)} %collective-permute-done.7.other, bf16[256,1024]{1,0:T(8,128)(2,1)S(1)} %broadcast_select_fusion.1.refs_0_, ...), custom_call_target="tpu_custom_call" | custom-call | flops 1000 | bytes 1000 | tf_op jit(solution)/shard_map/add_product/pallas_call | solution.py:202
  66.4 6.1 %collective-permute-done.12.refs_1_ = bf16[256,1024]{1,0:T(8,128)(2,1)S(1)} collective-permute-done((bf16[256,1024]{1,0:T(8,128)(2,1)S(1)}, bf16[256,1024]{1,0:T(8,128)(2,1)S(1)}, u32[]{:S(2)}, u32[]{:S(2)}) %collective-permute-start.12) | collective-permute-done | bytes 524320 | tf_op jit(solution)/shard_map/ppermute | solution.py:66
  72.5 0.8 collective-permute-done.13.refs_2_
  73.3 0.0 collective-permute-done.11.refs_0_
  73.3 1.2 collective-permute-start.16
  74.5 1.6 %collective-permute-start.15 = (bf16[256,1024]{1,0:T(8,128)(2,1)S(1)}, bf16[256,1024]{1,0:T(8,128)(2,1)S(1)}, u32[]{:S(2)}, u32[]{:S(2)}) collective-permute-start(bf16[256,1024]{1,0:T(8,128)(2,1)S(1)} %collective-permute-done.9.refs_2_), channel_id=1, source_target_pairs={{0,16},{1,17},{2,18},{3,19},{4,20},{5,21},{6,22},{7,23},{8,24},{9,... | collective-permute-start | bytes 1572872 | tf_op jit(solution)/shard_map/ppermute | solution.py:66
  76.1 0.6 collective-permute-start.14
  76.7 3.1 %add_product.6 = (f32[320,1024]{1,0:T(8,128)S(1)}, f32[320,1024]{1,0:T(8,128)S(1)}) custom-call(s32[11]{0:T(128)S(1)} %stack.47.place, bf16[16,320,256]{2,1,0:T(8,128)(2,1)S(1)} %get-tuple-element.49.mine, bf16[16,320,256]{2,1,0:T(8,128)(2,1)} %collective-permute-done.7.other, bf16[256,1024]{1,0:T(8,128)(2,1)S(1)} %collective-permute-done.11.refs_0_, ...), custom_call_target="tpu_custom_call" | custom-call | flops 1000 | bytes 1000 | tf_op jit(solution)/shard_map/add_product/pallas_call | solution.py:202
  79.8 4.2 %collective-permute-done.16.refs_2_ = bf16[256,1024]{1,0:T(8,128)(2,1)S(1)} collective-permute-done((bf16[256,1024]{1,0:T(8,128)(2,1)S(1)}, bf16[256,1024]{1,0:T(8,128)(2,1)S(1)}, u32[]{:S(2)}, u32[]{:S(2)}) %collective-permute-start.16) | collective-permute-done | bytes 524320 | tf_op jit(solution)/shard_map/ppermute | solution.py:66
  84.0 0.5 collective-permute-done.15.refs_1_
  84.5 1.4 %collective-permute-done.14.refs_0_ = bf16[256,1024]{1,0:T(8,128)(2,1)S(1)} collective-permute-done((bf16[256,1024]{1,0:T(8,128)(2,1)}, bf16[256,1024]{1,0:T(8,128)(2,1)S(1)}, u32[]{:S(2)}, u32[]{:S(2)}) %collective-permute-start.14) | collective-permute-done | bytes 524320 | tf_op jit(solution)/shard_map/ppermute | solution.py:66
  85.9 0.0 copy-start.6
  85.9 0.0 copy-start.7
  85.9 0.0 copy-start.11
  85.9 0.0 copy-start.12
  86.0 3.1 %add_product.7 = (f32[320,1024]{1,0:T(8,128)S(1)}, f32[320,1024]{1,0:T(8,128)S(1)}) custom-call(s32[11]{0:T(128)S(1)} %stack.47.place, bf16[16,320,256]{2,1,0:T(8,128)(2,1)S(1)} %get-tuple-element.49.mine, bf16[16,320,256]{2,1,0:T(8,128)(2,1)} %collective-permute-done.7.other, bf16[256,1024]{1,0:T(8,128)(2,1)S(1)} %collective-permute-done.14.refs_0_, ...), custom_call_target="tpu_custom_call" | custom-call | flops 1000 | bytes 1000 | tf_op jit(solution)/shard_map/add_product/pallas_call | solution.py:202
  89.1 0.1 collective-permute-start.17
  89.1 3.0 %collective-permute-done.17.refs_1_ = f32[320,1024]{1,0:T(8,128)S(1)} collective-permute-done((f32[320,1024]{1,0:T(8,128)S(1)}, f32[320,1024]{1,0:T(8,128)S(1)}, u32[]{:S(2)}, u32[]{:S(2)}) %collective-permute-start.17) | collective-permute-done | bytes 1310752 | tf_op jit(solution)/shard_map/ppermute | solution.py:66
  92.2 0.0 copy-done.2
  92.2 1.0 cache_rows.1
  93.3 0.0 copy-start.8
  93.3 0.0 copy-start.9
  93.3 0.0 copy-start.10
  93.3 20.9 %all_to_all.4 = bf16[16,80,256]{2,1,0:T(8,128)(2,1)S(1)} all-to-all(bf16[16,80,256]{2,1,0:T(8,128)(2,1)S(1)} %cache_rows.1), channel_id=1, replica_groups=mesh['groups'=2,'seq'=16] {'seq'}, dimensions={0} | all-to-all | bytes 1310720 | tf_op jit(solution)/shard_map/all_to_all | solution.py:487
  114.3 1.1 decode.1.mine
  115.4 0.4 collective-permute-start.18
  115.7 0.8 copied.1
  116.6 0.0 collective-permute-done.18.theirs
  116.6 1.3 %joined.1 = bf16[4,512]{1,0:T(4,128)(2,1)} custom-call(s32[11]{0:T(128)S(1)} %stack.47.place, f32[32,256]{1,0:T(8,128)S(1)} %decode.1.mine, f32[32,256]{1,0:T(8,128)S(1)} %collective-permute-done.18.theirs), custom_call_target="tpu_custom_call" | custom-call | flops 1000 | bytes 1000 | tf_op jit(solution)/shard_map/joined/pallas_call | solution.py:377
  (18 shorter events, 0.0 us)
Async XLA Ops:
  2.7 15.1 %collective-permute-start = (bf16[256,1024]{1,0:T(8,128)(2,1)S(1)}, bf16[256,1024]{1,0:T(8,128)(2,1)}, u32[]{:S(2)}, u32[]{:S(2)}) collective-permute-start(bf16[256,1024]{1,0:T(8,128)(2,1)S(1)} %pad_maximum_fusion.refs_0_), channel_id=1, source_target_pairs={{0,2},{1,3},{2,0},{3,1},{4,6},{5,7},{6,4},{7,5},{8,10},{9,11},{10,... | collective-permute-start | bytes 1572872 | tf_op jit(solution)/shard_map/ppermute | solution.py:66
  5.7 13.5 %collective-permute-start.1 = (bf16[256,1024]{1,0:T(8,128)(2,1)S(1)}, bf16[256,1024]{1,0:T(8,128)(2,1)}, u32[]{:S(2)}, u32[]{:S(2)}) collective-permute-start(bf16[256,1024]{1,0:T(8,128)(2,1)S(1)} %pad_maximum_fusion.refs_0_), channel_id=1, source_target_pairs={{0,4},{1,5},{2,6},{3,7},{4,0},{5,1},{6,2},{7,3},{8,12},{9,13},{10,... | collective-permute-start | bytes 1572872 | tf_op jit(solution)/shard_map/ppermute | solution.py:66
  7.3 11.9 %collective-permute-start.2 = (bf16[256,1024]{1,0:T(8,128)(2,1)S(1)}, bf16[256,1024]{1,0:T(8,128)(2,1)}, u32[]{:S(2)}, u32[]{:S(2)}) collective-permute-start(bf16[256,1024]{1,0:T(8,128)(2,1)S(1)} %pad_maximum_fusion.refs_0_), channel_id=1, source_target_pairs={{4,8},{5,9},{6,10},{7,11},{8,4},{9,5},{10,6},{11,7},{20,24},{21,25... | collective-permute-start | bytes 1572872 | tf_op jit(solution)/shard_map/ppermute | solution.py:66
  8.8 2.5 %copy-start = (bf16[2,160,8192]{2,1,0:T(8,128)(2,1)S(1)}, bf16[2,160,8192]{2,1,0:T(8,128)(2,1)}, u32[]{:S(2)}) copy-start(bf16[2,160,8192]{2,1,0:T(8,128)(2,1)} %param.14) | copy-start | bytes 15728644
  11.3 3.9 %copy-start.13 = (bf16[256,512]{1,0:T(8,128)(2,1)S(1)}, bf16[256,512]{1,0:T(8,128)(2,1)}, u32[]{:S(2)}) copy-start(bf16[256,512]{1,0:T(8,128)(2,1)} %get-tuple-element.57) | copy-start | bytes 786436
  19.2 22.4 %collective-permute-start.7 = (bf16[16,320,256]{2,1,0:T(8,128)(2,1)}, bf16[16,320,256]{2,1,0:T(8,128)(2,1)}, u32[]{:S(2)}, u32[]{:S(2)}) collective-permute-start(bf16[16,320,256]{2,1,0:T(8,128)(2,1)} %get-tuple-element.32), channel_id=1, source_target_pairs={{0,1},{1,0},{2,3},{3,2},{4,5},{5,4},{6,7},{7,6},{8,9},{9,8},{10,11... | collective-permute-start | bytes 7864328 | tf_op jit(solution)/shard_map/ppermute | solution.py:66
  19.2 22.4 %collective-permute-start.4 = (bf16[256,1024]{1,0:T(8,128)(2,1)}, bf16[256,1024]{1,0:T(8,128)(2,1)}, u32[]{:S(2)}, u32[]{:S(2)}) collective-permute-start(bf16[256,1024]{1,0:T(8,128)(2,1)} %collective-permute-done.1.refs_4_), channel_id=1, source_target_pairs={{4,8},{5,9},{6,10},{7,11},{8,4},{9,5},{10,6},{11,7},{20,24},{21,25... | collective-permute-start | bytes 1572872 | tf_op jit(solution)/shard_map/ppermute | solution.py:66
  20.6 21.0 %collective-permute-start.6 = (bf16[256,1024]{1,0:T(8,128)(2,1)}, bf16[256,1024]{1,0:T(8,128)(2,1)}, u32[]{:S(2)}, u32[]{:S(2)}) collective-permute-start(bf16[256,1024]{1,0:T(8,128)(2,1)} %collective-permute-done.1.refs_4_), channel_id=1, source_target_pairs={{0,2},{1,3},{2,0},{3,1},{4,6},{5,7},{6,4},{7,5},{8,10},{9,11},{10,... | collective-permute-start | bytes 1572872 | tf_op jit(solution)/shard_map/ppermute | solution.py:66
  21.0 20.6 %collective-permute-start.5 = (bf16[256,1024]{1,0:T(8,128)(2,1)}, bf16[256,1024]{1,0:T(8,128)(2,1)}, u32[]{:S(2)}, u32[]{:S(2)}) collective-permute-start(bf16[256,1024]{1,0:T(8,128)(2,1)} %collective-permute-done.2), channel_id=1, source_target_pairs={{4,0},{5,1},{6,2},{7,3},{8,12},{9,13},{10,14},{11,15},{20,16},{21,... | collective-permute-start | bytes 1572872 | tf_op jit(solution)/shard_map/ppermute | solution.py:66
  22.3 19.3 %collective-permute-start.3 = (bf16[256,1024]{1,0:T(8,128)(2,1)}, bf16[256,1024]{1,0:T(8,128)(2,1)}, u32[]{:S(2)}, u32[]{:S(2)}) collective-permute-start(bf16[256,1024]{1,0:T(8,128)(2,1)} %collective-permute-done.refs_2_), channel_id=1, source_target_pairs={{0,16},{1,17},{2,18},{3,19},{4,20},{5,21},{6,22},{7,23},{8,24},{9,... | collective-permute-start | bytes 1572872 | tf_op jit(solution)/shard_map/ppermute | solution.py:66
  24.0 23.1 %copy-start.1 = (bf16[256,1024]{1,0:T(8,128)(2,1)S(1)}, bf16[256,1024]{1,0:T(8,128)(2,1)}, u32[]{:S(2)}) copy-start(bf16[256,1024]{1,0:T(8,128)(2,1)} %pad_maximum_fusion.1.refs_1_) | copy-start | bytes 1572868
  42.7 13.3 %collective-permute-start.10 = (bf16[256,1024]{1,0:T(8,128)(2,1)S(1)}, bf16[256,1024]{1,0:T(8,128)(2,1)S(1)}, u32[]{:S(2)}, u32[]{:S(2)}) collective-permute-start(bf16[256,1024]{1,0:T(8,128)(2,1)S(1)} %broadcast_select_fusion.1.refs_0_), channel_id=1, source_target_pairs={{0,16},{1,17},{2,18},{3,19},{4,20},{5,21},{6,22},{7,23},{8,24},{9,... | collective-permute-start | bytes 1572872 | tf_op jit(solution)/shard_map/ppermute | solution.py:66
  44.3 13.0 %collective-permute-start.9 = (bf16[256,1024]{1,0:T(8,128)(2,1)S(1)}, bf16[256,1024]{1,0:T(8,128)(2,1)S(1)}, u32[]{:S(2)}, u32[]{:S(2)}) collective-permute-start(bf16[256,1024]{1,0:T(8,128)(2,1)S(1)} %broadcast_select_fusion.1.refs_0_), channel_id=1, source_target_pairs={{0,2},{1,3},{2,0},{3,1},{4,6},{5,7},{6,4},{7,5},{8,10},{9,11},{10,... | collective-permute-start | bytes 1572872 | tf_op jit(solution)/shard_map/ppermute | solution.py:66
  45.8 14.8 %collective-permute-start.8 = (bf16[256,1024]{1,0:T(8,128)(2,1)}, bf16[256,1024]{1,0:T(8,128)(2,1)S(1)}, u32[]{:S(2)}, u32[]{:S(2)}) collective-permute-start(bf16[256,1024]{1,0:T(8,128)(2,1)} %collective-permute-done.4), channel_id=1, source_target_pairs={{4,0},{5,1},{6,2},{7,3},{8,12},{9,13},{10,14},{11,15},{20,16},{21,... | collective-permute-start | bytes 1572872 | tf_op jit(solution)/shard_map/ppermute | solution.py:66
  60.7 11.8 %collective-permute-start.12 = (bf16[256,1024]{1,0:T(8,128)(2,1)S(1)}, bf16[256,1024]{1,0:T(8,128)(2,1)S(1)}, u32[]{:S(2)}, u32[]{:S(2)}) collective-permute-start(bf16[256,1024]{1,0:T(8,128)(2,1)S(1)} %broadcast_select_fusion.refs_3_), channel_id=1, source_target_pairs={{0,16},{1,17},{2,18},{3,19},{4,20},{5,21},{6,22},{7,23},{8,24},{9,... | collective-permute-start | bytes 1572872 | tf_op jit(solution)/shard_map/ppermute | solution.py:66
  61.3 12.1 %collective-permute-start.13 = (bf16[256,1024]{1,0:T(8,128)(2,1)S(1)}, bf16[256,1024]{1,0:T(8,128)(2,1)S(1)}, u32[]{:S(2)}, u32[]{:S(2)}) collective-permute-start(bf16[256,1024]{1,0:T(8,128)(2,1)S(1)} %broadcast_select_fusion.refs_3_), channel_id=1, source_target_pairs={{0,2},{1,3},{2,0},{3,1},{4,6},{5,7},{6,4},{7,5},{8,10},{9,11},{10,... | collective-permute-start | bytes 1572872 | tf_op jit(solution)/shard_map/ppermute | solution.py:66
  61.8 11.6 %collective-permute-start.11 = (bf16[256,1024]{1,0:T(8,128)(2,1)S(1)}, bf16[256,1024]{1,0:T(8,128)(2,1)S(1)}, u32[]{:S(2)}, u32[]{:S(2)}) collective-permute-start(bf16[256,1024]{1,0:T(8,128)(2,1)S(1)} %copy-done.1), channel_id=1, source_target_pairs={{0,4},{1,5},{2,6},{3,7},{4,0},{5,1},{6,2},{7,3},{8,12},{9,13},{10,... | collective-permute-start | bytes 1572872 | tf_op jit(solution)/shard_map/ppermute | solution.py:66
  73.3 10.7 %collective-permute-start.16 = (bf16[256,1024]{1,0:T(8,128)(2,1)S(1)}, bf16[256,1024]{1,0:T(8,128)(2,1)S(1)}, u32[]{:S(2)}, u32[]{:S(2)}) collective-permute-start(bf16[256,1024]{1,0:T(8,128)(2,1)S(1)} %collective-permute-done.12.refs_1_), channel_id=1, source_target_pairs={{0,2},{1,3},{2,0},{3,1},{4,6},{5,7},{6,4},{7,5},{8,10},{9,11},{10,... | collective-permute-start | bytes 1572872 | tf_op jit(solution)/shard_map/ppermute | solution.py:66
  74.5 10.0 %collective-permute-start.15 = (bf16[256,1024]{1,0:T(8,128)(2,1)S(1)}, bf16[256,1024]{1,0:T(8,128)(2,1)S(1)}, u32[]{:S(2)}, u32[]{:S(2)}) collective-permute-start(bf16[256,1024]{1,0:T(8,128)(2,1)S(1)} %collective-permute-done.9.refs_2_), channel_id=1, source_target_pairs={{0,16},{1,17},{2,18},{3,19},{4,20},{5,21},{6,22},{7,23},{8,24},{9,... | collective-permute-start | bytes 1572872 | tf_op jit(solution)/shard_map/ppermute | solution.py:66
  76.1 9.8 %collective-permute-start.14 = (bf16[256,1024]{1,0:T(8,128)(2,1)}, bf16[256,1024]{1,0:T(8,128)(2,1)S(1)}, u32[]{:S(2)}, u32[]{:S(2)}) collective-permute-start(bf16[256,1024]{1,0:T(8,128)(2,1)} %collective-permute-done.3.refs_3_), channel_id=1, source_target_pairs={{0,4},{1,5},{2,6},{3,7},{4,0},{5,1},{6,2},{7,3},{8,12},{9,13},{10,... | collective-permute-start | bytes 1572872 | tf_op jit(solution)/shard_map/ppermute | solution.py:66
  85.9 6.3 %copy-start.2 = (f32[64,128]{1,0:T(8,128)S(1)}, f32[64,128]{1,0:T(8,128)}, u32[]{:S(2)}) copy-start(f32[64,128]{1,0:T(8,128)} %constant.70.clone.refs_4_.refs_2_) | copy-start | bytes 98308
  85.9 6.3 %copy-start.3 = (f32[64,128]{1,0:T(8,128)S(1)}, f32[64,128]{1,0:T(8,128)}, u32[]{:S(2)}) copy-start(f32[64,128]{1,0:T(8,128)} %constant.71.clone.refs_5_.refs_3_) | copy-start | bytes 98308
  85.9 6.3 %copy-start.4 = (f32[41,128]{1,0:T(8,128)S(1)}, f32[41,128]{1,0:T(8,128)}, u32[]{:S(2)}) copy-start(f32[41,128]{1,0:T(8,128)} %constant.68.clone.refs_2_.refs_0_) | copy-start | bytes 62980
  85.9 6.3 %copy-start.5 = (f32[41,128]{1,0:T(8,128)S(1)}, f32[41,128]{1,0:T(8,128)}, u32[]{:S(2)}) copy-start(f32[41,128]{1,0:T(8,128)} %constant.69.clone.refs_3_.refs_1_) | copy-start | bytes 62980
  85.9 6.3 %copy-start.6 = (f32[160,128]{1,0:T(8,128)S(1)}, f32[160,128]{1,0:T(8,128)}, u32[]{:S(2)}) copy-start(f32[160,128]{1,0:T(8,128)} %constant.72.clone.refs_6_) | copy-start | bytes 245764
  85.9 6.3 %copy-start.7 = (f32[160,128]{1,0:T(8,128)S(1)}, f32[160,128]{1,0:T(8,128)}, u32[]{:S(2)}) copy-start(f32[160,128]{1,0:T(8,128)} %constant.73.clone.refs_7_) | copy-start | bytes 245764
  85.9 6.3 %copy-start.11 = (s32[2]{0:T(128)S(1)}, s32[2]{0:T(128)}, u32[]{:S(2)}) copy-start(s32[2]{0:T(128)} %lengths.3) | copy-start | bytes 28
  85.9 6.3 %copy-start.12 = (s32[8]{0:T(128)S(1)}, s32[8]{0:T(128)}, u32[]{:S(2)}) copy-start(s32[8]{0:T(128)} %owner.3) | copy-start | bytes 100
  89.1 3.1 %collective-permute-start.17 = (f32[320,1024]{1,0:T(8,128)S(1)}, f32[320,1024]{1,0:T(8,128)S(1)}, u32[]{:S(2)}, u32[]{:S(2)}) collective-permute-start(f32[320,1024]{1,0:T(8,128)S(1)} %get-tuple-element.51), channel_id=1, source_target_pairs={{0,1},{1,0},{2,3},{3,2},{4,5},{5,4},{6,7},{7,6},{8,9},{9,8},{10,11... | collective-permute-start | bytes 3932168 | tf_op jit(solution)/shard_map/ppermute | solution.py:66
  93.3 21.0 %copy-start.8 = (bf16[8,4,1024]{2,1,0:T(4,128)(2,1)S(1)}, bf16[8,4,1024]{2,1,0:T(4,128)(2,1)}, u32[]{:S(2)}) copy-start(bf16[8,4,1024]{2,1,0:T(4,128)(2,1)} %dec_query.1) | copy-start | bytes 196612
  93.3 21.0 %copy-start.9 = (bf16[8,4,128]{2,1,0:T(4,128)(2,1)S(1)}, bf16[8,4,128]{2,1,0:T(4,128)(2,1)}, u32[]{:S(2)}) copy-start(bf16[8,4,128]{2,1,0:T(4,128)(2,1)} %dec_key.1) | copy-start | bytes 24580
  93.3 21.0 %copy-start.10 = (bf16[8,4,128]{2,1,0:T(4,128)(2,1)S(1)}, bf16[8,4,128]{2,1,0:T(4,128)(2,1)}, u32[]{:S(2)}) copy-start(bf16[8,4,128]{2,1,0:T(4,128)(2,1)} %dec_value.1) | copy-start | bytes 24580
  115.4 1.3 %collective-permute-start.18 = (f32[32,256]{1,0:T(8,128)S(1)}, f32[32,256]{1,0:T(8,128)S(1)}, u32[]{:S(2)}, u32[]{:S(2)}) collective-permute-start(f32[32,256]{1,0:T(8,128)S(1)} %decode.1.mine), channel_id=1, source_target_pairs={{0,1},{1,0},{2,3},{3,2},{4,5},{5,4},{6,7},{7,6},{8,9},{9,8},{10,11... | collective-permute-start | bytes 98312 | tf_op jit(solution)/shard_map/ppermute | solution.py:66

commit v18 on v17

--- a/solution.py
+++ b/solution.py
@@ -94,6 +94,7 @@
 SMEM_REF = pl.BlockSpec(memory_space=pltpu.SMEM)
 ANY_REF = pl.BlockSpec(memory_space=pl.ANY)
 PARAMS = pltpu.CompilerParams(vmem_limit_bytes=20 << 20)
+LARGE = pltpu.CompilerParams(vmem_limit_bytes=58 << 20)
 SMALL = pltpu.CompilerParams(vmem_limit_bytes=16 << 20)
 
 
@@ -107,44 +108,45 @@
     return copy
 
 
-def prepare_kernel(place, rows_in, mine, kept):
-    depth = mine.shape[2]
-    rows, width = rows_in.shape
-    square = jnp.zeros((rows, depth), jnp.float32)
-    for first in range(0, width, depth):
-        part = rows_in[:, first : first + depth].astype(jnp.float32)
-        square += part * part
-    scale = lax.rsqrt(jnp.sum(square, -1, keepdims=True) / width + 1e-05)
-    for core in range(2):
-
-        @pl.when(place[1] == core)
-        def _():
-            for first in range(0, width, depth):
-                j, c, h = first // (4 * depth), first // (2 * depth) % 2, first // depth % 2
-                target = mine if c == core else kept
-                part = rows_in[:, first : first + depth].astype(jnp.float32)
-                target[2 * j + h] = (part * scale).astype(jnp.bfloat16)
-
-
-def prepared(place, flat, blocks):
-    rows, width = flat.shape
+def prepare_kernel(place, *refs):
+    depth = refs[2].shape[2]
+    for rows_in, target in zip(refs[:2], refs[2:]):
+        rows, width = rows_in.shape
+        square = jnp.zeros((rows, depth), jnp.float32)
+        for first in range(0, width, depth):
+            part = rows_in[:, first : first + depth].astype(jnp.float32)
+            square += part * part
+        scale = lax.rsqrt(jnp.sum(square, -1, keepdims=True) / width + 1e-05)
+        for core in range(2):
+
+            @pl.when(place[1] == core)
+            def _():
+                for k in range(width // (2 * depth)):
+                    first = (k // 2 * 4 + core * 2 + k % 2) * depth
+                    part = rows_in[:, first : first + depth].astype(jnp.float32)
+                    target[k] = (part * scale).astype(jnp.bfloat16)
+
+
+def prepared(place, mine, other, blocks):
+    rows, width = mine.shape
     depth = width // (4 * blocks)
     tile = 80 if rows % 80 == 0 else rows
     out = jax.ShapeDtypeStruct((2 * blocks, rows, depth), jnp.bfloat16)
-    spec = pl.BlockSpec((2 * blocks, tile, depth), lambda i, place: (0, i, 0))
+    taken = pl.BlockSpec((tile, width), lambda i, place: (i, 0))
+    given = pl.BlockSpec((2 * blocks, tile, depth), lambda i, place: (0, i, 0))
     return pl.pallas_call(
         prepare_kernel,
         grid_spec=pltpu.PrefetchScalarGridSpec(
             num_scalar_prefetch=1,
             grid=(rows // tile,),
-            in_specs=[pl.BlockSpec((tile, width), lambda i, place: (i, 0))],
-            out_specs=[spec, spec],
+            in_specs=[taken, taken],
+            out_specs=[given, given],
         ),
         out_shape=[out, out],
-        compiler_params=PARAMS,
+        compiler_params=LARGE,
         cost_estimate=cost(1000, 1000),
         name="normed_halves",
-    )(place, flat)
+    )(place, mine, other)
 
 
 def after(value, *events):
@@ -446,20 +448,20 @@
             ]
             return jnp.concatenate(halves, 1)
 
+        raw = moved(flat, to_core)
         sent = half_block(group_id * depth)
         tables = turn_tables(count_rows * seq + STEPS, count_rows)
         near = moved(sent, to_pair)
         middle = moved(sent, to_middle)
         across = moved(sent, to_row)
-        mine, kept = prepared(place, flat, seq // 2)
         rest = half_block(depth - group_id * depth)
-        came = (near, middle, across, mine, rest)
+        came = (near, middle, across, raw, rest)
         passed = moved(after(middle, *came), to_end)
         middle_c = moved(after(near, *came), to_middle)
         near_y = moved(after(near, *came), to_row)
         across_x = moved(after(across, *came), to_group)
-        other = moved(after(kept, *came), to_core)
-        came = (passed, middle_c, near_y, across_x, other)
+        mine, other = prepared(place, after(flat, *came), raw, seq // 2)
+        came = (passed, middle_c, near_y, across_x, mine)
         far = moved(after(middle_c, *came), to_end)
         block_b = jnp.where(is_end, after(passed, *came), middle)
         block_yb = moved(block_b, to_row)

time: 118 us -> 115 us (0.975)
  waiting for transfers between devices: 45.9 us -> 34.8 us
  starting transfers between devices: 21.1 us -> 26.5 us
  Pallas kernels: 22.4 us -> 24 us
    ppermute x19, waiting for transfers between devices: 45.9 us -> 34.8 us  [moved(): return lax.ppermute(block, ('groups', 'seq'), route)]
    ppermute x19, starting transfers between devices: 21.1 us -> 26.5 us  [moved(): return lax.ppermute(block, ('groups', 'seq'), route)]
    pallas_call x1, Pallas kernels: 3.9 us -> 8.51 us  [prepared(): pl.pallas_call(prepare_kernel, grid_spec=pltpu.PrefetchScalarGridSpec(num...]
    pallas_call x4, Pallas kernels: 14.2 us -> 11.2 us  [product(): pl.pallas_call(functools.partial(product_kernel, plan, group, bool(totals...]
  transfers between devices with their start and end apart: 19 -> 19, of which waited for: 12 -> 14; matrix products, arithmetic and copies ran while one was open for 1% -> 3% of each run, Pallas kernels for 13% -> 16%
where the time goes in v18:
time: 115 us
  waiting for transfers between devices  34.8 us (30%)
  starting transfers between devices  26.5 us (23%)
  Pallas kernels  24 us (21%)
  blocking collectives  21.6 us (19%)
  local copies, waits for them, and re-layouts  5.48 us (5%)
  other arithmetic  1.28 us (1%)
    ppermute x19, waiting for transfers between devices, moved(): return lax.ppermute(block, ('groups', 'seq'), route)  34.8 us
    ppermute x19, starting transfers between devices, moved(): return lax.ppermute(block, ('groups', 'seq'), route)  26.5 us
    all_to_all x1, blocking collectives, body(): lax.all_to_all(outgoing, 'seq', split_axis=0, concat_axis=1, tiled=True)  21.6 us
    pallas_call x4, Pallas kernels, product(): pl.pallas_call(functools.partial(product_kernel, plan, group, bool(totals...  11.2 us
    pallas_call x1, Pallas kernels, prepared(): pl.pallas_call(prepare_kernel, grid_spec=pltpu.PrefetchScalarGridSpec(num...  8.51 us
    unnamed x28, local copies, waits for them, and re-layouts  3.54 us
  transfers between devices with their start and end apart: 19, of which 14 were waited for; matrix products, arithmetic and copies ran while one was open for 3% of the time, Pallas kernels for 16%

profile of v18, /device:TPU:0, one launch (start us, length us, event | category | flops | bytes accessed | tf_op | source)
XLA Modules:
  0.0 114.6 jit_solution(4194602853096957062)
XLA Ops:
  0.6 0.5 collective-permute-start.3
  1.1 1.3 %constant_dynamic-slice_fusion = (bf16[256,512]{1,0:T(8,128)(2,1)S(1)}, bf16[256,512]{1,0:T(8,128)(2,1)S(1)}, bf16[256,512]{1,0:T(8,128)(2,1)S(1)}, bf16[256,512]{1,0:T(8,128)(2,1)S(1)}) fusion(bf16[512,512]{1,0:T(8,128)(2,1)} %param.16, s32[]{:T(128)S(6)} %select_n.52, s32[]{:T(128)S(6)} %select_n.51, bf16[512,512]{1,0:T(8,128)(2,1)} %param.15), kind=kLoop, calls=%fused_computation.4 | loop fusion | bytes 2097160 | tf_op jit(solution)/shard_map/dynamic_slice | solution.py:446
  2.4 0.1 pad_maximum_fusion.refs_0_
  2.5 2.6 %collective-permute-start.2 = (bf16[256,1024]{1,0:T(8,128)(2,1)S(1)}, bf16[256,1024]{1,0:T(8,128)(2,1)S(1)}, u32[]{:S(2)}, u32[]{:S(2)}) collective-permute-start(bf16[256,1024]{1,0:T(8,128)(2,1)S(1)} %pad_maximum_fusion.refs_0_), channel_id=1, source_target_pairs={{0,2},{1,3},{2,0},{3,1},{4,6},{5,7},{6,4},{7,5},{8,10},{9,11},{10,... | collective-permute-start | bytes 1572872 | tf_op jit(solution)/shard_map/ppermute | solution.py:66
  5.1 1.4 %collective-permute-start.1 = (bf16[256,1024]{1,0:T(8,128)(2,1)S(1)}, bf16[256,1024]{1,0:T(8,128)(2,1)}, u32[]{:S(2)}, u32[]{:S(2)}) collective-permute-start(bf16[256,1024]{1,0:T(8,128)(2,1)S(1)} %pad_maximum_fusion.refs_0_), channel_id=1, source_target_pairs={{4,8},{5,9},{6,10},{7,11},{8,4},{9,5},{10,6},{11,7},{20,24},{21,25... | collective-permute-start | bytes 1572872 | tf_op jit(solution)/shard_map/ppermute | solution.py:66
  6.5 3.7 %collective-permute-start = (bf16[256,1024]{1,0:T(8,128)(2,1)S(1)}, bf16[256,1024]{1,0:T(8,128)(2,1)S(1)}, u32[]{:S(2)}, u32[]{:S(2)}) collective-permute-start(bf16[256,1024]{1,0:T(8,128)(2,1)S(1)} %pad_maximum_fusion.refs_0_), channel_id=1, source_target_pairs={{0,4},{1,5},{2,6},{3,7},{4,0},{5,1},{6,2},{7,3},{8,12},{9,13},{10,... | collective-permute-start | bytes 1572872 | tf_op jit(solution)/shard_map/ppermute | solution.py:66
  10.2 0.1 pad_maximum_fusion.1.refs_1_
  10.3 7.4 %collective-permute-done.2.refs_2_ = bf16[256,1024]{1,0:T(8,128)(2,1)S(1)} collective-permute-done((bf16[256,1024]{1,0:T(8,128)(2,1)S(1)}, bf16[256,1024]{1,0:T(8,128)(2,1)S(1)}, u32[]{:S(2)}, u32[]{:S(2)}) %collective-permute-start.2) | collective-permute-done | bytes 524320 | tf_op jit(solution)/shard_map/ppermute | solution.py:66
  17.7 0.0 collective-permute-done.1
  17.7 4.6 %collective-permute-done.refs_4_ = bf16[256,1024]{1,0:T(8,128)(2,1)S(1)} collective-permute-done((bf16[256,1024]{1,0:T(8,128)(2,1)S(1)}, bf16[256,1024]{1,0:T(8,128)(2,1)S(1)}, u32[]{:S(2)}, u32[]{:S(2)}) %collective-permute-start) | collective-permute-done | bytes 524320 | tf_op jit(solution)/shard_map/ppermute | solution.py:66
  22.2 0.0 collective-permute-done.3.refs_1_
  22.2 0.5 collective-permute-start.7
  22.7 1.4 %collective-permute-start.5 = (bf16[256,1024]{1,0:T(8,128)(2,1)S(1)}, bf16[256,1024]{1,0:T(8,128)(2,1)}, u32[]{:S(2)}, u32[]{:S(2)}) collective-permute-start(bf16[256,1024]{1,0:T(8,128)(2,1)S(1)} %collective-permute-done.refs_4_), channel_id=1, source_target_pairs={{4,8},{5,9},{6,10},{7,11},{8,4},{9,5},{10,6},{11,7},{20,24},{21,25... | collective-permute-start | bytes 1572872 | tf_op jit(solution)/shard_map/ppermute | solution.py:66
  24.2 1.5 %collective-permute-start.4 = (bf16[256,1024]{1,0:T(8,128)(2,1)S(1)}, bf16[256,1024]{1,0:T(8,128)(2,1)S(1)}, u32[]{:S(2)}, u32[]{:S(2)}) collective-permute-start(bf16[256,1024]{1,0:T(8,128)(2,1)S(1)} %collective-permute-done.2.refs_2_), channel_id=1, source_target_pairs={{0,16},{1,17},{2,18},{3,19},{4,20},{5,21},{6,22},{7,23},{8,24},{9,... | collective-permute-start | bytes 1572872 | tf_op jit(solution)/shard_map/ppermute | solution.py:66
  25.7 1.3 %collective-permute-start.6 = (bf16[256,1024]{1,0:T(8,128)(2,1)}, bf16[256,1024]{1,0:T(8,128)(2,1)}, u32[]{:S(2)}, u32[]{:S(2)}) collective-permute-start(bf16[256,1024]{1,0:T(8,128)(2,1)} %collective-permute-done.1), channel_id=1, source_target_pairs={{4,0},{5,1},{6,2},{7,3},{8,12},{9,13},{10,14},{11,15},{20,16},{21,... | collective-permute-start | bytes 1572872 | tf_op jit(solution)/shard_map/ppermute | solution.py:66
  27.0 0.7 stack.47.place
  27.7 8.5 %normed_halves.1 = (bf16[16,320,256]{2,1,0:T(8,128)(2,1)}, bf16[16,320,256]{2,1,0:T(8,128)(2,1)}) custom-call(s32[11]{0:T(128)} %stack.47.place, bf16[320,8192]{1,0:T(8,128)(2,1)} %bitcast.17, bf16[320,8192]{1,0:T(8,128)(2,1)} %collective-permute-done.3.refs_1_), custom_call_target="tpu_custom_call" | custom-call | flops 1000 | bytes 1000 | tf_op jit(solution)/shard_map/normed_halves/pallas_call | solution.py:137
  36.2 0.9 collective-permute-done.4.refs_3_
  37.1 0.0 collective-permute-done.7.refs_5_
  37.1 0.0 collective-permute-done.5
  37.1 3.4 %collective-permute-done.6 = bf16[256,1024]{1,0:T(8,128)(2,1)} collective-permute-done((bf16[256,1024]{1,0:T(8,128)(2,1)}, bf16[256,1024]{1,0:T(8,128)(2,1)}, u32[]{:S(2)}, u32[]{:S(2)}) %collective-permute-start.6) | collective-permute-done | bytes 524320 | tf_op jit(solution)/shard_map/ppermute | solution.py:66
  40.5 1.3 %collective-permute-start.8 = (bf16[256,1024]{1,0:T(8,128)(2,1)}, bf16[256,1024]{1,0:T(8,128)(2,1)S(1)}, u32[]{:S(2)}, u32[]{:S(2)}) collective-permute-start(bf16[256,1024]{1,0:T(8,128)(2,1)} %collective-permute-done.5), channel_id=1, source_target_pairs={{4,0},{5,1},{6,2},{7,3},{8,12},{9,13},{10,14},{11,15},{20,16},{21,... | collective-permute-start | bytes 1572872 | tf_op jit(solution)/shard_map/ppermute | solution.py:66
  41.8 1.1 broadcast_select_fusion.1.refs_0_
  42.9 0.6 collective-permute-start.10
  43.5 1.5 %collective-permute-start.9 = (bf16[256,1024]{1,0:T(8,128)(2,1)S(1)}, bf16[256,1024]{1,0:T(8,128)(2,1)S(1)}, u32[]{:S(2)}, u32[]{:S(2)}) collective-permute-start(bf16[256,1024]{1,0:T(8,128)(2,1)S(1)} %broadcast_select_fusion.1.refs_0_), channel_id=1, source_target_pairs={{0,2},{1,3},{2,0},{3,1},{4,6},{5,7},{6,4},{7,5},{8,10},{9,11},{10,... | collective-permute-start | bytes 1572872 | tf_op jit(solution)/shard_map/ppermute | solution.py:66
  45.0 1.7 %copy-done = bf16[16,320,256]{2,1,0:T(8,128)(2,1)S(1)} copy-done((bf16[16,320,256]{2,1,0:T(8,128)(2,1)S(1)}, bf16[16,320,256]{2,1,0:T(8,128)(2,1)}, u32[]{:S(2)}) %copy-start) | copy-done | bytes 2621464
  46.8 1.7 %copy-done.1 = bf16[16,320,256]{2,1,0:T(8,128)(2,1)S(1)} copy-done((bf16[16,320,256]{2,1,0:T(8,128)(2,1)S(1)}, bf16[16,320,256]{2,1,0:T(8,128)(2,1)}, u32[]{:S(2)}) %copy-start.1) | copy-done | bytes 2621464
  48.5 3.5 %add_product.4 = (f32[320,1024]{1,0:T(8,128)S(1)}, f32[320,1024]{1,0:T(8,128)S(1)}) custom-call(s32[11]{0:T(128)S(1)} %copy-done.9, bf16[16,320,256]{2,1,0:T(8,128)(2,1)S(1)} %copy-done, bf16[16,320,256]{2,1,0:T(8,128)(2,1)S(1)} %copy-done.1, bf16[256,1024]{1,0:T(8,128)(2,1)S(1)} %pad_maximum_fusion.refs_0_, ...), custom_call_target="tpu_custom_call" | custom-call | flops 1000 | bytes 1000 | tf_op jit(solution)/shard_map/add_product/pallas_call | solution.py:204
  52.0 2.2 %collective-permute-done.8 = bf16[256,1024]{1,0:T(8,128)(2,1)S(1)} collective-permute-done((bf16[256,1024]{1,0:T(8,128)(2,1)}, bf16[256,1024]{1,0:T(8,128)(2,1)S(1)}, u32[]{:S(2)}, u32[]{:S(2)}) %collective-permute-start.8) | collective-permute-done | bytes 524320 | tf_op jit(solution)/shard_map/ppermute | solution.py:66
  54.3 0.4 collective-permute-done.10.refs_1_
  54.6 0.3 collective-permute-done.9.refs_2_
  54.9 2.4 %collective-permute-start.11 = (bf16[256,1024]{1,0:T(8,128)(2,1)S(1)}, bf16[256,1024]{1,0:T(8,128)(2,1)S(1)}, u32[]{:S(2)}, u32[]{:S(2)}) collective-permute-start(bf16[256,1024]{1,0:T(8,128)(2,1)S(1)} %pad_maximum_fusion.1.refs_1_), channel_id=1, source_target_pairs={{0,4},{1,5},{2,6},{3,7},{4,0},{5,1},{6,2},{7,3},{8,12},{9,13},{10,... | collective-permute-start | bytes 1572872 | tf_op jit(solution)/shard_map/ppermute | solution.py:66
  57.3 0.1 broadcast_select_fusion.refs_3_
  57.4 1.6 %collective-permute-start.13 = (bf16[256,1024]{1,0:T(8,128)(2,1)S(1)}, bf16[256,1024]{1,0:T(8,128)(2,1)S(1)}, u32[]{:S(2)}, u32[]{:S(2)}) collective-permute-start(bf16[256,1024]{1,0:T(8,128)(2,1)S(1)} %broadcast_select_fusion.refs_3_), channel_id=1, source_target_pairs={{0,2},{1,3},{2,0},{3,1},{4,6},{5,7},{6,4},{7,5},{8,10},{9,11},{10,... | collective-permute-start | bytes 1572872 | tf_op jit(solution)/shard_map/ppermute | solution.py:66
  58.9 1.5 %collective-permute-start.12 = (bf16[256,1024]{1,0:T(8,128)(2,1)S(1)}, bf16[256,1024]{1,0:T(8,128)(2,1)S(1)}, u32[]{:S(2)}, u32[]{:S(2)}) collective-permute-start(bf16[256,1024]{1,0:T(8,128)(2,1)S(1)} %broadcast_select_fusion.refs_3_), channel_id=1, source_target_pairs={{0,16},{1,17},{2,18},{3,19},{4,20},{5,21},{6,22},{7,23},{8,24},{9,... | collective-permute-start | bytes 1572872 | tf_op jit(solution)/shard_map/ppermute | solution.py:66
  60.4 2.9 %add_product.5 = (f32[320,1024]{1,0:T(8,128)S(1)}, f32[320,1024]{1,0:T(8,128)S(1)}) custom-call(s32[11]{0:T(128)S(1)} %copy-done.9, bf16[16,320,256]{2,1,0:T(8,128)(2,1)S(1)} %copy-done, bf16[16,320,256]{2,1,0:T(8,128)(2,1)S(1)} %copy-done.1, bf16[256,1024]{1,0:T(8,128)(2,1)S(1)} %broadcast_select_fusion.1.refs_0_, ...), custom_call_target="tpu_custom_call" | custom-call | flops 1000 | bytes 1000 | tf_op jit(solution)/shard_map/add_product/pallas_call | solution.py:204
  63.4 2.4 %collective-permute-done.11.refs_0_ = bf16[256,1024]{1,0:T(8,128)(2,1)S(1)} collective-permute-done((bf16[256,1024]{1,0:T(8,128)(2,1)S(1)}, bf16[256,1024]{1,0:T(8,128)(2,1)S(1)}, u32[]{:S(2)}, u32[]{:S(2)}) %collective-permute-start.11) | collective-permute-done | bytes 524320 | tf_op jit(solution)/shard_map/ppermute | solution.py:66
  65.7 1.6 %collective-permute-done.13.refs_2_ = bf16[256,1024]{1,0:T(8,128)(2,1)S(1)} collective-permute-done((bf16[256,1024]{1,0:T(8,128)(2,1)S(1)}, bf16[256,1024]{1,0:T(8,128)(2,1)S(1)}, u32[]{:S(2)}, u32[]{:S(2)}) %collective-permute-start.13) | collective-permute-done | bytes 524320 | tf_op jit(solution)/shard_map/ppermute | solution.py:66
  67.3 2.4 %collective-permute-done.12.refs_1_ = bf16[256,1024]{1,0:T(8,128)(2,1)S(1)} collective-permute-done((bf16[256,1024]{1,0:T(8,128)(2,1)S(1)}, bf16[256,1024]{1,0:T(8,128)(2,1)S(1)}, u32[]{:S(2)}, u32[]{:S(2)}) %collective-permute-start.12) | collective-permute-done | bytes 524320 | tf_op jit(solution)/shard_map/ppermute | solution.py:66
  69.7 2.2 %collective-permute-start.14 = (bf16[256,1024]{1,0:T(8,128)(2,1)S(1)}, bf16[256,1024]{1,0:T(8,128)(2,1)S(1)}, u32[]{:S(2)}, u32[]{:S(2)}) collective-permute-start(bf16[256,1024]{1,0:T(8,128)(2,1)S(1)} %collective-permute-done.4.refs_3_), channel_id=1, source_target_pairs={{0,4},{1,5},{2,6},{3,7},{4,0},{5,1},{6,2},{7,3},{8,12},{9,13},{10,... | collective-permute-start | bytes 1572872 | tf_op jit(solution)/shard_map/ppermute | solution.py:66
  71.9 1.5 %collective-permute-start.15 = (bf16[256,1024]{1,0:T(8,128)(2,1)S(1)}, bf16[256,1024]{1,0:T(8,128)(2,1)S(1)}, u32[]{:S(2)}, u32[]{:S(2)}) collective-permute-start(bf16[256,1024]{1,0:T(8,128)(2,1)S(1)} %collective-permute-done.9.refs_2_), channel_id=1, source_target_pairs={{0,16},{1,17},{2,18},{3,19},{4,20},{5,21},{6,22},{7,23},{8,24},{9,... | collective-permute-start | bytes 1572872 | tf_op jit(solution)/shard_map/ppermute | solution.py:66
  73.4 0.5 collective-permute-start.16
  73.9 2.4 %add_product.6 = (f32[320,1024]{1,0:T(8,128)S(1)}, f32[320,1024]{1,0:T(8,128)S(1)}) custom-call(s32[11]{0:T(128)S(1)} %copy-done.9, bf16[16,320,256]{2,1,0:T(8,128)(2,1)S(1)} %copy-done, bf16[16,320,256]{2,1,0:T(8,128)(2,1)S(1)} %copy-done.1, bf16[256,1024]{1,0:T(8,128)(2,1)S(1)} %collective-permute-done.11.refs_0_, ...), custom_call_target="tpu_custom_call" | custom-call | flops 1000 | bytes 1000 | tf_op jit(solution)/shard_map/add_product/pallas_call | solution.py:204
  76.2 2.8 %collective-permute-done.14.refs_0_ = bf16[256,1024]{1,0:T(8,128)(2,1)S(1)} collective-permute-done((bf16[256,1024]{1,0:T(8,128)(2,1)S(1)}, bf16[256,1024]{1,0:T(8,128)(2,1)S(1)}, u32[]{:S(2)}, u32[]{:S(2)}) %collective-permute-start.14) | collective-permute-done | bytes 524320 | tf_op jit(solution)/shard_map/ppermute | solution.py:66
  79.1 2.0 %collective-permute-done.15.refs_1_ = bf16[256,1024]{1,0:T(8,128)(2,1)S(1)} collective-permute-done((bf16[256,1024]{1,0:T(8,128)(2,1)S(1)}, bf16[256,1024]{1,0:T(8,128)(2,1)S(1)}, u32[]{:S(2)}, u32[]{:S(2)}) %collective-permute-start.15) | collective-permute-done | bytes 524320 | tf_op jit(solution)/shard_map/ppermute | solution.py:66
  81.1 1.5 %collective-permute-done.16.refs_2_ = bf16[256,1024]{1,0:T(8,128)(2,1)S(1)} collective-permute-done((bf16[256,1024]{1,0:T(8,128)(2,1)S(1)}, bf16[256,1024]{1,0:T(8,128)(2,1)S(1)}, u32[]{:S(2)}, u32[]{:S(2)}) %collective-permute-start.16) | collective-permute-done | bytes 524320 | tf_op jit(solution)/shard_map/ppermute | solution.py:66
  82.6 0.0 copy-start.6
  82.6 0.0 copy-start.7
  82.6 0.0 copy-start.12
  82.6 0.0 copy-start.13
  82.7 2.4 %add_product.7 = (f32[320,1024]{1,0:T(8,128)S(1)}, f32[320,1024]{1,0:T(8,128)S(1)}) custom-call(s32[11]{0:T(128)S(1)} %copy-done.9, bf16[16,320,256]{2,1,0:T(8,128)(2,1)S(1)} %copy-done, bf16[16,320,256]{2,1,0:T(8,128)(2,1)S(1)} %copy-done.1, bf16[256,1024]{1,0:T(8,128)(2,1)S(1)} %collective-permute-done.14.refs_0_, ...), custom_call_target="tpu_custom_call" | custom-call | flops 1000 | bytes 1000 | tf_op jit(solution)/shard_map/add_product/pallas_call | solution.py:204
  85.0 0.1 collective-permute-start.17
  85.1 3.0 %collective-permute-done.17.refs_1_ = f32[320,1024]{1,0:T(8,128)S(1)} collective-permute-done((f32[320,1024]{1,0:T(8,128)S(1)}, f32[320,1024]{1,0:T(8,128)S(1)}, u32[]{:S(2)}, u32[]{:S(2)}) %collective-permute-start.17) | collective-permute-done | bytes 1310752 | tf_op jit(solution)/shard_map/ppermute | solution.py:66
  88.1 0.0 copy-done.2
  88.2 1.0 cache_rows.1
  89.2 0.0 copy-start.8
  89.3 0.0 copy-start.10
  89.3 0.0 copy-start.11
  89.3 21.6 %all_to_all.4 = bf16[16,80,256]{2,1,0:T(8,128)(2,1)S(1)} all-to-all(bf16[16,80,256]{2,1,0:T(8,128)(2,1)S(1)} %cache_rows.1), channel_id=1, replica_groups=mesh['groups'=2,'seq'=16] {'seq'}, dimensions={0} | all-to-all | bytes 1310720 | tf_op jit(solution)/shard_map/all_to_all | solution.py:489
  110.9 1.1 decode.1.mine
  112.0 0.4 collective-permute-start.18
  112.4 0.8 copied.1
  113.2 0.0 collective-permute-done.18.theirs
  113.3 1.3 %joined.1 = bf16[4,512]{1,0:T(4,128)(2,1)} custom-call(s32[11]{0:T(128)S(1)} %copy-done.9, f32[32,256]{1,0:T(8,128)S(1)} %decode.1.mine, f32[32,256]{1,0:T(8,128)S(1)} %collective-permute-done.18.theirs), custom_call_target="tpu_custom_call" | custom-call | flops 1000 | bytes 1000 | tf_op jit(solution)/shard_map/joined/pallas_call | solution.py:379
  (18 shorter events, 0.0 us)
Async XLA Ops:
  0.6 21.6 %collective-permute-start.3 = (bf16[320,8192]{1,0:T(8,128)(2,1)}, bf16[320,8192]{1,0:T(8,128)(2,1)}, u32[]{:S(2)}, u32[]{:S(2)}) collective-permute-start(bf16[320,8192]{1,0:T(8,128)(2,1)} %bitcast.16), channel_id=1, source_target_pairs={{0,1},{1,0},{2,3},{3,2},{4,5},{5,4},{6,7},{7,6},{8,9},{9,8},{10,11... | collective-permute-start | bytes 15728648 | tf_op jit(solution)/shard_map/ppermute | solution.py:66
  2.5 15.2 %collective-permute-start.2 = (bf16[256,1024]{1,0:T(8,128)(2,1)S(1)}, bf16[256,1024]{1,0:T(8,128)(2,1)S(1)}, u32[]{:S(2)}, u32[]{:S(2)}) collective-permute-start(bf16[256,1024]{1,0:T(8,128)(2,1)S(1)} %pad_maximum_fusion.refs_0_), channel_id=1, source_target_pairs={{0,2},{1,3},{2,0},{3,1},{4,6},{5,7},{6,4},{7,5},{8,10},{9,11},{10,... | collective-permute-start | bytes 1572872 | tf_op jit(solution)/shard_map/ppermute | solution.py:66
  5.1 12.6 %collective-permute-start.1 = (bf16[256,1024]{1,0:T(8,128)(2,1)S(1)}, bf16[256,1024]{1,0:T(8,128)(2,1)}, u32[]{:S(2)}, u32[]{:S(2)}) collective-permute-start(bf16[256,1024]{1,0:T(8,128)(2,1)S(1)} %pad_maximum_fusion.refs_0_), channel_id=1, source_target_pairs={{4,8},{5,9},{6,10},{7,11},{8,4},{9,5},{10,6},{11,7},{20,24},{21,25... | collective-permute-start | bytes 1572872 | tf_op jit(solution)/shard_map/ppermute | solution.py:66
  6.5 15.7 %collective-permute-start = (bf16[256,1024]{1,0:T(8,128)(2,1)S(1)}, bf16[256,1024]{1,0:T(8,128)(2,1)S(1)}, u32[]{:S(2)}, u32[]{:S(2)}) collective-permute-start(bf16[256,1024]{1,0:T(8,128)(2,1)S(1)} %pad_maximum_fusion.refs_0_), channel_id=1, source_target_pairs={{0,4},{1,5},{2,6},{3,7},{4,0},{5,1},{6,2},{7,3},{8,12},{9,13},{10,... | collective-permute-start | bytes 1572872 | tf_op jit(solution)/shard_map/ppermute | solution.py:66
  22.2 14.9 %collective-permute-start.7 = (bf16[256,1024]{1,0:T(8,128)(2,1)S(1)}, bf16[256,1024]{1,0:T(8,128)(2,1)S(1)}, u32[]{:S(2)}, u32[]{:S(2)}) collective-permute-start(bf16[256,1024]{1,0:T(8,128)(2,1)S(1)} %collective-permute-done.refs_4_), channel_id=1, source_target_pairs={{0,2},{1,3},{2,0},{3,1},{4,6},{5,7},{6,4},{7,5},{8,10},{9,11},{10,... | collective-permute-start | bytes 1572872 | tf_op jit(solution)/shard_map/ppermute | solution.py:66
  22.7 14.4 %collective-permute-start.5 = (bf16[256,1024]{1,0:T(8,128)(2,1)S(1)}, bf16[256,1024]{1,0:T(8,128)(2,1)}, u32[]{:S(2)}, u32[]{:S(2)}) collective-permute-start(bf16[256,1024]{1,0:T(8,128)(2,1)S(1)} %collective-permute-done.refs_4_), channel_id=1, source_target_pairs={{4,8},{5,9},{6,10},{7,11},{8,4},{9,5},{10,6},{11,7},{20,24},{21,25... | collective-permute-start | bytes 1572872 | tf_op jit(solution)/shard_map/ppermute | solution.py:66
  24.2 12.9 %collective-permute-start.4 = (bf16[256,1024]{1,0:T(8,128)(2,1)S(1)}, bf16[256,1024]{1,0:T(8,128)(2,1)S(1)}, u32[]{:S(2)}, u32[]{:S(2)}) collective-permute-start(bf16[256,1024]{1,0:T(8,128)(2,1)S(1)} %collective-permute-done.2.refs_2_), channel_id=1, source_target_pairs={{0,16},{1,17},{2,18},{3,19},{4,20},{5,21},{6,22},{7,23},{8,24},{9,... | collective-permute-start | bytes 1572872 | tf_op jit(solution)/shard_map/ppermute | solution.py:66
  25.7 14.8 %collective-permute-start.6 = (bf16[256,1024]{1,0:T(8,128)(2,1)}, bf16[256,1024]{1,0:T(8,128)(2,1)}, u32[]{:S(2)}, u32[]{:S(2)}) collective-permute-start(bf16[256,1024]{1,0:T(8,128)(2,1)} %collective-permute-done.1), channel_id=1, source_target_pairs={{4,0},{5,1},{6,2},{7,3},{8,12},{9,13},{10,14},{11,15},{20,16},{21,... | collective-permute-start | bytes 1572872 | tf_op jit(solution)/shard_map/ppermute | solution.py:66
  36.2 8.8 %copy-start.9 = (s32[11]{0:T(128)S(1)}, s32[11]{0:T(128)}, u32[]{:S(2)}) copy-start(s32[11]{0:T(128)} %stack.47.place) | copy-start | bytes 136
  40.5 13.7 %collective-permute-start.8 = (bf16[256,1024]{1,0:T(8,128)(2,1)}, bf16[256,1024]{1,0:T(8,128)(2,1)S(1)}, u32[]{:S(2)}, u32[]{:S(2)}) collective-permute-start(bf16[256,1024]{1,0:T(8,128)(2,1)} %collective-permute-done.5), channel_id=1, source_target_pairs={{4,0},{5,1},{6,2},{7,3},{8,12},{9,13},{10,14},{11,15},{20,16},{21,... | collective-permute-start | bytes 1572872 | tf_op jit(solution)/shard_map/ppermute | solution.py:66
  42.9 11.7 %collective-permute-start.10 = (bf16[256,1024]{1,0:T(8,128)(2,1)S(1)}, bf16[256,1024]{1,0:T(8,128)(2,1)S(1)}, u32[]{:S(2)}, u32[]{:S(2)}) collective-permute-start(bf16[256,1024]{1,0:T(8,128)(2,1)S(1)} %broadcast_select_fusion.1.refs_0_), channel_id=1, source_target_pairs={{0,16},{1,17},{2,18},{3,19},{4,20},{5,21},{6,22},{7,23},{8,24},{9,... | collective-permute-start | bytes 1572872 | tf_op jit(solution)/shard_map/ppermute | solution.py:66
  43.5 11.4 %collective-permute-start.9 = (bf16[256,1024]{1,0:T(8,128)(2,1)S(1)}, bf16[256,1024]{1,0:T(8,128)(2,1)S(1)}, u32[]{:S(2)}, u32[]{:S(2)}) collective-permute-start(bf16[256,1024]{1,0:T(8,128)(2,1)S(1)} %broadcast_select_fusion.1.refs_0_), channel_id=1, source_target_pairs={{0,2},{1,3},{2,0},{3,1},{4,6},{5,7},{6,4},{7,5},{8,10},{9,11},{10,... | collective-permute-start | bytes 1572872 | tf_op jit(solution)/shard_map/ppermute | solution.py:66
  45.0 1.7 %copy-start = (bf16[16,320,256]{2,1,0:T(8,128)(2,1)S(1)}, bf16[16,320,256]{2,1,0:T(8,128)(2,1)}, u32[]{:S(2)}) copy-start(bf16[16,320,256]{2,1,0:T(8,128)(2,1)} %get-tuple-element.49.mine) | copy-start | bytes 7864324
  46.8 1.7 %copy-start.1 = (bf16[16,320,256]{2,1,0:T(8,128)(2,1)S(1)}, bf16[16,320,256]{2,1,0:T(8,128)(2,1)}, u32[]{:S(2)}) copy-start(bf16[16,320,256]{2,1,0:T(8,128)(2,1)} %get-tuple-element.35.other) | copy-start | bytes 7864324
  54.9 10.8 %collective-permute-start.11 = (bf16[256,1024]{1,0:T(8,128)(2,1)S(1)}, bf16[256,1024]{1,0:T(8,128)(2,1)S(1)}, u32[]{:S(2)}, u32[]{:S(2)}) collective-permute-start(bf16[256,1024]{1,0:T(8,128)(2,1)S(1)} %pad_maximum_fusion.1.refs_1_), channel_id=1, source_target_pairs={{0,4},{1,5},{2,6},{3,7},{4,0},{5,1},{6,2},{7,3},{8,12},{9,13},{10,... | collective-permute-start | bytes 1572872 | tf_op jit(solution)/shard_map/ppermute | solution.py:66
  57.4 10.0 %collective-permute-start.13 = (bf16[256,1024]{1,0:T(8,128)(2,1)S(1)}, bf16[256,1024]{1,0:T(8,128)(2,1)S(1)}, u32[]{:S(2)}, u32[]{:S(2)}) collective-permute-start(bf16[256,1024]{1,0:T(8,128)(2,1)S(1)} %broadcast_select_fusion.refs_3_), channel_id=1, source_target_pairs={{0,2},{1,3},{2,0},{3,1},{4,6},{5,7},{6,4},{7,5},{8,10},{9,11},{10,... | collective-permute-start | bytes 1572872 | tf_op jit(solution)/shard_map/ppermute | solution.py:66
  58.9 10.8 %collective-permute-start.12 = (bf16[256,1024]{1,0:T(8,128)(2,1)S(1)}, bf16[256,1024]{1,0:T(8,128)(2,1)S(1)}, u32[]{:S(2)}, u32[]{:S(2)}) collective-permute-start(bf16[256,1024]{1,0:T(8,128)(2,1)S(1)} %broadcast_select_fusion.refs_3_), channel_id=1, source_target_pairs={{0,16},{1,17},{2,18},{3,19},{4,20},{5,21},{6,22},{7,23},{8,24},{9,... | collective-permute-start | bytes 1572872 | tf_op jit(solution)/shard_map/ppermute | solution.py:66
  69.7 9.4 %collective-permute-start.14 = (bf16[256,1024]{1,0:T(8,128)(2,1)S(1)}, bf16[256,1024]{1,0:T(8,128)(2,1)S(1)}, u32[]{:S(2)}, u32[]{:S(2)}) collective-permute-start(bf16[256,1024]{1,0:T(8,128)(2,1)S(1)} %collective-permute-done.4.refs_3_), channel_id=1, source_target_pairs={{0,4},{1,5},{2,6},{3,7},{4,0},{5,1},{6,2},{7,3},{8,12},{9,13},{10,... | collective-permute-start | bytes 1572872 | tf_op jit(solution)/shard_map/ppermute | solution.py:66
  71.9 9.2 %collective-permute-start.15 = (bf16[256,1024]{1,0:T(8,128)(2,1)S(1)}, bf16[256,1024]{1,0:T(8,128)(2,1)S(1)}, u32[]{:S(2)}, u32[]{:S(2)}) collective-permute-start(bf16[256,1024]{1,0:T(8,128)(2,1)S(1)} %collective-permute-done.9.refs_2_), channel_id=1, source_target_pairs={{0,16},{1,17},{2,18},{3,19},{4,20},{5,21},{6,22},{7,23},{8,24},{9,... | collective-permute-start | bytes 1572872 | tf_op jit(solution)/shard_map/ppermute | solution.py:66
  73.4 9.2 %collective-permute-start.16 = (bf16[256,1024]{1,0:T(8,128)(2,1)S(1)}, bf16[256,1024]{1,0:T(8,128)(2,1)S(1)}, u32[]{:S(2)}, u32[]{:S(2)}) collective-permute-start(bf16[256,1024]{1,0:T(8,128)(2,1)S(1)} %collective-permute-done.12.refs_1_), channel_id=1, source_target_pairs={{0,2},{1,3},{2,0},{3,1},{4,6},{5,7},{6,4},{7,5},{8,10},{9,11},{10,... | collective-permute-start | bytes 1572872 | tf_op jit(solution)/shard_map/ppermute | solution.py:66
  82.6 5.5 %copy-start.2 = (f32[64,128]{1,0:T(8,128)S(1)}, f32[64,128]{1,0:T(8,128)}, u32[]{:S(2)}) copy-start(f32[64,128]{1,0:T(8,128)} %constant.71.clone.refs_5_.refs_3_) | copy-start | bytes 98308
  82.6 5.5 %copy-start.3 = (f32[64,128]{1,0:T(8,128)S(1)}, f32[64,128]{1,0:T(8,128)}, u32[]{:S(2)}) copy-start(f32[64,128]{1,0:T(8,128)} %constant.70.clone.refs_4_.refs_2_) | copy-start | bytes 98308
  82.6 5.5 %copy-start.4 = (f32[41,128]{1,0:T(8,128)S(1)}, f32[41,128]{1,0:T(8,128)}, u32[]{:S(2)}) copy-start(f32[41,128]{1,0:T(8,128)} %constant.69.clone.refs_3_.refs_1_) | copy-start | bytes 62980
  82.6 5.5 %copy-start.5 = (f32[41,128]{1,0:T(8,128)S(1)}, f32[41,128]{1,0:T(8,128)}, u32[]{:S(2)}) copy-start(f32[41,128]{1,0:T(8,128)} %constant.68.clone.refs_2_.refs_0_) | copy-start | bytes 62980
  82.6 5.6 %copy-start.6 = (f32[160,128]{1,0:T(8,128)S(1)}, f32[160,128]{1,0:T(8,128)}, u32[]{:S(2)}) copy-start(f32[160,128]{1,0:T(8,128)} %constant.73.clone.refs_7_) | copy-start | bytes 245764
  82.6 5.6 %copy-start.7 = (f32[160,128]{1,0:T(8,128)S(1)}, f32[160,128]{1,0:T(8,128)}, u32[]{:S(2)}) copy-start(f32[160,128]{1,0:T(8,128)} %constant.72.clone.refs_6_) | copy-start | bytes 245764
  82.6 5.5 %copy-start.12 = (s32[2]{0:T(128)S(1)}, s32[2]{0:T(128)}, u32[]{:S(2)}) copy-start(s32[2]{0:T(128)} %lengths.3) | copy-start | bytes 28
  82.6 5.5 %copy-start.13 = (s32[8]{0:T(128)S(1)}, s32[8]{0:T(128)}, u32[]{:S(2)}) copy-start(s32[8]{0:T(128)} %owner.3) | copy-start | bytes 100
  85.0 3.1 %collective-permute-start.17 = (f32[320,1024]{1,0:T(8,128)S(1)}, f32[320,1024]{1,0:T(8,128)S(1)}, u32[]{:S(2)}, u32[]{:S(2)}) collective-permute-start(f32[320,1024]{1,0:T(8,128)S(1)} %get-tuple-element.51), channel_id=1, source_target_pairs={{0,1},{1,0},{2,3},{3,2},{4,5},{5,4},{6,7},{7,6},{8,9},{9,8},{10,11... | collective-permute-start | bytes 3932168 | tf_op jit(solution)/shard_map/ppermute | solution.py:66
  89.2 21.6 %copy-start.8 = (bf16[8,4,1024]{2,1,0:T(4,128)(2,1)S(1)}, bf16[8,4,1024]{2,1,0:T(4,128)(2,1)}, u32[]{:S(2)}) copy-start(bf16[8,4,1024]{2,1,0:T(4,128)(2,1)} %dec_query.1) | copy-start | bytes 196612
  89.3 21.6 %copy-start.10 = (bf16[8,4,128]{2,1,0:T(4,128)(2,1)S(1)}, bf16[8,4,128]{2,1,0:T(4,128)(2,1)}, u32[]{:S(2)}) copy-start(bf16[8,4,128]{2,1,0:T(4,128)(2,1)} %dec_key.1) | copy-start | bytes 24580
  89.3 21.6 %copy-start.11 = (bf16[8,4,128]{2,1,0:T(4,128)(2,1)S(1)}, bf16[8,4,128]{2,1,0:T(4,128)(2,1)}, u32[]{:S(2)}) copy-start(bf16[8,4,128]{2,1,0:T(4,128)(2,1)} %dec_value.1) | copy-start | bytes 24580
  112.0 1.3 %collective-permute-start.18 = (f32[32,256]{1,0:T(8,128)S(1)}, f32[32,256]{1,0:T(8,128)S(1)}, u32[]{:S(2)}, u32[]{:S(2)}) collective-permute-start(f32[32,256]{1,0:T(8,128)S(1)} %decode.1.mine), channel_id=1, source_target_pairs={{0,1},{1,0},{2,3},{3,2},{4,5},{5,4},{6,7},{7,6},{8,9},{9,8},{10,11... | collective-permute-start | bytes 98312 | tf_op jit(solution)/shard_map/ppermute | solution.py:66

commit v19 on v18

--- a/solution.py
+++ b/solution.py
@@ -455,33 +455,32 @@
         middle = moved(sent, to_middle)
         across = moved(sent, to_row)
         rest = half_block(depth - group_id * depth)
-        came = (near, middle, across, raw, rest)
-        passed = moved(after(middle, *came), to_end)
-        middle_c = moved(after(near, *came), to_middle)
-        near_y = moved(after(near, *came), to_row)
-        across_x = moved(after(across, *came), to_group)
-        mine, other = prepared(place, after(flat, *came), raw, seq // 2)
-        came = (passed, middle_c, near_y, across_x, mine)
-        far = moved(after(middle_c, *came), to_end)
-        block_b = jnp.where(is_end, after(passed, *came), middle)
+        layers, rows = (near, middle), (near, middle, across, raw, rest)
+        passed = moved(after(middle, *layers), to_end)
+        middle_c = moved(after(near, *layers), to_middle)
+        near_y = moved(after(near, *rows), to_row)
+        across_x = moved(after(across, *rows), to_group)
+        mine, other = prepared(place, after(flat, *rows), raw, seq // 2)
+        layers, rows = (passed, middle_c), (near_y, across_x, mine, passed)
+        far = moved(after(middle_c, *layers), to_end)
+        block_b = jnp.where(is_end, after(passed, *rows), middle)
         block_yb = moved(block_b, to_row)
         block_xb = moved(block_b, to_group)
+        layers, rows = (far, near_y), (block_yb, block_xb, far)
+        near_rest = moved(after(rest, *layers), to_pair)
+        block_c = jnp.where(is_end, after(far, *rows), middle_c)
+        block_xc = moved(block_c, to_group)
+        block_yc = moved(block_c, to_row)
         pieces = [(HERE, 0, sent), (HERE, 1, rest), (THERE, 0, across)]
         pieces += [(THERE, 1, across_x), (HERE + 1, 0, near), (THERE + 1, 0, near_y)]
-        totals = product(place, after(mine, *came), other, pieces, (), 3)
-        came = (far, block_yb, block_xb, totals[0])
-        near_rest = moved(after(rest, *came), to_pair)
-        block_c = jnp.where(is_end, after(far, *came), middle_c)
-        block_xc = moved(block_c, to_group)
-        block_yc = moved(block_c, to_row)
-        pieces = [(HERE + 2, 0, block_b), (HERE + 2, 1, block_xb)]
-        pieces += [(THERE + 2, 0, block_yb), (HERE + 3, 0, block_c)]
-        totals = product(place, after(mine, *came), other, pieces, totals, 4)
-        came = (near_rest, block_xc, block_yc, totals[0])
-        end_a = moved(after(across_x, *came), to_pair)
-        ends = [moved(after(block_yb, *came), to_group), moved(after(block_xc, *came), to_row)]
-        pieces = [(HERE + 1, 1, near_rest), (HERE + 3, 1, block_xc), (THERE + 3, 0, block_yc)]
-        totals = product(place, after(mine, *came), other, pieces, totals, 3)
+        totals = product(place, after(mine, block_c), other, pieces, (), 3)
+        layers, rows = (near_rest, block_yb), (block_xc, block_yc, near_rest, totals[0])
+        end_a = moved(after(across_x, *layers), to_pair)
+        ends = [moved(after(block_yb, *rows), to_group), moved(after(block_xc, *rows), to_row)]
+        pieces = [(HERE + 2, 0, block_b), (HERE + 2, 1, block_xb), (THERE + 2, 0, block_yb)]
+        pieces += [(HERE + 3, 0, block_c), (HERE + 1, 1, near_rest)]
+        pieces += [(HERE + 3, 1, block_xc), (THERE + 3, 0, block_yc)]
+        totals = product(place, after(mine, *rows), other, pieces, totals, 7)
         came = (end_a, *ends, *totals)
         pieces = [(THERE + 1, 1, end_a), (THERE + 2, 1, ends[0]), (THERE + 3, 1, ends[1])]
         total, given = product(place, after(mine, *came), other, pieces, totals, 3)

time: 115 us -> 121 us (1.052)
  waiting for transfers between devices: 34.8 us -> 41.8 us
  blocking collectives: 21.6 us -> 25 us
  local copies, waits for them, and re-layouts: 5.48 us -> 3.74 us
  starting transfers between devices: 26.5 us -> 25.1 us
    ppermute x19, waiting for transfers between devices: 34.8 us -> 41.8 us  [moved(): return lax.ppermute(block, ('groups', 'seq'), route)]
    all_to_all x1, blocking collectives: 21.6 us -> 25 us  [body(): lax.all_to_all(outgoing, 'seq', split_axis=0, concat_axis=1, tiled=True)]
    unnamed x28 -> x30, local copies, waits for them, and re-layouts: 3.54 us -> 1.82 us
    ppermute x19, starting transfers between devices: 26.5 us -> 25.1 us  [moved(): return lax.ppermute(block, ('groups', 'seq'), route)]
    pallas_call x4 -> x3, Pallas kernels: 11.2 us -> 10.2 us  [product(): pl.pallas_call(functools.partial(product_kernel, plan, group, bool(totals...]
  transfers between devices with their start and end apart: 19 -> 19, of which waited for: 14 -> 10; matrix products, arithmetic and copies ran while one was open for 3% -> 3% of each run, Pallas kernels for 16% -> 14%
where the time goes in v19:
time: 121 us
  waiting for transfers between devices  41.8 us (35%)
  starting transfers between devices  25.1 us (21%)
  blocking collectives  25 us (21%)
  Pallas kernels  23 us (19%)
  local copies, waits for them, and re-layouts  3.74 us (3%)
  other arithmetic  1.43 us (1%)
    ppermute x19, waiting for transfers between devices, moved(): return lax.ppermute(block, ('groups', 'seq'), route)  41.8 us
    ppermute x19, starting transfers between devices, moved(): return lax.ppermute(block, ('groups', 'seq'), route)  25.1 us
    all_to_all x1, blocking collectives, body(): lax.all_to_all(outgoing, 'seq', split_axis=0, concat_axis=1, tiled=True)  25 us
    pallas_call x3, Pallas kernels, product(): pl.pallas_call(functools.partial(product_kernel, plan, group, bool(totals...  10.2 us
    pallas_call x1, Pallas kernels, prepared(): pl.pallas_call(prepare_kernel, grid_spec=pltpu.PrefetchScalarGridSpec(num...  8.5 us
  transfers between devices with their start and end apart: 19, of which 10 were waited for; matrix products, arithmetic and copies ran while one was open for 3% of the time, Pallas kernels for 14%

profile of v19, /device:TPU:0, one launch (start us, length us, event | category | flops | bytes accessed | tf_op | source)
XLA Modules:
  0.0 121.1 jit_solution(16741721839331592988)
XLA Ops:
  0.6 0.5 collective-permute-start.3
  1.1 1.3 %constant_dynamic-slice_fusion = (bf16[256,512]{1,0:T(8,128)(2,1)S(1)}, bf16[256,512]{1,0:T(8,128)(2,1)S(1)}, bf16[256,512]{1,0:T(8,128)(2,1)S(1)}, bf16[256,512]{1,0:T(8,128)(2,1)S(1)}) fusion(bf16[512,512]{1,0:T(8,128)(2,1)} %param.16, s32[]{:T(128)S(6)} %select_n.52, s32[]{:T(128)S(6)} %select_n.51, bf16[512,512]{1,0:T(8,128)(2,1)} %param.15), kind=kLoop, calls=%fused_computation.4 | loop fusion | bytes 2097160 | tf_op jit(solution)/shard_map/dynamic_slice | solution.py:446
  2.4 0.1 pad_maximum_fusion.refs_0_
  2.5 2.7 %collective-permute-start = (bf16[256,1024]{1,0:T(8,128)(2,1)S(1)}, bf16[256,1024]{1,0:T(8,128)(2,1)S(1)}, u32[]{:S(2)}, u32[]{:S(2)}) collective-permute-start(bf16[256,1024]{1,0:T(8,128)(2,1)S(1)} %pad_maximum_fusion.refs_0_), channel_id=1, source_target_pairs={{0,4},{1,5},{2,6},{3,7},{4,0},{5,1},{6,2},{7,3},{8,12},{9,13},{10,... | collective-permute-start | bytes 1572872 | tf_op jit(solution)/shard_map/ppermute | solution.py:66
  5.1 1.4 %collective-permute-start.1 = (bf16[256,1024]{1,0:T(8,128)(2,1)S(1)}, bf16[256,1024]{1,0:T(8,128)(2,1)}, u32[]{:S(2)}, u32[]{:S(2)}) collective-permute-start(bf16[256,1024]{1,0:T(8,128)(2,1)S(1)} %pad_maximum_fusion.refs_0_), channel_id=1, source_target_pairs={{4,8},{5,9},{6,10},{7,11},{8,4},{9,5},{10,6},{11,7},{20,24},{21,25... | collective-permute-start | bytes 1572872 | tf_op jit(solution)/shard_map/ppermute | solution.py:66
  6.6 1.5 %collective-permute-start.2 = (bf16[256,1024]{1,0:T(8,128)(2,1)S(1)}, bf16[256,1024]{1,0:T(8,128)(2,1)S(1)}, u32[]{:S(2)}, u32[]{:S(2)}) collective-permute-start(bf16[256,1024]{1,0:T(8,128)(2,1)S(1)} %pad_maximum_fusion.refs_0_), channel_id=1, source_target_pairs={{0,2},{1,3},{2,0},{3,1},{4,6},{5,7},{6,4},{7,5},{8,10},{9,11},{10,... | collective-permute-start | bytes 1572872 | tf_op jit(solution)/shard_map/ppermute | solution.py:66
  8.1 0.1 pad_maximum_fusion.1.refs_1_
  8.2 9.5 %collective-permute-done.refs_4_ = bf16[256,1024]{1,0:T(8,128)(2,1)S(1)} collective-permute-done((bf16[256,1024]{1,0:T(8,128)(2,1)S(1)}, bf16[256,1024]{1,0:T(8,128)(2,1)S(1)}, u32[]{:S(2)}, u32[]{:S(2)}) %collective-permute-start) | collective-permute-done | bytes 524320 | tf_op jit(solution)/shard_map/ppermute | solution.py:66
  17.7 0.0 collective-permute-done.1
  17.7 1.3 %collective-permute-start.6 = (bf16[256,1024]{1,0:T(8,128)(2,1)}, bf16[256,1024]{1,0:T(8,128)(2,1)}, u32[]{:S(2)}, u32[]{:S(2)}) collective-permute-start(bf16[256,1024]{1,0:T(8,128)(2,1)} %collective-permute-done.1), channel_id=1, source_target_pairs={{4,0},{5,1},{6,2},{7,3},{8,12},{9,13},{10,14},{11,15},{20,16},{21,... | collective-permute-start | bytes 1572872 | tf_op jit(solution)/shard_map/ppermute | solution.py:66
  19.0 1.5 %collective-permute-start.5 = (bf16[256,1024]{1,0:T(8,128)(2,1)S(1)}, bf16[256,1024]{1,0:T(8,128)(2,1)}, u32[]{:S(2)}, u32[]{:S(2)}) collective-permute-start(bf16[256,1024]{1,0:T(8,128)(2,1)S(1)} %collective-permute-done.refs_4_), channel_id=1, source_target_pairs={{4,8},{5,9},{6,10},{7,11},{8,4},{9,5},{10,6},{11,7},{20,24},{21,25... | collective-permute-start | bytes 1572872 | tf_op jit(solution)/shard_map/ppermute | solution.py:66
  20.5 0.1 collective-permute-done.2.refs_2_
  20.6 0.0 collective-permute-done.3.refs_1_
  20.6 1.6 %collective-permute-start.8 = (bf16[256,1024]{1,0:T(8,128)(2,1)S(1)}, bf16[256,1024]{1,0:T(8,128)(2,1)S(1)}, u32[]{:S(2)}, u32[]{:S(2)}) collective-permute-start(bf16[256,1024]{1,0:T(8,128)(2,1)S(1)} %collective-permute-done.refs_4_), channel_id=1, source_target_pairs={{0,2},{1,3},{2,0},{3,1},{4,6},{5,7},{6,4},{7,5},{8,10},{9,11},{10,... | collective-permute-start | bytes 1572872 | tf_op jit(solution)/shard_map/ppermute | solution.py:66
  22.2 1.5 %collective-permute-start.4 = (bf16[256,1024]{1,0:T(8,128)(2,1)S(1)}, bf16[256,1024]{1,0:T(8,128)(2,1)S(1)}, u32[]{:S(2)}, u32[]{:S(2)}) collective-permute-start(bf16[256,1024]{1,0:T(8,128)(2,1)S(1)} %collective-permute-done.2.refs_2_), channel_id=1, source_target_pairs={{0,16},{1,17},{2,18},{3,19},{4,20},{5,21},{6,22},{7,23},{8,24},{9,... | collective-permute-start | bytes 1572872 | tf_op jit(solution)/shard_map/ppermute | solution.py:66
  23.7 0.7 stack.47.place
  24.3 11.6 %collective-permute-done.6 = bf16[256,1024]{1,0:T(8,128)(2,1)} collective-permute-done((bf16[256,1024]{1,0:T(8,128)(2,1)}, bf16[256,1024]{1,0:T(8,128)(2,1)}, u32[]{:S(2)}, u32[]{:S(2)}) %collective-permute-start.6) | collective-permute-done | bytes 524320 | tf_op jit(solution)/shard_map/ppermute | solution.py:66
  35.9 0.0 collective-permute-done.5
  35.9 1.3 %collective-permute-start.7 = (bf16[256,1024]{1,0:T(8,128)(2,1)}, bf16[256,1024]{1,0:T(8,128)(2,1)S(1)}, u32[]{:S(2)}, u32[]{:S(2)}) collective-permute-start(bf16[256,1024]{1,0:T(8,128)(2,1)} %collective-permute-done.5), channel_id=1, source_target_pairs={{4,0},{5,1},{6,2},{7,3},{8,12},{9,13},{10,14},{11,15},{20,16},{21,... | collective-permute-start | bytes 1572872 | tf_op jit(solution)/shard_map/ppermute | solution.py:66
  37.2 8.5 %normed_halves.1 = (bf16[16,320,256]{2,1,0:T(8,128)(2,1)}, bf16[16,320,256]{2,1,0:T(8,128)(2,1)}) custom-call(s32[11]{0:T(128)} %stack.47.place, bf16[320,8192]{1,0:T(8,128)(2,1)} %bitcast.17, bf16[320,8192]{1,0:T(8,128)(2,1)} %collective-permute-done.3.refs_1_), custom_call_target="tpu_custom_call" | custom-call | flops 1000 | bytes 1000 | tf_op jit(solution)/shard_map/normed_halves/pallas_call | solution.py:137
  45.7 0.0 collective-permute-done.8.refs_5_
  45.7 0.0 collective-permute-done.4.refs_3_
  45.8 1.3 %broadcast_select_fusion.1.refs_0_ = bf16[256,1024]{1,0:T(8,128)(2,1)S(1)} fusion(bf16[256,1024]{1,0:T(8,128)(2,1)} %collective-permute-done.6, bf16[256,1024]{1,0:T(8,128)(2,1)} %collective-permute-done.1, pred[]{:T(512)S(6)} %or.3), kind=kLoop, calls=%fused_computation.3 | loop fusion | flops 262144 | bytes 1572865 | tf_op jit(solution)/shard_map/jit(_where)/select_n | solution.py:466
  47.0 1.6 %collective-permute-start.10 = (bf16[256,1024]{1,0:T(8,128)(2,1)S(1)}, bf16[256,1024]{1,0:T(8,128)(2,1)S(1)}, u32[]{:S(2)}, u32[]{:S(2)}) collective-permute-start(bf16[256,1024]{1,0:T(8,128)(2,1)S(1)} %broadcast_select_fusion.1.refs_0_), channel_id=1, source_target_pairs={{0,2},{1,3},{2,0},{3,1},{4,6},{5,7},{6,4},{7,5},{8,10},{9,11},{10,... | collective-permute-start | bytes 1572872 | tf_op jit(solution)/shard_map/ppermute | solution.py:66
  48.6 1.5 %collective-permute-start.12 = (bf16[256,1024]{1,0:T(8,128)(2,1)S(1)}, bf16[256,1024]{1,0:T(8,128)(2,1)S(1)}, u32[]{:S(2)}, u32[]{:S(2)}) collective-permute-start(bf16[256,1024]{1,0:T(8,128)(2,1)S(1)} %broadcast_select_fusion.1.refs_0_), channel_id=1, source_target_pairs={{0,16},{1,17},{2,18},{3,19},{4,20},{5,21},{6,22},{7,23},{8,24},{9,... | collective-permute-start | bytes 1572872 | tf_op jit(solution)/shard_map/ppermute | solution.py:66
  50.1 2.4 %collective-permute-done.7 = bf16[256,1024]{1,0:T(8,128)(2,1)S(1)} collective-permute-done((bf16[256,1024]{1,0:T(8,128)(2,1)}, bf16[256,1024]{1,0:T(8,128)(2,1)S(1)}, u32[]{:S(2)}, u32[]{:S(2)}) %collective-permute-start.7) | collective-permute-done | bytes 524320 | tf_op jit(solution)/shard_map/ppermute | solution.py:66
  52.5 1.8 %collective-permute-start.9 = (bf16[256,1024]{1,0:T(8,128)(2,1)S(1)}, bf16[256,1024]{1,0:T(8,128)(2,1)S(1)}, u32[]{:S(2)}, u32[]{:S(2)}) collective-permute-start(bf16[256,1024]{1,0:T(8,128)(2,1)S(1)} %pad_maximum_fusion.1.refs_1_), channel_id=1, source_target_pairs={{0,4},{1,5},{2,6},{3,7},{4,0},{5,1},{6,2},{7,3},{8,12},{9,13},{10,... | collective-permute-start | bytes 1572872 | tf_op jit(solution)/shard_map/ppermute | solution.py:66
  54.3 5.7 %collective-permute-done.10.refs_2_ = bf16[256,1024]{1,0:T(8,128)(2,1)S(1)} collective-permute-done((bf16[256,1024]{1,0:T(8,128)(2,1)S(1)}, bf16[256,1024]{1,0:T(8,128)(2,1)S(1)}, u32[]{:S(2)}, u32[]{:S(2)}) %collective-permute-start.10) | collective-permute-done | bytes 524320 | tf_op jit(solution)/shard_map/ppermute | solution.py:66
  60.1 1.2 %collective-permute-done.12.refs_1_ = bf16[256,1024]{1,0:T(8,128)(2,1)S(1)} collective-permute-done((bf16[256,1024]{1,0:T(8,128)(2,1)S(1)}, bf16[256,1024]{1,0:T(8,128)(2,1)S(1)}, u32[]{:S(2)}, u32[]{:S(2)}) %collective-permute-start.12) | collective-permute-done | bytes 524320 | tf_op jit(solution)/shard_map/ppermute | solution.py:66
  61.3 0.1 broadcast_select_fusion.refs_3_
  61.4 1.6 %collective-permute-start.13 = (bf16[256,1024]{1,0:T(8,128)(2,1)S(1)}, bf16[256,1024]{1,0:T(8,128)(2,1)S(1)}, u32[]{:S(2)}, u32[]{:S(2)}) collective-permute-start(bf16[256,1024]{1,0:T(8,128)(2,1)S(1)} %broadcast_select_fusion.refs_3_), channel_id=1, source_target_pairs={{0,16},{1,17},{2,18},{3,19},{4,20},{5,21},{6,22},{7,23},{8,24},{9,... | collective-permute-start | bytes 1572872 | tf_op jit(solution)/shard_map/ppermute | solution.py:66
  62.9 0.5 collective-permute-start.14
  63.4 1.3 %collective-permute-done.9.refs_4_ = bf16[256,1024]{1,0:T(8,128)(2,1)S(1)} collective-permute-done((bf16[256,1024]{1,0:T(8,128)(2,1)S(1)}, bf16[256,1024]{1,0:T(8,128)(2,1)S(1)}, u32[]{:S(2)}, u32[]{:S(2)}) %collective-permute-start.9) | collective-permute-done | bytes 524320 | tf_op jit(solution)/shard_map/ppermute | solution.py:66
  64.7 3.7 %collective-permute-start.11 = (bf16[256,1024]{1,0:T(8,128)(2,1)S(1)}, bf16[256,1024]{1,0:T(8,128)(2,1)S(1)}, u32[]{:S(2)}, u32[]{:S(2)}) collective-permute-start(bf16[256,1024]{1,0:T(8,128)(2,1)S(1)} %collective-permute-done.4.refs_3_), channel_id=1, source_target_pairs={{0,4},{1,5},{2,6},{3,7},{4,0},{5,1},{6,2},{7,3},{8,12},{9,13},{10,... | collective-permute-start | bytes 1572872 | tf_op jit(solution)/shard_map/ppermute | solution.py:66
  68.4 0.0 copy-done
  68.4 1.7 %copy-done.1 = bf16[16,320,256]{2,1,0:T(8,128)(2,1)S(1)} copy-done((bf16[16,320,256]{2,1,0:T(8,128)(2,1)S(1)}, bf16[16,320,256]{2,1,0:T(8,128)(2,1)}, u32[]{:S(2)}) %copy-start.1) | copy-done | bytes 2621464
  70.1 3.5 %add_product.3 = (f32[320,1024]{1,0:T(8,128)S(1)}, f32[320,1024]{1,0:T(8,128)S(1)}) custom-call(s32[11]{0:T(128)S(1)} %copy-done.10, bf16[16,320,256]{2,1,0:T(8,128)(2,1)S(1)} %copy-done, bf16[16,320,256]{2,1,0:T(8,128)(2,1)S(1)} %copy-done.1, bf16[256,1024]{1,0:T(8,128)(2,1)S(1)} %pad_maximum_fusion.refs_0_, ...), custom_call_target="tpu_custom_call" | custom-call | flops 1000 | bytes 1000 | tf_op jit(solution)/shard_map/add_product/pallas_call | solution.py:204
  73.7 0.0 collective-permute-done.13.refs_5_
  73.7 1.3 %collective-permute-done.14.refs_6_ = bf16[256,1024]{1,0:T(8,128)(2,1)S(1)} collective-permute-done((bf16[256,1024]{1,0:T(8,128)(2,1)S(1)}, bf16[256,1024]{1,0:T(8,128)(2,1)S(1)}, u32[]{:S(2)}, u32[]{:S(2)}) %collective-permute-start.14) | collective-permute-done | bytes 524320 | tf_op jit(solution)/shard_map/ppermute | solution.py:66
  75.0 0.3 collective-permute-start.16
  75.3 0.5 collective-permute-start.15
  75.8 0.0 copy-done.2
  75.8 4.3 %add_product.4 = (f32[320,1024]{1,0:T(8,128)S(1)}, f32[320,1024]{1,0:T(8,128)S(1)}) custom-call(s32[11]{0:T(128)S(1)} %copy-done.10, bf16[16,320,256]{2,1,0:T(8,128)(2,1)S(1)} %copy-done, bf16[16,320,256]{2,1,0:T(8,128)(2,1)S(1)} %copy-done.2, bf16[256,1024]{1,0:T(8,128)(2,1)S(1)} %broadcast_select_fusion.1.refs_0_, ...), custom_call_target="tpu_custom_call" | custom-call | flops 1000 | bytes 1000 | tf_op jit(solution)/shard_map/add_product/pallas_call | solution.py:204
  80.1 0.0 collective-permute-done.11.refs_0_
  80.2 5.5 %collective-permute-done.16.refs_2_ = bf16[256,1024]{1,0:T(8,128)(2,1)S(1)} collective-permute-done((bf16[256,1024]{1,0:T(8,128)(2,1)S(1)}, bf16[256,1024]{1,0:T(8,128)(2,1)S(1)}, u32[]{:S(2)}, u32[]{:S(2)}) %collective-permute-start.16) | collective-permute-done | bytes 524320 | tf_op jit(solution)/shard_map/ppermute | solution.py:66
  85.7 0.0 collective-permute-done.15.refs_1_
  85.7 0.0 copy-start.6
  85.7 0.0 copy-start.7
  85.7 0.0 copy-start.8
  85.7 0.0 copy-start.13
  85.7 0.0 copy-start.14
  85.7 2.4 %add_product.5 = (f32[320,1024]{1,0:T(8,128)S(1)}, f32[320,1024]{1,0:T(8,128)S(1)}) custom-call(s32[11]{0:T(128)S(1)} %copy-done.10, bf16[16,320,256]{2,1,0:T(8,128)(2,1)S(1)} %copy-done, bf16[16,320,256]{2,1,0:T(8,128)(2,1)S(1)} %copy-done.2, bf16[256,1024]{1,0:T(8,128)(2,1)S(1)} %collective-permute-done.11.refs_0_, ...), custom_call_target="tpu_custom_call" | custom-call | flops 1000 | bytes 1000 | tf_op jit(solution)/shard_map/add_product/pallas_call | solution.py:204
  88.1 0.1 collective-permute-start.17
  88.2 3.0 %collective-permute-done.17.refs_1_ = f32[320,1024]{1,0:T(8,128)S(1)} collective-permute-done((f32[320,1024]{1,0:T(8,128)S(1)}, f32[320,1024]{1,0:T(8,128)S(1)}, u32[]{:S(2)}, u32[]{:S(2)}) %collective-permute-start.17) | collective-permute-done | bytes 1310752 | tf_op jit(solution)/shard_map/ppermute | solution.py:66
  91.3 1.0 cache_rows.1
  92.3 0.0 copy-start.9
  92.3 0.0 copy-start.11
  92.3 0.0 copy-start.12
  92.4 25.0 %all_to_all.4 = bf16[16,80,256]{2,1,0:T(8,128)(2,1)S(1)} all-to-all(bf16[16,80,256]{2,1,0:T(8,128)(2,1)S(1)} %cache_rows.1), channel_id=1, replica_groups=mesh['groups'=2,'seq'=16] {'seq'}, dimensions={0} | all-to-all | bytes 1310720 | tf_op jit(solution)/shard_map/all_to_all | solution.py:488
  117.4 1.1 decode.1.mine
  118.5 0.4 collective-permute-start.18
  118.9 0.8 copied.1
  119.7 0.0 collective-permute-done.18.theirs
  119.8 1.3 %joined.1 = bf16[4,512]{1,0:T(4,128)(2,1)} custom-call(s32[11]{0:T(128)S(1)} %copy-done.10, f32[32,256]{1,0:T(8,128)S(1)} %decode.1.mine, f32[32,256]{1,0:T(8,128)S(1)} %collective-permute-done.18.theirs), custom_call_target="tpu_custom_call" | custom-call | flops 1000 | bytes 1000 | tf_op jit(solution)/shard_map/joined/pallas_call | solution.py:379
  (19 shorter events, 0.0 us)
Async XLA Ops:
  0.6 20.0 %collective-permute-start.3 = (bf16[320,8192]{1,0:T(8,128)(2,1)}, bf16[320,8192]{1,0:T(8,128)(2,1)}, u32[]{:S(2)}, u32[]{:S(2)}) collective-permute-start(bf16[320,8192]{1,0:T(8,128)(2,1)} %bitcast.16), channel_id=1, source_target_pairs={{0,1},{1,0},{2,3},{3,2},{4,5},{5,4},{6,7},{7,6},{8,9},{9,8},{10,11... | collective-permute-start | bytes 15728648 | tf_op jit(solution)/shard_map/ppermute | solution.py:66
  2.5 15.2 %collective-permute-start = (bf16[256,1024]{1,0:T(8,128)(2,1)S(1)}, bf16[256,1024]{1,0:T(8,128)(2,1)S(1)}, u32[]{:S(2)}, u32[]{:S(2)}) collective-permute-start(bf16[256,1024]{1,0:T(8,128)(2,1)S(1)} %pad_maximum_fusion.refs_0_), channel_id=1, source_target_pairs={{0,4},{1,5},{2,6},{3,7},{4,0},{5,1},{6,2},{7,3},{8,12},{9,13},{10,... | collective-permute-start | bytes 1572872 | tf_op jit(solution)/shard_map/ppermute | solution.py:66
  5.1 12.6 %collective-permute-start.1 = (bf16[256,1024]{1,0:T(8,128)(2,1)S(1)}, bf16[256,1024]{1,0:T(8,128)(2,1)}, u32[]{:S(2)}, u32[]{:S(2)}) collective-permute-start(bf16[256,1024]{1,0:T(8,128)(2,1)S(1)} %pad_maximum_fusion.refs_0_), channel_id=1, source_target_pairs={{4,8},{5,9},{6,10},{7,11},{8,4},{9,5},{10,6},{11,7},{20,24},{21,25... | collective-permute-start | bytes 1572872 | tf_op jit(solution)/shard_map/ppermute | solution.py:66
  6.6 14.0 %collective-permute-start.2 = (bf16[256,1024]{1,0:T(8,128)(2,1)S(1)}, bf16[256,1024]{1,0:T(8,128)(2,1)S(1)}, u32[]{:S(2)}, u32[]{:S(2)}) collective-permute-start(bf16[256,1024]{1,0:T(8,128)(2,1)S(1)} %pad_maximum_fusion.refs_0_), channel_id=1, source_target_pairs={{0,2},{1,3},{2,0},{3,1},{4,6},{5,7},{6,4},{7,5},{8,10},{9,11},{10,... | collective-permute-start | bytes 1572872 | tf_op jit(solution)/shard_map/ppermute | solution.py:66
  17.7 18.2 %collective-permute-start.6 = (bf16[256,1024]{1,0:T(8,128)(2,1)}, bf16[256,1024]{1,0:T(8,128)(2,1)}, u32[]{:S(2)}, u32[]{:S(2)}) collective-permute-start(bf16[256,1024]{1,0:T(8,128)(2,1)} %collective-permute-done.1), channel_id=1, source_target_pairs={{4,0},{5,1},{6,2},{7,3},{8,12},{9,13},{10,14},{11,15},{20,16},{21,... | collective-permute-start | bytes 1572872 | tf_op jit(solution)/shard_map/ppermute | solution.py:66
  19.0 16.9 %collective-permute-start.5 = (bf16[256,1024]{1,0:T(8,128)(2,1)S(1)}, bf16[256,1024]{1,0:T(8,128)(2,1)}, u32[]{:S(2)}, u32[]{:S(2)}) collective-permute-start(bf16[256,1024]{1,0:T(8,128)(2,1)S(1)} %collective-permute-done.refs_4_), channel_id=1, source_target_pairs={{4,8},{5,9},{6,10},{7,11},{8,4},{9,5},{10,6},{11,7},{20,24},{21,25... | collective-permute-start | bytes 1572872 | tf_op jit(solution)/shard_map/ppermute | solution.py:66
  20.6 25.1 %collective-permute-start.8 = (bf16[256,1024]{1,0:T(8,128)(2,1)S(1)}, bf16[256,1024]{1,0:T(8,128)(2,1)S(1)}, u32[]{:S(2)}, u32[]{:S(2)}) collective-permute-start(bf16[256,1024]{1,0:T(8,128)(2,1)S(1)} %collective-permute-done.refs_4_), channel_id=1, source_target_pairs={{0,2},{1,3},{2,0},{3,1},{4,6},{5,7},{6,4},{7,5},{8,10},{9,11},{10,... | collective-permute-start | bytes 1572872 | tf_op jit(solution)/shard_map/ppermute | solution.py:66
  22.2 23.6 %collective-permute-start.4 = (bf16[256,1024]{1,0:T(8,128)(2,1)S(1)}, bf16[256,1024]{1,0:T(8,128)(2,1)S(1)}, u32[]{:S(2)}, u32[]{:S(2)}) collective-permute-start(bf16[256,1024]{1,0:T(8,128)(2,1)S(1)} %collective-permute-done.2.refs_2_), channel_id=1, source_target_pairs={{0,16},{1,17},{2,18},{3,19},{4,20},{5,21},{6,22},{7,23},{8,24},{9,... | collective-permute-start | bytes 1572872 | tf_op jit(solution)/shard_map/ppermute | solution.py:66
  35.9 16.6 %collective-permute-start.7 = (bf16[256,1024]{1,0:T(8,128)(2,1)}, bf16[256,1024]{1,0:T(8,128)(2,1)S(1)}, u32[]{:S(2)}, u32[]{:S(2)}) collective-permute-start(bf16[256,1024]{1,0:T(8,128)(2,1)} %collective-permute-done.5), channel_id=1, source_target_pairs={{4,0},{5,1},{6,2},{7,3},{8,12},{9,13},{10,14},{11,15},{20,16},{21,... | collective-permute-start | bytes 1572872 | tf_op jit(solution)/shard_map/ppermute | solution.py:66
  45.7 22.7 %copy-start = (bf16[16,320,256]{2,1,0:T(8,128)(2,1)S(1)}, bf16[16,320,256]{2,1,0:T(8,128)(2,1)}, u32[]{:S(2)}) copy-start(bf16[16,320,256]{2,1,0:T(8,128)(2,1)} %get-tuple-element.45.mine) | copy-start | bytes 7864324
  45.7 22.7 %copy-start.10 = (s32[11]{0:T(128)S(1)}, s32[11]{0:T(128)}, u32[]{:S(2)}) copy-start(s32[11]{0:T(128)} %stack.47.place) | copy-start | bytes 136
  47.0 13.0 %collective-permute-start.10 = (bf16[256,1024]{1,0:T(8,128)(2,1)S(1)}, bf16[256,1024]{1,0:T(8,128)(2,1)S(1)}, u32[]{:S(2)}, u32[]{:S(2)}) collective-permute-start(bf16[256,1024]{1,0:T(8,128)(2,1)S(1)} %broadcast_select_fusion.1.refs_0_), channel_id=1, source_target_pairs={{0,2},{1,3},{2,0},{3,1},{4,6},{5,7},{6,4},{7,5},{8,10},{9,11},{10,... | collective-permute-start | bytes 1572872 | tf_op jit(solution)/shard_map/ppermute | solution.py:66
  48.6 12.7 %collective-permute-start.12 = (bf16[256,1024]{1,0:T(8,128)(2,1)S(1)}, bf16[256,1024]{1,0:T(8,128)(2,1)S(1)}, u32[]{:S(2)}, u32[]{:S(2)}) collective-permute-start(bf16[256,1024]{1,0:T(8,128)(2,1)S(1)} %broadcast_select_fusion.1.refs_0_), channel_id=1, source_target_pairs={{0,16},{1,17},{2,18},{3,19},{4,20},{5,21},{6,22},{7,23},{8,24},{9,... | collective-permute-start | bytes 1572872 | tf_op jit(solution)/shard_map/ppermute | solution.py:66
  52.5 12.2 %collective-permute-start.9 = (bf16[256,1024]{1,0:T(8,128)(2,1)S(1)}, bf16[256,1024]{1,0:T(8,128)(2,1)S(1)}, u32[]{:S(2)}, u32[]{:S(2)}) collective-permute-start(bf16[256,1024]{1,0:T(8,128)(2,1)S(1)} %pad_maximum_fusion.1.refs_1_), channel_id=1, source_target_pairs={{0,4},{1,5},{2,6},{3,7},{4,0},{5,1},{6,2},{7,3},{8,12},{9,13},{10,... | collective-permute-start | bytes 1572872 | tf_op jit(solution)/shard_map/ppermute | solution.py:66
  61.4 12.3 %collective-permute-start.13 = (bf16[256,1024]{1,0:T(8,128)(2,1)S(1)}, bf16[256,1024]{1,0:T(8,128)(2,1)S(1)}, u32[]{:S(2)}, u32[]{:S(2)}) collective-permute-start(bf16[256,1024]{1,0:T(8,128)(2,1)S(1)} %broadcast_select_fusion.refs_3_), channel_id=1, source_target_pairs={{0,16},{1,17},{2,18},{3,19},{4,20},{5,21},{6,22},{7,23},{8,24},{9,... | collective-permute-start | bytes 1572872 | tf_op jit(solution)/shard_map/ppermute | solution.py:66
  62.9 12.1 %collective-permute-start.14 = (bf16[256,1024]{1,0:T(8,128)(2,1)S(1)}, bf16[256,1024]{1,0:T(8,128)(2,1)S(1)}, u32[]{:S(2)}, u32[]{:S(2)}) collective-permute-start(bf16[256,1024]{1,0:T(8,128)(2,1)S(1)} %broadcast_select_fusion.refs_3_), channel_id=1, source_target_pairs={{0,2},{1,3},{2,0},{3,1},{4,6},{5,7},{6,4},{7,5},{8,10},{9,11},{10,... | collective-permute-start | bytes 1572872 | tf_op jit(solution)/shard_map/ppermute | solution.py:66
  64.7 15.4 %collective-permute-start.11 = (bf16[256,1024]{1,0:T(8,128)(2,1)S(1)}, bf16[256,1024]{1,0:T(8,128)(2,1)S(1)}, u32[]{:S(2)}, u32[]{:S(2)}) collective-permute-start(bf16[256,1024]{1,0:T(8,128)(2,1)S(1)} %collective-permute-done.4.refs_3_), channel_id=1, source_target_pairs={{0,4},{1,5},{2,6},{3,7},{4,0},{5,1},{6,2},{7,3},{8,12},{9,13},{10,... | collective-permute-start | bytes 1572872 | tf_op jit(solution)/shard_map/ppermute | solution.py:66
  68.4 1.7 %copy-start.1 = (bf16[16,320,256]{2,1,0:T(8,128)(2,1)S(1)}, bf16[16,320,256]{2,1,0:T(8,128)(2,1)}, u32[]{:S(2)}) copy-start(bf16[16,320,256]{2,1,0:T(8,128)(2,1)} %get-tuple-element.37.other) | copy-start | bytes 7864324
  70.1 5.7 %copy-start.2 = (bf16[16,320,256]{2,1,0:T(8,128)(2,1)S(1)}, bf16[16,320,256]{2,1,0:T(8,128)(2,1)}, u32[]{:S(2)}) copy-start(bf16[16,320,256]{2,1,0:T(8,128)(2,1)} %get-tuple-element.37.other) | copy-start | bytes 7864324
  75.0 10.6 %collective-permute-start.16 = (bf16[256,1024]{1,0:T(8,128)(2,1)S(1)}, bf16[256,1024]{1,0:T(8,128)(2,1)S(1)}, u32[]{:S(2)}, u32[]{:S(2)}) collective-permute-start(bf16[256,1024]{1,0:T(8,128)(2,1)S(1)} %collective-permute-done.13.refs_5_), channel_id=1, source_target_pairs={{0,2},{1,3},{2,0},{3,1},{4,6},{5,7},{6,4},{7,5},{8,10},{9,11},{10,... | collective-permute-start | bytes 1572872 | tf_op jit(solution)/shard_map/ppermute | solution.py:66
  75.3 10.4 %collective-permute-start.15 = (bf16[256,1024]{1,0:T(8,128)(2,1)S(1)}, bf16[256,1024]{1,0:T(8,128)(2,1)S(1)}, u32[]{:S(2)}, u32[]{:S(2)}) collective-permute-start(bf16[256,1024]{1,0:T(8,128)(2,1)S(1)} %collective-permute-done.10.refs_2_), channel_id=1, source_target_pairs={{0,16},{1,17},{2,18},{3,19},{4,20},{5,21},{6,22},{7,23},{8,24},{9,... | collective-permute-start | bytes 1572872 | tf_op jit(solution)/shard_map/ppermute | solution.py:66
  85.7 5.6 %copy-start.3 = (f32[64,128]{1,0:T(8,128)S(1)}, f32[64,128]{1,0:T(8,128)}, u32[]{:S(2)}) copy-start(f32[64,128]{1,0:T(8,128)} %constant.70.clone.refs_4_.refs_2_) | copy-start | bytes 98308
  85.7 5.6 %copy-start.4 = (f32[64,128]{1,0:T(8,128)S(1)}, f32[64,128]{1,0:T(8,128)}, u32[]{:S(2)}) copy-start(f32[64,128]{1,0:T(8,128)} %constant.71.clone.refs_5_.refs_3_) | copy-start | bytes 98308
  85.7 5.6 %copy-start.5 = (f32[41,128]{1,0:T(8,128)S(1)}, f32[41,128]{1,0:T(8,128)}, u32[]{:S(2)}) copy-start(f32[41,128]{1,0:T(8,128)} %constant.68.clone.refs_2_.refs_0_) | copy-start | bytes 62980
  85.7 5.6 %copy-start.6 = (f32[41,128]{1,0:T(8,128)S(1)}, f32[41,128]{1,0:T(8,128)}, u32[]{:S(2)}) copy-start(f32[41,128]{1,0:T(8,128)} %constant.69.clone.refs_3_.refs_1_) | copy-start | bytes 62980
  85.7 5.6 %copy-start.7 = (f32[160,128]{1,0:T(8,128)S(1)}, f32[160,128]{1,0:T(8,128)}, u32[]{:S(2)}) copy-start(f32[160,128]{1,0:T(8,128)} %constant.72.clone.refs_6_) | copy-start | bytes 245764
  85.7 5.6 %copy-start.8 = (f32[160,128]{1,0:T(8,128)S(1)}, f32[160,128]{1,0:T(8,128)}, u32[]{:S(2)}) copy-start(f32[160,128]{1,0:T(8,128)} %constant.73.clone.refs_7_) | copy-start | bytes 245764
  85.7 5.5 %copy-start.13 = (s32[2]{0:T(128)S(1)}, s32[2]{0:T(128)}, u32[]{:S(2)}) copy-start(s32[2]{0:T(128)} %lengths.3) | copy-start | bytes 28
  85.7 5.5 %copy-start.14 = (s32[8]{0:T(128)S(1)}, s32[8]{0:T(128)}, u32[]{:S(2)}) copy-start(s32[8]{0:T(128)} %owner.3) | copy-start | bytes 100
  88.1 3.1 %collective-permute-start.17 = (f32[320,1024]{1,0:T(8,128)S(1)}, f32[320,1024]{1,0:T(8,128)S(1)}, u32[]{:S(2)}, u32[]{:S(2)}) collective-permute-start(f32[320,1024]{1,0:T(8,128)S(1)} %get-tuple-element.47), channel_id=1, source_target_pairs={{0,1},{1,0},{2,3},{3,2},{4,5},{5,4},{6,7},{7,6},{8,9},{9,8},{10,11... | collective-permute-start | bytes 3932168 | tf_op jit(solution)/shard_map/ppermute | solution.py:66
  92.3 25.0 %copy-start.9 = (bf16[8,4,1024]{2,1,0:T(4,128)(2,1)S(1)}, bf16[8,4,1024]{2,1,0:T(4,128)(2,1)}, u32[]{:S(2)}) copy-start(bf16[8,4,1024]{2,1,0:T(4,128)(2,1)} %dec_query.1) | copy-start | bytes 196612
  92.3 25.0 %copy-start.11 = (bf16[8,4,128]{2,1,0:T(4,128)(2,1)S(1)}, bf16[8,4,128]{2,1,0:T(4,128)(2,1)}, u32[]{:S(2)}) copy-start(bf16[8,4,128]{2,1,0:T(4,128)(2,1)} %dec_key.1) | copy-start | bytes 24580
  92.3 25.0 %copy-start.12 = (bf16[8,4,128]{2,1,0:T(4,128)(2,1)S(1)}, bf16[8,4,128]{2,1,0:T(4,128)(2,1)}, u32[]{:S(2)}) copy-start(bf16[8,4,128]{2,1,0:T(4,128)(2,1)} %dec_value.1) | copy-start | bytes 24580
  118.5 1.3 %collective-permute-start.18 = (f32[32,256]{1,0:T(8,128)S(1)}, f32[32,256]{1,0:T(8,128)S(1)}, u32[]{:S(2)}, u32[]{:S(2)}) collective-permute-start(f32[32,256]{1,0:T(8,128)S(1)} %decode.1.mine), channel_id=1, source_target_pairs={{0,1},{1,0},{2,3},{3,2},{4,5},{5,4},{6,7},{7,6},{8,9},{9,8},{10,11... | collective-permute-start | bytes 98312 | tf_op jit(solution)/shard_map/ppermute | solution.py:66

commit v20 on v19

--- a/solution.py
+++ b/solution.py
@@ -461,7 +461,7 @@
         near_y = moved(after(near, *rows), to_row)
         across_x = moved(after(across, *rows), to_group)
         mine, other = prepared(place, after(flat, *rows), raw, seq // 2)
-        layers, rows = (passed, middle_c), (near_y, across_x, mine, passed)
+        layers, rows = (passed, middle_c, mine), (near_y, across_x, mine, passed)
         far = moved(after(middle_c, *layers), to_end)
         block_b = jnp.where(is_end, after(passed, *rows), middle)
         block_yb = moved(block_b, to_row)

time: 121 us -> 115 us (0.950)
  blocking collectives: 25 us -> 22 us
  waiting for transfers between devices: 41.8 us -> 39.5 us
    all_to_all x1, blocking collectives: 25 us -> 22 us  [body(): lax.all_to_all(outgoing, 'seq', split_axis=0, concat_axis=1, tiled=True)]
    ppermute x19, waiting for transfers between devices: 41.8 us -> 39.5 us  [moved(): return lax.ppermute(block, ('groups', 'seq'), route)]
  transfers between devices with their start and end apart: 19 -> 19, of which waited for: 10 -> 9; matrix products, arithmetic and copies ran while one was open for 3% -> 3% of each run, Pallas kernels for 14% -> 15%
where the time goes in v20:
time: 115 us
  waiting for transfers between devices  39.5 us (34%)
  starting transfers between devices  24.3 us (21%)
  Pallas kernels  23 us (20%)
  blocking collectives  22 us (19%)
  local copies, waits for them, and re-layouts  3.73 us (3%)
  other arithmetic  1.3 us (1%)
    ppermute x19, waiting for transfers between devices, moved(): return lax.ppermute(block, ('groups', 'seq'), route)  39.5 us
    ppermute x19, starting transfers between devices, moved(): return lax.ppermute(block, ('groups', 'seq'), route)  24.3 us
    all_to_all x1, blocking collectives, body(): lax.all_to_all(outgoing, 'seq', split_axis=0, concat_axis=1, tiled=True)  22 us
    pallas_call x3, Pallas kernels, product(): pl.pallas_call(functools.partial(product_kernel, plan, group, bool(totals...  10.2 us
    pallas_call x1, Pallas kernels, prepared(): pl.pallas_call(prepare_kernel, grid_spec=pltpu.PrefetchScalarGridSpec(num...  8.5 us
  transfers between devices with their start and end apart: 19, of which 9 were waited for; matrix products, arithmetic and copies ran while one was open for 3% of the time, Pallas kernels for 15%

profile of v20, /device:TPU:0, one launch (start us, length us, event | category | flops | bytes accessed | tf_op | source)
XLA Modules:
  0.0 114.7 jit_solution(18169607876276799424)
XLA Ops:
  0.6 0.5 collective-permute-start.3
  1.1 1.3 %constant_dynamic-slice_fusion = (bf16[256,512]{1,0:T(8,128)(2,1)S(1)}, bf16[256,512]{1,0:T(8,128)(2,1)S(1)}, bf16[256,512]{1,0:T(8,128)(2,1)S(1)}, bf16[256,512]{1,0:T(8,128)(2,1)S(1)}) fusion(bf16[512,512]{1,0:T(8,128)(2,1)} %param.16, s32[]{:T(128)S(6)} %select_n.52, s32[]{:T(128)S(6)} %select_n.51, bf16[512,512]{1,0:T(8,128)(2,1)} %param.15), kind=kLoop, calls=%fused_computation.4 | loop fusion | bytes 2097160 | tf_op jit(solution)/shard_map/dynamic_slice | solution.py:446
  2.4 0.1 pad_maximum_fusion.refs_0_
  2.5 1.4 %collective-permute-start.1 = (bf16[256,1024]{1,0:T(8,128)(2,1)S(1)}, bf16[256,1024]{1,0:T(8,128)(2,1)}, u32[]{:S(2)}, u32[]{:S(2)}) collective-permute-start(bf16[256,1024]{1,0:T(8,128)(2,1)S(1)} %pad_maximum_fusion.refs_0_), channel_id=1, source_target_pairs={{4,8},{5,9},{6,10},{7,11},{8,4},{9,5},{10,6},{11,7},{20,24},{21,25... | collective-permute-start | bytes 1572872 | tf_op jit(solution)/shard_map/ppermute | solution.py:66
  3.9 4.7 %collective-permute-start = (bf16[256,1024]{1,0:T(8,128)(2,1)S(1)}, bf16[256,1024]{1,0:T(8,128)(2,1)S(1)}, u32[]{:S(2)}, u32[]{:S(2)}) collective-permute-start(bf16[256,1024]{1,0:T(8,128)(2,1)S(1)} %pad_maximum_fusion.refs_0_), channel_id=1, source_target_pairs={{0,4},{1,5},{2,6},{3,7},{4,0},{5,1},{6,2},{7,3},{8,12},{9,13},{10,... | collective-permute-start | bytes 1572872 | tf_op jit(solution)/shard_map/ppermute | solution.py:66
  8.6 1.5 %collective-permute-start.2 = (bf16[256,1024]{1,0:T(8,128)(2,1)S(1)}, bf16[256,1024]{1,0:T(8,128)(2,1)S(1)}, u32[]{:S(2)}, u32[]{:S(2)}) collective-permute-start(bf16[256,1024]{1,0:T(8,128)(2,1)S(1)} %pad_maximum_fusion.refs_0_), channel_id=1, source_target_pairs={{0,2},{1,3},{2,0},{3,1},{4,6},{5,7},{6,4},{7,5},{8,10},{9,11},{10,... | collective-permute-start | bytes 1572872 | tf_op jit(solution)/shard_map/ppermute | solution.py:66
  10.2 0.1 pad_maximum_fusion.1.refs_1_
  10.2 0.0 collective-permute-done.1
  10.2 10.7 %collective-permute-done.refs_4_ = bf16[256,1024]{1,0:T(8,128)(2,1)S(1)} collective-permute-done((bf16[256,1024]{1,0:T(8,128)(2,1)S(1)}, bf16[256,1024]{1,0:T(8,128)(2,1)S(1)}, u32[]{:S(2)}, u32[]{:S(2)}) %collective-permute-start) | collective-permute-done | bytes 524320 | tf_op jit(solution)/shard_map/ppermute | solution.py:66
  20.9 1.5 %collective-permute-start.5 = (bf16[256,1024]{1,0:T(8,128)(2,1)S(1)}, bf16[256,1024]{1,0:T(8,128)(2,1)}, u32[]{:S(2)}, u32[]{:S(2)}) collective-permute-start(bf16[256,1024]{1,0:T(8,128)(2,1)S(1)} %collective-permute-done.refs_4_), channel_id=1, source_target_pairs={{4,8},{5,9},{6,10},{7,11},{8,4},{9,5},{10,6},{11,7},{20,24},{21,25... | collective-permute-start | bytes 1572872 | tf_op jit(solution)/shard_map/ppermute | solution.py:66
  22.4 1.3 %collective-permute-start.6 = (bf16[256,1024]{1,0:T(8,128)(2,1)}, bf16[256,1024]{1,0:T(8,128)(2,1)}, u32[]{:S(2)}, u32[]{:S(2)}) collective-permute-start(bf16[256,1024]{1,0:T(8,128)(2,1)} %collective-permute-done.1), channel_id=1, source_target_pairs={{4,0},{5,1},{6,2},{7,3},{8,12},{9,13},{10,14},{11,15},{20,16},{21,... | collective-permute-start | bytes 1572872 | tf_op jit(solution)/shard_map/ppermute | solution.py:66
  23.7 0.0 collective-permute-done.2.refs_2_
  23.7 0.0 collective-permute-done.3.refs_1_
  23.7 1.6 %collective-permute-start.4 = (bf16[256,1024]{1,0:T(8,128)(2,1)S(1)}, bf16[256,1024]{1,0:T(8,128)(2,1)S(1)}, u32[]{:S(2)}, u32[]{:S(2)}) collective-permute-start(bf16[256,1024]{1,0:T(8,128)(2,1)S(1)} %collective-permute-done.2.refs_2_), channel_id=1, source_target_pairs={{0,16},{1,17},{2,18},{3,19},{4,20},{5,21},{6,22},{7,23},{8,24},{9,... | collective-permute-start | bytes 1572872 | tf_op jit(solution)/shard_map/ppermute | solution.py:66
  25.2 1.5 %collective-permute-start.8 = (bf16[256,1024]{1,0:T(8,128)(2,1)S(1)}, bf16[256,1024]{1,0:T(8,128)(2,1)S(1)}, u32[]{:S(2)}, u32[]{:S(2)}) collective-permute-start(bf16[256,1024]{1,0:T(8,128)(2,1)S(1)} %collective-permute-done.refs_4_), channel_id=1, source_target_pairs={{0,2},{1,3},{2,0},{3,1},{4,6},{5,7},{6,4},{7,5},{8,10},{9,11},{10,... | collective-permute-start | bytes 1572872 | tf_op jit(solution)/shard_map/ppermute | solution.py:66
  26.8 0.7 stack.47.place
  27.4 8.5 %normed_halves.1 = (bf16[16,320,256]{2,1,0:T(8,128)(2,1)}, bf16[16,320,256]{2,1,0:T(8,128)(2,1)}) custom-call(s32[11]{0:T(128)} %stack.47.place, bf16[320,8192]{1,0:T(8,128)(2,1)} %bitcast.17, bf16[320,8192]{1,0:T(8,128)(2,1)} %collective-permute-done.3.refs_1_), custom_call_target="tpu_custom_call" | custom-call | flops 1000 | bytes 1000 | tf_op jit(solution)/shard_map/normed_halves/pallas_call | solution.py:137
  35.9 0.0 collective-permute-done.5
  35.9 2.2 %collective-permute-done.6 = bf16[256,1024]{1,0:T(8,128)(2,1)} collective-permute-done((bf16[256,1024]{1,0:T(8,128)(2,1)}, bf16[256,1024]{1,0:T(8,128)(2,1)}, u32[]{:S(2)}, u32[]{:S(2)}) %collective-permute-start.6) | collective-permute-done | bytes 524320 | tf_op jit(solution)/shard_map/ppermute | solution.py:66
  38.1 1.5 %collective-permute-start.7 = (bf16[256,1024]{1,0:T(8,128)(2,1)}, bf16[256,1024]{1,0:T(8,128)(2,1)S(1)}, u32[]{:S(2)}, u32[]{:S(2)}) collective-permute-start(bf16[256,1024]{1,0:T(8,128)(2,1)} %collective-permute-done.5), channel_id=1, source_target_pairs={{4,0},{5,1},{6,2},{7,3},{8,12},{9,13},{10,14},{11,15},{20,16},{21,... | collective-permute-start | bytes 1572872 | tf_op jit(solution)/shard_map/ppermute | solution.py:66
  39.6 0.0 collective-permute-done.4.refs_3_
  39.7 0.0 collective-permute-done.8.refs_5_
  39.7 1.1 broadcast_select_fusion.1.refs_0_
  40.8 1.6 %collective-permute-start.12 = (bf16[256,1024]{1,0:T(8,128)(2,1)S(1)}, bf16[256,1024]{1,0:T(8,128)(2,1)S(1)}, u32[]{:S(2)}, u32[]{:S(2)}) collective-permute-start(bf16[256,1024]{1,0:T(8,128)(2,1)S(1)} %broadcast_select_fusion.1.refs_0_), channel_id=1, source_target_pairs={{0,16},{1,17},{2,18},{3,19},{4,20},{5,21},{6,22},{7,23},{8,24},{9,... | collective-permute-start | bytes 1572872 | tf_op jit(solution)/shard_map/ppermute | solution.py:66
  42.3 1.5 %collective-permute-start.10 = (bf16[256,1024]{1,0:T(8,128)(2,1)S(1)}, bf16[256,1024]{1,0:T(8,128)(2,1)S(1)}, u32[]{:S(2)}, u32[]{:S(2)}) collective-permute-start(bf16[256,1024]{1,0:T(8,128)(2,1)S(1)} %broadcast_select_fusion.1.refs_0_), channel_id=1, source_target_pairs={{0,2},{1,3},{2,0},{3,1},{4,6},{5,7},{6,4},{7,5},{8,10},{9,11},{10,... | collective-permute-start | bytes 1572872 | tf_op jit(solution)/shard_map/ppermute | solution.py:66
  43.9 9.2 %collective-permute-done.7 = bf16[256,1024]{1,0:T(8,128)(2,1)S(1)} collective-permute-done((bf16[256,1024]{1,0:T(8,128)(2,1)}, bf16[256,1024]{1,0:T(8,128)(2,1)S(1)}, u32[]{:S(2)}, u32[]{:S(2)}) %collective-permute-start.7) | collective-permute-done | bytes 524320 | tf_op jit(solution)/shard_map/ppermute | solution.py:66
  53.1 0.0 collective-permute-start.9
  53.1 0.4 collective-permute-done.12.refs_1_
  53.5 1.2 %collective-permute-done.10.refs_2_ = bf16[256,1024]{1,0:T(8,128)(2,1)S(1)} collective-permute-done((bf16[256,1024]{1,0:T(8,128)(2,1)S(1)}, bf16[256,1024]{1,0:T(8,128)(2,1)S(1)}, u32[]{:S(2)}, u32[]{:S(2)}) %collective-permute-start.10) | collective-permute-done | bytes 524320 | tf_op jit(solution)/shard_map/ppermute | solution.py:66
  54.7 0.1 broadcast_select_fusion.refs_3_
  54.7 1.6 %collective-permute-start.14 = (bf16[256,1024]{1,0:T(8,128)(2,1)S(1)}, bf16[256,1024]{1,0:T(8,128)(2,1)S(1)}, u32[]{:S(2)}, u32[]{:S(2)}) collective-permute-start(bf16[256,1024]{1,0:T(8,128)(2,1)S(1)} %broadcast_select_fusion.refs_3_), channel_id=1, source_target_pairs={{0,2},{1,3},{2,0},{3,1},{4,6},{5,7},{6,4},{7,5},{8,10},{9,11},{10,... | collective-permute-start | bytes 1572872 | tf_op jit(solution)/shard_map/ppermute | solution.py:66
  56.3 0.5 collective-permute-start.13
  56.9 8.3 %collective-permute-done.9.refs_4_ = bf16[256,1024]{1,0:T(8,128)(2,1)S(1)} collective-permute-done((bf16[256,1024]{1,0:T(8,128)(2,1)S(1)}, bf16[256,1024]{1,0:T(8,128)(2,1)S(1)}, u32[]{:S(2)}, u32[]{:S(2)}) %collective-permute-start.9) | collective-permute-done | bytes 524320 | tf_op jit(solution)/shard_map/ppermute | solution.py:66
  65.2 0.0 collective-permute-start.11
  65.2 0.0 copy-done
  65.2 1.7 %copy-done.1 = bf16[16,320,256]{2,1,0:T(8,128)(2,1)S(1)} copy-done((bf16[16,320,256]{2,1,0:T(8,128)(2,1)S(1)}, bf16[16,320,256]{2,1,0:T(8,128)(2,1)}, u32[]{:S(2)}) %copy-start.1) | copy-done | bytes 2621464
  66.9 3.5 %add_product.3 = (f32[320,1024]{1,0:T(8,128)S(1)}, f32[320,1024]{1,0:T(8,128)S(1)}) custom-call(s32[11]{0:T(128)S(1)} %copy-done.10, bf16[16,320,256]{2,1,0:T(8,128)(2,1)S(1)} %copy-done, bf16[16,320,256]{2,1,0:T(8,128)(2,1)S(1)} %copy-done.1, bf16[256,1024]{1,0:T(8,128)(2,1)S(1)} %pad_maximum_fusion.refs_0_, ...), custom_call_target="tpu_custom_call" | custom-call | flops 1000 | bytes 1000 | tf_op jit(solution)/shard_map/add_product/pallas_call | solution.py:204
  70.4 0.0 collective-permute-done.14.refs_6_
  70.4 0.0 collective-permute-done.13.refs_5_
  70.4 1.6 %collective-permute-start.15 = (bf16[256,1024]{1,0:T(8,128)(2,1)S(1)}, bf16[256,1024]{1,0:T(8,128)(2,1)S(1)}, u32[]{:S(2)}, u32[]{:S(2)}) collective-permute-start(bf16[256,1024]{1,0:T(8,128)(2,1)S(1)} %collective-permute-done.10.refs_2_), channel_id=1, source_target_pairs={{0,16},{1,17},{2,18},{3,19},{4,20},{5,21},{6,22},{7,23},{8,24},{9,... | collective-permute-start | bytes 1572872 | tf_op jit(solution)/shard_map/ppermute | solution.py:66
  72.0 1.5 %collective-permute-start.16 = (bf16[256,1024]{1,0:T(8,128)(2,1)S(1)}, bf16[256,1024]{1,0:T(8,128)(2,1)S(1)}, u32[]{:S(2)}, u32[]{:S(2)}) collective-permute-start(bf16[256,1024]{1,0:T(8,128)(2,1)S(1)} %collective-permute-done.13.refs_5_), channel_id=1, source_target_pairs={{0,2},{1,3},{2,0},{3,1},{4,6},{5,7},{6,4},{7,5},{8,10},{9,11},{10,... | collective-permute-start | bytes 1572872 | tf_op jit(solution)/shard_map/ppermute | solution.py:66
  73.5 0.0 copy-done.2
  73.5 4.3 %add_product.4 = (f32[320,1024]{1,0:T(8,128)S(1)}, f32[320,1024]{1,0:T(8,128)S(1)}) custom-call(s32[11]{0:T(128)S(1)} %copy-done.10, bf16[16,320,256]{2,1,0:T(8,128)(2,1)S(1)} %copy-done, bf16[16,320,256]{2,1,0:T(8,128)(2,1)S(1)} %copy-done.2, bf16[256,1024]{1,0:T(8,128)(2,1)S(1)} %broadcast_select_fusion.1.refs_0_, ...), custom_call_target="tpu_custom_call" | custom-call | flops 1000 | bytes 1000 | tf_op jit(solution)/shard_map/add_product/pallas_call | solution.py:204
  77.9 0.0 collective-permute-done.11.refs_0_
  77.9 3.3 %collective-permute-done.15.refs_1_ = bf16[256,1024]{1,0:T(8,128)(2,1)S(1)} collective-permute-done((bf16[256,1024]{1,0:T(8,128)(2,1)S(1)}, bf16[256,1024]{1,0:T(8,128)(2,1)S(1)}, u32[]{:S(2)}, u32[]{:S(2)}) %collective-permute-start.15) | collective-permute-done | bytes 524320 | tf_op jit(solution)/shard_map/ppermute | solution.py:66
  81.2 1.2 %collective-permute-done.16.refs_2_ = bf16[256,1024]{1,0:T(8,128)(2,1)S(1)} collective-permute-done((bf16[256,1024]{1,0:T(8,128)(2,1)S(1)}, bf16[256,1024]{1,0:T(8,128)(2,1)S(1)}, u32[]{:S(2)}, u32[]{:S(2)}) %collective-permute-start.16) | collective-permute-done | bytes 524320 | tf_op jit(solution)/shard_map/ppermute | solution.py:66
  82.4 0.0 copy-start.7
  82.4 0.0 copy-start.8
  82.4 0.0 copy-start.13
  82.4 0.0 copy-start.14
  82.4 2.4 %add_product.5 = (f32[320,1024]{1,0:T(8,128)S(1)}, f32[320,1024]{1,0:T(8,128)S(1)}) custom-call(s32[11]{0:T(128)S(1)} %copy-done.10, bf16[16,320,256]{2,1,0:T(8,128)(2,1)S(1)} %copy-done, bf16[16,320,256]{2,1,0:T(8,128)(2,1)S(1)} %copy-done.2, bf16[256,1024]{1,0:T(8,128)(2,1)S(1)} %collective-permute-done.11.refs_0_, ...), custom_call_target="tpu_custom_call" | custom-call | flops 1000 | bytes 1000 | tf_op jit(solution)/shard_map/add_product/pallas_call | solution.py:204
  84.8 0.1 collective-permute-start.17
  84.9 3.0 %collective-permute-done.17.refs_1_ = f32[320,1024]{1,0:T(8,128)S(1)} collective-permute-done((f32[320,1024]{1,0:T(8,128)S(1)}, f32[320,1024]{1,0:T(8,128)S(1)}, u32[]{:S(2)}, u32[]{:S(2)}) %collective-permute-start.17) | collective-permute-done | bytes 1310752 | tf_op jit(solution)/shard_map/ppermute | solution.py:66
  87.9 0.0 copy-done.3
  88.0 1.1 cache_rows.1
  89.0 0.0 copy-start.9
  89.0 0.0 copy-start.11
  89.1 0.0 copy-start.12
  89.1 22.0 %all_to_all.4 = bf16[16,80,256]{2,1,0:T(8,128)(2,1)S(1)} all-to-all(bf16[16,80,256]{2,1,0:T(8,128)(2,1)S(1)} %cache_rows.1), channel_id=1, replica_groups=mesh['groups'=2,'seq'=16] {'seq'}, dimensions={0} | all-to-all | bytes 1310720 | tf_op jit(solution)/shard_map/all_to_all | solution.py:488
  111.0 1.1 decode.1.mine
  112.1 0.4 collective-permute-start.18
  112.5 0.8 copied.1
  113.4 0.0 collective-permute-done.18.theirs
  113.4 1.3 %joined.1 = bf16[4,512]{1,0:T(4,128)(2,1)} custom-call(s32[11]{0:T(128)S(1)} %copy-done.10, f32[32,256]{1,0:T(8,128)S(1)} %decode.1.mine, f32[32,256]{1,0:T(8,128)S(1)} %collective-permute-done.18.theirs), custom_call_target="tpu_custom_call" | custom-call | flops 1000 | bytes 1000 | tf_op jit(solution)/shard_map/joined/pallas_call | solution.py:379
  (19 shorter events, 0.0 us)
Async XLA Ops:
  0.6 23.0 %collective-permute-start.3 = (bf16[320,8192]{1,0:T(8,128)(2,1)}, bf16[320,8192]{1,0:T(8,128)(2,1)}, u32[]{:S(2)}, u32[]{:S(2)}) collective-permute-start(bf16[320,8192]{1,0:T(8,128)(2,1)} %bitcast.16), channel_id=1, source_target_pairs={{0,1},{1,0},{2,3},{3,2},{4,5},{5,4},{6,7},{7,6},{8,9},{9,8},{10,11... | collective-permute-start | bytes 15728648 | tf_op jit(solution)/shard_map/ppermute | solution.py:66
  2.5 7.7 %collective-permute-start.1 = (bf16[256,1024]{1,0:T(8,128)(2,1)S(1)}, bf16[256,1024]{1,0:T(8,128)(2,1)}, u32[]{:S(2)}, u32[]{:S(2)}) collective-permute-start(bf16[256,1024]{1,0:T(8,128)(2,1)S(1)} %pad_maximum_fusion.refs_0_), channel_id=1, source_target_pairs={{4,8},{5,9},{6,10},{7,11},{8,4},{9,5},{10,6},{11,7},{20,24},{21,25... | collective-permute-start | bytes 1572872 | tf_op jit(solution)/shard_map/ppermute | solution.py:66
  3.9 17.0 %collective-permute-start = (bf16[256,1024]{1,0:T(8,128)(2,1)S(1)}, bf16[256,1024]{1,0:T(8,128)(2,1)S(1)}, u32[]{:S(2)}, u32[]{:S(2)}) collective-permute-start(bf16[256,1024]{1,0:T(8,128)(2,1)S(1)} %pad_maximum_fusion.refs_0_), channel_id=1, source_target_pairs={{0,4},{1,5},{2,6},{3,7},{4,0},{5,1},{6,2},{7,3},{8,12},{9,13},{10,... | collective-permute-start | bytes 1572872 | tf_op jit(solution)/shard_map/ppermute | solution.py:66
  8.6 15.0 %collective-permute-start.2 = (bf16[256,1024]{1,0:T(8,128)(2,1)S(1)}, bf16[256,1024]{1,0:T(8,128)(2,1)S(1)}, u32[]{:S(2)}, u32[]{:S(2)}) collective-permute-start(bf16[256,1024]{1,0:T(8,128)(2,1)S(1)} %pad_maximum_fusion.refs_0_), channel_id=1, source_target_pairs={{0,2},{1,3},{2,0},{3,1},{4,6},{5,7},{6,4},{7,5},{8,10},{9,11},{10,... | collective-permute-start | bytes 1572872 | tf_op jit(solution)/shard_map/ppermute | solution.py:66
  20.9 15.0 %collective-permute-start.5 = (bf16[256,1024]{1,0:T(8,128)(2,1)S(1)}, bf16[256,1024]{1,0:T(8,128)(2,1)}, u32[]{:S(2)}, u32[]{:S(2)}) collective-permute-start(bf16[256,1024]{1,0:T(8,128)(2,1)S(1)} %collective-permute-done.refs_4_), channel_id=1, source_target_pairs={{4,8},{5,9},{6,10},{7,11},{8,4},{9,5},{10,6},{11,7},{20,24},{21,25... | collective-permute-start | bytes 1572872 | tf_op jit(solution)/shard_map/ppermute | solution.py:66
  22.4 15.7 %collective-permute-start.6 = (bf16[256,1024]{1,0:T(8,128)(2,1)}, bf16[256,1024]{1,0:T(8,128)(2,1)}, u32[]{:S(2)}, u32[]{:S(2)}) collective-permute-start(bf16[256,1024]{1,0:T(8,128)(2,1)} %collective-permute-done.1), channel_id=1, source_target_pairs={{4,0},{5,1},{6,2},{7,3},{8,12},{9,13},{10,14},{11,15},{20,16},{21,... | collective-permute-start | bytes 1572872 | tf_op jit(solution)/shard_map/ppermute | solution.py:66
  23.7 16.0 %collective-permute-start.4 = (bf16[256,1024]{1,0:T(8,128)(2,1)S(1)}, bf16[256,1024]{1,0:T(8,128)(2,1)S(1)}, u32[]{:S(2)}, u32[]{:S(2)}) collective-permute-start(bf16[256,1024]{1,0:T(8,128)(2,1)S(1)} %collective-permute-done.2.refs_2_), channel_id=1, source_target_pairs={{0,16},{1,17},{2,18},{3,19},{4,20},{5,21},{6,22},{7,23},{8,24},{9,... | collective-permute-start | bytes 1572872 | tf_op jit(solution)/shard_map/ppermute | solution.py:66
  25.2 14.4 %collective-permute-start.8 = (bf16[256,1024]{1,0:T(8,128)(2,1)S(1)}, bf16[256,1024]{1,0:T(8,128)(2,1)S(1)}, u32[]{:S(2)}, u32[]{:S(2)}) collective-permute-start(bf16[256,1024]{1,0:T(8,128)(2,1)S(1)} %collective-permute-done.refs_4_), channel_id=1, source_target_pairs={{0,2},{1,3},{2,0},{3,1},{4,6},{5,7},{6,4},{7,5},{8,10},{9,11},{10,... | collective-permute-start | bytes 1572872 | tf_op jit(solution)/shard_map/ppermute | solution.py:66
  38.1 27.1 %copy-start = (bf16[16,320,256]{2,1,0:T(8,128)(2,1)S(1)}, bf16[16,320,256]{2,1,0:T(8,128)(2,1)}, u32[]{:S(2)}) copy-start(bf16[16,320,256]{2,1,0:T(8,128)(2,1)} %get-tuple-element.45.mine) | copy-start | bytes 7864324
  38.1 27.1 %copy-start.10 = (s32[11]{0:T(128)S(1)}, s32[11]{0:T(128)}, u32[]{:S(2)}) copy-start(s32[11]{0:T(128)} %stack.47.place) | copy-start | bytes 136
  38.1 15.0 %collective-permute-start.7 = (bf16[256,1024]{1,0:T(8,128)(2,1)}, bf16[256,1024]{1,0:T(8,128)(2,1)S(1)}, u32[]{:S(2)}, u32[]{:S(2)}) collective-permute-start(bf16[256,1024]{1,0:T(8,128)(2,1)} %collective-permute-done.5), channel_id=1, source_target_pairs={{4,0},{5,1},{6,2},{7,3},{8,12},{9,13},{10,14},{11,15},{20,16},{21,... | collective-permute-start | bytes 1572872 | tf_op jit(solution)/shard_map/ppermute | solution.py:66
  40.8 12.7 %collective-permute-start.12 = (bf16[256,1024]{1,0:T(8,128)(2,1)S(1)}, bf16[256,1024]{1,0:T(8,128)(2,1)S(1)}, u32[]{:S(2)}, u32[]{:S(2)}) collective-permute-start(bf16[256,1024]{1,0:T(8,128)(2,1)S(1)} %broadcast_select_fusion.1.refs_0_), channel_id=1, source_target_pairs={{0,16},{1,17},{2,18},{3,19},{4,20},{5,21},{6,22},{7,23},{8,24},{9,... | collective-permute-start | bytes 1572872 | tf_op jit(solution)/shard_map/ppermute | solution.py:66
  42.3 12.3 %collective-permute-start.10 = (bf16[256,1024]{1,0:T(8,128)(2,1)S(1)}, bf16[256,1024]{1,0:T(8,128)(2,1)S(1)}, u32[]{:S(2)}, u32[]{:S(2)}) collective-permute-start(bf16[256,1024]{1,0:T(8,128)(2,1)S(1)} %broadcast_select_fusion.1.refs_0_), channel_id=1, source_target_pairs={{0,2},{1,3},{2,0},{3,1},{4,6},{5,7},{6,4},{7,5},{8,10},{9,11},{10,... | collective-permute-start | bytes 1572872 | tf_op jit(solution)/shard_map/ppermute | solution.py:66
  53.1 12.1 %collective-permute-start.9 = (bf16[256,1024]{1,0:T(8,128)(2,1)S(1)}, bf16[256,1024]{1,0:T(8,128)(2,1)S(1)}, u32[]{:S(2)}, u32[]{:S(2)}) collective-permute-start(bf16[256,1024]{1,0:T(8,128)(2,1)S(1)} %pad_maximum_fusion.1.refs_1_), channel_id=1, source_target_pairs={{0,4},{1,5},{2,6},{3,7},{4,0},{5,1},{6,2},{7,3},{8,12},{9,13},{10,... | collective-permute-start | bytes 1572872 | tf_op jit(solution)/shard_map/ppermute | solution.py:66
  54.7 15.7 %collective-permute-start.14 = (bf16[256,1024]{1,0:T(8,128)(2,1)S(1)}, bf16[256,1024]{1,0:T(8,128)(2,1)S(1)}, u32[]{:S(2)}, u32[]{:S(2)}) collective-permute-start(bf16[256,1024]{1,0:T(8,128)(2,1)S(1)} %broadcast_select_fusion.refs_3_), channel_id=1, source_target_pairs={{0,2},{1,3},{2,0},{3,1},{4,6},{5,7},{6,4},{7,5},{8,10},{9,11},{10,... | collective-permute-start | bytes 1572872 | tf_op jit(solution)/shard_map/ppermute | solution.py:66
  56.3 14.1 %collective-permute-start.13 = (bf16[256,1024]{1,0:T(8,128)(2,1)S(1)}, bf16[256,1024]{1,0:T(8,128)(2,1)S(1)}, u32[]{:S(2)}, u32[]{:S(2)}) collective-permute-start(bf16[256,1024]{1,0:T(8,128)(2,1)S(1)} %broadcast_select_fusion.refs_3_), channel_id=1, source_target_pairs={{0,16},{1,17},{2,18},{3,19},{4,20},{5,21},{6,22},{7,23},{8,24},{9,... | collective-permute-start | bytes 1572872 | tf_op jit(solution)/shard_map/ppermute | solution.py:66
  65.2 12.7 %collective-permute-start.11 = (bf16[256,1024]{1,0:T(8,128)(2,1)S(1)}, bf16[256,1024]{1,0:T(8,128)(2,1)S(1)}, u32[]{:S(2)}, u32[]{:S(2)}) collective-permute-start(bf16[256,1024]{1,0:T(8,128)(2,1)S(1)} %collective-permute-done.4.refs_3_), channel_id=1, source_target_pairs={{0,4},{1,5},{2,6},{3,7},{4,0},{5,1},{6,2},{7,3},{8,12},{9,13},{10,... | collective-permute-start | bytes 1572872 | tf_op jit(solution)/shard_map/ppermute | solution.py:66
  65.2 1.7 %copy-start.1 = (bf16[16,320,256]{2,1,0:T(8,128)(2,1)S(1)}, bf16[16,320,256]{2,1,0:T(8,128)(2,1)}, u32[]{:S(2)}) copy-start(bf16[16,320,256]{2,1,0:T(8,128)(2,1)} %get-tuple-element.37.other) | copy-start | bytes 7864324
  66.9 6.6 %copy-start.2 = (bf16[16,320,256]{2,1,0:T(8,128)(2,1)S(1)}, bf16[16,320,256]{2,1,0:T(8,128)(2,1)}, u32[]{:S(2)}) copy-start(bf16[16,320,256]{2,1,0:T(8,128)(2,1)} %get-tuple-element.37.other) | copy-start | bytes 7864324
  70.4 10.7 %collective-permute-start.15 = (bf16[256,1024]{1,0:T(8,128)(2,1)S(1)}, bf16[256,1024]{1,0:T(8,128)(2,1)S(1)}, u32[]{:S(2)}, u32[]{:S(2)}) collective-permute-start(bf16[256,1024]{1,0:T(8,128)(2,1)S(1)} %collective-permute-done.10.refs_2_), channel_id=1, source_target_pairs={{0,16},{1,17},{2,18},{3,19},{4,20},{5,21},{6,22},{7,23},{8,24},{9,... | collective-permute-start | bytes 1572872 | tf_op jit(solution)/shard_map/ppermute | solution.py:66
  72.0 10.4 %collective-permute-start.16 = (bf16[256,1024]{1,0:T(8,128)(2,1)S(1)}, bf16[256,1024]{1,0:T(8,128)(2,1)S(1)}, u32[]{:S(2)}, u32[]{:S(2)}) collective-permute-start(bf16[256,1024]{1,0:T(8,128)(2,1)S(1)} %collective-permute-done.13.refs_5_), channel_id=1, source_target_pairs={{0,2},{1,3},{2,0},{3,1},{4,6},{5,7},{6,4},{7,5},{8,10},{9,11},{10,... | collective-permute-start | bytes 1572872 | tf_op jit(solution)/shard_map/ppermute | solution.py:66
  82.4 5.5 %copy-start.3 = (f32[64,128]{1,0:T(8,128)S(1)}, f32[64,128]{1,0:T(8,128)}, u32[]{:S(2)}) copy-start(f32[64,128]{1,0:T(8,128)} %constant.71.clone.refs_5_.refs_3_) | copy-start | bytes 98308
  82.4 5.5 %copy-start.4 = (f32[64,128]{1,0:T(8,128)S(1)}, f32[64,128]{1,0:T(8,128)}, u32[]{:S(2)}) copy-start(f32[64,128]{1,0:T(8,128)} %constant.70.clone.refs_4_.refs_2_) | copy-start | bytes 98308
  82.4 5.5 %copy-start.5 = (f32[41,128]{1,0:T(8,128)S(1)}, f32[41,128]{1,0:T(8,128)}, u32[]{:S(2)}) copy-start(f32[41,128]{1,0:T(8,128)} %constant.69.clone.refs_3_.refs_1_) | copy-start | bytes 62980
  82.4 5.5 %copy-start.6 = (f32[41,128]{1,0:T(8,128)S(1)}, f32[41,128]{1,0:T(8,128)}, u32[]{:S(2)}) copy-start(f32[41,128]{1,0:T(8,128)} %constant.68.clone.refs_2_.refs_0_) | copy-start | bytes 62980
  82.4 5.6 %copy-start.7 = (f32[160,128]{1,0:T(8,128)S(1)}, f32[160,128]{1,0:T(8,128)}, u32[]{:S(2)}) copy-start(f32[160,128]{1,0:T(8,128)} %constant.73.clone.refs_7_) | copy-start | bytes 245764
  82.4 5.6 %copy-start.8 = (f32[160,128]{1,0:T(8,128)S(1)}, f32[160,128]{1,0:T(8,128)}, u32[]{:S(2)}) copy-start(f32[160,128]{1,0:T(8,128)} %constant.72.clone.refs_6_) | copy-start | bytes 245764
  82.4 5.5 %copy-start.13 = (s32[2]{0:T(128)S(1)}, s32[2]{0:T(128)}, u32[]{:S(2)}) copy-start(s32[2]{0:T(128)} %lengths.3) | copy-start | bytes 28
  82.4 5.5 %copy-start.14 = (s32[8]{0:T(128)S(1)}, s32[8]{0:T(128)}, u32[]{:S(2)}) copy-start(s32[8]{0:T(128)} %owner.3) | copy-start | bytes 100
  84.8 3.1 %collective-permute-start.17 = (f32[320,1024]{1,0:T(8,128)S(1)}, f32[320,1024]{1,0:T(8,128)S(1)}, u32[]{:S(2)}, u32[]{:S(2)}) collective-permute-start(f32[320,1024]{1,0:T(8,128)S(1)} %get-tuple-element.47), channel_id=1, source_target_pairs={{0,1},{1,0},{2,3},{3,2},{4,5},{5,4},{6,7},{7,6},{8,9},{9,8},{10,11... | collective-permute-start | bytes 3932168 | tf_op jit(solution)/shard_map/ppermute | solution.py:66
  89.0 22.0 %copy-start.9 = (bf16[8,4,1024]{2,1,0:T(4,128)(2,1)S(1)}, bf16[8,4,1024]{2,1,0:T(4,128)(2,1)}, u32[]{:S(2)}) copy-start(bf16[8,4,1024]{2,1,0:T(4,128)(2,1)} %dec_query.1) | copy-start | bytes 196612
  89.0 22.0 %copy-start.11 = (bf16[8,4,128]{2,1,0:T(4,128)(2,1)S(1)}, bf16[8,4,128]{2,1,0:T(4,128)(2,1)}, u32[]{:S(2)}) copy-start(bf16[8,4,128]{2,1,0:T(4,128)(2,1)} %dec_key.1) | copy-start | bytes 24580
  89.1 22.0 %copy-start.12 = (bf16[8,4,128]{2,1,0:T(4,128)(2,1)S(1)}, bf16[8,4,128]{2,1,0:T(4,128)(2,1)}, u32[]{:S(2)}) copy-start(bf16[8,4,128]{2,1,0:T(4,128)(2,1)} %dec_value.1) | copy-start | bytes 24580
  112.1 1.3 %collective-permute-start.18 = (f32[32,256]{1,0:T(8,128)S(1)}, f32[32,256]{1,0:T(8,128)S(1)}, u32[]{:S(2)}, u32[]{:S(2)}) collective-permute-start(f32[32,256]{1,0:T(8,128)S(1)} %decode.1.mine), channel_id=1, source_target_pairs={{0,1},{1,0},{2,3},{3,2},{4,5},{5,4},{6,7},{7,6},{8,9},{9,8},{10,11... | collective-permute-start | bytes 98312 | tf_op jit(solution)/shard_map/ppermute | solution.py:66

commit v21 on v20

--- a/solution.py
+++ b/solution.py
@@ -474,7 +474,7 @@
         pieces = [(HERE, 0, sent), (HERE, 1, rest), (THERE, 0, across)]
         pieces += [(THERE, 1, across_x), (HERE + 1, 0, near), (THERE + 1, 0, near_y)]
         totals = product(place, after(mine, block_c), other, pieces, (), 3)
-        layers, rows = (near_rest, block_yb), (block_xc, block_yc, near_rest, totals[0])
+        layers, rows = (near_rest, block_yb, totals[0]), (block_xc, block_yc, near_rest, totals[0])
         end_a = moved(after(across_x, *layers), to_pair)
         ends = [moved(after(block_yb, *rows), to_group), moved(after(block_xc, *rows), to_row)]
         pieces = [(HERE + 2, 0, block_b), (HERE + 2, 1, block_xb), (THERE + 2, 0, block_yb)]

time: 115 us -> 112 us (0.974)
  waiting for transfers between devices: 39.5 us -> 37.5 us
  starting transfers between devices: 24.3 us -> 22.7 us
    ppermute x19, waiting for transfers between devices: 39.5 us -> 37.5 us  [moved(): return lax.ppermute(block, ('groups', 'seq'), route)]
    ppermute x19, starting transfers between devices: 24.3 us -> 22.7 us  [moved(): return lax.ppermute(block, ('groups', 'seq'), route)]
  transfers between devices with their start and end apart: 19 -> 19, of which waited for: 9 -> 11; matrix products, arithmetic and copies ran while one was open for 3% -> 3% of each run, Pallas kernels for 15% -> 15%
where the time goes in v21:
time: 112 us
  waiting for transfers between devices  37.5 us (33%)
  Pallas kernels  23 us (21%)
  blocking collectives  22.8 us (20%)
  starting transfers between devices  22.7 us (20%)
  local copies, waits for them, and re-layouts  3.74 us (3%)
  other arithmetic  1.3 us (1%)
    ppermute x19, waiting for transfers between devices, moved(): return lax.ppermute(block, ('groups', 'seq'), route)  37.5 us
    all_to_all x1, blocking collectives, body(): lax.all_to_all(outgoing, 'seq', split_axis=0, concat_axis=1, tiled=True)  22.8 us
    ppermute x19, starting transfers between devices, moved(): return lax.ppermute(block, ('groups', 'seq'), route)  22.7 us
    pallas_call x3, Pallas kernels, product(): pl.pallas_call(functools.partial(product_kernel, plan, group, bool(totals...  10.2 us
    pallas_call x1, Pallas kernels, prepared(): pl.pallas_call(prepare_kernel, grid_spec=pltpu.PrefetchScalarGridSpec(num...  8.5 us
  transfers between devices with their start and end apart: 19, of which 11 were waited for; matrix products, arithmetic and copies ran while one was open for 3% of the time, Pallas kernels for 15%

profile of v21, /device:TPU:0, one launch (start us, length us, event | category | flops | bytes accessed | tf_op | source)
XLA Modules:
  0.0 111.9 jit_solution(4268019366889541747)
XLA Ops:
  0.6 0.5 collective-permute-start.3
  1.1 1.3 %constant_dynamic-slice_fusion = (bf16[256,512]{1,0:T(8,128)(2,1)S(1)}, bf16[256,512]{1,0:T(8,128)(2,1)S(1)}, bf16[256,512]{1,0:T(8,128)(2,1)S(1)}, bf16[256,512]{1,0:T(8,128)(2,1)S(1)}) fusion(bf16[512,512]{1,0:T(8,128)(2,1)} %param.16, s32[]{:T(128)S(6)} %select_n.52, s32[]{:T(128)S(6)} %select_n.51, bf16[512,512]{1,0:T(8,128)(2,1)} %param.15), kind=kLoop, calls=%fused_computation.4 | loop fusion | bytes 2097160 | tf_op jit(solution)/shard_map/dynamic_slice | solution.py:446
  2.4 0.1 pad_maximum_fusion.refs_0_
  2.5 1.4 %collective-permute-start.1 = (bf16[256,1024]{1,0:T(8,128)(2,1)S(1)}, bf16[256,1024]{1,0:T(8,128)(2,1)}, u32[]{:S(2)}, u32[]{:S(2)}) collective-permute-start(bf16[256,1024]{1,0:T(8,128)(2,1)S(1)} %pad_maximum_fusion.refs_0_), channel_id=1, source_target_pairs={{4,8},{5,9},{6,10},{7,11},{8,4},{9,5},{10,6},{11,7},{20,24},{21,25... | collective-permute-start | bytes 1572872 | tf_op jit(solution)/shard_map/ppermute | solution.py:66
  3.9 4.7 %collective-permute-start = (bf16[256,1024]{1,0:T(8,128)(2,1)S(1)}, bf16[256,1024]{1,0:T(8,128)(2,1)S(1)}, u32[]{:S(2)}, u32[]{:S(2)}) collective-permute-start(bf16[256,1024]{1,0:T(8,128)(2,1)S(1)} %pad_maximum_fusion.refs_0_), channel_id=1, source_target_pairs={{0,4},{1,5},{2,6},{3,7},{4,0},{5,1},{6,2},{7,3},{8,12},{9,13},{10,... | collective-permute-start | bytes 1572872 | tf_op jit(solution)/shard_map/ppermute | solution.py:66
  8.6 1.5 %collective-permute-start.2 = (bf16[256,1024]{1,0:T(8,128)(2,1)S(1)}, bf16[256,1024]{1,0:T(8,128)(2,1)S(1)}, u32[]{:S(2)}, u32[]{:S(2)}) collective-permute-start(bf16[256,1024]{1,0:T(8,128)(2,1)S(1)} %pad_maximum_fusion.refs_0_), channel_id=1, source_target_pairs={{0,2},{1,3},{2,0},{3,1},{4,6},{5,7},{6,4},{7,5},{8,10},{9,11},{10,... | collective-permute-start | bytes 1572872 | tf_op jit(solution)/shard_map/ppermute | solution.py:66
  10.2 0.1 pad_maximum_fusion.1.refs_1_
  10.2 0.0 collective-permute-done.1
  10.2 10.7 %collective-permute-done.refs_4_ = bf16[256,1024]{1,0:T(8,128)(2,1)S(1)} collective-permute-done((bf16[256,1024]{1,0:T(8,128)(2,1)S(1)}, bf16[256,1024]{1,0:T(8,128)(2,1)S(1)}, u32[]{:S(2)}, u32[]{:S(2)}) %collective-permute-start) | collective-permute-done | bytes 524320 | tf_op jit(solution)/shard_map/ppermute | solution.py:66
  20.9 1.5 %collective-permute-start.5 = (bf16[256,1024]{1,0:T(8,128)(2,1)S(1)}, bf16[256,1024]{1,0:T(8,128)(2,1)}, u32[]{:S(2)}, u32[]{:S(2)}) collective-permute-start(bf16[256,1024]{1,0:T(8,128)(2,1)S(1)} %collective-permute-done.refs_4_), channel_id=1, source_target_pairs={{4,8},{5,9},{6,10},{7,11},{8,4},{9,5},{10,6},{11,7},{20,24},{21,25... | collective-permute-start | bytes 1572872 | tf_op jit(solution)/shard_map/ppermute | solution.py:66
  22.4 1.3 %collective-permute-start.6 = (bf16[256,1024]{1,0:T(8,128)(2,1)}, bf16[256,1024]{1,0:T(8,128)(2,1)}, u32[]{:S(2)}, u32[]{:S(2)}) collective-permute-start(bf16[256,1024]{1,0:T(8,128)(2,1)} %collective-permute-done.1), channel_id=1, source_target_pairs={{4,0},{5,1},{6,2},{7,3},{8,12},{9,13},{10,14},{11,15},{20,16},{21,... | collective-permute-start | bytes 1572872 | tf_op jit(solution)/shard_map/ppermute | solution.py:66
  23.7 0.0 collective-permute-done.2.refs_2_
  23.7 0.0 collective-permute-done.3.refs_1_
  23.7 1.6 %collective-permute-start.4 = (bf16[256,1024]{1,0:T(8,128)(2,1)S(1)}, bf16[256,1024]{1,0:T(8,128)(2,1)S(1)}, u32[]{:S(2)}, u32[]{:S(2)}) collective-permute-start(bf16[256,1024]{1,0:T(8,128)(2,1)S(1)} %collective-permute-done.2.refs_2_), channel_id=1, source_target_pairs={{0,16},{1,17},{2,18},{3,19},{4,20},{5,21},{6,22},{7,23},{8,24},{9,... | collective-permute-start | bytes 1572872 | tf_op jit(solution)/shard_map/ppermute | solution.py:66
  25.2 1.5 %collective-permute-start.8 = (bf16[256,1024]{1,0:T(8,128)(2,1)S(1)}, bf16[256,1024]{1,0:T(8,128)(2,1)S(1)}, u32[]{:S(2)}, u32[]{:S(2)}) collective-permute-start(bf16[256,1024]{1,0:T(8,128)(2,1)S(1)} %collective-permute-done.refs_4_), channel_id=1, source_target_pairs={{0,2},{1,3},{2,0},{3,1},{4,6},{5,7},{6,4},{7,5},{8,10},{9,11},{10,... | collective-permute-start | bytes 1572872 | tf_op jit(solution)/shard_map/ppermute | solution.py:66
  26.8 0.7 stack.47.place
  27.4 8.5 %normed_halves.1 = (bf16[16,320,256]{2,1,0:T(8,128)(2,1)}, bf16[16,320,256]{2,1,0:T(8,128)(2,1)}) custom-call(s32[11]{0:T(128)} %stack.47.place, bf16[320,8192]{1,0:T(8,128)(2,1)} %bitcast.17, bf16[320,8192]{1,0:T(8,128)(2,1)} %collective-permute-done.3.refs_1_), custom_call_target="tpu_custom_call" | custom-call | flops 1000 | bytes 1000 | tf_op jit(solution)/shard_map/normed_halves/pallas_call | solution.py:137
  35.9 0.0 collective-permute-done.5
  35.9 2.2 %collective-permute-done.6 = bf16[256,1024]{1,0:T(8,128)(2,1)} collective-permute-done((bf16[256,1024]{1,0:T(8,128)(2,1)}, bf16[256,1024]{1,0:T(8,128)(2,1)}, u32[]{:S(2)}, u32[]{:S(2)}) %collective-permute-start.6) | collective-permute-done | bytes 524320 | tf_op jit(solution)/shard_map/ppermute | solution.py:66
  38.1 1.5 %collective-permute-start.7 = (bf16[256,1024]{1,0:T(8,128)(2,1)}, bf16[256,1024]{1,0:T(8,128)(2,1)S(1)}, u32[]{:S(2)}, u32[]{:S(2)}) collective-permute-start(bf16[256,1024]{1,0:T(8,128)(2,1)} %collective-permute-done.5), channel_id=1, source_target_pairs={{4,0},{5,1},{6,2},{7,3},{8,12},{9,13},{10,14},{11,15},{20,16},{21,... | collective-permute-start | bytes 1572872 | tf_op jit(solution)/shard_map/ppermute | solution.py:66
  39.6 0.0 collective-permute-done.4.refs_3_
  39.7 0.0 collective-permute-done.8.refs_5_
  39.7 1.1 broadcast_select_fusion.1.refs_0_
  40.8 1.6 %collective-permute-start.11 = (bf16[256,1024]{1,0:T(8,128)(2,1)S(1)}, bf16[256,1024]{1,0:T(8,128)(2,1)S(1)}, u32[]{:S(2)}, u32[]{:S(2)}) collective-permute-start(bf16[256,1024]{1,0:T(8,128)(2,1)S(1)} %broadcast_select_fusion.1.refs_0_), channel_id=1, source_target_pairs={{0,16},{1,17},{2,18},{3,19},{4,20},{5,21},{6,22},{7,23},{8,24},{9,... | collective-permute-start | bytes 1572872 | tf_op jit(solution)/shard_map/ppermute | solution.py:66
  42.3 1.5 %collective-permute-start.10 = (bf16[256,1024]{1,0:T(8,128)(2,1)S(1)}, bf16[256,1024]{1,0:T(8,128)(2,1)S(1)}, u32[]{:S(2)}, u32[]{:S(2)}) collective-permute-start(bf16[256,1024]{1,0:T(8,128)(2,1)S(1)} %broadcast_select_fusion.1.refs_0_), channel_id=1, source_target_pairs={{0,2},{1,3},{2,0},{3,1},{4,6},{5,7},{6,4},{7,5},{8,10},{9,11},{10,... | collective-permute-start | bytes 1572872 | tf_op jit(solution)/shard_map/ppermute | solution.py:66
  43.9 9.2 %collective-permute-done.7 = bf16[256,1024]{1,0:T(8,128)(2,1)S(1)} collective-permute-done((bf16[256,1024]{1,0:T(8,128)(2,1)}, bf16[256,1024]{1,0:T(8,128)(2,1)S(1)}, u32[]{:S(2)}, u32[]{:S(2)}) %collective-permute-start.7) | collective-permute-done | bytes 524320 | tf_op jit(solution)/shard_map/ppermute | solution.py:66
  53.1 0.0 collective-permute-start.9
  53.1 0.4 collective-permute-done.11.refs_1_
  53.5 1.2 %collective-permute-done.10.refs_2_ = bf16[256,1024]{1,0:T(8,128)(2,1)S(1)} collective-permute-done((bf16[256,1024]{1,0:T(8,128)(2,1)S(1)}, bf16[256,1024]{1,0:T(8,128)(2,1)S(1)}, u32[]{:S(2)}, u32[]{:S(2)}) %collective-permute-start.10) | collective-permute-done | bytes 524320 | tf_op jit(solution)/shard_map/ppermute | solution.py:66
  54.7 0.1 broadcast_select_fusion.refs_3_
  54.7 1.6 %collective-permute-start.14 = (bf16[256,1024]{1,0:T(8,128)(2,1)S(1)}, bf16[256,1024]{1,0:T(8,128)(2,1)S(1)}, u32[]{:S(2)}, u32[]{:S(2)}) collective-permute-start(bf16[256,1024]{1,0:T(8,128)(2,1)S(1)} %broadcast_select_fusion.refs_3_), channel_id=1, source_target_pairs={{0,2},{1,3},{2,0},{3,1},{4,6},{5,7},{6,4},{7,5},{8,10},{9,11},{10,... | collective-permute-start | bytes 1572872 | tf_op jit(solution)/shard_map/ppermute | solution.py:66
  56.3 0.5 collective-permute-start.13
  56.9 0.0 copy-done.10
  56.9 1.7 %copy-done.1 = bf16[16,320,256]{2,1,0:T(8,128)(2,1)S(1)} copy-done((bf16[16,320,256]{2,1,0:T(8,128)(2,1)S(1)}, bf16[16,320,256]{2,1,0:T(8,128)(2,1)}, u32[]{:S(2)}) %copy-start.1) | copy-done | bytes 2621464
  58.6 3.5 %add_product.3 = (f32[320,1024]{1,0:T(8,128)S(1)}, f32[320,1024]{1,0:T(8,128)S(1)}) custom-call(s32[11]{0:T(128)S(1)} %copy-done.10, bf16[16,320,256]{2,1,0:T(8,128)(2,1)S(1)} %copy-done, bf16[16,320,256]{2,1,0:T(8,128)(2,1)S(1)} %copy-done.1, bf16[256,1024]{1,0:T(8,128)(2,1)S(1)} %pad_maximum_fusion.refs_0_, ...), custom_call_target="tpu_custom_call" | custom-call | flops 1000 | bytes 1000 | tf_op jit(solution)/shard_map/add_product/pallas_call | solution.py:204
  62.1 3.0 %collective-permute-done.9.refs_4_ = bf16[256,1024]{1,0:T(8,128)(2,1)S(1)} collective-permute-done((bf16[256,1024]{1,0:T(8,128)(2,1)S(1)}, bf16[256,1024]{1,0:T(8,128)(2,1)S(1)}, u32[]{:S(2)}, u32[]{:S(2)}) %collective-permute-start.9) | collective-permute-done | bytes 524320 | tf_op jit(solution)/shard_map/ppermute | solution.py:66
  65.2 0.5 collective-permute-start.12
  65.6 0.6 collective-permute-done.14.refs_6_
  66.2 2.2 %collective-permute-done.13.refs_5_ = bf16[256,1024]{1,0:T(8,128)(2,1)S(1)} collective-permute-done((bf16[256,1024]{1,0:T(8,128)(2,1)S(1)}, bf16[256,1024]{1,0:T(8,128)(2,1)S(1)}, u32[]{:S(2)}, u32[]{:S(2)}) %collective-permute-start.13) | collective-permute-done | bytes 524320 | tf_op jit(solution)/shard_map/ppermute | solution.py:66
  68.4 0.5 collective-permute-start.15
  69.0 0.4 collective-permute-start.16
  69.4 0.0 copy-done.2
  69.4 4.3 %add_product.4 = (f32[320,1024]{1,0:T(8,128)S(1)}, f32[320,1024]{1,0:T(8,128)S(1)}) custom-call(s32[11]{0:T(128)S(1)} %copy-done.10, bf16[16,320,256]{2,1,0:T(8,128)(2,1)S(1)} %copy-done, bf16[16,320,256]{2,1,0:T(8,128)(2,1)S(1)} %copy-done.2, bf16[256,1024]{1,0:T(8,128)(2,1)S(1)} %broadcast_select_fusion.1.refs_0_, ...), custom_call_target="tpu_custom_call" | custom-call | flops 1000 | bytes 1000 | tf_op jit(solution)/shard_map/add_product/pallas_call | solution.py:204
  73.7 2.2 %collective-permute-done.12.refs_0_ = bf16[256,1024]{1,0:T(8,128)(2,1)S(1)} collective-permute-done((bf16[256,1024]{1,0:T(8,128)(2,1)S(1)}, bf16[256,1024]{1,0:T(8,128)(2,1)S(1)}, u32[]{:S(2)}, u32[]{:S(2)}) %collective-permute-start.12) | collective-permute-done | bytes 524320 | tf_op jit(solution)/shard_map/ppermute | solution.py:66
  76.0 2.7 %collective-permute-done.15.refs_1_ = bf16[256,1024]{1,0:T(8,128)(2,1)S(1)} collective-permute-done((bf16[256,1024]{1,0:T(8,128)(2,1)S(1)}, bf16[256,1024]{1,0:T(8,128)(2,1)S(1)}, u32[]{:S(2)}, u32[]{:S(2)}) %collective-permute-start.15) | collective-permute-done | bytes 524320 | tf_op jit(solution)/shard_map/ppermute | solution.py:66
  78.7 0.0 collective-permute-done.16.refs_2_
  78.7 0.0 copy-start.6
  78.7 0.0 copy-start.7
  78.7 0.0 copy-start.8
  78.8 0.0 copy-start.13
  78.8 0.0 copy-start.14
  78.8 2.4 %add_product.5 = (f32[320,1024]{1,0:T(8,128)S(1)}, f32[320,1024]{1,0:T(8,128)S(1)}) custom-call(s32[11]{0:T(128)S(1)} %copy-done.10, bf16[16,320,256]{2,1,0:T(8,128)(2,1)S(1)} %copy-done, bf16[16,320,256]{2,1,0:T(8,128)(2,1)S(1)} %copy-done.2, bf16[256,1024]{1,0:T(8,128)(2,1)S(1)} %collective-permute-done.12.refs_0_, ...), custom_call_target="tpu_custom_call" | custom-call | flops 1000 | bytes 1000 | tf_op jit(solution)/shard_map/add_product/pallas_call | solution.py:204
  81.2 0.1 collective-permute-start.17
  81.2 3.0 %collective-permute-done.17.refs_1_ = f32[320,1024]{1,0:T(8,128)S(1)} collective-permute-done((f32[320,1024]{1,0:T(8,128)S(1)}, f32[320,1024]{1,0:T(8,128)S(1)}, u32[]{:S(2)}, u32[]{:S(2)}) %collective-permute-start.17) | collective-permute-done | bytes 1310752 | tf_op jit(solution)/shard_map/ppermute | solution.py:66
  84.3 1.0 cache_rows.1
  85.4 0.0 copy-start.9
  85.4 0.0 copy-start.11
  85.4 0.0 copy-start.12
  85.4 22.8 %all_to_all.4 = bf16[16,80,256]{2,1,0:T(8,128)(2,1)S(1)} all-to-all(bf16[16,80,256]{2,1,0:T(8,128)(2,1)S(1)} %cache_rows.1), channel_id=1, replica_groups=mesh['groups'=2,'seq'=16] {'seq'}, dimensions={0} | all-to-all | bytes 1310720 | tf_op jit(solution)/shard_map/all_to_all | solution.py:488
  108.2 1.1 decode.1.mine
  109.3 0.4 collective-permute-start.18
  109.7 0.8 copied.1
  110.5 0.0 collective-permute-done.18.theirs
  110.6 1.3 %joined.1 = bf16[4,512]{1,0:T(4,128)(2,1)} custom-call(s32[11]{0:T(128)S(1)} %copy-done.10, f32[32,256]{1,0:T(8,128)S(1)} %decode.1.mine, f32[32,256]{1,0:T(8,128)S(1)} %collective-permute-done.18.theirs), custom_call_target="tpu_custom_call" | custom-call | flops 1000 | bytes 1000 | tf_op jit(solution)/shard_map/joined/pallas_call | solution.py:379
  (19 shorter events, 0.0 us)
Async XLA Ops:
  0.6 23.0 %collective-permute-start.3 = (bf16[320,8192]{1,0:T(8,128)(2,1)}, bf16[320,8192]{1,0:T(8,128)(2,1)}, u32[]{:S(2)}, u32[]{:S(2)}) collective-permute-start(bf16[320,8192]{1,0:T(8,128)(2,1)} %bitcast.16), channel_id=1, source_target_pairs={{0,1},{1,0},{2,3},{3,2},{4,5},{5,4},{6,7},{7,6},{8,9},{9,8},{10,11... | collective-permute-start | bytes 15728648 | tf_op jit(solution)/shard_map/ppermute | solution.py:66
  2.5 7.7 %collective-permute-start.1 = (bf16[256,1024]{1,0:T(8,128)(2,1)S(1)}, bf16[256,1024]{1,0:T(8,128)(2,1)}, u32[]{:S(2)}, u32[]{:S(2)}) collective-permute-start(bf16[256,1024]{1,0:T(8,128)(2,1)S(1)} %pad_maximum_fusion.refs_0_), channel_id=1, source_target_pairs={{4,8},{5,9},{6,10},{7,11},{8,4},{9,5},{10,6},{11,7},{20,24},{21,25... | collective-permute-start | bytes 1572872 | tf_op jit(solution)/shard_map/ppermute | solution.py:66
  3.9 17.0 %collective-permute-start = (bf16[256,1024]{1,0:T(8,128)(2,1)S(1)}, bf16[256,1024]{1,0:T(8,128)(2,1)S(1)}, u32[]{:S(2)}, u32[]{:S(2)}) collective-permute-start(bf16[256,1024]{1,0:T(8,128)(2,1)S(1)} %pad_maximum_fusion.refs_0_), channel_id=1, source_target_pairs={{0,4},{1,5},{2,6},{3,7},{4,0},{5,1},{6,2},{7,3},{8,12},{9,13},{10,... | collective-permute-start | bytes 1572872 | tf_op jit(solution)/shard_map/ppermute | solution.py:66
  8.6 15.0 %collective-permute-start.2 = (bf16[256,1024]{1,0:T(8,128)(2,1)S(1)}, bf16[256,1024]{1,0:T(8,128)(2,1)S(1)}, u32[]{:S(2)}, u32[]{:S(2)}) collective-permute-start(bf16[256,1024]{1,0:T(8,128)(2,1)S(1)} %pad_maximum_fusion.refs_0_), channel_id=1, source_target_pairs={{0,2},{1,3},{2,0},{3,1},{4,6},{5,7},{6,4},{7,5},{8,10},{9,11},{10,... | collective-permute-start | bytes 1572872 | tf_op jit(solution)/shard_map/ppermute | solution.py:66
  20.9 15.0 %collective-permute-start.5 = (bf16[256,1024]{1,0:T(8,128)(2,1)S(1)}, bf16[256,1024]{1,0:T(8,128)(2,1)}, u32[]{:S(2)}, u32[]{:S(2)}) collective-permute-start(bf16[256,1024]{1,0:T(8,128)(2,1)S(1)} %collective-permute-done.refs_4_), channel_id=1, source_target_pairs={{4,8},{5,9},{6,10},{7,11},{8,4},{9,5},{10,6},{11,7},{20,24},{21,25... | collective-permute-start | bytes 1572872 | tf_op jit(solution)/shard_map/ppermute | solution.py:66
  22.4 15.7 %collective-permute-start.6 = (bf16[256,1024]{1,0:T(8,128)(2,1)}, bf16[256,1024]{1,0:T(8,128)(2,1)}, u32[]{:S(2)}, u32[]{:S(2)}) collective-permute-start(bf16[256,1024]{1,0:T(8,128)(2,1)} %collective-permute-done.1), channel_id=1, source_target_pairs={{4,0},{5,1},{6,2},{7,3},{8,12},{9,13},{10,14},{11,15},{20,16},{21,... | collective-permute-start | bytes 1572872 | tf_op jit(solution)/shard_map/ppermute | solution.py:66
  23.7 16.0 %collective-permute-start.4 = (bf16[256,1024]{1,0:T(8,128)(2,1)S(1)}, bf16[256,1024]{1,0:T(8,128)(2,1)S(1)}, u32[]{:S(2)}, u32[]{:S(2)}) collective-permute-start(bf16[256,1024]{1,0:T(8,128)(2,1)S(1)} %collective-permute-done.2.refs_2_), channel_id=1, source_target_pairs={{0,16},{1,17},{2,18},{3,19},{4,20},{5,21},{6,22},{7,23},{8,24},{9,... | collective-permute-start | bytes 1572872 | tf_op jit(solution)/shard_map/ppermute | solution.py:66
  25.2 14.4 %collective-permute-start.8 = (bf16[256,1024]{1,0:T(8,128)(2,1)S(1)}, bf16[256,1024]{1,0:T(8,128)(2,1)S(1)}, u32[]{:S(2)}, u32[]{:S(2)}) collective-permute-start(bf16[256,1024]{1,0:T(8,128)(2,1)S(1)} %collective-permute-done.refs_4_), channel_id=1, source_target_pairs={{0,2},{1,3},{2,0},{3,1},{4,6},{5,7},{6,4},{7,5},{8,10},{9,11},{10,... | collective-permute-start | bytes 1572872 | tf_op jit(solution)/shard_map/ppermute | solution.py:66
  38.1 18.8 %copy-start = (bf16[16,320,256]{2,1,0:T(8,128)(2,1)S(1)}, bf16[16,320,256]{2,1,0:T(8,128)(2,1)}, u32[]{:S(2)}) copy-start(bf16[16,320,256]{2,1,0:T(8,128)(2,1)} %get-tuple-element.45.mine) | copy-start | bytes 7864324
  38.1 18.8 %copy-start.10 = (s32[11]{0:T(128)S(1)}, s32[11]{0:T(128)}, u32[]{:S(2)}) copy-start(s32[11]{0:T(128)} %stack.47.place) | copy-start | bytes 136
  38.1 15.0 %collective-permute-start.7 = (bf16[256,1024]{1,0:T(8,128)(2,1)}, bf16[256,1024]{1,0:T(8,128)(2,1)S(1)}, u32[]{:S(2)}, u32[]{:S(2)}) collective-permute-start(bf16[256,1024]{1,0:T(8,128)(2,1)} %collective-permute-done.5), channel_id=1, source_target_pairs={{4,0},{5,1},{6,2},{7,3},{8,12},{9,13},{10,14},{11,15},{20,16},{21,... | collective-permute-start | bytes 1572872 | tf_op jit(solution)/shard_map/ppermute | solution.py:66
  40.8 12.7 %collective-permute-start.11 = (bf16[256,1024]{1,0:T(8,128)(2,1)S(1)}, bf16[256,1024]{1,0:T(8,128)(2,1)S(1)}, u32[]{:S(2)}, u32[]{:S(2)}) collective-permute-start(bf16[256,1024]{1,0:T(8,128)(2,1)S(1)} %broadcast_select_fusion.1.refs_0_), channel_id=1, source_target_pairs={{0,16},{1,17},{2,18},{3,19},{4,20},{5,21},{6,22},{7,23},{8,24},{9,... | collective-permute-start | bytes 1572872 | tf_op jit(solution)/shard_map/ppermute | solution.py:66
  42.3 12.3 %collective-permute-start.10 = (bf16[256,1024]{1,0:T(8,128)(2,1)S(1)}, bf16[256,1024]{1,0:T(8,128)(2,1)S(1)}, u32[]{:S(2)}, u32[]{:S(2)}) collective-permute-start(bf16[256,1024]{1,0:T(8,128)(2,1)S(1)} %broadcast_select_fusion.1.refs_0_), channel_id=1, source_target_pairs={{0,2},{1,3},{2,0},{3,1},{4,6},{5,7},{6,4},{7,5},{8,10},{9,11},{10,... | collective-permute-start | bytes 1572872 | tf_op jit(solution)/shard_map/ppermute | solution.py:66
  53.1 12.1 %collective-permute-start.9 = (bf16[256,1024]{1,0:T(8,128)(2,1)S(1)}, bf16[256,1024]{1,0:T(8,128)(2,1)S(1)}, u32[]{:S(2)}, u32[]{:S(2)}) collective-permute-start(bf16[256,1024]{1,0:T(8,128)(2,1)S(1)} %pad_maximum_fusion.1.refs_1_), channel_id=1, source_target_pairs={{0,4},{1,5},{2,6},{3,7},{4,0},{5,1},{6,2},{7,3},{8,12},{9,13},{10,... | collective-permute-start | bytes 1572872 | tf_op jit(solution)/shard_map/ppermute | solution.py:66
  54.7 11.5 %collective-permute-start.14 = (bf16[256,1024]{1,0:T(8,128)(2,1)S(1)}, bf16[256,1024]{1,0:T(8,128)(2,1)S(1)}, u32[]{:S(2)}, u32[]{:S(2)}) collective-permute-start(bf16[256,1024]{1,0:T(8,128)(2,1)S(1)} %broadcast_select_fusion.refs_3_), channel_id=1, source_target_pairs={{0,2},{1,3},{2,0},{3,1},{4,6},{5,7},{6,4},{7,5},{8,10},{9,11},{10,... | collective-permute-start | bytes 1572872 | tf_op jit(solution)/shard_map/ppermute | solution.py:66
  56.3 12.1 %collective-permute-start.13 = (bf16[256,1024]{1,0:T(8,128)(2,1)S(1)}, bf16[256,1024]{1,0:T(8,128)(2,1)S(1)}, u32[]{:S(2)}, u32[]{:S(2)}) collective-permute-start(bf16[256,1024]{1,0:T(8,128)(2,1)S(1)} %broadcast_select_fusion.refs_3_), channel_id=1, source_target_pairs={{0,16},{1,17},{2,18},{3,19},{4,20},{5,21},{6,22},{7,23},{8,24},{9,... | collective-permute-start | bytes 1572872 | tf_op jit(solution)/shard_map/ppermute | solution.py:66
  56.9 1.7 %copy-start.1 = (bf16[16,320,256]{2,1,0:T(8,128)(2,1)S(1)}, bf16[16,320,256]{2,1,0:T(8,128)(2,1)}, u32[]{:S(2)}) copy-start(bf16[16,320,256]{2,1,0:T(8,128)(2,1)} %get-tuple-element.36.other) | copy-start | bytes 7864324
  58.6 10.8 %copy-start.2 = (bf16[16,320,256]{2,1,0:T(8,128)(2,1)S(1)}, bf16[16,320,256]{2,1,0:T(8,128)(2,1)}, u32[]{:S(2)}) copy-start(bf16[16,320,256]{2,1,0:T(8,128)(2,1)} %get-tuple-element.36.other) | copy-start | bytes 7864324
  65.2 10.8 %collective-permute-start.12 = (bf16[256,1024]{1,0:T(8,128)(2,1)S(1)}, bf16[256,1024]{1,0:T(8,128)(2,1)S(1)}, u32[]{:S(2)}, u32[]{:S(2)}) collective-permute-start(bf16[256,1024]{1,0:T(8,128)(2,1)S(1)} %collective-permute-done.4.refs_3_), channel_id=1, source_target_pairs={{0,4},{1,5},{2,6},{3,7},{4,0},{5,1},{6,2},{7,3},{8,12},{9,13},{10,... | collective-permute-start | bytes 1572872 | tf_op jit(solution)/shard_map/ppermute | solution.py:66
  68.4 10.3 %collective-permute-start.15 = (bf16[256,1024]{1,0:T(8,128)(2,1)S(1)}, bf16[256,1024]{1,0:T(8,128)(2,1)S(1)}, u32[]{:S(2)}, u32[]{:S(2)}) collective-permute-start(bf16[256,1024]{1,0:T(8,128)(2,1)S(1)} %collective-permute-done.10.refs_2_), channel_id=1, source_target_pairs={{0,16},{1,17},{2,18},{3,19},{4,20},{5,21},{6,22},{7,23},{8,24},{9,... | collective-permute-start | bytes 1572872 | tf_op jit(solution)/shard_map/ppermute | solution.py:66
  69.0 9.7 %collective-permute-start.16 = (bf16[256,1024]{1,0:T(8,128)(2,1)S(1)}, bf16[256,1024]{1,0:T(8,128)(2,1)S(1)}, u32[]{:S(2)}, u32[]{:S(2)}) collective-permute-start(bf16[256,1024]{1,0:T(8,128)(2,1)S(1)} %collective-permute-done.13.refs_5_), channel_id=1, source_target_pairs={{0,2},{1,3},{2,0},{3,1},{4,6},{5,7},{6,4},{7,5},{8,10},{9,11},{10,... | collective-permute-start | bytes 1572872 | tf_op jit(solution)/shard_map/ppermute | solution.py:66
  78.7 5.6 %copy-start.3 = (f32[64,128]{1,0:T(8,128)S(1)}, f32[64,128]{1,0:T(8,128)}, u32[]{:S(2)}) copy-start(f32[64,128]{1,0:T(8,128)} %constant.71.clone.refs_5_.refs_3_) | copy-start | bytes 98308
  78.7 5.6 %copy-start.4 = (f32[64,128]{1,0:T(8,128)S(1)}, f32[64,128]{1,0:T(8,128)}, u32[]{:S(2)}) copy-start(f32[64,128]{1,0:T(8,128)} %constant.70.clone.refs_4_.refs_2_) | copy-start | bytes 98308
  78.7 5.6 %copy-start.5 = (f32[41,128]{1,0:T(8,128)S(1)}, f32[41,128]{1,0:T(8,128)}, u32[]{:S(2)}) copy-start(f32[41,128]{1,0:T(8,128)} %constant.69.clone.refs_3_.refs_1_) | copy-start | bytes 62980
  78.7 5.6 %copy-start.6 = (f32[41,128]{1,0:T(8,128)S(1)}, f32[41,128]{1,0:T(8,128)}, u32[]{:S(2)}) copy-start(f32[41,128]{1,0:T(8,128)} %constant.68.clone.refs_2_.refs_0_) | copy-start | bytes 62980
  78.7 5.6 %copy-start.7 = (f32[160,128]{1,0:T(8,128)S(1)}, f32[160,128]{1,0:T(8,128)}, u32[]{:S(2)}) copy-start(f32[160,128]{1,0:T(8,128)} %constant.73.clone.refs_7_) | copy-start | bytes 245764
  78.7 5.6 %copy-start.8 = (f32[160,128]{1,0:T(8,128)S(1)}, f32[160,128]{1,0:T(8,128)}, u32[]{:S(2)}) copy-start(f32[160,128]{1,0:T(8,128)} %constant.72.clone.refs_6_) | copy-start | bytes 245764
  78.8 5.5 %copy-start.13 = (s32[2]{0:T(128)S(1)}, s32[2]{0:T(128)}, u32[]{:S(2)}) copy-start(s32[2]{0:T(128)} %lengths.3) | copy-start | bytes 28
  78.8 5.5 %copy-start.14 = (s32[8]{0:T(128)S(1)}, s32[8]{0:T(128)}, u32[]{:S(2)}) copy-start(s32[8]{0:T(128)} %owner.3) | copy-start | bytes 100
  81.2 3.1 %collective-permute-start.17 = (f32[320,1024]{1,0:T(8,128)S(1)}, f32[320,1024]{1,0:T(8,128)S(1)}, u32[]{:S(2)}, u32[]{:S(2)}) collective-permute-start(f32[320,1024]{1,0:T(8,128)S(1)} %get-tuple-element.47), channel_id=1, source_target_pairs={{0,1},{1,0},{2,3},{3,2},{4,5},{5,4},{6,7},{7,6},{8,9},{9,8},{10,11... | collective-permute-start | bytes 3932168 | tf_op jit(solution)/shard_map/ppermute | solution.py:66
  85.4 22.8 %copy-start.9 = (bf16[8,4,1024]{2,1,0:T(4,128)(2,1)S(1)}, bf16[8,4,1024]{2,1,0:T(4,128)(2,1)}, u32[]{:S(2)}) copy-start(bf16[8,4,1024]{2,1,0:T(4,128)(2,1)} %dec_query.1) | copy-start | bytes 196612
  85.4 22.8 %copy-start.11 = (bf16[8,4,128]{2,1,0:T(4,128)(2,1)S(1)}, bf16[8,4,128]{2,1,0:T(4,128)(2,1)}, u32[]{:S(2)}) copy-start(bf16[8,4,128]{2,1,0:T(4,128)(2,1)} %dec_key.1) | copy-start | bytes 24580
  85.4 22.8 %copy-start.12 = (bf16[8,4,128]{2,1,0:T(4,128)(2,1)S(1)}, bf16[8,4,128]{2,1,0:T(4,128)(2,1)}, u32[]{:S(2)}) copy-start(bf16[8,4,128]{2,1,0:T(4,128)(2,1)} %dec_value.1) | copy-start | bytes 24580
  109.3 1.3 %collective-permute-start.18 = (f32[32,256]{1,0:T(8,128)S(1)}, f32[32,256]{1,0:T(8,128)S(1)}, u32[]{:S(2)}, u32[]{:S(2)}) collective-permute-start(f32[32,256]{1,0:T(8,128)S(1)} %decode.1.mine), channel_id=1, source_target_pairs={{0,1},{1,0},{2,3},{3,2},{4,5},{5,4},{6,7},{7,6},{8,9},{9,8},{10,11... | collective-permute-start | bytes 98312 | tf_op jit(solution)/shard_map/ppermute | solution.py:66

commit v22 on v21

--- a/solution.py
+++ b/solution.py
@@ -94,7 +94,7 @@
 SMEM_REF = pl.BlockSpec(memory_space=pltpu.SMEM)
 ANY_REF = pl.BlockSpec(memory_space=pl.ANY)
 PARAMS = pltpu.CompilerParams(vmem_limit_bytes=20 << 20)
-LARGE = pltpu.CompilerParams(vmem_limit_bytes=58 << 20)
+LARGE = pltpu.CompilerParams(vmem_limit_bytes=53 << 20)
 SMALL = pltpu.CompilerParams(vmem_limit_bytes=16 << 20)
 
 
@@ -332,24 +332,6 @@
     out[:, HEAD_SIZE + half[1] :] = jnp.broadcast_to(total, half)
 
 
-def joined_kernel(place, mine, theirs, out):
-    share = QPK // 2
-    area = pl.ds(place[2] % 2 * share * STEPS, share * STEPS)
-    last = HEAD_SIZE + HEAD_SIZE // 2
-    sums, tops, totals = [], [], []
-    for ref in (mine, theirs):
-        sums.append(ref[area, :HEAD_SIZE])
-        tops.append(ref[area, HEAD_SIZE : HEAD_SIZE + 1])
-        totals.append(ref[area, last : last + 1])
-    top = jnp.maximum(tops[0], tops[1])
-    scales = [jnp.exp(one - top) for one in tops]
-    total = totals[0] * scales[0] + totals[1] * scales[1]
-    value = (sums[0] * scales[0] + sums[1] * scales[1]) / total
-    for j in range(share):
-        rows = value[j * STEPS : (j + 1) * STEPS]
-        out[:, j * HEAD_SIZE : (j + 1) * HEAD_SIZE] = rows.astype(jnp.bfloat16)
-
-
 def copied(cache):
     def kernel(source, out, sem):
         fetch(source, out, sem.at[0]).wait()
@@ -376,15 +358,21 @@
         cost_estimate=cost(1000, 1000),
         name="decode",
     )(place, lengths, owner, cache, dec_query, dec_key, dec_value, *tables[:4])
-    return pl.pallas_call(
-        joined_kernel,
-        in_specs=[SMEM_REF] + [VMEM_REF] * 2,
-        out_specs=VMEM_REF,
-        out_shape=jax.ShapeDtypeStruct((STEPS, QPK // 2 * HEAD_SIZE), jnp.bfloat16),
-        compiler_params=SMALL,
-        cost_estimate=cost(1000, 1000),
-        name="joined",
-    )(place, mine, moved(mine, to_core))
+    theirs = moved(mine, to_core)
+    share = QPK // 2
+    last = HEAD_SIZE + HEAD_SIZE // 2
+
+    def heads(array):
+        array = array.reshape(QPK, STEPS, 2 * HEAD_SIZE)
+        array = lax.dynamic_slice_in_dim(array, place[2] % 2 * share, share, 0)
+        return array[..., :HEAD_SIZE], array[..., HEAD_SIZE : HEAD_SIZE + 1], array[..., last : last + 1]
+
+    sums_a, top_a, total_a = heads(mine)
+    sums_b, top_b, total_b = heads(theirs)
+    top = jnp.maximum(top_a, top_b)
+    scale_a, scale_b = jnp.exp(top_a - top), jnp.exp(top_b - top)
+    value = (sums_a * scale_a + sums_b * scale_b) / (total_a * scale_a + total_b * scale_b)
+    return jnp.transpose(value, (1, 0, 2)).reshape(STEPS, share * HEAD_SIZE).astype(jnp.bfloat16)
 
 
 HERE, THERE = 3, 7
@@ -457,7 +445,7 @@
         rest = half_block(depth - group_id * depth)
         layers, rows = (near, middle), (near, middle, across, raw, rest)
         passed = moved(after(middle, *layers), to_end)
-        middle_c = moved(after(near, *layers), to_middle)
+        middle_c = moved(near, to_middle)
         near_y = moved(after(near, *rows), to_row)
         across_x = moved(after(across, *rows), to_group)
         mine, other = prepared(place, after(flat, *rows), raw, seq // 2)

time: 112 us -> 113 us (level)
  blocking collectives: 22.8 us -> 0 us
  waiting for transfers between devices: 37.5 us -> 54.6 us
  starting transfers between devices: 22.7 us -> 28.1 us
    all_to_all x1 -> x0, blocking collectives: 22.8 us -> none  [body(): lax.all_to_all(outgoing, 'seq', split_axis=0, concat_axis=1, tiled=True)]
    all_to_all x0 -> x1, waiting for transfers between devices: none -> 16.6 us  [body(): lax.all_to_all(outgoing, 'seq', split_axis=0, concat_axis=1, tiled=True)]
    all_to_all x0 -> x1, starting transfers between devices: none -> 6.06 us  [body(): lax.all_to_all(outgoing, 'seq', split_axis=0, concat_axis=1, tiled=True)]
    unnamed x30 -> x35, local copies, waits for them, and re-layouts: 1.81 us -> 3.18 us
    pallas_call x1 -> x0, Pallas kernels: 1.3 us -> none  [decoded(): pl.pallas_call(joined_kernel, in_specs=[SMEM_REF] + [VMEM_REF] * 2, out_s...]
  transfers between devices with their start and end apart: 19 -> 20, of which waited for: 11 -> 12; matrix products, arithmetic and copies ran while one was open for 3% -> 3% of each run, Pallas kernels for 15% -> 15%
where the time goes in v22:
time: 113 us; the launch traced here: 112 us
  waiting for transfers between devices  54.6 us (48%)
  starting transfers between devices  28.1 us (25%)
  Pallas kernels  22.4 us (20%)
  local copies, waits for them, and re-layouts  4.84 us (4%)
  other arithmetic  1.39 us (1%)
    ppermute x19, waiting for transfers between devices, moved(): return lax.ppermute(block, ('groups', 'seq'), route)  38 us
    ppermute x19, starting transfers between devices, moved(): return lax.ppermute(block, ('groups', 'seq'), route)  22.1 us
    all_to_all x1, waiting for transfers between devices, body(): lax.all_to_all(outgoing, 'seq', split_axis=0, concat_axis=1, tiled=True)  16.6 us
    pallas_call x3, Pallas kernels, product(): pl.pallas_call(functools.partial(product_kernel, plan, group, bool(totals...  10.2 us
    pallas_call x1, Pallas kernels, prepared(): pl.pallas_call(prepare_kernel, grid_spec=pltpu.PrefetchScalarGridSpec(num...  8.39 us
    all_to_all x1, starting transfers between devices, body(): lax.all_to_all(outgoing, 'seq', split_axis=0, concat_axis=1, tiled=True)  6.06 us
    unnamed x35, local copies, waits for them, and re-layouts  3.18 us
  transfers between devices with their start and end apart: 20, of which 12 were waited for; matrix products, arithmetic and copies ran while one was open for 3% of the time, Pallas kernels for 15%

profile of v22, /device:TPU:0, one launch (start us, length us, event | category | flops | bytes accessed | tf_op | source)
XLA Modules:
  0.0 112.3 jit_solution(3891603089127412934)
XLA Ops:
  0.6 0.5 collective-permute-start.3
  1.1 1.3 %constant_dynamic-slice_fusion.6 = (bf16[256,512]{1,0:T(8,128)(2,1)S(1)}, bf16[256,512]{1,0:T(8,128)(2,1)S(1)}, bf16[256,512]{1,0:T(8,128)(2,1)S(1)}, bf16[256,512]{1,0:T(8,128)(2,1)S(1)}) fusion(bf16[512,512]{1,0:T(8,128)(2,1)} %param.16, s32[]{:T(128)S(6)} %select_n.60, s32[]{:T(128)S(6)} %select_n.59, bf16[512,512]{1,0:T(8,128)(2,1)} %param.15), kind=kLoop, calls=%fused_computation.16 | loop fusion | bytes 2097160 | tf_op jit(solution)/shard_map/dynamic_slice | solution.py:434
  2.4 0.1 pad_maximum_fusion.refs_0_
  2.5 2.7 %collective-permute-start = (bf16[256,1024]{1,0:T(8,128)(2,1)S(1)}, bf16[256,1024]{1,0:T(8,128)(2,1)S(1)}, u32[]{:S(2)}, u32[]{:S(2)}) collective-permute-start(bf16[256,1024]{1,0:T(8,128)(2,1)S(1)} %pad_maximum_fusion.refs_0_), channel_id=1, source_target_pairs={{0,4},{1,5},{2,6},{3,7},{4,0},{5,1},{6,2},{7,3},{8,12},{9,13},{10,... | collective-permute-start | bytes 1572872 | tf_op jit(solution)/shard_map/ppermute | solution.py:66
  5.1 1.5 %collective-permute-start.1 = (bf16[256,1024]{1,0:T(8,128)(2,1)S(1)}, bf16[256,1024]{1,0:T(8,128)(2,1)}, u32[]{:S(2)}, u32[]{:S(2)}) collective-permute-start(bf16[256,1024]{1,0:T(8,128)(2,1)S(1)} %pad_maximum_fusion.refs_0_), channel_id=1, source_target_pairs={{4,8},{5,9},{6,10},{7,11},{8,4},{9,5},{10,6},{11,7},{20,24},{21,25... | collective-permute-start | bytes 1572872 | tf_op jit(solution)/shard_map/ppermute | solution.py:66
  6.6 1.5 %collective-permute-start.2 = (bf16[256,1024]{1,0:T(8,128)(2,1)S(1)}, bf16[256,1024]{1,0:T(8,128)(2,1)S(1)}, u32[]{:S(2)}, u32[]{:S(2)}) collective-permute-start(bf16[256,1024]{1,0:T(8,128)(2,1)S(1)} %pad_maximum_fusion.refs_0_), channel_id=1, source_target_pairs={{0,2},{1,3},{2,0},{3,1},{4,6},{5,7},{6,4},{7,5},{8,10},{9,11},{10,... | collective-permute-start | bytes 1572872 | tf_op jit(solution)/shard_map/ppermute | solution.py:66
  8.1 0.1 pad_maximum_fusion.1.refs_1_
  8.2 9.5 %collective-permute-done.refs_4_ = bf16[256,1024]{1,0:T(8,128)(2,1)S(1)} collective-permute-done((bf16[256,1024]{1,0:T(8,128)(2,1)S(1)}, bf16[256,1024]{1,0:T(8,128)(2,1)S(1)}, u32[]{:S(2)}, u32[]{:S(2)}) %collective-permute-start) | collective-permute-done | bytes 524320 | tf_op jit(solution)/shard_map/ppermute | solution.py:66
  17.7 0.0 collective-permute-done.1
  17.7 1.3 %collective-permute-start.6 = (bf16[256,1024]{1,0:T(8,128)(2,1)}, bf16[256,1024]{1,0:T(8,128)(2,1)}, u32[]{:S(2)}, u32[]{:S(2)}) collective-permute-start(bf16[256,1024]{1,0:T(8,128)(2,1)} %collective-permute-done.1), channel_id=1, source_target_pairs={{4,0},{5,1},{6,2},{7,3},{8,12},{9,13},{10,14},{11,15},{20,16},{21,... | collective-permute-start | bytes 1572872 | tf_op jit(solution)/shard_map/ppermute | solution.py:66
  19.0 1.5 %collective-permute-start.5 = (bf16[256,1024]{1,0:T(8,128)(2,1)S(1)}, bf16[256,1024]{1,0:T(8,128)(2,1)}, u32[]{:S(2)}, u32[]{:S(2)}) collective-permute-start(bf16[256,1024]{1,0:T(8,128)(2,1)S(1)} %collective-permute-done.refs_4_), channel_id=1, source_target_pairs={{4,8},{5,9},{6,10},{7,11},{8,4},{9,5},{10,6},{11,7},{20,24},{21,25... | collective-permute-start | bytes 1572872 | tf_op jit(solution)/shard_map/ppermute | solution.py:66
  20.5 0.1 collective-permute-done.2.refs_2_
  20.6 1.5 %collective-permute-start.8 = (bf16[256,1024]{1,0:T(8,128)(2,1)S(1)}, bf16[256,1024]{1,0:T(8,128)(2,1)S(1)}, u32[]{:S(2)}, u32[]{:S(2)}) collective-permute-start(bf16[256,1024]{1,0:T(8,128)(2,1)S(1)} %collective-permute-done.refs_4_), channel_id=1, source_target_pairs={{0,2},{1,3},{2,0},{3,1},{4,6},{5,7},{6,4},{7,5},{8,10},{9,11},{10,... | collective-permute-start | bytes 1572872 | tf_op jit(solution)/shard_map/ppermute | solution.py:66
  22.2 1.5 %collective-permute-start.4 = (bf16[256,1024]{1,0:T(8,128)(2,1)S(1)}, bf16[256,1024]{1,0:T(8,128)(2,1)S(1)}, u32[]{:S(2)}, u32[]{:S(2)}) collective-permute-start(bf16[256,1024]{1,0:T(8,128)(2,1)S(1)} %collective-permute-done.2.refs_2_), channel_id=1, source_target_pairs={{0,16},{1,17},{2,18},{3,19},{4,20},{5,21},{6,22},{7,23},{8,24},{9,... | collective-permute-start | bytes 1572872 | tf_op jit(solution)/shard_map/ppermute | solution.py:66
  23.7 0.1 stack.47.place
  23.8 8.4 %normed_halves.1 = (bf16[16,320,256]{2,1,0:T(8,128)(2,1)}, bf16[16,320,256]{2,1,0:T(8,128)(2,1)}) custom-call(s32[11]{0:T(128)S(1)} %stack.47.place, bf16[320,8192]{1,0:T(8,128)(2,1)} %bitcast.29, bf16[320,8192]{1,0:T(8,128)(2,1)} %collective-permute-done.3.refs_1_), custom_call_target="tpu_custom_call" | custom-call | flops 1000 | bytes 1000 | tf_op jit(solution)/shard_map/normed_halves/pallas_call | solution.py:137
  32.1 3.8 %collective-permute-done.6 = bf16[256,1024]{1,0:T(8,128)(2,1)} collective-permute-done((bf16[256,1024]{1,0:T(8,128)(2,1)}, bf16[256,1024]{1,0:T(8,128)(2,1)}, u32[]{:S(2)}, u32[]{:S(2)}) %collective-permute-start.6) | collective-permute-done | bytes 524320 | tf_op jit(solution)/shard_map/ppermute | solution.py:66
  35.9 0.0 collective-permute-done.5
  35.9 1.5 %collective-permute-start.7 = (bf16[256,1024]{1,0:T(8,128)(2,1)}, bf16[256,1024]{1,0:T(8,128)(2,1)S(1)}, u32[]{:S(2)}, u32[]{:S(2)}) collective-permute-start(bf16[256,1024]{1,0:T(8,128)(2,1)} %collective-permute-done.5), channel_id=1, source_target_pairs={{4,0},{5,1},{6,2},{7,3},{8,12},{9,13},{10,14},{11,15},{20,16},{21,... | collective-permute-start | bytes 1572872 | tf_op jit(solution)/shard_map/ppermute | solution.py:66
  37.5 0.0 collective-permute-done.8.refs_5_
  37.5 1.1 broadcast_select_fusion.1.refs_0_
  38.6 1.6 %collective-permute-start.10 = (bf16[256,1024]{1,0:T(8,128)(2,1)S(1)}, bf16[256,1024]{1,0:T(8,128)(2,1)S(1)}, u32[]{:S(2)}, u32[]{:S(2)}) collective-permute-start(bf16[256,1024]{1,0:T(8,128)(2,1)S(1)} %broadcast_select_fusion.1.refs_0_), channel_id=1, source_target_pairs={{0,2},{1,3},{2,0},{3,1},{4,6},{5,7},{6,4},{7,5},{8,10},{9,11},{10,... | collective-permute-start | bytes 1572872 | tf_op jit(solution)/shard_map/ppermute | solution.py:66
  40.2 1.5 %collective-permute-start.11 = (bf16[256,1024]{1,0:T(8,128)(2,1)S(1)}, bf16[256,1024]{1,0:T(8,128)(2,1)S(1)}, u32[]{:S(2)}, u32[]{:S(2)}) collective-permute-start(bf16[256,1024]{1,0:T(8,128)(2,1)S(1)} %broadcast_select_fusion.1.refs_0_), channel_id=1, source_target_pairs={{0,16},{1,17},{2,18},{3,19},{4,20},{5,21},{6,22},{7,23},{8,24},{9,... | collective-permute-start | bytes 1572872 | tf_op jit(solution)/shard_map/ppermute | solution.py:66
  41.7 11.1 %collective-permute-done.7 = bf16[256,1024]{1,0:T(8,128)(2,1)S(1)} collective-permute-done((bf16[256,1024]{1,0:T(8,128)(2,1)}, bf16[256,1024]{1,0:T(8,128)(2,1)S(1)}, u32[]{:S(2)}, u32[]{:S(2)}) %collective-permute-start.7) | collective-permute-done | bytes 524320 | tf_op jit(solution)/shard_map/ppermute | solution.py:66
  52.8 0.0 collective-permute-start.9
  52.8 0.1 collective-permute-done.11.refs_1_
  52.9 0.1 broadcast_select_fusion.refs_3_
  52.9 1.6 %collective-permute-start.13 = (bf16[256,1024]{1,0:T(8,128)(2,1)S(1)}, bf16[256,1024]{1,0:T(8,128)(2,1)S(1)}, u32[]{:S(2)}, u32[]{:S(2)}) collective-permute-start(bf16[256,1024]{1,0:T(8,128)(2,1)S(1)} %broadcast_select_fusion.refs_3_), channel_id=1, source_target_pairs={{0,16},{1,17},{2,18},{3,19},{4,20},{5,21},{6,22},{7,23},{8,24},{9,... | collective-permute-start | bytes 1572872 | tf_op jit(solution)/shard_map/ppermute | solution.py:66
  54.5 1.5 %collective-permute-start.14 = (bf16[256,1024]{1,0:T(8,128)(2,1)S(1)}, bf16[256,1024]{1,0:T(8,128)(2,1)S(1)}, u32[]{:S(2)}, u32[]{:S(2)}) collective-permute-start(bf16[256,1024]{1,0:T(8,128)(2,1)S(1)} %broadcast_select_fusion.refs_3_), channel_id=1, source_target_pairs={{0,2},{1,3},{2,0},{3,1},{4,6},{5,7},{6,4},{7,5},{8,10},{9,11},{10,... | collective-permute-start | bytes 1572872 | tf_op jit(solution)/shard_map/ppermute | solution.py:66
  56.0 1.7 %copy-done.1 = bf16[16,320,256]{2,1,0:T(8,128)(2,1)S(1)} copy-done((bf16[16,320,256]{2,1,0:T(8,128)(2,1)S(1)}, bf16[16,320,256]{2,1,0:T(8,128)(2,1)}, u32[]{:S(2)}) %copy-start.1) | copy-done | bytes 2621464
  57.7 3.5 %add_product.3 = (f32[320,1024]{1,0:T(8,128)S(1)}, f32[320,1024]{1,0:T(8,128)S(1)}) custom-call(s32[11]{0:T(128)S(1)} %stack.47.place, bf16[16,320,256]{2,1,0:T(8,128)(2,1)S(1)} %copy-done, bf16[16,320,256]{2,1,0:T(8,128)(2,1)S(1)} %copy-done.1, bf16[256,1024]{1,0:T(8,128)(2,1)S(1)} %pad_maximum_fusion.refs_0_, ...), custom_call_target="tpu_custom_call" | custom-call | flops 1000 | bytes 1000 | tf_op jit(solution)/shard_map/add_product/pallas_call | solution.py:204
  61.2 3.7 %collective-permute-done.9.refs_4_ = bf16[256,1024]{1,0:T(8,128)(2,1)S(1)} collective-permute-done((bf16[256,1024]{1,0:T(8,128)(2,1)S(1)}, bf16[256,1024]{1,0:T(8,128)(2,1)S(1)}, u32[]{:S(2)}, u32[]{:S(2)}) %collective-permute-start.9) | collective-permute-done | bytes 524320 | tf_op jit(solution)/shard_map/ppermute | solution.py:66
  64.9 0.4 collective-permute-start.12
  65.3 1.3 %collective-permute-done.14.refs_6_ = bf16[256,1024]{1,0:T(8,128)(2,1)S(1)} collective-permute-done((bf16[256,1024]{1,0:T(8,128)(2,1)S(1)}, bf16[256,1024]{1,0:T(8,128)(2,1)S(1)}, u32[]{:S(2)}, u32[]{:S(2)}) %collective-permute-start.14) | collective-permute-done | bytes 524320 | tf_op jit(solution)/shard_map/ppermute | solution.py:66
  66.6 1.4 %collective-permute-start.16 = (bf16[256,1024]{1,0:T(8,128)(2,1)S(1)}, bf16[256,1024]{1,0:T(8,128)(2,1)S(1)}, u32[]{:S(2)}, u32[]{:S(2)}) collective-permute-start(bf16[256,1024]{1,0:T(8,128)(2,1)S(1)} %collective-permute-done.13.refs_5_), channel_id=1, source_target_pairs={{0,2},{1,3},{2,0},{3,1},{4,6},{5,7},{6,4},{7,5},{8,10},{9,11},{10,... | collective-permute-start | bytes 1572872 | tf_op jit(solution)/shard_map/ppermute | solution.py:66
  68.0 0.4 collective-permute-start.15
  68.4 4.3 %add_product.4 = (f32[320,1024]{1,0:T(8,128)S(1)}, f32[320,1024]{1,0:T(8,128)S(1)}) custom-call(s32[11]{0:T(128)S(1)} %stack.47.place, bf16[16,320,256]{2,1,0:T(8,128)(2,1)S(1)} %copy-done, bf16[16,320,256]{2,1,0:T(8,128)(2,1)S(1)} %copy-done.2, bf16[256,1024]{1,0:T(8,128)(2,1)S(1)} %broadcast_select_fusion.1.refs_0_, ...), custom_call_target="tpu_custom_call" | custom-call | flops 1000 | bytes 1000 | tf_op jit(solution)/shard_map/add_product/pallas_call | solution.py:204
  72.8 3.3 %collective-permute-done.12.refs_0_ = bf16[256,1024]{1,0:T(8,128)(2,1)S(1)} collective-permute-done((bf16[256,1024]{1,0:T(8,128)(2,1)S(1)}, bf16[256,1024]{1,0:T(8,128)(2,1)S(1)}, u32[]{:S(2)}, u32[]{:S(2)}) %collective-permute-start.12) | collective-permute-done | bytes 524320 | tf_op jit(solution)/shard_map/ppermute | solution.py:66
  76.0 1.4 %collective-permute-done.16.refs_2_ = bf16[256,1024]{1,0:T(8,128)(2,1)S(1)} collective-permute-done((bf16[256,1024]{1,0:T(8,128)(2,1)S(1)}, bf16[256,1024]{1,0:T(8,128)(2,1)S(1)}, u32[]{:S(2)}, u32[]{:S(2)}) %collective-permute-start.16) | collective-permute-done | bytes 524320 | tf_op jit(solution)/shard_map/ppermute | solution.py:66
  77.4 0.8 collective-permute-done.15.refs_1_
  78.2 0.0 copy-start.7
  78.2 0.0 copy-start.8
  78.2 0.0 copy-start.12
  78.2 0.0 copy-start.13
  78.2 2.4 %add_product.5 = (f32[320,1024]{1,0:T(8,128)S(1)}, f32[320,1024]{1,0:T(8,128)S(1)}) custom-call(s32[11]{0:T(128)S(1)} %stack.47.place, bf16[16,320,256]{2,1,0:T(8,128)(2,1)S(1)} %copy-done, bf16[16,320,256]{2,1,0:T(8,128)(2,1)S(1)} %copy-done.2, bf16[256,1024]{1,0:T(8,128)(2,1)S(1)} %collective-permute-done.12.refs_0_, ...), custom_call_target="tpu_custom_call" | custom-call | flops 1000 | bytes 1000 | tf_op jit(solution)/shard_map/add_product/pallas_call | solution.py:204
  80.6 0.1 collective-permute-start.17
  80.7 3.0 %collective-permute-done.17.refs_1_ = f32[320,1024]{1,0:T(8,128)S(1)} collective-permute-done((f32[320,1024]{1,0:T(8,128)S(1)}, f32[320,1024]{1,0:T(8,128)S(1)}, u32[]{:S(2)}, u32[]{:S(2)}) %collective-permute-start.17) | collective-permute-done | bytes 1310752 | tf_op jit(solution)/shard_map/ppermute | solution.py:66
  83.8 1.9 %cache_rows.1 = bf16[16,80,256]{2,1,0:T(8,128)(2,1)} custom-call(s32[11]{0:T(128)S(1)} %stack.47.place, s32[2]{0:T(128)S(1)} %copy-done.12, s32[8]{0:T(128)S(1)} %copy-done.13, f32[320,1024]{1,0:T(8,128)S(1)} %get-tuple-element.44.refs_0_, f32[320,1024]{1,0:T(8,128)S(1)} %collective-permute-done.17.refs_1_, f32[41,128]{1,0:T(8,128)S(1)} %copy-done.5, ...), custom_call_target="tpu_custom_call" | custom-call | flops 1000 | bytes 1000 | tf_op jit(solution)/shard_map/cache_rows/pallas_call | solution.py:279
  85.7 6.1 %all-to-all-start = ((bf16[16,80,256]{2,1,0:T(8,128)(2,1)}), bf16[16,80,256]{2,1,0:T(8,128)(2,1)S(1)}, u32[]{:S(2)}, u32[]{:S(2)}) async-start(bf16[16,80,256]{2,1,0:T(8,128)(2,1)} %cache_rows.1), calls=%async_computation | async-start | bytes 1310720 | tf_op jit(solution)/shard_map/all_to_all | solution.py:476
  91.7 16.6 %all-to-all-done = bf16[16,80,256]{2,1,0:T(8,128)(2,1)S(1)} async-done(((bf16[16,80,256]{2,1,0:T(8,128)(2,1)}), bf16[16,80,256]{2,1,0:T(8,128)(2,1)S(1)}, u32[]{:S(2)}, u32[]{:S(2)}) %all-to-all-start) | async-done | bytes 655392 | tf_op jit(solution)/shard_map/all_to_all | solution.py:476
  108.3 1.1 decode.1
  109.4 0.1 collective-permute-start.18
  109.6 0.1 constant_dynamic-slice_fusion.2
  109.7 0.8 copied.1
  110.5 0.1 copy.21
  110.6 0.1 copy.25
  110.8 0.2 copy.20
  111.0 0.1 constant_dynamic-slice_fusion.1
  111.0 0.1 copy.23
  111.2 0.1 copy.26
  111.3 0.2 copy.24
  111.5 0.1 fusion.1
  111.6 0.1 copy.18
  111.7 0.6 copy.29
  (33 shorter events, 0.1 us)
Async XLA Ops:
  0.6 20.0 %collective-permute-start.3 = (bf16[320,8192]{1,0:T(8,128)(2,1)}, bf16[320,8192]{1,0:T(8,128)(2,1)}, u32[]{:S(2)}, u32[]{:S(2)}) collective-permute-start(bf16[320,8192]{1,0:T(8,128)(2,1)} %bitcast.28), channel_id=1, source_target_pairs={{0,1},{1,0},{2,3},{3,2},{4,5},{5,4},{6,7},{7,6},{8,9},{9,8},{10,11... | collective-permute-start | bytes 15728648 | tf_op jit(solution)/shard_map/ppermute | solution.py:66
  2.5 15.2 %collective-permute-start = (bf16[256,1024]{1,0:T(8,128)(2,1)S(1)}, bf16[256,1024]{1,0:T(8,128)(2,1)S(1)}, u32[]{:S(2)}, u32[]{:S(2)}) collective-permute-start(bf16[256,1024]{1,0:T(8,128)(2,1)S(1)} %pad_maximum_fusion.refs_0_), channel_id=1, source_target_pairs={{0,4},{1,5},{2,6},{3,7},{4,0},{5,1},{6,2},{7,3},{8,12},{9,13},{10,... | collective-permute-start | bytes 1572872 | tf_op jit(solution)/shard_map/ppermute | solution.py:66
  5.1 12.6 %collective-permute-start.1 = (bf16[256,1024]{1,0:T(8,128)(2,1)S(1)}, bf16[256,1024]{1,0:T(8,128)(2,1)}, u32[]{:S(2)}, u32[]{:S(2)}) collective-permute-start(bf16[256,1024]{1,0:T(8,128)(2,1)S(1)} %pad_maximum_fusion.refs_0_), channel_id=1, source_target_pairs={{4,8},{5,9},{6,10},{7,11},{8,4},{9,5},{10,6},{11,7},{20,24},{21,25... | collective-permute-start | bytes 1572872 | tf_op jit(solution)/shard_map/ppermute | solution.py:66
  6.6 14.0 %collective-permute-start.2 = (bf16[256,1024]{1,0:T(8,128)(2,1)S(1)}, bf16[256,1024]{1,0:T(8,128)(2,1)S(1)}, u32[]{:S(2)}, u32[]{:S(2)}) collective-permute-start(bf16[256,1024]{1,0:T(8,128)(2,1)S(1)} %pad_maximum_fusion.refs_0_), channel_id=1, source_target_pairs={{0,2},{1,3},{2,0},{3,1},{4,6},{5,7},{6,4},{7,5},{8,10},{9,11},{10,... | collective-permute-start | bytes 1572872 | tf_op jit(solution)/shard_map/ppermute | solution.py:66
  17.7 18.2 %collective-permute-start.6 = (bf16[256,1024]{1,0:T(8,128)(2,1)}, bf16[256,1024]{1,0:T(8,128)(2,1)}, u32[]{:S(2)}, u32[]{:S(2)}) collective-permute-start(bf16[256,1024]{1,0:T(8,128)(2,1)} %collective-permute-done.1), channel_id=1, source_target_pairs={{4,0},{5,1},{6,2},{7,3},{8,12},{9,13},{10,14},{11,15},{20,16},{21,... | collective-permute-start | bytes 1572872 | tf_op jit(solution)/shard_map/ppermute | solution.py:66
  19.0 16.9 %collective-permute-start.5 = (bf16[256,1024]{1,0:T(8,128)(2,1)S(1)}, bf16[256,1024]{1,0:T(8,128)(2,1)}, u32[]{:S(2)}, u32[]{:S(2)}) collective-permute-start(bf16[256,1024]{1,0:T(8,128)(2,1)S(1)} %collective-permute-done.refs_4_), channel_id=1, source_target_pairs={{4,8},{5,9},{6,10},{7,11},{8,4},{9,5},{10,6},{11,7},{20,24},{21,25... | collective-permute-start | bytes 1572872 | tf_op jit(solution)/shard_map/ppermute | solution.py:66
  20.6 16.9 %collective-permute-start.8 = (bf16[256,1024]{1,0:T(8,128)(2,1)S(1)}, bf16[256,1024]{1,0:T(8,128)(2,1)S(1)}, u32[]{:S(2)}, u32[]{:S(2)}) collective-permute-start(bf16[256,1024]{1,0:T(8,128)(2,1)S(1)} %collective-permute-done.refs_4_), channel_id=1, source_target_pairs={{0,2},{1,3},{2,0},{3,1},{4,6},{5,7},{6,4},{7,5},{8,10},{9,11},{10,... | collective-permute-start | bytes 1572872 | tf_op jit(solution)/shard_map/ppermute | solution.py:66
  22.2 15.3 %collective-permute-start.4 = (bf16[256,1024]{1,0:T(8,128)(2,1)S(1)}, bf16[256,1024]{1,0:T(8,128)(2,1)S(1)}, u32[]{:S(2)}, u32[]{:S(2)}) collective-permute-start(bf16[256,1024]{1,0:T(8,128)(2,1)S(1)} %collective-permute-done.2.refs_2_), channel_id=1, source_target_pairs={{0,16},{1,17},{2,18},{3,19},{4,20},{5,21},{6,22},{7,23},{8,24},{9,... | collective-permute-start | bytes 1572872 | tf_op jit(solution)/shard_map/ppermute | solution.py:66
  35.9 20.0 %copy-start = (bf16[16,320,256]{2,1,0:T(8,128)(2,1)S(1)}, bf16[16,320,256]{2,1,0:T(8,128)(2,1)}, u32[]{:S(2)}) copy-start(bf16[16,320,256]{2,1,0:T(8,128)(2,1)} %get-tuple-element.43.mine) | copy-start | bytes 7864324
  35.9 16.8 %collective-permute-start.7 = (bf16[256,1024]{1,0:T(8,128)(2,1)}, bf16[256,1024]{1,0:T(8,128)(2,1)S(1)}, u32[]{:S(2)}, u32[]{:S(2)}) collective-permute-start(bf16[256,1024]{1,0:T(8,128)(2,1)} %collective-permute-done.5), channel_id=1, source_target_pairs={{4,0},{5,1},{6,2},{7,3},{8,12},{9,13},{10,14},{11,15},{20,16},{21,... | collective-permute-start | bytes 1572872 | tf_op jit(solution)/shard_map/ppermute | solution.py:66
  38.6 14.2 %collective-permute-start.10 = (bf16[256,1024]{1,0:T(8,128)(2,1)S(1)}, bf16[256,1024]{1,0:T(8,128)(2,1)S(1)}, u32[]{:S(2)}, u32[]{:S(2)}) collective-permute-start(bf16[256,1024]{1,0:T(8,128)(2,1)S(1)} %broadcast_select_fusion.1.refs_0_), channel_id=1, source_target_pairs={{0,2},{1,3},{2,0},{3,1},{4,6},{5,7},{6,4},{7,5},{8,10},{9,11},{10,... | collective-permute-start | bytes 1572872 | tf_op jit(solution)/shard_map/ppermute | solution.py:66
  40.2 12.7 %collective-permute-start.11 = (bf16[256,1024]{1,0:T(8,128)(2,1)S(1)}, bf16[256,1024]{1,0:T(8,128)(2,1)S(1)}, u32[]{:S(2)}, u32[]{:S(2)}) collective-permute-start(bf16[256,1024]{1,0:T(8,128)(2,1)S(1)} %broadcast_select_fusion.1.refs_0_), channel_id=1, source_target_pairs={{0,16},{1,17},{2,18},{3,19},{4,20},{5,21},{6,22},{7,23},{8,24},{9,... | collective-permute-start | bytes 1572872 | tf_op jit(solution)/shard_map/ppermute | solution.py:66
  52.8 12.1 %collective-permute-start.9 = (bf16[256,1024]{1,0:T(8,128)(2,1)S(1)}, bf16[256,1024]{1,0:T(8,128)(2,1)S(1)}, u32[]{:S(2)}, u32[]{:S(2)}) collective-permute-start(bf16[256,1024]{1,0:T(8,128)(2,1)S(1)} %pad_maximum_fusion.1.refs_1_), channel_id=1, source_target_pairs={{0,4},{1,5},{2,6},{3,7},{4,0},{5,1},{6,2},{7,3},{8,12},{9,13},{10,... | collective-permute-start | bytes 1572872 | tf_op jit(solution)/shard_map/ppermute | solution.py:66
  52.9 12.4 %collective-permute-start.13 = (bf16[256,1024]{1,0:T(8,128)(2,1)S(1)}, bf16[256,1024]{1,0:T(8,128)(2,1)S(1)}, u32[]{:S(2)}, u32[]{:S(2)}) collective-permute-start(bf16[256,1024]{1,0:T(8,128)(2,1)S(1)} %broadcast_select_fusion.refs_3_), channel_id=1, source_target_pairs={{0,16},{1,17},{2,18},{3,19},{4,20},{5,21},{6,22},{7,23},{8,24},{9,... | collective-permute-start | bytes 1572872 | tf_op jit(solution)/shard_map/ppermute | solution.py:66
  54.5 12.1 %collective-permute-start.14 = (bf16[256,1024]{1,0:T(8,128)(2,1)S(1)}, bf16[256,1024]{1,0:T(8,128)(2,1)S(1)}, u32[]{:S(2)}, u32[]{:S(2)}) collective-permute-start(bf16[256,1024]{1,0:T(8,128)(2,1)S(1)} %broadcast_select_fusion.refs_3_), channel_id=1, source_target_pairs={{0,2},{1,3},{2,0},{3,1},{4,6},{5,7},{6,4},{7,5},{8,10},{9,11},{10,... | collective-permute-start | bytes 1572872 | tf_op jit(solution)/shard_map/ppermute | solution.py:66
  56.0 1.7 %copy-start.1 = (bf16[16,320,256]{2,1,0:T(8,128)(2,1)S(1)}, bf16[16,320,256]{2,1,0:T(8,128)(2,1)}, u32[]{:S(2)}) copy-start(bf16[16,320,256]{2,1,0:T(8,128)(2,1)} %get-tuple-element.34.other) | copy-start | bytes 7864324
  57.7 10.7 %copy-start.2 = (bf16[16,320,256]{2,1,0:T(8,128)(2,1)S(1)}, bf16[16,320,256]{2,1,0:T(8,128)(2,1)}, u32[]{:S(2)}) copy-start(bf16[16,320,256]{2,1,0:T(8,128)(2,1)} %get-tuple-element.34.other) | copy-start | bytes 7864324
  64.9 11.1 %collective-permute-start.12 = (bf16[256,1024]{1,0:T(8,128)(2,1)S(1)}, bf16[256,1024]{1,0:T(8,128)(2,1)S(1)}, u32[]{:S(2)}, u32[]{:S(2)}) collective-permute-start(bf16[256,1024]{1,0:T(8,128)(2,1)S(1)} %collective-permute-done.4.refs_3_), channel_id=1, source_target_pairs={{0,4},{1,5},{2,6},{3,7},{4,0},{5,1},{6,2},{7,3},{8,12},{9,13},{10,... | collective-permute-start | bytes 1572872 | tf_op jit(solution)/shard_map/ppermute | solution.py:66
  66.6 10.8 %collective-permute-start.16 = (bf16[256,1024]{1,0:T(8,128)(2,1)S(1)}, bf16[256,1024]{1,0:T(8,128)(2,1)S(1)}, u32[]{:S(2)}, u32[]{:S(2)}) collective-permute-start(bf16[256,1024]{1,0:T(8,128)(2,1)S(1)} %collective-permute-done.13.refs_5_), channel_id=1, source_target_pairs={{0,2},{1,3},{2,0},{3,1},{4,6},{5,7},{6,4},{7,5},{8,10},{9,11},{10,... | collective-permute-start | bytes 1572872 | tf_op jit(solution)/shard_map/ppermute | solution.py:66
  68.0 10.1 %collective-permute-start.15 = (bf16[256,1024]{1,0:T(8,128)(2,1)S(1)}, bf16[256,1024]{1,0:T(8,128)(2,1)S(1)}, u32[]{:S(2)}, u32[]{:S(2)}) collective-permute-start(bf16[256,1024]{1,0:T(8,128)(2,1)S(1)} %collective-permute-done.10.refs_2_), channel_id=1, source_target_pairs={{0,16},{1,17},{2,18},{3,19},{4,20},{5,21},{6,22},{7,23},{8,24},{9,... | collective-permute-start | bytes 1572872 | tf_op jit(solution)/shard_map/ppermute | solution.py:66
  78.2 5.5 %copy-start.3 = (f32[64,128]{1,0:T(8,128)S(1)}, f32[64,128]{1,0:T(8,128)}, u32[]{:S(2)}) copy-start(f32[64,128]{1,0:T(8,128)} %constant.77.clone.refs_4_.refs_2_) | copy-start | bytes 98308
  78.2 5.5 %copy-start.4 = (f32[64,128]{1,0:T(8,128)S(1)}, f32[64,128]{1,0:T(8,128)}, u32[]{:S(2)}) copy-start(f32[64,128]{1,0:T(8,128)} %constant.78.clone.refs_5_.refs_3_) | copy-start | bytes 98308
  78.2 5.5 %copy-start.5 = (f32[41,128]{1,0:T(8,128)S(1)}, f32[41,128]{1,0:T(8,128)}, u32[]{:S(2)}) copy-start(f32[41,128]{1,0:T(8,128)} %constant.75.clone.refs_2_.refs_0_) | copy-start | bytes 62980
  78.2 5.5 %copy-start.6 = (f32[41,128]{1,0:T(8,128)S(1)}, f32[41,128]{1,0:T(8,128)}, u32[]{:S(2)}) copy-start(f32[41,128]{1,0:T(8,128)} %constant.76.clone.refs_3_.refs_1_) | copy-start | bytes 62980
  78.2 5.6 %copy-start.7 = (f32[160,128]{1,0:T(8,128)S(1)}, f32[160,128]{1,0:T(8,128)}, u32[]{:S(2)}) copy-start(f32[160,128]{1,0:T(8,128)} %constant.79.clone.refs_6_) | copy-start | bytes 245764
  78.2 5.6 %copy-start.8 = (f32[160,128]{1,0:T(8,128)S(1)}, f32[160,128]{1,0:T(8,128)}, u32[]{:S(2)}) copy-start(f32[160,128]{1,0:T(8,128)} %constant.80.clone.refs_7_) | copy-start | bytes 245764
  78.2 5.5 %copy-start.12 = (s32[2]{0:T(128)S(1)}, s32[2]{0:T(128)}, u32[]{:S(2)}) copy-start(s32[2]{0:T(128)} %lengths.3) | copy-start | bytes 28
  78.2 5.5 %copy-start.13 = (s32[8]{0:T(128)S(1)}, s32[8]{0:T(128)}, u32[]{:S(2)}) copy-start(s32[8]{0:T(128)} %owner.3) | copy-start | bytes 100
  80.6 3.1 %collective-permute-start.17 = (f32[320,1024]{1,0:T(8,128)S(1)}, f32[320,1024]{1,0:T(8,128)S(1)}, u32[]{:S(2)}, u32[]{:S(2)}) collective-permute-start(f32[320,1024]{1,0:T(8,128)S(1)} %get-tuple-element.45), channel_id=1, source_target_pairs={{0,1},{1,0},{2,3},{3,2},{4,5},{5,4},{6,7},{7,6},{8,9},{9,8},{10,11... | collective-permute-start | bytes 3932168 | tf_op jit(solution)/shard_map/ppermute | solution.py:66
  85.6 22.7 %copy-start.9 = (bf16[8,4,1024]{2,1,0:T(4,128)(2,1)S(1)}, bf16[8,4,1024]{2,1,0:T(4,128)(2,1)}, u32[]{:S(2)}) copy-start(bf16[8,4,1024]{2,1,0:T(4,128)(2,1)} %dec_query.1) | copy-start | bytes 196612
  85.7 22.7 %copy-start.10 = (bf16[8,4,128]{2,1,0:T(4,128)(2,1)S(1)}, bf16[8,4,128]{2,1,0:T(4,128)(2,1)}, u32[]{:S(2)}) copy-start(bf16[8,4,128]{2,1,0:T(4,128)(2,1)} %dec_key.1) | copy-start | bytes 24580
  85.7 22.7 %copy-start.11 = (bf16[8,4,128]{2,1,0:T(4,128)(2,1)S(1)}, bf16[8,4,128]{2,1,0:T(4,128)(2,1)}, u32[]{:S(2)}) copy-start(bf16[8,4,128]{2,1,0:T(4,128)(2,1)} %dec_value.1) | copy-start | bytes 24580
  85.7 22.7 %all-to-all-start = ((bf16[16,80,256]{2,1,0:T(8,128)(2,1)}), bf16[16,80,256]{2,1,0:T(8,128)(2,1)S(1)}, u32[]{:S(2)}, u32[]{:S(2)}) async-start(bf16[16,80,256]{2,1,0:T(8,128)(2,1)} %cache_rows.1), calls=%async_computation | async-start | bytes 1310720 | tf_op jit(solution)/shard_map/all_to_all | solution.py:476
  109.4 1.5 %collective-permute-start.18 = (f32[32,256]{1,0:T(8,128)S(1)}, f32[32,256]{1,0:T(8,128)S(1)}, u32[]{:S(2)}, u32[]{:S(2)}) collective-permute-start(f32[32,256]{1,0:T(8,128)S(1)} %decode.1), channel_id=1, source_target_pairs={{0,1},{1,0},{2,3},{3,2},{4,5},{5,4},{6,7},{7,6},{8,9},{9,8},{10,11... | collective-permute-start | bytes 98312 | tf_op jit(solution)/shard_map/ppermute | solution.py:66

commit v23 on v22

--- a/solution.py
+++ b/solution.py
@@ -80,6 +80,10 @@
 
 def to_pair(g, z, y, c):
     return (g, z ^ 1, y, c)
+
+
+def to_next(g, z, y, c):
+    return (g, z ^ 2, y, c)
 
 
 def to_middle(g, z, y, c):
@@ -441,22 +445,20 @@
         tables = turn_tables(count_rows * seq + STEPS, count_rows)
         near = moved(sent, to_pair)
         middle = moved(sent, to_middle)
+        beyond = moved(sent, to_next)
         across = moved(sent, to_row)
         rest = half_block(depth - group_id * depth)
-        layers, rows = (near, middle), (near, middle, across, raw, rest)
-        passed = moved(after(middle, *layers), to_end)
-        middle_c = moved(near, to_middle)
+        rows = (near, across, raw, rest)
         near_y = moved(after(near, *rows), to_row)
         across_x = moved(after(across, *rows), to_group)
         mine, other = prepared(place, after(flat, *rows), raw, seq // 2)
-        layers, rows = (passed, middle_c, mine), (near_y, across_x, mine, passed)
-        far = moved(after(middle_c, *layers), to_end)
-        block_b = jnp.where(is_end, after(passed, *rows), middle)
+        far = moved(after(beyond, middle, mine), to_end)
+        block_b = after(jnp.where(is_end, beyond, middle), near_y, across_x, mine)
         block_yb = moved(block_b, to_row)
         block_xb = moved(block_b, to_group)
         layers, rows = (far, near_y), (block_yb, block_xb, far)
         near_rest = moved(after(rest, *layers), to_pair)
-        block_c = jnp.where(is_end, after(far, *rows), middle_c)
+        block_c = jnp.where(is_end, after(far, *rows), beyond)
         block_xc = moved(block_c, to_group)
         block_yc = moved(block_c, to_row)
         pieces = [(HERE, 0, sent), (HERE, 1, rest), (THERE, 0, across)]

time: 113 us -> 126 us (1.12)
  waiting for transfers between devices: 54.6 us -> 68.6 us
  starting transfers between devices: 28.1 us -> 25.9 us
  local copies, waits for them, and re-layouts: 4.84 us -> 6.57 us
    ppermute x19 -> x18, waiting for transfers between devices: 38 us -> 52 us  [moved(): return lax.ppermute(block, ('groups', 'seq'), route)]
    ppermute x19 -> x18, starting transfers between devices: 22.1 us -> 19.9 us  [moved(): return lax.ppermute(block, ('groups', 'seq'), route)]
    unnamed x35 -> x33, local copies, waits for them, and re-layouts: 3.18 us -> 4.92 us
  transfers between devices with their start and end apart: 20 -> 19, of which waited for: 12 -> 10; matrix products, arithmetic and copies ran while one was open for 3% -> 2% of each run, Pallas kernels for 15% -> 14%
where the time goes in v23:
time: 126 us
  waiting for transfers between devices  68.6 us (54%)
  starting transfers between devices  25.9 us (21%)
  Pallas kernels  22.4 us (18%)
  local copies, waits for them, and re-layouts  6.57 us (5%)
  other arithmetic  1.39 us (1%)
    ppermute x18, waiting for transfers between devices, moved(): return lax.ppermute(block, ('groups', 'seq'), route)  52 us
    ppermute x18, starting transfers between devices, moved(): return lax.ppermute(block, ('groups', 'seq'), route)  19.9 us
    all_to_all x1, waiting for transfers between devices, body(): lax.all_to_all(outgoing, 'seq', split_axis=0, concat_axis=1, tiled=True)  16.6 us
    pallas_call x3, Pallas kernels, product(): pl.pallas_call(functools.partial(product_kernel, plan, group, bool(totals...  10.2 us
    pallas_call x1, Pallas kernels, prepared(): pl.pallas_call(prepare_kernel, grid_spec=pltpu.PrefetchScalarGridSpec(num...  8.39 us
    all_to_all x1, starting transfers between devices, body(): lax.all_to_all(outgoing, 'seq', split_axis=0, concat_axis=1, tiled=True)  5.96 us
    unnamed x33, local copies, waits for them, and re-layouts  4.92 us
  transfers between devices with their start and end apart: 19, of which 10 were waited for; matrix products, arithmetic and copies ran while one was open for 2% of the time, Pallas kernels for 14%

profile of v23, /device:TPU:0, one launch (start us, length us, event | category | flops | bytes accessed | tf_op | source)
XLA Modules:
  0.0 125.7 jit_solution(16591062811760250308)
XLA Ops:
  0.6 0.5 collective-permute-start.2
  1.1 1.3 constant_dynamic-slice_fusion.6
  2.4 0.1 pad_maximum_fusion.refs_0_
  2.5 2.7 %collective-permute-start = (bf16[256,1024]{1,0:T(8,128)(2,1)S(1)}, bf16[256,1024]{1,0:T(8,128)(2,1)S(1)}, u32[]{:S(2)}, u32[]{:S(2)}) collective-permute-start(bf16[256,1024]{1,0:T(8,128)(2,1)S(1)} %pad_maximum_fusion.refs_0_), channel_id=1, source_target_pairs={{0,4},{1,5},{2,6},{3,7},{4,0},{5,1},{6,2},{7,3},{8,12},{9,13},{10,... | collective-permute-start | bytes 1572872 | tf_op jit(solution)/shard_map/ppermute | solution.py:66
  5.1 1.5 %collective-permute-start.1 = (bf16[256,1024]{1,0:T(8,128)(2,1)S(1)}, bf16[256,1024]{1,0:T(8,128)(2,1)S(1)}, u32[]{:S(2)}, u32[]{:S(2)}) collective-permute-start(bf16[256,1024]{1,0:T(8,128)(2,1)S(1)} %pad_maximum_fusion.refs_0_), channel_id=1, source_target_pairs={{0,2},{1,3},{2,0},{3,1},{4,6},{5,7},{6,4},{7,5},{8,10},{9,11},{10,... | collective-permute-start | bytes 1572872 | tf_op jit(solution)/shard_map/ppermute | solution.py:66
  6.7 2.6 %collective-permute-start.4 = (bf16[256,1024]{1,0:T(8,128)(2,1)S(1)}, bf16[256,1024]{1,0:T(8,128)(2,1)}, u32[]{:S(2)}, u32[]{:S(2)}) collective-permute-start(bf16[256,1024]{1,0:T(8,128)(2,1)S(1)} %pad_maximum_fusion.refs_0_), channel_id=1, source_target_pairs={{0,8},{1,9},{2,10},{3,11},{4,12},{5,13},{6,14},{7,15},{8,0},{9,1},... | collective-permute-start | bytes 1572872 | tf_op jit(solution)/shard_map/ppermute | solution.py:66
  9.2 1.4 %collective-permute-start.5 = (bf16[256,1024]{1,0:T(8,128)(2,1)S(1)}, bf16[256,1024]{1,0:T(8,128)(2,1)}, u32[]{:S(2)}, u32[]{:S(2)}) collective-permute-start(bf16[256,1024]{1,0:T(8,128)(2,1)S(1)} %pad_maximum_fusion.refs_0_), channel_id=1, source_target_pairs={{4,8},{5,9},{6,10},{7,11},{8,4},{9,5},{10,6},{11,7},{20,24},{21,25... | collective-permute-start | bytes 1572872 | tf_op jit(solution)/shard_map/ppermute | solution.py:66
  10.7 0.1 pad_maximum_fusion.1.refs_1_
  10.8 16.8 %collective-permute-done.refs_4_ = bf16[256,1024]{1,0:T(8,128)(2,1)S(1)} collective-permute-done((bf16[256,1024]{1,0:T(8,128)(2,1)S(1)}, bf16[256,1024]{1,0:T(8,128)(2,1)S(1)}, u32[]{:S(2)}, u32[]{:S(2)}) %collective-permute-start) | collective-permute-done | bytes 524320 | tf_op jit(solution)/shard_map/ppermute | solution.py:66
  27.6 0.0 collective-permute-done.1.refs_2_
  27.6 0.0 collective-permute-done.2.refs_1_
  27.6 1.7 %collective-permute-start.3 = (bf16[256,1024]{1,0:T(8,128)(2,1)S(1)}, bf16[256,1024]{1,0:T(8,128)(2,1)S(1)}, u32[]{:S(2)}, u32[]{:S(2)}) collective-permute-start(bf16[256,1024]{1,0:T(8,128)(2,1)S(1)} %collective-permute-done.1.refs_2_), channel_id=1, source_target_pairs={{0,16},{1,17},{2,18},{3,19},{4,20},{5,21},{6,22},{7,23},{8,24},{9,... | collective-permute-start | bytes 1572872 | tf_op jit(solution)/shard_map/ppermute | solution.py:66
  29.3 2.2 %collective-permute-start.7 = (bf16[256,1024]{1,0:T(8,128)(2,1)S(1)}, bf16[256,1024]{1,0:T(8,128)(2,1)S(1)}, u32[]{:S(2)}, u32[]{:S(2)}) collective-permute-start(bf16[256,1024]{1,0:T(8,128)(2,1)S(1)} %collective-permute-done.refs_4_), channel_id=1, source_target_pairs={{0,2},{1,3},{2,0},{3,1},{4,6},{5,7},{6,4},{7,5},{8,10},{9,11},{10,... | collective-permute-start | bytes 1572872 | tf_op jit(solution)/shard_map/ppermute | solution.py:66
  31.5 0.1 stack.47.place
  31.5 2.2 %collective-permute-done.4 = bf16[256,1024]{1,0:T(8,128)(2,1)} collective-permute-done((bf16[256,1024]{1,0:T(8,128)(2,1)S(1)}, bf16[256,1024]{1,0:T(8,128)(2,1)}, u32[]{:S(2)}, u32[]{:S(2)}) %collective-permute-start.4) | collective-permute-done | bytes 524320 | tf_op jit(solution)/shard_map/ppermute | solution.py:66
  33.7 0.0 collective-permute-done.5
  33.7 1.1 broadcast_select_fusion.1.refs_0_
  34.8 8.4 %normed_halves.1 = (bf16[16,320,256]{2,1,0:T(8,128)(2,1)}, bf16[16,320,256]{2,1,0:T(8,128)(2,1)}) custom-call(s32[11]{0:T(128)S(1)} %stack.47.place, bf16[320,8192]{1,0:T(8,128)(2,1)} %bitcast.29, bf16[320,8192]{1,0:T(8,128)(2,1)} %collective-permute-done.2.refs_1_), custom_call_target="tpu_custom_call" | custom-call | flops 1000 | bytes 1000 | tf_op jit(solution)/shard_map/normed_halves/pallas_call | solution.py:141
  43.2 1.3 %collective-permute-start.6 = (bf16[256,1024]{1,0:T(8,128)(2,1)}, bf16[256,1024]{1,0:T(8,128)(2,1)S(1)}, u32[]{:S(2)}, u32[]{:S(2)}) collective-permute-start(bf16[256,1024]{1,0:T(8,128)(2,1)} %collective-permute-done.4), channel_id=1, source_target_pairs={{4,0},{5,1},{6,2},{7,3},{8,12},{9,13},{10,14},{11,15},{20,16},{21,... | collective-permute-start | bytes 1572872 | tf_op jit(solution)/shard_map/ppermute | solution.py:66
  44.5 0.0 collective-permute-done.7.refs_5_
  44.5 1.6 %collective-permute-start.10 = (bf16[256,1024]{1,0:T(8,128)(2,1)S(1)}, bf16[256,1024]{1,0:T(8,128)(2,1)S(1)}, u32[]{:S(2)}, u32[]{:S(2)}) collective-permute-start(bf16[256,1024]{1,0:T(8,128)(2,1)S(1)} %broadcast_select_fusion.1.refs_0_), channel_id=1, source_target_pairs={{0,16},{1,17},{2,18},{3,19},{4,20},{5,21},{6,22},{7,23},{8,24},{9,... | collective-permute-start | bytes 1572872 | tf_op jit(solution)/shard_map/ppermute | solution.py:66
  46.1 0.5 collective-permute-start.9
  46.6 20.1 %collective-permute-done.6 = bf16[256,1024]{1,0:T(8,128)(2,1)S(1)} collective-permute-done((bf16[256,1024]{1,0:T(8,128)(2,1)}, bf16[256,1024]{1,0:T(8,128)(2,1)S(1)}, u32[]{:S(2)}, u32[]{:S(2)}) %collective-permute-start.6) | collective-permute-done | bytes 524320 | tf_op jit(solution)/shard_map/ppermute | solution.py:66
  66.7 0.1 broadcast_select_fusion.refs_3_
  66.8 1.6 %collective-permute-start.12 = (bf16[256,1024]{1,0:T(8,128)(2,1)S(1)}, bf16[256,1024]{1,0:T(8,128)(2,1)S(1)}, u32[]{:S(2)}, u32[]{:S(2)}) collective-permute-start(bf16[256,1024]{1,0:T(8,128)(2,1)S(1)} %broadcast_select_fusion.refs_3_), channel_id=1, source_target_pairs={{0,16},{1,17},{2,18},{3,19},{4,20},{5,21},{6,22},{7,23},{8,24},{9,... | collective-permute-start | bytes 1572872 | tf_op jit(solution)/shard_map/ppermute | solution.py:66
  68.3 0.5 collective-permute-start.13
  68.8 1.7 %copy-done = bf16[16,320,256]{2,1,0:T(8,128)(2,1)S(1)} copy-done((bf16[16,320,256]{2,1,0:T(8,128)(2,1)S(1)}, bf16[16,320,256]{2,1,0:T(8,128)(2,1)}, u32[]{:S(2)}) %copy-start) | copy-done | bytes 2621464
  70.6 1.7 %copy-done.1 = bf16[16,320,256]{2,1,0:T(8,128)(2,1)S(1)} copy-done((bf16[16,320,256]{2,1,0:T(8,128)(2,1)S(1)}, bf16[16,320,256]{2,1,0:T(8,128)(2,1)}, u32[]{:S(2)}) %copy-start.1) | copy-done | bytes 2621464
  72.3 3.5 %add_product.3 = (f32[320,1024]{1,0:T(8,128)S(1)}, f32[320,1024]{1,0:T(8,128)S(1)}) custom-call(s32[11]{0:T(128)S(1)} %stack.47.place, bf16[16,320,256]{2,1,0:T(8,128)(2,1)S(1)} %copy-done, bf16[16,320,256]{2,1,0:T(8,128)(2,1)S(1)} %copy-done.1, bf16[256,1024]{1,0:T(8,128)(2,1)S(1)} %pad_maximum_fusion.refs_0_, ...), custom_call_target="tpu_custom_call" | custom-call | flops 1000 | bytes 1000 | tf_op jit(solution)/shard_map/add_product/pallas_call | solution.py:208
  75.8 3.2 %collective-permute-done.8.refs_4_ = bf16[256,1024]{1,0:T(8,128)(2,1)S(1)} collective-permute-done((bf16[256,1024]{1,0:T(8,128)(2,1)S(1)}, bf16[256,1024]{1,0:T(8,128)(2,1)S(1)}, u32[]{:S(2)}, u32[]{:S(2)}) %collective-permute-start.8) | collective-permute-done | bytes 524320 | tf_op jit(solution)/shard_map/ppermute | solution.py:66
  79.0 0.3 collective-permute-start.11
  79.3 0.0 collective-permute-done.12.refs_5_
  79.3 1.1 collective-permute-done.13.refs_6_
  80.4 0.5 collective-permute-start.15
  80.9 0.9 collective-permute-start.14
  81.9 4.3 %add_product.4 = (f32[320,1024]{1,0:T(8,128)S(1)}, f32[320,1024]{1,0:T(8,128)S(1)}) custom-call(s32[11]{0:T(128)S(1)} %stack.47.place, bf16[16,320,256]{2,1,0:T(8,128)(2,1)S(1)} %copy-done, bf16[16,320,256]{2,1,0:T(8,128)(2,1)S(1)} %copy-done.1, bf16[256,1024]{1,0:T(8,128)(2,1)S(1)} %broadcast_select_fusion.1.refs_0_, ...), custom_call_target="tpu_custom_call" | custom-call | flops 1000 | bytes 1000 | tf_op jit(solution)/shard_map/add_product/pallas_call | solution.py:208
  86.2 4.2 %collective-permute-done.11.refs_0_ = bf16[256,1024]{1,0:T(8,128)(2,1)S(1)} collective-permute-done((bf16[256,1024]{1,0:T(8,128)(2,1)S(1)}, bf16[256,1024]{1,0:T(8,128)(2,1)S(1)}, u32[]{:S(2)}, u32[]{:S(2)}) %collective-permute-start.11) | collective-permute-done | bytes 524320 | tf_op jit(solution)/shard_map/ppermute | solution.py:66
  90.4 1.2 collective-permute-done.15.refs_2_
  91.6 0.1 collective-permute-done.14.refs_1_
  91.7 0.0 copy-start.6
  91.7 0.0 copy-start.7
  91.8 0.0 copy-start.11
  91.8 0.0 copy-start.12
  91.8 2.4 %add_product.5 = (f32[320,1024]{1,0:T(8,128)S(1)}, f32[320,1024]{1,0:T(8,128)S(1)}) custom-call(s32[11]{0:T(128)S(1)} %stack.47.place, bf16[16,320,256]{2,1,0:T(8,128)(2,1)S(1)} %copy-done, bf16[16,320,256]{2,1,0:T(8,128)(2,1)S(1)} %copy-done.1, bf16[256,1024]{1,0:T(8,128)(2,1)S(1)} %collective-permute-done.11.refs_0_, ...), custom_call_target="tpu_custom_call" | custom-call | flops 1000 | bytes 1000 | tf_op jit(solution)/shard_map/add_product/pallas_call | solution.py:208
  94.2 0.1 collective-permute-start.16
  94.2 3.0 %collective-permute-done.16.refs_1_ = f32[320,1024]{1,0:T(8,128)S(1)} collective-permute-done((f32[320,1024]{1,0:T(8,128)S(1)}, f32[320,1024]{1,0:T(8,128)S(1)}, u32[]{:S(2)}, u32[]{:S(2)}) %collective-permute-start.16) | collective-permute-done | bytes 1310752 | tf_op jit(solution)/shard_map/ppermute | solution.py:66
  97.3 1.9 %cache_rows.1 = bf16[16,80,256]{2,1,0:T(8,128)(2,1)} custom-call(s32[11]{0:T(128)S(1)} %stack.47.place, s32[2]{0:T(128)S(1)} %copy-done.11, s32[8]{0:T(128)S(1)} %copy-done.12, f32[320,1024]{1,0:T(8,128)S(1)} %get-tuple-element.42.refs_0_, f32[320,1024]{1,0:T(8,128)S(1)} %collective-permute-done.16.refs_1_, f32[41,128]{1,0:T(8,128)S(1)} %copy-done.4, ...), custom_call_target="tpu_custom_call" | custom-call | flops 1000 | bytes 1000 | tf_op jit(solution)/shard_map/cache_rows/pallas_call | solution.py:283
  99.2 6.0 %all-to-all-start = ((bf16[16,80,256]{2,1,0:T(8,128)(2,1)}), bf16[16,80,256]{2,1,0:T(8,128)(2,1)S(1)}, u32[]{:S(2)}, u32[]{:S(2)}) async-start(bf16[16,80,256]{2,1,0:T(8,128)(2,1)} %cache_rows.1), calls=%async_computation | async-start | bytes 1310720 | tf_op jit(solution)/shard_map/all_to_all | solution.py:478
  105.2 16.6 %all-to-all-done = bf16[16,80,256]{2,1,0:T(8,128)(2,1)S(1)} async-done(((bf16[16,80,256]{2,1,0:T(8,128)(2,1)}), bf16[16,80,256]{2,1,0:T(8,128)(2,1)S(1)}, u32[]{:S(2)}, u32[]{:S(2)}) %all-to-all-start) | async-done | bytes 655392 | tf_op jit(solution)/shard_map/all_to_all | solution.py:478
  121.8 1.1 decode.1
  122.9 0.1 collective-permute-start.17
  123.0 0.1 constant_dynamic-slice_fusion.2
  123.1 0.8 copied.1
  124.0 0.1 copy.21
  124.1 0.1 copy.25
  124.2 0.2 copy.20
  124.4 0.0 collective-permute-done.17
  124.4 0.1 constant_dynamic-slice_fusion.1
  124.5 0.1 copy.23
  124.6 0.1 copy.26
  124.7 0.2 copy.24
  124.9 0.1 fusion.1
  125.0 0.1 copy.18
  125.1 0.6 copy.29
  (29 shorter events, 0.1 us)
Async XLA Ops:
  0.6 27.0 %collective-permute-start.2 = (bf16[320,8192]{1,0:T(8,128)(2,1)}, bf16[320,8192]{1,0:T(8,128)(2,1)}, u32[]{:S(2)}, u32[]{:S(2)}) collective-permute-start(bf16[320,8192]{1,0:T(8,128)(2,1)} %bitcast.28), channel_id=1, source_target_pairs={{0,1},{1,0},{2,3},{3,2},{4,5},{5,4},{6,7},{7,6},{8,9},{9,8},{10,11... | collective-permute-start | bytes 15728648 | tf_op jit(solution)/shard_map/ppermute | solution.py:66
  2.5 25.1 %collective-permute-start = (bf16[256,1024]{1,0:T(8,128)(2,1)S(1)}, bf16[256,1024]{1,0:T(8,128)(2,1)S(1)}, u32[]{:S(2)}, u32[]{:S(2)}) collective-permute-start(bf16[256,1024]{1,0:T(8,128)(2,1)S(1)} %pad_maximum_fusion.refs_0_), channel_id=1, source_target_pairs={{0,4},{1,5},{2,6},{3,7},{4,0},{5,1},{6,2},{7,3},{8,12},{9,13},{10,... | collective-permute-start | bytes 1572872 | tf_op jit(solution)/shard_map/ppermute | solution.py:66
  5.1 22.5 %collective-permute-start.1 = (bf16[256,1024]{1,0:T(8,128)(2,1)S(1)}, bf16[256,1024]{1,0:T(8,128)(2,1)S(1)}, u32[]{:S(2)}, u32[]{:S(2)}) collective-permute-start(bf16[256,1024]{1,0:T(8,128)(2,1)S(1)} %pad_maximum_fusion.refs_0_), channel_id=1, source_target_pairs={{0,2},{1,3},{2,0},{3,1},{4,6},{5,7},{6,4},{7,5},{8,10},{9,11},{10,... | collective-permute-start | bytes 1572872 | tf_op jit(solution)/shard_map/ppermute | solution.py:66
  6.7 27.0 %collective-permute-start.4 = (bf16[256,1024]{1,0:T(8,128)(2,1)S(1)}, bf16[256,1024]{1,0:T(8,128)(2,1)}, u32[]{:S(2)}, u32[]{:S(2)}) collective-permute-start(bf16[256,1024]{1,0:T(8,128)(2,1)S(1)} %pad_maximum_fusion.refs_0_), channel_id=1, source_target_pairs={{0,8},{1,9},{2,10},{3,11},{4,12},{5,13},{6,14},{7,15},{8,0},{9,1},... | collective-permute-start | bytes 1572872 | tf_op jit(solution)/shard_map/ppermute | solution.py:66
  9.2 24.5 %collective-permute-start.5 = (bf16[256,1024]{1,0:T(8,128)(2,1)S(1)}, bf16[256,1024]{1,0:T(8,128)(2,1)}, u32[]{:S(2)}, u32[]{:S(2)}) collective-permute-start(bf16[256,1024]{1,0:T(8,128)(2,1)S(1)} %pad_maximum_fusion.refs_0_), channel_id=1, source_target_pairs={{4,8},{5,9},{6,10},{7,11},{8,4},{9,5},{10,6},{11,7},{20,24},{21,25... | collective-permute-start | bytes 1572872 | tf_op jit(solution)/shard_map/ppermute | solution.py:66
  27.6 16.9 %collective-permute-start.3 = (bf16[256,1024]{1,0:T(8,128)(2,1)S(1)}, bf16[256,1024]{1,0:T(8,128)(2,1)S(1)}, u32[]{:S(2)}, u32[]{:S(2)}) collective-permute-start(bf16[256,1024]{1,0:T(8,128)(2,1)S(1)} %collective-permute-done.1.refs_2_), channel_id=1, source_target_pairs={{0,16},{1,17},{2,18},{3,19},{4,20},{5,21},{6,22},{7,23},{8,24},{9,... | collective-permute-start | bytes 1572872 | tf_op jit(solution)/shard_map/ppermute | solution.py:66
  29.3 15.3 %collective-permute-start.7 = (bf16[256,1024]{1,0:T(8,128)(2,1)S(1)}, bf16[256,1024]{1,0:T(8,128)(2,1)S(1)}, u32[]{:S(2)}, u32[]{:S(2)}) collective-permute-start(bf16[256,1024]{1,0:T(8,128)(2,1)S(1)} %collective-permute-done.refs_4_), channel_id=1, source_target_pairs={{0,2},{1,3},{2,0},{3,1},{4,6},{5,7},{6,4},{7,5},{8,10},{9,11},{10,... | collective-permute-start | bytes 1572872 | tf_op jit(solution)/shard_map/ppermute | solution.py:66
  43.2 23.5 %collective-permute-start.6 = (bf16[256,1024]{1,0:T(8,128)(2,1)}, bf16[256,1024]{1,0:T(8,128)(2,1)S(1)}, u32[]{:S(2)}, u32[]{:S(2)}) collective-permute-start(bf16[256,1024]{1,0:T(8,128)(2,1)} %collective-permute-done.4), channel_id=1, source_target_pairs={{4,0},{5,1},{6,2},{7,3},{8,12},{9,13},{10,14},{11,15},{20,16},{21,... | collective-permute-start | bytes 1572872 | tf_op jit(solution)/shard_map/ppermute | solution.py:66
  44.5 22.2 %collective-permute-start.10 = (bf16[256,1024]{1,0:T(8,128)(2,1)S(1)}, bf16[256,1024]{1,0:T(8,128)(2,1)S(1)}, u32[]{:S(2)}, u32[]{:S(2)}) collective-permute-start(bf16[256,1024]{1,0:T(8,128)(2,1)S(1)} %broadcast_select_fusion.1.refs_0_), channel_id=1, source_target_pairs={{0,16},{1,17},{2,18},{3,19},{4,20},{5,21},{6,22},{7,23},{8,24},{9,... | collective-permute-start | bytes 1572872 | tf_op jit(solution)/shard_map/ppermute | solution.py:66
  46.1 20.6 %collective-permute-start.9 = (bf16[256,1024]{1,0:T(8,128)(2,1)S(1)}, bf16[256,1024]{1,0:T(8,128)(2,1)S(1)}, u32[]{:S(2)}, u32[]{:S(2)}) collective-permute-start(bf16[256,1024]{1,0:T(8,128)(2,1)S(1)} %broadcast_select_fusion.1.refs_0_), channel_id=1, source_target_pairs={{0,2},{1,3},{2,0},{3,1},{4,6},{5,7},{6,4},{7,5},{8,10},{9,11},{10,... | collective-permute-start | bytes 1572872 | tf_op jit(solution)/shard_map/ppermute | solution.py:66
  66.7 12.3 %collective-permute-start.8 = (bf16[256,1024]{1,0:T(8,128)(2,1)S(1)}, bf16[256,1024]{1,0:T(8,128)(2,1)S(1)}, u32[]{:S(2)}, u32[]{:S(2)}) collective-permute-start(bf16[256,1024]{1,0:T(8,128)(2,1)S(1)} %pad_maximum_fusion.1.refs_1_), channel_id=1, source_target_pairs={{0,4},{1,5},{2,6},{3,7},{4,0},{5,1},{6,2},{7,3},{8,12},{9,13},{10,... | collective-permute-start | bytes 1572872 | tf_op jit(solution)/shard_map/ppermute | solution.py:66
  66.8 12.5 %collective-permute-start.12 = (bf16[256,1024]{1,0:T(8,128)(2,1)S(1)}, bf16[256,1024]{1,0:T(8,128)(2,1)S(1)}, u32[]{:S(2)}, u32[]{:S(2)}) collective-permute-start(bf16[256,1024]{1,0:T(8,128)(2,1)S(1)} %broadcast_select_fusion.refs_3_), channel_id=1, source_target_pairs={{0,16},{1,17},{2,18},{3,19},{4,20},{5,21},{6,22},{7,23},{8,24},{9,... | collective-permute-start | bytes 1572872 | tf_op jit(solution)/shard_map/ppermute | solution.py:66
  68.3 12.1 %collective-permute-start.13 = (bf16[256,1024]{1,0:T(8,128)(2,1)S(1)}, bf16[256,1024]{1,0:T(8,128)(2,1)S(1)}, u32[]{:S(2)}, u32[]{:S(2)}) collective-permute-start(bf16[256,1024]{1,0:T(8,128)(2,1)S(1)} %broadcast_select_fusion.refs_3_), channel_id=1, source_target_pairs={{0,2},{1,3},{2,0},{3,1},{4,6},{5,7},{6,4},{7,5},{8,10},{9,11},{10,... | collective-permute-start | bytes 1572872 | tf_op jit(solution)/shard_map/ppermute | solution.py:66
  68.8 1.7 %copy-start = (bf16[16,320,256]{2,1,0:T(8,128)(2,1)S(1)}, bf16[16,320,256]{2,1,0:T(8,128)(2,1)}, u32[]{:S(2)}) copy-start(bf16[16,320,256]{2,1,0:T(8,128)(2,1)} %get-tuple-element.41.mine) | copy-start | bytes 7864324
  70.6 1.7 %copy-start.1 = (bf16[16,320,256]{2,1,0:T(8,128)(2,1)S(1)}, bf16[16,320,256]{2,1,0:T(8,128)(2,1)}, u32[]{:S(2)}) copy-start(bf16[16,320,256]{2,1,0:T(8,128)(2,1)} %get-tuple-element.32.other) | copy-start | bytes 7864324
  79.0 11.4 %collective-permute-start.11 = (bf16[256,1024]{1,0:T(8,128)(2,1)S(1)}, bf16[256,1024]{1,0:T(8,128)(2,1)S(1)}, u32[]{:S(2)}, u32[]{:S(2)}) collective-permute-start(bf16[256,1024]{1,0:T(8,128)(2,1)S(1)} %collective-permute-done.3.refs_3_), channel_id=1, source_target_pairs={{0,4},{1,5},{2,6},{3,7},{4,0},{5,1},{6,2},{7,3},{8,12},{9,13},{10,... | collective-permute-start | bytes 1572872 | tf_op jit(solution)/shard_map/ppermute | solution.py:66
  80.4 11.2 %collective-permute-start.15 = (bf16[256,1024]{1,0:T(8,128)(2,1)S(1)}, bf16[256,1024]{1,0:T(8,128)(2,1)S(1)}, u32[]{:S(2)}, u32[]{:S(2)}) collective-permute-start(bf16[256,1024]{1,0:T(8,128)(2,1)S(1)} %collective-permute-done.12.refs_5_), channel_id=1, source_target_pairs={{0,2},{1,3},{2,0},{3,1},{4,6},{5,7},{6,4},{7,5},{8,10},{9,11},{10,... | collective-permute-start | bytes 1572872 | tf_op jit(solution)/shard_map/ppermute | solution.py:66
  80.9 10.8 %collective-permute-start.14 = (bf16[256,1024]{1,0:T(8,128)(2,1)S(1)}, bf16[256,1024]{1,0:T(8,128)(2,1)S(1)}, u32[]{:S(2)}, u32[]{:S(2)}) collective-permute-start(bf16[256,1024]{1,0:T(8,128)(2,1)S(1)} %collective-permute-done.9.refs_2_), channel_id=1, source_target_pairs={{0,16},{1,17},{2,18},{3,19},{4,20},{5,21},{6,22},{7,23},{8,24},{9,... | collective-permute-start | bytes 1572872 | tf_op jit(solution)/shard_map/ppermute | solution.py:66
  91.7 5.5 %copy-start.2 = (f32[64,128]{1,0:T(8,128)S(1)}, f32[64,128]{1,0:T(8,128)}, u32[]{:S(2)}) copy-start(f32[64,128]{1,0:T(8,128)} %constant.77.clone.refs_4_.refs_2_) | copy-start | bytes 98308
  91.7 5.5 %copy-start.3 = (f32[64,128]{1,0:T(8,128)S(1)}, f32[64,128]{1,0:T(8,128)}, u32[]{:S(2)}) copy-start(f32[64,128]{1,0:T(8,128)} %constant.78.clone.refs_5_.refs_3_) | copy-start | bytes 98308
  91.7 5.5 %copy-start.4 = (f32[41,128]{1,0:T(8,128)S(1)}, f32[41,128]{1,0:T(8,128)}, u32[]{:S(2)}) copy-start(f32[41,128]{1,0:T(8,128)} %constant.75.clone.refs_2_.refs_0_) | copy-start | bytes 62980
  91.7 5.5 %copy-start.5 = (f32[41,128]{1,0:T(8,128)S(1)}, f32[41,128]{1,0:T(8,128)}, u32[]{:S(2)}) copy-start(f32[41,128]{1,0:T(8,128)} %constant.76.clone.refs_3_.refs_1_) | copy-start | bytes 62980
  91.7 5.6 %copy-start.6 = (f32[160,128]{1,0:T(8,128)S(1)}, f32[160,128]{1,0:T(8,128)}, u32[]{:S(2)}) copy-start(f32[160,128]{1,0:T(8,128)} %constant.79.clone.refs_6_) | copy-start | bytes 245764
  91.7 5.6 %copy-start.7 = (f32[160,128]{1,0:T(8,128)S(1)}, f32[160,128]{1,0:T(8,128)}, u32[]{:S(2)}) copy-start(f32[160,128]{1,0:T(8,128)} %constant.80.clone.refs_7_) | copy-start | bytes 245764
  91.8 5.5 %copy-start.11 = (s32[2]{0:T(128)S(1)}, s32[2]{0:T(128)}, u32[]{:S(2)}) copy-start(s32[2]{0:T(128)} %lengths.3) | copy-start | bytes 28
  91.8 5.5 %copy-start.12 = (s32[8]{0:T(128)S(1)}, s32[8]{0:T(128)}, u32[]{:S(2)}) copy-start(s32[8]{0:T(128)} %owner.3) | copy-start | bytes 100
  94.2 3.1 %collective-permute-start.16 = (f32[320,1024]{1,0:T(8,128)S(1)}, f32[320,1024]{1,0:T(8,128)S(1)}, u32[]{:S(2)}, u32[]{:S(2)}) collective-permute-start(f32[320,1024]{1,0:T(8,128)S(1)} %get-tuple-element.43), channel_id=1, source_target_pairs={{0,1},{1,0},{2,3},{3,2},{4,5},{5,4},{6,7},{7,6},{8,9},{9,8},{10,11... | collective-permute-start | bytes 3932168 | tf_op jit(solution)/shard_map/ppermute | solution.py:66
  99.2 22.6 %copy-start.8 = (bf16[8,4,1024]{2,1,0:T(4,128)(2,1)S(1)}, bf16[8,4,1024]{2,1,0:T(4,128)(2,1)}, u32[]{:S(2)}) copy-start(bf16[8,4,1024]{2,1,0:T(4,128)(2,1)} %dec_query.1) | copy-start | bytes 196612
  99.2 22.6 %copy-start.9 = (bf16[8,4,128]{2,1,0:T(4,128)(2,1)S(1)}, bf16[8,4,128]{2,1,0:T(4,128)(2,1)}, u32[]{:S(2)}) copy-start(bf16[8,4,128]{2,1,0:T(4,128)(2,1)} %dec_key.1) | copy-start | bytes 24580
  99.2 22.6 %copy-start.10 = (bf16[8,4,128]{2,1,0:T(4,128)(2,1)S(1)}, bf16[8,4,128]{2,1,0:T(4,128)(2,1)}, u32[]{:S(2)}) copy-start(bf16[8,4,128]{2,1,0:T(4,128)(2,1)} %dec_value.1) | copy-start | bytes 24580
  99.2 22.6 %all-to-all-start = ((bf16[16,80,256]{2,1,0:T(8,128)(2,1)}), bf16[16,80,256]{2,1,0:T(8,128)(2,1)S(1)}, u32[]{:S(2)}, u32[]{:S(2)}) async-start(bf16[16,80,256]{2,1,0:T(8,128)(2,1)} %cache_rows.1), calls=%async_computation | async-start | bytes 1310720 | tf_op jit(solution)/shard_map/all_to_all | solution.py:478
  122.9 1.5 %collective-permute-start.17 = (f32[32,256]{1,0:T(8,128)S(1)}, f32[32,256]{1,0:T(8,128)S(1)}, u32[]{:S(2)}, u32[]{:S(2)}) collective-permute-start(f32[32,256]{1,0:T(8,128)S(1)} %decode.1), channel_id=1, source_target_pairs={{0,1},{1,0},{2,3},{3,2},{4,5},{5,4},{6,7},{7,6},{8,9},{9,8},{10,11... | collective-permute-start | bytes 98312 | tf_op jit(solution)/shard_map/ppermute | solution.py:66

commit v24 on v21

--- a/solution.py
+++ b/solution.py
@@ -457,9 +457,9 @@
         rest = half_block(depth - group_id * depth)
         layers, rows = (near, middle), (near, middle, across, raw, rest)
         passed = moved(after(middle, *layers), to_end)
-        middle_c = moved(after(near, *layers), to_middle)
-        near_y = moved(after(near, *rows), to_row)
-        across_x = moved(after(across, *rows), to_group)
+        middle_c = moved(near, to_middle)
+        near_y = moved(after(near, across), to_row)
+        across_x = moved(across, to_group)
         mine, other = prepared(place, after(flat, *rows), raw, seq // 2)
         layers, rows = (passed, middle_c, mine), (near_y, across_x, mine, passed)
         far = moved(after(middle_c, *layers), to_end)

time: 112 us -> 111 us (level)
  waiting for transfers between devices: 37.5 us -> 39 us
  blocking collectives: 22.8 us -> 21.5 us
    ppermute x19, waiting for transfers between devices: 37.5 us -> 39 us  [moved(): return lax.ppermute(block, ('groups', 'seq'), route)]
    all_to_all x1, blocking collectives: 22.8 us -> 21.5 us  [body(): lax.all_to_all(outgoing, 'seq', split_axis=0, concat_axis=1, tiled=True)]
  transfers between devices with their start and end apart: 19 -> 19, of which waited for: 11 -> 13; matrix products, arithmetic and copies ran while one was open for 3% -> 3% of each run, Pallas kernels for 15% -> 15%
where the time goes in v24:
time: 111 us
  waiting for transfers between devices  39 us (35%)
  Pallas kernels  23 us (21%)
  starting transfers between devices  21.6 us (19%)
  blocking collectives  21.5 us (19%)
  local copies, waits for them, and re-layouts  3.74 us (3%)
  other arithmetic  1.44 us (1%)
    ppermute x19, waiting for transfers between devices, moved(): return lax.ppermute(block, ('groups', 'seq'), route)  39 us
    ppermute x19, starting transfers between devices, moved(): return lax.ppermute(block, ('groups', 'seq'), route)  21.6 us
    all_to_all x1, blocking collectives, body(): lax.all_to_all(outgoing, 'seq', split_axis=0, concat_axis=1, tiled=True)  21.5 us
    pallas_call x3, Pallas kernels, product(): pl.pallas_call(functools.partial(product_kernel, plan, group, bool(totals...  10.2 us
    pallas_call x1, Pallas kernels, prepared(): pl.pallas_call(prepare_kernel, grid_spec=pltpu.PrefetchScalarGridSpec(num...  8.5 us
  transfers between devices with their start and end apart: 19, of which 13 were waited for; matrix products, arithmetic and copies ran while one was open for 3% of the time, Pallas kernels for 15%

profile of v24, /device:TPU:0, one launch (start us, length us, event | category | flops | bytes accessed | tf_op | source)
XLA Modules:
  0.0 111.1 jit_solution(184451701036531252)
XLA Ops:
  0.6 0.5 collective-permute-start.3
  1.1 1.3 %constant_dynamic-slice_fusion = (bf16[256,512]{1,0:T(8,128)(2,1)S(1)}, bf16[256,512]{1,0:T(8,128)(2,1)S(1)}, bf16[256,512]{1,0:T(8,128)(2,1)S(1)}, bf16[256,512]{1,0:T(8,128)(2,1)S(1)}) fusion(bf16[512,512]{1,0:T(8,128)(2,1)} %param.16, s32[]{:T(128)S(6)} %select_n.52, s32[]{:T(128)S(6)} %select_n.51, bf16[512,512]{1,0:T(8,128)(2,1)} %param.15), kind=kLoop, calls=%fused_computation.4 | loop fusion | bytes 2097160 | tf_op jit(solution)/shard_map/dynamic_slice | solution.py:446
  2.4 0.1 pad_maximum_fusion.refs_0_
  2.5 2.7 %collective-permute-start = (bf16[256,1024]{1,0:T(8,128)(2,1)S(1)}, bf16[256,1024]{1,0:T(8,128)(2,1)S(1)}, u32[]{:S(2)}, u32[]{:S(2)}) collective-permute-start(bf16[256,1024]{1,0:T(8,128)(2,1)S(1)} %pad_maximum_fusion.refs_0_), channel_id=1, source_target_pairs={{0,4},{1,5},{2,6},{3,7},{4,0},{5,1},{6,2},{7,3},{8,12},{9,13},{10,... | collective-permute-start | bytes 1572872 | tf_op jit(solution)/shard_map/ppermute | solution.py:66
  5.1 1.5 %collective-permute-start.2 = (bf16[256,1024]{1,0:T(8,128)(2,1)S(1)}, bf16[256,1024]{1,0:T(8,128)(2,1)S(1)}, u32[]{:S(2)}, u32[]{:S(2)}) collective-permute-start(bf16[256,1024]{1,0:T(8,128)(2,1)S(1)} %pad_maximum_fusion.refs_0_), channel_id=1, source_target_pairs={{0,2},{1,3},{2,0},{3,1},{4,6},{5,7},{6,4},{7,5},{8,10},{9,11},{10,... | collective-permute-start | bytes 1572872 | tf_op jit(solution)/shard_map/ppermute | solution.py:66
  6.7 1.4 %collective-permute-start.1 = (bf16[256,1024]{1,0:T(8,128)(2,1)S(1)}, bf16[256,1024]{1,0:T(8,128)(2,1)}, u32[]{:S(2)}, u32[]{:S(2)}) collective-permute-start(bf16[256,1024]{1,0:T(8,128)(2,1)S(1)} %pad_maximum_fusion.refs_0_), channel_id=1, source_target_pairs={{4,8},{5,9},{6,10},{7,11},{8,4},{9,5},{10,6},{11,7},{20,24},{21,25... | collective-permute-start | bytes 1572872 | tf_op jit(solution)/shard_map/ppermute | solution.py:66
  8.1 9.6 %collective-permute-done.refs_4_ = bf16[256,1024]{1,0:T(8,128)(2,1)S(1)} collective-permute-done((bf16[256,1024]{1,0:T(8,128)(2,1)S(1)}, bf16[256,1024]{1,0:T(8,128)(2,1)S(1)}, u32[]{:S(2)}, u32[]{:S(2)}) %collective-permute-start) | collective-permute-done | bytes 524320 | tf_op jit(solution)/shard_map/ppermute | solution.py:66
  17.7 1.5 %collective-permute-done.2.refs_2_ = bf16[256,1024]{1,0:T(8,128)(2,1)S(1)} collective-permute-done((bf16[256,1024]{1,0:T(8,128)(2,1)S(1)}, bf16[256,1024]{1,0:T(8,128)(2,1)S(1)}, u32[]{:S(2)}, u32[]{:S(2)}) %collective-permute-start.2) | collective-permute-done | bytes 524320 | tf_op jit(solution)/shard_map/ppermute | solution.py:66
  19.2 1.5 %collective-permute-start.8 = (bf16[256,1024]{1,0:T(8,128)(2,1)S(1)}, bf16[256,1024]{1,0:T(8,128)(2,1)S(1)}, u32[]{:S(2)}, u32[]{:S(2)}) collective-permute-start(bf16[256,1024]{1,0:T(8,128)(2,1)S(1)} %collective-permute-done.refs_4_), channel_id=1, source_target_pairs={{0,2},{1,3},{2,0},{3,1},{4,6},{5,7},{6,4},{7,5},{8,10},{9,11},{10,... | collective-permute-start | bytes 1572872 | tf_op jit(solution)/shard_map/ppermute | solution.py:66
  20.7 0.0 collective-permute-done.1
  20.7 1.3 %collective-permute-start.6 = (bf16[256,1024]{1,0:T(8,128)(2,1)}, bf16[256,1024]{1,0:T(8,128)(2,1)}, u32[]{:S(2)}, u32[]{:S(2)}) collective-permute-start(bf16[256,1024]{1,0:T(8,128)(2,1)} %collective-permute-done.1), channel_id=1, source_target_pairs={{4,0},{5,1},{6,2},{7,3},{8,12},{9,13},{10,14},{11,15},{20,16},{21,... | collective-permute-start | bytes 1572872 | tf_op jit(solution)/shard_map/ppermute | solution.py:66
  22.0 1.6 %collective-permute-start.4 = (bf16[256,1024]{1,0:T(8,128)(2,1)S(1)}, bf16[256,1024]{1,0:T(8,128)(2,1)S(1)}, u32[]{:S(2)}, u32[]{:S(2)}) collective-permute-start(bf16[256,1024]{1,0:T(8,128)(2,1)S(1)} %collective-permute-done.2.refs_2_), channel_id=1, source_target_pairs={{0,16},{1,17},{2,18},{3,19},{4,20},{5,21},{6,22},{7,23},{8,24},{9,... | collective-permute-start | bytes 1572872 | tf_op jit(solution)/shard_map/ppermute | solution.py:66
  23.5 1.5 %collective-permute-start.5 = (bf16[256,1024]{1,0:T(8,128)(2,1)S(1)}, bf16[256,1024]{1,0:T(8,128)(2,1)}, u32[]{:S(2)}, u32[]{:S(2)}) collective-permute-start(bf16[256,1024]{1,0:T(8,128)(2,1)S(1)} %collective-permute-done.refs_4_), channel_id=1, source_target_pairs={{4,8},{5,9},{6,10},{7,11},{8,4},{9,5},{10,6},{11,7},{20,24},{21,25... | collective-permute-start | bytes 1572872 | tf_op jit(solution)/shard_map/ppermute | solution.py:66
  25.0 0.7 stack.47.place
  25.7 0.1 pad_maximum_fusion.1.refs_1_
  25.7 0.0 collective-permute-done.3.refs_1_
  25.8 8.5 %normed_halves.1 = (bf16[16,320,256]{2,1,0:T(8,128)(2,1)}, bf16[16,320,256]{2,1,0:T(8,128)(2,1)}) custom-call(s32[11]{0:T(128)} %stack.47.place, bf16[320,8192]{1,0:T(8,128)(2,1)} %bitcast.17, bf16[320,8192]{1,0:T(8,128)(2,1)} %collective-permute-done.3.refs_1_), custom_call_target="tpu_custom_call" | custom-call | flops 1000 | bytes 1000 | tf_op jit(solution)/shard_map/normed_halves/pallas_call | solution.py:137
  34.3 0.0 collective-permute-done.8.refs_5_
  34.3 2.6 %collective-permute-done.6 = bf16[256,1024]{1,0:T(8,128)(2,1)} collective-permute-done((bf16[256,1024]{1,0:T(8,128)(2,1)}, bf16[256,1024]{1,0:T(8,128)(2,1)}, u32[]{:S(2)}, u32[]{:S(2)}) %collective-permute-start.6) | collective-permute-done | bytes 524320 | tf_op jit(solution)/shard_map/ppermute | solution.py:66
  36.9 0.0 collective-permute-done.4.refs_3_
  36.9 1.3 %broadcast_select_fusion.1.refs_0_ = bf16[256,1024]{1,0:T(8,128)(2,1)S(1)} fusion(bf16[256,1024]{1,0:T(8,128)(2,1)} %collective-permute-done.6, bf16[256,1024]{1,0:T(8,128)(2,1)} %collective-permute-done.1, pred[]{:T(512)S(6)} %or.3), kind=kLoop, calls=%fused_computation.3 | loop fusion | flops 262144 | bytes 1572865 | tf_op jit(solution)/shard_map/jit(_where)/select_n | solution.py:466
  38.1 0.6 collective-permute-start.10
  38.7 1.5 %collective-permute-start.11 = (bf16[256,1024]{1,0:T(8,128)(2,1)S(1)}, bf16[256,1024]{1,0:T(8,128)(2,1)S(1)}, u32[]{:S(2)}, u32[]{:S(2)}) collective-permute-start(bf16[256,1024]{1,0:T(8,128)(2,1)S(1)} %broadcast_select_fusion.1.refs_0_), channel_id=1, source_target_pairs={{0,16},{1,17},{2,18},{3,19},{4,20},{5,21},{6,22},{7,23},{8,24},{9,... | collective-permute-start | bytes 1572872 | tf_op jit(solution)/shard_map/ppermute | solution.py:66
  40.2 0.0 collective-permute-done.5
  40.2 1.3 %collective-permute-start.7 = (bf16[256,1024]{1,0:T(8,128)(2,1)}, bf16[256,1024]{1,0:T(8,128)(2,1)S(1)}, u32[]{:S(2)}, u32[]{:S(2)}) collective-permute-start(bf16[256,1024]{1,0:T(8,128)(2,1)} %collective-permute-done.5), channel_id=1, source_target_pairs={{4,0},{5,1},{6,2},{7,3},{8,12},{9,13},{10,14},{11,15},{20,16},{21,... | collective-permute-start | bytes 1572872 | tf_op jit(solution)/shard_map/ppermute | solution.py:66
  41.5 9.3 %collective-permute-done.10.refs_2_ = bf16[256,1024]{1,0:T(8,128)(2,1)S(1)} collective-permute-done((bf16[256,1024]{1,0:T(8,128)(2,1)S(1)}, bf16[256,1024]{1,0:T(8,128)(2,1)S(1)}, u32[]{:S(2)}, u32[]{:S(2)}) %collective-permute-start.10) | collective-permute-done | bytes 524320 | tf_op jit(solution)/shard_map/ppermute | solution.py:66
  50.8 0.2 collective-permute-done.11.refs_1_
  51.0 3.3 %collective-permute-done.7 = bf16[256,1024]{1,0:T(8,128)(2,1)S(1)} collective-permute-done((bf16[256,1024]{1,0:T(8,128)(2,1)}, bf16[256,1024]{1,0:T(8,128)(2,1)S(1)}, u32[]{:S(2)}, u32[]{:S(2)}) %collective-permute-start.7) | collective-permute-done | bytes 524320 | tf_op jit(solution)/shard_map/ppermute | solution.py:66
  54.3 0.1 broadcast_select_fusion.refs_3_
  54.4 1.5 %collective-permute-start.13 = (bf16[256,1024]{1,0:T(8,128)(2,1)S(1)}, bf16[256,1024]{1,0:T(8,128)(2,1)S(1)}, u32[]{:S(2)}, u32[]{:S(2)}) collective-permute-start(bf16[256,1024]{1,0:T(8,128)(2,1)S(1)} %broadcast_select_fusion.refs_3_), channel_id=1, source_target_pairs={{0,16},{1,17},{2,18},{3,19},{4,20},{5,21},{6,22},{7,23},{8,24},{9,... | collective-permute-start | bytes 1572872 | tf_op jit(solution)/shard_map/ppermute | solution.py:66
  55.9 1.5 %collective-permute-start.14 = (bf16[256,1024]{1,0:T(8,128)(2,1)S(1)}, bf16[256,1024]{1,0:T(8,128)(2,1)S(1)}, u32[]{:S(2)}, u32[]{:S(2)}) collective-permute-start(bf16[256,1024]{1,0:T(8,128)(2,1)S(1)} %broadcast_select_fusion.refs_3_), channel_id=1, source_target_pairs={{0,2},{1,3},{2,0},{3,1},{4,6},{5,7},{6,4},{7,5},{8,10},{9,11},{10,... | collective-permute-start | bytes 1572872 | tf_op jit(solution)/shard_map/ppermute | solution.py:66
  57.4 0.7 collective-permute-start.9
  58.1 0.0 copy-done
  58.1 0.0 copy-done.10
  58.1 1.7 %copy-done.1 = bf16[16,320,256]{2,1,0:T(8,128)(2,1)S(1)} copy-done((bf16[16,320,256]{2,1,0:T(8,128)(2,1)S(1)}, bf16[16,320,256]{2,1,0:T(8,128)(2,1)}, u32[]{:S(2)}) %copy-start.1) | copy-done | bytes 2621464
  59.9 3.5 %add_product.3 = (f32[320,1024]{1,0:T(8,128)S(1)}, f32[320,1024]{1,0:T(8,128)S(1)}) custom-call(s32[11]{0:T(128)S(1)} %copy-done.10, bf16[16,320,256]{2,1,0:T(8,128)(2,1)S(1)} %copy-done, bf16[16,320,256]{2,1,0:T(8,128)(2,1)S(1)} %copy-done.1, bf16[256,1024]{1,0:T(8,128)(2,1)S(1)} %pad_maximum_fusion.refs_0_, ...), custom_call_target="tpu_custom_call" | custom-call | flops 1000 | bytes 1000 | tf_op jit(solution)/shard_map/add_product/pallas_call | solution.py:204
  63.4 2.2 %collective-permute-done.13.refs_5_ = bf16[256,1024]{1,0:T(8,128)(2,1)S(1)} collective-permute-done((bf16[256,1024]{1,0:T(8,128)(2,1)S(1)}, bf16[256,1024]{1,0:T(8,128)(2,1)S(1)}, u32[]{:S(2)}, u32[]{:S(2)}) %collective-permute-start.13) | collective-permute-done | bytes 524320 | tf_op jit(solution)/shard_map/ppermute | solution.py:66
  65.6 1.5 %collective-permute-done.14.refs_6_ = bf16[256,1024]{1,0:T(8,128)(2,1)S(1)} collective-permute-done((bf16[256,1024]{1,0:T(8,128)(2,1)S(1)}, bf16[256,1024]{1,0:T(8,128)(2,1)S(1)}, u32[]{:S(2)}, u32[]{:S(2)}) %collective-permute-start.14) | collective-permute-done | bytes 524320 | tf_op jit(solution)/shard_map/ppermute | solution.py:66
  67.0 1.9 %collective-permute-done.9.refs_4_ = bf16[256,1024]{1,0:T(8,128)(2,1)S(1)} collective-permute-done((bf16[256,1024]{1,0:T(8,128)(2,1)S(1)}, bf16[256,1024]{1,0:T(8,128)(2,1)S(1)}, u32[]{:S(2)}, u32[]{:S(2)}) %collective-permute-start.9) | collective-permute-done | bytes 524320 | tf_op jit(solution)/shard_map/ppermute | solution.py:66
  68.9 0.6 collective-permute-start.16
  69.5 0.5 collective-permute-start.15
  70.0 1.0 collective-permute-start.12
  71.0 0.0 copy-done.2
  71.0 4.3 %add_product.4 = (f32[320,1024]{1,0:T(8,128)S(1)}, f32[320,1024]{1,0:T(8,128)S(1)}) custom-call(s32[11]{0:T(128)S(1)} %copy-done.10, bf16[16,320,256]{2,1,0:T(8,128)(2,1)S(1)} %copy-done, bf16[16,320,256]{2,1,0:T(8,128)(2,1)S(1)} %copy-done.2, bf16[256,1024]{1,0:T(8,128)(2,1)S(1)} %broadcast_select_fusion.1.refs_0_, ...), custom_call_target="tpu_custom_call" | custom-call | flops 1000 | bytes 1000 | tf_op jit(solution)/shard_map/add_product/pallas_call | solution.py:204
  75.4 2.7 %collective-permute-done.16.refs_2_ = bf16[256,1024]{1,0:T(8,128)(2,1)S(1)} collective-permute-done((bf16[256,1024]{1,0:T(8,128)(2,1)S(1)}, bf16[256,1024]{1,0:T(8,128)(2,1)S(1)}, u32[]{:S(2)}, u32[]{:S(2)}) %collective-permute-start.16) | collective-permute-done | bytes 524320 | tf_op jit(solution)/shard_map/ppermute | solution.py:66
  78.1 0.6 collective-permute-done.15.refs_1_
  78.7 0.6 collective-permute-done.12.refs_0_
  79.3 0.0 copy-start.7
  79.3 0.0 copy-start.8
  79.3 0.0 copy-start.13
  79.3 0.0 copy-start.14
  79.3 2.4 %add_product.5 = (f32[320,1024]{1,0:T(8,128)S(1)}, f32[320,1024]{1,0:T(8,128)S(1)}) custom-call(s32[11]{0:T(128)S(1)} %copy-done.10, bf16[16,320,256]{2,1,0:T(8,128)(2,1)S(1)} %copy-done, bf16[16,320,256]{2,1,0:T(8,128)(2,1)S(1)} %copy-done.2, bf16[256,1024]{1,0:T(8,128)(2,1)S(1)} %collective-permute-done.12.refs_0_, ...), custom_call_target="tpu_custom_call" | custom-call | flops 1000 | bytes 1000 | tf_op jit(solution)/shard_map/add_product/pallas_call | solution.py:204
  81.7 0.1 collective-permute-start.17
  81.8 3.0 %collective-permute-done.17.refs_1_ = f32[320,1024]{1,0:T(8,128)S(1)} collective-permute-done((f32[320,1024]{1,0:T(8,128)S(1)}, f32[320,1024]{1,0:T(8,128)S(1)}, u32[]{:S(2)}, u32[]{:S(2)}) %collective-permute-start.17) | collective-permute-done | bytes 1310752 | tf_op jit(solution)/shard_map/ppermute | solution.py:66
  84.9 1.0 cache_rows.1
  85.9 0.0 copy-start.9
  85.9 0.0 copy-start.11
  85.9 0.0 copy-start.12
  85.9 21.5 %all_to_all.4 = bf16[16,80,256]{2,1,0:T(8,128)(2,1)S(1)} all-to-all(bf16[16,80,256]{2,1,0:T(8,128)(2,1)S(1)} %cache_rows.1), channel_id=1, replica_groups=mesh['groups'=2,'seq'=16] {'seq'}, dimensions={0} | all-to-all | bytes 1310720 | tf_op jit(solution)/shard_map/all_to_all | solution.py:488
  107.4 1.1 decode.1.mine
  108.5 0.4 collective-permute-start.18
  108.9 0.8 copied.1
  109.8 0.0 collective-permute-done.18.theirs
  109.8 1.3 %joined.1 = bf16[4,512]{1,0:T(4,128)(2,1)} custom-call(s32[11]{0:T(128)S(1)} %copy-done.10, f32[32,256]{1,0:T(8,128)S(1)} %decode.1.mine, f32[32,256]{1,0:T(8,128)S(1)} %collective-permute-done.18.theirs), custom_call_target="tpu_custom_call" | custom-call | flops 1000 | bytes 1000 | tf_op jit(solution)/shard_map/joined/pallas_call | solution.py:379
  (19 shorter events, 0.0 us)
Async XLA Ops:
  0.6 25.1 %collective-permute-start.3 = (bf16[320,8192]{1,0:T(8,128)(2,1)}, bf16[320,8192]{1,0:T(8,128)(2,1)}, u32[]{:S(2)}, u32[]{:S(2)}) collective-permute-start(bf16[320,8192]{1,0:T(8,128)(2,1)} %bitcast.16), channel_id=1, source_target_pairs={{0,1},{1,0},{2,3},{3,2},{4,5},{5,4},{6,7},{7,6},{8,9},{9,8},{10,11... | collective-permute-start | bytes 15728648 | tf_op jit(solution)/shard_map/ppermute | solution.py:66
  2.5 15.2 %collective-permute-start = (bf16[256,1024]{1,0:T(8,128)(2,1)S(1)}, bf16[256,1024]{1,0:T(8,128)(2,1)S(1)}, u32[]{:S(2)}, u32[]{:S(2)}) collective-permute-start(bf16[256,1024]{1,0:T(8,128)(2,1)S(1)} %pad_maximum_fusion.refs_0_), channel_id=1, source_target_pairs={{0,4},{1,5},{2,6},{3,7},{4,0},{5,1},{6,2},{7,3},{8,12},{9,13},{10,... | collective-permute-start | bytes 1572872 | tf_op jit(solution)/shard_map/ppermute | solution.py:66
  5.1 14.0 %collective-permute-start.2 = (bf16[256,1024]{1,0:T(8,128)(2,1)S(1)}, bf16[256,1024]{1,0:T(8,128)(2,1)S(1)}, u32[]{:S(2)}, u32[]{:S(2)}) collective-permute-start(bf16[256,1024]{1,0:T(8,128)(2,1)S(1)} %pad_maximum_fusion.refs_0_), channel_id=1, source_target_pairs={{0,2},{1,3},{2,0},{3,1},{4,6},{5,7},{6,4},{7,5},{8,10},{9,11},{10,... | collective-permute-start | bytes 1572872 | tf_op jit(solution)/shard_map/ppermute | solution.py:66
  6.7 14.0 %collective-permute-start.1 = (bf16[256,1024]{1,0:T(8,128)(2,1)S(1)}, bf16[256,1024]{1,0:T(8,128)(2,1)}, u32[]{:S(2)}, u32[]{:S(2)}) collective-permute-start(bf16[256,1024]{1,0:T(8,128)(2,1)S(1)} %pad_maximum_fusion.refs_0_), channel_id=1, source_target_pairs={{4,8},{5,9},{6,10},{7,11},{8,4},{9,5},{10,6},{11,7},{20,24},{21,25... | collective-permute-start | bytes 1572872 | tf_op jit(solution)/shard_map/ppermute | solution.py:66
  19.2 15.1 %collective-permute-start.8 = (bf16[256,1024]{1,0:T(8,128)(2,1)S(1)}, bf16[256,1024]{1,0:T(8,128)(2,1)S(1)}, u32[]{:S(2)}, u32[]{:S(2)}) collective-permute-start(bf16[256,1024]{1,0:T(8,128)(2,1)S(1)} %collective-permute-done.refs_4_), channel_id=1, source_target_pairs={{0,2},{1,3},{2,0},{3,1},{4,6},{5,7},{6,4},{7,5},{8,10},{9,11},{10,... | collective-permute-start | bytes 1572872 | tf_op jit(solution)/shard_map/ppermute | solution.py:66
  20.7 16.2 %collective-permute-start.6 = (bf16[256,1024]{1,0:T(8,128)(2,1)}, bf16[256,1024]{1,0:T(8,128)(2,1)}, u32[]{:S(2)}, u32[]{:S(2)}) collective-permute-start(bf16[256,1024]{1,0:T(8,128)(2,1)} %collective-permute-done.1), channel_id=1, source_target_pairs={{4,0},{5,1},{6,2},{7,3},{8,12},{9,13},{10,14},{11,15},{20,16},{21,... | collective-permute-start | bytes 1572872 | tf_op jit(solution)/shard_map/ppermute | solution.py:66
  22.0 14.9 %collective-permute-start.4 = (bf16[256,1024]{1,0:T(8,128)(2,1)S(1)}, bf16[256,1024]{1,0:T(8,128)(2,1)S(1)}, u32[]{:S(2)}, u32[]{:S(2)}) collective-permute-start(bf16[256,1024]{1,0:T(8,128)(2,1)S(1)} %collective-permute-done.2.refs_2_), channel_id=1, source_target_pairs={{0,16},{1,17},{2,18},{3,19},{4,20},{5,21},{6,22},{7,23},{8,24},{9,... | collective-permute-start | bytes 1572872 | tf_op jit(solution)/shard_map/ppermute | solution.py:66
  23.5 16.7 %collective-permute-start.5 = (bf16[256,1024]{1,0:T(8,128)(2,1)S(1)}, bf16[256,1024]{1,0:T(8,128)(2,1)}, u32[]{:S(2)}, u32[]{:S(2)}) collective-permute-start(bf16[256,1024]{1,0:T(8,128)(2,1)S(1)} %collective-permute-done.refs_4_), channel_id=1, source_target_pairs={{4,8},{5,9},{6,10},{7,11},{8,4},{9,5},{10,6},{11,7},{20,24},{21,25... | collective-permute-start | bytes 1572872 | tf_op jit(solution)/shard_map/ppermute | solution.py:66
  36.9 21.3 %copy-start = (bf16[16,320,256]{2,1,0:T(8,128)(2,1)S(1)}, bf16[16,320,256]{2,1,0:T(8,128)(2,1)}, u32[]{:S(2)}) copy-start(bf16[16,320,256]{2,1,0:T(8,128)(2,1)} %get-tuple-element.41.mine) | copy-start | bytes 7864324
  36.9 21.3 %copy-start.10 = (s32[11]{0:T(128)S(1)}, s32[11]{0:T(128)}, u32[]{:S(2)}) copy-start(s32[11]{0:T(128)} %stack.47.place) | copy-start | bytes 136
  38.1 12.6 %collective-permute-start.10 = (bf16[256,1024]{1,0:T(8,128)(2,1)S(1)}, bf16[256,1024]{1,0:T(8,128)(2,1)S(1)}, u32[]{:S(2)}, u32[]{:S(2)}) collective-permute-start(bf16[256,1024]{1,0:T(8,128)(2,1)S(1)} %broadcast_select_fusion.1.refs_0_), channel_id=1, source_target_pairs={{0,2},{1,3},{2,0},{3,1},{4,6},{5,7},{6,4},{7,5},{8,10},{9,11},{10,... | collective-permute-start | bytes 1572872 | tf_op jit(solution)/shard_map/ppermute | solution.py:66
  38.7 12.3 %collective-permute-start.11 = (bf16[256,1024]{1,0:T(8,128)(2,1)S(1)}, bf16[256,1024]{1,0:T(8,128)(2,1)S(1)}, u32[]{:S(2)}, u32[]{:S(2)}) collective-permute-start(bf16[256,1024]{1,0:T(8,128)(2,1)S(1)} %broadcast_select_fusion.1.refs_0_), channel_id=1, source_target_pairs={{0,16},{1,17},{2,18},{3,19},{4,20},{5,21},{6,22},{7,23},{8,24},{9,... | collective-permute-start | bytes 1572872 | tf_op jit(solution)/shard_map/ppermute | solution.py:66
  40.2 14.1 %collective-permute-start.7 = (bf16[256,1024]{1,0:T(8,128)(2,1)}, bf16[256,1024]{1,0:T(8,128)(2,1)S(1)}, u32[]{:S(2)}, u32[]{:S(2)}) collective-permute-start(bf16[256,1024]{1,0:T(8,128)(2,1)} %collective-permute-done.5), channel_id=1, source_target_pairs={{4,0},{5,1},{6,2},{7,3},{8,12},{9,13},{10,14},{11,15},{20,16},{21,... | collective-permute-start | bytes 1572872 | tf_op jit(solution)/shard_map/ppermute | solution.py:66
  54.4 11.2 %collective-permute-start.13 = (bf16[256,1024]{1,0:T(8,128)(2,1)S(1)}, bf16[256,1024]{1,0:T(8,128)(2,1)S(1)}, u32[]{:S(2)}, u32[]{:S(2)}) collective-permute-start(bf16[256,1024]{1,0:T(8,128)(2,1)S(1)} %broadcast_select_fusion.refs_3_), channel_id=1, source_target_pairs={{0,16},{1,17},{2,18},{3,19},{4,20},{5,21},{6,22},{7,23},{8,24},{9,... | collective-permute-start | bytes 1572872 | tf_op jit(solution)/shard_map/ppermute | solution.py:66
  55.9 11.1 %collective-permute-start.14 = (bf16[256,1024]{1,0:T(8,128)(2,1)S(1)}, bf16[256,1024]{1,0:T(8,128)(2,1)S(1)}, u32[]{:S(2)}, u32[]{:S(2)}) collective-permute-start(bf16[256,1024]{1,0:T(8,128)(2,1)S(1)} %broadcast_select_fusion.refs_3_), channel_id=1, source_target_pairs={{0,2},{1,3},{2,0},{3,1},{4,6},{5,7},{6,4},{7,5},{8,10},{9,11},{10,... | collective-permute-start | bytes 1572872 | tf_op jit(solution)/shard_map/ppermute | solution.py:66
  57.4 11.5 %collective-permute-start.9 = (bf16[256,1024]{1,0:T(8,128)(2,1)S(1)}, bf16[256,1024]{1,0:T(8,128)(2,1)S(1)}, u32[]{:S(2)}, u32[]{:S(2)}) collective-permute-start(bf16[256,1024]{1,0:T(8,128)(2,1)S(1)} %pad_maximum_fusion.1.refs_1_), channel_id=1, source_target_pairs={{0,4},{1,5},{2,6},{3,7},{4,0},{5,1},{6,2},{7,3},{8,12},{9,13},{10,... | collective-permute-start | bytes 1572872 | tf_op jit(solution)/shard_map/ppermute | solution.py:66
  58.1 1.7 %copy-start.1 = (bf16[16,320,256]{2,1,0:T(8,128)(2,1)S(1)}, bf16[16,320,256]{2,1,0:T(8,128)(2,1)}, u32[]{:S(2)}) copy-start(bf16[16,320,256]{2,1,0:T(8,128)(2,1)} %get-tuple-element.32.other) | copy-start | bytes 7864324
  59.9 11.2 %copy-start.2 = (bf16[16,320,256]{2,1,0:T(8,128)(2,1)S(1)}, bf16[16,320,256]{2,1,0:T(8,128)(2,1)}, u32[]{:S(2)}) copy-start(bf16[16,320,256]{2,1,0:T(8,128)(2,1)} %get-tuple-element.32.other) | copy-start | bytes 7864324
  68.9 9.2 %collective-permute-start.16 = (bf16[256,1024]{1,0:T(8,128)(2,1)S(1)}, bf16[256,1024]{1,0:T(8,128)(2,1)S(1)}, u32[]{:S(2)}, u32[]{:S(2)}) collective-permute-start(bf16[256,1024]{1,0:T(8,128)(2,1)S(1)} %collective-permute-done.13.refs_5_), channel_id=1, source_target_pairs={{0,2},{1,3},{2,0},{3,1},{4,6},{5,7},{6,4},{7,5},{8,10},{9,11},{10,... | collective-permute-start | bytes 1572872 | tf_op jit(solution)/shard_map/ppermute | solution.py:66
  69.5 9.2 %collective-permute-start.15 = (bf16[256,1024]{1,0:T(8,128)(2,1)S(1)}, bf16[256,1024]{1,0:T(8,128)(2,1)S(1)}, u32[]{:S(2)}, u32[]{:S(2)}) collective-permute-start(bf16[256,1024]{1,0:T(8,128)(2,1)S(1)} %collective-permute-done.10.refs_2_), channel_id=1, source_target_pairs={{0,16},{1,17},{2,18},{3,19},{4,20},{5,21},{6,22},{7,23},{8,24},{9,... | collective-permute-start | bytes 1572872 | tf_op jit(solution)/shard_map/ppermute | solution.py:66
  70.0 9.3 %collective-permute-start.12 = (bf16[256,1024]{1,0:T(8,128)(2,1)S(1)}, bf16[256,1024]{1,0:T(8,128)(2,1)S(1)}, u32[]{:S(2)}, u32[]{:S(2)}) collective-permute-start(bf16[256,1024]{1,0:T(8,128)(2,1)S(1)} %collective-permute-done.4.refs_3_), channel_id=1, source_target_pairs={{0,4},{1,5},{2,6},{3,7},{4,0},{5,1},{6,2},{7,3},{8,12},{9,13},{10,... | collective-permute-start | bytes 1572872 | tf_op jit(solution)/shard_map/ppermute | solution.py:66
  79.2 5.5 %copy-start.3 = (f32[64,128]{1,0:T(8,128)S(1)}, f32[64,128]{1,0:T(8,128)}, u32[]{:S(2)}) copy-start(f32[64,128]{1,0:T(8,128)} %constant.70.clone.refs_4_.refs_2_) | copy-start | bytes 98308
  79.3 5.5 %copy-start.4 = (f32[64,128]{1,0:T(8,128)S(1)}, f32[64,128]{1,0:T(8,128)}, u32[]{:S(2)}) copy-start(f32[64,128]{1,0:T(8,128)} %constant.71.clone.refs_5_.refs_3_) | copy-start | bytes 98308
  79.3 5.5 %copy-start.5 = (f32[41,128]{1,0:T(8,128)S(1)}, f32[41,128]{1,0:T(8,128)}, u32[]{:S(2)}) copy-start(f32[41,128]{1,0:T(8,128)} %constant.68.clone.refs_2_.refs_0_) | copy-start | bytes 62980
  79.3 5.5 %copy-start.6 = (f32[41,128]{1,0:T(8,128)S(1)}, f32[41,128]{1,0:T(8,128)}, u32[]{:S(2)}) copy-start(f32[41,128]{1,0:T(8,128)} %constant.69.clone.refs_3_.refs_1_) | copy-start | bytes 62980
  79.3 5.6 %copy-start.7 = (f32[160,128]{1,0:T(8,128)S(1)}, f32[160,128]{1,0:T(8,128)}, u32[]{:S(2)}) copy-start(f32[160,128]{1,0:T(8,128)} %constant.72.clone.refs_6_) | copy-start | bytes 245764
  79.3 5.6 %copy-start.8 = (f32[160,128]{1,0:T(8,128)S(1)}, f32[160,128]{1,0:T(8,128)}, u32[]{:S(2)}) copy-start(f32[160,128]{1,0:T(8,128)} %constant.73.clone.refs_7_) | copy-start | bytes 245764
  79.3 5.5 %copy-start.13 = (s32[2]{0:T(128)S(1)}, s32[2]{0:T(128)}, u32[]{:S(2)}) copy-start(s32[2]{0:T(128)} %lengths.3) | copy-start | bytes 28
  79.3 5.5 %copy-start.14 = (s32[8]{0:T(128)S(1)}, s32[8]{0:T(128)}, u32[]{:S(2)}) copy-start(s32[8]{0:T(128)} %owner.3) | copy-start | bytes 100
  81.7 3.1 %collective-permute-start.17 = (f32[320,1024]{1,0:T(8,128)S(1)}, f32[320,1024]{1,0:T(8,128)S(1)}, u32[]{:S(2)}, u32[]{:S(2)}) collective-permute-start(f32[320,1024]{1,0:T(8,128)S(1)} %get-tuple-element.43), channel_id=1, source_target_pairs={{0,1},{1,0},{2,3},{3,2},{4,5},{5,4},{6,7},{7,6},{8,9},{9,8},{10,11... | collective-permute-start | bytes 3932168 | tf_op jit(solution)/shard_map/ppermute | solution.py:66
  85.9 21.5 %copy-start.9 = (bf16[8,4,1024]{2,1,0:T(4,128)(2,1)S(1)}, bf16[8,4,1024]{2,1,0:T(4,128)(2,1)}, u32[]{:S(2)}) copy-start(bf16[8,4,1024]{2,1,0:T(4,128)(2,1)} %dec_query.1) | copy-start | bytes 196612
  85.9 21.5 %copy-start.11 = (bf16[8,4,128]{2,1,0:T(4,128)(2,1)S(1)}, bf16[8,4,128]{2,1,0:T(4,128)(2,1)}, u32[]{:S(2)}) copy-start(bf16[8,4,128]{2,1,0:T(4,128)(2,1)} %dec_key.1) | copy-start | bytes 24580
  85.9 21.5 %copy-start.12 = (bf16[8,4,128]{2,1,0:T(4,128)(2,1)S(1)}, bf16[8,4,128]{2,1,0:T(4,128)(2,1)}, u32[]{:S(2)}) copy-start(bf16[8,4,128]{2,1,0:T(4,128)(2,1)} %dec_value.1) | copy-start | bytes 24580
  108.5 1.3 %collective-permute-start.18 = (f32[32,256]{1,0:T(8,128)S(1)}, f32[32,256]{1,0:T(8,128)S(1)}, u32[]{:S(2)}, u32[]{:S(2)}) collective-permute-start(f32[32,256]{1,0:T(8,128)S(1)} %decode.1.mine), channel_id=1, source_target_pairs={{0,1},{1,0},{2,3},{3,2},{4,5},{5,4},{6,7},{7,6},{8,9},{9,8},{10,11... | collective-permute-start | bytes 98312 | tf_op jit(solution)/shard_map/ppermute | solution.py:66

commit v25 on v21

--- a/solution.py
+++ b/solution.py
@@ -459,7 +459,7 @@
         passed = moved(after(middle, *layers), to_end)
         middle_c = moved(after(near, *layers), to_middle)
         near_y = moved(after(near, *rows), to_row)
-        across_x = moved(after(across, *rows), to_group)
+        across_x = moved(across, to_group)
         mine, other = prepared(place, after(flat, *rows), raw, seq // 2)
         layers, rows = (passed, middle_c, mine), (near_y, across_x, mine, passed)
         far = moved(after(middle_c, *layers), to_end)

time: 112 us -> 113 us (level)
  blocking collectives: 22.8 us -> 24.1 us
    all_to_all x1, blocking collectives: 22.8 us -> 24.1 us  [body(): lax.all_to_all(outgoing, 'seq', split_axis=0, concat_axis=1, tiled=True)]
  transfers between devices with their start and end apart: 19 -> 19, of which waited for: 11 -> 10; matrix products, arithmetic and copies ran while one was open for 3% -> 3% of each run, Pallas kernels for 15% -> 15%
where the time goes in v25:
time: 113 us
  waiting for transfers between devices  37.4 us (33%)
  blocking collectives  24.1 us (21%)
  Pallas kernels  23 us (20%)
  starting transfers between devices  22.2 us (20%)
  local copies, waits for them, and re-layouts  3.74 us (3%)
  other arithmetic  1.3 us (1%)
    ppermute x19, waiting for transfers between devices, moved(): return lax.ppermute(block, ('groups', 'seq'), route)  37.4 us
    all_to_all x1, blocking collectives, body(): lax.all_to_all(outgoing, 'seq', split_axis=0, concat_axis=1, tiled=True)  24.1 us
    ppermute x19, starting transfers between devices, moved(): return lax.ppermute(block, ('groups', 'seq'), route)  22.2 us
    pallas_call x3, Pallas kernels, product(): pl.pallas_call(functools.partial(product_kernel, plan, group, bool(totals...  10.2 us
    pallas_call x1, Pallas kernels, prepared(): pl.pallas_call(prepare_kernel, grid_spec=pltpu.PrefetchScalarGridSpec(num...  8.5 us
  transfers between devices with their start and end apart: 19, of which 10 were waited for; matrix products, arithmetic and copies ran while one was open for 3% of the time, Pallas kernels for 15%

profile of v25, /device:TPU:0, one launch (start us, length us, event | category | flops | bytes accessed | tf_op | source)
XLA Modules:
  0.0 112.6 jit_solution(17780315307570936236)
XLA Ops:
  0.6 0.5 collective-permute-start.3
  1.1 1.3 %constant_dynamic-slice_fusion = (bf16[256,512]{1,0:T(8,128)(2,1)S(1)}, bf16[256,512]{1,0:T(8,128)(2,1)S(1)}, bf16[256,512]{1,0:T(8,128)(2,1)S(1)}, bf16[256,512]{1,0:T(8,128)(2,1)S(1)}) fusion(bf16[512,512]{1,0:T(8,128)(2,1)} %param.16, s32[]{:T(128)S(6)} %select_n.52, s32[]{:T(128)S(6)} %select_n.51, bf16[512,512]{1,0:T(8,128)(2,1)} %param.15), kind=kLoop, calls=%fused_computation.4 | loop fusion | bytes 2097160 | tf_op jit(solution)/shard_map/dynamic_slice | solution.py:446
  2.4 0.1 pad_maximum_fusion.refs_0_
  2.5 2.7 %collective-permute-start = (bf16[256,1024]{1,0:T(8,128)(2,1)S(1)}, bf16[256,1024]{1,0:T(8,128)(2,1)S(1)}, u32[]{:S(2)}, u32[]{:S(2)}) collective-permute-start(bf16[256,1024]{1,0:T(8,128)(2,1)S(1)} %pad_maximum_fusion.refs_0_), channel_id=1, source_target_pairs={{0,4},{1,5},{2,6},{3,7},{4,0},{5,1},{6,2},{7,3},{8,12},{9,13},{10,... | collective-permute-start | bytes 1572872 | tf_op jit(solution)/shard_map/ppermute | solution.py:66
  5.1 1.4 %collective-permute-start.1 = (bf16[256,1024]{1,0:T(8,128)(2,1)S(1)}, bf16[256,1024]{1,0:T(8,128)(2,1)}, u32[]{:S(2)}, u32[]{:S(2)}) collective-permute-start(bf16[256,1024]{1,0:T(8,128)(2,1)S(1)} %pad_maximum_fusion.refs_0_), channel_id=1, source_target_pairs={{4,8},{5,9},{6,10},{7,11},{8,4},{9,5},{10,6},{11,7},{20,24},{21,25... | collective-permute-start | bytes 1572872 | tf_op jit(solution)/shard_map/ppermute | solution.py:66
  6.6 1.5 %collective-permute-start.2 = (bf16[256,1024]{1,0:T(8,128)(2,1)S(1)}, bf16[256,1024]{1,0:T(8,128)(2,1)S(1)}, u32[]{:S(2)}, u32[]{:S(2)}) collective-permute-start(bf16[256,1024]{1,0:T(8,128)(2,1)S(1)} %pad_maximum_fusion.refs_0_), channel_id=1, source_target_pairs={{0,2},{1,3},{2,0},{3,1},{4,6},{5,7},{6,4},{7,5},{8,10},{9,11},{10,... | collective-permute-start | bytes 1572872 | tf_op jit(solution)/shard_map/ppermute | solution.py:66
  8.1 0.1 pad_maximum_fusion.1.refs_1_
  8.2 9.5 %collective-permute-done.refs_4_ = bf16[256,1024]{1,0:T(8,128)(2,1)S(1)} collective-permute-done((bf16[256,1024]{1,0:T(8,128)(2,1)S(1)}, bf16[256,1024]{1,0:T(8,128)(2,1)S(1)}, u32[]{:S(2)}, u32[]{:S(2)}) %collective-permute-start) | collective-permute-done | bytes 524320 | tf_op jit(solution)/shard_map/ppermute | solution.py:66
  17.7 0.0 collective-permute-done.1
  17.7 1.3 %collective-permute-start.6 = (bf16[256,1024]{1,0:T(8,128)(2,1)}, bf16[256,1024]{1,0:T(8,128)(2,1)}, u32[]{:S(2)}, u32[]{:S(2)}) collective-permute-start(bf16[256,1024]{1,0:T(8,128)(2,1)} %collective-permute-done.1), channel_id=1, source_target_pairs={{4,0},{5,1},{6,2},{7,3},{8,12},{9,13},{10,14},{11,15},{20,16},{21,... | collective-permute-start | bytes 1572872 | tf_op jit(solution)/shard_map/ppermute | solution.py:66
  19.0 1.5 %collective-permute-start.5 = (bf16[256,1024]{1,0:T(8,128)(2,1)S(1)}, bf16[256,1024]{1,0:T(8,128)(2,1)}, u32[]{:S(2)}, u32[]{:S(2)}) collective-permute-start(bf16[256,1024]{1,0:T(8,128)(2,1)S(1)} %collective-permute-done.refs_4_), channel_id=1, source_target_pairs={{4,8},{5,9},{6,10},{7,11},{8,4},{9,5},{10,6},{11,7},{20,24},{21,25... | collective-permute-start | bytes 1572872 | tf_op jit(solution)/shard_map/ppermute | solution.py:66
  20.5 0.1 collective-permute-done.2.refs_2_
  20.6 1.5 %collective-permute-start.4 = (bf16[256,1024]{1,0:T(8,128)(2,1)S(1)}, bf16[256,1024]{1,0:T(8,128)(2,1)S(1)}, u32[]{:S(2)}, u32[]{:S(2)}) collective-permute-start(bf16[256,1024]{1,0:T(8,128)(2,1)S(1)} %collective-permute-done.2.refs_2_), channel_id=1, source_target_pairs={{0,16},{1,17},{2,18},{3,19},{4,20},{5,21},{6,22},{7,23},{8,24},{9,... | collective-permute-start | bytes 1572872 | tf_op jit(solution)/shard_map/ppermute | solution.py:66
  22.1 0.0 collective-permute-done.3.refs_1_
  22.1 1.5 %collective-permute-start.8 = (bf16[256,1024]{1,0:T(8,128)(2,1)S(1)}, bf16[256,1024]{1,0:T(8,128)(2,1)S(1)}, u32[]{:S(2)}, u32[]{:S(2)}) collective-permute-start(bf16[256,1024]{1,0:T(8,128)(2,1)S(1)} %collective-permute-done.refs_4_), channel_id=1, source_target_pairs={{0,2},{1,3},{2,0},{3,1},{4,6},{5,7},{6,4},{7,5},{8,10},{9,11},{10,... | collective-permute-start | bytes 1572872 | tf_op jit(solution)/shard_map/ppermute | solution.py:66
  23.7 0.7 stack.47.place
  24.3 8.5 %normed_halves.1 = (bf16[16,320,256]{2,1,0:T(8,128)(2,1)}, bf16[16,320,256]{2,1,0:T(8,128)(2,1)}) custom-call(s32[11]{0:T(128)} %stack.47.place, bf16[320,8192]{1,0:T(8,128)(2,1)} %bitcast.17, bf16[320,8192]{1,0:T(8,128)(2,1)} %collective-permute-done.3.refs_1_), custom_call_target="tpu_custom_call" | custom-call | flops 1000 | bytes 1000 | tf_op jit(solution)/shard_map/normed_halves/pallas_call | solution.py:137
  32.8 3.1 %collective-permute-done.6 = bf16[256,1024]{1,0:T(8,128)(2,1)} collective-permute-done((bf16[256,1024]{1,0:T(8,128)(2,1)}, bf16[256,1024]{1,0:T(8,128)(2,1)}, u32[]{:S(2)}, u32[]{:S(2)}) %collective-permute-start.6) | collective-permute-done | bytes 524320 | tf_op jit(solution)/shard_map/ppermute | solution.py:66
  35.9 0.0 collective-permute-done.5
  35.9 1.6 %collective-permute-start.7 = (bf16[256,1024]{1,0:T(8,128)(2,1)}, bf16[256,1024]{1,0:T(8,128)(2,1)S(1)}, u32[]{:S(2)}, u32[]{:S(2)}) collective-permute-start(bf16[256,1024]{1,0:T(8,128)(2,1)} %collective-permute-done.5), channel_id=1, source_target_pairs={{4,0},{5,1},{6,2},{7,3},{8,12},{9,13},{10,14},{11,15},{20,16},{21,... | collective-permute-start | bytes 1572872 | tf_op jit(solution)/shard_map/ppermute | solution.py:66
  37.5 0.0 collective-permute-done.4.refs_3_
  37.5 0.0 collective-permute-done.8.refs_5_
  37.5 1.1 broadcast_select_fusion.1.refs_0_
  38.6 1.6 %collective-permute-start.10 = (bf16[256,1024]{1,0:T(8,128)(2,1)S(1)}, bf16[256,1024]{1,0:T(8,128)(2,1)S(1)}, u32[]{:S(2)}, u32[]{:S(2)}) collective-permute-start(bf16[256,1024]{1,0:T(8,128)(2,1)S(1)} %broadcast_select_fusion.1.refs_0_), channel_id=1, source_target_pairs={{0,2},{1,3},{2,0},{3,1},{4,6},{5,7},{6,4},{7,5},{8,10},{9,11},{10,... | collective-permute-start | bytes 1572872 | tf_op jit(solution)/shard_map/ppermute | solution.py:66
  40.2 1.5 %collective-permute-start.11 = (bf16[256,1024]{1,0:T(8,128)(2,1)S(1)}, bf16[256,1024]{1,0:T(8,128)(2,1)S(1)}, u32[]{:S(2)}, u32[]{:S(2)}) collective-permute-start(bf16[256,1024]{1,0:T(8,128)(2,1)S(1)} %broadcast_select_fusion.1.refs_0_), channel_id=1, source_target_pairs={{0,16},{1,17},{2,18},{3,19},{4,20},{5,21},{6,22},{7,23},{8,24},{9,... | collective-permute-start | bytes 1572872 | tf_op jit(solution)/shard_map/ppermute | solution.py:66
  41.7 11.1 %collective-permute-done.7 = bf16[256,1024]{1,0:T(8,128)(2,1)S(1)} collective-permute-done((bf16[256,1024]{1,0:T(8,128)(2,1)}, bf16[256,1024]{1,0:T(8,128)(2,1)S(1)}, u32[]{:S(2)}, u32[]{:S(2)}) %collective-permute-start.7) | collective-permute-done | bytes 524320 | tf_op jit(solution)/shard_map/ppermute | solution.py:66
  52.8 0.0 collective-permute-start.9
  52.8 0.0 collective-permute-done.10.refs_2_
  52.8 0.0 collective-permute-done.11.refs_1_
  52.9 0.1 broadcast_select_fusion.refs_3_
  53.0 1.6 %collective-permute-start.13 = (bf16[256,1024]{1,0:T(8,128)(2,1)S(1)}, bf16[256,1024]{1,0:T(8,128)(2,1)S(1)}, u32[]{:S(2)}, u32[]{:S(2)}) collective-permute-start(bf16[256,1024]{1,0:T(8,128)(2,1)S(1)} %broadcast_select_fusion.refs_3_), channel_id=1, source_target_pairs={{0,16},{1,17},{2,18},{3,19},{4,20},{5,21},{6,22},{7,23},{8,24},{9,... | collective-permute-start | bytes 1572872 | tf_op jit(solution)/shard_map/ppermute | solution.py:66
  54.5 1.4 %collective-permute-start.14 = (bf16[256,1024]{1,0:T(8,128)(2,1)S(1)}, bf16[256,1024]{1,0:T(8,128)(2,1)S(1)}, u32[]{:S(2)}, u32[]{:S(2)}) collective-permute-start(bf16[256,1024]{1,0:T(8,128)(2,1)S(1)} %broadcast_select_fusion.refs_3_), channel_id=1, source_target_pairs={{0,2},{1,3},{2,0},{3,1},{4,6},{5,7},{6,4},{7,5},{8,10},{9,11},{10,... | collective-permute-start | bytes 1572872 | tf_op jit(solution)/shard_map/ppermute | solution.py:66
  56.0 0.0 copy-done.10
  56.0 1.7 %copy-done.1 = bf16[16,320,256]{2,1,0:T(8,128)(2,1)S(1)} copy-done((bf16[16,320,256]{2,1,0:T(8,128)(2,1)S(1)}, bf16[16,320,256]{2,1,0:T(8,128)(2,1)}, u32[]{:S(2)}) %copy-start.1) | copy-done | bytes 2621464
  57.7 3.5 %add_product.3 = (f32[320,1024]{1,0:T(8,128)S(1)}, f32[320,1024]{1,0:T(8,128)S(1)}) custom-call(s32[11]{0:T(128)S(1)} %copy-done.10, bf16[16,320,256]{2,1,0:T(8,128)(2,1)S(1)} %copy-done, bf16[16,320,256]{2,1,0:T(8,128)(2,1)S(1)} %copy-done.1, bf16[256,1024]{1,0:T(8,128)(2,1)S(1)} %pad_maximum_fusion.refs_0_, ...), custom_call_target="tpu_custom_call" | custom-call | flops 1000 | bytes 1000 | tf_op jit(solution)/shard_map/add_product/pallas_call | solution.py:204
  61.2 3.7 %collective-permute-done.9.refs_4_ = bf16[256,1024]{1,0:T(8,128)(2,1)S(1)} collective-permute-done((bf16[256,1024]{1,0:T(8,128)(2,1)S(1)}, bf16[256,1024]{1,0:T(8,128)(2,1)S(1)}, u32[]{:S(2)}, u32[]{:S(2)}) %collective-permute-start.9) | collective-permute-done | bytes 524320 | tf_op jit(solution)/shard_map/ppermute | solution.py:66
  64.9 0.4 collective-permute-start.12
  65.3 0.0 collective-permute-done.13.refs_5_
  65.3 1.3 %collective-permute-done.14.refs_6_ = bf16[256,1024]{1,0:T(8,128)(2,1)S(1)} collective-permute-done((bf16[256,1024]{1,0:T(8,128)(2,1)S(1)}, bf16[256,1024]{1,0:T(8,128)(2,1)S(1)}, u32[]{:S(2)}, u32[]{:S(2)}) %collective-permute-start.14) | collective-permute-done | bytes 524320 | tf_op jit(solution)/shard_map/ppermute | solution.py:66
  66.6 1.4 %collective-permute-start.16 = (bf16[256,1024]{1,0:T(8,128)(2,1)S(1)}, bf16[256,1024]{1,0:T(8,128)(2,1)S(1)}, u32[]{:S(2)}, u32[]{:S(2)}) collective-permute-start(bf16[256,1024]{1,0:T(8,128)(2,1)S(1)} %collective-permute-done.13.refs_5_), channel_id=1, source_target_pairs={{0,2},{1,3},{2,0},{3,1},{4,6},{5,7},{6,4},{7,5},{8,10},{9,11},{10,... | collective-permute-start | bytes 1572872 | tf_op jit(solution)/shard_map/ppermute | solution.py:66
  68.0 0.4 collective-permute-start.15
  68.4 4.3 %add_product.4 = (f32[320,1024]{1,0:T(8,128)S(1)}, f32[320,1024]{1,0:T(8,128)S(1)}) custom-call(s32[11]{0:T(128)S(1)} %copy-done.10, bf16[16,320,256]{2,1,0:T(8,128)(2,1)S(1)} %copy-done, bf16[16,320,256]{2,1,0:T(8,128)(2,1)S(1)} %copy-done.2, bf16[256,1024]{1,0:T(8,128)(2,1)S(1)} %broadcast_select_fusion.1.refs_0_, ...), custom_call_target="tpu_custom_call" | custom-call | flops 1000 | bytes 1000 | tf_op jit(solution)/shard_map/add_product/pallas_call | solution.py:204
  72.8 3.1 %collective-permute-done.12.refs_0_ = bf16[256,1024]{1,0:T(8,128)(2,1)S(1)} collective-permute-done((bf16[256,1024]{1,0:T(8,128)(2,1)S(1)}, bf16[256,1024]{1,0:T(8,128)(2,1)S(1)}, u32[]{:S(2)}, u32[]{:S(2)}) %collective-permute-start.12) | collective-permute-done | bytes 524320 | tf_op jit(solution)/shard_map/ppermute | solution.py:66
  75.8 1.5 %collective-permute-done.16.refs_2_ = bf16[256,1024]{1,0:T(8,128)(2,1)S(1)} collective-permute-done((bf16[256,1024]{1,0:T(8,128)(2,1)S(1)}, bf16[256,1024]{1,0:T(8,128)(2,1)S(1)}, u32[]{:S(2)}, u32[]{:S(2)}) %collective-permute-start.16) | collective-permute-done | bytes 524320 | tf_op jit(solution)/shard_map/ppermute | solution.py:66
  77.4 0.8 collective-permute-done.15.refs_1_
  78.2 0.0 copy-start.7
  78.2 0.0 copy-start.8
  78.2 0.0 copy-start.13
  78.2 0.0 copy-start.14
  78.2 2.4 %add_product.5 = (f32[320,1024]{1,0:T(8,128)S(1)}, f32[320,1024]{1,0:T(8,128)S(1)}) custom-call(s32[11]{0:T(128)S(1)} %copy-done.10, bf16[16,320,256]{2,1,0:T(8,128)(2,1)S(1)} %copy-done, bf16[16,320,256]{2,1,0:T(8,128)(2,1)S(1)} %copy-done.2, bf16[256,1024]{1,0:T(8,128)(2,1)S(1)} %collective-permute-done.12.refs_0_, ...), custom_call_target="tpu_custom_call" | custom-call | flops 1000 | bytes 1000 | tf_op jit(solution)/shard_map/add_product/pallas_call | solution.py:204
  80.6 0.1 collective-permute-start.17
  80.7 3.0 %collective-permute-done.17.refs_1_ = f32[320,1024]{1,0:T(8,128)S(1)} collective-permute-done((f32[320,1024]{1,0:T(8,128)S(1)}, f32[320,1024]{1,0:T(8,128)S(1)}, u32[]{:S(2)}, u32[]{:S(2)}) %collective-permute-start.17) | collective-permute-done | bytes 1310752 | tf_op jit(solution)/shard_map/ppermute | solution.py:66
  83.7 0.0 copy-done.6
  83.7 0.0 copy-done.7
  83.8 1.0 cache_rows.1
  84.8 0.0 copy-start.9
  84.8 0.0 copy-start.11
  84.8 0.0 copy-start.12
  84.9 24.1 %all_to_all.4 = bf16[16,80,256]{2,1,0:T(8,128)(2,1)S(1)} all-to-all(bf16[16,80,256]{2,1,0:T(8,128)(2,1)S(1)} %cache_rows.1), channel_id=1, replica_groups=mesh['groups'=2,'seq'=16] {'seq'}, dimensions={0} | all-to-all | bytes 1310720 | tf_op jit(solution)/shard_map/all_to_all | solution.py:488
  109.0 1.1 decode.1.mine
  110.1 0.4 collective-permute-start.18
  110.5 0.8 copied.1
  111.3 0.0 collective-permute-done.18.theirs
  111.3 1.3 %joined.1 = bf16[4,512]{1,0:T(4,128)(2,1)} custom-call(s32[11]{0:T(128)S(1)} %copy-done.10, f32[32,256]{1,0:T(8,128)S(1)} %decode.1.mine, f32[32,256]{1,0:T(8,128)S(1)} %collective-permute-done.18.theirs), custom_call_target="tpu_custom_call" | custom-call | flops 1000 | bytes 1000 | tf_op jit(solution)/shard_map/joined/pallas_call | solution.py:379
  (19 shorter events, 0.0 us)
Async XLA Ops:
  0.6 21.5 %collective-permute-start.3 = (bf16[320,8192]{1,0:T(8,128)(2,1)}, bf16[320,8192]{1,0:T(8,128)(2,1)}, u32[]{:S(2)}, u32[]{:S(2)}) collective-permute-start(bf16[320,8192]{1,0:T(8,128)(2,1)} %bitcast.16), channel_id=1, source_target_pairs={{0,1},{1,0},{2,3},{3,2},{4,5},{5,4},{6,7},{7,6},{8,9},{9,8},{10,11... | collective-permute-start | bytes 15728648 | tf_op jit(solution)/shard_map/ppermute | solution.py:66
  2.5 15.2 %collective-permute-start = (bf16[256,1024]{1,0:T(8,128)(2,1)S(1)}, bf16[256,1024]{1,0:T(8,128)(2,1)S(1)}, u32[]{:S(2)}, u32[]{:S(2)}) collective-permute-start(bf16[256,1024]{1,0:T(8,128)(2,1)S(1)} %pad_maximum_fusion.refs_0_), channel_id=1, source_target_pairs={{0,4},{1,5},{2,6},{3,7},{4,0},{5,1},{6,2},{7,3},{8,12},{9,13},{10,... | collective-permute-start | bytes 1572872 | tf_op jit(solution)/shard_map/ppermute | solution.py:66
  5.1 12.6 %collective-permute-start.1 = (bf16[256,1024]{1,0:T(8,128)(2,1)S(1)}, bf16[256,1024]{1,0:T(8,128)(2,1)}, u32[]{:S(2)}, u32[]{:S(2)}) collective-permute-start(bf16[256,1024]{1,0:T(8,128)(2,1)S(1)} %pad_maximum_fusion.refs_0_), channel_id=1, source_target_pairs={{4,8},{5,9},{6,10},{7,11},{8,4},{9,5},{10,6},{11,7},{20,24},{21,25... | collective-permute-start | bytes 1572872 | tf_op jit(solution)/shard_map/ppermute | solution.py:66
  6.6 14.0 %collective-permute-start.2 = (bf16[256,1024]{1,0:T(8,128)(2,1)S(1)}, bf16[256,1024]{1,0:T(8,128)(2,1)S(1)}, u32[]{:S(2)}, u32[]{:S(2)}) collective-permute-start(bf16[256,1024]{1,0:T(8,128)(2,1)S(1)} %pad_maximum_fusion.refs_0_), channel_id=1, source_target_pairs={{0,2},{1,3},{2,0},{3,1},{4,6},{5,7},{6,4},{7,5},{8,10},{9,11},{10,... | collective-permute-start | bytes 1572872 | tf_op jit(solution)/shard_map/ppermute | solution.py:66
  17.7 18.2 %collective-permute-start.6 = (bf16[256,1024]{1,0:T(8,128)(2,1)}, bf16[256,1024]{1,0:T(8,128)(2,1)}, u32[]{:S(2)}, u32[]{:S(2)}) collective-permute-start(bf16[256,1024]{1,0:T(8,128)(2,1)} %collective-permute-done.1), channel_id=1, source_target_pairs={{4,0},{5,1},{6,2},{7,3},{8,12},{9,13},{10,14},{11,15},{20,16},{21,... | collective-permute-start | bytes 1572872 | tf_op jit(solution)/shard_map/ppermute | solution.py:66
  19.0 16.9 %collective-permute-start.5 = (bf16[256,1024]{1,0:T(8,128)(2,1)S(1)}, bf16[256,1024]{1,0:T(8,128)(2,1)}, u32[]{:S(2)}, u32[]{:S(2)}) collective-permute-start(bf16[256,1024]{1,0:T(8,128)(2,1)S(1)} %collective-permute-done.refs_4_), channel_id=1, source_target_pairs={{4,8},{5,9},{6,10},{7,11},{8,4},{9,5},{10,6},{11,7},{20,24},{21,25... | collective-permute-start | bytes 1572872 | tf_op jit(solution)/shard_map/ppermute | solution.py:66
  20.6 16.9 %collective-permute-start.4 = (bf16[256,1024]{1,0:T(8,128)(2,1)S(1)}, bf16[256,1024]{1,0:T(8,128)(2,1)S(1)}, u32[]{:S(2)}, u32[]{:S(2)}) collective-permute-start(bf16[256,1024]{1,0:T(8,128)(2,1)S(1)} %collective-permute-done.2.refs_2_), channel_id=1, source_target_pairs={{0,16},{1,17},{2,18},{3,19},{4,20},{5,21},{6,22},{7,23},{8,24},{9,... | collective-permute-start | bytes 1572872 | tf_op jit(solution)/shard_map/ppermute | solution.py:66
  22.1 15.4 %collective-permute-start.8 = (bf16[256,1024]{1,0:T(8,128)(2,1)S(1)}, bf16[256,1024]{1,0:T(8,128)(2,1)S(1)}, u32[]{:S(2)}, u32[]{:S(2)}) collective-permute-start(bf16[256,1024]{1,0:T(8,128)(2,1)S(1)} %collective-permute-done.refs_4_), channel_id=1, source_target_pairs={{0,2},{1,3},{2,0},{3,1},{4,6},{5,7},{6,4},{7,5},{8,10},{9,11},{10,... | collective-permute-start | bytes 1572872 | tf_op jit(solution)/shard_map/ppermute | solution.py:66
  35.9 20.0 %copy-start = (bf16[16,320,256]{2,1,0:T(8,128)(2,1)S(1)}, bf16[16,320,256]{2,1,0:T(8,128)(2,1)}, u32[]{:S(2)}) copy-start(bf16[16,320,256]{2,1,0:T(8,128)(2,1)} %get-tuple-element.43.mine) | copy-start | bytes 7864324
  35.9 20.0 %copy-start.10 = (s32[11]{0:T(128)S(1)}, s32[11]{0:T(128)}, u32[]{:S(2)}) copy-start(s32[11]{0:T(128)} %stack.47.place) | copy-start | bytes 136
  35.9 16.9 %collective-permute-start.7 = (bf16[256,1024]{1,0:T(8,128)(2,1)}, bf16[256,1024]{1,0:T(8,128)(2,1)S(1)}, u32[]{:S(2)}, u32[]{:S(2)}) collective-permute-start(bf16[256,1024]{1,0:T(8,128)(2,1)} %collective-permute-done.5), channel_id=1, source_target_pairs={{4,0},{5,1},{6,2},{7,3},{8,12},{9,13},{10,14},{11,15},{20,16},{21,... | collective-permute-start | bytes 1572872 | tf_op jit(solution)/shard_map/ppermute | solution.py:66
  38.6 14.2 %collective-permute-start.10 = (bf16[256,1024]{1,0:T(8,128)(2,1)S(1)}, bf16[256,1024]{1,0:T(8,128)(2,1)S(1)}, u32[]{:S(2)}, u32[]{:S(2)}) collective-permute-start(bf16[256,1024]{1,0:T(8,128)(2,1)S(1)} %broadcast_select_fusion.1.refs_0_), channel_id=1, source_target_pairs={{0,2},{1,3},{2,0},{3,1},{4,6},{5,7},{6,4},{7,5},{8,10},{9,11},{10,... | collective-permute-start | bytes 1572872 | tf_op jit(solution)/shard_map/ppermute | solution.py:66
  40.2 12.7 %collective-permute-start.11 = (bf16[256,1024]{1,0:T(8,128)(2,1)S(1)}, bf16[256,1024]{1,0:T(8,128)(2,1)S(1)}, u32[]{:S(2)}, u32[]{:S(2)}) collective-permute-start(bf16[256,1024]{1,0:T(8,128)(2,1)S(1)} %broadcast_select_fusion.1.refs_0_), channel_id=1, source_target_pairs={{0,16},{1,17},{2,18},{3,19},{4,20},{5,21},{6,22},{7,23},{8,24},{9,... | collective-permute-start | bytes 1572872 | tf_op jit(solution)/shard_map/ppermute | solution.py:66
  52.8 12.1 %collective-permute-start.9 = (bf16[256,1024]{1,0:T(8,128)(2,1)S(1)}, bf16[256,1024]{1,0:T(8,128)(2,1)S(1)}, u32[]{:S(2)}, u32[]{:S(2)}) collective-permute-start(bf16[256,1024]{1,0:T(8,128)(2,1)S(1)} %pad_maximum_fusion.1.refs_1_), channel_id=1, source_target_pairs={{0,4},{1,5},{2,6},{3,7},{4,0},{5,1},{6,2},{7,3},{8,12},{9,13},{10,... | collective-permute-start | bytes 1572872 | tf_op jit(solution)/shard_map/ppermute | solution.py:66
  53.0 12.4 %collective-permute-start.13 = (bf16[256,1024]{1,0:T(8,128)(2,1)S(1)}, bf16[256,1024]{1,0:T(8,128)(2,1)S(1)}, u32[]{:S(2)}, u32[]{:S(2)}) collective-permute-start(bf16[256,1024]{1,0:T(8,128)(2,1)S(1)} %broadcast_select_fusion.refs_3_), channel_id=1, source_target_pairs={{0,16},{1,17},{2,18},{3,19},{4,20},{5,21},{6,22},{7,23},{8,24},{9,... | collective-permute-start | bytes 1572872 | tf_op jit(solution)/shard_map/ppermute | solution.py:66
  54.5 12.1 %collective-permute-start.14 = (bf16[256,1024]{1,0:T(8,128)(2,1)S(1)}, bf16[256,1024]{1,0:T(8,128)(2,1)S(1)}, u32[]{:S(2)}, u32[]{:S(2)}) collective-permute-start(bf16[256,1024]{1,0:T(8,128)(2,1)S(1)} %broadcast_select_fusion.refs_3_), channel_id=1, source_target_pairs={{0,2},{1,3},{2,0},{3,1},{4,6},{5,7},{6,4},{7,5},{8,10},{9,11},{10,... | collective-permute-start | bytes 1572872 | tf_op jit(solution)/shard_map/ppermute | solution.py:66
  56.0 1.7 %copy-start.1 = (bf16[16,320,256]{2,1,0:T(8,128)(2,1)S(1)}, bf16[16,320,256]{2,1,0:T(8,128)(2,1)}, u32[]{:S(2)}) copy-start(bf16[16,320,256]{2,1,0:T(8,128)(2,1)} %get-tuple-element.34.other) | copy-start | bytes 7864324
  57.7 10.7 %copy-start.2 = (bf16[16,320,256]{2,1,0:T(8,128)(2,1)S(1)}, bf16[16,320,256]{2,1,0:T(8,128)(2,1)}, u32[]{:S(2)}) copy-start(bf16[16,320,256]{2,1,0:T(8,128)(2,1)} %get-tuple-element.34.other) | copy-start | bytes 7864324
  64.9 10.9 %collective-permute-start.12 = (bf16[256,1024]{1,0:T(8,128)(2,1)S(1)}, bf16[256,1024]{1,0:T(8,128)(2,1)S(1)}, u32[]{:S(2)}, u32[]{:S(2)}) collective-permute-start(bf16[256,1024]{1,0:T(8,128)(2,1)S(1)} %collective-permute-done.4.refs_3_), channel_id=1, source_target_pairs={{0,4},{1,5},{2,6},{3,7},{4,0},{5,1},{6,2},{7,3},{8,12},{9,13},{10,... | collective-permute-start | bytes 1572872 | tf_op jit(solution)/shard_map/ppermute | solution.py:66
  66.6 10.8 %collective-permute-start.16 = (bf16[256,1024]{1,0:T(8,128)(2,1)S(1)}, bf16[256,1024]{1,0:T(8,128)(2,1)S(1)}, u32[]{:S(2)}, u32[]{:S(2)}) collective-permute-start(bf16[256,1024]{1,0:T(8,128)(2,1)S(1)} %collective-permute-done.13.refs_5_), channel_id=1, source_target_pairs={{0,2},{1,3},{2,0},{3,1},{4,6},{5,7},{6,4},{7,5},{8,10},{9,11},{10,... | collective-permute-start | bytes 1572872 | tf_op jit(solution)/shard_map/ppermute | solution.py:66
  68.0 10.1 %collective-permute-start.15 = (bf16[256,1024]{1,0:T(8,128)(2,1)S(1)}, bf16[256,1024]{1,0:T(8,128)(2,1)S(1)}, u32[]{:S(2)}, u32[]{:S(2)}) collective-permute-start(bf16[256,1024]{1,0:T(8,128)(2,1)S(1)} %collective-permute-done.10.refs_2_), channel_id=1, source_target_pairs={{0,16},{1,17},{2,18},{3,19},{4,20},{5,21},{6,22},{7,23},{8,24},{9,... | collective-permute-start | bytes 1572872 | tf_op jit(solution)/shard_map/ppermute | solution.py:66
  78.2 5.5 %copy-start.3 = (f32[64,128]{1,0:T(8,128)S(1)}, f32[64,128]{1,0:T(8,128)}, u32[]{:S(2)}) copy-start(f32[64,128]{1,0:T(8,128)} %constant.70.clone.refs_4_.refs_2_) | copy-start | bytes 98308
  78.2 5.5 %copy-start.4 = (f32[64,128]{1,0:T(8,128)S(1)}, f32[64,128]{1,0:T(8,128)}, u32[]{:S(2)}) copy-start(f32[64,128]{1,0:T(8,128)} %constant.71.clone.refs_5_.refs_3_) | copy-start | bytes 98308
  78.2 5.5 %copy-start.5 = (f32[41,128]{1,0:T(8,128)S(1)}, f32[41,128]{1,0:T(8,128)}, u32[]{:S(2)}) copy-start(f32[41,128]{1,0:T(8,128)} %constant.68.clone.refs_2_.refs_0_) | copy-start | bytes 62980
  78.2 5.5 %copy-start.6 = (f32[41,128]{1,0:T(8,128)S(1)}, f32[41,128]{1,0:T(8,128)}, u32[]{:S(2)}) copy-start(f32[41,128]{1,0:T(8,128)} %constant.69.clone.refs_3_.refs_1_) | copy-start | bytes 62980
  78.2 5.6 %copy-start.7 = (f32[160,128]{1,0:T(8,128)S(1)}, f32[160,128]{1,0:T(8,128)}, u32[]{:S(2)}) copy-start(f32[160,128]{1,0:T(8,128)} %constant.72.clone.refs_6_) | copy-start | bytes 245764
  78.2 5.6 %copy-start.8 = (f32[160,128]{1,0:T(8,128)S(1)}, f32[160,128]{1,0:T(8,128)}, u32[]{:S(2)}) copy-start(f32[160,128]{1,0:T(8,128)} %constant.73.clone.refs_7_) | copy-start | bytes 245764
  78.2 5.5 %copy-start.13 = (s32[2]{0:T(128)S(1)}, s32[2]{0:T(128)}, u32[]{:S(2)}) copy-start(s32[2]{0:T(128)} %lengths.3) | copy-start | bytes 28
  78.2 5.5 %copy-start.14 = (s32[8]{0:T(128)S(1)}, s32[8]{0:T(128)}, u32[]{:S(2)}) copy-start(s32[8]{0:T(128)} %owner.3) | copy-start | bytes 100
  80.6 3.1 %collective-permute-start.17 = (f32[320,1024]{1,0:T(8,128)S(1)}, f32[320,1024]{1,0:T(8,128)S(1)}, u32[]{:S(2)}, u32[]{:S(2)}) collective-permute-start(f32[320,1024]{1,0:T(8,128)S(1)} %get-tuple-element.45), channel_id=1, source_target_pairs={{0,1},{1,0},{2,3},{3,2},{4,5},{5,4},{6,7},{7,6},{8,9},{9,8},{10,11... | collective-permute-start | bytes 3932168 | tf_op jit(solution)/shard_map/ppermute | solution.py:66
  84.8 24.1 %copy-start.9 = (bf16[8,4,1024]{2,1,0:T(4,128)(2,1)S(1)}, bf16[8,4,1024]{2,1,0:T(4,128)(2,1)}, u32[]{:S(2)}) copy-start(bf16[8,4,1024]{2,1,0:T(4,128)(2,1)} %dec_query.1) | copy-start | bytes 196612
  84.8 24.1 %copy-start.11 = (bf16[8,4,128]{2,1,0:T(4,128)(2,1)S(1)}, bf16[8,4,128]{2,1,0:T(4,128)(2,1)}, u32[]{:S(2)}) copy-start(bf16[8,4,128]{2,1,0:T(4,128)(2,1)} %dec_key.1) | copy-start | bytes 24580
  84.8 24.1 %copy-start.12 = (bf16[8,4,128]{2,1,0:T(4,128)(2,1)S(1)}, bf16[8,4,128]{2,1,0:T(4,128)(2,1)}, u32[]{:S(2)}) copy-start(bf16[8,4,128]{2,1,0:T(4,128)(2,1)} %dec_value.1) | copy-start | bytes 24580
  110.1 1.3 %collective-permute-start.18 = (f32[32,256]{1,0:T(8,128)S(1)}, f32[32,256]{1,0:T(8,128)S(1)}, u32[]{:S(2)}, u32[]{:S(2)}) collective-permute-start(f32[32,256]{1,0:T(8,128)S(1)} %decode.1.mine), channel_id=1, source_target_pairs={{0,1},{1,0},{2,3},{3,2},{4,5},{5,4},{6,7},{7,6},{8,9},{9,8},{10,11... | collective-permute-start | bytes 98312 | tf_op jit(solution)/shard_map/ppermute | solution.py:66

commit v26 on v24

--- a/solution.py
+++ b/solution.py
@@ -94,7 +94,7 @@
 SMEM_REF = pl.BlockSpec(memory_space=pltpu.SMEM)
 ANY_REF = pl.BlockSpec(memory_space=pl.ANY)
 PARAMS = pltpu.CompilerParams(vmem_limit_bytes=20 << 20)
-LARGE = pltpu.CompilerParams(vmem_limit_bytes=58 << 20)
+LARGE = pltpu.CompilerParams(vmem_limit_bytes=40 << 20)
 SMALL = pltpu.CompilerParams(vmem_limit_bytes=16 << 20)
 
 

time: 111 us -> 112 us (level)
  Pallas kernels: 23 us -> 20.3 us
  waiting for transfers between devices: 39 us -> 41.2 us
    pallas_call x1, Pallas kernels: 8.5 us -> 5.8 us  [prepared(): pl.pallas_call(prepare_kernel, grid_spec=pltpu.PrefetchScalarGridSpec(num...]
    ppermute x19, waiting for transfers between devices: 39 us -> 41.2 us  [moved(): return lax.ppermute(block, ('groups', 'seq'), route)]
    unnamed x30 -> x24, local copies, waits for them, and re-layouts: 1.81 us -> 2.54 us
  transfers between devices with their start and end apart: 19 -> 19, of which waited for: 13 -> 13; matrix products, arithmetic and copies ran while one was open for 3% -> 2% of each run, Pallas kernels for 15% -> 13%
where the time goes in v26:
time: 112 us
  waiting for transfers between devices  41.2 us (37%)
  blocking collectives  22.4 us (20%)
  starting transfers between devices  21.9 us (20%)
  Pallas kernels  20.3 us (18%)
  local copies, waits for them, and re-layouts  3.88 us (3%)
  other arithmetic  1.28 us (1%)
    ppermute x19, waiting for transfers between devices, moved(): return lax.ppermute(block, ('groups', 'seq'), route)  41.2 us
    all_to_all x1, blocking collectives, body(): lax.all_to_all(outgoing, 'seq', split_axis=0, concat_axis=1, tiled=True)  22.4 us
    ppermute x19, starting transfers between devices, moved(): return lax.ppermute(block, ('groups', 'seq'), route)  21.9 us
    pallas_call x3, Pallas kernels, product(): pl.pallas_call(functools.partial(product_kernel, plan, group, bool(totals...  10.2 us
    pallas_call x1, Pallas kernels, prepared(): pl.pallas_call(prepare_kernel, grid_spec=pltpu.PrefetchScalarGridSpec(num...  5.8 us
    unnamed x24, local copies, waits for them, and re-layouts  2.54 us
  transfers between devices with their start and end apart: 19, of which 13 were waited for; matrix products, arithmetic and copies ran while one was open for 2% of the time, Pallas kernels for 13%

profile of v26, /device:TPU:0, one launch (start us, length us, event | category | flops | bytes accessed | tf_op | source)
XLA Modules:
  0.0 111.9 jit_solution(13411449317954862087)
XLA Ops:
  0.6 0.5 collective-permute-start.3
  1.1 1.3 %constant_dynamic-slice_fusion = (bf16[256,512]{1,0:T(8,128)(2,1)S(1)}, bf16[256,512]{1,0:T(8,128)(2,1)S(1)}, bf16[256,512]{1,0:T(8,128)(2,1)S(1)}, bf16[256,512]{1,0:T(8,128)(2,1)S(1)}) fusion(bf16[512,512]{1,0:T(8,128)(2,1)} %param.16, s32[]{:T(128)S(6)} %select_n.52, s32[]{:T(128)S(6)} %select_n.51, bf16[512,512]{1,0:T(8,128)(2,1)} %param.15), kind=kLoop, calls=%fused_computation.4 | loop fusion | bytes 2097160 | tf_op jit(solution)/shard_map/dynamic_slice | solution.py:446
  2.4 0.1 pad_maximum_fusion.refs_0_
  2.5 2.7 %collective-permute-start = (bf16[256,1024]{1,0:T(8,128)(2,1)S(1)}, bf16[256,1024]{1,0:T(8,128)(2,1)S(1)}, u32[]{:S(2)}, u32[]{:S(2)}) collective-permute-start(bf16[256,1024]{1,0:T(8,128)(2,1)S(1)} %pad_maximum_fusion.refs_0_), channel_id=1, source_target_pairs={{0,4},{1,5},{2,6},{3,7},{4,0},{5,1},{6,2},{7,3},{8,12},{9,13},{10,... | collective-permute-start | bytes 1572872 | tf_op jit(solution)/shard_map/ppermute | solution.py:66
  5.1 1.5 %collective-permute-start.2 = (bf16[256,1024]{1,0:T(8,128)(2,1)S(1)}, bf16[256,1024]{1,0:T(8,128)(2,1)S(1)}, u32[]{:S(2)}, u32[]{:S(2)}) collective-permute-start(bf16[256,1024]{1,0:T(8,128)(2,1)S(1)} %pad_maximum_fusion.refs_0_), channel_id=1, source_target_pairs={{0,2},{1,3},{2,0},{3,1},{4,6},{5,7},{6,4},{7,5},{8,10},{9,11},{10,... | collective-permute-start | bytes 1572872 | tf_op jit(solution)/shard_map/ppermute | solution.py:66
  6.7 1.4 %collective-permute-start.1 = (bf16[256,1024]{1,0:T(8,128)(2,1)S(1)}, bf16[256,1024]{1,0:T(8,128)(2,1)}, u32[]{:S(2)}, u32[]{:S(2)}) collective-permute-start(bf16[256,1024]{1,0:T(8,128)(2,1)S(1)} %pad_maximum_fusion.refs_0_), channel_id=1, source_target_pairs={{4,8},{5,9},{6,10},{7,11},{8,4},{9,5},{10,6},{11,7},{20,24},{21,25... | collective-permute-start | bytes 1572872 | tf_op jit(solution)/shard_map/ppermute | solution.py:66
  8.1 9.6 %collective-permute-done.refs_4_ = bf16[256,1024]{1,0:T(8,128)(2,1)S(1)} collective-permute-done((bf16[256,1024]{1,0:T(8,128)(2,1)S(1)}, bf16[256,1024]{1,0:T(8,128)(2,1)S(1)}, u32[]{:S(2)}, u32[]{:S(2)}) %collective-permute-start) | collective-permute-done | bytes 524320 | tf_op jit(solution)/shard_map/ppermute | solution.py:66
  17.7 1.5 %collective-permute-done.2.refs_2_ = bf16[256,1024]{1,0:T(8,128)(2,1)S(1)} collective-permute-done((bf16[256,1024]{1,0:T(8,128)(2,1)S(1)}, bf16[256,1024]{1,0:T(8,128)(2,1)S(1)}, u32[]{:S(2)}, u32[]{:S(2)}) %collective-permute-start.2) | collective-permute-done | bytes 524320 | tf_op jit(solution)/shard_map/ppermute | solution.py:66
  19.2 1.5 %collective-permute-start.8 = (bf16[256,1024]{1,0:T(8,128)(2,1)S(1)}, bf16[256,1024]{1,0:T(8,128)(2,1)S(1)}, u32[]{:S(2)}, u32[]{:S(2)}) collective-permute-start(bf16[256,1024]{1,0:T(8,128)(2,1)S(1)} %collective-permute-done.refs_4_), channel_id=1, source_target_pairs={{0,2},{1,3},{2,0},{3,1},{4,6},{5,7},{6,4},{7,5},{8,10},{9,11},{10,... | collective-permute-start | bytes 1572872 | tf_op jit(solution)/shard_map/ppermute | solution.py:66
  20.7 0.0 collective-permute-done.1
  20.7 1.3 %collective-permute-start.6 = (bf16[256,1024]{1,0:T(8,128)(2,1)}, bf16[256,1024]{1,0:T(8,128)(2,1)}, u32[]{:S(2)}, u32[]{:S(2)}) collective-permute-start(bf16[256,1024]{1,0:T(8,128)(2,1)} %collective-permute-done.1), channel_id=1, source_target_pairs={{4,0},{5,1},{6,2},{7,3},{8,12},{9,13},{10,14},{11,15},{20,16},{21,... | collective-permute-start | bytes 1572872 | tf_op jit(solution)/shard_map/ppermute | solution.py:66
  22.0 1.6 %collective-permute-start.4 = (bf16[256,1024]{1,0:T(8,128)(2,1)S(1)}, bf16[256,1024]{1,0:T(8,128)(2,1)S(1)}, u32[]{:S(2)}, u32[]{:S(2)}) collective-permute-start(bf16[256,1024]{1,0:T(8,128)(2,1)S(1)} %collective-permute-done.2.refs_2_), channel_id=1, source_target_pairs={{0,16},{1,17},{2,18},{3,19},{4,20},{5,21},{6,22},{7,23},{8,24},{9,... | collective-permute-start | bytes 1572872 | tf_op jit(solution)/shard_map/ppermute | solution.py:66
  23.5 1.5 %collective-permute-start.5 = (bf16[256,1024]{1,0:T(8,128)(2,1)S(1)}, bf16[256,1024]{1,0:T(8,128)(2,1)}, u32[]{:S(2)}, u32[]{:S(2)}) collective-permute-start(bf16[256,1024]{1,0:T(8,128)(2,1)S(1)} %collective-permute-done.refs_4_), channel_id=1, source_target_pairs={{4,8},{5,9},{6,10},{7,11},{8,4},{9,5},{10,6},{11,7},{20,24},{21,25... | collective-permute-start | bytes 1572872 | tf_op jit(solution)/shard_map/ppermute | solution.py:66
  25.0 0.1 stack.47.place
  25.1 0.1 pad_maximum_fusion.1.refs_1_
  25.2 0.0 collective-permute-done.3.refs_1_
  25.2 0.0 copy-start
  25.2 2.5 %copy-done = bf16[2,160,8192]{2,1,0:T(8,128)(2,1)S(1)} copy-done((bf16[2,160,8192]{2,1,0:T(8,128)(2,1)S(1)}, bf16[2,160,8192]{2,1,0:T(8,128)(2,1)}, u32[]{:S(2)}) %copy-start) | copy-done | bytes 5242904
  27.7 5.8 %normed_halves.1 = (bf16[16,320,256]{2,1,0:T(8,128)(2,1)S(1)}, bf16[16,320,256]{2,1,0:T(8,128)(2,1)S(1)}) custom-call(s32[11]{0:T(128)S(1)} %stack.47.place, bf16[320,8192]{1,0:T(8,128)(2,1)S(1)} %bitcast.17, bf16[320,8192]{1,0:T(8,128)(2,1)} %collective-permute-done.3.refs_1_), custom_call_target="tpu_custom_call" | custom-call | flops 1000 | bytes 1000 | tf_op jit(solution)/shard_map/normed_halves/pallas_call | solution.py:137
  33.5 0.0 collective-permute-done.8.refs_5_
  33.5 3.4 %collective-permute-done.6 = bf16[256,1024]{1,0:T(8,128)(2,1)} collective-permute-done((bf16[256,1024]{1,0:T(8,128)(2,1)}, bf16[256,1024]{1,0:T(8,128)(2,1)}, u32[]{:S(2)}, u32[]{:S(2)}) %collective-permute-start.6) | collective-permute-done | bytes 524320 | tf_op jit(solution)/shard_map/ppermute | solution.py:66
  36.9 0.0 collective-permute-done.4.refs_3_
  36.9 1.1 broadcast_select_fusion.1.refs_0_
  38.0 0.6 collective-permute-start.10
  38.5 1.5 %collective-permute-start.11 = (bf16[256,1024]{1,0:T(8,128)(2,1)S(1)}, bf16[256,1024]{1,0:T(8,128)(2,1)S(1)}, u32[]{:S(2)}, u32[]{:S(2)}) collective-permute-start(bf16[256,1024]{1,0:T(8,128)(2,1)S(1)} %broadcast_select_fusion.1.refs_0_), channel_id=1, source_target_pairs={{0,16},{1,17},{2,18},{3,19},{4,20},{5,21},{6,22},{7,23},{8,24},{9,... | collective-permute-start | bytes 1572872 | tf_op jit(solution)/shard_map/ppermute | solution.py:66
  40.0 0.0 collective-permute-done.5
  40.0 1.3 %collective-permute-start.7 = (bf16[256,1024]{1,0:T(8,128)(2,1)}, bf16[256,1024]{1,0:T(8,128)(2,1)S(1)}, u32[]{:S(2)}, u32[]{:S(2)}) collective-permute-start(bf16[256,1024]{1,0:T(8,128)(2,1)} %collective-permute-done.5), channel_id=1, source_target_pairs={{4,0},{5,1},{6,2},{7,3},{8,12},{9,13},{10,14},{11,15},{20,16},{21,... | collective-permute-start | bytes 1572872 | tf_op jit(solution)/shard_map/ppermute | solution.py:66
  41.3 9.3 %collective-permute-done.10.refs_2_ = bf16[256,1024]{1,0:T(8,128)(2,1)S(1)} collective-permute-done((bf16[256,1024]{1,0:T(8,128)(2,1)S(1)}, bf16[256,1024]{1,0:T(8,128)(2,1)S(1)}, u32[]{:S(2)}, u32[]{:S(2)}) %collective-permute-start.10) | collective-permute-done | bytes 524320 | tf_op jit(solution)/shard_map/ppermute | solution.py:66
  50.6 0.2 collective-permute-done.11.refs_1_
  50.8 3.3 %collective-permute-done.7 = bf16[256,1024]{1,0:T(8,128)(2,1)S(1)} collective-permute-done((bf16[256,1024]{1,0:T(8,128)(2,1)}, bf16[256,1024]{1,0:T(8,128)(2,1)S(1)}, u32[]{:S(2)}, u32[]{:S(2)}) %collective-permute-start.7) | collective-permute-done | bytes 524320 | tf_op jit(solution)/shard_map/ppermute | solution.py:66
  54.1 0.1 broadcast_select_fusion.refs_3_
  54.2 0.8 collective-permute-start.13
  55.0 1.5 %collective-permute-start.14 = (bf16[256,1024]{1,0:T(8,128)(2,1)S(1)}, bf16[256,1024]{1,0:T(8,128)(2,1)S(1)}, u32[]{:S(2)}, u32[]{:S(2)}) collective-permute-start(bf16[256,1024]{1,0:T(8,128)(2,1)S(1)} %broadcast_select_fusion.refs_3_), channel_id=1, source_target_pairs={{0,2},{1,3},{2,0},{3,1},{4,6},{5,7},{6,4},{7,5},{8,10},{9,11},{10,... | collective-permute-start | bytes 1572872 | tf_op jit(solution)/shard_map/ppermute | solution.py:66
  56.5 0.7 collective-permute-start.9
  57.2 3.5 %add_product.3 = (f32[320,1024]{1,0:T(8,128)S(1)}, f32[320,1024]{1,0:T(8,128)S(1)}) custom-call(s32[11]{0:T(128)S(1)} %stack.47.place, bf16[16,320,256]{2,1,0:T(8,128)(2,1)S(1)} %get-tuple-element.41.mine, bf16[16,320,256]{2,1,0:T(8,128)(2,1)S(1)} %get-tuple-element.32.other, bf16[256,1024]{1,0:T(8,128)(2,1)S(1)} %pad_maximum_fusion.refs_0_, ...), custom_call_target="tpu_custom_call" | custom-call | flops 1000 | bytes 1000 | tf_op jit(solution)/shard_map/add_product/pallas_call | solution.py:204
  60.7 4.7 %collective-permute-done.13.refs_5_ = bf16[256,1024]{1,0:T(8,128)(2,1)S(1)} collective-permute-done((bf16[256,1024]{1,0:T(8,128)(2,1)S(1)}, bf16[256,1024]{1,0:T(8,128)(2,1)S(1)}, u32[]{:S(2)}, u32[]{:S(2)}) %collective-permute-start.13) | collective-permute-done | bytes 524320 | tf_op jit(solution)/shard_map/ppermute | solution.py:66
  65.4 0.7 collective-permute-done.14.refs_6_
  66.1 1.3 %collective-permute-done.9.refs_4_ = bf16[256,1024]{1,0:T(8,128)(2,1)S(1)} collective-permute-done((bf16[256,1024]{1,0:T(8,128)(2,1)S(1)}, bf16[256,1024]{1,0:T(8,128)(2,1)S(1)}, u32[]{:S(2)}, u32[]{:S(2)}) %collective-permute-start.9) | collective-permute-done | bytes 524320 | tf_op jit(solution)/shard_map/ppermute | solution.py:66
  67.4 1.2 %collective-permute-start.16 = (bf16[256,1024]{1,0:T(8,128)(2,1)S(1)}, bf16[256,1024]{1,0:T(8,128)(2,1)S(1)}, u32[]{:S(2)}, u32[]{:S(2)}) collective-permute-start(bf16[256,1024]{1,0:T(8,128)(2,1)S(1)} %collective-permute-done.13.refs_5_), channel_id=1, source_target_pairs={{0,2},{1,3},{2,0},{3,1},{4,6},{5,7},{6,4},{7,5},{8,10},{9,11},{10,... | collective-permute-start | bytes 1572872 | tf_op jit(solution)/shard_map/ppermute | solution.py:66
  68.6 1.3 %collective-permute-start.15 = (bf16[256,1024]{1,0:T(8,128)(2,1)S(1)}, bf16[256,1024]{1,0:T(8,128)(2,1)S(1)}, u32[]{:S(2)}, u32[]{:S(2)}) collective-permute-start(bf16[256,1024]{1,0:T(8,128)(2,1)S(1)} %collective-permute-done.10.refs_2_), channel_id=1, source_target_pairs={{0,16},{1,17},{2,18},{3,19},{4,20},{5,21},{6,22},{7,23},{8,24},{9,... | collective-permute-start | bytes 1572872 | tf_op jit(solution)/shard_map/ppermute | solution.py:66
  69.9 0.7 collective-permute-start.12
  70.6 4.3 %add_product.4 = (f32[320,1024]{1,0:T(8,128)S(1)}, f32[320,1024]{1,0:T(8,128)S(1)}) custom-call(s32[11]{0:T(128)S(1)} %stack.47.place, bf16[16,320,256]{2,1,0:T(8,128)(2,1)S(1)} %get-tuple-element.41.mine, bf16[16,320,256]{2,1,0:T(8,128)(2,1)S(1)} %get-tuple-element.32.other, bf16[256,1024]{1,0:T(8,128)(2,1)S(1)} %broadcast_select_fusion.1.refs_0_, ...), custom_call_target="tpu_custom_call" | custom-call | flops 1000 | bytes 1000 | tf_op jit(solution)/shard_map/add_product/pallas_call | solution.py:204
  74.9 2.2 %collective-permute-done.16.refs_2_ = bf16[256,1024]{1,0:T(8,128)(2,1)S(1)} collective-permute-done((bf16[256,1024]{1,0:T(8,128)(2,1)S(1)}, bf16[256,1024]{1,0:T(8,128)(2,1)S(1)}, u32[]{:S(2)}, u32[]{:S(2)}) %collective-permute-start.16) | collective-permute-done | bytes 524320 | tf_op jit(solution)/shard_map/ppermute | solution.py:66
  77.1 0.7 collective-permute-done.15.refs_1_
  77.8 1.3 %collective-permute-done.12.refs_0_ = bf16[256,1024]{1,0:T(8,128)(2,1)S(1)} collective-permute-done((bf16[256,1024]{1,0:T(8,128)(2,1)S(1)}, bf16[256,1024]{1,0:T(8,128)(2,1)S(1)}, u32[]{:S(2)}, u32[]{:S(2)}) %collective-permute-start.12) | collective-permute-done | bytes 524320 | tf_op jit(solution)/shard_map/ppermute | solution.py:66
  79.1 0.0 copy-start.5
  79.1 0.0 copy-start.6
  79.1 0.0 copy-start.10
  79.1 0.0 copy-start.11
  79.2 2.4 %add_product.5 = (f32[320,1024]{1,0:T(8,128)S(1)}, f32[320,1024]{1,0:T(8,128)S(1)}) custom-call(s32[11]{0:T(128)S(1)} %stack.47.place, bf16[16,320,256]{2,1,0:T(8,128)(2,1)S(1)} %get-tuple-element.41.mine, bf16[16,320,256]{2,1,0:T(8,128)(2,1)S(1)} %get-tuple-element.32.other, bf16[256,1024]{1,0:T(8,128)(2,1)S(1)} %collective-permute-done.12.refs_0_, ...), custom_call_target="tpu_custom_call" | custom-call | flops 1000 | bytes 1000 | tf_op jit(solution)/shard_map/add_product/pallas_call | solution.py:204
  81.5 0.1 collective-permute-start.17
  81.6 3.0 %collective-permute-done.17.refs_1_ = f32[320,1024]{1,0:T(8,128)S(1)} collective-permute-done((f32[320,1024]{1,0:T(8,128)S(1)}, f32[320,1024]{1,0:T(8,128)S(1)}, u32[]{:S(2)}, u32[]{:S(2)}) %collective-permute-start.17) | collective-permute-done | bytes 1310752 | tf_op jit(solution)/shard_map/ppermute | solution.py:66
  84.6 0.0 copy-done.2
  84.7 1.0 cache_rows.1
  85.7 0.0 copy-start.7
  85.8 0.0 copy-start.8
  85.8 0.0 copy-start.9
  85.8 22.4 %all_to_all.4 = bf16[16,80,256]{2,1,0:T(8,128)(2,1)S(1)} all-to-all(bf16[16,80,256]{2,1,0:T(8,128)(2,1)S(1)} %cache_rows.1), channel_id=1, replica_groups=mesh['groups'=2,'seq'=16] {'seq'}, dimensions={0} | all-to-all | bytes 1310720 | tf_op jit(solution)/shard_map/all_to_all | solution.py:488
  108.2 0.0 copy-done.7
  108.2 1.1 decode.1.mine
  109.3 0.4 collective-permute-start.18
  109.7 0.8 copied.1
  110.5 0.0 collective-permute-done.18.theirs
  110.6 1.3 %joined.1 = bf16[4,512]{1,0:T(4,128)(2,1)} custom-call(s32[11]{0:T(128)S(1)} %stack.47.place, f32[32,256]{1,0:T(8,128)S(1)} %decode.1.mine, f32[32,256]{1,0:T(8,128)S(1)} %collective-permute-done.18.theirs), custom_call_target="tpu_custom_call" | custom-call | flops 1000 | bytes 1000 | tf_op jit(solution)/shard_map/joined/pallas_call | solution.py:379
  (13 shorter events, 0.0 us)
Async XLA Ops:
  0.6 24.5 %collective-permute-start.3 = (bf16[320,8192]{1,0:T(8,128)(2,1)}, bf16[320,8192]{1,0:T(8,128)(2,1)}, u32[]{:S(2)}, u32[]{:S(2)}) collective-permute-start(bf16[320,8192]{1,0:T(8,128)(2,1)} %bitcast.16), channel_id=1, source_target_pairs={{0,1},{1,0},{2,3},{3,2},{4,5},{5,4},{6,7},{7,6},{8,9},{9,8},{10,11... | collective-permute-start | bytes 15728648 | tf_op jit(solution)/shard_map/ppermute | solution.py:66
  2.5 15.2 %collective-permute-start = (bf16[256,1024]{1,0:T(8,128)(2,1)S(1)}, bf16[256,1024]{1,0:T(8,128)(2,1)S(1)}, u32[]{:S(2)}, u32[]{:S(2)}) collective-permute-start(bf16[256,1024]{1,0:T(8,128)(2,1)S(1)} %pad_maximum_fusion.refs_0_), channel_id=1, source_target_pairs={{0,4},{1,5},{2,6},{3,7},{4,0},{5,1},{6,2},{7,3},{8,12},{9,13},{10,... | collective-permute-start | bytes 1572872 | tf_op jit(solution)/shard_map/ppermute | solution.py:66
  5.1 14.0 %collective-permute-start.2 = (bf16[256,1024]{1,0:T(8,128)(2,1)S(1)}, bf16[256,1024]{1,0:T(8,128)(2,1)S(1)}, u32[]{:S(2)}, u32[]{:S(2)}) collective-permute-start(bf16[256,1024]{1,0:T(8,128)(2,1)S(1)} %pad_maximum_fusion.refs_0_), channel_id=1, source_target_pairs={{0,2},{1,3},{2,0},{3,1},{4,6},{5,7},{6,4},{7,5},{8,10},{9,11},{10,... | collective-permute-start | bytes 1572872 | tf_op jit(solution)/shard_map/ppermute | solution.py:66
  6.7 14.0 %collective-permute-start.1 = (bf16[256,1024]{1,0:T(8,128)(2,1)S(1)}, bf16[256,1024]{1,0:T(8,128)(2,1)}, u32[]{:S(2)}, u32[]{:S(2)}) collective-permute-start(bf16[256,1024]{1,0:T(8,128)(2,1)S(1)} %pad_maximum_fusion.refs_0_), channel_id=1, source_target_pairs={{4,8},{5,9},{6,10},{7,11},{8,4},{9,5},{10,6},{11,7},{20,24},{21,25... | collective-permute-start | bytes 1572872 | tf_op jit(solution)/shard_map/ppermute | solution.py:66
  19.2 14.3 %collective-permute-start.8 = (bf16[256,1024]{1,0:T(8,128)(2,1)S(1)}, bf16[256,1024]{1,0:T(8,128)(2,1)S(1)}, u32[]{:S(2)}, u32[]{:S(2)}) collective-permute-start(bf16[256,1024]{1,0:T(8,128)(2,1)S(1)} %collective-permute-done.refs_4_), channel_id=1, source_target_pairs={{0,2},{1,3},{2,0},{3,1},{4,6},{5,7},{6,4},{7,5},{8,10},{9,11},{10,... | collective-permute-start | bytes 1572872 | tf_op jit(solution)/shard_map/ppermute | solution.py:66
  20.7 16.2 %collective-permute-start.6 = (bf16[256,1024]{1,0:T(8,128)(2,1)}, bf16[256,1024]{1,0:T(8,128)(2,1)}, u32[]{:S(2)}, u32[]{:S(2)}) collective-permute-start(bf16[256,1024]{1,0:T(8,128)(2,1)} %collective-permute-done.1), channel_id=1, source_target_pairs={{4,0},{5,1},{6,2},{7,3},{8,12},{9,13},{10,14},{11,15},{20,16},{21,... | collective-permute-start | bytes 1572872 | tf_op jit(solution)/shard_map/ppermute | solution.py:66
  22.0 14.9 %collective-permute-start.4 = (bf16[256,1024]{1,0:T(8,128)(2,1)S(1)}, bf16[256,1024]{1,0:T(8,128)(2,1)S(1)}, u32[]{:S(2)}, u32[]{:S(2)}) collective-permute-start(bf16[256,1024]{1,0:T(8,128)(2,1)S(1)} %collective-permute-done.2.refs_2_), channel_id=1, source_target_pairs={{0,16},{1,17},{2,18},{3,19},{4,20},{5,21},{6,22},{7,23},{8,24},{9,... | collective-permute-start | bytes 1572872 | tf_op jit(solution)/shard_map/ppermute | solution.py:66
  23.5 16.5 %collective-permute-start.5 = (bf16[256,1024]{1,0:T(8,128)(2,1)S(1)}, bf16[256,1024]{1,0:T(8,128)(2,1)}, u32[]{:S(2)}, u32[]{:S(2)}) collective-permute-start(bf16[256,1024]{1,0:T(8,128)(2,1)S(1)} %collective-permute-done.refs_4_), channel_id=1, source_target_pairs={{4,8},{5,9},{6,10},{7,11},{8,4},{9,5},{10,6},{11,7},{20,24},{21,25... | collective-permute-start | bytes 1572872 | tf_op jit(solution)/shard_map/ppermute | solution.py:66
  25.2 2.5 %copy-start = (bf16[2,160,8192]{2,1,0:T(8,128)(2,1)S(1)}, bf16[2,160,8192]{2,1,0:T(8,128)(2,1)}, u32[]{:S(2)}) copy-start(bf16[2,160,8192]{2,1,0:T(8,128)(2,1)} %param.14) | copy-start | bytes 15728644
  38.0 12.6 %collective-permute-start.10 = (bf16[256,1024]{1,0:T(8,128)(2,1)S(1)}, bf16[256,1024]{1,0:T(8,128)(2,1)S(1)}, u32[]{:S(2)}, u32[]{:S(2)}) collective-permute-start(bf16[256,1024]{1,0:T(8,128)(2,1)S(1)} %broadcast_select_fusion.1.refs_0_), channel_id=1, source_target_pairs={{0,2},{1,3},{2,0},{3,1},{4,6},{5,7},{6,4},{7,5},{8,10},{9,11},{10,... | collective-permute-start | bytes 1572872 | tf_op jit(solution)/shard_map/ppermute | solution.py:66
  38.5 12.3 %collective-permute-start.11 = (bf16[256,1024]{1,0:T(8,128)(2,1)S(1)}, bf16[256,1024]{1,0:T(8,128)(2,1)S(1)}, u32[]{:S(2)}, u32[]{:S(2)}) collective-permute-start(bf16[256,1024]{1,0:T(8,128)(2,1)S(1)} %broadcast_select_fusion.1.refs_0_), channel_id=1, source_target_pairs={{0,16},{1,17},{2,18},{3,19},{4,20},{5,21},{6,22},{7,23},{8,24},{9,... | collective-permute-start | bytes 1572872 | tf_op jit(solution)/shard_map/ppermute | solution.py:66
  40.0 14.1 %collective-permute-start.7 = (bf16[256,1024]{1,0:T(8,128)(2,1)}, bf16[256,1024]{1,0:T(8,128)(2,1)S(1)}, u32[]{:S(2)}, u32[]{:S(2)}) collective-permute-start(bf16[256,1024]{1,0:T(8,128)(2,1)} %collective-permute-done.5), channel_id=1, source_target_pairs={{4,0},{5,1},{6,2},{7,3},{8,12},{9,13},{10,14},{11,15},{20,16},{21,... | collective-permute-start | bytes 1572872 | tf_op jit(solution)/shard_map/ppermute | solution.py:66
  54.2 11.2 %collective-permute-start.13 = (bf16[256,1024]{1,0:T(8,128)(2,1)S(1)}, bf16[256,1024]{1,0:T(8,128)(2,1)S(1)}, u32[]{:S(2)}, u32[]{:S(2)}) collective-permute-start(bf16[256,1024]{1,0:T(8,128)(2,1)S(1)} %broadcast_select_fusion.refs_3_), channel_id=1, source_target_pairs={{0,16},{1,17},{2,18},{3,19},{4,20},{5,21},{6,22},{7,23},{8,24},{9,... | collective-permute-start | bytes 1572872 | tf_op jit(solution)/shard_map/ppermute | solution.py:66
  55.0 11.1 %collective-permute-start.14 = (bf16[256,1024]{1,0:T(8,128)(2,1)S(1)}, bf16[256,1024]{1,0:T(8,128)(2,1)S(1)}, u32[]{:S(2)}, u32[]{:S(2)}) collective-permute-start(bf16[256,1024]{1,0:T(8,128)(2,1)S(1)} %broadcast_select_fusion.refs_3_), channel_id=1, source_target_pairs={{0,2},{1,3},{2,0},{3,1},{4,6},{5,7},{6,4},{7,5},{8,10},{9,11},{10,... | collective-permute-start | bytes 1572872 | tf_op jit(solution)/shard_map/ppermute | solution.py:66
  56.5 10.9 %collective-permute-start.9 = (bf16[256,1024]{1,0:T(8,128)(2,1)S(1)}, bf16[256,1024]{1,0:T(8,128)(2,1)S(1)}, u32[]{:S(2)}, u32[]{:S(2)}) collective-permute-start(bf16[256,1024]{1,0:T(8,128)(2,1)S(1)} %pad_maximum_fusion.1.refs_1_), channel_id=1, source_target_pairs={{0,4},{1,5},{2,6},{3,7},{4,0},{5,1},{6,2},{7,3},{8,12},{9,13},{10,... | collective-permute-start | bytes 1572872 | tf_op jit(solution)/shard_map/ppermute | solution.py:66
  67.4 9.7 %collective-permute-start.16 = (bf16[256,1024]{1,0:T(8,128)(2,1)S(1)}, bf16[256,1024]{1,0:T(8,128)(2,1)S(1)}, u32[]{:S(2)}, u32[]{:S(2)}) collective-permute-start(bf16[256,1024]{1,0:T(8,128)(2,1)S(1)} %collective-permute-done.13.refs_5_), channel_id=1, source_target_pairs={{0,2},{1,3},{2,0},{3,1},{4,6},{5,7},{6,4},{7,5},{8,10},{9,11},{10,... | collective-permute-start | bytes 1572872 | tf_op jit(solution)/shard_map/ppermute | solution.py:66
  68.6 9.2 %collective-permute-start.15 = (bf16[256,1024]{1,0:T(8,128)(2,1)S(1)}, bf16[256,1024]{1,0:T(8,128)(2,1)S(1)}, u32[]{:S(2)}, u32[]{:S(2)}) collective-permute-start(bf16[256,1024]{1,0:T(8,128)(2,1)S(1)} %collective-permute-done.10.refs_2_), channel_id=1, source_target_pairs={{0,16},{1,17},{2,18},{3,19},{4,20},{5,21},{6,22},{7,23},{8,24},{9,... | collective-permute-start | bytes 1572872 | tf_op jit(solution)/shard_map/ppermute | solution.py:66
  69.9 9.2 %collective-permute-start.12 = (bf16[256,1024]{1,0:T(8,128)(2,1)S(1)}, bf16[256,1024]{1,0:T(8,128)(2,1)S(1)}, u32[]{:S(2)}, u32[]{:S(2)}) collective-permute-start(bf16[256,1024]{1,0:T(8,128)(2,1)S(1)} %collective-permute-done.4.refs_3_), channel_id=1, source_target_pairs={{0,4},{1,5},{2,6},{3,7},{4,0},{5,1},{6,2},{7,3},{8,12},{9,13},{10,... | collective-permute-start | bytes 1572872 | tf_op jit(solution)/shard_map/ppermute | solution.py:66
  79.1 5.5 %copy-start.1 = (f32[64,128]{1,0:T(8,128)S(1)}, f32[64,128]{1,0:T(8,128)}, u32[]{:S(2)}) copy-start(f32[64,128]{1,0:T(8,128)} %constant.70.clone.refs_4_.refs_2_) | copy-start | bytes 98308
  79.1 5.5 %copy-start.2 = (f32[64,128]{1,0:T(8,128)S(1)}, f32[64,128]{1,0:T(8,128)}, u32[]{:S(2)}) copy-start(f32[64,128]{1,0:T(8,128)} %constant.71.clone.refs_5_.refs_3_) | copy-start | bytes 98308
  79.1 5.5 %copy-start.3 = (f32[41,128]{1,0:T(8,128)S(1)}, f32[41,128]{1,0:T(8,128)}, u32[]{:S(2)}) copy-start(f32[41,128]{1,0:T(8,128)} %constant.68.clone.refs_2_.refs_0_) | copy-start | bytes 62980
  79.1 5.5 %copy-start.4 = (f32[41,128]{1,0:T(8,128)S(1)}, f32[41,128]{1,0:T(8,128)}, u32[]{:S(2)}) copy-start(f32[41,128]{1,0:T(8,128)} %constant.69.clone.refs_3_.refs_1_) | copy-start | bytes 62980
  79.1 5.6 %copy-start.5 = (f32[160,128]{1,0:T(8,128)S(1)}, f32[160,128]{1,0:T(8,128)}, u32[]{:S(2)}) copy-start(f32[160,128]{1,0:T(8,128)} %constant.72.clone.refs_6_) | copy-start | bytes 245764
  79.1 5.6 %copy-start.6 = (f32[160,128]{1,0:T(8,128)S(1)}, f32[160,128]{1,0:T(8,128)}, u32[]{:S(2)}) copy-start(f32[160,128]{1,0:T(8,128)} %constant.73.clone.refs_7_) | copy-start | bytes 245764
  79.1 5.5 %copy-start.10 = (s32[2]{0:T(128)S(1)}, s32[2]{0:T(128)}, u32[]{:S(2)}) copy-start(s32[2]{0:T(128)} %lengths.3) | copy-start | bytes 28
  79.1 5.5 %copy-start.11 = (s32[8]{0:T(128)S(1)}, s32[8]{0:T(128)}, u32[]{:S(2)}) copy-start(s32[8]{0:T(128)} %owner.3) | copy-start | bytes 100
  81.5 3.1 %collective-permute-start.17 = (f32[320,1024]{1,0:T(8,128)S(1)}, f32[320,1024]{1,0:T(8,128)S(1)}, u32[]{:S(2)}, u32[]{:S(2)}) collective-permute-start(f32[320,1024]{1,0:T(8,128)S(1)} %get-tuple-element.43), channel_id=1, source_target_pairs={{0,1},{1,0},{2,3},{3,2},{4,5},{5,4},{6,7},{7,6},{8,9},{9,8},{10,11... | collective-permute-start | bytes 3932168 | tf_op jit(solution)/shard_map/ppermute | solution.py:66
  85.7 22.5 %copy-start.7 = (bf16[8,4,1024]{2,1,0:T(4,128)(2,1)S(1)}, bf16[8,4,1024]{2,1,0:T(4,128)(2,1)}, u32[]{:S(2)}) copy-start(bf16[8,4,1024]{2,1,0:T(4,128)(2,1)} %dec_query.1) | copy-start | bytes 196612
  85.8 22.4 %copy-start.8 = (bf16[8,4,128]{2,1,0:T(4,128)(2,1)S(1)}, bf16[8,4,128]{2,1,0:T(4,128)(2,1)}, u32[]{:S(2)}) copy-start(bf16[8,4,128]{2,1,0:T(4,128)(2,1)} %dec_key.1) | copy-start | bytes 24580
  85.8 22.4 %copy-start.9 = (bf16[8,4,128]{2,1,0:T(4,128)(2,1)S(1)}, bf16[8,4,128]{2,1,0:T(4,128)(2,1)}, u32[]{:S(2)}) copy-start(bf16[8,4,128]{2,1,0:T(4,128)(2,1)} %dec_value.1) | copy-start | bytes 24580
  109.3 1.3 %collective-permute-start.18 = (f32[32,256]{1,0:T(8,128)S(1)}, f32[32,256]{1,0:T(8,128)S(1)}, u32[]{:S(2)}, u32[]{:S(2)}) collective-permute-start(f32[32,256]{1,0:T(8,128)S(1)} %decode.1.mine), channel_id=1, source_target_pairs={{0,1},{1,0},{2,3},{3,2},{4,5},{5,4},{6,7},{7,6},{8,9},{9,8},{10,11... | collective-permute-start | bytes 98312 | tf_op jit(solution)/shard_map/ppermute | solution.py:66

commit v27 on v24

--- a/solution.py
+++ b/solution.py
@@ -158,23 +158,25 @@
     return place[entry] * 2 + half
 
 
-def product_kernel(plan, group, with_total, place, mine, other, *refs):
+def product_kernel(plan, group, part, with_total, place, mine, other, *refs):
     count = len(plan)
     outs = refs[-7:-5]
     left, right, total, sems, total_sems = refs[-5:]
     rows, depth = mine.shape[1], mine.shape[2]
+    columns = right.shape[2]
+    taken = pl.ds(part, columns)
     waits = []
     for k, (entry, kind) in enumerate(plan):
         area = pl.ds((k % group) * depth, depth)
         slot = k // group
         index = half_index(place, entry, kind)
-        sources = (mine.at[index], other.at[index], refs[k])
+        sources = (mine.at[index], other.at[index], refs[k].at[:, taken])
         targets = (left.at[slot, 0, :, area], left.at[slot, 1, :, area], right.at[slot, area])
         waits.append(
             [fetch(a, b, sems.at[3 * k + i]) for i, (a, b) in enumerate(zip(sources, targets))]
         )
     carried = [
-        fetch(ref, total.at[pl.ds(k * rows, rows)], total_sems.at[k])
+        fetch(ref.at[:, taken], total.at[pl.ds(k * rows, rows)], total_sems.at[k])
         for k, ref in enumerate(refs[count : count + 2 * with_total])
     ]
     for slot in range(count // group):
@@ -195,14 +197,14 @@
             outs[1][...] = value[rows:]
 
 
-def product(place, mine, other, pieces, totals, group, moved_bytes=1000):
+def product(place, mine, other, pieces, totals, group, part=0, columns=None):
     _, rows, depth = mine.shape
-    columns = pieces[0][2].shape[1]
+    columns = columns or pieces[0][2].shape[1]
     plan = [(entry, kind) for entry, kind, _ in pieces]
     count = len(plan)
     out = jax.ShapeDtypeStruct((rows, columns), jnp.float32)
     return pl.pallas_call(
-        functools.partial(product_kernel, plan, group, bool(totals)),
+        functools.partial(product_kernel, plan, group, part, bool(totals)),
         in_specs=[SMEM_REF] + [ANY_REF] * (2 + count + len(totals)),
         out_specs=[VMEM_REF] * 2,
         out_shape=[out] * 2,
@@ -214,7 +216,7 @@
             pltpu.SemaphoreType.DMA((2,)),
         ],
         compiler_params=PARAMS,
-        cost_estimate=cost(1000, moved_bytes),
+        cost_estimate=cost(1000, 1000),
         name="add_product",
     )(place, mine, other, *[array for _, _, array in pieces], *totals)
 
@@ -248,8 +250,7 @@
 
 
 def rows_kernel(place, lengths, owner, *refs):
-    total, came, *tables, out, scratch = refs
-    columns = total.shape[1] // 2
+    totals, came, tables, (out, scratch) = refs[:2], refs[2:4], refs[4:10], refs[10:]
     count_requests, count_rows = lengths.shape[0], scratch.shape[0]
     cosine, sine = turned_by(place[2] * count_rows, tables, tables[4][...], tables[5][...])
     index = place[2] * count_rows + lax.broadcasted_iota(jnp.int32, scratch.shape, 0)
@@ -257,12 +258,14 @@
         live = index < lengths[r]
         for h in range(KEY_VALUE_HEADS):
             for part in range(2):
-                first = part * columns + h * HEAD_SIZE
+                first = (part * KEY_VALUE_HEADS + h) * HEAD_SIZE
+                which = int(first >= totals[0].shape[1])
+                first -= which * totals[0].shape[1]
                 area = (
                     slice(r * count_rows, (r + 1) * count_rows),
                     slice(first, first + HEAD_SIZE),
                 )
-                rows = total[area] + came[area]
+                rows = totals[which][area] + came[which][area]
                 if part == 0:
                     rows = rotated(rows, cosine, sine)
                 scratch[...] = jnp.where(live, rows, 0.0)
@@ -273,19 +276,19 @@
                     out[peer * 2 + b, :, lanes] = picked.astype(jnp.bfloat16)
 
 
-def outgoing_rows(place, lengths, owner, total, came, tables):
-    count_rows = total.shape[0] // lengths.shape[0]
+def outgoing_rows(place, lengths, owner, totals, came, tables):
+    count_rows = totals[0].shape[0] // lengths.shape[0]
     out = (owner.shape[0] * 2, count_rows // 2, 2 * HEAD_SIZE)
     return pl.pallas_call(
         rows_kernel,
-        in_specs=[SMEM_REF] * 3 + [VMEM_REF] * 8,
+        in_specs=[SMEM_REF] * 3 + [VMEM_REF] * 10,
         out_specs=VMEM_REF,
         out_shape=jax.ShapeDtypeStruct(out, jnp.bfloat16),
         scratch_shapes=[pltpu.VMEM((count_rows, HEAD_SIZE), jnp.float32)],
         compiler_params=SMALL,
         cost_estimate=cost(1000, 1000),
         name="cache_rows",
-    )(place, lengths, owner, total, came, *tables)
+    )(place, lengths, owner, *totals, *came, *tables)
 
 
 def decode_kernel(place, lengths, owner, cache, dec_query, dec_key, dec_value, *refs):
@@ -483,8 +486,15 @@
         totals = product(place, after(mine, *rows), other, pieces, totals, 7)
         came = (end_a, *ends, *totals)
         pieces = [(THERE + 1, 1, end_a), (THERE + 2, 1, ends[0]), (THERE + 3, 1, ends[1])]
-        total, given = product(place, after(mine, *came), other, pieces, totals, 3)
-        outgoing = outgoing_rows(place, lengths, owner, total, moved(given, to_core), tables)
+        sums, given = [], []
+        width = end_a.shape[1]
+        split = width * 3 // 4
+        for first, columns in ((0, split), (split, width - split)):
+            left = after(mine, *came, *sums)
+            total, theirs = product(place, left, other, pieces, totals, 3, first, columns)
+            sums.append(total)
+            given.append(moved(theirs, to_core))
+        outgoing = outgoing_rows(place, lengths, owner, sums, given, tables)
         incoming = lax.all_to_all(outgoing, "seq", split_axis=0, concat_axis=1, tiled=True)
         attended = decoded(
             place, lengths, owner, incoming[0], dec_query, dec_key, dec_value, tables

time: 111 us -> 111 us (level)
  waiting for transfers between devices: 39 us -> 37.4 us
    ppermute x19 -> x20, waiting for transfers between devices: 39 us -> 37.4 us  [moved(): return lax.ppermute(block, ('groups', 'seq'), route)]
    pallas_call x4 -> x5, Pallas kernels: 11.3 us -> 12.3 us  [the longest x4 11.3 us: product(): pl.pallas_call(functools.partial(product_kernel, plan, group, part, bool(...]
    ppermute x19 -> x20, starting transfers between devices: 21.6 us -> 22.1 us  [moved(): return lax.ppermute(block, ('groups', 'seq'), route)]
  transfers between devices with their start and end apart: 19 -> 20, of which waited for: 13 -> 13; matrix products, arithmetic and copies ran while one was open for 3% -> 3% of each run, Pallas kernels for 15% -> 17%
where the time goes in v27:
time: 111 us
  waiting for transfers between devices  37.4 us (34%)
  Pallas kernels  24.1 us (22%)
  starting transfers between devices  22.1 us (20%)
  blocking collectives  21.3 us (19%)
  local copies, waits for them, and re-layouts  3.65 us (3%)
  other arithmetic  1.27 us (1%)
    ppermute x20, waiting for transfers between devices, moved(): return lax.ppermute(block, ('groups', 'seq'), route)  37.4 us
    ppermute x20, starting transfers between devices, moved(): return lax.ppermute(block, ('groups', 'seq'), route)  22.1 us
    all_to_all x1, blocking collectives, body(): lax.all_to_all(outgoing, 'seq', split_axis=0, concat_axis=1, tiled=True)  21.3 us
    pallas_call x4, Pallas kernels, product(): pl.pallas_call(functools.partial(product_kernel, plan, group, part, bool(...  11.3 us
    pallas_call x1, Pallas kernels, prepared(): pl.pallas_call(prepare_kernel, grid_spec=pltpu.PrefetchScalarGridSpec(num...  8.51 us
  transfers between devices with their start and end apart: 20, of which 13 were waited for; matrix products, arithmetic and copies ran while one was open for 3% of the time, Pallas kernels for 17%

profile of v27, /device:TPU:0, one launch (start us, length us, event | category | flops | bytes accessed | tf_op | source)
XLA Modules:
  0.0 110.7 jit_solution(679144075709098137)
XLA Ops:
  0.6 0.5 collective-permute-start.3
  1.1 1.3 %constant_dynamic-slice_fusion = (bf16[256,512]{1,0:T(8,128)(2,1)S(1)}, bf16[256,512]{1,0:T(8,128)(2,1)S(1)}, bf16[256,512]{1,0:T(8,128)(2,1)S(1)}, bf16[256,512]{1,0:T(8,128)(2,1)S(1)}) fusion(bf16[512,512]{1,0:T(8,128)(2,1)} %param.16, s32[]{:T(128)S(6)} %select_n.52, s32[]{:T(128)S(6)} %select_n.51, bf16[512,512]{1,0:T(8,128)(2,1)} %param.15), kind=kLoop, calls=%fused_computation.4 | loop fusion | bytes 2097160 | tf_op jit(solution)/shard_map/dynamic_slice | solution.py:449
  2.4 0.1 pad_maximum_fusion.refs_0_
  2.5 2.7 %collective-permute-start = (bf16[256,1024]{1,0:T(8,128)(2,1)S(1)}, bf16[256,1024]{1,0:T(8,128)(2,1)S(1)}, u32[]{:S(2)}, u32[]{:S(2)}) collective-permute-start(bf16[256,1024]{1,0:T(8,128)(2,1)S(1)} %pad_maximum_fusion.refs_0_), channel_id=1, source_target_pairs={{0,4},{1,5},{2,6},{3,7},{4,0},{5,1},{6,2},{7,3},{8,12},{9,13},{10,... | collective-permute-start | bytes 1572872 | tf_op jit(solution)/shard_map/ppermute | solution.py:66
  5.1 1.5 %collective-permute-start.2 = (bf16[256,1024]{1,0:T(8,128)(2,1)S(1)}, bf16[256,1024]{1,0:T(8,128)(2,1)S(1)}, u32[]{:S(2)}, u32[]{:S(2)}) collective-permute-start(bf16[256,1024]{1,0:T(8,128)(2,1)S(1)} %pad_maximum_fusion.refs_0_), channel_id=1, source_target_pairs={{0,2},{1,3},{2,0},{3,1},{4,6},{5,7},{6,4},{7,5},{8,10},{9,11},{10,... | collective-permute-start | bytes 1572872 | tf_op jit(solution)/shard_map/ppermute | solution.py:66
  6.7 1.4 %collective-permute-start.1 = (bf16[256,1024]{1,0:T(8,128)(2,1)S(1)}, bf16[256,1024]{1,0:T(8,128)(2,1)}, u32[]{:S(2)}, u32[]{:S(2)}) collective-permute-start(bf16[256,1024]{1,0:T(8,128)(2,1)S(1)} %pad_maximum_fusion.refs_0_), channel_id=1, source_target_pairs={{4,8},{5,9},{6,10},{7,11},{8,4},{9,5},{10,6},{11,7},{20,24},{21,25... | collective-permute-start | bytes 1572872 | tf_op jit(solution)/shard_map/ppermute | solution.py:66
  8.1 9.6 %collective-permute-done.refs_4_ = bf16[256,1024]{1,0:T(8,128)(2,1)S(1)} collective-permute-done((bf16[256,1024]{1,0:T(8,128)(2,1)S(1)}, bf16[256,1024]{1,0:T(8,128)(2,1)S(1)}, u32[]{:S(2)}, u32[]{:S(2)}) %collective-permute-start) | collective-permute-done | bytes 524320 | tf_op jit(solution)/shard_map/ppermute | solution.py:66
  17.7 1.5 %collective-permute-done.2.refs_2_ = bf16[256,1024]{1,0:T(8,128)(2,1)S(1)} collective-permute-done((bf16[256,1024]{1,0:T(8,128)(2,1)S(1)}, bf16[256,1024]{1,0:T(8,128)(2,1)S(1)}, u32[]{:S(2)}, u32[]{:S(2)}) %collective-permute-start.2) | collective-permute-done | bytes 524320 | tf_op jit(solution)/shard_map/ppermute | solution.py:66
  19.2 1.5 %collective-permute-start.8 = (bf16[256,1024]{1,0:T(8,128)(2,1)S(1)}, bf16[256,1024]{1,0:T(8,128)(2,1)S(1)}, u32[]{:S(2)}, u32[]{:S(2)}) collective-permute-start(bf16[256,1024]{1,0:T(8,128)(2,1)S(1)} %collective-permute-done.refs_4_), channel_id=1, source_target_pairs={{0,2},{1,3},{2,0},{3,1},{4,6},{5,7},{6,4},{7,5},{8,10},{9,11},{10,... | collective-permute-start | bytes 1572872 | tf_op jit(solution)/shard_map/ppermute | solution.py:66
  20.7 1.3 %collective-permute-start.6 = (bf16[256,1024]{1,0:T(8,128)(2,1)}, bf16[256,1024]{1,0:T(8,128)(2,1)}, u32[]{:S(2)}, u32[]{:S(2)}) collective-permute-start(bf16[256,1024]{1,0:T(8,128)(2,1)} %collective-permute-done.1), channel_id=1, source_target_pairs={{4,0},{5,1},{6,2},{7,3},{8,12},{9,13},{10,14},{11,15},{20,16},{21,... | collective-permute-start | bytes 1572872 | tf_op jit(solution)/shard_map/ppermute | solution.py:66
  22.0 1.6 %collective-permute-start.4 = (bf16[256,1024]{1,0:T(8,128)(2,1)S(1)}, bf16[256,1024]{1,0:T(8,128)(2,1)S(1)}, u32[]{:S(2)}, u32[]{:S(2)}) collective-permute-start(bf16[256,1024]{1,0:T(8,128)(2,1)S(1)} %collective-permute-done.2.refs_2_), channel_id=1, source_target_pairs={{0,16},{1,17},{2,18},{3,19},{4,20},{5,21},{6,22},{7,23},{8,24},{9,... | collective-permute-start | bytes 1572872 | tf_op jit(solution)/shard_map/ppermute | solution.py:66
  23.5 1.5 %collective-permute-start.5 = (bf16[256,1024]{1,0:T(8,128)(2,1)S(1)}, bf16[256,1024]{1,0:T(8,128)(2,1)}, u32[]{:S(2)}, u32[]{:S(2)}) collective-permute-start(bf16[256,1024]{1,0:T(8,128)(2,1)S(1)} %collective-permute-done.refs_4_), channel_id=1, source_target_pairs={{4,8},{5,9},{6,10},{7,11},{8,4},{9,5},{10,6},{11,7},{20,24},{21,25... | collective-permute-start | bytes 1572872 | tf_op jit(solution)/shard_map/ppermute | solution.py:66
  25.0 0.6 stack.47.place
  25.6 0.1 pad_maximum_fusion.1.refs_1_
  25.6 0.0 collective-permute-done.3.refs_1_
  25.6 8.5 %normed_halves.1 = (bf16[16,320,256]{2,1,0:T(8,128)(2,1)}, bf16[16,320,256]{2,1,0:T(8,128)(2,1)}) custom-call(s32[11]{0:T(128)} %stack.47.place, bf16[320,8192]{1,0:T(8,128)(2,1)} %bitcast.17, bf16[320,8192]{1,0:T(8,128)(2,1)} %collective-permute-done.3.refs_1_), custom_call_target="tpu_custom_call" | custom-call | flops 1000 | bytes 1000 | tf_op jit(solution)/shard_map/normed_halves/pallas_call | solution.py:137
  34.2 0.0 collective-permute-done.8.refs_5_
  34.2 2.7 %collective-permute-done.6 = bf16[256,1024]{1,0:T(8,128)(2,1)} collective-permute-done((bf16[256,1024]{1,0:T(8,128)(2,1)}, bf16[256,1024]{1,0:T(8,128)(2,1)}, u32[]{:S(2)}, u32[]{:S(2)}) %collective-permute-start.6) | collective-permute-done | bytes 524320 | tf_op jit(solution)/shard_map/ppermute | solution.py:66
  36.9 1.1 broadcast_select_fusion.1.refs_0_
  38.0 0.6 collective-permute-start.10
  38.5 1.5 %collective-permute-start.11 = (bf16[256,1024]{1,0:T(8,128)(2,1)S(1)}, bf16[256,1024]{1,0:T(8,128)(2,1)S(1)}, u32[]{:S(2)}, u32[]{:S(2)}) collective-permute-start(bf16[256,1024]{1,0:T(8,128)(2,1)S(1)} %broadcast_select_fusion.1.refs_0_), channel_id=1, source_target_pairs={{0,16},{1,17},{2,18},{3,19},{4,20},{5,21},{6,22},{7,23},{8,24},{9,... | collective-permute-start | bytes 1572872 | tf_op jit(solution)/shard_map/ppermute | solution.py:66
  40.0 1.3 %collective-permute-start.7 = (bf16[256,1024]{1,0:T(8,128)(2,1)}, bf16[256,1024]{1,0:T(8,128)(2,1)S(1)}, u32[]{:S(2)}, u32[]{:S(2)}) collective-permute-start(bf16[256,1024]{1,0:T(8,128)(2,1)} %collective-permute-done.5), channel_id=1, source_target_pairs={{4,0},{5,1},{6,2},{7,3},{8,12},{9,13},{10,14},{11,15},{20,16},{21,... | collective-permute-start | bytes 1572872 | tf_op jit(solution)/shard_map/ppermute | solution.py:66
  41.3 9.3 %collective-permute-done.10.refs_2_ = bf16[256,1024]{1,0:T(8,128)(2,1)S(1)} collective-permute-done((bf16[256,1024]{1,0:T(8,128)(2,1)S(1)}, bf16[256,1024]{1,0:T(8,128)(2,1)S(1)}, u32[]{:S(2)}, u32[]{:S(2)}) %collective-permute-start.10) | collective-permute-done | bytes 524320 | tf_op jit(solution)/shard_map/ppermute | solution.py:66
  50.6 0.2 collective-permute-done.11.refs_1_
  50.8 3.4 %collective-permute-done.7 = bf16[256,1024]{1,0:T(8,128)(2,1)S(1)} collective-permute-done((bf16[256,1024]{1,0:T(8,128)(2,1)}, bf16[256,1024]{1,0:T(8,128)(2,1)S(1)}, u32[]{:S(2)}, u32[]{:S(2)}) %collective-permute-start.7) | collective-permute-done | bytes 524320 | tf_op jit(solution)/shard_map/ppermute | solution.py:66
  54.2 0.1 broadcast_select_fusion.refs_3_
  54.3 1.6 %collective-permute-start.13 = (bf16[256,1024]{1,0:T(8,128)(2,1)S(1)}, bf16[256,1024]{1,0:T(8,128)(2,1)S(1)}, u32[]{:S(2)}, u32[]{:S(2)}) collective-permute-start(bf16[256,1024]{1,0:T(8,128)(2,1)S(1)} %broadcast_select_fusion.refs_3_), channel_id=1, source_target_pairs={{0,16},{1,17},{2,18},{3,19},{4,20},{5,21},{6,22},{7,23},{8,24},{9,... | collective-permute-start | bytes 1572872 | tf_op jit(solution)/shard_map/ppermute | solution.py:66
  55.8 1.5 %collective-permute-start.14 = (bf16[256,1024]{1,0:T(8,128)(2,1)S(1)}, bf16[256,1024]{1,0:T(8,128)(2,1)S(1)}, u32[]{:S(2)}, u32[]{:S(2)}) collective-permute-start(bf16[256,1024]{1,0:T(8,128)(2,1)S(1)} %broadcast_select_fusion.refs_3_), channel_id=1, source_target_pairs={{0,2},{1,3},{2,0},{3,1},{4,6},{5,7},{6,4},{7,5},{8,10},{9,11},{10,... | collective-permute-start | bytes 1572872 | tf_op jit(solution)/shard_map/ppermute | solution.py:66
  57.3 0.7 collective-permute-start.9
  58.0 1.7 %copy-done.1 = bf16[16,320,256]{2,1,0:T(8,128)(2,1)S(1)} copy-done((bf16[16,320,256]{2,1,0:T(8,128)(2,1)S(1)}, bf16[16,320,256]{2,1,0:T(8,128)(2,1)}, u32[]{:S(2)}) %copy-start.1) | copy-done | bytes 2621464
  59.8 3.5 %add_product.4 = (f32[320,1024]{1,0:T(8,128)S(1)}, f32[320,1024]{1,0:T(8,128)S(1)}) custom-call(s32[11]{0:T(128)S(1)} %copy-done.10, bf16[16,320,256]{2,1,0:T(8,128)(2,1)S(1)} %copy-done, bf16[16,320,256]{2,1,0:T(8,128)(2,1)S(1)} %copy-done.1, bf16[256,1024]{1,0:T(8,128)(2,1)S(1)} %pad_maximum_fusion.refs_0_, ...), custom_call_target="tpu_custom_call" | custom-call | flops 1000 | bytes 1000 | tf_op jit(solution)/shard_map/add_product/pallas_call | solution.py:206
  63.3 2.2 %collective-permute-done.13.refs_5_ = bf16[256,1024]{1,0:T(8,128)(2,1)S(1)} collective-permute-done((bf16[256,1024]{1,0:T(8,128)(2,1)S(1)}, bf16[256,1024]{1,0:T(8,128)(2,1)S(1)}, u32[]{:S(2)}, u32[]{:S(2)}) %collective-permute-start.13) | collective-permute-done | bytes 524320 | tf_op jit(solution)/shard_map/ppermute | solution.py:66
  65.5 1.5 %collective-permute-done.14.refs_6_ = bf16[256,1024]{1,0:T(8,128)(2,1)S(1)} collective-permute-done((bf16[256,1024]{1,0:T(8,128)(2,1)S(1)}, bf16[256,1024]{1,0:T(8,128)(2,1)S(1)}, u32[]{:S(2)}, u32[]{:S(2)}) %collective-permute-start.14) | collective-permute-done | bytes 524320 | tf_op jit(solution)/shard_map/ppermute | solution.py:66
  66.9 1.9 %collective-permute-done.9.refs_4_ = bf16[256,1024]{1,0:T(8,128)(2,1)S(1)} collective-permute-done((bf16[256,1024]{1,0:T(8,128)(2,1)S(1)}, bf16[256,1024]{1,0:T(8,128)(2,1)S(1)}, u32[]{:S(2)}, u32[]{:S(2)}) %collective-permute-start.9) | collective-permute-done | bytes 524320 | tf_op jit(solution)/shard_map/ppermute | solution.py:66
  68.9 0.6 collective-permute-start.16
  69.4 0.5 collective-permute-start.15
  69.9 1.0 collective-permute-start.12
  71.0 4.3 %add_product.5 = (f32[320,1024]{1,0:T(8,128)S(1)}, f32[320,1024]{1,0:T(8,128)S(1)}) custom-call(s32[11]{0:T(128)S(1)} %copy-done.10, bf16[16,320,256]{2,1,0:T(8,128)(2,1)S(1)} %copy-done, bf16[16,320,256]{2,1,0:T(8,128)(2,1)S(1)} %copy-done.2, bf16[256,1024]{1,0:T(8,128)(2,1)S(1)} %broadcast_select_fusion.1.refs_0_, ...), custom_call_target="tpu_custom_call" | custom-call | flops 1000 | bytes 1000 | tf_op jit(solution)/shard_map/add_product/pallas_call | solution.py:206
  75.3 2.7 %collective-permute-done.16.refs_2_ = bf16[256,1024]{1,0:T(8,128)(2,1)S(1)} collective-permute-done((bf16[256,1024]{1,0:T(8,128)(2,1)S(1)}, bf16[256,1024]{1,0:T(8,128)(2,1)S(1)}, u32[]{:S(2)}, u32[]{:S(2)}) %collective-permute-start.16) | collective-permute-done | bytes 524320 | tf_op jit(solution)/shard_map/ppermute | solution.py:66
  78.0 0.6 collective-permute-done.15.refs_1_
  78.6 0.6 collective-permute-done.12.refs_0_
  79.2 2.1 %add_product.6 = (f32[320,768]{1,0:T(8,128)S(1)}, f32[320,768]{1,0:T(8,128)S(1)}) custom-call(s32[11]{0:T(128)S(1)} %copy-done.10, bf16[16,320,256]{2,1,0:T(8,128)(2,1)S(1)} %copy-done, bf16[16,320,256]{2,1,0:T(8,128)(2,1)S(1)} %copy-done.2, bf16[256,1024]{1,0:T(8,128)(2,1)S(1)} %collective-permute-done.12.refs_0_, ...), custom_call_target="tpu_custom_call" | custom-call | flops 1000 | bytes 1000 | tf_op jit(solution)/shard_map/add_product/pallas_call | solution.py:206
  81.2 0.1 collective-permute-start.17
  81.3 0.0 copy-start.3
  81.3 0.0 copy-start.4
  81.4 0.0 copy-start.5
  81.4 0.0 copy-start.6
  81.4 0.0 copy-start.7
  81.4 0.0 copy-start.8
  81.4 0.0 copy-start.13
  81.4 0.0 copy-start.14
  81.4 1.4 %add_product.7 = (f32[320,256]{1,0:T(8,128)S(1)}, f32[320,256]{1,0:T(8,128)S(1)}) custom-call(s32[11]{0:T(128)S(1)} %copy-done.10, bf16[16,320,256]{2,1,0:T(8,128)(2,1)S(1)} %copy-done, bf16[16,320,256]{2,1,0:T(8,128)(2,1)S(1)} %copy-done.2, bf16[256,1024]{1,0:T(8,128)(2,1)S(1)} %collective-permute-done.12.refs_0_, ...), custom_call_target="tpu_custom_call" | custom-call | flops 1000 | bytes 1000 | tf_op jit(solution)/shard_map/add_product/pallas_call | solution.py:206
  82.8 0.0 copy-start.9
  82.8 0.0 copy-start.11
  82.8 0.0 copy-start.12
  82.8 0.5 collective-permute-start.18
  83.4 1.3 %collective-permute-done.18.refs_3_ = f32[320,256]{1,0:T(8,128)S(1)} collective-permute-done((f32[320,256]{1,0:T(8,128)S(1)}, f32[320,256]{1,0:T(8,128)S(1)}, u32[]{:S(2)}, u32[]{:S(2)}) %collective-permute-start.18) | collective-permute-done | bytes 327712 | tf_op jit(solution)/shard_map/ppermute | solution.py:66
  84.7 1.0 cache_rows.1
  85.7 21.3 %all_to_all.4 = bf16[16,80,256]{2,1,0:T(8,128)(2,1)S(1)} all-to-all(bf16[16,80,256]{2,1,0:T(8,128)(2,1)S(1)} %cache_rows.1), channel_id=1, replica_groups=mesh['groups'=2,'seq'=16] {'seq'}, dimensions={0} | all-to-all | bytes 1310720 | tf_op jit(solution)/shard_map/all_to_all | solution.py:498
  107.0 1.1 decode.1.mine
  108.1 0.4 collective-permute-start.19
  108.5 0.8 copied.1
  109.3 0.0 collective-permute-done.19.theirs
  109.4 1.3 %joined.1 = bf16[4,512]{1,0:T(4,128)(2,1)} custom-call(s32[11]{0:T(128)S(1)} %copy-done.10, f32[32,256]{1,0:T(8,128)S(1)} %decode.1.mine, f32[32,256]{1,0:T(8,128)S(1)} %collective-permute-done.19.theirs), custom_call_target="tpu_custom_call" | custom-call | flops 1000 | bytes 1000 | tf_op jit(solution)/shard_map/joined/pallas_call | solution.py:382
  (22 shorter events, 0.0 us)
Async XLA Ops:
  0.6 25.0 %collective-permute-start.3 = (bf16[320,8192]{1,0:T(8,128)(2,1)}, bf16[320,8192]{1,0:T(8,128)(2,1)}, u32[]{:S(2)}, u32[]{:S(2)}) collective-permute-start(bf16[320,8192]{1,0:T(8,128)(2,1)} %bitcast.16), channel_id=1, source_target_pairs={{0,1},{1,0},{2,3},{3,2},{4,5},{5,4},{6,7},{7,6},{8,9},{9,8},{10,11... | collective-permute-start | bytes 15728648 | tf_op jit(solution)/shard_map/ppermute | solution.py:66
  2.5 15.2 %collective-permute-start = (bf16[256,1024]{1,0:T(8,128)(2,1)S(1)}, bf16[256,1024]{1,0:T(8,128)(2,1)S(1)}, u32[]{:S(2)}, u32[]{:S(2)}) collective-permute-start(bf16[256,1024]{1,0:T(8,128)(2,1)S(1)} %pad_maximum_fusion.refs_0_), channel_id=1, source_target_pairs={{0,4},{1,5},{2,6},{3,7},{4,0},{5,1},{6,2},{7,3},{8,12},{9,13},{10,... | collective-permute-start | bytes 1572872 | tf_op jit(solution)/shard_map/ppermute | solution.py:66
  5.1 14.0 %collective-permute-start.2 = (bf16[256,1024]{1,0:T(8,128)(2,1)S(1)}, bf16[256,1024]{1,0:T(8,128)(2,1)S(1)}, u32[]{:S(2)}, u32[]{:S(2)}) collective-permute-start(bf16[256,1024]{1,0:T(8,128)(2,1)S(1)} %pad_maximum_fusion.refs_0_), channel_id=1, source_target_pairs={{0,2},{1,3},{2,0},{3,1},{4,6},{5,7},{6,4},{7,5},{8,10},{9,11},{10,... | collective-permute-start | bytes 1572872 | tf_op jit(solution)/shard_map/ppermute | solution.py:66
  6.7 14.0 %collective-permute-start.1 = (bf16[256,1024]{1,0:T(8,128)(2,1)S(1)}, bf16[256,1024]{1,0:T(8,128)(2,1)}, u32[]{:S(2)}, u32[]{:S(2)}) collective-permute-start(bf16[256,1024]{1,0:T(8,128)(2,1)S(1)} %pad_maximum_fusion.refs_0_), channel_id=1, source_target_pairs={{4,8},{5,9},{6,10},{7,11},{8,4},{9,5},{10,6},{11,7},{20,24},{21,25... | collective-permute-start | bytes 1572872 | tf_op jit(solution)/shard_map/ppermute | solution.py:66
  19.2 15.0 %collective-permute-start.8 = (bf16[256,1024]{1,0:T(8,128)(2,1)S(1)}, bf16[256,1024]{1,0:T(8,128)(2,1)S(1)}, u32[]{:S(2)}, u32[]{:S(2)}) collective-permute-start(bf16[256,1024]{1,0:T(8,128)(2,1)S(1)} %collective-permute-done.refs_4_), channel_id=1, source_target_pairs={{0,2},{1,3},{2,0},{3,1},{4,6},{5,7},{6,4},{7,5},{8,10},{9,11},{10,... | collective-permute-start | bytes 1572872 | tf_op jit(solution)/shard_map/ppermute | solution.py:66
  20.7 16.2 %collective-permute-start.6 = (bf16[256,1024]{1,0:T(8,128)(2,1)}, bf16[256,1024]{1,0:T(8,128)(2,1)}, u32[]{:S(2)}, u32[]{:S(2)}) collective-permute-start(bf16[256,1024]{1,0:T(8,128)(2,1)} %collective-permute-done.1), channel_id=1, source_target_pairs={{4,0},{5,1},{6,2},{7,3},{8,12},{9,13},{10,14},{11,15},{20,16},{21,... | collective-permute-start | bytes 1572872 | tf_op jit(solution)/shard_map/ppermute | solution.py:66
  22.0 14.9 %collective-permute-start.4 = (bf16[256,1024]{1,0:T(8,128)(2,1)S(1)}, bf16[256,1024]{1,0:T(8,128)(2,1)S(1)}, u32[]{:S(2)}, u32[]{:S(2)}) collective-permute-start(bf16[256,1024]{1,0:T(8,128)(2,1)S(1)} %collective-permute-done.2.refs_2_), channel_id=1, source_target_pairs={{0,16},{1,17},{2,18},{3,19},{4,20},{5,21},{6,22},{7,23},{8,24},{9,... | collective-permute-start | bytes 1572872 | tf_op jit(solution)/shard_map/ppermute | solution.py:66
  23.5 16.5 %collective-permute-start.5 = (bf16[256,1024]{1,0:T(8,128)(2,1)S(1)}, bf16[256,1024]{1,0:T(8,128)(2,1)}, u32[]{:S(2)}, u32[]{:S(2)}) collective-permute-start(bf16[256,1024]{1,0:T(8,128)(2,1)S(1)} %collective-permute-done.refs_4_), channel_id=1, source_target_pairs={{4,8},{5,9},{6,10},{7,11},{8,4},{9,5},{10,6},{11,7},{20,24},{21,25... | collective-permute-start | bytes 1572872 | tf_op jit(solution)/shard_map/ppermute | solution.py:66
  34.2 23.9 %copy-start = (bf16[16,320,256]{2,1,0:T(8,128)(2,1)S(1)}, bf16[16,320,256]{2,1,0:T(8,128)(2,1)}, u32[]{:S(2)}) copy-start(bf16[16,320,256]{2,1,0:T(8,128)(2,1)} %get-tuple-element.46.mine) | copy-start | bytes 7864324
  34.2 23.9 %copy-start.10 = (s32[11]{0:T(128)S(1)}, s32[11]{0:T(128)}, u32[]{:S(2)}) copy-start(s32[11]{0:T(128)} %stack.47.place) | copy-start | bytes 136
  38.0 12.6 %collective-permute-start.10 = (bf16[256,1024]{1,0:T(8,128)(2,1)S(1)}, bf16[256,1024]{1,0:T(8,128)(2,1)S(1)}, u32[]{:S(2)}, u32[]{:S(2)}) collective-permute-start(bf16[256,1024]{1,0:T(8,128)(2,1)S(1)} %broadcast_select_fusion.1.refs_0_), channel_id=1, source_target_pairs={{0,2},{1,3},{2,0},{3,1},{4,6},{5,7},{6,4},{7,5},{8,10},{9,11},{10,... | collective-permute-start | bytes 1572872 | tf_op jit(solution)/shard_map/ppermute | solution.py:66
  38.5 12.3 %collective-permute-start.11 = (bf16[256,1024]{1,0:T(8,128)(2,1)S(1)}, bf16[256,1024]{1,0:T(8,128)(2,1)S(1)}, u32[]{:S(2)}, u32[]{:S(2)}) collective-permute-start(bf16[256,1024]{1,0:T(8,128)(2,1)S(1)} %broadcast_select_fusion.1.refs_0_), channel_id=1, source_target_pairs={{0,16},{1,17},{2,18},{3,19},{4,20},{5,21},{6,22},{7,23},{8,24},{9,... | collective-permute-start | bytes 1572872 | tf_op jit(solution)/shard_map/ppermute | solution.py:66
  40.0 14.2 %collective-permute-start.7 = (bf16[256,1024]{1,0:T(8,128)(2,1)}, bf16[256,1024]{1,0:T(8,128)(2,1)S(1)}, u32[]{:S(2)}, u32[]{:S(2)}) collective-permute-start(bf16[256,1024]{1,0:T(8,128)(2,1)} %collective-permute-done.5), channel_id=1, source_target_pairs={{4,0},{5,1},{6,2},{7,3},{8,12},{9,13},{10,14},{11,15},{20,16},{21,... | collective-permute-start | bytes 1572872 | tf_op jit(solution)/shard_map/ppermute | solution.py:66
  54.3 11.2 %collective-permute-start.13 = (bf16[256,1024]{1,0:T(8,128)(2,1)S(1)}, bf16[256,1024]{1,0:T(8,128)(2,1)S(1)}, u32[]{:S(2)}, u32[]{:S(2)}) collective-permute-start(bf16[256,1024]{1,0:T(8,128)(2,1)S(1)} %broadcast_select_fusion.refs_3_), channel_id=1, source_target_pairs={{0,16},{1,17},{2,18},{3,19},{4,20},{5,21},{6,22},{7,23},{8,24},{9,... | collective-permute-start | bytes 1572872 | tf_op jit(solution)/shard_map/ppermute | solution.py:66
  55.8 11.1 %collective-permute-start.14 = (bf16[256,1024]{1,0:T(8,128)(2,1)S(1)}, bf16[256,1024]{1,0:T(8,128)(2,1)S(1)}, u32[]{:S(2)}, u32[]{:S(2)}) collective-permute-start(bf16[256,1024]{1,0:T(8,128)(2,1)S(1)} %broadcast_select_fusion.refs_3_), channel_id=1, source_target_pairs={{0,2},{1,3},{2,0},{3,1},{4,6},{5,7},{6,4},{7,5},{8,10},{9,11},{10,... | collective-permute-start | bytes 1572872 | tf_op jit(solution)/shard_map/ppermute | solution.py:66
  57.3 11.5 %collective-permute-start.9 = (bf16[256,1024]{1,0:T(8,128)(2,1)S(1)}, bf16[256,1024]{1,0:T(8,128)(2,1)S(1)}, u32[]{:S(2)}, u32[]{:S(2)}) collective-permute-start(bf16[256,1024]{1,0:T(8,128)(2,1)S(1)} %pad_maximum_fusion.1.refs_1_), channel_id=1, source_target_pairs={{0,4},{1,5},{2,6},{3,7},{4,0},{5,1},{6,2},{7,3},{8,12},{9,13},{10,... | collective-permute-start | bytes 1572872 | tf_op jit(solution)/shard_map/ppermute | solution.py:66
  58.0 1.7 %copy-start.1 = (bf16[16,320,256]{2,1,0:T(8,128)(2,1)S(1)}, bf16[16,320,256]{2,1,0:T(8,128)(2,1)}, u32[]{:S(2)}) copy-start(bf16[16,320,256]{2,1,0:T(8,128)(2,1)} %get-tuple-element.35.other) | copy-start | bytes 7864324
  59.8 11.2 %copy-start.2 = (bf16[16,320,256]{2,1,0:T(8,128)(2,1)S(1)}, bf16[16,320,256]{2,1,0:T(8,128)(2,1)}, u32[]{:S(2)}) copy-start(bf16[16,320,256]{2,1,0:T(8,128)(2,1)} %get-tuple-element.35.other) | copy-start | bytes 7864324
  68.9 9.2 %collective-permute-start.16 = (bf16[256,1024]{1,0:T(8,128)(2,1)S(1)}, bf16[256,1024]{1,0:T(8,128)(2,1)S(1)}, u32[]{:S(2)}, u32[]{:S(2)}) collective-permute-start(bf16[256,1024]{1,0:T(8,128)(2,1)S(1)} %collective-permute-done.13.refs_5_), channel_id=1, source_target_pairs={{0,2},{1,3},{2,0},{3,1},{4,6},{5,7},{6,4},{7,5},{8,10},{9,11},{10,... | collective-permute-start | bytes 1572872 | tf_op jit(solution)/shard_map/ppermute | solution.py:66
  69.4 9.2 %collective-permute-start.15 = (bf16[256,1024]{1,0:T(8,128)(2,1)S(1)}, bf16[256,1024]{1,0:T(8,128)(2,1)S(1)}, u32[]{:S(2)}, u32[]{:S(2)}) collective-permute-start(bf16[256,1024]{1,0:T(8,128)(2,1)S(1)} %collective-permute-done.10.refs_2_), channel_id=1, source_target_pairs={{0,16},{1,17},{2,18},{3,19},{4,20},{5,21},{6,22},{7,23},{8,24},{9,... | collective-permute-start | bytes 1572872 | tf_op jit(solution)/shard_map/ppermute | solution.py:66
  69.9 9.2 %collective-permute-start.12 = (bf16[256,1024]{1,0:T(8,128)(2,1)S(1)}, bf16[256,1024]{1,0:T(8,128)(2,1)S(1)}, u32[]{:S(2)}, u32[]{:S(2)}) collective-permute-start(bf16[256,1024]{1,0:T(8,128)(2,1)S(1)} %collective-permute-done.4.refs_3_), channel_id=1, source_target_pairs={{0,4},{1,5},{2,6},{3,7},{4,0},{5,1},{6,2},{7,3},{8,12},{9,13},{10,... | collective-permute-start | bytes 1572872 | tf_op jit(solution)/shard_map/ppermute | solution.py:66
  81.2 3.4 %collective-permute-start.17 = (f32[320,768]{1,0:T(8,128)S(1)}, f32[320,768]{1,0:T(8,128)S(1)}, u32[]{:S(2)}, u32[]{:S(2)}) collective-permute-start(f32[320,768]{1,0:T(8,128)S(1)} %get-tuple-element.48), channel_id=1, source_target_pairs={{0,1},{1,0},{2,3},{3,2},{4,5},{5,4},{6,7},{7,6},{8,9},{9,8},{10,11... | collective-permute-start | bytes 2949128 | tf_op jit(solution)/shard_map/ppermute | solution.py:66
  81.3 3.3 %copy-start.3 = (f32[64,128]{1,0:T(8,128)S(1)}, f32[64,128]{1,0:T(8,128)}, u32[]{:S(2)}) copy-start(f32[64,128]{1,0:T(8,128)} %constant.70.clone.refs_6_.refs_2_) | copy-start | bytes 98308
  81.3 3.3 %copy-start.4 = (f32[64,128]{1,0:T(8,128)S(1)}, f32[64,128]{1,0:T(8,128)}, u32[]{:S(2)}) copy-start(f32[64,128]{1,0:T(8,128)} %constant.71.clone.refs_7_.refs_3_) | copy-start | bytes 98308
  81.4 3.3 %copy-start.5 = (f32[41,128]{1,0:T(8,128)S(1)}, f32[41,128]{1,0:T(8,128)}, u32[]{:S(2)}) copy-start(f32[41,128]{1,0:T(8,128)} %constant.68.clone.refs_4_.refs_0_) | copy-start | bytes 62980
  81.4 3.3 %copy-start.6 = (f32[41,128]{1,0:T(8,128)S(1)}, f32[41,128]{1,0:T(8,128)}, u32[]{:S(2)}) copy-start(f32[41,128]{1,0:T(8,128)} %constant.69.clone.refs_5_.refs_1_) | copy-start | bytes 62980
  81.4 3.3 %copy-start.7 = (f32[160,128]{1,0:T(8,128)S(1)}, f32[160,128]{1,0:T(8,128)}, u32[]{:S(2)}) copy-start(f32[160,128]{1,0:T(8,128)} %constant.72.clone.refs_8_) | copy-start | bytes 245764
  81.4 3.3 %copy-start.8 = (f32[160,128]{1,0:T(8,128)S(1)}, f32[160,128]{1,0:T(8,128)}, u32[]{:S(2)}) copy-start(f32[160,128]{1,0:T(8,128)} %constant.73.clone.refs_9_) | copy-start | bytes 245764
  81.4 3.3 %copy-start.13 = (s32[2]{0:T(128)S(1)}, s32[2]{0:T(128)}, u32[]{:S(2)}) copy-start(s32[2]{0:T(128)} %lengths.3) | copy-start | bytes 28
  81.4 3.3 %copy-start.14 = (s32[8]{0:T(128)S(1)}, s32[8]{0:T(128)}, u32[]{:S(2)}) copy-start(s32[8]{0:T(128)} %owner.3) | copy-start | bytes 100
  82.8 24.2 %copy-start.9 = (bf16[8,4,1024]{2,1,0:T(4,128)(2,1)S(1)}, bf16[8,4,1024]{2,1,0:T(4,128)(2,1)}, u32[]{:S(2)}) copy-start(bf16[8,4,1024]{2,1,0:T(4,128)(2,1)} %dec_query.1) | copy-start | bytes 196612
  82.8 24.2 %copy-start.11 = (bf16[8,4,128]{2,1,0:T(4,128)(2,1)S(1)}, bf16[8,4,128]{2,1,0:T(4,128)(2,1)}, u32[]{:S(2)}) copy-start(bf16[8,4,128]{2,1,0:T(4,128)(2,1)} %dec_key.1) | copy-start | bytes 24580
  82.8 24.2 %copy-start.12 = (bf16[8,4,128]{2,1,0:T(4,128)(2,1)S(1)}, bf16[8,4,128]{2,1,0:T(4,128)(2,1)}, u32[]{:S(2)}) copy-start(bf16[8,4,128]{2,1,0:T(4,128)(2,1)} %dec_value.1) | copy-start | bytes 24580
  82.8 1.8 %collective-permute-start.18 = (f32[320,256]{1,0:T(8,128)S(1)}, f32[320,256]{1,0:T(8,128)S(1)}, u32[]{:S(2)}, u32[]{:S(2)}) collective-permute-start(f32[320,256]{1,0:T(8,128)S(1)} %get-tuple-element.49), channel_id=1, source_target_pairs={{0,1},{1,0},{2,3},{3,2},{4,5},{5,4},{6,7},{7,6},{8,9},{9,8},{10,11... | collective-permute-start | bytes 983048 | tf_op jit(solution)/shard_map/ppermute | solution.py:66
  108.1 1.3 %collective-permute-start.19 = (f32[32,256]{1,0:T(8,128)S(1)}, f32[32,256]{1,0:T(8,128)S(1)}, u32[]{:S(2)}, u32[]{:S(2)}) collective-permute-start(f32[32,256]{1,0:T(8,128)S(1)} %decode.1.mine), channel_id=1, source_target_pairs={{0,1},{1,0},{2,3},{3,2},{4,5},{5,4},{6,7},{7,6},{8,9},{9,8},{10,11... | collective-permute-start | bytes 98312 | tf_op jit(solution)/shard_map/ppermute | solution.py:66

commit v28 on v27

--- a/solution.py
+++ b/solution.py
@@ -461,7 +461,7 @@
         layers, rows = (near, middle), (near, middle, across, raw, rest)
         passed = moved(after(middle, *layers), to_end)
         middle_c = moved(near, to_middle)
-        near_y = moved(after(near, across), to_row)
+        near_y = moved(near, to_row)
         across_x = moved(across, to_group)
         mine, other = prepared(place, after(flat, *rows), raw, seq // 2)
         layers, rows = (passed, middle_c, mine), (near_y, across_x, mine, passed)

time: 111 us -> 111 us (level)
  starting transfers between devices: 22.1 us -> 23.4 us
    ppermute x20, starting transfers between devices: 22.1 us -> 23.4 us  [moved(): return lax.ppermute(block, ('groups', 'seq'), route)]
  transfers between devices with their start and end apart: 20 -> 20, of which waited for: 13 -> 12; matrix products, arithmetic and copies ran while one was open for 3% -> 3% of each run, Pallas kernels for 17% -> 17%
where the time goes in v28:
time: 111 us
  waiting for transfers between devices  36.5 us (33%)
  Pallas kernels  24.1 us (22%)
  starting transfers between devices  23.4 us (21%)
  blocking collectives  21.3 us (19%)
  local copies, waits for them, and re-layouts  3.65 us (3%)
  other arithmetic  1.28 us (1%)
    ppermute x20, waiting for transfers between devices, moved(): return lax.ppermute(block, ('groups', 'seq'), route)  36.5 us
    ppermute x20, starting transfers between devices, moved(): return lax.ppermute(block, ('groups', 'seq'), route)  23.4 us
    all_to_all x1, blocking collectives, body(): lax.all_to_all(outgoing, 'seq', split_axis=0, concat_axis=1, tiled=True)  21.3 us
    pallas_call x4, Pallas kernels, product(): pl.pallas_call(functools.partial(product_kernel, plan, group, part, bool(...  11.3 us
    pallas_call x1, Pallas kernels, prepared(): pl.pallas_call(prepare_kernel, grid_spec=pltpu.PrefetchScalarGridSpec(num...  8.51 us
  transfers between devices with their start and end apart: 20, of which 12 were waited for; matrix products, arithmetic and copies ran while one was open for 3% of the time, Pallas kernels for 17%

profile of v28, /device:TPU:0, one launch (start us, length us, event | category | flops | bytes accessed | tf_op | source)
XLA Modules:
  0.0 111.0 jit_solution(1804140215549156431)
XLA Ops:
  0.6 0.5 collective-permute-start.3
  1.1 1.3 %constant_dynamic-slice_fusion = (bf16[256,512]{1,0:T(8,128)(2,1)S(1)}, bf16[256,512]{1,0:T(8,128)(2,1)S(1)}, bf16[256,512]{1,0:T(8,128)(2,1)S(1)}, bf16[256,512]{1,0:T(8,128)(2,1)S(1)}) fusion(bf16[512,512]{1,0:T(8,128)(2,1)} %param.16, s32[]{:T(128)S(6)} %select_n.52, s32[]{:T(128)S(6)} %select_n.51, bf16[512,512]{1,0:T(8,128)(2,1)} %param.15), kind=kLoop, calls=%fused_computation.4 | loop fusion | bytes 2097160 | tf_op jit(solution)/shard_map/dynamic_slice | solution.py:449
  2.4 0.1 pad_maximum_fusion.refs_0_
  2.5 2.7 %collective-permute-start = (bf16[256,1024]{1,0:T(8,128)(2,1)S(1)}, bf16[256,1024]{1,0:T(8,128)(2,1)S(1)}, u32[]{:S(2)}, u32[]{:S(2)}) collective-permute-start(bf16[256,1024]{1,0:T(8,128)(2,1)S(1)} %pad_maximum_fusion.refs_0_), channel_id=1, source_target_pairs={{0,4},{1,5},{2,6},{3,7},{4,0},{5,1},{6,2},{7,3},{8,12},{9,13},{10,... | collective-permute-start | bytes 1572872 | tf_op jit(solution)/shard_map/ppermute | solution.py:66
  5.1 1.4 %collective-permute-start.1 = (bf16[256,1024]{1,0:T(8,128)(2,1)S(1)}, bf16[256,1024]{1,0:T(8,128)(2,1)}, u32[]{:S(2)}, u32[]{:S(2)}) collective-permute-start(bf16[256,1024]{1,0:T(8,128)(2,1)S(1)} %pad_maximum_fusion.refs_0_), channel_id=1, source_target_pairs={{4,8},{5,9},{6,10},{7,11},{8,4},{9,5},{10,6},{11,7},{20,24},{21,25... | collective-permute-start | bytes 1572872 | tf_op jit(solution)/shard_map/ppermute | solution.py:66
  6.6 1.5 %collective-permute-start.2 = (bf16[256,1024]{1,0:T(8,128)(2,1)S(1)}, bf16[256,1024]{1,0:T(8,128)(2,1)S(1)}, u32[]{:S(2)}, u32[]{:S(2)}) collective-permute-start(bf16[256,1024]{1,0:T(8,128)(2,1)S(1)} %pad_maximum_fusion.refs_0_), channel_id=1, source_target_pairs={{0,2},{1,3},{2,0},{3,1},{4,6},{5,7},{6,4},{7,5},{8,10},{9,11},{10,... | collective-permute-start | bytes 1572872 | tf_op jit(solution)/shard_map/ppermute | solution.py:66
  8.1 9.6 %collective-permute-done.refs_4_ = bf16[256,1024]{1,0:T(8,128)(2,1)S(1)} collective-permute-done((bf16[256,1024]{1,0:T(8,128)(2,1)S(1)}, bf16[256,1024]{1,0:T(8,128)(2,1)S(1)}, u32[]{:S(2)}, u32[]{:S(2)}) %collective-permute-start) | collective-permute-done | bytes 524320 | tf_op jit(solution)/shard_map/ppermute | solution.py:66
  17.7 0.0 collective-permute-done.1
  17.7 1.3 %collective-permute-start.6 = (bf16[256,1024]{1,0:T(8,128)(2,1)}, bf16[256,1024]{1,0:T(8,128)(2,1)}, u32[]{:S(2)}, u32[]{:S(2)}) collective-permute-start(bf16[256,1024]{1,0:T(8,128)(2,1)} %collective-permute-done.1), channel_id=1, source_target_pairs={{4,0},{5,1},{6,2},{7,3},{8,12},{9,13},{10,14},{11,15},{20,16},{21,... | collective-permute-start | bytes 1572872 | tf_op jit(solution)/shard_map/ppermute | solution.py:66
  19.0 1.7 %collective-permute-start.8 = (bf16[256,1024]{1,0:T(8,128)(2,1)S(1)}, bf16[256,1024]{1,0:T(8,128)(2,1)S(1)}, u32[]{:S(2)}, u32[]{:S(2)}) collective-permute-start(bf16[256,1024]{1,0:T(8,128)(2,1)S(1)} %collective-permute-done.refs_4_), channel_id=1, source_target_pairs={{0,2},{1,3},{2,0},{3,1},{4,6},{5,7},{6,4},{7,5},{8,10},{9,11},{10,... | collective-permute-start | bytes 1572872 | tf_op jit(solution)/shard_map/ppermute | solution.py:66
  20.7 0.0 collective-permute-done.2.refs_2_
  20.8 1.5 %collective-permute-start.4 = (bf16[256,1024]{1,0:T(8,128)(2,1)S(1)}, bf16[256,1024]{1,0:T(8,128)(2,1)S(1)}, u32[]{:S(2)}, u32[]{:S(2)}) collective-permute-start(bf16[256,1024]{1,0:T(8,128)(2,1)S(1)} %collective-permute-done.2.refs_2_), channel_id=1, source_target_pairs={{0,16},{1,17},{2,18},{3,19},{4,20},{5,21},{6,22},{7,23},{8,24},{9,... | collective-permute-start | bytes 1572872 | tf_op jit(solution)/shard_map/ppermute | solution.py:66
  22.2 1.5 %collective-permute-start.5 = (bf16[256,1024]{1,0:T(8,128)(2,1)S(1)}, bf16[256,1024]{1,0:T(8,128)(2,1)}, u32[]{:S(2)}, u32[]{:S(2)}) collective-permute-start(bf16[256,1024]{1,0:T(8,128)(2,1)S(1)} %collective-permute-done.refs_4_), channel_id=1, source_target_pairs={{4,8},{5,9},{6,10},{7,11},{8,4},{9,5},{10,6},{11,7},{20,24},{21,25... | collective-permute-start | bytes 1572872 | tf_op jit(solution)/shard_map/ppermute | solution.py:66
  23.7 0.6 stack.47.place
  24.3 0.1 pad_maximum_fusion.1.refs_1_
  24.3 0.0 collective-permute-done.3.refs_1_
  24.4 8.5 %normed_halves.1 = (bf16[16,320,256]{2,1,0:T(8,128)(2,1)}, bf16[16,320,256]{2,1,0:T(8,128)(2,1)}) custom-call(s32[11]{0:T(128)} %stack.47.place, bf16[320,8192]{1,0:T(8,128)(2,1)} %bitcast.17, bf16[320,8192]{1,0:T(8,128)(2,1)} %collective-permute-done.3.refs_1_), custom_call_target="tpu_custom_call" | custom-call | flops 1000 | bytes 1000 | tf_op jit(solution)/shard_map/normed_halves/pallas_call | solution.py:137
  32.9 3.1 %collective-permute-done.6 = bf16[256,1024]{1,0:T(8,128)(2,1)} collective-permute-done((bf16[256,1024]{1,0:T(8,128)(2,1)}, bf16[256,1024]{1,0:T(8,128)(2,1)}, u32[]{:S(2)}, u32[]{:S(2)}) %collective-permute-start.6) | collective-permute-done | bytes 524320 | tf_op jit(solution)/shard_map/ppermute | solution.py:66
  35.9 1.1 broadcast_select_fusion.1.refs_0_
  37.0 1.6 %collective-permute-start.10 = (bf16[256,1024]{1,0:T(8,128)(2,1)S(1)}, bf16[256,1024]{1,0:T(8,128)(2,1)S(1)}, u32[]{:S(2)}, u32[]{:S(2)}) collective-permute-start(bf16[256,1024]{1,0:T(8,128)(2,1)S(1)} %broadcast_select_fusion.1.refs_0_), channel_id=1, source_target_pairs={{0,2},{1,3},{2,0},{3,1},{4,6},{5,7},{6,4},{7,5},{8,10},{9,11},{10,... | collective-permute-start | bytes 1572872 | tf_op jit(solution)/shard_map/ppermute | solution.py:66
  38.6 1.5 %collective-permute-start.11 = (bf16[256,1024]{1,0:T(8,128)(2,1)S(1)}, bf16[256,1024]{1,0:T(8,128)(2,1)S(1)}, u32[]{:S(2)}, u32[]{:S(2)}) collective-permute-start(bf16[256,1024]{1,0:T(8,128)(2,1)S(1)} %broadcast_select_fusion.1.refs_0_), channel_id=1, source_target_pairs={{0,16},{1,17},{2,18},{3,19},{4,20},{5,21},{6,22},{7,23},{8,24},{9,... | collective-permute-start | bytes 1572872 | tf_op jit(solution)/shard_map/ppermute | solution.py:66
  40.1 1.3 %collective-permute-start.7 = (bf16[256,1024]{1,0:T(8,128)(2,1)}, bf16[256,1024]{1,0:T(8,128)(2,1)S(1)}, u32[]{:S(2)}, u32[]{:S(2)}) collective-permute-start(bf16[256,1024]{1,0:T(8,128)(2,1)} %collective-permute-done.5), channel_id=1, source_target_pairs={{4,0},{5,1},{6,2},{7,3},{8,12},{9,13},{10,14},{11,15},{20,16},{21,... | collective-permute-start | bytes 1572872 | tf_op jit(solution)/shard_map/ppermute | solution.py:66
  41.4 8.6 %collective-permute-done.10.refs_2_ = bf16[256,1024]{1,0:T(8,128)(2,1)S(1)} collective-permute-done((bf16[256,1024]{1,0:T(8,128)(2,1)S(1)}, bf16[256,1024]{1,0:T(8,128)(2,1)S(1)}, u32[]{:S(2)}, u32[]{:S(2)}) %collective-permute-start.10) | collective-permute-done | bytes 524320 | tf_op jit(solution)/shard_map/ppermute | solution.py:66
  50.1 1.2 %collective-permute-done.11.refs_1_ = bf16[256,1024]{1,0:T(8,128)(2,1)S(1)} collective-permute-done((bf16[256,1024]{1,0:T(8,128)(2,1)S(1)}, bf16[256,1024]{1,0:T(8,128)(2,1)S(1)}, u32[]{:S(2)}, u32[]{:S(2)}) %collective-permute-start.11) | collective-permute-done | bytes 524320 | tf_op jit(solution)/shard_map/ppermute | solution.py:66
  51.3 3.3 %collective-permute-done.7 = bf16[256,1024]{1,0:T(8,128)(2,1)S(1)} collective-permute-done((bf16[256,1024]{1,0:T(8,128)(2,1)}, bf16[256,1024]{1,0:T(8,128)(2,1)S(1)}, u32[]{:S(2)}, u32[]{:S(2)}) %collective-permute-start.7) | collective-permute-done | bytes 524320 | tf_op jit(solution)/shard_map/ppermute | solution.py:66
  54.6 0.1 broadcast_select_fusion.refs_3_
  54.7 1.5 %collective-permute-start.13 = (bf16[256,1024]{1,0:T(8,128)(2,1)S(1)}, bf16[256,1024]{1,0:T(8,128)(2,1)S(1)}, u32[]{:S(2)}, u32[]{:S(2)}) collective-permute-start(bf16[256,1024]{1,0:T(8,128)(2,1)S(1)} %broadcast_select_fusion.refs_3_), channel_id=1, source_target_pairs={{0,16},{1,17},{2,18},{3,19},{4,20},{5,21},{6,22},{7,23},{8,24},{9,... | collective-permute-start | bytes 1572872 | tf_op jit(solution)/shard_map/ppermute | solution.py:66
  56.1 1.5 %collective-permute-start.14 = (bf16[256,1024]{1,0:T(8,128)(2,1)S(1)}, bf16[256,1024]{1,0:T(8,128)(2,1)S(1)}, u32[]{:S(2)}, u32[]{:S(2)}) collective-permute-start(bf16[256,1024]{1,0:T(8,128)(2,1)S(1)} %broadcast_select_fusion.refs_3_), channel_id=1, source_target_pairs={{0,2},{1,3},{2,0},{3,1},{4,6},{5,7},{6,4},{7,5},{8,10},{9,11},{10,... | collective-permute-start | bytes 1572872 | tf_op jit(solution)/shard_map/ppermute | solution.py:66
  57.7 0.7 collective-permute-start.9
  58.4 1.7 %copy-done.1 = bf16[16,320,256]{2,1,0:T(8,128)(2,1)S(1)} copy-done((bf16[16,320,256]{2,1,0:T(8,128)(2,1)S(1)}, bf16[16,320,256]{2,1,0:T(8,128)(2,1)}, u32[]{:S(2)}) %copy-start.1) | copy-done | bytes 2621464
  60.1 3.5 %add_product.4 = (f32[320,1024]{1,0:T(8,128)S(1)}, f32[320,1024]{1,0:T(8,128)S(1)}) custom-call(s32[11]{0:T(128)S(1)} %copy-done.10, bf16[16,320,256]{2,1,0:T(8,128)(2,1)S(1)} %copy-done, bf16[16,320,256]{2,1,0:T(8,128)(2,1)S(1)} %copy-done.1, bf16[256,1024]{1,0:T(8,128)(2,1)S(1)} %pad_maximum_fusion.refs_0_, ...), custom_call_target="tpu_custom_call" | custom-call | flops 1000 | bytes 1000 | tf_op jit(solution)/shard_map/add_product/pallas_call | solution.py:206
  63.6 2.4 %collective-permute-done.13.refs_5_ = bf16[256,1024]{1,0:T(8,128)(2,1)S(1)} collective-permute-done((bf16[256,1024]{1,0:T(8,128)(2,1)S(1)}, bf16[256,1024]{1,0:T(8,128)(2,1)S(1)}, u32[]{:S(2)}, u32[]{:S(2)}) %collective-permute-start.13) | collective-permute-done | bytes 524320 | tf_op jit(solution)/shard_map/ppermute | solution.py:66
  66.0 1.3 %collective-permute-done.14.refs_6_ = bf16[256,1024]{1,0:T(8,128)(2,1)S(1)} collective-permute-done((bf16[256,1024]{1,0:T(8,128)(2,1)S(1)}, bf16[256,1024]{1,0:T(8,128)(2,1)S(1)}, u32[]{:S(2)}, u32[]{:S(2)}) %collective-permute-start.14) | collective-permute-done | bytes 524320 | tf_op jit(solution)/shard_map/ppermute | solution.py:66
  67.3 1.7 %collective-permute-done.9.refs_4_ = bf16[256,1024]{1,0:T(8,128)(2,1)S(1)} collective-permute-done((bf16[256,1024]{1,0:T(8,128)(2,1)S(1)}, bf16[256,1024]{1,0:T(8,128)(2,1)S(1)}, u32[]{:S(2)}, u32[]{:S(2)}) %collective-permute-start.9) | collective-permute-done | bytes 524320 | tf_op jit(solution)/shard_map/ppermute | solution.py:66
  69.0 0.7 collective-permute-start.16
  69.7 0.3 collective-permute-start.15
  70.1 1.2 %collective-permute-start.12 = (bf16[256,1024]{1,0:T(8,128)(2,1)S(1)}, bf16[256,1024]{1,0:T(8,128)(2,1)S(1)}, u32[]{:S(2)}, u32[]{:S(2)}) collective-permute-start(bf16[256,1024]{1,0:T(8,128)(2,1)S(1)} %collective-permute-done.4.refs_3_), channel_id=1, source_target_pairs={{0,4},{1,5},{2,6},{3,7},{4,0},{5,1},{6,2},{7,3},{8,12},{9,13},{10,... | collective-permute-start | bytes 1572872 | tf_op jit(solution)/shard_map/ppermute | solution.py:66
  71.3 4.3 %add_product.5 = (f32[320,1024]{1,0:T(8,128)S(1)}, f32[320,1024]{1,0:T(8,128)S(1)}) custom-call(s32[11]{0:T(128)S(1)} %copy-done.10, bf16[16,320,256]{2,1,0:T(8,128)(2,1)S(1)} %copy-done, bf16[16,320,256]{2,1,0:T(8,128)(2,1)S(1)} %copy-done.2, bf16[256,1024]{1,0:T(8,128)(2,1)S(1)} %broadcast_select_fusion.1.refs_0_, ...), custom_call_target="tpu_custom_call" | custom-call | flops 1000 | bytes 1000 | tf_op jit(solution)/shard_map/add_product/pallas_call | solution.py:206
  75.6 2.7 %collective-permute-done.16.refs_2_ = bf16[256,1024]{1,0:T(8,128)(2,1)S(1)} collective-permute-done((bf16[256,1024]{1,0:T(8,128)(2,1)S(1)}, bf16[256,1024]{1,0:T(8,128)(2,1)S(1)}, u32[]{:S(2)}, u32[]{:S(2)}) %collective-permute-start.16) | collective-permute-done | bytes 524320 | tf_op jit(solution)/shard_map/ppermute | solution.py:66
  78.3 0.6 collective-permute-done.15.refs_1_
  78.9 0.6 collective-permute-done.12.refs_0_
  79.5 2.1 %add_product.6 = (f32[320,768]{1,0:T(8,128)S(1)}, f32[320,768]{1,0:T(8,128)S(1)}) custom-call(s32[11]{0:T(128)S(1)} %copy-done.10, bf16[16,320,256]{2,1,0:T(8,128)(2,1)S(1)} %copy-done, bf16[16,320,256]{2,1,0:T(8,128)(2,1)S(1)} %copy-done.2, bf16[256,1024]{1,0:T(8,128)(2,1)S(1)} %collective-permute-done.12.refs_0_, ...), custom_call_target="tpu_custom_call" | custom-call | flops 1000 | bytes 1000 | tf_op jit(solution)/shard_map/add_product/pallas_call | solution.py:206
  81.6 0.1 collective-permute-start.17
  81.7 0.0 copy-start.3
  81.7 0.0 copy-start.4
  81.7 0.0 copy-start.5
  81.7 0.0 copy-start.6
  81.7 0.0 copy-start.7
  81.8 0.0 copy-start.8
  81.8 0.0 copy-start.13
  81.8 0.0 copy-start.14
  81.8 1.4 %add_product.7 = (f32[320,256]{1,0:T(8,128)S(1)}, f32[320,256]{1,0:T(8,128)S(1)}) custom-call(s32[11]{0:T(128)S(1)} %copy-done.10, bf16[16,320,256]{2,1,0:T(8,128)(2,1)S(1)} %copy-done, bf16[16,320,256]{2,1,0:T(8,128)(2,1)S(1)} %copy-done.2, bf16[256,1024]{1,0:T(8,128)(2,1)S(1)} %collective-permute-done.12.refs_0_, ...), custom_call_target="tpu_custom_call" | custom-call | flops 1000 | bytes 1000 | tf_op jit(solution)/shard_map/add_product/pallas_call | solution.py:206
  83.2 0.0 copy-start.9
  83.2 0.0 copy-start.11
  83.2 0.0 copy-start.12
  83.2 0.5 collective-permute-start.18
  83.7 1.3 %collective-permute-done.18.refs_3_ = f32[320,256]{1,0:T(8,128)S(1)} collective-permute-done((f32[320,256]{1,0:T(8,128)S(1)}, f32[320,256]{1,0:T(8,128)S(1)}, u32[]{:S(2)}, u32[]{:S(2)}) %collective-permute-start.18) | collective-permute-done | bytes 327712 | tf_op jit(solution)/shard_map/ppermute | solution.py:66
  85.0 1.0 cache_rows.1
  86.1 21.3 %all_to_all.4 = bf16[16,80,256]{2,1,0:T(8,128)(2,1)S(1)} all-to-all(bf16[16,80,256]{2,1,0:T(8,128)(2,1)S(1)} %cache_rows.1), channel_id=1, replica_groups=mesh['groups'=2,'seq'=16] {'seq'}, dimensions={0} | all-to-all | bytes 1310720 | tf_op jit(solution)/shard_map/all_to_all | solution.py:498
  107.3 1.1 decode.1.mine
  108.4 0.4 collective-permute-start.19
  108.8 0.8 copied.1
  109.7 0.0 collective-permute-done.19.theirs
  109.7 1.3 %joined.1 = bf16[4,512]{1,0:T(4,128)(2,1)} custom-call(s32[11]{0:T(128)S(1)} %copy-done.10, f32[32,256]{1,0:T(8,128)S(1)} %decode.1.mine, f32[32,256]{1,0:T(8,128)S(1)} %collective-permute-done.19.theirs), custom_call_target="tpu_custom_call" | custom-call | flops 1000 | bytes 1000 | tf_op jit(solution)/shard_map/joined/pallas_call | solution.py:382
  (22 shorter events, 0.0 us)
Async XLA Ops:
  0.6 23.7 %collective-permute-start.3 = (bf16[320,8192]{1,0:T(8,128)(2,1)}, bf16[320,8192]{1,0:T(8,128)(2,1)}, u32[]{:S(2)}, u32[]{:S(2)}) collective-permute-start(bf16[320,8192]{1,0:T(8,128)(2,1)} %bitcast.16), channel_id=1, source_target_pairs={{0,1},{1,0},{2,3},{3,2},{4,5},{5,4},{6,7},{7,6},{8,9},{9,8},{10,11... | collective-permute-start | bytes 15728648 | tf_op jit(solution)/shard_map/ppermute | solution.py:66
  2.5 15.2 %collective-permute-start = (bf16[256,1024]{1,0:T(8,128)(2,1)S(1)}, bf16[256,1024]{1,0:T(8,128)(2,1)S(1)}, u32[]{:S(2)}, u32[]{:S(2)}) collective-permute-start(bf16[256,1024]{1,0:T(8,128)(2,1)S(1)} %pad_maximum_fusion.refs_0_), channel_id=1, source_target_pairs={{0,4},{1,5},{2,6},{3,7},{4,0},{5,1},{6,2},{7,3},{8,12},{9,13},{10,... | collective-permute-start | bytes 1572872 | tf_op jit(solution)/shard_map/ppermute | solution.py:66
  5.1 12.6 %collective-permute-start.1 = (bf16[256,1024]{1,0:T(8,128)(2,1)S(1)}, bf16[256,1024]{1,0:T(8,128)(2,1)}, u32[]{:S(2)}, u32[]{:S(2)}) collective-permute-start(bf16[256,1024]{1,0:T(8,128)(2,1)S(1)} %pad_maximum_fusion.refs_0_), channel_id=1, source_target_pairs={{4,8},{5,9},{6,10},{7,11},{8,4},{9,5},{10,6},{11,7},{20,24},{21,25... | collective-permute-start | bytes 1572872 | tf_op jit(solution)/shard_map/ppermute | solution.py:66
  6.6 14.2 %collective-permute-start.2 = (bf16[256,1024]{1,0:T(8,128)(2,1)S(1)}, bf16[256,1024]{1,0:T(8,128)(2,1)S(1)}, u32[]{:S(2)}, u32[]{:S(2)}) collective-permute-start(bf16[256,1024]{1,0:T(8,128)(2,1)S(1)} %pad_maximum_fusion.refs_0_), channel_id=1, source_target_pairs={{0,2},{1,3},{2,0},{3,1},{4,6},{5,7},{6,4},{7,5},{8,10},{9,11},{10,... | collective-permute-start | bytes 1572872 | tf_op jit(solution)/shard_map/ppermute | solution.py:66
  17.7 18.2 %collective-permute-start.6 = (bf16[256,1024]{1,0:T(8,128)(2,1)}, bf16[256,1024]{1,0:T(8,128)(2,1)}, u32[]{:S(2)}, u32[]{:S(2)}) collective-permute-start(bf16[256,1024]{1,0:T(8,128)(2,1)} %collective-permute-done.1), channel_id=1, source_target_pairs={{4,0},{5,1},{6,2},{7,3},{8,12},{9,13},{10,14},{11,15},{20,16},{21,... | collective-permute-start | bytes 1572872 | tf_op jit(solution)/shard_map/ppermute | solution.py:66
  19.0 16.9 %collective-permute-start.8 = (bf16[256,1024]{1,0:T(8,128)(2,1)S(1)}, bf16[256,1024]{1,0:T(8,128)(2,1)S(1)}, u32[]{:S(2)}, u32[]{:S(2)}) collective-permute-start(bf16[256,1024]{1,0:T(8,128)(2,1)S(1)} %collective-permute-done.refs_4_), channel_id=1, source_target_pairs={{0,2},{1,3},{2,0},{3,1},{4,6},{5,7},{6,4},{7,5},{8,10},{9,11},{10,... | collective-permute-start | bytes 1572872 | tf_op jit(solution)/shard_map/ppermute | solution.py:66
  20.8 15.2 %collective-permute-start.4 = (bf16[256,1024]{1,0:T(8,128)(2,1)S(1)}, bf16[256,1024]{1,0:T(8,128)(2,1)S(1)}, u32[]{:S(2)}, u32[]{:S(2)}) collective-permute-start(bf16[256,1024]{1,0:T(8,128)(2,1)S(1)} %collective-permute-done.2.refs_2_), channel_id=1, source_target_pairs={{0,16},{1,17},{2,18},{3,19},{4,20},{5,21},{6,22},{7,23},{8,24},{9,... | collective-permute-start | bytes 1572872 | tf_op jit(solution)/shard_map/ppermute | solution.py:66
  22.2 17.9 %collective-permute-start.5 = (bf16[256,1024]{1,0:T(8,128)(2,1)S(1)}, bf16[256,1024]{1,0:T(8,128)(2,1)}, u32[]{:S(2)}, u32[]{:S(2)}) collective-permute-start(bf16[256,1024]{1,0:T(8,128)(2,1)S(1)} %collective-permute-done.refs_4_), channel_id=1, source_target_pairs={{4,8},{5,9},{6,10},{7,11},{8,4},{9,5},{10,6},{11,7},{20,24},{21,25... | collective-permute-start | bytes 1572872 | tf_op jit(solution)/shard_map/ppermute | solution.py:66
  32.9 25.5 %copy-start = (bf16[16,320,256]{2,1,0:T(8,128)(2,1)S(1)}, bf16[16,320,256]{2,1,0:T(8,128)(2,1)}, u32[]{:S(2)}) copy-start(bf16[16,320,256]{2,1,0:T(8,128)(2,1)} %get-tuple-element.44.mine) | copy-start | bytes 7864324
  32.9 25.5 %copy-start.10 = (s32[11]{0:T(128)S(1)}, s32[11]{0:T(128)}, u32[]{:S(2)}) copy-start(s32[11]{0:T(128)} %stack.47.place) | copy-start | bytes 136
  37.0 13.0 %collective-permute-start.10 = (bf16[256,1024]{1,0:T(8,128)(2,1)S(1)}, bf16[256,1024]{1,0:T(8,128)(2,1)S(1)}, u32[]{:S(2)}, u32[]{:S(2)}) collective-permute-start(bf16[256,1024]{1,0:T(8,128)(2,1)S(1)} %broadcast_select_fusion.1.refs_0_), channel_id=1, source_target_pairs={{0,2},{1,3},{2,0},{3,1},{4,6},{5,7},{6,4},{7,5},{8,10},{9,11},{10,... | collective-permute-start | bytes 1572872 | tf_op jit(solution)/shard_map/ppermute | solution.py:66
  38.6 12.7 %collective-permute-start.11 = (bf16[256,1024]{1,0:T(8,128)(2,1)S(1)}, bf16[256,1024]{1,0:T(8,128)(2,1)S(1)}, u32[]{:S(2)}, u32[]{:S(2)}) collective-permute-start(bf16[256,1024]{1,0:T(8,128)(2,1)S(1)} %broadcast_select_fusion.1.refs_0_), channel_id=1, source_target_pairs={{0,16},{1,17},{2,18},{3,19},{4,20},{5,21},{6,22},{7,23},{8,24},{9,... | collective-permute-start | bytes 1572872 | tf_op jit(solution)/shard_map/ppermute | solution.py:66
  40.1 14.5 %collective-permute-start.7 = (bf16[256,1024]{1,0:T(8,128)(2,1)}, bf16[256,1024]{1,0:T(8,128)(2,1)S(1)}, u32[]{:S(2)}, u32[]{:S(2)}) collective-permute-start(bf16[256,1024]{1,0:T(8,128)(2,1)} %collective-permute-done.5), channel_id=1, source_target_pairs={{4,0},{5,1},{6,2},{7,3},{8,12},{9,13},{10,14},{11,15},{20,16},{21,... | collective-permute-start | bytes 1572872 | tf_op jit(solution)/shard_map/ppermute | solution.py:66
  54.7 11.3 %collective-permute-start.13 = (bf16[256,1024]{1,0:T(8,128)(2,1)S(1)}, bf16[256,1024]{1,0:T(8,128)(2,1)S(1)}, u32[]{:S(2)}, u32[]{:S(2)}) collective-permute-start(bf16[256,1024]{1,0:T(8,128)(2,1)S(1)} %broadcast_select_fusion.refs_3_), channel_id=1, source_target_pairs={{0,16},{1,17},{2,18},{3,19},{4,20},{5,21},{6,22},{7,23},{8,24},{9,... | collective-permute-start | bytes 1572872 | tf_op jit(solution)/shard_map/ppermute | solution.py:66
  56.1 11.1 %collective-permute-start.14 = (bf16[256,1024]{1,0:T(8,128)(2,1)S(1)}, bf16[256,1024]{1,0:T(8,128)(2,1)S(1)}, u32[]{:S(2)}, u32[]{:S(2)}) collective-permute-start(bf16[256,1024]{1,0:T(8,128)(2,1)S(1)} %broadcast_select_fusion.refs_3_), channel_id=1, source_target_pairs={{0,2},{1,3},{2,0},{3,1},{4,6},{5,7},{6,4},{7,5},{8,10},{9,11},{10,... | collective-permute-start | bytes 1572872 | tf_op jit(solution)/shard_map/ppermute | solution.py:66
  57.7 11.3 %collective-permute-start.9 = (bf16[256,1024]{1,0:T(8,128)(2,1)S(1)}, bf16[256,1024]{1,0:T(8,128)(2,1)S(1)}, u32[]{:S(2)}, u32[]{:S(2)}) collective-permute-start(bf16[256,1024]{1,0:T(8,128)(2,1)S(1)} %pad_maximum_fusion.1.refs_1_), channel_id=1, source_target_pairs={{0,4},{1,5},{2,6},{3,7},{4,0},{5,1},{6,2},{7,3},{8,12},{9,13},{10,... | collective-permute-start | bytes 1572872 | tf_op jit(solution)/shard_map/ppermute | solution.py:66
  58.4 1.7 %copy-start.1 = (bf16[16,320,256]{2,1,0:T(8,128)(2,1)S(1)}, bf16[16,320,256]{2,1,0:T(8,128)(2,1)}, u32[]{:S(2)}) copy-start(bf16[16,320,256]{2,1,0:T(8,128)(2,1)} %get-tuple-element.33.other) | copy-start | bytes 7864324
  60.1 11.2 %copy-start.2 = (bf16[16,320,256]{2,1,0:T(8,128)(2,1)S(1)}, bf16[16,320,256]{2,1,0:T(8,128)(2,1)}, u32[]{:S(2)}) copy-start(bf16[16,320,256]{2,1,0:T(8,128)(2,1)} %get-tuple-element.33.other) | copy-start | bytes 7864324
  69.0 9.3 %collective-permute-start.16 = (bf16[256,1024]{1,0:T(8,128)(2,1)S(1)}, bf16[256,1024]{1,0:T(8,128)(2,1)S(1)}, u32[]{:S(2)}, u32[]{:S(2)}) collective-permute-start(bf16[256,1024]{1,0:T(8,128)(2,1)S(1)} %collective-permute-done.13.refs_5_), channel_id=1, source_target_pairs={{0,2},{1,3},{2,0},{3,1},{4,6},{5,7},{6,4},{7,5},{8,10},{9,11},{10,... | collective-permute-start | bytes 1572872 | tf_op jit(solution)/shard_map/ppermute | solution.py:66
  69.7 9.2 %collective-permute-start.15 = (bf16[256,1024]{1,0:T(8,128)(2,1)S(1)}, bf16[256,1024]{1,0:T(8,128)(2,1)S(1)}, u32[]{:S(2)}, u32[]{:S(2)}) collective-permute-start(bf16[256,1024]{1,0:T(8,128)(2,1)S(1)} %collective-permute-done.10.refs_2_), channel_id=1, source_target_pairs={{0,16},{1,17},{2,18},{3,19},{4,20},{5,21},{6,22},{7,23},{8,24},{9,... | collective-permute-start | bytes 1572872 | tf_op jit(solution)/shard_map/ppermute | solution.py:66
  70.1 9.4 %collective-permute-start.12 = (bf16[256,1024]{1,0:T(8,128)(2,1)S(1)}, bf16[256,1024]{1,0:T(8,128)(2,1)S(1)}, u32[]{:S(2)}, u32[]{:S(2)}) collective-permute-start(bf16[256,1024]{1,0:T(8,128)(2,1)S(1)} %collective-permute-done.4.refs_3_), channel_id=1, source_target_pairs={{0,4},{1,5},{2,6},{3,7},{4,0},{5,1},{6,2},{7,3},{8,12},{9,13},{10,... | collective-permute-start | bytes 1572872 | tf_op jit(solution)/shard_map/ppermute | solution.py:66
  81.6 3.4 %collective-permute-start.17 = (f32[320,768]{1,0:T(8,128)S(1)}, f32[320,768]{1,0:T(8,128)S(1)}, u32[]{:S(2)}, u32[]{:S(2)}) collective-permute-start(f32[320,768]{1,0:T(8,128)S(1)} %get-tuple-element.46), channel_id=1, source_target_pairs={{0,1},{1,0},{2,3},{3,2},{4,5},{5,4},{6,7},{7,6},{8,9},{9,8},{10,11... | collective-permute-start | bytes 2949128 | tf_op jit(solution)/shard_map/ppermute | solution.py:66
  81.7 3.3 %copy-start.3 = (f32[64,128]{1,0:T(8,128)S(1)}, f32[64,128]{1,0:T(8,128)}, u32[]{:S(2)}) copy-start(f32[64,128]{1,0:T(8,128)} %constant.70.clone.refs_6_.refs_2_) | copy-start | bytes 98308
  81.7 3.3 %copy-start.4 = (f32[64,128]{1,0:T(8,128)S(1)}, f32[64,128]{1,0:T(8,128)}, u32[]{:S(2)}) copy-start(f32[64,128]{1,0:T(8,128)} %constant.71.clone.refs_7_.refs_3_) | copy-start | bytes 98308
  81.7 3.3 %copy-start.5 = (f32[41,128]{1,0:T(8,128)S(1)}, f32[41,128]{1,0:T(8,128)}, u32[]{:S(2)}) copy-start(f32[41,128]{1,0:T(8,128)} %constant.68.clone.refs_4_.refs_0_) | copy-start | bytes 62980
  81.7 3.3 %copy-start.6 = (f32[41,128]{1,0:T(8,128)S(1)}, f32[41,128]{1,0:T(8,128)}, u32[]{:S(2)}) copy-start(f32[41,128]{1,0:T(8,128)} %constant.69.clone.refs_5_.refs_1_) | copy-start | bytes 62980
  81.7 3.3 %copy-start.7 = (f32[160,128]{1,0:T(8,128)S(1)}, f32[160,128]{1,0:T(8,128)}, u32[]{:S(2)}) copy-start(f32[160,128]{1,0:T(8,128)} %constant.72.clone.refs_8_) | copy-start | bytes 245764
  81.8 3.3 %copy-start.8 = (f32[160,128]{1,0:T(8,128)S(1)}, f32[160,128]{1,0:T(8,128)}, u32[]{:S(2)}) copy-start(f32[160,128]{1,0:T(8,128)} %constant.73.clone.refs_9_) | copy-start | bytes 245764
  81.8 3.3 %copy-start.13 = (s32[2]{0:T(128)S(1)}, s32[2]{0:T(128)}, u32[]{:S(2)}) copy-start(s32[2]{0:T(128)} %lengths.3) | copy-start | bytes 28
  81.8 3.3 %copy-start.14 = (s32[8]{0:T(128)S(1)}, s32[8]{0:T(128)}, u32[]{:S(2)}) copy-start(s32[8]{0:T(128)} %owner.3) | copy-start | bytes 100
  83.2 24.2 %copy-start.9 = (bf16[8,4,1024]{2,1,0:T(4,128)(2,1)S(1)}, bf16[8,4,1024]{2,1,0:T(4,128)(2,1)}, u32[]{:S(2)}) copy-start(bf16[8,4,1024]{2,1,0:T(4,128)(2,1)} %dec_query.1) | copy-start | bytes 196612
  83.2 24.2 %copy-start.11 = (bf16[8,4,128]{2,1,0:T(4,128)(2,1)S(1)}, bf16[8,4,128]{2,1,0:T(4,128)(2,1)}, u32[]{:S(2)}) copy-start(bf16[8,4,128]{2,1,0:T(4,128)(2,1)} %dec_key.1) | copy-start | bytes 24580
  83.2 24.2 %copy-start.12 = (bf16[8,4,128]{2,1,0:T(4,128)(2,1)S(1)}, bf16[8,4,128]{2,1,0:T(4,128)(2,1)}, u32[]{:S(2)}) copy-start(bf16[8,4,128]{2,1,0:T(4,128)(2,1)} %dec_value.1) | copy-start | bytes 24580
  83.2 1.8 %collective-permute-start.18 = (f32[320,256]{1,0:T(8,128)S(1)}, f32[320,256]{1,0:T(8,128)S(1)}, u32[]{:S(2)}, u32[]{:S(2)}) collective-permute-start(f32[320,256]{1,0:T(8,128)S(1)} %get-tuple-element.47), channel_id=1, source_target_pairs={{0,1},{1,0},{2,3},{3,2},{4,5},{5,4},{6,7},{7,6},{8,9},{9,8},{10,11... | collective-permute-start | bytes 983048 | tf_op jit(solution)/shard_map/ppermute | solution.py:66
  108.4 1.3 %collective-permute-start.19 = (f32[32,256]{1,0:T(8,128)S(1)}, f32[32,256]{1,0:T(8,128)S(1)}, u32[]{:S(2)}, u32[]{:S(2)}) collective-permute-start(f32[32,256]{1,0:T(8,128)S(1)} %decode.1.mine), channel_id=1, source_target_pairs={{0,1},{1,0},{2,3},{3,2},{4,5},{5,4},{6,7},{7,6},{8,9},{9,8},{10,11... | collective-permute-start | bytes 98312 | tf_op jit(solution)/shard_map/ppermute | solution.py:66
